TPU v7x, 32 devices: a whole 2x2x4 slice. The times are simulated.
32 devices in a mesh: rep: 16 (over z, x, core), fsdp: 2 (over y).
Axes of the slice: x: 2, y: 2, z: 4, core: 2. Of those that a mesh axis runs over, the one named last changes fastest.
Arguments:
- global_weights: bfloat16 [8192, 1024], P(None, 'fsdp'), may hold values from -0.75 to 0.75
- momentum: float32 [8192, 1024], P('rep', 'fsdp'), may hold values from -0.3125 to 0.3125
- first_moment: float32 [16, 8192, 1024], P('rep', None, 'fsdp'), may hold values from -0.0029296875 to 0.0029296875
- second_moment: float32 [16, 8192, 1024], P('rep', None, 'fsdp'), may hold values from 1e-08 to 1e-07
- hidden_bank: bfloat16 [16, 256, 8192], P('rep', 'fsdp'), may hold values from -0.15625 to 0.15625
- target_bank: bfloat16 [16, 256, 1024], P('rep', None, 'fsdp'), may hold values from -6 to 6
- token_ids: int32 [16, 2, 512], P('rep'), may hold values from 0 to 255
Outputs:
- new_weights: bfloat16 [8192, 1024], P(None, 'fsdp')
- new_momentum: float32 [8192, 1024], P('rep', 'fsdp')
All inputs are finite; a program needn't handle non-finite values.
Results may differ from a plain program's by a relative error of at most 0.0034.
Values may be sent and summed in bfloat16 or wider, within the bound.
No kernel may reach another device: no remote copies, remote signals or barrier semaphores. Data moves between devices by JAX's collectives and lax.ppermute only.
A program may use at most 192 MiB of HBM per device.

v0:
```python
import jax
import jax.numpy as jnp
from jax import lax
from jax.sharding import PartitionSpec as P


def per_device(
    global_weights, momentum, first_moment, second_moment, hidden_bank, target_bank, token_ids
):
    ids_all = token_ids[0]
    inner_count = ids_all.shape[0]
    token_count = ids_all.shape[1]
    flat_ids = ids_all.reshape(-1)
    local_bank = hidden_bank[0]
    whole_bank = lax.all_gather(local_bank, "fsdp", axis=0, tiled=True)
    picked_all = jnp.take(whole_bank, flat_ids, axis=0)
    picked_all = picked_all.reshape(inner_count, token_count, local_bank.shape[1])
    targets = target_bank[0]
    start_weights = global_weights.astype(jnp.float32)
    weights = start_weights
    first_state = first_moment[0]
    second_state = second_moment[0]
    for inner_step in range(inner_count):
        picked = picked_all[inner_step]
        wanted = jnp.take(targets, ids_all[inner_step], axis=0)
        output = jnp.dot(picked, weights.astype(jnp.bfloat16), preferred_element_type=jnp.float32)
        residual_out = ((output - wanted.astype(jnp.float32)) / token_count).astype(jnp.bfloat16)
        gradient = lax.dot_general(
            picked, residual_out, (((0,), (0,)), ((), ())), preferred_element_type=jnp.float32
        )
        first_state = 0.9 * first_state + 0.1 * gradient
        second_state = 0.95 * second_state + 0.05 * gradient * gradient
        weights = weights - 0.1 * (first_state / (jnp.sqrt(second_state) + 1e-08) + 0.1 * weights)
    local_change = start_weights - weights
    share_rows = momentum.shape[0]
    row_begin = lax.axis_index("rep") * share_rows
    full_momentum = lax.all_gather(momentum, "rep", axis=0, tiled=True)
    summed = lax.psum(local_change, "rep")
    average = summed / lax.axis_size("rep")
    full_new = 0.9 * full_momentum + average
    new_weights = (start_weights - 0.7 * (average + 0.9 * full_new)).astype(jnp.bfloat16)
    new_momentum = lax.dynamic_slice_in_dim(full_new, row_begin, share_rows, 0)
    return (new_weights, new_momentum)


def solution(mesh):
    return jax.shard_map(
        per_device,
        mesh=mesh,
        in_specs=(
            P(None, "fsdp"),
            P("rep", "fsdp"),
            P("rep", None, "fsdp"),
            P("rep", None, "fsdp"),
            P("rep", "fsdp", None),
            P("rep", None, "fsdp"),
            P("rep", None, None),
        ),
        out_specs=(P(None, "fsdp"), P("rep", "fsdp")),
        check_vma=False,
    )
```

profile of v0, /device:TPU:0, one launch (start us, length us, event | category | flops | bytes accessed | tf_op | source)
XLA Modules:
  0.0 646.9 jit_solution(32025852965930049)
XLA Ops:
  7.2 0.0 copy-start
  7.2 0.0 all-gather.6.cloned.1.call-start
  7.2 0.7 all-gather.6.cloned.1.call-update
  7.9 0.0 all-reduce.2.cloned.1.call-start
  8.0 0.7 copy.10
  8.7 0.7 copy.9
  9.3 0.8 fusion.51
  10.1 0.0 copy-done
  10.1 2.0 gather_fusion.1
  12.1 2.0 gather_fusion.2
  14.2 54.9 %all-gather.6.cloned.1.call-done = bf16[1,256,8192]{2,1,0:T(8,128)(2,1)} async-done(((bf16[1,128,8192]{2,1,0:T(8,128)(2,1)}), bf16[1,256,8192]{2,1,0:T(8,128)(2,1)}) %all-gather.6.cloned.1.call-update) | async-done | bytes 4194320 | tf_op jit(solution)/shard_map/all_gather | solution.py:15
  69.0 30.6 %gather_fusion = bf16[1024,8192]{1,0:T(8,128)(2,1)} fusion(bf16[256,8192]{1,0:T(8,128)(2,1)} %bitcast.41, s32[1024]{0:T(1024)S(1)} %broadcast_clamp_fusion), kind=kCustom, calls=%fused_computation.2 | custom fusion | bytes 33558528 | tf_op jit(solution)/shard_map/jit(_take)/gather | solution.py:16
  99.6 8.5 %broadcast_select_fusion = bf16[1024,8192]{1,0:T(8,128)(2,1)S(1)} fusion(bf16[1024,8192]{1,0:T(8,128)(2,1)} %gather_fusion, pred[1024]{0:T(1024)(128)(4,1)S(1)} %compare_and_fusion), kind=kLoop, calls=%fused_computation.22 | loop fusion | flops 8388608 | bytes 33555456 | tf_op jit(solution)/shard_map/jit(_take)/select_n | solution.py:16
  108.2 0.0 copy-start.2
  108.2 13.9 %fusion.38 = bf16[512,512]{1,0:T(8,128)(2,1)S(1)} fusion(bf16[8192,512]{1,0:T(8,128)(2,1)} %param.9, bf16[1024,8192]{1,0:T(8,128)(2,1)S(1)} %broadcast_select_fusion, bf16[512,512]{1,0:T(8,128)(2,1)S(1)} %gather_fusion.1, pred[512]{0:T(512)(128)(4,1)S(1)} %compare_and_fusion.2), kind=kOutput, calls=%fused_computation.36 | convolution fusion | flops 4296278016 | bytes 17826304 | tf_op jit(solution)/shard_map/dot_general | solution.py:26
  122.1 0.0 copy-done.2
  122.1 8.2 %fusion.17 = f32[8192,512]{1,0:T(8,128)} fusion(bf16[512,512]{1,0:T(8,128)(2,1)S(1)} %fusion.38, bf16[1024,8192]{1,0:T(8,128)(2,1)S(1)} %broadcast_select_fusion), kind=kOutput, calls=%fused_computation.28 | convolution fusion | flops 4294967296 | bytes 25690112 | tf_op jit(solution)/shard_map/dot_general | solution.py:28
  130.3 26.1 %fusion.41 = bf16[512,512]{1,0:T(8,128)(2,1)S(1)} fusion(bf16[8192,512]{1,0:T(8,128)(2,1)} %param.9, f32[8192,512]{1,0:T(8,128)} %fusion.17, f32[1,8192,512]{2,1,0:T(8,128)} %param.11, f32[1,8192,512]{2,1,0:T(8,128)} %param.12, bf16[1024,8192]{1,0:T(8,128)(2,1)} %copy-done.2, bf16[512,512]{1,0:T(8,128)(2,1)S(1)} %gather_fusion.2, ...), kind=kOutput, calls=%fused_computation.37 | convolution fusion | flops 4359192576 | bytes 68157952 | tf_op jit(solution)/shard_map/dot_general | solution.py:26
  156.4 37.5 %convert_subtract_fusion.1 = f32[8192,512]{1,0:T(8,128)} fusion(bf16[8192,512]{1,0:T(8,128)(2,1)} %param.9, f32[8192,512]{1,0:T(8,128)} %fusion.17, f32[1,8192,512]{2,1,0:T(8,128)} %param.11, f32[1,8192,512]{2,1,0:T(8,128)} %param.12, bf16[512,512]{1,0:T(8,128)(2,1)S(1)} %fusion.41, bf16[1024,8192]{1,0:T(8,128)(2,1)} %copy-done.2), kind=kOutput, calls=%fused_computation.4 | convolution fusion | flops 4412407808 | bytes 84410368 | tf_op jit(solution)/shard_map/dot_general | solution.py:28
  193.9 0.0 all-reduce.2.cloned.1.call-update
  193.9 0.0 all-gather.4.cloned.1.call-start
  193.9 0.7 all-gather.4.cloned.1.call-update
  194.6 297.7 %all-reduce.2.cloned.1.call-done = f32[8192,512]{1,0:T(8,128)} async-done(((f32[8192,512]{1,0:T(8,128)}), f32[8192,512]{1,0:T(8,128)}) %all-reduce.2.cloned.1.call-update) | async-done | bytes 16777232 | tf_op jit(solution)/shard_map/psum | solution.py:38
  492.3 128.8 %all-gather.4.cloned.1.call-done = f32[8192,512]{1,0:T(8,128)} async-done(((f32[512,512]{1,0:T(8,128)}), f32[8192,512]{1,0:T(8,128)}) %all-gather.4.cloned.1.call-update) | async-done | bytes 16777232 | tf_op jit(solution)/shard_map/all_gather | solution.py:37
  621.1 0.0 copy-start.1
  621.1 18.2 %multiply_add_fusion = (f32[8192,512]{1,0:T(8,128)S(1)}, bf16[8192,512]{1,0:T(8,128)(2,1)}) fusion(f32[8192,512]{1,0:T(8,128)} %all-gather.4.cloned.1.call-done, f32[8192,512]{1,0:T(8,128)} %all-reduce.2.cloned.1.call-done, bf16[8192,512]{1,0:T(8,128)(2,1)} %param.9), kind=kLoop, calls=%fused_computation.21 | loop fusion | flops 37748736 | bytes 67108864 | tf_op jit(solution)/shard_map/add | solution.py:40
  639.3 1.0 constant_dynamic-slice_fusion
  640.3 0.0 copy-done.1
  (9 shorter events, 0.1 us)
Async XLA Ops:
  7.2 3.0 copy-start
  7.2 61.9 %all-gather.6.cloned.1.call-start = ((), (), s32[]{:S(2)}) async-start(), calls=%async_computation.2 | async-start | bytes 6291456 | tf_op jit(solution)/shard_map/all_gather | solution.py:15
  7.9 484.4 %all-reduce.2.cloned.1.call-start = ((), (), s32[]{:S(2)}) async-start(), calls=%async_computation | async-start | bytes 33554432 | tf_op jit(solution)/shard_map/psum | solution.py:38
  108.2 13.9 %copy-start.2 = (bf16[1024,8192]{1,0:T(8,128)(2,1)}, bf16[1024,8192]{1,0:T(8,128)(2,1)S(1)}, u32[]{:S(2)}) copy-start(bf16[1024,8192]{1,0:T(8,128)(2,1)S(1)} %broadcast_select_fusion) | copy-start | bytes 50331652
  193.9 427.3 %all-gather.4.cloned.1.call-start = ((), (), s32[]{:S(2)}) async-start(), calls=%async_computation.1 | async-start | bytes 17825792 | tf_op jit(solution)/shard_map/all_gather | solution.py:37
  621.1 19.2 %copy-start.1 = (bf16[1,256,512]{2,1,0:T(8,128)(2,1)S(1)}, bf16[1,256,512]{2,1,0:T(8,128)(2,1)}, u32[]{:S(2)}) copy-start(bf16[1,256,512]{2,1,0:T(8,128)(2,1)} %param.14) | copy-start | bytes 786436
Sparse Core Ops, SparseCore 0:
  9.6 59.4 all-gather.5
  194.0 298.2 all-reduce.1
  494.5 126.6 all-gather.3
where the time goes:
time: 647 us
  waiting for transfers between devices  483 us (75%)
  matrix products  85.7 us (13%)
  local copies, waits for them, and re-layouts  37.7 us (6%)
  other arithmetic  26.7 us (4%)
  between operations  13.9 us (2%)
    psum x1, waiting for transfers between devices, per_device(): summed = lax.psum(local_change, 'rep')  298 us
    all_gather x1, waiting for transfers between devices, per_device(): full_momentum = lax.all_gather(momentum, 'rep', axis=0, tiled=True)  129 us
    all_gather x1, waiting for transfers between devices, per_device(): whole_bank = lax.all_gather(local_bank, 'fsdp', axis=0, tiled=True)  54.9 us
    dot_general x2, matrix products, per_device(): lax.dot_general(picked, residual_out, (((0,), (0,)), ((), ())), preferred...  45.7 us
    dot_general x2, matrix products, per_device(): jnp.dot(picked, weights.astype(jnp.bfloat16), preferred_element_type=jnp....  40 us
    gather x1, local copies, waits for them, and re-layouts, per_device(): picked_all = jnp.take(whole_bank, flat_ids, axis=0)  30.6 us
    add x1, other arithmetic, per_device(): full_new = 0.9 * full_momentum + average  18.2 us
  transfers between devices with their start and end apart: 3, of which 3 were waited for; matrix products, arithmetic and copies ran while one was open for 1% of the time, Pallas kernels for 0%

commit v1 on v0

v1 whole, which is shorter than its diff:
```python
import functools
import jax
import jax.numpy as jnp
from jax import lax
from jax.experimental import pallas as pl
from jax.experimental.pallas import tpu as pltpu
from jax.sharding import PartitionSpec as P

F32 = jnp.float32
BF16 = jnp.bfloat16
WIRE = jnp.float16
WIRE_SCALE = 64.0
CORES = 2
LANES = 128
VMEM_LIMIT = 50 * 1024 * 1024


def forward_kernel(part_ref, weights_ref, turned_ref, product_ref):
    @pl.when(pl.program_id(0) == 0)
    def _():
        product_ref[...] = jnp.zeros_like(product_ref)

    part = part_ref[...]
    turned_ref[...] = part.T
    product_ref[...] += jnp.dot(part, weights_ref[...], preferred_element_type=F32)


def forward(part, weights):
    rows, depth = part.shape
    columns = weights.shape[1]
    block = min(depth, 2048)
    return pl.pallas_call(
        forward_kernel,
        grid=(depth // block,),
        in_specs=[
            pl.BlockSpec((rows, block), lambda d: (0, d)),
            pl.BlockSpec((block, columns), lambda d: (d, 0)),
        ],
        out_specs=[
            pl.BlockSpec((block, rows), lambda d: (d, 0)),
            pl.BlockSpec((rows, columns), lambda d: (0, 0)),
        ],
        out_shape=[
            jax.ShapeDtypeStruct((depth, rows), BF16),
            jax.ShapeDtypeStruct((rows, columns), F32),
        ],
        compiler_params=pltpu.CompilerParams(vmem_limit_bytes=VMEM_LIMIT),
        cost_estimate=pl.CostEstimate(
            flops=2 * rows * depth * columns,
            bytes_accessed=2 * depth * columns + 4 * rows * depth,
            transcendentals=0,
        ),
        name="forward",
    )(part, weights)


def inner_kernel(
    tokens,
    core_ref,
    low_ref,
    high_ref,
    low_turned_ref,
    high_turned_ref,
    start_ref,
    first_ref,
    second_ref,
    low_product_ref,
    high_product_ref,
    target_ref,
    count_ref,
    send_ref,
    keep_ref,
    first_state,
    second_state,
    weights_state,
    output_state,
    residual_state,
):
    step = pl.program_id(0)
    slab = pl.program_id(1)
    groups, cores, rows, columns = start_ref.shape
    core = core_ref[0]

    def weigh(output, which):
        residual = ((output - target_ref[...].astype(F32)) / tokens).astype(BF16)
        residual_state[...] = (residual.astype(F32) * count_ref[which]).astype(BF16)

    def update(first, second, weights, gradient):
        first = 0.9 * first + 0.1 * gradient
        second = 0.95 * second + 0.05 * gradient * gradient
        weights = weights - 0.1 * (first / (jnp.sqrt(second) + 1e-08) + 0.1 * weights)
        return first, second, weights

    def gradient_of(group, which):
        turned = jnp.concatenate(
            [low_turned_ref[group, which], high_turned_ref[group, which]], axis=1
        )
        return jnp.dot(turned, residual_state[...], preferred_element_type=F32)

    @pl.when((step == 0) & (slab == 0))
    def _():
        weigh(jnp.concatenate([low_product_ref[...], high_product_ref[...]], axis=0), 0)
        output_state[...] = jnp.zeros_like(output_state)

    @pl.when((step == 1) & (slab == 0))
    def _():
        weigh(output_state[...], 1)

    @pl.when(step == 0)
    def _():
        total = jnp.zeros(output_state.shape, F32)
        for group in range(groups):
            for which in range(cores):
                first, second, weights = update(
                    first_ref[group, which],
                    second_ref[group, which],
                    start_ref[group, which].astype(F32),
                    gradient_of(group, which),
                )
                first_state[slab, group, which] = first
                second_state[slab, group, which] = second
                weights_state[slab, group, which] = weights
                place = pl.ds((group * cores + which) * rows, rows)
                picked = jnp.concatenate([low_ref[:, place], high_ref[:, place]], axis=0)
                total += jnp.dot(picked, weights.astype(BF16), preferred_element_type=F32)
        output_state[...] += total

    @pl.when(step == 1)
    def _():
        for group in range(groups):
            for which, out_ref in ((1 - core, send_ref), (core, keep_ref)):
                _, _, weights = update(
                    first_state[slab, group, which],
                    second_state[slab, group, which],
                    weights_state[slab, group, which],
                    gradient_of(group, which),
                )
                change = start_ref[group, which].astype(F32) - weights
                out_ref[group] = change * WIRE_SCALE


def inner(chunk, width, core, banks, turned, start, first, second, products, target, count, tokens):
    slabs, groups, cores, rows, _ = start.shape
    half, depth = banks[0].shape
    block = depth // slabs

    def held(step, slab):
        return jnp.where(step == 0, slab, slabs - 1)

    def drawn(step, slab):
        return jnp.where(step == 0, 0, slab)

    natural = pl.BlockSpec((half, block), lambda s, z, c: (0, held(s, z)))
    flipped = pl.BlockSpec((None, groups, cores, rows, half), lambda s, z, c: (z, 0, 0, 0, 0))
    state = pl.BlockSpec(
        (None, groups, cores, rows, width), lambda s, z, c: (held(s, z), 0, 0, 0, chunk)
    )
    product = pl.BlockSpec((half, width), lambda s, z, c: (0, chunk))
    change = pl.BlockSpec((None, groups, rows, width), lambda s, z, c: (drawn(s, z), 0, 0, 0))
    elements = depth * width
    return pl.pallas_call(
        functools.partial(inner_kernel, float(tokens)),
        grid_spec=pltpu.PrefetchScalarGridSpec(
            num_scalar_prefetch=1,
            grid=(2, slabs),
            in_specs=[
                natural,
                natural,
                flipped,
                flipped,
                pl.BlockSpec(
                    (None, groups, cores, rows, width), lambda s, z, c: (z, 0, 0, 0, chunk)
                ),
                state,
                state,
                product,
                product,
                pl.BlockSpec((2 * half, width), lambda s, z, c: (0, chunk)),
                pl.BlockSpec(count.shape, lambda s, z, c: (0, 0, 0)),
            ],
            out_specs=[change, change],
            scratch_shapes=[
                pltpu.VMEM((slabs, groups, cores, rows, width), F32),
                pltpu.VMEM((slabs, groups, cores, rows, width), F32),
                pltpu.VMEM((slabs, groups, cores, rows, width), F32),
                pltpu.VMEM((2 * half, width), F32),
                pltpu.VMEM((2 * half, width), BF16),
            ],
        ),
        out_shape=[
            jax.ShapeDtypeStruct((slabs, groups, rows, width), F32),
            jax.ShapeDtypeStruct((slabs, groups, rows, width), F32),
        ],
        compiler_params=pltpu.CompilerParams(vmem_limit_bytes=VMEM_LIMIT),
        cost_estimate=pl.CostEstimate(
            flops=12 * half * elements,
            bytes_accessed=16 * elements + 12 * half * depth,
            transcendentals=4 * elements,
        ),
        name="inner",
    )(core, *banks, *turned, start, first, second, *products, target, count)


def split_rep(mesh_size):
    slabs = 4 if mesh_size % 8 == 0 else 1
    return slabs, mesh_size // (slabs * CORES), CORES


def per_device(sizes, global_weights, momentum, first_moment, second_moment, hidden_bank, target_bank, token_ids):
    reps, shards = sizes
    slabs, groups, cores = split_rep(reps)
    depth, columns = global_weights.shape
    rows = depth // reps
    store = hidden_bank.shape[1] * shards
    ids = token_ids[0]
    tokens = ids.shape[1]
    width = min(columns, LANES)
    chunks = columns // width

    mine = lax.axis_index("rep")
    my_core = lax.rem(mine, cores)
    my_group = lax.rem(mine // cores, groups)
    my_slab = mine // (cores * groups)

    def index_of(slab, group, core):
        return (slab * groups + group) * cores + core

    places = [(s, g, c) for s in range(slabs) for g in range(groups) for c in range(cores)]

    def shifted(array, slab=0, group=0, core=0):
        pairs = [
            (
                index_of(s, g, c),
                index_of((s + slab) % slabs, (g + group) % groups, (c + core) % cores),
            )
            for s, g, c in places
        ]
        return lax.ppermute(array, "rep", pairs)

    own_bank = hidden_bank[0]
    target = target_bank[0]
    count = jnp.sum(
        ids[:, :, None] == jnp.arange(store, dtype=ids.dtype)[None, None, :], axis=1
    ).astype(F32)
    if shards == 2:
        banks = (own_bank, lax.ppermute(own_bank, "fsdp", [(0, 1), (1, 0)]))
        swap = lax.axis_index("fsdp") == 1
        half = store // 2
        target = jnp.where(swap, jnp.roll(target, half, axis=0), target)
        count = jnp.where(swap, jnp.roll(count, half, axis=1), count)
    else:
        whole = lax.all_gather(own_bank, "fsdp", axis=0, tiled=True)
        banks = (whole[: store // 2], whole[store // 2 :])
    count = count[:, :, None]

    turned, products = zip(*(forward(bank, global_weights) for bank in banks))
    turned = [array.reshape(slabs, groups, cores, rows, store // 2) for array in turned]
    cut = (slabs, groups, cores, rows, columns)
    start = global_weights.reshape(cut)
    first = first_moment.reshape(cut)
    second = second_moment.reshape(cut)
    core_operand = my_core.reshape(1).astype(jnp.int32)
    my_start = lax.dynamic_slice_in_dim(global_weights, mine * rows, rows, 0)

    def wire(array):
        return array.astype(WIRE)

    def pick(array, index):
        return lax.dynamic_index_in_dim(array, index, 0, keepdims=False)

    new_momentum = []
    new_weights = []
    for chunk in range(chunks):
        send, keep = inner(
            chunk, width, core_operand, banks, turned, start, first, second, products, target, count, tokens
        )
        total = keep + shifted(wire(send), core=1).astype(F32)

        by_group = jnp.swapaxes(total, 0, 1)
        total = pick(by_group, my_group)
        for ahead in range(1, groups):
            outgoing = wire(pick(by_group, lax.rem(my_group + ahead, groups)))
            total = total + shifted(outgoing, group=ahead).astype(F32)

        by_slab = total
        total = pick(by_slab, my_slab)
        for ahead in range(1, slabs):
            outgoing = wire(pick(by_slab, lax.rem(my_slab + ahead, slabs)))
            total = total + shifted(outgoing, slab=ahead).astype(F32)

        share = slice(chunk * width, (chunk + 1) * width)
        average = total * (1.0 / (WIRE_SCALE * reps))
        moved = 0.9 * momentum[:, share] + average
        new_momentum.append(moved)
        fresh = (my_start[:, share].astype(F32) - 0.7 * (average + 0.9 * moved)).astype(BF16)

        stack = jnp.stack([fresh] + [shifted(fresh, slab=ahead) for ahead in range(1, slabs)])
        stack = jnp.stack([stack] + [shifted(stack, group=ahead) for ahead in range(1, groups)])
        stack = jnp.stack([stack, shifted(stack, core=1)])
        new_weights.append(stack)

    place = jnp.stack([my_slab, my_group, my_core]).astype(jnp.int32)
    return assemble(place, new_weights, cut), jnp.concatenate(new_momentum, axis=1)


def assemble_kernel(chunks, width, place_ref, *refs):
    stacks, out_ref, semaphore = refs[:chunks], refs[chunks], refs[chunks + 1]
    cores, groups, slabs = stacks[0].shape[:3]
    copies = []
    for chunk, stack in enumerate(stacks):
        for c in range(cores):
            for g in range(groups):
                for s in range(slabs):
                    target = out_ref.at[
                        lax.rem(place_ref[0] + (slabs - s), slabs),
                        lax.rem(place_ref[1] + (groups - g), groups),
                        lax.rem(place_ref[2] + (cores - c), cores),
                        :,
                        pl.ds(chunk * width, width),
                    ]
                    copies.append(
                        pltpu.make_async_copy(stack.at[c, g, s], target, semaphore.at[len(copies)])
                    )
    for copy in copies:
        copy.start()
    for copy in copies:
        copy.wait()


def assemble(place, stacks, cut):
    count = len(stacks) * cut[0] * cut[1] * cut[2]
    width = stacks[0].shape[-1]
    out = pl.pallas_call(
        functools.partial(assemble_kernel, len(stacks), width),
        in_specs=[pl.BlockSpec(memory_space=pltpu.SMEM)]
        + [pl.BlockSpec(memory_space=pl.ANY)] * len(stacks),
        out_specs=pl.BlockSpec(memory_space=pl.ANY),
        out_shape=jax.ShapeDtypeStruct(cut, BF16),
        scratch_shapes=[pltpu.SemaphoreType.DMA((count,))],
        compiler_params=pltpu.CompilerParams(vmem_limit_bytes=VMEM_LIMIT),
        name="assemble",
    )(place, *stacks)
    return out.reshape(cut[0] * cut[1] * cut[2] * cut[3], cut[4])


def solution(mesh):
    sizes = (mesh.shape["rep"], mesh.shape["fsdp"])
    return jax.shard_map(
        functools.partial(per_device, sizes),
        mesh=mesh,
        in_specs=(
            P(None, "fsdp"),
            P("rep", "fsdp"),
            P("rep", None, "fsdp"),
            P("rep", None, "fsdp"),
            P("rep", "fsdp", None),
            P("rep", None, "fsdp"),
            P("rep", None, None),
        ),
        out_specs=(P(None, "fsdp"), P("rep", "fsdp")),
        check_vma=False,
    )
```

time: 647 us -> 461 us (0.71)
  waiting for transfers between devices: 483 us -> 86.3 us
  Pallas kernels: 0 us -> 264 us
  matrix products: 85.7 us -> 0 us
  starting transfers between devices: 0.12 us -> 83.5 us
  local copies, waits for them, and re-layouts: 37.7 us -> 5.89 us
  between operations: 13.9 us -> 1.21 us
  other arithmetic: 26.7 us -> 16.6 us
    psum x1 -> x0, waiting for transfers between devices: 298 us -> none  [per_device(): summed = lax.psum(local_change, 'rep')]
    pallas_call x0 -> x7, Pallas kernels: none -> 264 us  [the longest x1 193 us: assemble(): pl.pallas_call(functools.partial(assemble_kernel, len(stacks), width), in...]
    all_gather x2 -> x0, waiting for transfers between devices: 184 us -> none  [the longest x1 129 us: per_device(): full_momentum = lax.all_gather(momentum, 'rep', axis=0, tiled=True)]
    ppermute x0 -> x41, waiting for transfers between devices: none -> 86.3 us  [the longest x40 48.7 us: shifted(): return lax.ppermute(array, 'rep', pairs)]
    dot_general x4 -> x0, matrix products: 85.7 us -> none  [the longest x2 45.7 us: per_device(): lax.dot_general(picked, residual_out, (((0,), (0,)), ((), ())), preferred...]
    ppermute x0 -> x41, starting transfers between devices: none -> 83.5 us  [the longest x40 80.4 us: shifted(): return lax.ppermute(array, 'rep', pairs)]
    gather x3 -> x0, local copies, waits for them, and re-layouts: 34.5 us -> none  [the longest x1 30.6 us: per_device(): picked_all = jnp.take(whole_bank, flat_ids, axis=0)]
    add x1 -> x8, other arithmetic: 18.2 us -> 1.62 us  [the longest x4 1.14 us: per_device(): total = keep + shifted(wire(send), core=1).astype(F32)]
  transfers between devices with their start and end apart: 3 -> 41, of which waited for: 3 -> 12; matrix products, arithmetic and copies ran while one was open for 1% -> 4% of each run, Pallas kernels for 0% -> 11%
where the time goes in v1:
time: 461 us; the launch traced here: 457 us
  Pallas kernels  264 us (57%)
  waiting for transfers between devices  86.3 us (19%)
  starting transfers between devices  83.5 us (18%)
  other arithmetic  16.6 us (4%)
  local copies, waits for them, and re-layouts  5.89 us (1%)
    pallas_call x1, Pallas kernels, assemble(): pl.pallas_call(functools.partial(assemble_kernel, len(stacks), width), in...  193 us
    ppermute x40, starting transfers between devices, shifted(): return lax.ppermute(array, 'rep', pairs)  80.4 us
    pallas_call x4, Pallas kernels, inner(): pl.pallas_call(functools.partial(inner_kernel, float(tokens)), grid_spec=...  59.9 us
    ppermute x40, waiting for transfers between devices, shifted(): return lax.ppermute(array, 'rep', pairs)  48.7 us
    ppermute x1, waiting for transfers between devices, per_device(): banks = (own_bank, lax.ppermute(own_bank, 'fsdp', [(0, 1), (1, 0)]))  37.6 us
    pallas_call x2, Pallas kernels, forward(): pl.pallas_call(forward_kernel, grid=(depth // block,), in_specs=[pl.Block...  10.9 us
  transfers between devices with their start and end apart: 41, of which 12 were waited for; matrix products, arithmetic and copies ran while one was open for 4% of the time, Pallas kernels for 11%

profile of v1, /device:TPU:0, one launch (start us, length us, event | category | flops | bytes accessed | tf_op | source)
XLA Modules:
  0.0 457.1 jit_solution(16313803882562502582)
XLA Ops:
  0.6 3.0 collective-permute-start
  3.7 0.9 convert_reduce_fusion
  5.0 5.5 %forward.2 = (bf16[8192,128]{1,0:T(8,128)(2,1)S(1)}, f32[128,512]{1,0:T(8,128)S(1)}) custom-call(bf16[128,8192]{1,0:T(8,128)(2,1)} %bitcast.176, bf16[8192,512]{1,0:T(8,128)(2,1)} %weights_ref.3), custom_call_target="tpu_custom_call" | custom-call | flops 1073741824 | bytes 12582912 | tf_op jit(solution)/shard_map/forward/pallas_call | solution.py:32
  10.4 1.3 copy-done
  11.9 37.6 %collective-permute-done.part_ref.high_ref = bf16[128,8192]{1,0:T(8,128)(2,1)S(1)} collective-permute-done((bf16[128,8192]{1,0:T(8,128)(2,1)}, bf16[128,8192]{1,0:T(8,128)(2,1)S(1)}, u32[]{:S(2)}, u32[]{:S(2)}) %collective-permute-start) | collective-permute-done | bytes 2097184 | tf_op jit(solution)/shard_map/ppermute | solution.py:246
  49.5 1.3 copy-done.2
  50.8 5.4 %forward.3 = (bf16[8192,128]{1,0:T(8,128)(2,1)S(1)}, f32[128,512]{1,0:T(8,128)S(1)}) custom-call(bf16[128,8192]{1,0:T(8,128)(2,1)} %copy-done.2, bf16[8192,512]{1,0:T(8,128)(2,1)} %weights_ref.3), custom_call_target="tpu_custom_call" | custom-call | flops 1073741824 | bytes 12582912 | tf_op jit(solution)/shard_map/forward/pallas_call | solution.py:32
  56.3 1.4 copy-done.1
  57.6 15.0 %inner.6 = (f32[4,2,512,128]{3,2,1,0:T(8,128)S(1)}, f32[4,2,512,128]{3,2,1,0:T(8,128)}) custom-call(s32[1]{0:T(128)} %bitcast.2.core_ref, bf16[128,8192]{1,0:T(8,128)(2,1)} %bitcast.177, bf16[128,8192]{1,0:T(8,128)(2,1)} %copy-done.2, bf16[4,2,2,512,128]{4,3,2,1,0:T(8,128)(2,1)} %bitcast.155, bf16[4,2,2,512,128]{4,3,2,1,0:T(8,128)(2,1)} %bitcast.159, ...), custom_call_target="tpu_custom_call" | custom-call | flops 1610612736 | bytes 29360128 | tf_op jit(solution)/shard_map/inner/pallas_call | solution.py:161
  72.8 15.0 %inner.7 = (f32[4,2,512,128]{3,2,1,0:T(8,128)S(1)}, f32[4,2,512,128]{3,2,1,0:T(8,128)}) custom-call(s32[1]{0:T(128)} %bitcast.2.core_ref, bf16[128,8192]{1,0:T(8,128)(2,1)} %bitcast.178, bf16[128,8192]{1,0:T(8,128)(2,1)} %copy-done.2, bf16[4,2,2,512,128]{4,3,2,1,0:T(8,128)(2,1)} %bitcast.156, bf16[4,2,2,512,128]{4,3,2,1,0:T(8,128)(2,1)} %bitcast.160, ...), custom_call_target="tpu_custom_call" | custom-call | flops 1610612736 | bytes 29360128 | tf_op jit(solution)/shard_map/inner/pallas_call | solution.py:161
  88.4 15.0 %inner.4 = (f32[4,2,512,128]{3,2,1,0:T(8,128)S(1)}, f32[4,2,512,128]{3,2,1,0:T(8,128)}) custom-call(s32[1]{0:T(128)} %bitcast.2.core_ref, bf16[128,8192]{1,0:T(8,128)(2,1)} %bitcast.179, bf16[128,8192]{1,0:T(8,128)(2,1)} %copy-done.2, bf16[4,2,2,512,128]{4,3,2,1,0:T(8,128)(2,1)} %bitcast.157, bf16[4,2,2,512,128]{4,3,2,1,0:T(8,128)(2,1)} %bitcast.161, ...), custom_call_target="tpu_custom_call" | custom-call | flops 1610612736 | bytes 29360128 | tf_op jit(solution)/shard_map/inner/pallas_call | solution.py:161
  103.7 14.9 %inner.5 = (f32[4,2,512,128]{3,2,1,0:T(8,128)S(1)}, f32[4,2,512,128]{3,2,1,0:T(8,128)}) custom-call(s32[1]{0:T(128)} %bitcast.2.core_ref, bf16[128,8192]{1,0:T(8,128)(2,1)} %bitcast.180, bf16[128,8192]{1,0:T(8,128)(2,1)} %copy-done.2, bf16[4,2,2,512,128]{4,3,2,1,0:T(8,128)(2,1)} %bitcast.158, bf16[4,2,2,512,128]{4,3,2,1,0:T(8,128)(2,1)} %bitcast.162, ...), custom_call_target="tpu_custom_call" | custom-call | flops 1610612736 | bytes 29360128 | tf_op jit(solution)/shard_map/inner/pallas_call | solution.py:161
  119.3 0.9 copy-done.6
  120.6 1.8 collective-permute-start.22
  122.8 1.2 collective-permute-start.32
  124.4 1.2 collective-permute-start.2
  125.9 1.2 collective-permute-start.12
  127.1 8.3 %collective-permute-done.22 = f16[4,512,128]{2,1,0:T(8,128)(2,1)S(1)} collective-permute-done((f16[4,512,128]{2,1,0:T(8,128)(2,1)S(1)}, f16[4,512,128]{2,1,0:T(8,128)(2,1)S(1)}, u32[]{:S(2)}, u32[]{:S(2)}) %collective-permute-start.22) | collective-permute-done | bytes 524320 | tf_op jit(solution)/shard_map/ppermute | solution.py:238
  135.6 1.9 collective-permute-start.23
  137.5 2.6 collective-permute-start.24
  140.1 6.6 %collective-permute-done.32 = f16[4,512,128]{2,1,0:T(8,128)(2,1)S(1)} collective-permute-done((f16[4,512,128]{2,1,0:T(8,128)(2,1)S(1)}, f16[4,512,128]{2,1,0:T(8,128)(2,1)S(1)}, u32[]{:S(2)}, u32[]{:S(2)}) %collective-permute-start.32) | collective-permute-done | bytes 524320 | tf_op jit(solution)/shard_map/ppermute | solution.py:238
  146.7 3.8 collective-permute-start.25
  150.7 7.2 %collective-permute-done.2 = f16[4,512,128]{2,1,0:T(8,128)(2,1)S(1)} collective-permute-done((f16[4,512,128]{2,1,0:T(8,128)(2,1)S(1)}, f16[4,512,128]{2,1,0:T(8,128)(2,1)S(1)}, u32[]{:S(2)}, u32[]{:S(2)}) %collective-permute-start.2) | collective-permute-done | bytes 524320 | tf_op jit(solution)/shard_map/ppermute | solution.py:238
  157.9 1.8 collective-permute-start.33
  159.7 2.6 collective-permute-start.34
  162.3 1.3 collective-permute-start.35
  163.8 0.8 fusion.16
  164.6 0.7 collective-permute-start.3
  165.2 1.0 collective-permute-done.33
  166.3 6.5 %collective-permute-start.4 = (f16[512,128]{1,0:T(8,128)(2,1)}, f16[512,128]{1,0:T(8,128)(2,1)}, u32[]{:S(2)}, u32[]{:S(2)}) collective-permute-start(f16[512,128]{1,0:T(8,128)(2,1)} %get-tuple-element.57), channel_id=1, source_target_pairs={{0,16},{2,18},{4,20},{6,22},{8,24},{10,26},{12,28},{14,30},{16,0},... | collective-permute-start | bytes 393224 | tf_op jit(solution)/shard_map/ppermute | solution.py:238
  172.8 1.7 collective-permute-done.34
  174.6 1.9 subtract_convert_fusion
  176.5 6.2 %collective-permute-start.36 = (bf16[512,128]{1,0:T(8,128)(2,1)S(1)}, bf16[512,128]{1,0:T(8,128)(2,1)S(1)}, u32[]{:S(2)}, u32[]{:S(2)}) collective-permute-start(bf16[512,128]{1,0:T(8,128)(2,1)S(1)} %get-tuple-element.26), channel_id=1, source_target_pairs={{0,8},{2,10},{4,12},{6,14},{8,16},{10,18},{12,20},{14,22},{16,24},... | collective-permute-start | bytes 393224 | tf_op jit(solution)/shard_map/ppermute | solution.py:238
  182.7 2.4 collective-permute-start.38
  185.2 0.8 fusion.19
  186.0 2.0 collective-permute-start.5
  188.0 1.0 collective-permute-start.13
  189.1 2.2 collective-permute-done.37
  191.3 1.6 collective-permute-start.14
  192.9 0.6 copy-done.14
  193.5 8.4 %collective-permute-start.15 = (f16[512,128]{1,0:T(8,128)(2,1)}, f16[512,128]{1,0:T(8,128)(2,1)}, u32[]{:S(2)}, u32[]{:S(2)}) collective-permute-start(f16[512,128]{1,0:T(8,128)(2,1)} %get-tuple-element.51), channel_id=1, source_target_pairs={{0,24},{2,26},{4,28},{6,30},{8,0},{10,2},{12,4},{14,6},{16,8},{18,... | collective-permute-start | bytes 393224 | tf_op jit(solution)/shard_map/ppermute | solution.py:238
  201.9 1.2 fusion.32
  203.7 1.5 collective-permute-start.27
  205.2 2.8 collective-permute-start.28
  208.1 1.5 collective-permute-start.39
  209.5 1.6 subtract_convert_fusion.2
  211.1 6.8 %collective-permute-start.16 = (bf16[512,128]{1,0:T(8,128)(2,1)S(1)}, bf16[512,128]{1,0:T(8,128)(2,1)S(1)}, u32[]{:S(2)}, u32[]{:S(2)}) collective-permute-start(bf16[512,128]{1,0:T(8,128)(2,1)S(1)} %get-tuple-element.30), channel_id=1, source_target_pairs={{0,8},{2,10},{4,12},{6,14},{8,16},{10,18},{12,20},{14,22},{16,24},... | collective-permute-start | bytes 393224 | tf_op jit(solution)/shard_map/ppermute | solution.py:238
  217.9 3.4 collective-permute-start.17
  221.3 1.9 collective-permute-start.18
  223.2 1.9 collective-permute-start.29
  225.2 3.2 collective-permute-start.6
  228.3 1.6 collective-permute-done.17
  229.9 0.7 collective-permute-start.7
  230.6 4.0 collective-permute-start.8
  234.7 1.9 collective-permute-start.19
  236.6 3.2 collective-permute-done.7
  239.8 1.2 collective-permute-done.8
  242.3 7.4 %collective-permute-done.19 = bf16[4,512,128]{2,1,0:T(8,128)(2,1)S(1)} collective-permute-done((bf16[4,512,128]{2,1,0:T(8,128)(2,1)S(1)}, bf16[4,512,128]{2,1,0:T(8,128)(2,1)S(1)}, u32[]{:S(2)}, u32[]{:S(2)}) %collective-permute-start.19) | collective-permute-done | bytes 524320 | tf_op jit(solution)/shard_map/ppermute | solution.py:238
  249.9 8.1 %collective-permute-done.9 = bf16[4,512,128]{2,1,0:T(8,128)(2,1)S(1)} collective-permute-done((bf16[4,512,128]{2,1,0:T(8,128)(2,1)S(1)}, bf16[4,512,128]{2,1,0:T(8,128)(2,1)S(1)}, u32[]{:S(2)}, u32[]{:S(2)}) %collective-permute-start.9) | collective-permute-done | bytes 524320 | tf_op jit(solution)/shard_map/ppermute | solution.py:238
  258.2 1.1 pad_maximum_fusion.8
  259.3 1.5 pad_maximum_fusion.3.refs_3_
  260.9 1.5 pad_maximum_fusion.2.refs_2_
  262.4 1.5 pad_maximum_fusion.1.refs_1_
  264.1 192.9 %assemble.1 = bf16[4,2,2,512,512]{4,3,2,1,0:T(8,128)(2,1)} custom-call(s32[3]{0:T(128)S(1)} %pad_add_fusion.place_ref, bf16[2,2,4,512,128]{4,3,2,1,0:T(8,128)(2,1)S(1)} %pad_maximum_fusion.refs_0_, bf16[2,2,4,512,128]{4,3,2,1,0:T(8,128)(2,1)} %pad_maximum_fusion.1.refs_1_, bf16[2,2,4,512,128]{4,3,2,1,0:T(8,128)(2,1)} %pad_maximum_fusion.2.refs_2_, ...), custom_call_target="tpu_custom_call" | custom-call | tf_op jit(solution)/shard_map/assemble/pallas_call | solution.py:333
  (100 shorter events, 7.1 us)
Async XLA Ops:
  0.6 48.9 %collective-permute-start = (bf16[128,8192]{1,0:T(8,128)(2,1)}, bf16[128,8192]{1,0:T(8,128)(2,1)S(1)}, u32[]{:S(2)}, u32[]{:S(2)}) collective-permute-start(bf16[128,8192]{1,0:T(8,128)(2,1)} %bitcast.175), channel_id=1, source_target_pairs={{0,1},{1,0},{2,3},{3,2},{4,5},{5,4},{6,7},{7,6},{8,9},{9,8},{10,11... | collective-permute-start | bytes 6291464 | tf_op jit(solution)/shard_map/ppermute | solution.py:246
  4.9 6.8 %copy-start.8 = (bf16[1,256,512]{2,1,0:T(8,128)(2,1)S(1)}, bf16[1,256,512]{2,1,0:T(8,128)(2,1)}, u32[]{:S(2)}) copy-start(bf16[1,256,512]{2,1,0:T(8,128)(2,1)} %param.12) | copy-start | bytes 786436
  10.4 1.3 copy-start
  49.5 1.3 copy-start.2
  56.2 1.4 copy-start.1
  72.7 46.6 %collective-permute-start.21 = (f16[4,2,512,128]{3,2,0,1:T(8,128)(2,1)S(1)}, f16[4,2,512,128]{3,2,0,1:T(8,128)(2,1)S(1)}, u32[]{:S(2)}, u32[]{:S(2)}) collective-permute-start(f16[4,2,512,128]{3,2,0,1:T(8,128)(2,1)S(1)} %copy_convert_fusion.1), channel_id=1, source_target_pairs={{0,2},{2,0},{4,6},{6,4},{8,10},{10,8},{12,14},{14,12},{16,18},{18,... | collective-permute-start | bytes 3145736 | tf_op jit(solution)/shard_map/ppermute | solution.py:238
  87.9 34.5 %collective-permute-start.31 = (f16[4,2,512,128]{3,2,0,1:T(8,128)(2,1)S(1)}, f16[4,2,512,128]{3,2,0,1:T(8,128)(2,1)S(1)}, u32[]{:S(2)}, u32[]{:S(2)}) collective-permute-start(f16[4,2,512,128]{3,2,0,1:T(8,128)(2,1)S(1)} %copy_convert_fusion), channel_id=1, source_target_pairs={{0,2},{2,0},{4,6},{6,4},{8,10},{10,8},{12,14},{14,12},{16,18},{18,... | collective-permute-start | bytes 3145736 | tf_op jit(solution)/shard_map/ppermute | solution.py:238
  103.6 20.4 %collective-permute-start.1 = (f16[4,2,512,128]{3,2,0,1:T(8,128)(2,1)S(1)}, f16[4,2,512,128]{3,2,0,1:T(8,128)(2,1)S(1)}, u32[]{:S(2)}, u32[]{:S(2)}) collective-permute-start(f16[4,2,512,128]{3,2,0,1:T(8,128)(2,1)S(1)} %copy_convert_fusion.3), channel_id=1, source_target_pairs={{0,2},{2,0},{4,6},{6,4},{8,10},{10,8},{12,14},{14,12},{16,18},{18,... | collective-permute-start | bytes 3145736 | tf_op jit(solution)/shard_map/ppermute | solution.py:238
  118.7 1.6 copy-start.6
  118.8 6.8 %collective-permute-start.11 = (f16[4,2,512,128]{3,2,0,1:T(8,128)(2,1)S(1)}, f16[4,2,512,128]{3,2,0,1:T(8,128)(2,1)S(1)}, u32[]{:S(2)}, u32[]{:S(2)}) collective-permute-start(f16[4,2,512,128]{3,2,0,1:T(8,128)(2,1)S(1)} %copy_convert_fusion.2), channel_id=1, source_target_pairs={{0,2},{2,0},{4,6},{6,4},{8,10},{10,8},{12,14},{14,12},{16,18},{18,... | collective-permute-start | bytes 3145736 | tf_op jit(solution)/shard_map/ppermute | solution.py:238
  120.2 2.2 copy-start.5
  120.6 14.8 %collective-permute-start.22 = (f16[4,512,128]{2,1,0:T(8,128)(2,1)S(1)}, f16[4,512,128]{2,1,0:T(8,128)(2,1)S(1)}, u32[]{:S(2)}, u32[]{:S(2)}) collective-permute-start(f16[4,512,128]{2,1,0:T(8,128)(2,1)S(1)} %fusion.2), channel_id=1, source_target_pairs={{0,4},{2,6},{4,0},{6,2},{8,12},{10,14},{12,8},{14,10},{16,20},{18,... | collective-permute-start | bytes 1572872 | tf_op jit(solution)/shard_map/ppermute | solution.py:238
  122.4 1.6 copy-start.4
  122.8 23.8 %collective-permute-start.32 = (f16[4,512,128]{2,1,0:T(8,128)(2,1)S(1)}, f16[4,512,128]{2,1,0:T(8,128)(2,1)S(1)}, u32[]{:S(2)}, u32[]{:S(2)}) collective-permute-start(f16[4,512,128]{2,1,0:T(8,128)(2,1)S(1)} %fusion.3), channel_id=1, source_target_pairs={{0,4},{2,6},{4,0},{6,2},{8,12},{10,14},{12,8},{14,10},{16,20},{18,... | collective-permute-start | bytes 1572872 | tf_op jit(solution)/shard_map/ppermute | solution.py:238
  124.0 1.6 copy-start.3
  124.4 33.5 %collective-permute-start.2 = (f16[4,512,128]{2,1,0:T(8,128)(2,1)S(1)}, f16[4,512,128]{2,1,0:T(8,128)(2,1)S(1)}, u32[]{:S(2)}, u32[]{:S(2)}) collective-permute-start(f16[4,512,128]{2,1,0:T(8,128)(2,1)S(1)} %fusion), channel_id=1, source_target_pairs={{0,4},{2,6},{4,0},{6,2},{8,12},{10,14},{12,8},{14,10},{16,20},{18,... | collective-permute-start | bytes 1572872 | tf_op jit(solution)/shard_map/ppermute | solution.py:238
  125.9 56.8 %collective-permute-start.12 = (f16[4,512,128]{2,1,0:T(8,128)(2,1)S(1)}, f16[4,512,128]{2,1,0:T(8,128)(2,1)S(1)}, u32[]{:S(2)}, u32[]{:S(2)}) collective-permute-start(f16[4,512,128]{2,1,0:T(8,128)(2,1)S(1)} %fusion.1), channel_id=1, source_target_pairs={{0,4},{2,6},{4,0},{6,2},{8,12},{10,14},{12,8},{14,10},{16,20},{18,... | collective-permute-start | bytes 1572872 | tf_op jit(solution)/shard_map/ppermute | solution.py:238
  135.6 24.1 %collective-permute-start.23 = (f16[512,128]{1,0:T(8,128)(2,1)S(1)}, f16[512,128]{1,0:T(8,128)(2,1)S(1)}, u32[]{:S(2)}, u32[]{:S(2)}) collective-permute-start(f16[512,128]{1,0:T(8,128)(2,1)S(1)} %get-tuple-element.45), channel_id=1, source_target_pairs={{0,8},{2,10},{4,12},{6,14},{8,16},{10,18},{12,20},{14,22},{16,24},... | collective-permute-start | bytes 393224 | tf_op jit(solution)/shard_map/ppermute | solution.py:238
  137.5 24.8 %collective-permute-start.24 = (f16[512,128]{1,0:T(8,128)(2,1)S(1)}, f16[512,128]{1,0:T(8,128)(2,1)S(1)}, u32[]{:S(2)}, u32[]{:S(2)}) collective-permute-start(f16[512,128]{1,0:T(8,128)(2,1)S(1)} %get-tuple-element.47), channel_id=1, source_target_pairs={{0,16},{2,18},{4,20},{6,22},{8,24},{10,26},{12,28},{14,30},{16,0},... | collective-permute-start | bytes 393224 | tf_op jit(solution)/shard_map/ppermute | solution.py:238
  146.7 17.9 %collective-permute-start.25 = (f16[512,128]{1,0:T(8,128)(2,1)S(1)}, f16[512,128]{1,0:T(8,128)(2,1)S(1)}, u32[]{:S(2)}, u32[]{:S(2)}) collective-permute-start(f16[512,128]{1,0:T(8,128)(2,1)S(1)} %get-tuple-element.46), channel_id=1, source_target_pairs={{0,24},{2,26},{4,28},{6,30},{8,0},{10,2},{12,4},{14,6},{16,8},{18,... | collective-permute-start | bytes 393224 | tf_op jit(solution)/shard_map/ppermute | solution.py:238
  150.7 23.9 %copy-start.7 = (f32[512,512]{1,0:T(8,128)S(1)}, f32[512,512]{1,0:T(8,128)}, u32[]{:S(2)}) copy-start(f32[512,512]{1,0:T(8,128)} %param.8) | copy-start | bytes 3145732
  157.9 8.4 %collective-permute-start.33 = (f16[512,128]{1,0:T(8,128)(2,1)S(1)}, f16[512,128]{1,0:T(8,128)(2,1)S(1)}, u32[]{:S(2)}, u32[]{:S(2)}) collective-permute-start(f16[512,128]{1,0:T(8,128)(2,1)S(1)} %get-tuple-element.40), channel_id=1, source_target_pairs={{0,8},{2,10},{4,12},{6,14},{8,16},{10,18},{12,20},{14,22},{16,24},... | collective-permute-start | bytes 393224 | tf_op jit(solution)/shard_map/ppermute | solution.py:238
  159.7 14.8 %collective-permute-start.34 = (f16[512,128]{1,0:T(8,128)(2,1)S(1)}, f16[512,128]{1,0:T(8,128)(2,1)S(1)}, u32[]{:S(2)}, u32[]{:S(2)}) collective-permute-start(f16[512,128]{1,0:T(8,128)(2,1)S(1)} %get-tuple-element.42), channel_id=1, source_target_pairs={{0,16},{2,18},{4,20},{6,22},{8,24},{10,26},{12,28},{14,30},{16,0},... | collective-permute-start | bytes 393224 | tf_op jit(solution)/shard_map/ppermute | solution.py:238
  162.3 12.2 %collective-permute-start.35 = (f16[512,128]{1,0:T(8,128)(2,1)S(1)}, f16[512,128]{1,0:T(8,128)(2,1)S(1)}, u32[]{:S(2)}, u32[]{:S(2)}) collective-permute-start(f16[512,128]{1,0:T(8,128)(2,1)S(1)} %get-tuple-element.41), channel_id=1, source_target_pairs={{0,24},{2,26},{4,28},{6,30},{8,0},{10,2},{12,4},{14,6},{16,8},{18,... | collective-permute-start | bytes 393224 | tf_op jit(solution)/shard_map/ppermute | solution.py:238
  164.6 21.4 %collective-permute-start.3 = (f16[512,128]{1,0:T(8,128)(2,1)S(1)}, f16[512,128]{1,0:T(8,128)(2,1)S(1)}, u32[]{:S(2)}, u32[]{:S(2)}) collective-permute-start(f16[512,128]{1,0:T(8,128)(2,1)S(1)} %get-tuple-element.55), channel_id=1, source_target_pairs={{0,8},{2,10},{4,12},{6,14},{8,16},{10,18},{12,20},{14,22},{16,24},... | collective-permute-start | bytes 393224 | tf_op jit(solution)/shard_map/ppermute | solution.py:238
  166.3 36.8 %collective-permute-start.4 = (f16[512,128]{1,0:T(8,128)(2,1)}, f16[512,128]{1,0:T(8,128)(2,1)}, u32[]{:S(2)}, u32[]{:S(2)}) collective-permute-start(f16[512,128]{1,0:T(8,128)(2,1)} %get-tuple-element.57), channel_id=1, source_target_pairs={{0,16},{2,18},{4,20},{6,22},{8,24},{10,26},{12,28},{14,30},{16,0},... | collective-permute-start | bytes 393224 | tf_op jit(solution)/shard_map/ppermute | solution.py:238
  176.5 8.7 %copy-start.10 = (bf16[512,128]{1,0:T(8,128)(2,1)}, bf16[512,128]{1,0:T(8,128)(2,1)S(1)}, u32[]{:S(2)}) copy-start(bf16[512,128]{1,0:T(8,128)(2,1)S(1)} %get-tuple-element.26) | copy-start | bytes 393220
  176.5 11.5 %collective-permute-start.36 = (bf16[512,128]{1,0:T(8,128)(2,1)S(1)}, bf16[512,128]{1,0:T(8,128)(2,1)S(1)}, u32[]{:S(2)}, u32[]{:S(2)}) collective-permute-start(bf16[512,128]{1,0:T(8,128)(2,1)S(1)} %get-tuple-element.26), channel_id=1, source_target_pairs={{0,8},{2,10},{4,12},{6,14},{8,16},{10,18},{12,20},{14,22},{16,24},... | collective-permute-start | bytes 393224 | tf_op jit(solution)/shard_map/ppermute | solution.py:238
  182.7 8.6 %collective-permute-start.37 = (bf16[512,128]{1,0:T(8,128)(2,1)S(1)}, bf16[512,128]{1,0:T(8,128)(2,1)S(1)}, u32[]{:S(2)}, u32[]{:S(2)}) collective-permute-start(bf16[512,128]{1,0:T(8,128)(2,1)S(1)} %get-tuple-element.26), channel_id=1, source_target_pairs={{0,16},{2,18},{4,20},{6,22},{8,24},{10,26},{12,28},{14,30},{16,0},... | collective-permute-start | bytes 393224 | tf_op jit(solution)/shard_map/ppermute | solution.py:238
  182.7 10.2 %collective-permute-start.38 = (bf16[512,128]{1,0:T(8,128)(2,1)S(1)}, bf16[512,128]{1,0:T(8,128)(2,1)S(1)}, u32[]{:S(2)}, u32[]{:S(2)}) collective-permute-start(bf16[512,128]{1,0:T(8,128)(2,1)S(1)} %get-tuple-element.26), channel_id=1, source_target_pairs={{0,24},{2,26},{4,28},{6,30},{8,0},{10,2},{12,4},{14,6},{16,8},{18,... | collective-permute-start | bytes 393224 | tf_op jit(solution)/shard_map/ppermute | solution.py:238
  186.0 6.9 %copy-start.11 = (f16[512,128]{1,0:T(8,128)(2,1)}, f16[512,128]{1,0:T(8,128)(2,1)S(1)}, u32[]{:S(2)}) copy-start(f16[512,128]{1,0:T(8,128)(2,1)S(1)} %collective-permute-done.3) | copy-start | bytes 393220
  186.0 17.7 %collective-permute-start.5 = (f16[512,128]{1,0:T(8,128)(2,1)}, f16[512,128]{1,0:T(8,128)(2,1)}, u32[]{:S(2)}, u32[]{:S(2)}) collective-permute-start(f16[512,128]{1,0:T(8,128)(2,1)} %get-tuple-element.56), channel_id=1, source_target_pairs={{0,24},{2,26},{4,28},{6,30},{8,0},{10,2},{12,4},{14,6},{16,8},{18,... | collective-permute-start | bytes 393224 | tf_op jit(solution)/shard_map/ppermute | solution.py:238
  188.0 4.9 %copy-start.12 = (bf16[512,128]{1,0:T(8,128)(2,1)}, bf16[512,128]{1,0:T(8,128)(2,1)S(1)}, u32[]{:S(2)}) copy-start(bf16[512,128]{1,0:T(8,128)(2,1)S(1)} %collective-permute-done.36) | copy-start | bytes 393220
  188.0 17.2 %collective-permute-start.13 = (f16[512,128]{1,0:T(8,128)(2,1)}, f16[512,128]{1,0:T(8,128)(2,1)}, u32[]{:S(2)}, u32[]{:S(2)}) collective-permute-start(f16[512,128]{1,0:T(8,128)(2,1)} %get-tuple-element.50), channel_id=1, source_target_pairs={{0,8},{2,10},{4,12},{6,14},{8,16},{10,18},{12,20},{14,22},{16,24},... | collective-permute-start | bytes 393224 | tf_op jit(solution)/shard_map/ppermute | solution.py:238
  191.3 1.6 copy-start.13
  191.3 16.8 %collective-permute-start.14 = (f16[512,128]{1,0:T(8,128)(2,1)}, f16[512,128]{1,0:T(8,128)(2,1)}, u32[]{:S(2)}, u32[]{:S(2)}) collective-permute-start(f16[512,128]{1,0:T(8,128)(2,1)} %get-tuple-element.52), channel_id=1, source_target_pairs={{0,16},{2,18},{4,20},{6,22},{8,24},{10,26},{12,28},{14,30},{16,0},... | collective-permute-start | bytes 393224 | tf_op jit(solution)/shard_map/ppermute | solution.py:238
  192.9 0.7 copy-start.14
  193.5 16.0 %collective-permute-start.15 = (f16[512,128]{1,0:T(8,128)(2,1)}, f16[512,128]{1,0:T(8,128)(2,1)}, u32[]{:S(2)}, u32[]{:S(2)}) collective-permute-start(f16[512,128]{1,0:T(8,128)(2,1)} %get-tuple-element.51), channel_id=1, source_target_pairs={{0,24},{2,26},{4,28},{6,30},{8,0},{10,2},{12,4},{14,6},{16,8},{18,... | collective-permute-start | bytes 393224 | tf_op jit(solution)/shard_map/ppermute | solution.py:238
  203.1 14.8 %collective-permute-start.26 = (bf16[512,128]{1,0:T(8,128)(2,1)S(1)}, bf16[512,128]{1,0:T(8,128)(2,1)S(1)}, u32[]{:S(2)}, u32[]{:S(2)}) collective-permute-start(bf16[512,128]{1,0:T(8,128)(2,1)S(1)} %get-tuple-element.34), channel_id=1, source_target_pairs={{0,8},{2,10},{4,12},{6,14},{8,16},{10,18},{12,20},{14,22},{16,24},... | collective-permute-start | bytes 393224 | tf_op jit(solution)/shard_map/ppermute | solution.py:238
  203.7 17.6 %collective-permute-start.27 = (bf16[512,128]{1,0:T(8,128)(2,1)S(1)}, bf16[512,128]{1,0:T(8,128)(2,1)S(1)}, u32[]{:S(2)}, u32[]{:S(2)}) collective-permute-start(bf16[512,128]{1,0:T(8,128)(2,1)S(1)} %get-tuple-element.34), channel_id=1, source_target_pairs={{0,16},{2,18},{4,20},{6,22},{8,24},{10,26},{12,28},{14,30},{16,0},... | collective-permute-start | bytes 393224 | tf_op jit(solution)/shard_map/ppermute | solution.py:238
  205.2 17.9 %collective-permute-start.28 = (bf16[512,128]{1,0:T(8,128)(2,1)S(1)}, bf16[512,128]{1,0:T(8,128)(2,1)S(1)}, u32[]{:S(2)}, u32[]{:S(2)}) collective-permute-start(bf16[512,128]{1,0:T(8,128)(2,1)S(1)} %get-tuple-element.34), channel_id=1, source_target_pairs={{0,24},{2,26},{4,28},{6,30},{8,0},{10,2},{12,4},{14,6},{16,8},{18,... | collective-permute-start | bytes 393224 | tf_op jit(solution)/shard_map/ppermute | solution.py:238
  208.1 33.3 %collective-permute-start.39 = (bf16[4,512,128]{2,1,0:T(8,128)(2,1)S(1)}, bf16[4,512,128]{2,1,0:T(8,128)(2,1)S(1)}, u32[]{:S(2)}, u32[]{:S(2)}) collective-permute-start(bf16[4,512,128]{2,1,0:T(8,128)(2,1)S(1)} %get-tuple-element.59), channel_id=1, source_target_pairs={{0,4},{2,6},{4,0},{6,2},{8,12},{10,14},{12,8},{14,10},{16,20},{18,... | collective-permute-start | bytes 1572872 | tf_op jit(solution)/shard_map/ppermute | solution.py:238
  211.1 14.1 %collective-permute-start.16 = (bf16[512,128]{1,0:T(8,128)(2,1)S(1)}, bf16[512,128]{1,0:T(8,128)(2,1)S(1)}, u32[]{:S(2)}, u32[]{:S(2)}) collective-permute-start(bf16[512,128]{1,0:T(8,128)(2,1)S(1)} %get-tuple-element.30), channel_id=1, source_target_pairs={{0,8},{2,10},{4,12},{6,14},{8,16},{10,18},{12,20},{14,22},{16,24},... | collective-permute-start | bytes 393224 | tf_op jit(solution)/shard_map/ppermute | solution.py:238
  217.9 12.1 %collective-permute-start.17 = (bf16[512,128]{1,0:T(8,128)(2,1)S(1)}, bf16[512,128]{1,0:T(8,128)(2,1)S(1)}, u32[]{:S(2)}, u32[]{:S(2)}) collective-permute-start(bf16[512,128]{1,0:T(8,128)(2,1)S(1)} %get-tuple-element.30), channel_id=1, source_target_pairs={{0,16},{2,18},{4,20},{6,22},{8,24},{10,26},{12,28},{14,30},{16,0},... | collective-permute-start | bytes 393224 | tf_op jit(solution)/shard_map/ppermute | solution.py:238
  221.3 9.4 %collective-permute-start.18 = (bf16[512,128]{1,0:T(8,128)(2,1)S(1)}, bf16[512,128]{1,0:T(8,128)(2,1)S(1)}, u32[]{:S(2)}, u32[]{:S(2)}) collective-permute-start(bf16[512,128]{1,0:T(8,128)(2,1)S(1)} %get-tuple-element.30), channel_id=1, source_target_pairs={{0,24},{2,26},{4,28},{6,30},{8,0},{10,2},{12,4},{14,6},{16,8},{18,... | collective-permute-start | bytes 393224 | tf_op jit(solution)/shard_map/ppermute | solution.py:238
  223.2 18.4 %collective-permute-start.29 = (bf16[4,512,128]{2,1,0:T(8,128)(2,1)S(1)}, bf16[4,512,128]{2,1,0:T(8,128)(2,1)S(1)}, u32[]{:S(2)}, u32[]{:S(2)}) collective-permute-start(bf16[4,512,128]{2,1,0:T(8,128)(2,1)S(1)} %get-tuple-element.61), channel_id=1, source_target_pairs={{0,4},{2,6},{4,0},{6,2},{8,12},{10,14},{12,8},{14,10},{16,20},{18,... | collective-permute-start | bytes 1572872 | tf_op jit(solution)/shard_map/ppermute | solution.py:238
  225.2 9.6 %collective-permute-start.6 = (bf16[512,128]{1,0:T(8,128)(2,1)S(1)}, bf16[512,128]{1,0:T(8,128)(2,1)S(1)}, u32[]{:S(2)}, u32[]{:S(2)}) collective-permute-start(bf16[512,128]{1,0:T(8,128)(2,1)S(1)} %get-tuple-element.36), channel_id=1, source_target_pairs={{0,8},{2,10},{4,12},{6,14},{8,16},{10,18},{12,20},{14,22},{16,24},... | collective-permute-start | bytes 393224 | tf_op jit(solution)/shard_map/ppermute | solution.py:238
  229.9 9.9 %collective-permute-start.7 = (bf16[512,128]{1,0:T(8,128)(2,1)S(1)}, bf16[512,128]{1,0:T(8,128)(2,1)S(1)}, u32[]{:S(2)}, u32[]{:S(2)}) collective-permute-start(bf16[512,128]{1,0:T(8,128)(2,1)S(1)} %get-tuple-element.36), channel_id=1, source_target_pairs={{0,16},{2,18},{4,20},{6,22},{8,24},{10,26},{12,28},{14,30},{16,0},... | collective-permute-start | bytes 393224 | tf_op jit(solution)/shard_map/ppermute | solution.py:238
  230.6 10.4 %collective-permute-start.8 = (bf16[512,128]{1,0:T(8,128)(2,1)S(1)}, bf16[512,128]{1,0:T(8,128)(2,1)S(1)}, u32[]{:S(2)}, u32[]{:S(2)}) collective-permute-start(bf16[512,128]{1,0:T(8,128)(2,1)S(1)} %get-tuple-element.36), channel_id=1, source_target_pairs={{0,24},{2,26},{4,28},{6,30},{8,0},{10,2},{12,4},{14,6},{16,8},{18,... | collective-permute-start | bytes 393224 | tf_op jit(solution)/shard_map/ppermute | solution.py:238
  234.7 14.9 %collective-permute-start.19 = (bf16[4,512,128]{2,1,0:T(8,128)(2,1)S(1)}, bf16[4,512,128]{2,1,0:T(8,128)(2,1)S(1)}, u32[]{:S(2)}, u32[]{:S(2)}) collective-permute-start(bf16[4,512,128]{2,1,0:T(8,128)(2,1)S(1)} %get-tuple-element.63), channel_id=1, source_target_pairs={{0,4},{2,6},{4,0},{6,2},{8,12},{10,14},{12,8},{14,10},{16,20},{18,... | collective-permute-start | bytes 1572872 | tf_op jit(solution)/shard_map/ppermute | solution.py:238
  241.1 16.8 %collective-permute-start.9 = (bf16[4,512,128]{2,1,0:T(8,128)(2,1)S(1)}, bf16[4,512,128]{2,1,0:T(8,128)(2,1)S(1)}, u32[]{:S(2)}, u32[]{:S(2)}) collective-permute-start(bf16[4,512,128]{2,1,0:T(8,128)(2,1)S(1)} %get-tuple-element.65), channel_id=1, source_target_pairs={{0,4},{2,6},{4,0},{6,2},{8,12},{10,14},{12,8},{14,10},{16,20},{18,... | collective-permute-start | bytes 1572872 | tf_op jit(solution)/shard_map/ppermute | solution.py:238
  241.5 17.8 %collective-permute-start.40 = (bf16[2,4,512,128]{3,2,1,0:T(8,128)(2,1)S(1)}, bf16[2,4,512,128]{3,2,1,0:T(8,128)(2,1)S(1)}, u32[]{:S(2)}, u32[]{:S(2)}) collective-permute-start(bf16[2,4,512,128]{3,2,1,0:T(8,128)(2,1)S(1)} %get-tuple-element.39), channel_id=1, source_target_pairs={{0,2},{2,0},{4,6},{6,4},{8,10},{10,8},{12,14},{14,12},{16,18},{18,... | collective-permute-start | bytes 3145736 | tf_op jit(solution)/shard_map/ppermute | solution.py:238
  241.7 19.1 %collective-permute-start.30 = (bf16[2,4,512,128]{3,2,1,0:T(8,128)(2,1)S(1)}, bf16[2,4,512,128]{3,2,1,0:T(8,128)(2,1)S(1)}, u32[]{:S(2)}, u32[]{:S(2)}) collective-permute-start(bf16[2,4,512,128]{3,2,1,0:T(8,128)(2,1)S(1)} %get-tuple-element.44), channel_id=1, source_target_pairs={{0,2},{2,0},{4,6},{6,4},{8,10},{10,8},{12,14},{14,12},{16,18},{18,... | collective-permute-start | bytes 3145736 | tf_op jit(solution)/shard_map/ppermute | solution.py:238
  249.8 8.5 %copy-start.9 = (f32[512,128]{1,0:T(8,128)S(1)}, f32[512,128]{1,0:T(8,128)}, u32[]{:S(2)}) copy-start(f32[512,128]{1,0:T(8,128)} %get-tuple-element.35) | copy-start | bytes 786436
  249.8 12.6 %collective-permute-start.20 = (bf16[2,4,512,128]{3,2,1,0:T(8,128)(2,1)S(1)}, bf16[2,4,512,128]{3,2,1,0:T(8,128)(2,1)S(1)}, u32[]{:S(2)}, u32[]{:S(2)}) collective-permute-start(bf16[2,4,512,128]{3,2,1,0:T(8,128)(2,1)S(1)} %get-tuple-element.49), channel_id=1, source_target_pairs={{0,2},{2,0},{4,6},{6,4},{8,10},{10,8},{12,14},{14,12},{16,18},{18,... | collective-permute-start | bytes 3145736 | tf_op jit(solution)/shard_map/ppermute | solution.py:238
  258.1 5.8 %collective-permute-start.10 = (bf16[2,4,512,128]{3,2,1,0:T(8,128)(2,1)S(1)}, bf16[2,4,512,128]{3,2,1,0:T(8,128)(2,1)S(1)}, u32[]{:S(2)}, u32[]{:S(2)}) collective-permute-start(bf16[2,4,512,128]{3,2,1,0:T(8,128)(2,1)S(1)} %get-tuple-element.54), channel_id=1, source_target_pairs={{0,2},{2,0},{4,6},{6,4},{8,10},{10,8},{12,14},{14,12},{16,18},{18,... | collective-permute-start | bytes 3145736 | tf_op jit(solution)/shard_map/ppermute | solution.py:238

commit v2 on v1

v2 whole, which is shorter than its diff:
```python
import functools
import math
import jax
import jax.numpy as jnp
from jax import lax
from jax.experimental import pallas as pl
from jax.experimental.pallas import tpu as pltpu
from jax.sharding import PartitionSpec as P

F32 = jnp.float32
BF16 = jnp.bfloat16
WIRE = jnp.float16
WIRE_SCALE = 64.0
LANES = 128
SLABS = 4
PIECE = 64
MIB = 1024 * 1024


def forward_kernel(part_ref, weights_ref, turned_ref, product_ref):
    @pl.when(pl.program_id(0) == 0)
    def _():
        product_ref[...] = jnp.zeros_like(product_ref)

    part = part_ref[...]
    turned_ref[...] = part.T
    product_ref[...] += jnp.dot(part, weights_ref[...], preferred_element_type=F32)


def forward(part, weights):
    rows, depth = part.shape
    columns = weights.shape[1]
    block = depth // SLABS
    return pl.pallas_call(
        forward_kernel,
        grid=(SLABS,),
        in_specs=[
            pl.BlockSpec((rows, block), lambda d: (0, d)),
            pl.BlockSpec((block, columns), lambda d: (d, 0)),
        ],
        out_specs=[
            pl.BlockSpec((block, rows), lambda d: (d, 0)),
            pl.BlockSpec((rows, columns), lambda d: (0, 0)),
        ],
        out_shape=[
            jax.ShapeDtypeStruct((depth, rows), BF16),
            jax.ShapeDtypeStruct((rows, columns), F32),
        ],
        compiler_params=pltpu.CompilerParams(vmem_limit_bytes=24 * MIB),
        cost_estimate=pl.CostEstimate(
            flops=2 * rows * depth * columns,
            bytes_accessed=2 * depth * columns + 4 * rows * depth,
            transcendentals=0,
        ),
        name="forward",
    )(part, weights)


def arrive_kernel(part_ref, weights_ref, *refs):
    natural_ref, turned_ref, product_ref = refs[-3:]
    part = part_ref[...]
    natural_ref[...] = part
    turned_ref[...] = part.T
    product = jnp.dot(part, weights_ref[...], preferred_element_type=F32)
    if len(refs) > 3:
        product = product + refs[2][...]
    product_ref[...] = product


def arrive(piece, part, weights, before):
    rows, block = part.shape
    depth, columns = weights.shape
    whole = pl.BlockSpec((rows, columns), lambda d: (0, 0))
    return pl.pallas_call(
        arrive_kernel,
        grid=(1,),
        in_specs=[
            pl.BlockSpec((rows, block), lambda d: (0, 0)),
            pl.BlockSpec((block, columns), lambda d: (piece, 0)),
        ]
        + ([pl.BlockSpec(memory_space=pl.ANY)] * 2 + [whole] if before else []),
        out_specs=[
            pl.BlockSpec((rows, block), lambda d: (0, piece)),
            pl.BlockSpec((block, rows), lambda d: (piece, 0)),
            whole,
        ],
        out_shape=[
            jax.ShapeDtypeStruct((rows, depth), BF16),
            jax.ShapeDtypeStruct((depth, rows), BF16),
            jax.ShapeDtypeStruct((rows, columns), F32),
        ],
        input_output_aliases={2: 0, 3: 1} if before else {},
        compiler_params=pltpu.CompilerParams(vmem_limit_bytes=24 * MIB),
        cost_estimate=pl.CostEstimate(
            flops=2 * rows * block * columns,
            bytes_accessed=2 * block * columns + 6 * rows * block,
            transcendentals=0,
        ),
        name="arrive",
    )(part, weights, *before)


def inner_kernel(
    tokens,
    core_ref,
    low_ref,
    high_ref,
    low_turned_ref,
    high_turned_ref,
    start_ref,
    first_ref,
    second_ref,
    low_product_ref,
    high_product_ref,
    target_ref,
    count_ref,
    send_ref,
    keep_ref,
    first_state,
    second_state,
    weights_state,
    output_state,
    residual_state,
    gradient_state,
    rounded_state,
):
    step = pl.program_id(0)
    slab = pl.program_id(1)
    pairs, cores, rows, _ = start_ref.shape
    core = core_ref[0]
    pieces = [pl.ds(begin, PIECE) for begin in range(0, rows, PIECE)]

    def weigh(output, which):
        residual = ((output - target_ref[...].astype(F32)) / tokens).astype(BF16)
        residual_state[...] = (residual.astype(F32) * count_ref[which]).astype(BF16)

    def descend(first, second, weights):
        root = second * lax.rsqrt(second)
        below = (100.0 * math.sqrt(0.05)) * root + 1e-06
        return 0.99 * weights - first * lax.rsqrt(below * below)

    def gradient_of(pair, which, slot):
        turned = jnp.concatenate(
            [low_turned_ref[pair, which], high_turned_ref[pair, which]], axis=1
        )
        gradient_state[slot] = jnp.dot(
            turned, residual_state[...], preferred_element_type=F32
        )

    @pl.when((step == 0) & (slab == 0))
    def _():
        weigh(jnp.concatenate([low_product_ref[...], high_product_ref[...]], axis=0), 0)
        output_state[...] = jnp.zeros_like(output_state)

    @pl.when((step == 1) & (slab == 0))
    def _():
        weigh(output_state[...], 1)

    @pl.when(step == 0)
    def _():
        total = jnp.zeros(output_state.shape, F32)
        for pair in range(pairs):
            for which in range(cores):
                slot = pair * cores + which
                gradient_of(pair, which, slot)
                for piece in pieces:
                    gradient = gradient_state[slot, piece]
                    first = 9.0 * first_ref[pair, which, piece] + gradient
                    second = 19.0 * second_ref[pair, which, piece] + gradient * gradient
                    weights = descend(first, second, start_ref[pair, which, piece].astype(F32))
                    first_state[slab, pair, which, piece] = first
                    second_state[slab, pair, which, piece] = second
                    weights_state[slab, pair, which, piece] = weights
                    rounded_state[slot, piece] = weights.astype(BF16)
                place = pl.ds(slot * rows, rows)
                picked = jnp.concatenate([low_ref[:, place], high_ref[:, place]], axis=0)
                total += jnp.dot(picked, rounded_state[slot], preferred_element_type=F32)
        output_state[...] += total

    @pl.when(step == 1)
    def _():
        for pair in range(pairs):
            for slot, which, out_ref in ((0, 1 - core, send_ref), (1, core, keep_ref)):
                slot = pair * cores + slot
                gradient_of(pair, which, slot)
                for piece in pieces:
                    gradient = gradient_state[slot, piece]
                    first = 0.9 * first_state[slab, pair, which, piece] + gradient
                    second = 0.95 * second_state[slab, pair, which, piece] + gradient * gradient
                    weights = descend(first, second, weights_state[slab, pair, which, piece])
                    change = start_ref[pair, which, piece].astype(F32) - weights
                    out_ref[pair, piece] = change * WIRE_SCALE


def inner(chunk, width, core, banks, turned, start, first, second, products, target, count, tokens):
    slabs, pairs, cores, rows, _ = start.shape
    half, depth = banks[0].shape
    block = depth // slabs

    def held(step, slab):
        return jnp.where(step == 0, slab, slabs - 1)

    def drawn(step, slab):
        return jnp.where(step == 0, 0, slab)

    natural = pl.BlockSpec((half, block), lambda s, z, c: (0, held(s, z)))
    flipped = pl.BlockSpec((None, pairs, cores, rows, half), lambda s, z, c: (z, 0, 0, 0, 0))
    tile = (None, pairs, cores, rows, width)
    state = pl.BlockSpec(tile, lambda s, z, c: (held(s, z), 0, 0, 0, chunk))
    product = pl.BlockSpec((half, width), lambda s, z, c: (0, chunk))
    change = pl.BlockSpec((None, pairs, rows, width), lambda s, z, c: (drawn(s, z), 0, 0, 0))
    elements = depth * width
    return pl.pallas_call(
        functools.partial(inner_kernel, float(tokens)),
        grid_spec=pltpu.PrefetchScalarGridSpec(
            num_scalar_prefetch=1,
            grid=(2, slabs),
            in_specs=[
                natural,
                natural,
                flipped,
                flipped,
                pl.BlockSpec(tile, lambda s, z, c: (z, 0, 0, 0, chunk)),
                state,
                state,
                product,
                product,
                pl.BlockSpec((2 * half, width), lambda s, z, c: (0, chunk)),
                pl.BlockSpec(count.shape, lambda s, z, c: (0, 0, 0)),
            ],
            out_specs=[change, change],
            scratch_shapes=[
                pltpu.VMEM((slabs, pairs, cores, rows, width), F32),
                pltpu.VMEM((slabs, pairs, cores, rows, width), F32),
                pltpu.VMEM((slabs, pairs, cores, rows, width), F32),
                pltpu.VMEM((2 * half, width), F32),
                pltpu.VMEM((2 * half, width), BF16),
                pltpu.VMEM((pairs * cores, rows, width), F32),
                pltpu.VMEM((pairs * cores, rows, width), BF16),
            ],
        ),
        out_shape=[
            jax.ShapeDtypeStruct((slabs, pairs, rows, width), F32),
            jax.ShapeDtypeStruct((slabs, pairs, rows, width), F32),
        ],
        compiler_params=pltpu.CompilerParams(vmem_limit_bytes=36 * MIB),
        cost_estimate=pl.CostEstimate(
            flops=12 * half * elements,
            bytes_accessed=16 * elements + 12 * half * depth,
            transcendentals=4 * elements,
        ),
        name="inner",
    )(core, *banks, *turned, start, first, second, *products, target, count)


def assemble_kernel(chunk, offsets, place_ref, *refs):
    received = refs[: len(offsets)]
    out_ref, semaphore = refs[-2:]
    width = received[0].shape[-1]
    mine = place_ref[0]
    copies = []
    for ref, group in zip(received, offsets):
        for entry, offset in enumerate(group):
            copies.append(
                pltpu.make_async_copy(
                    ref.at[entry],
                    out_ref.at[lax.bitwise_xor(mine, offset), :, pl.ds(chunk * width, width)],
                    semaphore.at[len(copies)],
                )
            )
    for copy in copies:
        copy.start()
    for copy in copies:
        copy.wait()


def assemble(chunk, place, received, offsets, shape, before):
    vmem = pl.BlockSpec(memory_space=pltpu.VMEM)
    return pl.pallas_call(
        functools.partial(assemble_kernel, chunk, offsets),
        in_specs=[pl.BlockSpec(memory_space=pltpu.SMEM)]
        + [vmem] * len(received)
        + [pl.BlockSpec(memory_space=pl.ANY)] * len(before),
        out_specs=pl.BlockSpec(memory_space=pl.ANY),
        out_shape=jax.ShapeDtypeStruct(shape, BF16),
        input_output_aliases={1 + len(received): 0} if before else {},
        scratch_shapes=[pltpu.SemaphoreType.DMA((sum(map(len, offsets)),))],
        compiler_params=pltpu.CompilerParams(vmem_limit_bytes=12 * MIB),
        cost_estimate=pl.CostEstimate(
            flops=0, bytes_accessed=4 * shape[0] * shape[1] * received[0].shape[-1], transcendentals=0
        ),
        name="assemble",
    )(place, *received, *before)


def tied(first, second):
    return lax.optimization_barrier((first, second))


def per_device(sizes, global_weights, momentum, first_moment, second_moment, hidden_bank, target_bank, token_ids):
    reps, shards = sizes
    bits = reps.bit_length() - 1
    depth, columns = global_weights.shape
    rows = depth // reps
    store = hidden_bank.shape[1] * shards
    half = store // 2
    ids = token_ids[0]
    tokens = ids.shape[1]
    width = min(columns, LANES)
    chunks = columns // width
    mine = lax.axis_index("rep")

    def swapped(array, bit):
        pairs = [(index, index ^ (1 << bit)) for index in range(reps)]
        return lax.ppermute(array, "rep", pairs)

    own_bank = hidden_bank[0]
    target = target_bank[0]
    count = jnp.sum(
        ids[:, :, None] == jnp.arange(store, dtype=ids.dtype)[None, None, :], axis=1
    ).astype(F32)
    if shards == 2:
        block = depth // SLABS
        parts = [
            lax.ppermute(own_bank[:, d * block : (d + 1) * block], "fsdp", [(0, 1), (1, 0)])
            for d in range(SLABS)
        ]
        own_turned, own_product = forward(own_bank, global_weights)
        joined = ()
        for d, part in enumerate(parts):
            joined = arrive(d, part, global_weights, joined)
        banks = (own_bank, joined[0])
        turned = (own_turned, joined[1])
        products = (own_product, joined[2])
        swap = lax.axis_index("fsdp") == 1
        target = jnp.where(swap, jnp.roll(target, half, axis=0), target)
        count = jnp.where(swap, jnp.roll(count, half, axis=1), count)
    else:
        whole = lax.all_gather(own_bank, "fsdp", axis=0, tiled=True)
        banks = (whole[:half], whole[half:])
        turned, products = zip(*(forward(bank, global_weights) for bank in banks))
    count = count[:, :, None]

    cut = (SLABS, reps // (2 * SLABS), 2, rows, columns)
    turned = [array.reshape(cut[:4] + (half,)) for array in turned]
    start = global_weights.reshape(cut)
    first = first_moment.reshape(cut)
    second = second_moment.reshape(cut)
    core = (mine & 1).reshape(1).astype(jnp.int32)
    place = mine.reshape(1).astype(jnp.int32)
    my_start = lax.dynamic_slice_in_dim(global_weights, mine * rows, rows, 0)
    shares = [
        tied(momentum[:, begin : begin + width], my_start[:, begin : begin + width])
        for begin in range(0, columns, width)
    ]

    def halved(terms, bit):
        side = (mine >> bit) & 1
        terms = [term.reshape(-1, 2, rows, width) for term in terms]

        def half_of(which):
            return [
                lax.dynamic_index_in_dim(term, which, 1, keepdims=False).astype(F32)
                for term in terms
            ]

        outgoing = sum(half_of(1 - side)).astype(WIRE)
        return outgoing, [
            lax.dynamic_index_in_dim(term, side, 1, keepdims=False) for term in terms
        ]

    new_momentum = []
    result = ()

    live = {}
    for chunk in range(chunks):
        send, keep = inner(
            chunk, width, core, banks, turned, start, first, second, products, target, count, tokens
        )
        formed = [(chunk, 0, send.reshape(-1, rows, width).astype(WIRE), [keep.reshape(-1, rows, width)])]
        for earlier in range(max(chunk - bits + 1, 0), chunk):
            bit = chunk - earlier
            formed.append((earlier, bit, *halved(live[earlier], bit)))
        if chunk + 1 < chunks:
            outgoing, core = tied([entry[2] for entry in formed], core)
            formed = [entry[:2] + (out, entry[3]) for entry, out in zip(formed, outgoing)]
        for which, bit, outgoing, terms in formed:
            live[which] = terms + [swapped(outgoing, bit)]

    for chunk in range(chunks):
        terms = live[chunk]
        for bit in range(min(chunks - chunk, bits), bits):
            outgoing, terms = halved(terms, bit)
            terms = terms + [swapped(outgoing, bit)]
        total = sum(term.astype(F32) for term in terms)[0]

        average = total * (1.0 / (WIRE_SCALE * reps))
        moved = 0.9 * shares[chunk][0] + average
        new_momentum.append(moved)
        fresh = (shares[chunk][1].astype(F32) - 0.7 * (average + 0.9 * moved)).astype(BF16)

        stack = fresh[None]
        offsets = [0]
        for bit in range(bits - 1, 1, -1):
            stack = jnp.concatenate([stack, swapped(stack, bit)])
            offsets = offsets + [offset ^ (1 << bit) for offset in offsets]
        across = swapped(stack, 1)
        received = [stack, across, swapped(stack, 0), swapped(across, 0)]
        offsets = [[offset ^ low for offset in offsets] for low in (0, 2, 1, 3)]
        result = (
            assemble(chunk, place, received, offsets, (reps, rows, columns), result),
        )

    return result[0].reshape(depth, columns), jnp.concatenate(new_momentum, axis=1)


def solution(mesh):
    sizes = (mesh.shape["rep"], mesh.shape["fsdp"])
    return jax.shard_map(
        functools.partial(per_device, sizes),
        mesh=mesh,
        in_specs=(
            P(None, "fsdp"),
            P("rep", "fsdp"),
            P("rep", None, "fsdp"),
            P("rep", None, "fsdp"),
            P("rep", "fsdp", None),
            P("rep", None, "fsdp"),
            P("rep", None, None),
        ),
        out_specs=(P(None, "fsdp"), P("rep", "fsdp")),
        check_vma=False,
    )
```

time: 461 us -> 262 us (0.57)
  Pallas kernels: 264 us -> 56.6 us
  starting transfers between devices: 83.5 us -> 35.6 us
  local copies, waits for them, and re-layouts: 5.89 us -> 40.9 us
  waiting for transfers between devices: 86.3 us -> 106 us
    pallas_call x3 -> x9, Pallas kernels: 204 us -> 11.6 us  [the longest x4 5.76 us: assemble(): pl.pallas_call(functools.partial(assemble_kernel, chunk, offsets), in_spe...]
    ppermute x41 -> x40, starting transfers between devices: 83.5 us -> 35.6 us  [the longest x36 30.6 us: swapped(): return lax.ppermute(array, 'rep', pairs)]
    unnamed x30 -> x74, local copies, waits for them, and re-layouts: 5.57 us -> 32.2 us
    ppermute x41 -> x40, waiting for transfers between devices: 86.3 us -> 106 us  [the longest x36 78.1 us: swapped(): return lax.ppermute(array, 'rep', pairs)]
    pallas_call x4, Pallas kernels: 59.9 us -> 45 us  [inner(): pl.pallas_call(functools.partial(inner_kernel, float(tokens)), grid_spec=...]
    another operation x13 -> x0, other arithmetic: 6.84 us -> none  [the longest x8 5.32 us: per_device(): stack = jnp.stack([stack, shifted(stack, core=1)])]
    slice x0 -> x3, local copies, waits for them, and re-layouts: none -> 4.94 us  [the longest x1 2.86 us: per_device(): own_bank[:, d * block:(d + 1) * block]]
    dynamic_slice x0 -> x2, other arithmetic: none -> 4.87 us  [halved(): lax.dynamic_index_in_dim(term, side, 1, keepdims=False)]
  transfers between devices with their start and end apart: 41 -> 40, of which waited for: 12 -> 19; matrix products, arithmetic and copies ran while one was open for 4% -> 7% of each run, Pallas kernels for 11% -> 17%
where the time goes in v2:
time: 262 us; the launch traced here: 259 us
  waiting for transfers between devices  106 us (40%)
  Pallas kernels  56.6 us (22%)
  local copies, waits for them, and re-layouts  40.9 us (16%)
  starting transfers between devices  35.6 us (14%)
  other arithmetic  18.7 us (7%)
    ppermute x36, waiting for transfers between devices, swapped(): return lax.ppermute(array, 'rep', pairs)  78.1 us
    pallas_call x4, Pallas kernels, inner(): pl.pallas_call(functools.partial(inner_kernel, float(tokens)), grid_spec=...  45 us
    unnamed x74, local copies, waits for them, and re-layouts  32.2 us
    ppermute x36, starting transfers between devices, swapped(): return lax.ppermute(array, 'rep', pairs)  30.6 us
    ppermute x4, waiting for transfers between devices, per_device(): lax.ppermute(own_bank[:, d * block:(d + 1) * block], 'fsdp', [(0, 1), (1,...  27.4 us
    convert_element_type x10, other arithmetic, halved(): outgoing = sum(half_of(1 - side)).astype(WIRE)  5.98 us
    pallas_call x4, Pallas kernels, assemble(): pl.pallas_call(functools.partial(assemble_kernel, chunk, offsets), in_spe...  5.76 us
  transfers between devices with their start and end apart: 40, of which 19 were waited for; matrix products, arithmetic and copies ran while one was open for 7% of the time, Pallas kernels for 17%

profile of v2, /device:TPU:0, one launch (start us, length us, event | category | flops | bytes accessed | tf_op | source)
XLA Modules:
  0.0 258.8 jit_solution(15753399374354940634)
XLA Ops:
  0.7 2.9 %fusion.40 = (bf16[128,2048]{1,0:T(8,128)(2,1)S(1)}, bf16[128,2048]{1,0:T(8,128)(2,1)}, bf16[128,2048]{1,0:T(8,128)(2,1)}, bf16[128,2048]{1,0:T(8,128)(2,1)}) fusion(bf16[128,8192]{1,0:T(8,128)(2,1)} %bitcast.170), kind=kLoop, calls=%fused_computation.88 | loop fusion | bytes 4194304 | tf_op jit(solution)/shard_map/slice | solution.py:325
  3.5 3.0 %collective-permute-start.3 = (bf16[128,2048]{1,0:T(8,128)(2,1)S(1)}, bf16[128,2048]{1,0:T(8,128)(2,1)S(1)}, u32[]{:S(2)}, u32[]{:S(2)}) collective-permute-start(bf16[128,2048]{1,0:T(8,128)(2,1)S(1)} %get-tuple-element.100), channel_id=1, source_target_pairs={{0,1},{1,0},{2,3},{3,2},{4,5},{5,4},{6,7},{7,6},{8,9},{9,8},{10,11... | collective-permute-start | bytes 1572872 | tf_op jit(solution)/shard_map/ppermute | solution.py:325
  6.5 2.0 collective-permute-start.1
  8.9 3.4 %copy-done = bf16[8192,512]{1,0:T(8,128)(2,1)S(1)} copy-done((bf16[8192,512]{1,0:T(8,128)(2,1)S(1)}, bf16[8192,512]{1,0:T(8,128)(2,1)}, u32[]{:S(2)}) %copy-start) | copy-done | bytes 8388632
  12.3 2.0 forward.1
  14.3 1.3 copy-done.11
  16.0 3.2 %collective-permute-done.3.part_ref = bf16[128,2048]{1,0:T(8,128)(2,1)S(1)} collective-permute-done((bf16[128,2048]{1,0:T(8,128)(2,1)S(1)}, bf16[128,2048]{1,0:T(8,128)(2,1)S(1)}, u32[]{:S(2)}, u32[]{:S(2)}) %collective-permute-start.3) | collective-permute-done | bytes 524320 | tf_op jit(solution)/shard_map/ppermute | solution.py:325
  20.0 3.4 %copy-done.1 = bf16[8192,512]{1,0:T(8,128)(2,1)S(1)} copy-done((bf16[8192,512]{1,0:T(8,128)(2,1)S(1)}, bf16[8192,512]{1,0:T(8,128)(2,1)}, u32[]{:S(2)}) %copy-start.1) | copy-done | bytes 8388632
  24.9 5.7 %collective-permute-done.2.part_ref = bf16[128,2048]{1,0:T(8,128)(2,1)} collective-permute-done((bf16[128,2048]{1,0:T(8,128)(2,1)}, bf16[128,2048]{1,0:T(8,128)(2,1)}, u32[]{:S(2)}, u32[]{:S(2)}) %collective-permute-start.2) | collective-permute-done | bytes 524320 | tf_op jit(solution)/shard_map/ppermute | solution.py:325
  30.6 1.5 arrive.5
  32.1 9.7 %collective-permute-done.1.part_ref = bf16[128,2048]{1,0:T(8,128)(2,1)} collective-permute-done((bf16[128,2048]{1,0:T(8,128)(2,1)}, bf16[128,2048]{1,0:T(8,128)(2,1)}, u32[]{:S(2)}, u32[]{:S(2)}) %collective-permute-start.1) | collective-permute-done | bytes 524320 | tf_op jit(solution)/shard_map/ppermute | solution.py:325
  41.8 1.5 arrive.6
  43.3 8.8 %collective-permute-done.part_ref = bf16[128,2048]{1,0:T(8,128)(2,1)S(1)} collective-permute-done((bf16[128,2048]{1,0:T(8,128)(2,1)}, bf16[128,2048]{1,0:T(8,128)(2,1)S(1)}, u32[]{:S(2)}, u32[]{:S(2)}) %collective-permute-start) | collective-permute-done | bytes 524320 | tf_op jit(solution)/shard_map/ppermute | solution.py:325
  54.4 1.5 copy-done.7
  56.9 11.2 %inner.4 = (f32[4,2,512,128]{3,2,1,0:T(8,128)S(1)}, f32[4,2,512,128]{3,2,1,0:T(8,128)S(1)}) custom-call(s32[1]{0:T(128)} %bitcast.1.core_ref, bf16[128,8192]{1,0:T(8,128)(2,1)S(1)} %bitcast.172, bf16[128,8192]{1,0:T(8,128)(2,1)S(1)} %get-tuple-element.51.high_ref, bf16[4,2,2,512,128]{4,3,2,1,0:T(8,128)(2,1)S(1)} %bitcast.176, ...), custom_call_target="tpu_custom_call" | custom-call | flops 1610612736 | bytes 29360128 | tf_op jit(solution)/shard_map/inner/pallas_call | solution.py:213
  68.2 1.3 copy-done.20
  70.7 1.6 copy-done.3
  72.3 1.6 copy-done.8
  73.9 1.6 copy-done.13
  75.4 11.2 %inner.5 = (f32[4,2,512,128]{3,2,1,0:T(8,128)S(1)}, f32[4,2,512,128]{3,2,1,0:T(8,128)S(1)}) custom-call(s32[1]{0:T(128)} %bitcast.1.core_ref, bf16[128,8192]{1,0:T(8,128)(2,1)S(1)} %bitcast.173, bf16[128,8192]{1,0:T(8,128)(2,1)S(1)} %get-tuple-element.51.high_ref, bf16[4,2,2,512,128]{4,3,2,1,0:T(8,128)(2,1)S(1)} %bitcast.177, ...), custom_call_target="tpu_custom_call" | custom-call | flops 1610612736 | bytes 29360128 | tf_op jit(solution)/shard_map/inner/pallas_call | solution.py:213
  87.8 1.6 copy-done.21
  89.4 2.4 constant_dynamic-slice_fusion.7
  92.3 1.7 collective-permute-start.5
  94.1 1.6 copy-done.4
  95.7 1.6 copy-done.9
  97.3 1.6 copy-done.14
  98.9 11.3 %inner.6 = (f32[4,2,512,128]{3,2,1,0:T(8,128)S(1)}, f32[4,2,512,128]{3,2,1,0:T(8,128)S(1)}) custom-call(s32[1]{0:T(128)} %bitcast.1.core_ref, bf16[128,8192]{1,0:T(8,128)(2,1)S(1)} %bitcast.174, bf16[128,8192]{1,0:T(8,128)(2,1)S(1)} %get-tuple-element.51.high_ref, bf16[4,2,2,512,128]{4,3,2,1,0:T(8,128)(2,1)S(1)} %bitcast.178, ...), custom_call_target="tpu_custom_call" | custom-call | flops 1610612736 | bytes 29360128 | tf_op jit(solution)/shard_map/inner/pallas_call | solution.py:213
  111.3 2.1 constant_dynamic-slice_fusion.6
  113.4 1.9 fusion.4
  115.4 2.5 constant_dynamic-slice_fusion.3
  119.1 1.8 collective-permute-start.33
  122.1 1.6 copy-done.5
  123.7 1.6 copy-done.10
  125.3 1.6 copy-done.15
  126.9 11.3 %inner.7 = (f32[4,2,512,128]{3,2,1,0:T(8,128)S(1)}, f32[4,2,512,128]{3,2,1,0:T(8,128)S(1)}) custom-call(s32[1]{0:T(128)} %bitcast.1.core_ref, bf16[128,8192]{1,0:T(8,128)(2,1)S(1)} %bitcast.175, bf16[128,8192]{1,0:T(8,128)(2,1)S(1)} %get-tuple-element.51.high_ref, bf16[4,2,2,512,128]{4,3,2,1,0:T(8,128)(2,1)S(1)} %bitcast.179, ...), custom_call_target="tpu_custom_call" | custom-call | flops 1610612736 | bytes 29360128 | tf_op jit(solution)/shard_map/inner/pallas_call | solution.py:213
  140.5 2.6 %collective-permute-start.34 = (f16[1,512,128]{2,1,0:T(8,128)(2,1)S(1)}, f16[1,512,128]{2,1,0:T(8,128)(2,1)S(1)}, u32[]{:S(2)}, u32[]{:S(2)}) collective-permute-start(f16[1,512,128]{2,1,0:T(8,128)(2,1)S(1)} %fusion.11), channel_id=1, source_target_pairs={{0,16},{2,18},{4,20},{6,22},{8,24},{10,26},{12,28},{14,30},{16,0},... | collective-permute-start | bytes 393224 | tf_op jit(solution)/shard_map/ppermute | solution.py:315
  146.1 4.0 %collective-permute-done.34 = f16[1,512,128]{2,1,0:T(8,128)(2,1)S(1)} collective-permute-done((f16[1,512,128]{2,1,0:T(8,128)(2,1)S(1)}, f16[1,512,128]{2,1,0:T(8,128)(2,1)S(1)}, u32[]{:S(2)}, u32[]{:S(2)}) %collective-permute-start.34) | collective-permute-done | bytes 131104 | tf_op jit(solution)/shard_map/ppermute | solution.py:315
  151.3 4.4 %collective-permute-done.26 = f16[2,512,128]{2,1,0:T(8,128)(2,1)S(1)} collective-permute-done((f16[2,512,128]{2,1,0:T(8,128)(2,1)S(1)}, f16[2,512,128]{2,1,0:T(8,128)(2,1)S(1)}, u32[]{:S(2)}, u32[]{:S(2)}) %collective-permute-start.26) | collective-permute-done | bytes 262176 | tf_op jit(solution)/shard_map/ppermute | solution.py:315
  157.0 1.7 collective-permute-start.17
  158.6 4.2 %collective-permute-done.35 = bf16[1,512,128]{2,1,0:T(8,128)(2,1)S(1)} collective-permute-done((bf16[1,512,128]{2,1,0:T(8,128)(2,1)S(1)}, bf16[1,512,128]{2,1,0:T(8,128)(2,1)S(1)}, u32[]{:S(2)}, u32[]{:S(2)}) %collective-permute-start.35) | collective-permute-done | bytes 131104 | tf_op jit(solution)/shard_map/ppermute | solution.py:315
  163.2 1.6 collective-permute-start.8
  166.9 5.0 %collective-permute-done.17 = f16[4,512,128]{2,1,0:T(8,128)(2,1)S(1)} collective-permute-done((f16[4,512,128]{2,1,0:T(8,128)(2,1)S(1)}, f16[4,512,128]{2,1,0:T(8,128)(2,1)S(1)}, u32[]{:S(2)}, u32[]{:S(2)}) %collective-permute-start.17) | collective-permute-done | bytes 524320 | tf_op jit(solution)/shard_map/ppermute | solution.py:315
  173.0 2.2 collective-permute-start.28
  175.1 7.0 %collective-permute-done.8 = f16[4,512,128]{2,1,0:T(8,128)(2,1)S(1)} collective-permute-done((f16[4,512,128]{2,1,0:T(8,128)(2,1)S(1)}, f16[4,512,128]{2,1,0:T(8,128)(2,1)S(1)}, u32[]{:S(2)}, u32[]{:S(2)}) %collective-permute-start.8) | collective-permute-done | bytes 524320 | tf_op jit(solution)/shard_map/ppermute | solution.py:315
  182.4 1.7 collective-permute-start.37
  184.2 2.7 %collective-permute-start.19 = (f16[1,512,128]{2,1,0:T(8,128)(2,1)S(1)}, f16[1,512,128]{2,1,0:T(8,128)(2,1)S(1)}, u32[]{:S(2)}, u32[]{:S(2)}) collective-permute-start(f16[1,512,128]{2,1,0:T(8,128)(2,1)S(1)} %fusion.23), channel_id=1, source_target_pairs={{0,16},{2,18},{4,20},{6,22},{8,24},{10,26},{12,28},{14,30},{16,0},... | collective-permute-start | bytes 393224 | tf_op jit(solution)/shard_map/ppermute | solution.py:315
  186.9 2.1 collective-permute-start.29
  188.9 5.6 %collective-permute-done.9 = f16[2,512,128]{2,1,0:T(8,128)(2,1)S(1)} collective-permute-done((f16[2,512,128]{2,1,0:T(8,128)(2,1)S(1)}, f16[2,512,128]{2,1,0:T(8,128)(2,1)S(1)}, u32[]{:S(2)}, u32[]{:S(2)}) %collective-permute-start.9) | collective-permute-done | bytes 262176 | tf_op jit(solution)/shard_map/ppermute | solution.py:315
  194.7 2.7 %collective-permute-start.10 = (f16[1,512,128]{2,1,0:T(8,128)(2,1)S(1)}, f16[1,512,128]{2,1,0:T(8,128)(2,1)S(1)}, u32[]{:S(2)}, u32[]{:S(2)}) collective-permute-start(f16[1,512,128]{2,1,0:T(8,128)(2,1)S(1)} %fusion.29), channel_id=1, source_target_pairs={{0,16},{2,18},{4,20},{6,22},{8,24},{10,26},{12,28},{14,30},{16,0},... | collective-permute-start | bytes 393224 | tf_op jit(solution)/shard_map/ppermute | solution.py:315
  197.9 9.1 %collective-permute-done.10 = f16[1,512,128]{2,1,0:T(8,128)(2,1)S(1)} collective-permute-done((f16[1,512,128]{2,1,0:T(8,128)(2,1)S(1)}, f16[1,512,128]{2,1,0:T(8,128)(2,1)S(1)}, u32[]{:S(2)}, u32[]{:S(2)}) %collective-permute-start.10) | collective-permute-done | bytes 131104 | tf_op jit(solution)/shard_map/ppermute | solution.py:315
  207.4 2.3 collective-permute-done.20
  209.7 1.3 collective-permute-start.21
  211.0 3.7 %collective-permute-done.11 = bf16[1,512,128]{2,1,0:T(8,128)(2,1)S(1)} collective-permute-done((bf16[1,512,128]{2,1,0:T(8,128)(2,1)S(1)}, bf16[1,512,128]{2,1,0:T(8,128)(2,1)S(1)}, u32[]{:S(2)}, u32[]{:S(2)}) %collective-permute-start.11) | collective-permute-done | bytes 131104 | tf_op jit(solution)/shard_map/ppermute | solution.py:315
  215.0 1.7 collective-permute-start.30
  216.6 3.4 %collective-permute-done.21 = bf16[2,512,128]{2,1,0:T(8,128)(2,1)S(1)} collective-permute-done((bf16[2,512,128]{2,1,0:T(8,128)(2,1)S(1)}, bf16[2,512,128]{2,1,0:T(8,128)(2,1)S(1)}, u32[]{:S(2)}, u32[]{:S(2)}) %collective-permute-start.21) | collective-permute-done | bytes 262176 | tf_op jit(solution)/shard_map/ppermute | solution.py:315
  220.1 4.7 %collective-permute-done.12 = bf16[2,512,128]{2,1,0:T(8,128)(2,1)S(1)} collective-permute-done((bf16[2,512,128]{2,1,0:T(8,128)(2,1)S(1)}, bf16[2,512,128]{2,1,0:T(8,128)(2,1)S(1)}, u32[]{:S(2)}, u32[]{:S(2)}) %collective-permute-start.12) | collective-permute-done | bytes 262176 | tf_op jit(solution)/shard_map/ppermute | solution.py:315
  224.8 1.6 collective-permute-start.22
  227.0 2.8 %collective-permute-done.30.refs_1_ = bf16[4,512,128]{2,1,0:T(8,128)(2,1)S(1)} collective-permute-done((bf16[4,512,128]{2,1,0:T(8,128)(2,1)S(1)}, bf16[4,512,128]{2,1,0:T(8,128)(2,1)S(1)}, u32[]{:S(2)}, u32[]{:S(2)}) %collective-permute-start.30) | collective-permute-done | bytes 524320 | tf_op jit(solution)/shard_map/ppermute | solution.py:315
  230.3 10.7 %collective-permute-done.22.refs_1_ = bf16[4,512,128]{2,1,0:T(8,128)(2,1)S(1)} collective-permute-done((bf16[4,512,128]{2,1,0:T(8,128)(2,1)S(1)}, bf16[4,512,128]{2,1,0:T(8,128)(2,1)S(1)}, u32[]{:S(2)}, u32[]{:S(2)}) %collective-permute-start.22) | collective-permute-done | bytes 524320 | tf_op jit(solution)/shard_map/ppermute | solution.py:315
  241.5 10.3 %collective-permute-done.13.refs_1_ = bf16[4,512,128]{2,1,0:T(8,128)(2,1)S(1)} collective-permute-done((bf16[4,512,128]{2,1,0:T(8,128)(2,1)S(1)}, bf16[4,512,128]{2,1,0:T(8,128)(2,1)S(1)}, u32[]{:S(2)}, u32[]{:S(2)}) %collective-permute-start.13) | collective-permute-done | bytes 524320 | tf_op jit(solution)/shard_map/ppermute | solution.py:315
  251.8 1.4 assemble.4.refs_4_
  254.3 1.4 assemble.5.refs_4_
  255.8 1.4 assemble.6.refs_4_
  257.2 1.4 assemble.7
  (151 shorter events, 28.1 us)
Async XLA Ops:
  0.6 7.9 %copy-start.36 = (s32[1,2,512]{2,1,0:T(2,128)S(1)}, s32[1,2,512]{2,1,0:T(2,128)}, u32[]{:S(2)}) copy-start(s32[1,2,512]{2,1,0:T(2,128)} %param.13) | copy-start | bytes 12292
  0.6 8.2 %copy-start.35 = (bf16[1,256,512]{2,1,0:T(8,128)(2,1)S(1)}, bf16[1,256,512]{2,1,0:T(8,128)(2,1)}, u32[]{:S(2)}) copy-start(bf16[1,256,512]{2,1,0:T(8,128)(2,1)} %param.12) | copy-start | bytes 786436
  0.6 8.2 %copy-start.6 = (bf16[1,128,8192]{2,1,0:T(8,128)(2,1)S(1)}, bf16[1,128,8192]{2,1,0:T(8,128)(2,1)}, u32[]{:S(2)}) copy-start(bf16[1,128,8192]{2,1,0:T(8,128)(2,1)} %param.11) | copy-start | bytes 6291460
  3.5 15.7 %collective-permute-start.3 = (bf16[128,2048]{1,0:T(8,128)(2,1)S(1)}, bf16[128,2048]{1,0:T(8,128)(2,1)S(1)}, u32[]{:S(2)}, u32[]{:S(2)}) collective-permute-start(bf16[128,2048]{1,0:T(8,128)(2,1)S(1)} %get-tuple-element.100), channel_id=1, source_target_pairs={{0,1},{1,0},{2,3},{3,2},{4,5},{5,4},{6,7},{7,6},{8,9},{9,8},{10,11... | collective-permute-start | bytes 1572872 | tf_op jit(solution)/shard_map/ppermute | solution.py:325
  6.5 24.1 %collective-permute-start.2 = (bf16[128,2048]{1,0:T(8,128)(2,1)}, bf16[128,2048]{1,0:T(8,128)(2,1)}, u32[]{:S(2)}, u32[]{:S(2)}) collective-permute-start(bf16[128,2048]{1,0:T(8,128)(2,1)} %get-tuple-element.101), channel_id=1, source_target_pairs={{0,1},{1,0},{2,3},{3,2},{4,5},{5,4},{6,7},{7,6},{8,9},{9,8},{10,11... | collective-permute-start | bytes 1572872 | tf_op jit(solution)/shard_map/ppermute | solution.py:325
  6.5 35.3 %collective-permute-start.1 = (bf16[128,2048]{1,0:T(8,128)(2,1)}, bf16[128,2048]{1,0:T(8,128)(2,1)}, u32[]{:S(2)}, u32[]{:S(2)}) collective-permute-start(bf16[128,2048]{1,0:T(8,128)(2,1)} %get-tuple-element.102), channel_id=1, source_target_pairs={{0,1},{1,0},{2,3},{3,2},{4,5},{5,4},{6,7},{7,6},{8,9},{9,8},{10,11... | collective-permute-start | bytes 1572872 | tf_op jit(solution)/shard_map/ppermute | solution.py:325
  8.5 43.6 %collective-permute-start = (bf16[128,2048]{1,0:T(8,128)(2,1)}, bf16[128,2048]{1,0:T(8,128)(2,1)S(1)}, u32[]{:S(2)}, u32[]{:S(2)}) collective-permute-start(bf16[128,2048]{1,0:T(8,128)(2,1)} %get-tuple-element.103), channel_id=1, source_target_pairs={{0,1},{1,0},{2,3},{3,2},{4,5},{5,4},{6,7},{7,6},{8,9},{9,8},{10,11... | collective-permute-start | bytes 1572872 | tf_op jit(solution)/shard_map/ppermute | solution.py:325
  8.9 3.4 %copy-start = (bf16[8192,512]{1,0:T(8,128)(2,1)S(1)}, bf16[8192,512]{1,0:T(8,128)(2,1)}, u32[]{:S(2)}) copy-start(bf16[8192,512]{1,0:T(8,128)(2,1)} %weights_ref.9) | copy-start | bytes 25165828
  20.0 3.4 %copy-start.1 = (bf16[8192,512]{1,0:T(8,128)(2,1)S(1)}, bf16[8192,512]{1,0:T(8,128)(2,1)}, u32[]{:S(2)}) copy-start(bf16[8192,512]{1,0:T(8,128)(2,1)} %weights_ref.9) | copy-start | bytes 25165828
  54.0 2.0 copy-start.7
  54.0 3.0 %copy-start.12 = (bf16[8192,128]{1,0:T(8,128)(2,1)S(1)}, bf16[8192,128]{1,0:T(8,128)(2,1)}, u32[]{:S(2)}) copy-start(bf16[8192,128]{1,0:T(8,128)(2,1)} %copy-done.11) | copy-start | bytes 6291460
  54.4 13.8 %copy-start.2 = (bf16[8192,128]{1,0:T(8,128)(2,1)}, bf16[8192,128]{1,0:T(8,128)(2,1)S(1)}, u32[]{:S(2)}) copy-start(bf16[8192,128]{1,0:T(8,128)(2,1)S(1)} %get-tuple-element.53) | copy-start | bytes 6291460
  70.7 17.2 %collective-permute-start.4 = (f16[8,512,128]{2,1,0:T(8,128)(2,1)}, f16[8,512,128]{2,1,0:T(8,128)(2,1)}, u32[]{:S(2)}, u32[]{:S(2)}) collective-permute-start(f16[8,512,128]{2,1,0:T(8,128)(2,1)} %bitcast.15), channel_id=1, source_target_pairs={{0,2},{2,0},{4,6},{6,4},{8,10},{10,8},{12,14},{14,12},{16,18},{18,... | collective-permute-start | bytes 3145736 | tf_op jit(solution)/shard_map/ppermute | solution.py:315
  70.7 1.6 copy-start.3
  72.3 1.6 copy-start.8
  73.9 1.6 copy-start.13
  86.7 5.1 %copy-start.18 = (f32[4,2,512,128]{3,2,1,0:T(8,128)}, f32[4,2,512,128]{3,2,1,0:T(8,128)S(1)}, u32[]{:S(2)}) copy-start(f32[4,2,512,128]{3,2,1,0:T(8,128)S(1)} %get-tuple-element.64) | copy-start | bytes 6291460
  86.7 2.7 %copy-start.21 = (f32[4,2,512,128]{3,2,1,0:T(8,128)S(1)}, f32[4,2,512,128]{3,2,1,0:T(8,128)}, u32[]{:S(2)}) copy-start(f32[4,2,512,128]{3,2,1,0:T(8,128)} %copy-done.20) | copy-start | bytes 6291460
  91.8 23.5 %collective-permute-start.6 = (f16[8,512,128]{2,1,0:T(8,128)(2,1)}, f16[8,512,128]{2,1,0:T(8,128)(2,1)}, u32[]{:S(2)}, u32[]{:S(2)}) collective-permute-start(f16[8,512,128]{2,1,0:T(8,128)(2,1)} %bitcast.16), channel_id=1, source_target_pairs={{0,2},{2,0},{4,6},{6,4},{8,10},{10,8},{12,14},{14,12},{16,18},{18,... | collective-permute-start | bytes 3145736 | tf_op jit(solution)/shard_map/ppermute | solution.py:315
  92.3 21.0 %collective-permute-start.5 = (f16[4,512,128]{2,1,0:T(8,128)(2,1)}, f16[4,512,128]{2,1,0:T(8,128)(2,1)}, u32[]{:S(2)}, u32[]{:S(2)}) collective-permute-start(f16[4,512,128]{2,1,0:T(8,128)(2,1)} %get-tuple-element.63), channel_id=1, source_target_pairs={{0,4},{2,6},{4,0},{6,2},{8,12},{10,14},{12,8},{14,10},{16,20},{18,... | collective-permute-start | bytes 1572872 | tf_op jit(solution)/shard_map/ppermute | solution.py:315
  110.1 3.2 %copy-start.16 = (f32[4,2,512,128]{3,2,1,0:T(8,128)}, f32[4,2,512,128]{3,2,1,0:T(8,128)S(1)}, u32[]{:S(2)}) copy-start(f32[4,2,512,128]{3,2,1,0:T(8,128)S(1)} %get-tuple-element.71) | copy-start | bytes 6291460
  110.1 3.3 %copy-start.27 = (f32[4,1,512,128]{3,2,1,0:T(8,128)S(1)}, f32[4,1,512,128]{3,2,1,0:T(8,128)}, u32[]{:S(2)}) copy-start(f32[4,1,512,128]{3,2,1,0:T(8,128)} %get-tuple-element.98) | copy-start | bytes 3145732
  110.1 5.2 %copy-start.19 = (f32[4,2,512,128]{3,2,1,0:T(8,128)S(1)}, f32[4,2,512,128]{3,2,1,0:T(8,128)}, u32[]{:S(2)}) copy-start(f32[4,2,512,128]{3,2,1,0:T(8,128)} %copy-done.18) | copy-start | bytes 6291460
  113.4 4.5 %copy-start.32 = (f16[4,1,512,128]{3,2,1,0:T(8,128)(2,1)}, f16[4,1,512,128]{3,2,1,0:T(8,128)(2,1)S(1)}, u32[]{:S(2)}) copy-start(f16[4,1,512,128]{3,2,1,0:T(8,128)(2,1)S(1)} %constant_dynamic-slice_fusion.6) | copy-start | bytes 1572868
  115.3 2.8 %copy-start.34 = (f32[512,512]{1,0:T(8,128)S(1)}, f32[512,512]{1,0:T(8,128)}, u32[]{:S(2)}) copy-start(f32[512,512]{1,0:T(8,128)} %param.8) | copy-start | bytes 3145732
  117.8 26.4 %collective-permute-start.25 = (f16[4,512,128]{2,1,0:T(8,128)(2,1)}, f16[4,512,128]{2,1,0:T(8,128)(2,1)}, u32[]{:S(2)}, u32[]{:S(2)}) collective-permute-start(f16[4,512,128]{2,1,0:T(8,128)(2,1)} %get-tuple-element.75), channel_id=1, source_target_pairs={{0,4},{2,6},{4,0},{6,2},{8,12},{10,14},{12,8},{14,10},{16,20},{18,... | collective-permute-start | bytes 1572872 | tf_op jit(solution)/shard_map/ppermute | solution.py:315
  119.1 19.8 %collective-permute-start.33 = (f16[2,512,128]{2,1,0:T(8,128)(2,1)}, f16[2,512,128]{2,1,0:T(8,128)(2,1)S(1)}, u32[]{:S(2)}, u32[]{:S(2)}) collective-permute-start(f16[2,512,128]{2,1,0:T(8,128)(2,1)} %fusion.4), channel_id=1, source_target_pairs={{0,8},{2,10},{4,12},{6,14},{8,0},{10,2},{12,4},{14,6},{16,24},{18,... | collective-permute-start | bytes 786440 | tf_op jit(solution)/shard_map/ppermute | solution.py:315
  122.0 34.7 %collective-permute-start.16 = (f16[8,512,128]{2,1,0:T(8,128)(2,1)}, f16[8,512,128]{2,1,0:T(8,128)(2,1)S(1)}, u32[]{:S(2)}, u32[]{:S(2)}) collective-permute-start(f16[8,512,128]{2,1,0:T(8,128)(2,1)} %bitcast.213), channel_id=1, source_target_pairs={{0,2},{2,0},{4,6},{6,4},{8,10},{10,8},{12,14},{14,12},{16,18},{18,... | collective-permute-start | bytes 3145736 | tf_op jit(solution)/shard_map/ppermute | solution.py:315
  122.1 1.6 copy-start.5
  138.2 6.1 %copy-start.26 = (f32[4,1,512,128]{3,2,1,0:T(8,128)S(1)}, f32[4,1,512,128]{3,2,1,0:T(8,128)}, u32[]{:S(2)}) copy-start(f32[4,1,512,128]{3,2,1,0:T(8,128)} %get-tuple-element.92) | copy-start | bytes 3145732
  138.3 11.7 %copy-start.31 = (f32[512,128]{1,0:T(8,128)S(1)}, f32[512,128]{1,0:T(8,128)}, u32[]{:S(2)}) copy-start(f32[512,128]{1,0:T(8,128)} %get-tuple-element.79) | copy-start | bytes 786436
  138.3 24.7 %collective-permute-start.7 = (f16[8,512,128]{2,1,0:T(8,128)(2,1)S(1)}, f16[8,512,128]{2,1,0:T(8,128)(2,1)S(1)}, u32[]{:S(2)}, u32[]{:S(2)}) collective-permute-start(f16[8,512,128]{2,1,0:T(8,128)(2,1)S(1)} %bitcast.218), channel_id=1, source_target_pairs={{0,2},{2,0},{4,6},{6,4},{8,10},{10,8},{12,14},{14,12},{16,18},{18,... | collective-permute-start | bytes 3145736 | tf_op jit(solution)/shard_map/ppermute | solution.py:315
  140.5 9.6 %collective-permute-start.34 = (f16[1,512,128]{2,1,0:T(8,128)(2,1)S(1)}, f16[1,512,128]{2,1,0:T(8,128)(2,1)S(1)}, u32[]{:S(2)}, u32[]{:S(2)}) collective-permute-start(f16[1,512,128]{2,1,0:T(8,128)(2,1)S(1)} %fusion.11), channel_id=1, source_target_pairs={{0,16},{2,18},{4,20},{6,22},{8,24},{10,26},{12,28},{14,30},{16,0},... | collective-permute-start | bytes 393224 | tf_op jit(solution)/shard_map/ppermute | solution.py:315
  144.3 12.5 %copy-start.17 = (f32[4,2,512,128]{3,2,1,0:T(8,128)S(1)}, f32[4,2,512,128]{3,2,1,0:T(8,128)}, u32[]{:S(2)}) copy-start(f32[4,2,512,128]{3,2,1,0:T(8,128)} %copy-done.16) | copy-start | bytes 6291460
  145.5 10.1 %collective-permute-start.26 = (f16[2,512,128]{2,1,0:T(8,128)(2,1)S(1)}, f16[2,512,128]{2,1,0:T(8,128)(2,1)S(1)}, u32[]{:S(2)}, u32[]{:S(2)}) collective-permute-start(f16[2,512,128]{2,1,0:T(8,128)(2,1)S(1)} %fusion.7), channel_id=1, source_target_pairs={{0,8},{2,10},{4,12},{6,14},{8,0},{10,2},{12,4},{14,6},{16,24},{18,... | collective-permute-start | bytes 786440 | tf_op jit(solution)/shard_map/ppermute | solution.py:315
  151.2 11.7 %collective-permute-start.35 = (bf16[1,512,128]{2,1,0:T(8,128)(2,1)S(1)}, bf16[1,512,128]{2,1,0:T(8,128)(2,1)S(1)}, u32[]{:S(2)}, u32[]{:S(2)}) collective-permute-start(bf16[1,512,128]{2,1,0:T(8,128)(2,1)S(1)} %fusion.35), channel_id=1, source_target_pairs={{0,16},{2,18},{4,20},{6,22},{8,24},{10,26},{12,28},{14,30},{16,0},... | collective-permute-start | bytes 393224 | tf_op jit(solution)/shard_map/ppermute | solution.py:315
  156.6 8.9 %collective-permute-start.27 = (f16[1,512,128]{2,1,0:T(8,128)(2,1)S(1)}, f16[1,512,128]{2,1,0:T(8,128)(2,1)S(1)}, u32[]{:S(2)}, u32[]{:S(2)}) collective-permute-start(f16[1,512,128]{2,1,0:T(8,128)(2,1)S(1)} %fusion.17), channel_id=1, source_target_pairs={{0,16},{2,18},{4,20},{6,22},{8,24},{10,26},{12,28},{14,30},{16,0},... | collective-permute-start | bytes 393224 | tf_op jit(solution)/shard_map/ppermute | solution.py:315
  157.0 14.8 %collective-permute-start.17 = (f16[4,512,128]{2,1,0:T(8,128)(2,1)S(1)}, f16[4,512,128]{2,1,0:T(8,128)(2,1)S(1)}, u32[]{:S(2)}, u32[]{:S(2)}) collective-permute-start(f16[4,512,128]{2,1,0:T(8,128)(2,1)S(1)} %get-tuple-element.94), channel_id=1, source_target_pairs={{0,4},{2,6},{4,0},{6,2},{8,12},{10,14},{12,8},{14,10},{16,20},{18,... | collective-permute-start | bytes 1572872 | tf_op jit(solution)/shard_map/ppermute | solution.py:315
  162.9 19.5 %collective-permute-start.36 = (bf16[2,512,128]{2,1,0:T(8,128)(2,1)S(1)}, bf16[2,512,128]{2,1,0:T(8,128)(2,1)S(1)}, u32[]{:S(2)}, u32[]{:S(2)}) collective-permute-start(bf16[2,512,128]{2,1,0:T(8,128)(2,1)S(1)} %pad_maximum_fusion.8), channel_id=1, source_target_pairs={{0,8},{2,10},{4,12},{6,14},{8,0},{10,2},{12,4},{14,6},{16,24},{18,... | collective-permute-start | bytes 786440 | tf_op jit(solution)/shard_map/ppermute | solution.py:315
  163.0 2.6 %copy-start.30 = (f32[512,128]{1,0:T(8,128)S(1)}, f32[512,128]{1,0:T(8,128)}, u32[]{:S(2)}) copy-start(f32[512,128]{1,0:T(8,128)} %get-tuple-element.76) | copy-start | bytes 786436
  163.2 18.9 %collective-permute-start.8 = (f16[4,512,128]{2,1,0:T(8,128)(2,1)S(1)}, f16[4,512,128]{2,1,0:T(8,128)(2,1)S(1)}, u32[]{:S(2)}, u32[]{:S(2)}) collective-permute-start(f16[4,512,128]{2,1,0:T(8,128)(2,1)S(1)} %get-tuple-element.96), channel_id=1, source_target_pairs={{0,4},{2,6},{4,0},{6,2},{8,12},{10,14},{12,8},{14,10},{16,20},{18,... | collective-permute-start | bytes 1572872 | tf_op jit(solution)/shard_map/ppermute | solution.py:315
  172.0 12.1 %collective-permute-start.18 = (f16[2,512,128]{2,1,0:T(8,128)(2,1)S(1)}, f16[2,512,128]{2,1,0:T(8,128)(2,1)S(1)}, u32[]{:S(2)}, u32[]{:S(2)}) collective-permute-start(f16[2,512,128]{2,1,0:T(8,128)(2,1)S(1)} %fusion.6), channel_id=1, source_target_pairs={{0,8},{2,10},{4,12},{6,14},{8,0},{10,2},{12,4},{14,6},{16,24},{18,... | collective-permute-start | bytes 786440 | tf_op jit(solution)/shard_map/ppermute | solution.py:315
  173.0 13.9 %collective-permute-start.28 = (bf16[1,512,128]{2,1,0:T(8,128)(2,1)S(1)}, bf16[1,512,128]{2,1,0:T(8,128)(2,1)S(1)}, u32[]{:S(2)}, u32[]{:S(2)}) collective-permute-start(bf16[1,512,128]{2,1,0:T(8,128)(2,1)S(1)} %fusion.34), channel_id=1, source_target_pairs={{0,16},{2,18},{4,20},{6,22},{8,24},{10,26},{12,28},{14,30},{16,0},... | collective-permute-start | bytes 393224 | tf_op jit(solution)/shard_map/ppermute | solution.py:315
  182.1 15.2 %copy-start.29 = (f32[512,128]{1,0:T(8,128)S(1)}, f32[512,128]{1,0:T(8,128)}, u32[]{:S(2)}) copy-start(f32[512,128]{1,0:T(8,128)} %get-tuple-element.73) | copy-start | bytes 786436
  182.3 12.3 %collective-permute-start.9 = (f16[2,512,128]{2,1,0:T(8,128)(2,1)S(1)}, f16[2,512,128]{2,1,0:T(8,128)(2,1)S(1)}, u32[]{:S(2)}, u32[]{:S(2)}) collective-permute-start(f16[2,512,128]{2,1,0:T(8,128)(2,1)S(1)} %fusion.5), channel_id=1, source_target_pairs={{0,8},{2,10},{4,12},{6,14},{8,0},{10,2},{12,4},{14,6},{16,24},{18,... | collective-permute-start | bytes 786440 | tf_op jit(solution)/shard_map/ppermute | solution.py:315
  182.4 32.4 %collective-permute-start.37 = (bf16[4,512,128]{2,1,0:T(8,128)(2,1)S(1)}, bf16[4,512,128]{2,1,0:T(8,128)(2,1)S(1)}, u32[]{:S(2)}, u32[]{:S(2)}) collective-permute-start(bf16[4,512,128]{2,1,0:T(8,128)(2,1)S(1)} %pad_maximum_fusion.4.refs_0_), channel_id=1, source_target_pairs={{0,4},{2,6},{4,0},{6,2},{8,12},{10,14},{12,8},{14,10},{16,20},{18,... | collective-permute-start | bytes 1572872 | tf_op jit(solution)/shard_map/ppermute | solution.py:315
  184.2 13.2 %collective-permute-start.19 = (f16[1,512,128]{2,1,0:T(8,128)(2,1)S(1)}, f16[1,512,128]{2,1,0:T(8,128)(2,1)S(1)}, u32[]{:S(2)}, u32[]{:S(2)}) collective-permute-start(f16[1,512,128]{2,1,0:T(8,128)(2,1)S(1)} %fusion.23), channel_id=1, source_target_pairs={{0,16},{2,18},{4,20},{6,22},{8,24},{10,26},{12,28},{14,30},{16,0},... | collective-permute-start | bytes 393224 | tf_op jit(solution)/shard_map/ppermute | solution.py:315
  186.9 28.0 %collective-permute-start.29 = (bf16[2,512,128]{2,1,0:T(8,128)(2,1)S(1)}, bf16[2,512,128]{2,1,0:T(8,128)(2,1)S(1)}, u32[]{:S(2)}, u32[]{:S(2)}) collective-permute-start(bf16[2,512,128]{2,1,0:T(8,128)(2,1)S(1)} %pad_maximum_fusion.7), channel_id=1, source_target_pairs={{0,8},{2,10},{4,12},{6,14},{8,0},{10,2},{12,4},{14,6},{16,24},{18,... | collective-permute-start | bytes 786440 | tf_op jit(solution)/shard_map/ppermute | solution.py:315
  194.7 12.4 %collective-permute-start.10 = (f16[1,512,128]{2,1,0:T(8,128)(2,1)S(1)}, f16[1,512,128]{2,1,0:T(8,128)(2,1)S(1)}, u32[]{:S(2)}, u32[]{:S(2)}) collective-permute-start(f16[1,512,128]{2,1,0:T(8,128)(2,1)S(1)} %fusion.29), channel_id=1, source_target_pairs={{0,16},{2,18},{4,20},{6,22},{8,24},{10,26},{12,28},{14,30},{16,0},... | collective-permute-start | bytes 393224 | tf_op jit(solution)/shard_map/ppermute | solution.py:315
  197.6 12.1 %collective-permute-start.20 = (bf16[1,512,128]{2,1,0:T(8,128)(2,1)S(1)}, bf16[1,512,128]{2,1,0:T(8,128)(2,1)S(1)}, u32[]{:S(2)}, u32[]{:S(2)}) collective-permute-start(bf16[1,512,128]{2,1,0:T(8,128)(2,1)S(1)} %fusion.33), channel_id=1, source_target_pairs={{0,16},{2,18},{4,20},{6,22},{8,24},{10,26},{12,28},{14,30},{16,0},... | collective-permute-start | bytes 393224 | tf_op jit(solution)/shard_map/ppermute | solution.py:315
  207.3 7.4 %collective-permute-start.11 = (bf16[1,512,128]{2,1,0:T(8,128)(2,1)S(1)}, bf16[1,512,128]{2,1,0:T(8,128)(2,1)S(1)}, u32[]{:S(2)}, u32[]{:S(2)}) collective-permute-start(bf16[1,512,128]{2,1,0:T(8,128)(2,1)S(1)} %fusion.32), channel_id=1, source_target_pairs={{0,16},{2,18},{4,20},{6,22},{8,24},{10,26},{12,28},{14,30},{16,0},... | collective-permute-start | bytes 393224 | tf_op jit(solution)/shard_map/ppermute | solution.py:315
  207.3 19.1 %collective-permute-start.38 = (bf16[4,512,128]{2,1,0:T(8,128)(2,1)S(1)}, bf16[4,512,128]{2,1,0:T(8,128)(2,1)S(1)}, u32[]{:S(2)}, u32[]{:S(2)}) collective-permute-start(bf16[4,512,128]{2,1,0:T(8,128)(2,1)S(1)} %pad_maximum_fusion.4.refs_0_), channel_id=1, source_target_pairs={{0,2},{2,0},{4,6},{6,4},{8,10},{10,8},{12,14},{14,12},{16,18},{18,... | collective-permute-start | bytes 1572872 | tf_op jit(solution)/shard_map/ppermute | solution.py:315
  209.7 10.3 %collective-permute-start.21 = (bf16[2,512,128]{2,1,0:T(8,128)(2,1)S(1)}, bf16[2,512,128]{2,1,0:T(8,128)(2,1)S(1)}, u32[]{:S(2)}, u32[]{:S(2)}) collective-permute-start(bf16[2,512,128]{2,1,0:T(8,128)(2,1)S(1)} %pad_maximum_fusion.6), channel_id=1, source_target_pairs={{0,8},{2,10},{4,12},{6,14},{8,0},{10,2},{12,4},{14,6},{16,24},{18,... | collective-permute-start | bytes 786440 | tf_op jit(solution)/shard_map/ppermute | solution.py:315
  214.7 10.1 %collective-permute-start.12 = (bf16[2,512,128]{2,1,0:T(8,128)(2,1)S(1)}, bf16[2,512,128]{2,1,0:T(8,128)(2,1)S(1)}, u32[]{:S(2)}, u32[]{:S(2)}) collective-permute-start(bf16[2,512,128]{2,1,0:T(8,128)(2,1)S(1)} %pad_maximum_fusion.5), channel_id=1, source_target_pairs={{0,8},{2,10},{4,12},{6,14},{8,0},{10,2},{12,4},{14,6},{16,24},{18,... | collective-permute-start | bytes 786440 | tf_op jit(solution)/shard_map/ppermute | solution.py:315
  214.8 14.9 %collective-permute-start.39 = (bf16[4,512,128]{2,1,0:T(8,128)(2,1)S(1)}, bf16[4,512,128]{2,1,0:T(8,128)(2,1)S(1)}, u32[]{:S(2)}, u32[]{:S(2)}) collective-permute-start(bf16[4,512,128]{2,1,0:T(8,128)(2,1)S(1)} %collective-permute-done.37.refs_1_), channel_id=1, source_target_pairs={{0,2},{2,0},{4,6},{6,4},{8,10},{10,8},{12,14},{14,12},{16,18},{18,... | collective-permute-start | bytes 1572872 | tf_op jit(solution)/shard_map/ppermute | solution.py:315
  215.0 14.8 %collective-permute-start.30 = (bf16[4,512,128]{2,1,0:T(8,128)(2,1)S(1)}, bf16[4,512,128]{2,1,0:T(8,128)(2,1)S(1)}, u32[]{:S(2)}, u32[]{:S(2)}) collective-permute-start(bf16[4,512,128]{2,1,0:T(8,128)(2,1)S(1)} %pad_maximum_fusion.3.refs_0_), channel_id=1, source_target_pairs={{0,4},{2,6},{4,0},{6,2},{8,12},{10,14},{12,8},{14,10},{16,20},{18,... | collective-permute-start | bytes 1572872 | tf_op jit(solution)/shard_map/ppermute | solution.py:315
  220.0 21.0 %collective-permute-start.31 = (bf16[4,512,128]{2,1,0:T(8,128)(2,1)S(1)}, bf16[4,512,128]{2,1,0:T(8,128)(2,1)S(1)}, u32[]{:S(2)}, u32[]{:S(2)}) collective-permute-start(bf16[4,512,128]{2,1,0:T(8,128)(2,1)S(1)} %pad_maximum_fusion.3.refs_0_), channel_id=1, source_target_pairs={{0,2},{2,0},{4,6},{6,4},{8,10},{10,8},{12,14},{14,12},{16,18},{18,... | collective-permute-start | bytes 1572872 | tf_op jit(solution)/shard_map/ppermute | solution.py:315
  224.8 16.2 %collective-permute-start.22 = (bf16[4,512,128]{2,1,0:T(8,128)(2,1)S(1)}, bf16[4,512,128]{2,1,0:T(8,128)(2,1)S(1)}, u32[]{:S(2)}, u32[]{:S(2)}) collective-permute-start(bf16[4,512,128]{2,1,0:T(8,128)(2,1)S(1)} %pad_maximum_fusion.2.refs_0_), channel_id=1, source_target_pairs={{0,4},{2,6},{4,0},{6,2},{8,12},{10,14},{12,8},{14,10},{16,20},{18,... | collective-permute-start | bytes 1572872 | tf_op jit(solution)/shard_map/ppermute | solution.py:315
  226.5 25.3 %collective-permute-start.13 = (bf16[4,512,128]{2,1,0:T(8,128)(2,1)S(1)}, bf16[4,512,128]{2,1,0:T(8,128)(2,1)S(1)}, u32[]{:S(2)}, u32[]{:S(2)}) collective-permute-start(bf16[4,512,128]{2,1,0:T(8,128)(2,1)S(1)} %pad_maximum_fusion.1.refs_0_), channel_id=1, source_target_pairs={{0,4},{2,6},{4,0},{6,2},{8,12},{10,14},{12,8},{14,10},{16,20},{18,... | collective-permute-start | bytes 1572872 | tf_op jit(solution)/shard_map/ppermute | solution.py:315
  229.8 24.6 %collective-permute-start.32 = (bf16[4,512,128]{2,1,0:T(8,128)(2,1)S(1)}, bf16[4,512,128]{2,1,0:T(8,128)(2,1)S(1)}, u32[]{:S(2)}, u32[]{:S(2)}) collective-permute-start(bf16[4,512,128]{2,1,0:T(8,128)(2,1)S(1)} %collective-permute-done.30.refs_1_), channel_id=1, source_target_pairs={{0,2},{2,0},{4,6},{6,4},{8,10},{10,8},{12,14},{14,12},{16,18},{18,... | collective-permute-start | bytes 1572872 | tf_op jit(solution)/shard_map/ppermute | solution.py:315
  229.8 26.0 %collective-permute-start.23 = (bf16[4,512,128]{2,1,0:T(8,128)(2,1)S(1)}, bf16[4,512,128]{2,1,0:T(8,128)(2,1)S(1)}, u32[]{:S(2)}, u32[]{:S(2)}) collective-permute-start(bf16[4,512,128]{2,1,0:T(8,128)(2,1)S(1)} %pad_maximum_fusion.2.refs_0_), channel_id=1, source_target_pairs={{0,2},{2,0},{4,6},{6,4},{8,10},{10,8},{12,14},{14,12},{16,18},{18,... | collective-permute-start | bytes 1572872 | tf_op jit(solution)/shard_map/ppermute | solution.py:315
  241.0 14.8 %collective-permute-start.24 = (bf16[4,512,128]{2,1,0:T(8,128)(2,1)S(1)}, bf16[4,512,128]{2,1,0:T(8,128)(2,1)S(1)}, u32[]{:S(2)}, u32[]{:S(2)}) collective-permute-start(bf16[4,512,128]{2,1,0:T(8,128)(2,1)S(1)} %collective-permute-done.22.refs_1_), channel_id=1, source_target_pairs={{0,2},{2,0},{4,6},{6,4},{8,10},{10,8},{12,14},{14,12},{16,18},{18,... | collective-permute-start | bytes 1572872 | tf_op jit(solution)/shard_map/ppermute | solution.py:315
  241.0 16.2 %collective-permute-start.14 = (bf16[4,512,128]{2,1,0:T(8,128)(2,1)S(1)}, bf16[4,512,128]{2,1,0:T(8,128)(2,1)S(1)}, u32[]{:S(2)}, u32[]{:S(2)}) collective-permute-start(bf16[4,512,128]{2,1,0:T(8,128)(2,1)S(1)} %pad_maximum_fusion.1.refs_0_), channel_id=1, source_target_pairs={{0,2},{2,0},{4,6},{6,4},{8,10},{10,8},{12,14},{14,12},{16,18},{18,... | collective-permute-start | bytes 1572872 | tf_op jit(solution)/shard_map/ppermute | solution.py:315
  251.8 5.4 %collective-permute-start.15 = (bf16[4,512,128]{2,1,0:T(8,128)(2,1)S(1)}, bf16[4,512,128]{2,1,0:T(8,128)(2,1)S(1)}, u32[]{:S(2)}, u32[]{:S(2)}) collective-permute-start(bf16[4,512,128]{2,1,0:T(8,128)(2,1)S(1)} %collective-permute-done.13.refs_1_), channel_id=1, source_target_pairs={{0,2},{2,0},{4,6},{6,4},{8,10},{10,8},{12,14},{14,12},{16,18},{18,... | collective-permute-start | bytes 1572872 | tf_op jit(solution)/shard_map/ppermute | solution.py:315
  (13 other events, 16.9 us)

commit v3 on v2

--- a/solution.py
+++ b/solution.py
@@ -46,21 +46,23 @@
             jax.ShapeDtypeStruct((depth, rows), BF16),
             jax.ShapeDtypeStruct((rows, columns), F32),
         ],
-        compiler_params=pltpu.CompilerParams(vmem_limit_bytes=24 * MIB),
+        compiler_params=pltpu.CompilerParams(vmem_limit_bytes=14 * MIB),
         cost_estimate=pl.CostEstimate(
             flops=2 * rows * depth * columns,
             bytes_accessed=2 * depth * columns + 4 * rows * depth,
             transcendentals=0,
         ),
         name="forward",
-    )(part, weights)
-
-
-def arrive_kernel(part_ref, weights_ref, *refs):
+    )(part, pinned(weights))
+
+
+def arrive_kernel(piece, part_ref, weights_ref, *refs):
     natural_ref, turned_ref, product_ref = refs[-3:]
+    block = part_ref.shape[1]
+    place = pl.ds(piece * block, block)
     part = part_ref[...]
-    natural_ref[...] = part
-    turned_ref[...] = part.T
+    natural_ref[:, place] = part
+    turned_ref[place, :] = part.T
     product = jnp.dot(part, weights_ref[...], preferred_element_type=F32)
     if len(refs) > 3:
         product = product + refs[2][...]
@@ -70,39 +72,45 @@
 def arrive(piece, part, weights, before):
     rows, block = part.shape
     depth, columns = weights.shape
-    whole = pl.BlockSpec((rows, columns), lambda d: (0, 0))
+    whole = pl.BlockSpec(memory_space=pltpu.VMEM)
     return pl.pallas_call(
-        arrive_kernel,
+        functools.partial(arrive_kernel, piece),
         grid=(1,),
-        in_specs=[
-            pl.BlockSpec((rows, block), lambda d: (0, 0)),
-            pl.BlockSpec((block, columns), lambda d: (piece, 0)),
-        ]
-        + ([pl.BlockSpec(memory_space=pl.ANY)] * 2 + [whole] if before else []),
-        out_specs=[
-            pl.BlockSpec((rows, block), lambda d: (0, piece)),
-            pl.BlockSpec((block, rows), lambda d: (piece, 0)),
-            whole,
-        ],
+        in_specs=[whole, pl.BlockSpec((block, columns), lambda d: (piece, 0))]
+        + [whole] * len(before),
+        out_specs=[whole] * 3,
         out_shape=[
             jax.ShapeDtypeStruct((rows, depth), BF16),
             jax.ShapeDtypeStruct((depth, rows), BF16),
             jax.ShapeDtypeStruct((rows, columns), F32),
         ],
-        input_output_aliases={2: 0, 3: 1} if before else {},
-        compiler_params=pltpu.CompilerParams(vmem_limit_bytes=24 * MIB),
+        input_output_aliases={2: 0, 3: 1, 4: 2} if before else {},
+        compiler_params=pltpu.CompilerParams(vmem_limit_bytes=10 * MIB),
         cost_estimate=pl.CostEstimate(
             flops=2 * rows * block * columns,
             bytes_accessed=2 * block * columns + 6 * rows * block,
             transcendentals=0,
         ),
         name="arrive",
-    )(part, weights, *before)
+    )(part, pinned(weights), *before)
+
+
+def pinned(array):
+    return pltpu.with_memory_space_constraint(array, pltpu.HBM)
+
+
+def changed_place(mine, slab, pair, pairs):
+    offset = lax.bitwise_xor(slab * pairs + pair, mine // 2)
+    bits = (SLABS * pairs).bit_length() - 1
+    place = jnp.int32(0)
+    for bit in range(bits):
+        place = place * 2 + lax.rem(lax.shift_right_logical(offset, bit), 2)
+    return place
 
 
 def inner_kernel(
     tokens,
-    core_ref,
+    mine_ref,
     low_ref,
     high_ref,
     low_turned_ref,
@@ -127,7 +135,8 @@
     step = pl.program_id(0)
     slab = pl.program_id(1)
     pairs, cores, rows, _ = start_ref.shape
-    core = core_ref[0]
+    mine = mine_ref[0]
+    core = lax.rem(mine, cores)
     pieces = [pl.ds(begin, PIECE) for begin in range(0, rows, PIECE)]
 
     def weigh(output, which):
@@ -141,7 +150,7 @@
 
     def gradient_of(pair, which, slot):
         turned = jnp.concatenate(
-            [low_turned_ref[pair, which], high_turned_ref[pair, which]], axis=1
+            [low_turned_ref[slab, pair, which], high_turned_ref[slab, pair, which]], axis=1
         )
         gradient_state[slot] = jnp.dot(
             turned, residual_state[...], preferred_element_type=F32
@@ -172,7 +181,8 @@
                     second_state[slab, pair, which, piece] = second
                     weights_state[slab, pair, which, piece] = weights
                     rounded_state[slot, piece] = weights.astype(BF16)
-                place = pl.ds(slot * rows, rows)
+                begin = (slab * pairs * cores + slot) * rows
+                place = pl.ds(pl.multiple_of(begin, rows), rows)
                 picked = jnp.concatenate([low_ref[:, place], high_ref[:, place]], axis=0)
                 total += jnp.dot(picked, rounded_state[slot], preferred_element_type=F32)
         output_state[...] += total
@@ -180,6 +190,7 @@
     @pl.when(step == 1)
     def _():
         for pair in range(pairs):
+            place = changed_place(mine, slab, pair, pairs)
             for slot, which, out_ref in ((0, 1 - core, send_ref), (1, core, keep_ref)):
                 slot = pair * cores + slot
                 gradient_of(pair, which, slot)
@@ -189,37 +200,28 @@
                     second = 0.95 * second_state[slab, pair, which, piece] + gradient * gradient
                     weights = descend(first, second, weights_state[slab, pair, which, piece])
                     change = start_ref[pair, which, piece].astype(F32) - weights
-                    out_ref[pair, piece] = change * WIRE_SCALE
-
-
-def inner(chunk, width, core, banks, turned, start, first, second, products, target, count, tokens):
+                    out_ref[place, piece] = change * WIRE_SCALE
+
+
+def inner(chunk, width, mine, banks, turned, start, first, second, products, target, count, tokens):
     slabs, pairs, cores, rows, _ = start.shape
     half, depth = banks[0].shape
-    block = depth // slabs
 
     def held(step, slab):
         return jnp.where(step == 0, slab, slabs - 1)
 
-    def drawn(step, slab):
-        return jnp.where(step == 0, 0, slab)
-
-    natural = pl.BlockSpec((half, block), lambda s, z, c: (0, held(s, z)))
-    flipped = pl.BlockSpec((None, pairs, cores, rows, half), lambda s, z, c: (z, 0, 0, 0, 0))
+    whole = pl.BlockSpec(memory_space=pltpu.VMEM)
     tile = (None, pairs, cores, rows, width)
     state = pl.BlockSpec(tile, lambda s, z, c: (held(s, z), 0, 0, 0, chunk))
     product = pl.BlockSpec((half, width), lambda s, z, c: (0, chunk))
-    change = pl.BlockSpec((None, pairs, rows, width), lambda s, z, c: (drawn(s, z), 0, 0, 0))
     elements = depth * width
     return pl.pallas_call(
         functools.partial(inner_kernel, float(tokens)),
         grid_spec=pltpu.PrefetchScalarGridSpec(
             num_scalar_prefetch=1,
             grid=(2, slabs),
-            in_specs=[
-                natural,
-                natural,
-                flipped,
-                flipped,
+            in_specs=[whole] * 4
+            + [
                 pl.BlockSpec(tile, lambda s, z, c: (z, 0, 0, 0, chunk)),
                 state,
                 state,
@@ -228,7 +230,7 @@
                 pl.BlockSpec((2 * half, width), lambda s, z, c: (0, chunk)),
                 pl.BlockSpec(count.shape, lambda s, z, c: (0, 0, 0)),
             ],
-            out_specs=[change, change],
+            out_specs=[whole, whole],
             scratch_shapes=[
                 pltpu.VMEM((slabs, pairs, cores, rows, width), F32),
                 pltpu.VMEM((slabs, pairs, cores, rows, width), F32),
@@ -240,17 +242,17 @@
             ],
         ),
         out_shape=[
-            jax.ShapeDtypeStruct((slabs, pairs, rows, width), F32),
-            jax.ShapeDtypeStruct((slabs, pairs, rows, width), F32),
+            jax.ShapeDtypeStruct((slabs * pairs, rows, width), F32),
+            jax.ShapeDtypeStruct((slabs * pairs, rows, width), F32),
         ],
-        compiler_params=pltpu.CompilerParams(vmem_limit_bytes=36 * MIB),
+        compiler_params=pltpu.CompilerParams(vmem_limit_bytes=22 * MIB),
         cost_estimate=pl.CostEstimate(
             flops=12 * half * elements,
-            bytes_accessed=16 * elements + 12 * half * depth,
+            bytes_accessed=20 * elements,
             transcendentals=4 * elements,
         ),
         name="inner",
-    )(core, *banks, *turned, start, first, second, *products, target, count)
+    )(mine, *banks, *turned, pinned(start), pinned(first), pinned(second), *products, target, count)
 
 
 def assemble_kernel(chunk, offsets, place_ref, *refs):
@@ -321,10 +323,11 @@
     ).astype(F32)
     if shards == 2:
         block = depth // SLABS
-        parts = [
-            lax.ppermute(own_bank[:, d * block : (d + 1) * block], "fsdp", [(0, 1), (1, 0)])
-            for d in range(SLABS)
-        ]
+        parts = []
+        source = own_bank
+        for d in range(SLABS):
+            part, source = tied(source[:, d * block : (d + 1) * block], source)
+            parts.append(lax.ppermute(part, "fsdp", [(0, 1), (1, 0)]))
         own_turned, own_product = forward(own_bank, global_weights)
         joined = ()
         for d, part in enumerate(parts):
@@ -346,7 +349,6 @@
     start = global_weights.reshape(cut)
     first = first_moment.reshape(cut)
     second = second_moment.reshape(cut)
-    core = (mine & 1).reshape(1).astype(jnp.int32)
     place = mine.reshape(1).astype(jnp.int32)
     my_start = lax.dynamic_slice_in_dim(global_weights, mine * rows, rows, 0)
     shares = [
@@ -354,43 +356,41 @@
         for begin in range(0, columns, width)
     ]
 
-    def halved(terms, bit):
-        side = (mine >> bit) & 1
-        terms = [term.reshape(-1, 2, rows, width) for term in terms]
-
-        def half_of(which):
-            return [
-                lax.dynamic_index_in_dim(term, which, 1, keepdims=False).astype(F32)
-                for term in terms
-            ]
-
-        outgoing = sum(half_of(1 - side)).astype(WIRE)
-        return outgoing, [
-            lax.dynamic_index_in_dim(term, side, 1, keepdims=False) for term in terms
-        ]
+    def halved(terms):
+        middle = terms[0].shape[0] // 2
+        outgoing = sum(term[middle:].astype(F32) for term in terms).astype(WIRE)
+        return outgoing, [term[:middle] for term in terms]
 
     new_momentum = []
     result = ()
 
     live = {}
+    token = place
     for chunk in range(chunks):
         send, keep = inner(
-            chunk, width, core, banks, turned, start, first, second, products, target, count, tokens
+            chunk, width, token, banks, turned, start, first, second, products, target, count, tokens
         )
-        formed = [(chunk, 0, send.reshape(-1, rows, width).astype(WIRE), [keep.reshape(-1, rows, width)])]
-        for earlier in range(max(chunk - bits + 1, 0), chunk):
-            bit = chunk - earlier
-            formed.append((earlier, bit, *halved(live[earlier], bit)))
+        send = send.astype(WIRE)
+        moving = {}
+        for earlier in range(max(chunk - bits + 2, 0), chunk):
+            outgoing, terms = halved(live[earlier])
+            outgoing, send = tied(outgoing, send)
+            moving[earlier] = (outgoing, terms)
+        outgoing, terms = halved([keep, swapped(send, 0)])
+        moving[chunk] = (outgoing, terms)
         if chunk + 1 < chunks:
-            outgoing, core = tied([entry[2] for entry in formed], core)
-            formed = [entry[:2] + (out, entry[3]) for entry, out in zip(formed, outgoing)]
-        for which, bit, outgoing, terms in formed:
-            live[which] = terms + [swapped(outgoing, bit)]
+            formed, token = tied([outgoing for outgoing, _ in moving.values()], token)
+            moving = {
+                which: (outgoing, terms)
+                for (which, (_, terms)), outgoing in zip(moving.items(), formed)
+            }
+        for which, (outgoing, terms) in moving.items():
+            live[which] = terms + [swapped(outgoing, chunk - which + 1)]
 
     for chunk in range(chunks):
         terms = live[chunk]
-        for bit in range(min(chunks - chunk, bits), bits):
-            outgoing, terms = halved(terms, bit)
+        for bit in range(min(chunks - chunk + 1, bits), bits):
+            outgoing, terms = halved(terms)
             terms = terms + [swapped(outgoing, bit)]
         total = sum(term.astype(F32) for term in terms)[0]
 
@@ -405,6 +405,8 @@
             stack = jnp.concatenate([stack, swapped(stack, bit)])
             offsets = offsets + [offset ^ (1 << bit) for offset in offsets]
         across = swapped(stack, 1)
+        if result:
+            across, *result = tied(across, result[0])
         received = [stack, across, swapped(stack, 0), swapped(across, 0)]
         offsets = [[offset ^ low for offset in offsets] for low in (0, 2, 1, 3)]
         result = (

time: 262 us -> 223 us (0.85)
  local copies, waits for them, and re-layouts: 40.9 us -> 11.9 us
  starting transfers between devices: 35.6 us -> 27.5 us
  Pallas kernels: 56.6 us -> 63.7 us
  other arithmetic: 18.7 us -> 12.8 us
    unnamed x74 -> x48, local copies, waits for them, and re-layouts: 32.2 us -> 1.66 us
    ppermute x36, starting transfers between devices: 30.6 us -> 22.5 us  [swapped(): return lax.ppermute(array, 'rep', pairs)]
    dynamic_slice x2 -> x0, other arithmetic: 4.87 us -> none  [halved(): lax.dynamic_index_in_dim(term, side, 1, keepdims=False)]
    pallas_call x4, Pallas kernels: 3.85 us -> 8.67 us  [arrive(): pl.pallas_call(functools.partial(arrive_kernel, piece), grid=(1,), in_spe...]
    convert_element_type x14 -> x16, other arithmetic: 9.51 us -> 5.16 us  [the longest x12 4.59 us: halved(): outgoing = sum((term[middle:].astype(F32) for term in terms)).astype(WIRE)]
    dynamic_slice x3 -> x0, local copies, waits for them, and re-layouts: 3.45 us -> none  [halved(): lax.dynamic_index_in_dim(term, side, 1, keepdims=False)]
    pallas_call x1, Pallas kernels: 2.01 us -> 4.97 us  [forward(): pl.pallas_call(forward_kernel, grid=(SLABS,), in_specs=[pl.BlockSpec((row...]
    ppermute x4, waiting for transfers between devices: 27.4 us -> 24.6 us  [per_device(): parts.append(lax.ppermute(part, 'fsdp', [(0, 1), (1, 0)]))]
  transfers between devices with their start and end apart: 40 -> 40, of which waited for: 19 -> 22; matrix products, arithmetic and copies ran while one was open for 7% -> 8% of each run, Pallas kernels for 17% -> 22%
where the time goes in v3:
time: 223 us; the launch traced here: 222 us
  waiting for transfers between devices  105 us (47%)
  Pallas kernels  63.7 us (29%)
  starting transfers between devices  27.5 us (12%)
  other arithmetic  12.8 us (6%)
  local copies, waits for them, and re-layouts  11.9 us (5%)
    ppermute x36, waiting for transfers between devices, swapped(): return lax.ppermute(array, 'rep', pairs)  80.2 us
    pallas_call x4, Pallas kernels, inner(): pl.pallas_call(functools.partial(inner_kernel, float(tokens)), grid_spec=...  44.3 us
    ppermute x4, waiting for transfers between devices, per_device(): parts.append(lax.ppermute(part, 'fsdp', [(0, 1), (1, 0)]))  24.6 us
    ppermute x36, starting transfers between devices, swapped(): return lax.ppermute(array, 'rep', pairs)  22.5 us
    pallas_call x4, Pallas kernels, arrive(): pl.pallas_call(functools.partial(arrive_kernel, piece), grid=(1,), in_spe...  8.67 us
    pallas_call x4, Pallas kernels, assemble(): pl.pallas_call(functools.partial(assemble_kernel, chunk, offsets), in_spe...  5.75 us
    slice x4, local copies, waits for them, and re-layouts, per_device(): part, source = tied(source[:, d * block:(d + 1) * block], source)  5.64 us
    ppermute x4, starting transfers between devices, per_device(): parts.append(lax.ppermute(part, 'fsdp', [(0, 1), (1, 0)]))  5.03 us
  transfers between devices with their start and end apart: 40, of which 22 were waited for; matrix products, arithmetic and copies ran while one was open for 8% of the time, Pallas kernels for 22%

profile of v3, /device:TPU:0, one launch (start us, length us, event | category | flops | bytes accessed | tf_op | source)
XLA Modules:
  0.0 222.1 jit_solution(2668941590595490722)
XLA Ops:
  0.7 2.1 slice.344
  2.7 1.9 slice.277
  4.6 3.0 %collective-permute-start.2 = (bf16[128,2048]{1,0:T(8,128)(2,1)}, bf16[128,2048]{1,0:T(8,128)(2,1)}, u32[]{:S(2)}, u32[]{:S(2)}) collective-permute-start(bf16[128,2048]{1,0:T(8,128)(2,1)} %slice.277), channel_id=1, source_target_pairs={{0,1},{1,0},{2,3},{3,2},{4,5},{5,4},{6,7},{7,6},{8,9},{9,8},{10,11... | collective-permute-start | bytes 1572872 | tf_op jit(solution)/shard_map/ppermute | solution.py:330
  7.6 0.8 slice.278
  8.5 2.0 collective-permute-start.1
  10.5 0.8 slice.279
  12.3 5.0 %forward.1 = (bf16[8192,128]{1,0:T(8,128)(2,1)S(1)}, f32[128,512]{1,0:T(8,128)S(1)}) custom-call(bf16[128,8192]{1,0:T(8,128)(2,1)S(1)} %bitcast.89, bf16[8192,512]{1,0:T(8,128)(2,1)} %weights_ref.9), custom_call_target="tpu_custom_call" | custom-call | flops 1073741824 | bytes 12582912 | tf_op jit(solution)/shard_map/forward/pallas_call | solution.py:34
  17.3 1.3 copy-done.1
  18.6 0.9 copy.31
  19.4 0.8 copy.32
  20.3 1.1 maximum_select_fusion.target_ref
  21.4 1.0 broadcast_select_fusion.count_ref
  22.4 9.5 %collective-permute-done.3.part_ref = bf16[128,2048]{1,0:T(8,128)(2,1)} collective-permute-done((bf16[128,2048]{1,0:T(8,128)(2,1)}, bf16[128,2048]{1,0:T(8,128)(2,1)}, u32[]{:S(2)}, u32[]{:S(2)}) %collective-permute-start.3) | collective-permute-done | bytes 524320 | tf_op jit(solution)/shard_map/ppermute | solution.py:330
  31.9 2.2 arrive.4
  34.1 2.2 %arrive.5 = (bf16[128,8192]{1,0:T(8,128)(2,1)S(1)}, bf16[8192,128]{1,0:T(8,128)(2,1)S(1)}, f32[128,512]{1,0:T(8,128)S(1)}) custom-call(bf16[128,2048]{1,0:T(8,128)(2,1)} %collective-permute-done.2.part_ref, bf16[8192,512]{1,0:T(8,128)(2,1)} %weights_ref.9, ...), custom_call_target="tpu_custom_call", output_to_operand_aliasing={{0}: (2, {}), {1}: (3, {}), {2}: (4, {})} | custom-call | flops 268435456 | bytes 3670016 | tf_op jit(solution)/shard_map/arrive/pallas_call | solution.py:76
  36.4 6.7 %collective-permute-done.1.part_ref = bf16[128,2048]{1,0:T(8,128)(2,1)S(1)} collective-permute-done((bf16[128,2048]{1,0:T(8,128)(2,1)}, bf16[128,2048]{1,0:T(8,128)(2,1)S(1)}, u32[]{:S(2)}, u32[]{:S(2)}) %collective-permute-start.1) | collective-permute-done | bytes 524320 | tf_op jit(solution)/shard_map/ppermute | solution.py:330
  43.0 2.0 arrive.6
  45.1 8.3 %collective-permute-done.part_ref = bf16[128,2048]{1,0:T(8,128)(2,1)S(1)} collective-permute-done((bf16[128,2048]{1,0:T(8,128)(2,1)}, bf16[128,2048]{1,0:T(8,128)(2,1)S(1)}, u32[]{:S(2)}, u32[]{:S(2)}) %collective-permute-start) | collective-permute-done | bytes 524320 | tf_op jit(solution)/shard_map/ppermute | solution.py:330
  53.4 2.2 arrive.7
  55.7 11.0 %inner.4 = (f32[8,512,128]{2,1,0:T(8,128)S(1)}, f32[8,512,128]{2,1,0:T(8,128)S(1)}) custom-call(s32[1]{0:T(128)} %bitcast.mine_ref.place_ref, bf16[128,8192]{1,0:T(8,128)(2,1)S(1)} %bitcast.90, bf16[128,8192]{1,0:T(8,128)(2,1)S(1)} %get-tuple-element.81.high_ref, bf16[4,2,2,512,128]{4,3,2,1,0:T(8,128)(2,1)S(1)} %bitcast.94, ...), custom_call_target="tpu_custom_call" | custom-call | flops 1610612736 | bytes 20971520 | tf_op jit(solution)/shard_map/inner/pallas_call | solution.py:218
  67.0 2.6 %collective-permute-done.4 = f16[8,512,128]{2,1,0:T(8,128)(2,1)S(1)} collective-permute-done((f16[8,512,128]{2,1,0:T(8,128)(2,1)S(1)}, f16[8,512,128]{2,1,0:T(8,128)(2,1)S(1)}, u32[]{:S(2)}, u32[]{:S(2)}) %collective-permute-start.4) | collective-permute-done | bytes 1048608 | tf_op jit(solution)/shard_map/ppermute | solution.py:317
  69.8 1.8 collective-permute-start.5
  71.6 11.0 %inner.5 = (f32[8,512,128]{2,1,0:T(8,128)S(1)}, f32[8,512,128]{2,1,0:T(8,128)S(1)}) custom-call(s32[1]{0:T(128)} %bitcast.mine_ref.place_ref, bf16[128,8192]{1,0:T(8,128)(2,1)S(1)} %bitcast.91, bf16[128,8192]{1,0:T(8,128)(2,1)S(1)} %get-tuple-element.81.high_ref, bf16[4,2,2,512,128]{4,3,2,1,0:T(8,128)(2,1)S(1)} %bitcast.95, ...), custom_call_target="tpu_custom_call" | custom-call | flops 1610612736 | bytes 20971520 | tf_op jit(solution)/shard_map/inner/pallas_call | solution.py:218
  82.7 1.1 collective-permute-done.5
  84.0 2.6 %collective-permute-done.6 = f16[8,512,128]{2,1,0:T(8,128)(2,1)S(1)} collective-permute-done((f16[8,512,128]{2,1,0:T(8,128)(2,1)S(1)}, f16[8,512,128]{2,1,0:T(8,128)(2,1)S(1)}, u32[]{:S(2)}, u32[]{:S(2)}) %collective-permute-start.6) | collective-permute-done | bytes 1048608 | tf_op jit(solution)/shard_map/ppermute | solution.py:317
  86.8 1.8 collective-permute-start.8
  88.6 1.6 collective-permute-start.7
  90.2 11.0 %inner.6 = (f32[8,512,128]{2,1,0:T(8,128)S(1)}, f32[8,512,128]{2,1,0:T(8,128)S(1)}) custom-call(s32[1]{0:T(128)} %bitcast.mine_ref.place_ref, bf16[128,8192]{1,0:T(8,128)(2,1)S(1)} %bitcast.92, bf16[128,8192]{1,0:T(8,128)(2,1)S(1)} %get-tuple-element.81.high_ref, bf16[4,2,2,512,128]{4,3,2,1,0:T(8,128)(2,1)S(1)} %bitcast.96, ...), custom_call_target="tpu_custom_call" | custom-call | flops 1610612736 | bytes 20971520 | tf_op jit(solution)/shard_map/inner/pallas_call | solution.py:218
  101.4 1.0 add_convert_fusion.11
  102.6 2.6 %collective-permute-done.9 = f16[8,512,128]{2,1,0:T(8,128)(2,1)S(1)} collective-permute-done((f16[8,512,128]{2,1,0:T(8,128)(2,1)S(1)}, f16[8,512,128]{2,1,0:T(8,128)(2,1)S(1)}, u32[]{:S(2)}, u32[]{:S(2)}) %collective-permute-start.9) | collective-permute-done | bytes 1048608 | tf_op jit(solution)/shard_map/ppermute | solution.py:317
  106.0 1.2 collective-permute-start.11
  107.2 2.6 %collective-permute-start.28 = (f16[1,512,128]{2,1,0:T(8,128)(2,1)}, f16[1,512,128]{2,1,0:T(8,128)(2,1)S(1)}, u32[]{:S(2)}, u32[]{:S(2)}) collective-permute-start(f16[1,512,128]{2,1,0:T(8,128)(2,1)} %add_convert_fusion.11), channel_id=1, source_target_pairs={{0,16},{2,18},{4,20},{6,22},{8,24},{10,26},{12,28},{14,30},{16,0},... | collective-permute-start | bytes 393224 | tf_op jit(solution)/shard_map/ppermute | solution.py:317
  109.8 11.2 %inner.7 = (f32[8,512,128]{2,1,0:T(8,128)S(1)}, f32[8,512,128]{2,1,0:T(8,128)S(1)}) custom-call(s32[1]{0:T(128)} %bitcast.mine_ref.place_ref, bf16[128,8192]{1,0:T(8,128)(2,1)S(1)} %bitcast.93, bf16[128,8192]{1,0:T(8,128)(2,1)S(1)} %get-tuple-element.81.high_ref, bf16[4,2,2,512,128]{4,3,2,1,0:T(8,128)(2,1)S(1)} %bitcast.97, ...), custom_call_target="tpu_custom_call" | custom-call | flops 1610612736 | bytes 20971520 | tf_op jit(solution)/shard_map/inner/pallas_call | solution.py:218
  122.0 0.8 add_convert_fusion.5
  123.0 1.0 fusion.16
  124.0 1.2 constant_dynamic-slice_fusion
  125.3 1.5 bitcast_add_fusion.1
  127.2 2.6 %collective-permute-start.24 = (f16[1,512,128]{2,1,0:T(8,128)(2,1)}, f16[1,512,128]{2,1,0:T(8,128)(2,1)S(1)}, u32[]{:S(2)}, u32[]{:S(2)}) collective-permute-start(f16[1,512,128]{2,1,0:T(8,128)(2,1)} %add_convert_fusion.10), channel_id=1, source_target_pairs={{0,16},{2,18},{4,20},{6,22},{8,24},{10,26},{12,28},{14,30},{16,0},... | collective-permute-start | bytes 393224 | tf_op jit(solution)/shard_map/ppermute | solution.py:317
  129.8 9.6 %collective-permute-done.29 = bf16[1,512,128]{2,1,0:T(8,128)(2,1)S(1)} collective-permute-done((bf16[1,512,128]{2,1,0:T(8,128)(2,1)S(1)}, bf16[1,512,128]{2,1,0:T(8,128)(2,1)S(1)}, u32[]{:S(2)}, u32[]{:S(2)}) %collective-permute-start.29) | collective-permute-done | bytes 131104 | tf_op jit(solution)/shard_map/ppermute | solution.py:317
  139.5 2.4 %collective-permute-done.24 = f16[1,512,128]{2,1,0:T(8,128)(2,1)S(1)} collective-permute-done((f16[1,512,128]{2,1,0:T(8,128)(2,1)}, f16[1,512,128]{2,1,0:T(8,128)(2,1)S(1)}, u32[]{:S(2)}, u32[]{:S(2)}) %collective-permute-start.24) | collective-permute-done | bytes 131104 | tf_op jit(solution)/shard_map/ppermute | solution.py:317
  141.9 1.2 bitcast_add_fusion.3
  143.2 1.2 collective-permute-start.19
  144.4 5.7 %collective-permute-done.30 = bf16[2,512,128]{2,1,0:T(8,128)(2,1)S(1)} collective-permute-done((bf16[2,512,128]{2,1,0:T(8,128)(2,1)S(1)}, bf16[2,512,128]{2,1,0:T(8,128)(2,1)S(1)}, u32[]{:S(2)}, u32[]{:S(2)}) %collective-permute-start.30) | collective-permute-done | bytes 262176 | tf_op jit(solution)/shard_map/ppermute | solution.py:317
  150.2 2.5 %collective-permute-start.31 = (bf16[4,512,128]{2,1,0:T(8,128)(2,1)S(1)}, bf16[4,512,128]{2,1,0:T(8,128)(2,1)S(1)}, u32[]{:S(2)}, u32[]{:S(2)}) collective-permute-start(bf16[4,512,128]{2,1,0:T(8,128)(2,1)S(1)} %pad_maximum_fusion.4.refs_0_), channel_id=1, source_target_pairs={{0,4},{2,6},{4,0},{6,2},{8,12},{10,14},{12,8},{14,10},{16,20},{18,... | collective-permute-start | bytes 1572872 | tf_op jit(solution)/shard_map/ppermute | solution.py:317
  153.0 2.9 %collective-permute-done.19 = f16[2,512,128]{2,1,0:T(8,128)(2,1)S(1)} collective-permute-done((f16[2,512,128]{2,1,0:T(8,128)(2,1)S(1)}, f16[2,512,128]{2,1,0:T(8,128)(2,1)S(1)}, u32[]{:S(2)}, u32[]{:S(2)}) %collective-permute-start.19) | collective-permute-done | bytes 262176 | tf_op jit(solution)/shard_map/ppermute | solution.py:317
  155.9 1.0 add_convert_fusion.8
  157.1 1.1 collective-permute-start.26
  158.3 6.3 %collective-permute-done.20 = f16[1,512,128]{2,1,0:T(8,128)(2,1)S(1)} collective-permute-done((f16[1,512,128]{2,1,0:T(8,128)(2,1)S(1)}, f16[1,512,128]{2,1,0:T(8,128)(2,1)S(1)}, u32[]{:S(2)}, u32[]{:S(2)}) %collective-permute-start.20) | collective-permute-done | bytes 131104 | tf_op jit(solution)/shard_map/ppermute | solution.py:317
  164.5 1.1 bitcast_add_fusion.5
  165.8 5.9 %collective-permute-done.13 = f16[4,512,128]{2,1,0:T(8,128)(2,1)S(1)} collective-permute-done((f16[4,512,128]{2,1,0:T(8,128)(2,1)S(1)}, f16[4,512,128]{2,1,0:T(8,128)(2,1)S(1)}, u32[]{:S(2)}, u32[]{:S(2)}) %collective-permute-start.13) | collective-permute-done | bytes 524320 | tf_op jit(solution)/shard_map/ppermute | solution.py:317
  172.3 1.5 collective-permute-done.21
  174.4 7.0 %collective-permute-done.14 = f16[2,512,128]{2,1,0:T(8,128)(2,1)S(1)} collective-permute-done((f16[2,512,128]{2,1,0:T(8,128)(2,1)S(1)}, f16[2,512,128]{2,1,0:T(8,128)(2,1)S(1)}, u32[]{:S(2)}, u32[]{:S(2)}) %collective-permute-start.14) | collective-permute-done | bytes 262176 | tf_op jit(solution)/shard_map/ppermute | solution.py:317
  181.6 3.7 %collective-permute-done.22 = bf16[2,512,128]{2,1,0:T(8,128)(2,1)S(1)} collective-permute-done((bf16[2,512,128]{2,1,0:T(8,128)(2,1)S(1)}, bf16[2,512,128]{2,1,0:T(8,128)(2,1)S(1)}, u32[]{:S(2)}, u32[]{:S(2)}) %collective-permute-start.22) | collective-permute-done | bytes 262176 | tf_op jit(solution)/shard_map/ppermute | solution.py:317
  185.7 1.4 assemble.4.refs_4_
  188.4 8.4 %collective-permute-done.16 = bf16[1,512,128]{2,1,0:T(8,128)(2,1)S(1)} collective-permute-done((bf16[1,512,128]{2,1,0:T(8,128)(2,1)S(1)}, bf16[1,512,128]{2,1,0:T(8,128)(2,1)S(1)}, u32[]{:S(2)}, u32[]{:S(2)}) %collective-permute-start.16) | collective-permute-done | bytes 131104 | tf_op jit(solution)/shard_map/ppermute | solution.py:317
  197.0 1.4 assemble.5.refs_4_
  198.5 1.3 collective-permute-done.23.refs_1_
  199.7 5.4 %collective-permute-done.17 = bf16[2,512,128]{2,1,0:T(8,128)(2,1)S(1)} collective-permute-done((bf16[2,512,128]{2,1,0:T(8,128)(2,1)S(1)}, bf16[2,512,128]{2,1,0:T(8,128)(2,1)S(1)}, u32[]{:S(2)}, u32[]{:S(2)}) %collective-permute-start.17) | collective-permute-done | bytes 262176 | tf_op jit(solution)/shard_map/ppermute | solution.py:317
  205.2 2.1 collective-permute-start.18
  207.3 1.4 assemble.6.refs_4_
  208.8 9.8 %collective-permute-done.18.refs_1_ = bf16[4,512,128]{2,1,0:T(8,128)(2,1)S(1)} collective-permute-done((bf16[4,512,128]{2,1,0:T(8,128)(2,1)S(1)}, bf16[4,512,128]{2,1,0:T(8,128)(2,1)S(1)}, u32[]{:S(2)}, u32[]{:S(2)}) %collective-permute-start.18) | collective-permute-done | bytes 524320 | tf_op jit(solution)/shard_map/ppermute | solution.py:317
  218.6 1.0 pad_maximum_fusion
  219.6 0.9 collective-permute-done.39.refs_3_
  220.5 1.4 assemble.7
  (121 shorter events, 8.6 us)
Async XLA Ops:
  0.6 7.0 %copy-start = (bf16[1,128,8192]{2,1,0:T(8,128)(2,1)S(1)}, bf16[1,128,8192]{2,1,0:T(8,128)(2,1)}, u32[]{:S(2)}) copy-start(bf16[1,128,8192]{2,1,0:T(8,128)(2,1)} %param.11) | copy-start | bytes 6291460
  0.6 10.7 %copy-start.23 = (s32[1,2,512]{2,1,0:T(2,128)S(1)}, s32[1,2,512]{2,1,0:T(2,128)}, u32[]{:S(2)}) copy-start(s32[1,2,512]{2,1,0:T(2,128)} %param.13) | copy-start | bytes 12292
  0.7 10.9 %copy-start.11 = (bf16[1,256,512]{2,1,0:T(8,128)(2,1)S(1)}, bf16[1,256,512]{2,1,0:T(8,128)(2,1)}, u32[]{:S(2)}) copy-start(bf16[1,256,512]{2,1,0:T(8,128)(2,1)} %param.12) | copy-start | bytes 786436
  4.6 29.5 %collective-permute-start.2 = (bf16[128,2048]{1,0:T(8,128)(2,1)}, bf16[128,2048]{1,0:T(8,128)(2,1)}, u32[]{:S(2)}, u32[]{:S(2)}) collective-permute-start(bf16[128,2048]{1,0:T(8,128)(2,1)} %slice.277), channel_id=1, source_target_pairs={{0,1},{1,0},{2,3},{3,2},{4,5},{5,4},{6,7},{7,6},{8,9},{9,8},{10,11... | collective-permute-start | bytes 1572872 | tf_op jit(solution)/shard_map/ppermute | solution.py:330
  7.6 24.3 %collective-permute-start.3 = (bf16[128,2048]{1,0:T(8,128)(2,1)}, bf16[128,2048]{1,0:T(8,128)(2,1)}, u32[]{:S(2)}, u32[]{:S(2)}) collective-permute-start(bf16[128,2048]{1,0:T(8,128)(2,1)} %slice.344), channel_id=1, source_target_pairs={{0,1},{1,0},{2,3},{3,2},{4,5},{5,4},{6,7},{7,6},{8,9},{9,8},{10,11... | collective-permute-start | bytes 1572872 | tf_op jit(solution)/shard_map/ppermute | solution.py:330
  8.5 34.5 %collective-permute-start.1 = (bf16[128,2048]{1,0:T(8,128)(2,1)}, bf16[128,2048]{1,0:T(8,128)(2,1)S(1)}, u32[]{:S(2)}, u32[]{:S(2)}) collective-permute-start(bf16[128,2048]{1,0:T(8,128)(2,1)} %slice.278), channel_id=1, source_target_pairs={{0,1},{1,0},{2,3},{3,2},{4,5},{5,4},{6,7},{7,6},{8,9},{9,8},{10,11... | collective-permute-start | bytes 1572872 | tf_op jit(solution)/shard_map/ppermute | solution.py:330
  11.3 42.1 %collective-permute-start = (bf16[128,2048]{1,0:T(8,128)(2,1)}, bf16[128,2048]{1,0:T(8,128)(2,1)S(1)}, u32[]{:S(2)}, u32[]{:S(2)}) collective-permute-start(bf16[128,2048]{1,0:T(8,128)(2,1)} %slice.279), channel_id=1, source_target_pairs={{0,1},{1,0},{2,3},{3,2},{4,5},{5,4},{6,7},{7,6},{8,9},{9,8},{10,11... | collective-permute-start | bytes 1572872 | tf_op jit(solution)/shard_map/ppermute | solution.py:330
  17.2 1.3 copy-start.1
  53.4 2.2 %copy-start.2 = (bf16[8192,128]{1,0:T(8,128)(2,1)S(1)}, bf16[8192,128]{1,0:T(8,128)(2,1)}, u32[]{:S(2)}) copy-start(bf16[8192,128]{1,0:T(8,128)(2,1)} %copy-done.1) | copy-start | bytes 6291460
  66.7 34.7 %copy-start.7 = (f32[8,512,128]{2,1,0:T(8,128)}, f32[8,512,128]{2,1,0:T(8,128)S(1)}, u32[]{:S(2)}) copy-start(f32[8,512,128]{2,1,0:T(8,128)S(1)} %get-tuple-element.86) | copy-start | bytes 6291460
  66.9 2.7 %collective-permute-start.4 = (f16[8,512,128]{2,1,0:T(8,128)(2,1)S(1)}, f16[8,512,128]{2,1,0:T(8,128)(2,1)S(1)}, u32[]{:S(2)}, u32[]{:S(2)}) collective-permute-start(f16[8,512,128]{2,1,0:T(8,128)(2,1)S(1)} %convert_element_type.212), channel_id=1, source_target_pairs={{0,2},{2,0},{4,6},{6,4},{8,10},{10,8},{12,14},{14,12},{16,18},{18,... | collective-permute-start | bytes 3145736 | tf_op jit(solution)/shard_map/ppermute | solution.py:317
  69.6 31.8 %copy-start.10 = (f16[8,512,128]{2,1,0:T(8,128)(2,1)}, f16[8,512,128]{2,1,0:T(8,128)(2,1)S(1)}, u32[]{:S(2)}) copy-start(f16[8,512,128]{2,1,0:T(8,128)(2,1)S(1)} %collective-permute-done.4) | copy-start | bytes 3145732
  69.8 14.0 %collective-permute-start.5 = (f16[4,512,128]{2,1,0:T(8,128)(2,1)S(1)}, f16[4,512,128]{2,1,0:T(8,128)(2,1)S(1)}, u32[]{:S(2)}, u32[]{:S(2)}) collective-permute-start(f16[4,512,128]{2,1,0:T(8,128)(2,1)S(1)} %add_convert_fusion.3), channel_id=1, source_target_pairs={{0,4},{2,6},{4,0},{6,2},{8,12},{10,14},{12,8},{14,10},{16,20},{18,... | collective-permute-start | bytes 1572872 | tf_op jit(solution)/shard_map/ppermute | solution.py:317
  82.6 38.6 %copy-start.6 = (f32[8,512,128]{2,1,0:T(8,128)}, f32[8,512,128]{2,1,0:T(8,128)S(1)}, u32[]{:S(2)}) copy-start(f32[8,512,128]{2,1,0:T(8,128)S(1)} %get-tuple-element.92) | copy-start | bytes 6291460
  83.8 17.6 %copy-start.18 = (f16[4,512,128]{2,1,0:T(8,128)(2,1)}, f16[4,512,128]{2,1,0:T(8,128)(2,1)S(1)}, u32[]{:S(2)}) copy-start(f16[4,512,128]{2,1,0:T(8,128)(2,1)S(1)} %collective-permute-done.5) | copy-start | bytes 1572868
  83.9 2.7 %collective-permute-start.6 = (f16[8,512,128]{2,1,0:T(8,128)(2,1)S(1)}, f16[8,512,128]{2,1,0:T(8,128)(2,1)S(1)}, u32[]{:S(2)}, u32[]{:S(2)}) collective-permute-start(f16[8,512,128]{2,1,0:T(8,128)(2,1)S(1)} %convert_element_type.220), channel_id=1, source_target_pairs={{0,2},{2,0},{4,6},{6,4},{8,10},{10,8},{12,14},{14,12},{16,18},{18,... | collective-permute-start | bytes 3145736 | tf_op jit(solution)/shard_map/ppermute | solution.py:317
  86.7 34.5 %copy-start.9 = (f16[8,512,128]{2,1,0:T(8,128)(2,1)}, f16[8,512,128]{2,1,0:T(8,128)(2,1)S(1)}, u32[]{:S(2)}) copy-start(f16[8,512,128]{2,1,0:T(8,128)(2,1)S(1)} %collective-permute-done.6) | copy-start | bytes 3145732
  86.8 15.6 %collective-permute-start.8 = (f16[4,512,128]{2,1,0:T(8,128)(2,1)S(1)}, f16[4,512,128]{2,1,0:T(8,128)(2,1)S(1)}, u32[]{:S(2)}, u32[]{:S(2)}) collective-permute-start(f16[4,512,128]{2,1,0:T(8,128)(2,1)S(1)} %add_convert_fusion.2), channel_id=1, source_target_pairs={{0,4},{2,6},{4,0},{6,2},{8,12},{10,14},{12,8},{14,10},{16,20},{18,... | collective-permute-start | bytes 1572872 | tf_op jit(solution)/shard_map/ppermute | solution.py:317
  88.6 12.8 %collective-permute-start.7 = (f16[2,512,128]{2,1,0:T(8,128)(2,1)S(1)}, f16[2,512,128]{2,1,0:T(8,128)(2,1)S(1)}, u32[]{:S(2)}, u32[]{:S(2)}) collective-permute-start(f16[2,512,128]{2,1,0:T(8,128)(2,1)S(1)} %add_convert_fusion.7), channel_id=1, source_target_pairs={{0,8},{2,10},{4,12},{6,14},{8,0},{10,2},{12,4},{14,6},{16,24},{18,... | collective-permute-start | bytes 786440 | tf_op jit(solution)/shard_map/ppermute | solution.py:317
  101.2 20.7 %copy-start.5 = (f32[8,512,128]{2,1,0:T(8,128)}, f32[8,512,128]{2,1,0:T(8,128)S(1)}, u32[]{:S(2)}) copy-start(f32[8,512,128]{2,1,0:T(8,128)S(1)} %get-tuple-element.101) | copy-start | bytes 6291460
  101.4 4.0 %copy-start.20 = (f16[2,512,128]{2,1,0:T(8,128)(2,1)}, f16[2,512,128]{2,1,0:T(8,128)(2,1)S(1)}, u32[]{:S(2)}) copy-start(f16[2,512,128]{2,1,0:T(8,128)(2,1)S(1)} %collective-permute-done.7) | copy-start | bytes 786436
  102.4 18.8 %copy-start.17 = (f16[4,512,128]{2,1,0:T(8,128)(2,1)}, f16[4,512,128]{2,1,0:T(8,128)(2,1)S(1)}, u32[]{:S(2)}) copy-start(f16[4,512,128]{2,1,0:T(8,128)(2,1)S(1)} %collective-permute-done.8) | copy-start | bytes 1572868
  102.5 2.7 %collective-permute-start.9 = (f16[8,512,128]{2,1,0:T(8,128)(2,1)S(1)}, f16[8,512,128]{2,1,0:T(8,128)(2,1)S(1)}, u32[]{:S(2)}, u32[]{:S(2)}) collective-permute-start(f16[8,512,128]{2,1,0:T(8,128)(2,1)S(1)} %convert_element_type.225), channel_id=1, source_target_pairs={{0,2},{2,0},{4,6},{6,4},{8,10},{10,8},{12,14},{14,12},{16,18},{18,... | collective-permute-start | bytes 3145736 | tf_op jit(solution)/shard_map/ppermute | solution.py:317
  105.4 16.5 %collective-permute-start.10 = (f16[4,512,128]{2,1,0:T(8,128)(2,1)S(1)}, f16[4,512,128]{2,1,0:T(8,128)(2,1)S(1)}, u32[]{:S(2)}, u32[]{:S(2)}) collective-permute-start(f16[4,512,128]{2,1,0:T(8,128)(2,1)S(1)} %add_convert_fusion.1), channel_id=1, source_target_pairs={{0,4},{2,6},{4,0},{6,2},{8,12},{10,14},{12,8},{14,10},{16,20},{18,... | collective-permute-start | bytes 1572872 | tf_op jit(solution)/shard_map/ppermute | solution.py:317
  106.0 15.2 %collective-permute-start.11 = (f16[2,512,128]{2,1,0:T(8,128)(2,1)S(1)}, f16[2,512,128]{2,1,0:T(8,128)(2,1)S(1)}, u32[]{:S(2)}, u32[]{:S(2)}) collective-permute-start(f16[2,512,128]{2,1,0:T(8,128)(2,1)S(1)} %add_convert_fusion.6), channel_id=1, source_target_pairs={{0,8},{2,10},{4,12},{6,14},{8,0},{10,2},{12,4},{14,6},{16,24},{18,... | collective-permute-start | bytes 786440 | tf_op jit(solution)/shard_map/ppermute | solution.py:317
  107.2 18.0 %collective-permute-start.28 = (f16[1,512,128]{2,1,0:T(8,128)(2,1)}, f16[1,512,128]{2,1,0:T(8,128)(2,1)S(1)}, u32[]{:S(2)}, u32[]{:S(2)}) collective-permute-start(f16[1,512,128]{2,1,0:T(8,128)(2,1)} %add_convert_fusion.11), channel_id=1, source_target_pairs={{0,16},{2,18},{4,20},{6,22},{8,24},{10,26},{12,28},{14,30},{16,0},... | collective-permute-start | bytes 393224 | tf_op jit(solution)/shard_map/ppermute | solution.py:317
  121.0 1.8 copy-start.3
  121.0 2.0 copy-start.8
  121.2 1.6 copy-start.21
  122.0 0.9 copy-start.15
  122.8 29.9 %collective-permute-start.12 = (f16[8,512,128]{2,1,0:T(8,128)(2,1)S(1)}, f16[8,512,128]{2,1,0:T(8,128)(2,1)S(1)}, u32[]{:S(2)}, u32[]{:S(2)}) collective-permute-start(f16[8,512,128]{2,1,0:T(8,128)(2,1)S(1)} %convert_element_type.238), channel_id=1, source_target_pairs={{0,2},{2,0},{4,6},{6,4},{8,10},{10,8},{12,14},{14,12},{16,18},{18,... | collective-permute-start | bytes 3145736 | tf_op jit(solution)/shard_map/ppermute | solution.py:317
  124.0 17.9 %copy-start.14 = (f32[512,128]{1,0:T(8,128)S(1)}, f32[512,128]{1,0:T(8,128)}, u32[]{:S(2)}) copy-start(f32[512,128]{1,0:T(8,128)} %get-tuple-element.116) | copy-start | bytes 786436
  124.0 17.9 %copy-start.22 = (f16[2,512,128]{2,1,0:T(8,128)(2,1)S(1)}, f16[2,512,128]{2,1,0:T(8,128)(2,1)}, u32[]{:S(2)}) copy-start(f16[2,512,128]{2,1,0:T(8,128)(2,1)} %copy-done.21) | copy-start | bytes 786436
  125.2 18.0 %copy-start.19 = (f16[2,512,128]{2,1,0:T(8,128)(2,1)S(1)}, f16[2,512,128]{2,1,0:T(8,128)(2,1)}, u32[]{:S(2)}) copy-start(f16[2,512,128]{2,1,0:T(8,128)(2,1)} %add_convert_fusion.5) | copy-start | bytes 786436
  125.3 27.5 %copy-start.4 = (f32[8,512,128]{2,1,0:T(8,128)S(1)}, f32[8,512,128]{2,1,0:T(8,128)}, u32[]{:S(2)}) copy-start(f32[8,512,128]{2,1,0:T(8,128)} %copy-done.3) | copy-start | bytes 6291460
  126.8 12.6 %collective-permute-start.29 = (bf16[1,512,128]{2,1,0:T(8,128)(2,1)S(1)}, bf16[1,512,128]{2,1,0:T(8,128)(2,1)S(1)}, u32[]{:S(2)}, u32[]{:S(2)}) collective-permute-start(bf16[1,512,128]{2,1,0:T(8,128)(2,1)S(1)} %get-tuple-element.131), channel_id=1, source_target_pairs={{0,16},{2,18},{4,20},{6,22},{8,24},{10,26},{12,28},{14,30},{16,0},... | collective-permute-start | bytes 393224 | tf_op jit(solution)/shard_map/ppermute | solution.py:317
  127.2 14.7 %collective-permute-start.24 = (f16[1,512,128]{2,1,0:T(8,128)(2,1)}, f16[1,512,128]{2,1,0:T(8,128)(2,1)S(1)}, u32[]{:S(2)}, u32[]{:S(2)}) collective-permute-start(f16[1,512,128]{2,1,0:T(8,128)(2,1)} %add_convert_fusion.10), channel_id=1, source_target_pairs={{0,16},{2,18},{4,20},{6,22},{8,24},{10,26},{12,28},{14,30},{16,0},... | collective-permute-start | bytes 393224 | tf_op jit(solution)/shard_map/ppermute | solution.py:317
  139.4 10.8 %collective-permute-start.30 = (bf16[2,512,128]{2,1,0:T(8,128)(2,1)S(1)}, bf16[2,512,128]{2,1,0:T(8,128)(2,1)S(1)}, u32[]{:S(2)}, u32[]{:S(2)}) collective-permute-start(bf16[2,512,128]{2,1,0:T(8,128)(2,1)S(1)} %pad_maximum_fusion.8), channel_id=1, source_target_pairs={{0,8},{2,10},{4,12},{6,14},{8,0},{10,2},{12,4},{14,6},{16,24},{18,... | collective-permute-start | bytes 786440 | tf_op jit(solution)/shard_map/ppermute | solution.py:317
  139.5 16.4 %copy-start.16 = (f16[4,512,128]{2,1,0:T(8,128)(2,1)S(1)}, f16[4,512,128]{2,1,0:T(8,128)(2,1)}, u32[]{:S(2)}) copy-start(f16[4,512,128]{2,1,0:T(8,128)(2,1)} %copy-done.15) | copy-start | bytes 1572868
  143.1 21.4 %copy-start.13 = (f32[512,128]{1,0:T(8,128)S(1)}, f32[512,128]{1,0:T(8,128)}, u32[]{:S(2)}) copy-start(f32[512,128]{1,0:T(8,128)} %get-tuple-element.113) | copy-start | bytes 786436
  143.1 13.9 %collective-permute-start.25 = (bf16[1,512,128]{2,1,0:T(8,128)(2,1)S(1)}, bf16[1,512,128]{2,1,0:T(8,128)(2,1)S(1)}, u32[]{:S(2)}, u32[]{:S(2)}) collective-permute-start(bf16[1,512,128]{2,1,0:T(8,128)(2,1)S(1)} %get-tuple-element.133), channel_id=1, source_target_pairs={{0,16},{2,18},{4,20},{6,22},{8,24},{10,26},{12,28},{14,30},{16,0},... | collective-permute-start | bytes 393224 | tf_op jit(solution)/shard_map/ppermute | solution.py:317
  143.2 12.7 %collective-permute-start.19 = (f16[2,512,128]{2,1,0:T(8,128)(2,1)S(1)}, f16[2,512,128]{2,1,0:T(8,128)(2,1)S(1)}, u32[]{:S(2)}, u32[]{:S(2)}) collective-permute-start(f16[2,512,128]{2,1,0:T(8,128)(2,1)S(1)} %copy-done.19), channel_id=1, source_target_pairs={{0,8},{2,10},{4,12},{6,14},{8,0},{10,2},{12,4},{14,6},{16,24},{18,... | collective-permute-start | bytes 786440 | tf_op jit(solution)/shard_map/ppermute | solution.py:317
  150.2 15.5 %collective-permute-start.31 = (bf16[4,512,128]{2,1,0:T(8,128)(2,1)S(1)}, bf16[4,512,128]{2,1,0:T(8,128)(2,1)S(1)}, u32[]{:S(2)}, u32[]{:S(2)}) collective-permute-start(bf16[4,512,128]{2,1,0:T(8,128)(2,1)S(1)} %pad_maximum_fusion.4.refs_0_), channel_id=1, source_target_pairs={{0,4},{2,6},{4,0},{6,2},{8,12},{10,14},{12,8},{14,10},{16,20},{18,... | collective-permute-start | bytes 1572872 | tf_op jit(solution)/shard_map/ppermute | solution.py:317
  152.9 18.8 %collective-permute-start.13 = (f16[4,512,128]{2,1,0:T(8,128)(2,1)S(1)}, f16[4,512,128]{2,1,0:T(8,128)(2,1)S(1)}, u32[]{:S(2)}, u32[]{:S(2)}) collective-permute-start(f16[4,512,128]{2,1,0:T(8,128)(2,1)S(1)} %add_convert_fusion), channel_id=1, source_target_pairs={{0,4},{2,6},{4,0},{6,2},{8,12},{10,14},{12,8},{14,10},{16,20},{18,... | collective-permute-start | bytes 1572872 | tf_op jit(solution)/shard_map/ppermute | solution.py:317
  156.9 7.6 %collective-permute-start.20 = (f16[1,512,128]{2,1,0:T(8,128)(2,1)S(1)}, f16[1,512,128]{2,1,0:T(8,128)(2,1)S(1)}, u32[]{:S(2)}, u32[]{:S(2)}) collective-permute-start(f16[1,512,128]{2,1,0:T(8,128)(2,1)S(1)} %add_convert_fusion.8), channel_id=1, source_target_pairs={{0,16},{2,18},{4,20},{6,22},{8,24},{10,26},{12,28},{14,30},{16,0},... | collective-permute-start | bytes 393224 | tf_op jit(solution)/shard_map/ppermute | solution.py:317
  157.0 28.3 %collective-permute-start.32 = (bf16[4,512,128]{2,1,0:T(8,128)(2,1)S(1)}, bf16[4,512,128]{2,1,0:T(8,128)(2,1)S(1)}, u32[]{:S(2)}, u32[]{:S(2)}) collective-permute-start(bf16[4,512,128]{2,1,0:T(8,128)(2,1)S(1)} %pad_maximum_fusion.4.refs_0_), channel_id=1, source_target_pairs={{0,2},{2,0},{4,6},{6,4},{8,10},{10,8},{12,14},{14,12},{16,18},{18,... | collective-permute-start | bytes 1572872 | tf_op jit(solution)/shard_map/ppermute | solution.py:317
  157.1 15.0 %collective-permute-start.26 = (bf16[2,512,128]{2,1,0:T(8,128)(2,1)S(1)}, bf16[2,512,128]{2,1,0:T(8,128)(2,1)S(1)}, u32[]{:S(2)}, u32[]{:S(2)}) collective-permute-start(bf16[2,512,128]{2,1,0:T(8,128)(2,1)S(1)} %pad_maximum_fusion.7), channel_id=1, source_target_pairs={{0,8},{2,10},{4,12},{6,14},{8,0},{10,2},{12,4},{14,6},{16,24},{18,... | collective-permute-start | bytes 786440 | tf_op jit(solution)/shard_map/ppermute | solution.py:317
  165.6 8.2 %collective-permute-start.21 = (bf16[1,512,128]{2,1,0:T(8,128)(2,1)S(1)}, bf16[1,512,128]{2,1,0:T(8,128)(2,1)S(1)}, u32[]{:S(2)}, u32[]{:S(2)}) collective-permute-start(bf16[1,512,128]{2,1,0:T(8,128)(2,1)S(1)} %get-tuple-element.135), channel_id=1, source_target_pairs={{0,16},{2,18},{4,20},{6,22},{8,24},{10,26},{12,28},{14,30},{16,0},... | collective-permute-start | bytes 393224 | tf_op jit(solution)/shard_map/ppermute | solution.py:317
  165.7 20.0 %collective-permute-start.33 = (bf16[4,512,128]{2,1,0:T(8,128)(2,1)S(1)}, bf16[4,512,128]{2,1,0:T(8,128)(2,1)S(1)}, u32[]{:S(2)}, u32[]{:S(2)}) collective-permute-start(bf16[4,512,128]{2,1,0:T(8,128)(2,1)S(1)} %collective-permute-done.31.refs_1_), channel_id=1, source_target_pairs={{0,2},{2,0},{4,6},{6,4},{8,10},{10,8},{12,14},{14,12},{16,18},{18,... | collective-permute-start | bytes 1572872 | tf_op jit(solution)/shard_map/ppermute | solution.py:317
  171.8 9.6 %collective-permute-start.14 = (f16[2,512,128]{2,1,0:T(8,128)(2,1)S(1)}, f16[2,512,128]{2,1,0:T(8,128)(2,1)S(1)}, u32[]{:S(2)}, u32[]{:S(2)}) collective-permute-start(f16[2,512,128]{2,1,0:T(8,128)(2,1)S(1)} %add_convert_fusion.4), channel_id=1, source_target_pairs={{0,8},{2,10},{4,12},{6,14},{8,0},{10,2},{12,4},{14,6},{16,24},{18,... | collective-permute-start | bytes 786440 | tf_op jit(solution)/shard_map/ppermute | solution.py:317
  172.2 15.0 %collective-permute-start.27 = (bf16[4,512,128]{2,1,0:T(8,128)(2,1)S(1)}, bf16[4,512,128]{2,1,0:T(8,128)(2,1)S(1)}, u32[]{:S(2)}, u32[]{:S(2)}) collective-permute-start(bf16[4,512,128]{2,1,0:T(8,128)(2,1)S(1)} %pad_maximum_fusion.3.refs_0_), channel_id=1, source_target_pairs={{0,4},{2,6},{4,0},{6,2},{8,12},{10,14},{12,8},{14,10},{16,20},{18,... | collective-permute-start | bytes 1572872 | tf_op jit(solution)/shard_map/ppermute | solution.py:317
  173.9 11.4 %collective-permute-start.22 = (bf16[2,512,128]{2,1,0:T(8,128)(2,1)S(1)}, bf16[2,512,128]{2,1,0:T(8,128)(2,1)S(1)}, u32[]{:S(2)}, u32[]{:S(2)}) collective-permute-start(bf16[2,512,128]{2,1,0:T(8,128)(2,1)S(1)} %pad_maximum_fusion.6), channel_id=1, source_target_pairs={{0,8},{2,10},{4,12},{6,14},{8,0},{10,2},{12,4},{14,6},{16,24},{18,... | collective-permute-start | bytes 786440 | tf_op jit(solution)/shard_map/ppermute | solution.py:317
  181.5 6.3 %collective-permute-start.15 = (f16[1,512,128]{2,1,0:T(8,128)(2,1)S(1)}, f16[1,512,128]{2,1,0:T(8,128)(2,1)S(1)}, u32[]{:S(2)}, u32[]{:S(2)}) collective-permute-start(f16[1,512,128]{2,1,0:T(8,128)(2,1)S(1)} %add_convert_fusion.9), channel_id=1, source_target_pairs={{0,16},{2,18},{4,20},{6,22},{8,24},{10,26},{12,28},{14,30},{16,0},... | collective-permute-start | bytes 393224 | tf_op jit(solution)/shard_map/ppermute | solution.py:317
  185.2 11.8 %collective-permute-start.34 = (bf16[4,512,128]{2,1,0:T(8,128)(2,1)S(1)}, bf16[4,512,128]{2,1,0:T(8,128)(2,1)S(1)}, u32[]{:S(2)}, u32[]{:S(2)}) collective-permute-start(bf16[4,512,128]{2,1,0:T(8,128)(2,1)S(1)} %pad_maximum_fusion.3.refs_0_), channel_id=1, source_target_pairs={{0,2},{2,0},{4,6},{6,4},{8,10},{10,8},{12,14},{14,12},{16,18},{18,... | collective-permute-start | bytes 1572872 | tf_op jit(solution)/shard_map/ppermute | solution.py:317
  185.3 2.5 %copy-start.12 = (f32[512,128]{1,0:T(8,128)S(1)}, f32[512,128]{1,0:T(8,128)}, u32[]{:S(2)}) copy-start(f32[512,128]{1,0:T(8,128)} %get-tuple-element.110) | copy-start | bytes 786436
  185.3 14.4 %collective-permute-start.23 = (bf16[4,512,128]{2,1,0:T(8,128)(2,1)S(1)}, bf16[4,512,128]{2,1,0:T(8,128)(2,1)S(1)}, u32[]{:S(2)}, u32[]{:S(2)}) collective-permute-start(bf16[4,512,128]{2,1,0:T(8,128)(2,1)S(1)} %pad_maximum_fusion.2.refs_0_), channel_id=1, source_target_pairs={{0,4},{2,6},{4,0},{6,2},{8,12},{10,14},{12,8},{14,10},{16,20},{18,... | collective-permute-start | bytes 1572872 | tf_op jit(solution)/shard_map/ppermute | solution.py:317
  187.1 9.9 %collective-permute-start.35 = (bf16[4,512,128]{2,1,0:T(8,128)(2,1)S(1)}, bf16[4,512,128]{2,1,0:T(8,128)(2,1)S(1)}, u32[]{:S(2)}, u32[]{:S(2)}) collective-permute-start(bf16[4,512,128]{2,1,0:T(8,128)(2,1)S(1)} %collective-permute-done.27.refs_1_), channel_id=1, source_target_pairs={{0,2},{2,0},{4,6},{6,4},{8,10},{10,8},{12,14},{14,12},{16,18},{18,... | collective-permute-start | bytes 1572872 | tf_op jit(solution)/shard_map/ppermute | solution.py:317
  188.0 8.8 %collective-permute-start.16 = (bf16[1,512,128]{2,1,0:T(8,128)(2,1)S(1)}, bf16[1,512,128]{2,1,0:T(8,128)(2,1)S(1)}, u32[]{:S(2)}, u32[]{:S(2)}) collective-permute-start(bf16[1,512,128]{2,1,0:T(8,128)(2,1)S(1)} %get-tuple-element.137), channel_id=1, source_target_pairs={{0,16},{2,18},{4,20},{6,22},{8,24},{10,26},{12,28},{14,30},{16,0},... | collective-permute-start | bytes 393224 | tf_op jit(solution)/shard_map/ppermute | solution.py:317
  196.8 8.3 %collective-permute-start.17 = (bf16[2,512,128]{2,1,0:T(8,128)(2,1)S(1)}, bf16[2,512,128]{2,1,0:T(8,128)(2,1)S(1)}, u32[]{:S(2)}, u32[]{:S(2)}) collective-permute-start(bf16[2,512,128]{2,1,0:T(8,128)(2,1)S(1)} %pad_maximum_fusion.5), channel_id=1, source_target_pairs={{0,8},{2,10},{4,12},{6,14},{8,0},{10,2},{12,4},{14,6},{16,24},{18,... | collective-permute-start | bytes 786440 | tf_op jit(solution)/shard_map/ppermute | solution.py:317
  196.9 10.3 %collective-permute-start.36 = (bf16[4,512,128]{2,1,0:T(8,128)(2,1)S(1)}, bf16[4,512,128]{2,1,0:T(8,128)(2,1)S(1)}, u32[]{:S(2)}, u32[]{:S(2)}) collective-permute-start(bf16[4,512,128]{2,1,0:T(8,128)(2,1)S(1)} %pad_maximum_fusion.2.refs_0_), channel_id=1, source_target_pairs={{0,2},{2,0},{4,6},{6,4},{8,10},{10,8},{12,14},{14,12},{16,18},{18,... | collective-permute-start | bytes 1572872 | tf_op jit(solution)/shard_map/ppermute | solution.py:317
  199.7 7.5 %collective-permute-start.37 = (bf16[4,512,128]{2,1,0:T(8,128)(2,1)S(1)}, bf16[4,512,128]{2,1,0:T(8,128)(2,1)S(1)}, u32[]{:S(2)}, u32[]{:S(2)}) collective-permute-start(bf16[4,512,128]{2,1,0:T(8,128)(2,1)S(1)} %collective-permute-done.23.refs_1_), channel_id=1, source_target_pairs={{0,2},{2,0},{4,6},{6,4},{8,10},{10,8},{12,14},{14,12},{16,18},{18,... | collective-permute-start | bytes 1572872 | tf_op jit(solution)/shard_map/ppermute | solution.py:317
  205.2 13.4 %collective-permute-start.18 = (bf16[4,512,128]{2,1,0:T(8,128)(2,1)S(1)}, bf16[4,512,128]{2,1,0:T(8,128)(2,1)S(1)}, u32[]{:S(2)}, u32[]{:S(2)}) collective-permute-start(bf16[4,512,128]{2,1,0:T(8,128)(2,1)S(1)} %pad_maximum_fusion.1.refs_0_), channel_id=1, source_target_pairs={{0,4},{2,6},{4,0},{6,2},{8,12},{10,14},{12,8},{14,10},{16,20},{18,... | collective-permute-start | bytes 1572872 | tf_op jit(solution)/shard_map/ppermute | solution.py:317
  208.7 10.9 %collective-permute-start.38 = (bf16[4,512,128]{2,1,0:T(8,128)(2,1)S(1)}, bf16[4,512,128]{2,1,0:T(8,128)(2,1)S(1)}, u32[]{:S(2)}, u32[]{:S(2)}) collective-permute-start(bf16[4,512,128]{2,1,0:T(8,128)(2,1)S(1)} %pad_maximum_fusion.1.refs_0_), channel_id=1, source_target_pairs={{0,2},{2,0},{4,6},{6,4},{8,10},{10,8},{12,14},{14,12},{16,18},{18,... | collective-permute-start | bytes 1572872 | tf_op jit(solution)/shard_map/ppermute | solution.py:317
  218.5 1.9 collective-permute-start.39

commit v4 on v3

--- a/solution.py
+++ b/solution.py
@@ -371,21 +371,24 @@
             chunk, width, token, banks, turned, start, first, second, products, target, count, tokens
         )
         send = send.astype(WIRE)
+        last = chunk + 1 == chunks
         moving = {}
         for earlier in range(max(chunk - bits + 2, 0), chunk):
             outgoing, terms = halved(live[earlier])
             outgoing, send = tied(outgoing, send)
             moving[earlier] = (outgoing, terms)
-        outgoing, terms = halved([keep, swapped(send, 0)])
-        moving[chunk] = (outgoing, terms)
-        if chunk + 1 < chunks:
+        moving[chunk] = halved([keep, swapped(send, 0)])
+        if not last:
             formed, token = tied([outgoing for outgoing, _ in moving.values()], token)
-            moving = {
-                which: (outgoing, terms)
-                for (which, (_, terms)), outgoing in zip(moving.items(), formed)
-            }
+            for (which, (_, terms)), outgoing in zip(moving.items(), formed):
+                live[which] = terms + [swapped(outgoing, chunk - which + 1)]
+            continue
+        head, terms = moving.pop(chunk)
+        live[chunk] = terms + [swapped(head, 1)]
         for which, (outgoing, terms) in moving.items():
             live[which] = terms + [swapped(outgoing, chunk - which + 1)]
+        for which in range(chunk):
+            live[which][-1], _ = tied(live[which][-1], head)
 
     for chunk in range(chunks):
         terms = live[chunk]
@@ -393,22 +396,20 @@
             outgoing, terms = halved(terms)
             terms = terms + [swapped(outgoing, bit)]
         total = sum(term.astype(F32) for term in terms)[0]
-
         average = total * (1.0 / (WIRE_SCALE * reps))
         moved = 0.9 * shares[chunk][0] + average
+        fresh = (shares[chunk][1].astype(F32) - 0.7 * (average + 0.9 * moved)).astype(BF16)
         new_momentum.append(moved)
-        fresh = (shares[chunk][1].astype(F32) - 0.7 * (average + 0.9 * moved)).astype(BF16)
-
         stack = fresh[None]
         offsets = [0]
         for bit in range(bits - 1, 1, -1):
             stack = jnp.concatenate([stack, swapped(stack, bit)])
             offsets = offsets + [offset ^ (1 << bit) for offset in offsets]
         across = swapped(stack, 1)
+        offsets = [[offset ^ low for offset in offsets] for low in (0, 2, 1, 3)]
         if result:
             across, *result = tied(across, result[0])
         received = [stack, across, swapped(stack, 0), swapped(across, 0)]
-        offsets = [[offset ^ low for offset in offsets] for low in (0, 2, 1, 3)]
         result = (
             assemble(chunk, place, received, offsets, (reps, rows, columns), result),
         )

time: 223 us -> 222 us (level)
  waiting for transfers between devices: 105 us -> 96.8 us
  starting transfers between devices: 27.5 us -> 31 us
  other arithmetic: 12.8 us -> 15.1 us
    ppermute x36, waiting for transfers between devices: 80.2 us -> 72.2 us  [swapped(): return lax.ppermute(array, 'rep', pairs)]
    ppermute x36, starting transfers between devices: 22.5 us -> 26 us  [swapped(): return lax.ppermute(array, 'rep', pairs)]
  transfers between devices with their start and end apart: 40 -> 40, of which waited for: 22 -> 23; matrix products, arithmetic and copies ran while one was open for 8% -> 9% of each run, Pallas kernels for 22% -> 22%
where the time goes in v4:
time: 222 us; the launch traced here: 221 us
  waiting for transfers between devices  96.8 us (44%)
  Pallas kernels  63.7 us (29%)
  starting transfers between devices  31 us (14%)
  other arithmetic  15.1 us (7%)
  local copies, waits for them, and re-layouts  12.7 us (6%)
    ppermute x36, waiting for transfers between devices, swapped(): return lax.ppermute(array, 'rep', pairs)  72.2 us
    pallas_call x4, Pallas kernels, inner(): pl.pallas_call(functools.partial(inner_kernel, float(tokens)), grid_spec=...  44.3 us
    ppermute x36, starting transfers between devices, swapped(): return lax.ppermute(array, 'rep', pairs)  26 us
    ppermute x4, waiting for transfers between devices, per_device(): parts.append(lax.ppermute(part, 'fsdp', [(0, 1), (1, 0)]))  24.6 us
    pallas_call x4, Pallas kernels, arrive(): pl.pallas_call(functools.partial(arrive_kernel, piece), grid=(1,), in_spe...  8.66 us
    convert_element_type x12, other arithmetic, halved(): outgoing = sum((term[middle:].astype(F32) for term in terms)).astype(WIRE)  6.14 us
    pallas_call x4, Pallas kernels, assemble(): pl.pallas_call(functools.partial(assemble_kernel, chunk, offsets), in_spe...  5.76 us
    slice x4, local copies, waits for them, and re-layouts, per_device(): part, source = tied(source[:, d * block:(d + 1) * block], source)  5.63 us
  transfers between devices with their start and end apart: 40, of which 23 were waited for; matrix products, arithmetic and copies ran while one was open for 9% of the time, Pallas kernels for 22%

profile of v4, /device:TPU:0, one launch (start us, length us, event | category | flops | bytes accessed | tf_op | source)
XLA Modules:
  0.0 220.6 jit_solution(9577509263660769014)
XLA Ops:
  0.7 2.0 slice.344
  2.7 1.9 slice.277
  4.6 3.0 %collective-permute-start.2 = (bf16[128,2048]{1,0:T(8,128)(2,1)}, bf16[128,2048]{1,0:T(8,128)(2,1)}, u32[]{:S(2)}, u32[]{:S(2)}) collective-permute-start(bf16[128,2048]{1,0:T(8,128)(2,1)} %slice.277), channel_id=1, source_target_pairs={{0,1},{1,0},{2,3},{3,2},{4,5},{5,4},{6,7},{7,6},{8,9},{9,8},{10,11... | collective-permute-start | bytes 1572872 | tf_op jit(solution)/shard_map/ppermute | solution.py:330
  8.5 2.0 collective-permute-start.1
  12.2 5.0 %forward.1 = (bf16[8192,128]{1,0:T(8,128)(2,1)S(1)}, f32[128,512]{1,0:T(8,128)S(1)}) custom-call(bf16[128,8192]{1,0:T(8,128)(2,1)S(1)} %bitcast.89, bf16[8192,512]{1,0:T(8,128)(2,1)} %weights_ref.9), custom_call_target="tpu_custom_call" | custom-call | flops 1073741824 | bytes 12582912 | tf_op jit(solution)/shard_map/forward/pallas_call | solution.py:34
  17.2 1.3 copy-done.1
  20.2 1.1 maximum_select_fusion.target_ref
  21.3 1.0 broadcast_select_fusion.count_ref
  22.3 9.6 %collective-permute-done.3.part_ref = bf16[128,2048]{1,0:T(8,128)(2,1)} collective-permute-done((bf16[128,2048]{1,0:T(8,128)(2,1)}, bf16[128,2048]{1,0:T(8,128)(2,1)}, u32[]{:S(2)}, u32[]{:S(2)}) %collective-permute-start.3) | collective-permute-done | bytes 524320 | tf_op jit(solution)/shard_map/ppermute | solution.py:330
  31.9 2.2 %arrive.4 = (bf16[128,8192]{1,0:T(8,128)(2,1)S(1)}, bf16[8192,128]{1,0:T(8,128)(2,1)S(1)}, f32[128,512]{1,0:T(8,128)S(1)}) custom-call(bf16[128,2048]{1,0:T(8,128)(2,1)} %collective-permute-done.3.part_ref, bf16[8192,512]{1,0:T(8,128)(2,1)} %weights_ref.9), custom_call_target="tpu_custom_call" | custom-call | flops 268435456 | bytes 3670016 | tf_op jit(solution)/shard_map/arrive/pallas_call | solution.py:76
  34.1 2.2 %arrive.5 = (bf16[128,8192]{1,0:T(8,128)(2,1)S(1)}, bf16[8192,128]{1,0:T(8,128)(2,1)S(1)}, f32[128,512]{1,0:T(8,128)S(1)}) custom-call(bf16[128,2048]{1,0:T(8,128)(2,1)} %collective-permute-done.2.part_ref, bf16[8192,512]{1,0:T(8,128)(2,1)} %weights_ref.9, ...), custom_call_target="tpu_custom_call", output_to_operand_aliasing={{0}: (2, {}), {1}: (3, {}), {2}: (4, {})} | custom-call | flops 268435456 | bytes 3670016 | tf_op jit(solution)/shard_map/arrive/pallas_call | solution.py:76
  36.3 6.7 %collective-permute-done.1.part_ref = bf16[128,2048]{1,0:T(8,128)(2,1)S(1)} collective-permute-done((bf16[128,2048]{1,0:T(8,128)(2,1)}, bf16[128,2048]{1,0:T(8,128)(2,1)S(1)}, u32[]{:S(2)}, u32[]{:S(2)}) %collective-permute-start.1) | collective-permute-done | bytes 524320 | tf_op jit(solution)/shard_map/ppermute | solution.py:330
  43.0 2.0 arrive.6
  45.1 8.4 %collective-permute-done.part_ref = bf16[128,2048]{1,0:T(8,128)(2,1)S(1)} collective-permute-done((bf16[128,2048]{1,0:T(8,128)(2,1)}, bf16[128,2048]{1,0:T(8,128)(2,1)S(1)}, u32[]{:S(2)}, u32[]{:S(2)}) %collective-permute-start) | collective-permute-done | bytes 524320 | tf_op jit(solution)/shard_map/ppermute | solution.py:330
  53.4 2.2 arrive.7
  55.7 11.0 %inner.4 = (f32[8,512,128]{2,1,0:T(8,128)S(1)}, f32[8,512,128]{2,1,0:T(8,128)S(1)}) custom-call(s32[1]{0:T(128)} %bitcast.mine_ref.place_ref, bf16[128,8192]{1,0:T(8,128)(2,1)S(1)} %bitcast.90, bf16[128,8192]{1,0:T(8,128)(2,1)S(1)} %get-tuple-element.84.high_ref, bf16[4,2,2,512,128]{4,3,2,1,0:T(8,128)(2,1)S(1)} %bitcast.94, ...), custom_call_target="tpu_custom_call" | custom-call | flops 1610612736 | bytes 20971520 | tf_op jit(solution)/shard_map/inner/pallas_call | solution.py:218
  66.9 2.6 %collective-permute-done.4 = f16[8,512,128]{2,1,0:T(8,128)(2,1)S(1)} collective-permute-done((f16[8,512,128]{2,1,0:T(8,128)(2,1)S(1)}, f16[8,512,128]{2,1,0:T(8,128)(2,1)S(1)}, u32[]{:S(2)}, u32[]{:S(2)}) %collective-permute-start.4) | collective-permute-done | bytes 1048608 | tf_op jit(solution)/shard_map/ppermute | solution.py:317
  69.7 1.8 collective-permute-start.5
  71.5 11.0 %inner.5 = (f32[8,512,128]{2,1,0:T(8,128)S(1)}, f32[8,512,128]{2,1,0:T(8,128)S(1)}) custom-call(s32[1]{0:T(128)} %bitcast.mine_ref.place_ref, bf16[128,8192]{1,0:T(8,128)(2,1)S(1)} %bitcast.91, bf16[128,8192]{1,0:T(8,128)(2,1)S(1)} %get-tuple-element.84.high_ref, bf16[4,2,2,512,128]{4,3,2,1,0:T(8,128)(2,1)S(1)} %bitcast.95, ...), custom_call_target="tpu_custom_call" | custom-call | flops 1610612736 | bytes 20971520 | tf_op jit(solution)/shard_map/inner/pallas_call | solution.py:218
  82.7 1.1 collective-permute-done.5
  84.0 2.6 %collective-permute-done.6 = f16[8,512,128]{2,1,0:T(8,128)(2,1)S(1)} collective-permute-done((f16[8,512,128]{2,1,0:T(8,128)(2,1)S(1)}, f16[8,512,128]{2,1,0:T(8,128)(2,1)S(1)}, u32[]{:S(2)}, u32[]{:S(2)}) %collective-permute-start.6) | collective-permute-done | bytes 1048608 | tf_op jit(solution)/shard_map/ppermute | solution.py:317
  86.8 1.8 collective-permute-start.8
  88.5 1.6 collective-permute-start.7
  90.1 11.0 %inner.6 = (f32[8,512,128]{2,1,0:T(8,128)S(1)}, f32[8,512,128]{2,1,0:T(8,128)S(1)}) custom-call(s32[1]{0:T(128)} %bitcast.mine_ref.place_ref, bf16[128,8192]{1,0:T(8,128)(2,1)S(1)} %bitcast.92, bf16[128,8192]{1,0:T(8,128)(2,1)S(1)} %get-tuple-element.84.high_ref, bf16[4,2,2,512,128]{4,3,2,1,0:T(8,128)(2,1)S(1)} %bitcast.96, ...), custom_call_target="tpu_custom_call" | custom-call | flops 1610612736 | bytes 20971520 | tf_op jit(solution)/shard_map/inner/pallas_call | solution.py:218
  101.7 2.6 %collective-permute-done.9 = f16[8,512,128]{2,1,0:T(8,128)(2,1)S(1)} collective-permute-done((f16[8,512,128]{2,1,0:T(8,128)(2,1)S(1)}, f16[8,512,128]{2,1,0:T(8,128)(2,1)S(1)}, u32[]{:S(2)}, u32[]{:S(2)}) %collective-permute-start.9) | collective-permute-done | bytes 1048608 | tf_op jit(solution)/shard_map/ppermute | solution.py:317
  104.5 1.1 collective-permute-start.10
  105.6 1.6 collective-permute-start.11
  107.2 11.2 %inner.7 = (f32[8,512,128]{2,1,0:T(8,128)S(1)}, f32[8,512,128]{2,1,0:T(8,128)S(1)}) custom-call(s32[1]{0:T(128)} %bitcast.mine_ref.place_ref, bf16[128,8192]{1,0:T(8,128)(2,1)S(1)} %bitcast.93, bf16[128,8192]{1,0:T(8,128)(2,1)S(1)} %get-tuple-element.84.high_ref, bf16[4,2,2,512,128]{4,3,2,1,0:T(8,128)(2,1)S(1)} %bitcast.97, ...), custom_call_target="tpu_custom_call" | custom-call | flops 1610612736 | bytes 20971520 | tf_op jit(solution)/shard_map/inner/pallas_call | solution.py:218
  120.4 1.3 constant_dynamic-slice_fusion
  121.7 1.3 fusion.16
  123.0 2.7 %collective-permute-start.28 = (f16[1,512,128]{2,1,0:T(8,128)(2,1)S(1)}, f16[1,512,128]{2,1,0:T(8,128)(2,1)S(1)}, u32[]{:S(2)}, u32[]{:S(2)}) collective-permute-start(f16[1,512,128]{2,1,0:T(8,128)(2,1)S(1)} %add_convert_fusion.11), channel_id=1, source_target_pairs={{0,16},{2,18},{4,20},{6,22},{8,24},{10,26},{12,28},{14,30},{16,0},... | collective-permute-start | bytes 393224 | tf_op jit(solution)/shard_map/ppermute | solution.py:317
  126.0 1.2 add_convert_fusion
  127.2 8.2 %collective-permute-done.28 = f16[1,512,128]{2,1,0:T(8,128)(2,1)S(1)} collective-permute-done((f16[1,512,128]{2,1,0:T(8,128)(2,1)S(1)}, f16[1,512,128]{2,1,0:T(8,128)(2,1)S(1)}, u32[]{:S(2)}, u32[]{:S(2)}) %collective-permute-start.28) | collective-permute-done | bytes 131104 | tf_op jit(solution)/shard_map/ppermute | solution.py:317
  135.4 1.2 bitcast_add_fusion.1
  136.7 3.5 %collective-permute-start.19 = (f16[2,512,128]{2,1,0:T(8,128)(2,1)S(1)}, f16[2,512,128]{2,1,0:T(8,128)(2,1)S(1)}, u32[]{:S(2)}, u32[]{:S(2)}) collective-permute-start(f16[2,512,128]{2,1,0:T(8,128)(2,1)S(1)} %add_convert_fusion.5), channel_id=1, source_target_pairs={{0,8},{2,10},{4,12},{6,14},{8,0},{10,2},{12,4},{14,6},{16,24},{18,... | collective-permute-start | bytes 786440 | tf_op jit(solution)/shard_map/ppermute | solution.py:317
  140.2 1.1 collective-permute-start.13
  141.3 4.2 %collective-permute-done.29 = bf16[1,512,128]{2,1,0:T(8,128)(2,1)S(1)} collective-permute-done((bf16[1,512,128]{2,1,0:T(8,128)(2,1)S(1)}, bf16[1,512,128]{2,1,0:T(8,128)(2,1)S(1)}, u32[]{:S(2)}, u32[]{:S(2)}) %collective-permute-start.29) | collective-permute-done | bytes 131104 | tf_op jit(solution)/shard_map/ppermute | solution.py:317
  145.7 1.2 bitcast_add_fusion.3
  146.9 1.9 collective-permute-done.19
  149.1 1.1 add_convert_fusion.8
  150.2 2.7 %collective-permute-start.20 = (f16[1,512,128]{2,1,0:T(8,128)(2,1)S(1)}, f16[1,512,128]{2,1,0:T(8,128)(2,1)S(1)}, u32[]{:S(2)}, u32[]{:S(2)}) collective-permute-start(f16[1,512,128]{2,1,0:T(8,128)(2,1)S(1)} %add_convert_fusion.8), channel_id=1, source_target_pairs={{0,16},{2,18},{4,20},{6,22},{8,24},{10,26},{12,28},{14,30},{16,0},... | collective-permute-start | bytes 393224 | tf_op jit(solution)/shard_map/ppermute | solution.py:317
  152.9 3.6 %collective-permute-done.30 = bf16[2,512,128]{2,1,0:T(8,128)(2,1)S(1)} collective-permute-done((bf16[2,512,128]{2,1,0:T(8,128)(2,1)S(1)}, bf16[2,512,128]{2,1,0:T(8,128)(2,1)S(1)}, u32[]{:S(2)}, u32[]{:S(2)}) %collective-permute-start.30) | collective-permute-done | bytes 262176 | tf_op jit(solution)/shard_map/ppermute | solution.py:317
  156.6 1.7 collective-permute-start.31
  158.3 3.3 %collective-permute-done.25 = bf16[1,512,128]{2,1,0:T(8,128)(2,1)S(1)} collective-permute-done((bf16[1,512,128]{2,1,0:T(8,128)(2,1)S(1)}, bf16[1,512,128]{2,1,0:T(8,128)(2,1)S(1)}, u32[]{:S(2)}, u32[]{:S(2)}) %collective-permute-start.25) | collective-permute-done | bytes 131104 | tf_op jit(solution)/shard_map/ppermute | solution.py:317
  161.7 1.3 collective-permute-done.20
  163.0 1.2 bitcast_add_fusion.5
  165.1 1.1 add_convert_fusion.4
  166.2 1.7 collective-permute-start.14
  167.8 2.1 collective-permute-done.31.refs_1_
  169.9 2.2 %collective-permute-done.26 = bf16[2,512,128]{2,1,0:T(8,128)(2,1)S(1)} collective-permute-done((bf16[2,512,128]{2,1,0:T(8,128)(2,1)S(1)}, bf16[2,512,128]{2,1,0:T(8,128)(2,1)S(1)}, u32[]{:S(2)}, u32[]{:S(2)}) %collective-permute-start.26) | collective-permute-done | bytes 262176 | tf_op jit(solution)/shard_map/ppermute | solution.py:317
  172.4 5.4 %collective-permute-done.14 = f16[2,512,128]{2,1,0:T(8,128)(2,1)S(1)} collective-permute-done((f16[2,512,128]{2,1,0:T(8,128)(2,1)S(1)}, f16[2,512,128]{2,1,0:T(8,128)(2,1)S(1)}, u32[]{:S(2)}, u32[]{:S(2)}) %collective-permute-start.14) | collective-permute-done | bytes 262176 | tf_op jit(solution)/shard_map/ppermute | solution.py:317
  177.8 1.0 add_convert_fusion.9
  178.8 5.0 %collective-permute-done.22 = bf16[2,512,128]{2,1,0:T(8,128)(2,1)S(1)} collective-permute-done((bf16[2,512,128]{2,1,0:T(8,128)(2,1)S(1)}, bf16[2,512,128]{2,1,0:T(8,128)(2,1)S(1)}, u32[]{:S(2)}, u32[]{:S(2)}) %collective-permute-start.22) | collective-permute-done | bytes 262176 | tf_op jit(solution)/shard_map/ppermute | solution.py:317
  184.0 1.4 assemble.4.refs_4_
  186.4 1.1 bitcast_add_fusion.7
  187.5 8.2 %collective-permute-done.16 = bf16[1,512,128]{2,1,0:T(8,128)(2,1)S(1)} collective-permute-done((bf16[1,512,128]{2,1,0:T(8,128)(2,1)S(1)}, bf16[1,512,128]{2,1,0:T(8,128)(2,1)S(1)}, u32[]{:S(2)}, u32[]{:S(2)}) %collective-permute-start.16) | collective-permute-done | bytes 131104 | tf_op jit(solution)/shard_map/ppermute | solution.py:317
  195.9 1.4 assemble.5.refs_4_
  197.3 1.0 collective-permute-done.23.refs_1_
  198.3 5.7 %collective-permute-done.17 = bf16[2,512,128]{2,1,0:T(8,128)(2,1)S(1)} collective-permute-done((bf16[2,512,128]{2,1,0:T(8,128)(2,1)S(1)}, bf16[2,512,128]{2,1,0:T(8,128)(2,1)S(1)}, u32[]{:S(2)}, u32[]{:S(2)}) %collective-permute-start.17) | collective-permute-done | bytes 262176 | tf_op jit(solution)/shard_map/ppermute | solution.py:317
  204.1 1.7 collective-permute-start.18
  205.8 1.4 assemble.6.refs_4_
  207.2 9.9 %collective-permute-done.18.refs_1_ = bf16[4,512,128]{2,1,0:T(8,128)(2,1)S(1)} collective-permute-done((bf16[4,512,128]{2,1,0:T(8,128)(2,1)S(1)}, bf16[4,512,128]{2,1,0:T(8,128)(2,1)S(1)}, u32[]{:S(2)}, u32[]{:S(2)}) %collective-permute-start.18) | collective-permute-done | bytes 524320 | tf_op jit(solution)/shard_map/ppermute | solution.py:317
  217.1 1.0 pad_maximum_fusion
  219.0 1.4 assemble.7
  (117 shorter events, 12.2 us)
Async XLA Ops:
  0.6 7.0 %copy-start = (bf16[1,128,8192]{2,1,0:T(8,128)(2,1)S(1)}, bf16[1,128,8192]{2,1,0:T(8,128)(2,1)}, u32[]{:S(2)}) copy-start(bf16[1,128,8192]{2,1,0:T(8,128)(2,1)} %param.11) | copy-start | bytes 6291460
  0.6 10.7 %copy-start.21 = (s32[1,2,512]{2,1,0:T(2,128)S(1)}, s32[1,2,512]{2,1,0:T(2,128)}, u32[]{:S(2)}) copy-start(s32[1,2,512]{2,1,0:T(2,128)} %param.13) | copy-start | bytes 12292
  0.7 10.9 %copy-start.11 = (bf16[1,256,512]{2,1,0:T(8,128)(2,1)S(1)}, bf16[1,256,512]{2,1,0:T(8,128)(2,1)}, u32[]{:S(2)}) copy-start(bf16[1,256,512]{2,1,0:T(8,128)(2,1)} %param.12) | copy-start | bytes 786436
  4.6 29.5 %collective-permute-start.2 = (bf16[128,2048]{1,0:T(8,128)(2,1)}, bf16[128,2048]{1,0:T(8,128)(2,1)}, u32[]{:S(2)}, u32[]{:S(2)}) collective-permute-start(bf16[128,2048]{1,0:T(8,128)(2,1)} %slice.277), channel_id=1, source_target_pairs={{0,1},{1,0},{2,3},{3,2},{4,5},{5,4},{6,7},{7,6},{8,9},{9,8},{10,11... | collective-permute-start | bytes 1572872 | tf_op jit(solution)/shard_map/ppermute | solution.py:330
  7.6 24.3 %collective-permute-start.3 = (bf16[128,2048]{1,0:T(8,128)(2,1)}, bf16[128,2048]{1,0:T(8,128)(2,1)}, u32[]{:S(2)}, u32[]{:S(2)}) collective-permute-start(bf16[128,2048]{1,0:T(8,128)(2,1)} %slice.344), channel_id=1, source_target_pairs={{0,1},{1,0},{2,3},{3,2},{4,5},{5,4},{6,7},{7,6},{8,9},{9,8},{10,11... | collective-permute-start | bytes 1572872 | tf_op jit(solution)/shard_map/ppermute | solution.py:330
  8.5 34.6 %collective-permute-start.1 = (bf16[128,2048]{1,0:T(8,128)(2,1)}, bf16[128,2048]{1,0:T(8,128)(2,1)S(1)}, u32[]{:S(2)}, u32[]{:S(2)}) collective-permute-start(bf16[128,2048]{1,0:T(8,128)(2,1)} %slice.278), channel_id=1, source_target_pairs={{0,1},{1,0},{2,3},{3,2},{4,5},{5,4},{6,7},{7,6},{8,9},{9,8},{10,11... | collective-permute-start | bytes 1572872 | tf_op jit(solution)/shard_map/ppermute | solution.py:330
  11.3 42.1 %collective-permute-start = (bf16[128,2048]{1,0:T(8,128)(2,1)}, bf16[128,2048]{1,0:T(8,128)(2,1)S(1)}, u32[]{:S(2)}, u32[]{:S(2)}) collective-permute-start(bf16[128,2048]{1,0:T(8,128)(2,1)} %slice.279), channel_id=1, source_target_pairs={{0,1},{1,0},{2,3},{3,2},{4,5},{5,4},{6,7},{7,6},{8,9},{9,8},{10,11... | collective-permute-start | bytes 1572872 | tf_op jit(solution)/shard_map/ppermute | solution.py:330
  17.2 1.3 copy-start.1
  53.4 2.2 %copy-start.2 = (bf16[8192,128]{1,0:T(8,128)(2,1)S(1)}, bf16[8192,128]{1,0:T(8,128)(2,1)}, u32[]{:S(2)}) copy-start(bf16[8192,128]{1,0:T(8,128)(2,1)} %copy-done.1) | copy-start | bytes 6291460
  66.7 34.6 %copy-start.7 = (f32[8,512,128]{2,1,0:T(8,128)}, f32[8,512,128]{2,1,0:T(8,128)S(1)}, u32[]{:S(2)}) copy-start(f32[8,512,128]{2,1,0:T(8,128)S(1)} %get-tuple-element.89) | copy-start | bytes 6291460
  66.9 2.7 %collective-permute-start.4 = (f16[8,512,128]{2,1,0:T(8,128)(2,1)S(1)}, f16[8,512,128]{2,1,0:T(8,128)(2,1)S(1)}, u32[]{:S(2)}, u32[]{:S(2)}) collective-permute-start(f16[8,512,128]{2,1,0:T(8,128)(2,1)S(1)} %convert_element_type.212), channel_id=1, source_target_pairs={{0,2},{2,0},{4,6},{6,4},{8,10},{10,8},{12,14},{14,12},{16,18},{18,... | collective-permute-start | bytes 3145736 | tf_op jit(solution)/shard_map/ppermute | solution.py:317
  69.6 31.7 %copy-start.10 = (f16[8,512,128]{2,1,0:T(8,128)(2,1)}, f16[8,512,128]{2,1,0:T(8,128)(2,1)S(1)}, u32[]{:S(2)}) copy-start(f16[8,512,128]{2,1,0:T(8,128)(2,1)S(1)} %collective-permute-done.4) | copy-start | bytes 3145732
  69.7 14.0 %collective-permute-start.5 = (f16[4,512,128]{2,1,0:T(8,128)(2,1)S(1)}, f16[4,512,128]{2,1,0:T(8,128)(2,1)S(1)}, u32[]{:S(2)}, u32[]{:S(2)}) collective-permute-start(f16[4,512,128]{2,1,0:T(8,128)(2,1)S(1)} %add_convert_fusion.3), channel_id=1, source_target_pairs={{0,4},{2,6},{4,0},{6,2},{8,12},{10,14},{12,8},{14,10},{16,20},{18,... | collective-permute-start | bytes 1572872 | tf_op jit(solution)/shard_map/ppermute | solution.py:317
  82.5 36.0 %copy-start.6 = (f32[8,512,128]{2,1,0:T(8,128)}, f32[8,512,128]{2,1,0:T(8,128)S(1)}, u32[]{:S(2)}) copy-start(f32[8,512,128]{2,1,0:T(8,128)S(1)} %get-tuple-element.95) | copy-start | bytes 6291460
  83.8 17.6 %copy-start.15 = (f16[4,512,128]{2,1,0:T(8,128)(2,1)}, f16[4,512,128]{2,1,0:T(8,128)(2,1)S(1)}, u32[]{:S(2)}) copy-start(f16[4,512,128]{2,1,0:T(8,128)(2,1)S(1)} %collective-permute-done.5) | copy-start | bytes 1572868
  83.9 2.7 %collective-permute-start.6 = (f16[8,512,128]{2,1,0:T(8,128)(2,1)S(1)}, f16[8,512,128]{2,1,0:T(8,128)(2,1)S(1)}, u32[]{:S(2)}, u32[]{:S(2)}) collective-permute-start(f16[8,512,128]{2,1,0:T(8,128)(2,1)S(1)} %convert_element_type.220), channel_id=1, source_target_pairs={{0,2},{2,0},{4,6},{6,4},{8,10},{10,8},{12,14},{14,12},{16,18},{18,... | collective-permute-start | bytes 3145736 | tf_op jit(solution)/shard_map/ppermute | solution.py:317
  86.6 31.9 %copy-start.9 = (f16[8,512,128]{2,1,0:T(8,128)(2,1)}, f16[8,512,128]{2,1,0:T(8,128)(2,1)S(1)}, u32[]{:S(2)}) copy-start(f16[8,512,128]{2,1,0:T(8,128)(2,1)S(1)} %collective-permute-done.6) | copy-start | bytes 3145732
  86.8 14.7 %collective-permute-start.8 = (f16[4,512,128]{2,1,0:T(8,128)(2,1)S(1)}, f16[4,512,128]{2,1,0:T(8,128)(2,1)S(1)}, u32[]{:S(2)}, u32[]{:S(2)}) collective-permute-start(f16[4,512,128]{2,1,0:T(8,128)(2,1)S(1)} %add_convert_fusion.2), channel_id=1, source_target_pairs={{0,4},{2,6},{4,0},{6,2},{8,12},{10,14},{12,8},{14,10},{16,20},{18,... | collective-permute-start | bytes 1572872 | tf_op jit(solution)/shard_map/ppermute | solution.py:317
  88.5 12.8 %collective-permute-start.7 = (f16[2,512,128]{2,1,0:T(8,128)(2,1)S(1)}, f16[2,512,128]{2,1,0:T(8,128)(2,1)S(1)}, u32[]{:S(2)}, u32[]{:S(2)}) collective-permute-start(f16[2,512,128]{2,1,0:T(8,128)(2,1)S(1)} %add_convert_fusion.7), channel_id=1, source_target_pairs={{0,8},{2,10},{4,12},{6,14},{8,0},{10,2},{12,4},{14,6},{16,24},{18,... | collective-permute-start | bytes 786440 | tf_op jit(solution)/shard_map/ppermute | solution.py:317
  101.2 18.4 %copy-start.5 = (f32[8,512,128]{2,1,0:T(8,128)}, f32[8,512,128]{2,1,0:T(8,128)S(1)}, u32[]{:S(2)}) copy-start(f32[8,512,128]{2,1,0:T(8,128)S(1)} %get-tuple-element.104) | copy-start | bytes 6291460
  101.4 3.1 %copy-start.18 = (f16[2,512,128]{2,1,0:T(8,128)(2,1)}, f16[2,512,128]{2,1,0:T(8,128)(2,1)S(1)}, u32[]{:S(2)}) copy-start(f16[2,512,128]{2,1,0:T(8,128)(2,1)S(1)} %collective-permute-done.7) | copy-start | bytes 786436
  101.5 17.1 %copy-start.14 = (f16[4,512,128]{2,1,0:T(8,128)(2,1)}, f16[4,512,128]{2,1,0:T(8,128)(2,1)S(1)}, u32[]{:S(2)}) copy-start(f16[4,512,128]{2,1,0:T(8,128)(2,1)S(1)} %collective-permute-done.8) | copy-start | bytes 1572868
  101.6 2.7 %collective-permute-start.9 = (f16[8,512,128]{2,1,0:T(8,128)(2,1)S(1)}, f16[8,512,128]{2,1,0:T(8,128)(2,1)S(1)}, u32[]{:S(2)}, u32[]{:S(2)}) collective-permute-start(f16[8,512,128]{2,1,0:T(8,128)(2,1)S(1)} %convert_element_type.225), channel_id=1, source_target_pairs={{0,2},{2,0},{4,6},{6,4},{8,10},{10,8},{12,14},{14,12},{16,18},{18,... | collective-permute-start | bytes 3145736 | tf_op jit(solution)/shard_map/ppermute | solution.py:317
  104.3 15.2 %copy-start.8 = (f16[8,512,128]{2,1,0:T(8,128)(2,1)}, f16[8,512,128]{2,1,0:T(8,128)(2,1)S(1)}, u32[]{:S(2)}) copy-start(f16[8,512,128]{2,1,0:T(8,128)(2,1)S(1)} %collective-permute-done.9) | copy-start | bytes 3145732
  104.5 15.1 %collective-permute-start.10 = (f16[4,512,128]{2,1,0:T(8,128)(2,1)S(1)}, f16[4,512,128]{2,1,0:T(8,128)(2,1)S(1)}, u32[]{:S(2)}, u32[]{:S(2)}) collective-permute-start(f16[4,512,128]{2,1,0:T(8,128)(2,1)S(1)} %add_convert_fusion.1), channel_id=1, source_target_pairs={{0,4},{2,6},{4,0},{6,2},{8,12},{10,14},{12,8},{14,10},{16,20},{18,... | collective-permute-start | bytes 1572872 | tf_op jit(solution)/shard_map/ppermute | solution.py:317
  105.6 13.0 %collective-permute-start.11 = (f16[2,512,128]{2,1,0:T(8,128)(2,1)S(1)}, f16[2,512,128]{2,1,0:T(8,128)(2,1)S(1)}, u32[]{:S(2)}, u32[]{:S(2)}) collective-permute-start(f16[2,512,128]{2,1,0:T(8,128)(2,1)S(1)} %add_convert_fusion.6), channel_id=1, source_target_pairs={{0,8},{2,10},{4,12},{6,14},{8,0},{10,2},{12,4},{14,6},{16,24},{18,... | collective-permute-start | bytes 786440 | tf_op jit(solution)/shard_map/ppermute | solution.py:317
  118.4 1.4 copy-start.3
  118.6 1.2 copy-start.16
  119.6 0.8 copy-start.12
  120.4 5.6 %collective-permute-start.12 = (f16[8,512,128]{2,1,0:T(8,128)(2,1)S(1)}, f16[8,512,128]{2,1,0:T(8,128)(2,1)}, u32[]{:S(2)}, u32[]{:S(2)}) collective-permute-start(f16[8,512,128]{2,1,0:T(8,128)(2,1)S(1)} %convert_element_type.238), channel_id=1, source_target_pairs={{0,2},{2,0},{4,6},{6,4},{8,10},{10,8},{12,14},{14,12},{16,18},{18,... | collective-permute-start | bytes 3145736 | tf_op jit(solution)/shard_map/ppermute | solution.py:317
  120.4 5.6 %copy-start.4 = (f32[8,512,128]{2,1,0:T(8,128)S(1)}, f32[8,512,128]{2,1,0:T(8,128)}, u32[]{:S(2)}) copy-start(f32[8,512,128]{2,1,0:T(8,128)} %copy-done.3) | copy-start | bytes 6291460
  120.4 5.3 %copy-start.20 = (f16[1,512,128]{2,1,0:T(8,128)(2,1)S(1)}, f16[1,512,128]{2,1,0:T(8,128)(2,1)}, u32[]{:S(2)}) copy-start(f16[1,512,128]{2,1,0:T(8,128)(2,1)} %add_convert_fusion.10) | copy-start | bytes 393220
  121.7 13.7 %copy-start.19 = (f16[2,512,128]{2,1,0:T(8,128)(2,1)S(1)}, f16[2,512,128]{2,1,0:T(8,128)(2,1)}, u32[]{:S(2)}) copy-start(f16[2,512,128]{2,1,0:T(8,128)(2,1)} %copy-done.18) | copy-start | bytes 786436
  123.0 12.4 %collective-permute-start.28 = (f16[1,512,128]{2,1,0:T(8,128)(2,1)S(1)}, f16[1,512,128]{2,1,0:T(8,128)(2,1)S(1)}, u32[]{:S(2)}, u32[]{:S(2)}) collective-permute-start(f16[1,512,128]{2,1,0:T(8,128)(2,1)S(1)} %add_convert_fusion.11), channel_id=1, source_target_pairs={{0,16},{2,18},{4,20},{6,22},{8,24},{10,26},{12,28},{14,30},{16,0},... | collective-permute-start | bytes 393224 | tf_op jit(solution)/shard_map/ppermute | solution.py:317
  125.7 15.7 %collective-permute-start.24 = (f16[1,512,128]{2,1,0:T(8,128)(2,1)S(1)}, f16[1,512,128]{2,1,0:T(8,128)(2,1)S(1)}, u32[]{:S(2)}, u32[]{:S(2)}) collective-permute-start(f16[1,512,128]{2,1,0:T(8,128)(2,1)S(1)} %copy-done.20), channel_id=1, source_target_pairs={{0,16},{2,18},{4,20},{6,22},{8,24},{10,26},{12,28},{14,30},{16,0},... | collective-permute-start | bytes 393224 | tf_op jit(solution)/shard_map/ppermute | solution.py:317
  126.0 19.7 %copy-start.17 = (f16[2,512,128]{2,1,0:T(8,128)(2,1)S(1)}, f16[2,512,128]{2,1,0:T(8,128)(2,1)}, u32[]{:S(2)}) copy-start(f16[2,512,128]{2,1,0:T(8,128)(2,1)} %copy-done.16) | copy-start | bytes 786436
  127.2 21.9 %copy-start.13 = (f16[4,512,128]{2,1,0:T(8,128)(2,1)S(1)}, f16[4,512,128]{2,1,0:T(8,128)(2,1)}, u32[]{:S(2)}) copy-start(f16[4,512,128]{2,1,0:T(8,128)(2,1)} %copy-done.12) | copy-start | bytes 1572868
  136.7 8.9 %collective-permute-start.29 = (bf16[1,512,128]{2,1,0:T(8,128)(2,1)S(1)}, bf16[1,512,128]{2,1,0:T(8,128)(2,1)S(1)}, u32[]{:S(2)}, u32[]{:S(2)}) collective-permute-start(bf16[1,512,128]{2,1,0:T(8,128)(2,1)S(1)} %get-tuple-element.137), channel_id=1, source_target_pairs={{0,16},{2,18},{4,20},{6,22},{8,24},{10,26},{12,28},{14,30},{16,0},... | collective-permute-start | bytes 393224 | tf_op jit(solution)/shard_map/ppermute | solution.py:317
  136.7 12.1 %collective-permute-start.19 = (f16[2,512,128]{2,1,0:T(8,128)(2,1)S(1)}, f16[2,512,128]{2,1,0:T(8,128)(2,1)S(1)}, u32[]{:S(2)}, u32[]{:S(2)}) collective-permute-start(f16[2,512,128]{2,1,0:T(8,128)(2,1)S(1)} %add_convert_fusion.5), channel_id=1, source_target_pairs={{0,8},{2,10},{4,12},{6,14},{8,0},{10,2},{12,4},{14,6},{16,24},{18,... | collective-permute-start | bytes 786440 | tf_op jit(solution)/shard_map/ppermute | solution.py:317
  140.2 24.9 %collective-permute-start.13 = (f16[4,512,128]{2,1,0:T(8,128)(2,1)S(1)}, f16[4,512,128]{2,1,0:T(8,128)(2,1)S(1)}, u32[]{:S(2)}, u32[]{:S(2)}) collective-permute-start(f16[4,512,128]{2,1,0:T(8,128)(2,1)S(1)} %add_convert_fusion), channel_id=1, source_target_pairs={{0,4},{2,6},{4,0},{6,2},{8,12},{10,14},{12,8},{14,10},{16,20},{18,... | collective-permute-start | bytes 1572872 | tf_op jit(solution)/shard_map/ppermute | solution.py:317
  145.6 10.9 %collective-permute-start.30 = (bf16[2,512,128]{2,1,0:T(8,128)(2,1)S(1)}, bf16[2,512,128]{2,1,0:T(8,128)(2,1)S(1)}, u32[]{:S(2)}, u32[]{:S(2)}) collective-permute-start(bf16[2,512,128]{2,1,0:T(8,128)(2,1)S(1)} %pad_maximum_fusion.8), channel_id=1, source_target_pairs={{0,8},{2,10},{4,12},{6,14},{8,0},{10,2},{12,4},{14,6},{16,24},{18,... | collective-permute-start | bytes 786440 | tf_op jit(solution)/shard_map/ppermute | solution.py:317
  148.8 12.7 %collective-permute-start.25 = (bf16[1,512,128]{2,1,0:T(8,128)(2,1)S(1)}, bf16[1,512,128]{2,1,0:T(8,128)(2,1)S(1)}, u32[]{:S(2)}, u32[]{:S(2)}) collective-permute-start(bf16[1,512,128]{2,1,0:T(8,128)(2,1)S(1)} %get-tuple-element.139), channel_id=1, source_target_pairs={{0,16},{2,18},{4,20},{6,22},{8,24},{10,26},{12,28},{14,30},{16,0},... | collective-permute-start | bytes 393224 | tf_op jit(solution)/shard_map/ppermute | solution.py:317
  150.2 12.8 %collective-permute-start.20 = (f16[1,512,128]{2,1,0:T(8,128)(2,1)S(1)}, f16[1,512,128]{2,1,0:T(8,128)(2,1)S(1)}, u32[]{:S(2)}, u32[]{:S(2)}) collective-permute-start(f16[1,512,128]{2,1,0:T(8,128)(2,1)S(1)} %add_convert_fusion.8), channel_id=1, source_target_pairs={{0,16},{2,18},{4,20},{6,22},{8,24},{10,26},{12,28},{14,30},{16,0},... | collective-permute-start | bytes 393224 | tf_op jit(solution)/shard_map/ppermute | solution.py:317
  156.6 13.3 %collective-permute-start.31 = (bf16[4,512,128]{2,1,0:T(8,128)(2,1)S(1)}, bf16[4,512,128]{2,1,0:T(8,128)(2,1)S(1)}, u32[]{:S(2)}, u32[]{:S(2)}) collective-permute-start(bf16[4,512,128]{2,1,0:T(8,128)(2,1)S(1)} %pad_maximum_fusion.4.refs_0_), channel_id=1, source_target_pairs={{0,4},{2,6},{4,0},{6,2},{8,12},{10,14},{12,8},{14,10},{16,20},{18,... | collective-permute-start | bytes 1572872 | tf_op jit(solution)/shard_map/ppermute | solution.py:317
  161.6 10.5 %collective-permute-start.26 = (bf16[2,512,128]{2,1,0:T(8,128)(2,1)S(1)}, bf16[2,512,128]{2,1,0:T(8,128)(2,1)S(1)}, u32[]{:S(2)}, u32[]{:S(2)}) collective-permute-start(bf16[2,512,128]{2,1,0:T(8,128)(2,1)S(1)} %pad_maximum_fusion.7), channel_id=1, source_target_pairs={{0,8},{2,10},{4,12},{6,14},{8,0},{10,2},{12,4},{14,6},{16,24},{18,... | collective-permute-start | bytes 786440 | tf_op jit(solution)/shard_map/ppermute | solution.py:317
  164.2 8.1 %collective-permute-start.21 = (bf16[1,512,128]{2,1,0:T(8,128)(2,1)S(1)}, bf16[1,512,128]{2,1,0:T(8,128)(2,1)S(1)}, u32[]{:S(2)}, u32[]{:S(2)}) collective-permute-start(bf16[1,512,128]{2,1,0:T(8,128)(2,1)S(1)} %get-tuple-element.141), channel_id=1, source_target_pairs={{0,16},{2,18},{4,20},{6,22},{8,24},{10,26},{12,28},{14,30},{16,0},... | collective-permute-start | bytes 393224 | tf_op jit(solution)/shard_map/ppermute | solution.py:317
  165.1 18.8 %collective-permute-start.32 = (bf16[4,512,128]{2,1,0:T(8,128)(2,1)S(1)}, bf16[4,512,128]{2,1,0:T(8,128)(2,1)S(1)}, u32[]{:S(2)}, u32[]{:S(2)}) collective-permute-start(bf16[4,512,128]{2,1,0:T(8,128)(2,1)S(1)} %pad_maximum_fusion.4.refs_0_), channel_id=1, source_target_pairs={{0,2},{2,0},{4,6},{6,4},{8,10},{10,8},{12,14},{14,12},{16,18},{18,... | collective-permute-start | bytes 1572872 | tf_op jit(solution)/shard_map/ppermute | solution.py:317
  166.2 11.6 %collective-permute-start.14 = (f16[2,512,128]{2,1,0:T(8,128)(2,1)S(1)}, f16[2,512,128]{2,1,0:T(8,128)(2,1)S(1)}, u32[]{:S(2)}, u32[]{:S(2)}) collective-permute-start(f16[2,512,128]{2,1,0:T(8,128)(2,1)S(1)} %add_convert_fusion.4), channel_id=1, source_target_pairs={{0,8},{2,10},{4,12},{6,14},{8,0},{10,2},{12,4},{14,6},{16,24},{18,... | collective-permute-start | bytes 786440 | tf_op jit(solution)/shard_map/ppermute | solution.py:317
  169.9 14.1 %collective-permute-start.33 = (bf16[4,512,128]{2,1,0:T(8,128)(2,1)S(1)}, bf16[4,512,128]{2,1,0:T(8,128)(2,1)S(1)}, u32[]{:S(2)}, u32[]{:S(2)}) collective-permute-start(bf16[4,512,128]{2,1,0:T(8,128)(2,1)S(1)} %collective-permute-done.31.refs_1_), channel_id=1, source_target_pairs={{0,2},{2,0},{4,6},{6,4},{8,10},{10,8},{12,14},{14,12},{16,18},{18,... | collective-permute-start | bytes 1572872 | tf_op jit(solution)/shard_map/ppermute | solution.py:317
  172.2 13.3 %collective-permute-start.27 = (bf16[4,512,128]{2,1,0:T(8,128)(2,1)S(1)}, bf16[4,512,128]{2,1,0:T(8,128)(2,1)S(1)}, u32[]{:S(2)}, u32[]{:S(2)}) collective-permute-start(bf16[4,512,128]{2,1,0:T(8,128)(2,1)S(1)} %pad_maximum_fusion.3.refs_0_), channel_id=1, source_target_pairs={{0,4},{2,6},{4,0},{6,2},{8,12},{10,14},{12,8},{14,10},{16,20},{18,... | collective-permute-start | bytes 1572872 | tf_op jit(solution)/shard_map/ppermute | solution.py:317
  172.3 11.5 %collective-permute-start.22 = (bf16[2,512,128]{2,1,0:T(8,128)(2,1)S(1)}, bf16[2,512,128]{2,1,0:T(8,128)(2,1)S(1)}, u32[]{:S(2)}, u32[]{:S(2)}) collective-permute-start(bf16[2,512,128]{2,1,0:T(8,128)(2,1)S(1)} %pad_maximum_fusion.6), channel_id=1, source_target_pairs={{0,8},{2,10},{4,12},{6,14},{8,0},{10,2},{12,4},{14,6},{16,24},{18,... | collective-permute-start | bytes 786440 | tf_op jit(solution)/shard_map/ppermute | solution.py:317
  178.8 7.6 %collective-permute-start.15 = (f16[1,512,128]{2,1,0:T(8,128)(2,1)S(1)}, f16[1,512,128]{2,1,0:T(8,128)(2,1)S(1)}, u32[]{:S(2)}, u32[]{:S(2)}) collective-permute-start(f16[1,512,128]{2,1,0:T(8,128)(2,1)S(1)} %add_convert_fusion.9), channel_id=1, source_target_pairs={{0,16},{2,18},{4,20},{6,22},{8,24},{10,26},{12,28},{14,30},{16,0},... | collective-permute-start | bytes 393224 | tf_op jit(solution)/shard_map/ppermute | solution.py:317
  183.9 12.0 %collective-permute-start.34 = (bf16[4,512,128]{2,1,0:T(8,128)(2,1)S(1)}, bf16[4,512,128]{2,1,0:T(8,128)(2,1)S(1)}, u32[]{:S(2)}, u32[]{:S(2)}) collective-permute-start(bf16[4,512,128]{2,1,0:T(8,128)(2,1)S(1)} %pad_maximum_fusion.3.refs_0_), channel_id=1, source_target_pairs={{0,2},{2,0},{4,6},{6,4},{8,10},{10,8},{12,14},{14,12},{16,18},{18,... | collective-permute-start | bytes 1572872 | tf_op jit(solution)/shard_map/ppermute | solution.py:317
  183.9 14.4 %collective-permute-start.23 = (bf16[4,512,128]{2,1,0:T(8,128)(2,1)S(1)}, bf16[4,512,128]{2,1,0:T(8,128)(2,1)S(1)}, u32[]{:S(2)}, u32[]{:S(2)}) collective-permute-start(bf16[4,512,128]{2,1,0:T(8,128)(2,1)S(1)} %pad_maximum_fusion.2.refs_0_), channel_id=1, source_target_pairs={{0,4},{2,6},{4,0},{6,2},{8,12},{10,14},{12,8},{14,10},{16,20},{18,... | collective-permute-start | bytes 1572872 | tf_op jit(solution)/shard_map/ppermute | solution.py:317
  185.5 10.4 %collective-permute-start.35 = (bf16[4,512,128]{2,1,0:T(8,128)(2,1)S(1)}, bf16[4,512,128]{2,1,0:T(8,128)(2,1)S(1)}, u32[]{:S(2)}, u32[]{:S(2)}) collective-permute-start(bf16[4,512,128]{2,1,0:T(8,128)(2,1)S(1)} %collective-permute-done.27.refs_1_), channel_id=1, source_target_pairs={{0,2},{2,0},{4,6},{6,4},{8,10},{10,8},{12,14},{14,12},{16,18},{18,... | collective-permute-start | bytes 1572872 | tf_op jit(solution)/shard_map/ppermute | solution.py:317
  187.4 8.3 %collective-permute-start.16 = (bf16[1,512,128]{2,1,0:T(8,128)(2,1)S(1)}, bf16[1,512,128]{2,1,0:T(8,128)(2,1)S(1)}, u32[]{:S(2)}, u32[]{:S(2)}) collective-permute-start(bf16[1,512,128]{2,1,0:T(8,128)(2,1)S(1)} %get-tuple-element.143), channel_id=1, source_target_pairs={{0,16},{2,18},{4,20},{6,22},{8,24},{10,26},{12,28},{14,30},{16,0},... | collective-permute-start | bytes 393224 | tf_op jit(solution)/shard_map/ppermute | solution.py:317
  195.7 8.3 %collective-permute-start.17 = (bf16[2,512,128]{2,1,0:T(8,128)(2,1)S(1)}, bf16[2,512,128]{2,1,0:T(8,128)(2,1)S(1)}, u32[]{:S(2)}, u32[]{:S(2)}) collective-permute-start(bf16[2,512,128]{2,1,0:T(8,128)(2,1)S(1)} %pad_maximum_fusion.5), channel_id=1, source_target_pairs={{0,8},{2,10},{4,12},{6,14},{8,0},{10,2},{12,4},{14,6},{16,24},{18,... | collective-permute-start | bytes 786440 | tf_op jit(solution)/shard_map/ppermute | solution.py:317
  195.8 10.0 %collective-permute-start.36 = (bf16[4,512,128]{2,1,0:T(8,128)(2,1)S(1)}, bf16[4,512,128]{2,1,0:T(8,128)(2,1)S(1)}, u32[]{:S(2)}, u32[]{:S(2)}) collective-permute-start(bf16[4,512,128]{2,1,0:T(8,128)(2,1)S(1)} %pad_maximum_fusion.2.refs_0_), channel_id=1, source_target_pairs={{0,2},{2,0},{4,6},{6,4},{8,10},{10,8},{12,14},{14,12},{16,18},{18,... | collective-permute-start | bytes 1572872 | tf_op jit(solution)/shard_map/ppermute | solution.py:317
  198.3 7.4 %collective-permute-start.37 = (bf16[4,512,128]{2,1,0:T(8,128)(2,1)S(1)}, bf16[4,512,128]{2,1,0:T(8,128)(2,1)S(1)}, u32[]{:S(2)}, u32[]{:S(2)}) collective-permute-start(bf16[4,512,128]{2,1,0:T(8,128)(2,1)S(1)} %collective-permute-done.23.refs_1_), channel_id=1, source_target_pairs={{0,2},{2,0},{4,6},{6,4},{8,10},{10,8},{12,14},{14,12},{16,18},{18,... | collective-permute-start | bytes 1572872 | tf_op jit(solution)/shard_map/ppermute | solution.py:317
  204.1 13.1 %collective-permute-start.18 = (bf16[4,512,128]{2,1,0:T(8,128)(2,1)S(1)}, bf16[4,512,128]{2,1,0:T(8,128)(2,1)S(1)}, u32[]{:S(2)}, u32[]{:S(2)}) collective-permute-start(bf16[4,512,128]{2,1,0:T(8,128)(2,1)S(1)} %pad_maximum_fusion.1.refs_0_), channel_id=1, source_target_pairs={{0,4},{2,6},{4,0},{6,2},{8,12},{10,14},{12,8},{14,10},{16,20},{18,... | collective-permute-start | bytes 1572872 | tf_op jit(solution)/shard_map/ppermute | solution.py:317
  205.8 12.4 %collective-permute-start.38 = (bf16[4,512,128]{2,1,0:T(8,128)(2,1)S(1)}, bf16[4,512,128]{2,1,0:T(8,128)(2,1)S(1)}, u32[]{:S(2)}, u32[]{:S(2)}) collective-permute-start(bf16[4,512,128]{2,1,0:T(8,128)(2,1)S(1)} %pad_maximum_fusion.1.refs_0_), channel_id=1, source_target_pairs={{0,2},{2,0},{4,6},{6,4},{8,10},{10,8},{12,14},{14,12},{16,18},{18,... | collective-permute-start | bytes 1572872 | tf_op jit(solution)/shard_map/ppermute | solution.py:317
  217.1 1.9 collective-permute-start.39

commit v5 on v3

--- a/solution.py
+++ b/solution.py
@@ -148,7 +148,7 @@
         below = (100.0 * math.sqrt(0.05)) * root + 1e-06
         return 0.99 * weights - first * lax.rsqrt(below * below)
 
-    def gradient_of(pair, which, slot):
+    def differentiate(pair, which, slot):
         turned = jnp.concatenate(
             [low_turned_ref[slab, pair, which], high_turned_ref[slab, pair, which]], axis=1
         )
@@ -156,6 +156,12 @@
             turned, residual_state[...], preferred_element_type=F32
         )
 
+    def project(slot):
+        begin = (slab * pairs * cores + slot) * rows
+        place = pl.ds(pl.multiple_of(begin, rows), rows)
+        picked = jnp.concatenate([low_ref[:, place], high_ref[:, place]], axis=0)
+        return jnp.dot(picked, rounded_state[slot], preferred_element_type=F32)
+
     @pl.when((step == 0) & (slab == 0))
     def _():
         weigh(jnp.concatenate([low_product_ref[...], high_product_ref[...]], axis=0), 0)
@@ -165,42 +171,46 @@
     def _():
         weigh(output_state[...], 1)
 
+    slots = [(slot, *divmod(slot, cores)) for slot in range(pairs * cores)]
+
     @pl.when(step == 0)
     def _():
         total = jnp.zeros(output_state.shape, F32)
-        for pair in range(pairs):
-            for which in range(cores):
-                slot = pair * cores + which
-                gradient_of(pair, which, slot)
-                for piece in pieces:
-                    gradient = gradient_state[slot, piece]
-                    first = 9.0 * first_ref[pair, which, piece] + gradient
-                    second = 19.0 * second_ref[pair, which, piece] + gradient * gradient
-                    weights = descend(first, second, start_ref[pair, which, piece].astype(F32))
-                    first_state[slab, pair, which, piece] = first
-                    second_state[slab, pair, which, piece] = second
-                    weights_state[slab, pair, which, piece] = weights
-                    rounded_state[slot, piece] = weights.astype(BF16)
-                begin = (slab * pairs * cores + slot) * rows
-                place = pl.ds(pl.multiple_of(begin, rows), rows)
-                picked = jnp.concatenate([low_ref[:, place], high_ref[:, place]], axis=0)
-                total += jnp.dot(picked, rounded_state[slot], preferred_element_type=F32)
-        output_state[...] += total
+        differentiate(0, 0, 0)
+        for slot, pair, which in slots:
+            if slot + 1 < len(slots):
+                ahead, *place = slots[slot + 1]
+                differentiate(*place, ahead)
+            for piece in pieces:
+                gradient = gradient_state[slot, piece]
+                first = 9.0 * first_ref[pair, which, piece] + gradient
+                second = 19.0 * second_ref[pair, which, piece] + gradient * gradient
+                weights = descend(first, second, start_ref[pair, which, piece].astype(F32))
+                first_state[slab, pair, which, piece] = first
+                second_state[slab, pair, which, piece] = second
+                weights_state[slab, pair, which, piece] = weights
+                rounded_state[slot, piece] = weights.astype(BF16)
+            if slot:
+                total += project(slot - 1)
+        output_state[...] += total + project(len(slots) - 1)
 
     @pl.when(step == 1)
     def _():
-        for pair in range(pairs):
+        sides = ((1 - core, send_ref), (core, keep_ref))
+        differentiate(0, sides[0][0], 0)
+        for slot, pair, side in slots:
+            if slot + 1 < len(slots):
+                ahead, next_pair, next_side = slots[slot + 1]
+                differentiate(next_pair, sides[next_side][0], ahead)
+            which, out_ref = sides[side]
             place = changed_place(mine, slab, pair, pairs)
-            for slot, which, out_ref in ((0, 1 - core, send_ref), (1, core, keep_ref)):
-                slot = pair * cores + slot
-                gradient_of(pair, which, slot)
-                for piece in pieces:
-                    gradient = gradient_state[slot, piece]
-                    first = 0.9 * first_state[slab, pair, which, piece] + gradient
-                    second = 0.95 * second_state[slab, pair, which, piece] + gradient * gradient
-                    weights = descend(first, second, weights_state[slab, pair, which, piece])
-                    change = start_ref[pair, which, piece].astype(F32) - weights
-                    out_ref[place, piece] = change * WIRE_SCALE
+            for piece in pieces:
+                gradient = gradient_state[slot, piece]
+                first = 0.9 * first_state[slab, pair, which, piece] + gradient
+                second = 0.95 * second_state[slab, pair, which, piece] + gradient * gradient
+                weights = descend(first, second, weights_state[slab, pair, which, piece])
+                change = start_ref[pair, which, piece].astype(F32) - weights
+                out_ref[place, piece] = change * WIRE_SCALE
 
 
 def inner(chunk, width, mine, banks, turned, start, first, second, products, target, count, tokens):
@@ -312,9 +322,11 @@
     chunks = columns // width
     mine = lax.axis_index("rep")
 
-    def swapped(array, bit):
-        pairs = [(index, index ^ (1 << bit)) for index in range(reps)]
+    def swapped(array, offset):
+        pairs = [(index, index ^ offset) for index in range(reps)]
         return lax.ppermute(array, "rep", pairs)
+
+    spans = [[0, 1 << bit] for bit in range(1, bits)]
 
     own_bank = hidden_bank[0]
     target = target_bank[0]
@@ -356,59 +368,83 @@
         for begin in range(0, columns, width)
     ]
 
-    def halved(terms):
-        middle = terms[0].shape[0] // 2
-        outgoing = sum(term[middle:].astype(F32) for term in terms).astype(WIRE)
-        return outgoing, [term[:middle] for term in terms]
+    def parted(terms, span):
+        size = terms[0].shape[0] // len(span)
+        parts = [[term[begin : begin + size] for term in terms] for begin in range(0, size * len(span), size)]
+        outgoing = [sum(term.astype(F32) for term in part).astype(WIRE) for part in parts[1:]]
+        return outgoing, parts[0]
+
+    def sent(outgoing, span):
+        return [swapped(array, offset) for array, offset in zip(outgoing, span[1:])]
 
     new_momentum = []
     result = ()
 
-    live = {}
+    def chain(chunk, send, keep):
+        send = yield send
+        terms = [keep, swapped(send, 1)]
+        for span in spans:
+            outgoing, terms = parted(terms, span)
+            outgoing = yield outgoing
+            terms = terms + held_back(sent(outgoing, span))
+        total = sum(term.astype(F32) for term in terms)[0]
+        average = total * (1.0 / (WIRE_SCALE * reps))
+        moved = 0.9 * shares[chunk][0] + average
+        stack = (shares[chunk][1].astype(F32) - 0.7 * (average + 0.9 * moved)).astype(BF16)[None]
+        offsets = [0]
+        for span in spans[:0:-1]:
+            stack = yield stack
+            arrived = held_back(sent([stack] * (len(span) - 1), span))
+            stack = jnp.concatenate([stack] + arrived)
+            offsets = [offset ^ far for far in span for offset in offsets]
+        stack = yield stack
+        across = swapped(stack, 2)
+        finished[chunk] = (moved, stack, across, offsets)
+
+    finished = {}
+    running = {}
+    formed = {}
+    gate = []
+
+    def held_back(arrived):
+        return tied(arrived, gate)[0] if gate else arrived
+
+    def move_on(which, behind=()):
+        gate[:] = [formed[other] for other in behind]
+        try:
+            formed[which] = running[which].send(formed[which])
+        except StopIteration:
+            del formed[which]
+
     token = place
     for chunk in range(chunks):
         send, keep = inner(
             chunk, width, token, banks, turned, start, first, second, products, target, count, tokens
         )
         send = send.astype(WIRE)
-        moving = {}
-        for earlier in range(max(chunk - bits + 2, 0), chunk):
-            outgoing, terms = halved(live[earlier])
-            outgoing, send = tied(outgoing, send)
-            moving[earlier] = (outgoing, terms)
-        outgoing, terms = halved([keep, swapped(send, 0)])
-        moving[chunk] = (outgoing, terms)
+        for earlier in list(formed):
+            move_on(earlier)
+            formed[earlier], send = tied(formed[earlier], send)
+        running[chunk] = chain(chunk, send, keep)
+        formed[chunk] = running[chunk].send(next(running[chunk]))
         if chunk + 1 < chunks:
-            formed, token = tied([outgoing for outgoing, _ in moving.values()], token)
-            moving = {
-                which: (outgoing, terms)
-                for (which, (_, terms)), outgoing in zip(moving.items(), formed)
-            }
-        for which, (outgoing, terms) in moving.items():
-            live[which] = terms + [swapped(outgoing, chunk - which + 1)]
+            formed, token = tied(formed, token)
+    if chunks == 4:
+        move_on(0, behind=[3])
+        move_on(3, behind=[0])
+        for which in (1, 2, 0):
+            move_on(which, behind=[3])
+    for which in range(chunks):
+        while which in formed:
+            move_on(which)
 
     for chunk in range(chunks):
-        terms = live[chunk]
-        for bit in range(min(chunks - chunk + 1, bits), bits):
-            outgoing, terms = halved(terms)
-            terms = terms + [swapped(outgoing, bit)]
-        total = sum(term.astype(F32) for term in terms)[0]
-
-        average = total * (1.0 / (WIRE_SCALE * reps))
-        moved = 0.9 * shares[chunk][0] + average
+        moved, stack, across, offsets = finished[chunk]
         new_momentum.append(moved)
-        fresh = (shares[chunk][1].astype(F32) - 0.7 * (average + 0.9 * moved)).astype(BF16)
-
-        stack = fresh[None]
-        offsets = [0]
-        for bit in range(bits - 1, 1, -1):
-            stack = jnp.concatenate([stack, swapped(stack, bit)])
-            offsets = offsets + [offset ^ (1 << bit) for offset in offsets]
-        across = swapped(stack, 1)
+        offsets = [[offset ^ low for offset in offsets] for low in (0, 2, 1, 3)]
         if result:
             across, *result = tied(across, result[0])
-        received = [stack, across, swapped(stack, 0), swapped(across, 0)]
-        offsets = [[offset ^ low for offset in offsets] for low in (0, 2, 1, 3)]
+        received = [stack, across, swapped(stack, 1), swapped(across, 1)]
         result = (
             assemble(chunk, place, received, offsets, (reps, rows, columns), result),
         )

time: 223 us -> 229 us (1.027)
  starting transfers between devices: 27.5 us -> 35.5 us
  waiting for transfers between devices: 105 us -> 101 us
  local copies, waits for them, and re-layouts: 11.9 us -> 14.7 us
    ppermute x36, starting transfers between devices: 22.5 us -> 30.4 us  [swapped(): return lax.ppermute(array, 'rep', pairs)]
    ppermute x36, waiting for transfers between devices: 80.2 us -> 74.4 us  [swapped(): return lax.ppermute(array, 'rep', pairs)]
    unnamed x48, local copies, waits for them, and re-layouts: 1.66 us -> 6.97 us
  transfers between devices with their start and end apart: 40 -> 40, of which waited for: 22 -> 20; matrix products, arithmetic and copies ran while one was open for 8% -> 6% of each run, Pallas kernels for 22% -> 21%
where the time goes in v5:
time: 229 us; the launch traced here: 228 us
  waiting for transfers between devices  101 us (44%)
  Pallas kernels  62.5 us (27%)
  starting transfers between devices  35.5 us (16%)
  local copies, waits for them, and re-layouts  14.7 us (6%)
  other arithmetic  12.6 us (6%)
    ppermute x36, waiting for transfers between devices, swapped(): return lax.ppermute(array, 'rep', pairs)  74.4 us
    pallas_call x4, Pallas kernels, inner(): pl.pallas_call(functools.partial(inner_kernel, float(tokens)), grid_spec=...  42.9 us
    ppermute x36, starting transfers between devices, swapped(): return lax.ppermute(array, 'rep', pairs)  30.4 us
    ppermute x4, waiting for transfers between devices, per_device(): parts.append(lax.ppermute(part, 'fsdp', [(0, 1), (1, 0)]))  26.8 us
    pallas_call x4, Pallas kernels, arrive(): pl.pallas_call(functools.partial(arrive_kernel, piece), grid=(1,), in_spe...  8.81 us
    unnamed x48, local copies, waits for them, and re-layouts  6.97 us
    pallas_call x4, Pallas kernels, assemble(): pl.pallas_call(functools.partial(assemble_kernel, chunk, offsets), in_spe...  5.76 us
    convert_element_type x12, other arithmetic, parted(): sum((term.astype(F32) for term in part)).astype(WIRE)  5.62 us
  transfers between devices with their start and end apart: 40, of which 20 were waited for; matrix products, arithmetic and copies ran while one was open for 6% of the time, Pallas kernels for 21%

profile of v5, /device:TPU:0, one launch (start us, length us, event | category | flops | bytes accessed | tf_op | source)
XLA Modules:
  0.0 227.9 jit_solution(14050337244994559848)
XLA Ops:
  0.7 1.2 slice.344
  1.9 1.9 slice.277
  3.8 3.0 %collective-permute-start.2 = (bf16[128,2048]{1,0:T(8,128)(2,1)}, bf16[128,2048]{1,0:T(8,128)(2,1)}, u32[]{:S(2)}, u32[]{:S(2)}) collective-permute-start(bf16[128,2048]{1,0:T(8,128)(2,1)} %slice.277), channel_id=1, source_target_pairs={{0,1},{1,0},{2,3},{3,2},{4,5},{5,4},{6,7},{7,6},{8,9},{9,8},{10,11... | collective-permute-start | bytes 1572872 | tf_op jit(solution)/shard_map/ppermute | solution.py:342
  6.8 0.9 slice.278
  7.7 2.0 collective-permute-start.1
  10.8 5.0 %forward.1 = (bf16[8192,128]{1,0:T(8,128)(2,1)S(1)}, f32[128,512]{1,0:T(8,128)S(1)}) custom-call(bf16[128,8192]{1,0:T(8,128)(2,1)S(1)} %bitcast.89, bf16[8192,512]{1,0:T(8,128)(2,1)} %weights_ref.9), custom_call_target="tpu_custom_call" | custom-call | flops 1073741824 | bytes 12582912 | tf_op jit(solution)/shard_map/forward/pallas_call | solution.py:34
  15.8 1.3 copy-done.5
  17.6 13.4 %collective-permute-done.3.part_ref = bf16[128,2048]{1,0:T(8,128)(2,1)S(1)} collective-permute-done((bf16[128,2048]{1,0:T(8,128)(2,1)S(1)}, bf16[128,2048]{1,0:T(8,128)(2,1)S(1)}, u32[]{:S(2)}, u32[]{:S(2)}) %collective-permute-start.3) | collective-permute-done | bytes 524320 | tf_op jit(solution)/shard_map/ppermute | solution.py:342
  31.8 1.0 copy-done.13
  32.8 2.0 arrive.4
  34.9 2.2 arrive.5
  37.1 5.2 %collective-permute-done.1.part_ref = bf16[128,2048]{1,0:T(8,128)(2,1)} collective-permute-done((bf16[128,2048]{1,0:T(8,128)(2,1)}, bf16[128,2048]{1,0:T(8,128)(2,1)}, u32[]{:S(2)}, u32[]{:S(2)}) %collective-permute-start.1) | collective-permute-done | bytes 524320 | tf_op jit(solution)/shard_map/ppermute | solution.py:342
  42.3 2.2 arrive.6
  44.5 8.2 %collective-permute-done.part_ref = bf16[128,2048]{1,0:T(8,128)(2,1)} collective-permute-done((bf16[128,2048]{1,0:T(8,128)(2,1)}, bf16[128,2048]{1,0:T(8,128)(2,1)}, u32[]{:S(2)}, u32[]{:S(2)}) %collective-permute-start) | collective-permute-done | bytes 524320 | tf_op jit(solution)/shard_map/ppermute | solution.py:342
  52.7 2.3 %arrive.7 = (bf16[128,8192]{1,0:T(8,128)(2,1)S(1)}, bf16[8192,128]{1,0:T(8,128)(2,1)S(1)}, f32[128,512]{1,0:T(8,128)S(1)}) custom-call(bf16[128,2048]{1,0:T(8,128)(2,1)} %collective-permute-done.part_ref, bf16[8192,512]{1,0:T(8,128)(2,1)} %weights_ref.9, ...), custom_call_target="tpu_custom_call", output_to_operand_aliasing={{0}: (2, {}), {1}: (3, {}), {2}: (4, {})} | custom-call | flops 268435456 | bytes 3670016 | tf_op jit(solution)/shard_map/arrive/pallas_call | solution.py:76
  55.7 10.7 %inner.4 = (f32[8,512,128]{2,1,0:T(8,128)S(1)}, f32[8,512,128]{2,1,0:T(8,128)S(1)}) custom-call(s32[1]{0:T(128)} %bitcast.mine_ref.place_ref, bf16[128,8192]{1,0:T(8,128)(2,1)S(1)} %bitcast.90, bf16[128,8192]{1,0:T(8,128)(2,1)S(1)} %get-tuple-element.88.high_ref, bf16[4,2,2,512,128]{4,3,2,1,0:T(8,128)(2,1)S(1)} %bitcast.94, ...), custom_call_target="tpu_custom_call" | custom-call | flops 1610612736 | bytes 20971520 | tf_op jit(solution)/shard_map/inner/pallas_call | solution.py:228
  66.7 2.6 %collective-permute-done.4 = f16[8,512,128]{2,1,0:T(8,128)(2,1)S(1)} collective-permute-done((f16[8,512,128]{2,1,0:T(8,128)(2,1)S(1)}, f16[8,512,128]{2,1,0:T(8,128)(2,1)S(1)}, u32[]{:S(2)}, u32[]{:S(2)}) %collective-permute-start.4) | collective-permute-done | bytes 1048608 | tf_op jit(solution)/shard_map/ppermute | solution.py:327
  69.5 1.8 collective-permute-start.5
  71.3 10.7 %inner.5 = (f32[8,512,128]{2,1,0:T(8,128)S(1)}, f32[8,512,128]{2,1,0:T(8,128)S(1)}) custom-call(s32[1]{0:T(128)} %bitcast.mine_ref.place_ref, bf16[128,8192]{1,0:T(8,128)(2,1)S(1)} %bitcast.91, bf16[128,8192]{1,0:T(8,128)(2,1)S(1)} %get-tuple-element.88.high_ref, bf16[4,2,2,512,128]{4,3,2,1,0:T(8,128)(2,1)S(1)} %bitcast.95, ...), custom_call_target="tpu_custom_call" | custom-call | flops 1610612736 | bytes 20971520 | tf_op jit(solution)/shard_map/inner/pallas_call | solution.py:228
  82.1 1.4 collective-permute-done.5
  83.7 2.6 %collective-permute-done.6 = f16[8,512,128]{2,1,0:T(8,128)(2,1)S(1)} collective-permute-done((f16[8,512,128]{2,1,0:T(8,128)(2,1)S(1)}, f16[8,512,128]{2,1,0:T(8,128)(2,1)S(1)}, u32[]{:S(2)}, u32[]{:S(2)}) %collective-permute-start.6) | collective-permute-done | bytes 1048608 | tf_op jit(solution)/shard_map/ppermute | solution.py:327
  86.6 1.8 collective-permute-start.8
  88.3 1.6 collective-permute-start.7
  89.9 10.7 %inner.6 = (f32[8,512,128]{2,1,0:T(8,128)S(1)}, f32[8,512,128]{2,1,0:T(8,128)S(1)}) custom-call(s32[1]{0:T(128)} %bitcast.mine_ref.place_ref, bf16[128,8192]{1,0:T(8,128)(2,1)S(1)} %bitcast.92, bf16[128,8192]{1,0:T(8,128)(2,1)S(1)} %get-tuple-element.88.high_ref, bf16[4,2,2,512,128]{4,3,2,1,0:T(8,128)(2,1)S(1)} %bitcast.96, ...), custom_call_target="tpu_custom_call" | custom-call | flops 1610612736 | bytes 20971520 | tf_op jit(solution)/shard_map/inner/pallas_call | solution.py:228
  100.6 1.3 convert_element_type.225
  102.9 1.1 fusion.16
  104.1 1.4 fusion.17
  105.9 1.5 add_convert_fusion.1
  107.4 2.6 %collective-permute-start.12 = (f16[1,512,128]{2,1,0:T(8,128)(2,1)S(1)}, f16[1,512,128]{2,1,0:T(8,128)(2,1)S(1)}, u32[]{:S(2)}, u32[]{:S(2)}) collective-permute-start(f16[1,512,128]{2,1,0:T(8,128)(2,1)S(1)} %add_convert_fusion.11), channel_id=1, source_target_pairs={{0,16},{2,18},{4,20},{6,22},{8,24},{10,26},{12,28},{14,30},{16,0},... | collective-permute-start | bytes 393224 | tf_op jit(solution)/shard_map/ppermute | solution.py:327
  110.5 1.4 collective-permute-start.10
  111.9 1.6 copy-done.7
  113.5 10.9 %inner.7 = (f32[8,512,128]{2,1,0:T(8,128)S(1)}, f32[8,512,128]{2,1,0:T(8,128)S(1)}) custom-call(s32[1]{0:T(128)} %bitcast.mine_ref.place_ref, bf16[128,8192]{1,0:T(8,128)(2,1)S(1)} %bitcast.93, bf16[128,8192]{1,0:T(8,128)(2,1)S(1)} %get-tuple-element.88.high_ref, bf16[4,2,2,512,128]{4,3,2,1,0:T(8,128)(2,1)S(1)} %bitcast.97, ...), custom_call_target="tpu_custom_call" | custom-call | flops 1610612736 | bytes 20971520 | tf_op jit(solution)/shard_map/inner/pallas_call | solution.py:228
  125.3 1.3 bitcast_add_fusion.7
  126.6 1.1 add_convert_fusion.10
  127.7 1.1 add_convert_fusion.5
  128.8 2.6 %collective-permute-done.13 = f16[8,512,128]{2,1,0:T(8,128)(2,1)S(1)} collective-permute-done((f16[8,512,128]{2,1,0:T(8,128)(2,1)S(1)}, f16[8,512,128]{2,1,0:T(8,128)(2,1)S(1)}, u32[]{:S(2)}, u32[]{:S(2)}) %collective-permute-start.13) | collective-permute-done | bytes 1048608 | tf_op jit(solution)/shard_map/ppermute | solution.py:327
  132.7 1.6 collective-permute-start.21
  134.3 7.1 %collective-permute-done.15 = bf16[1,512,128]{2,1,0:T(8,128)(2,1)S(1)} collective-permute-done((bf16[1,512,128]{2,1,0:T(8,128)(2,1)S(1)}, bf16[1,512,128]{2,1,0:T(8,128)(2,1)S(1)}, u32[]{:S(2)}, u32[]{:S(2)}) %collective-permute-start.15) | collective-permute-done | bytes 131104 | tf_op jit(solution)/shard_map/ppermute | solution.py:327
  141.6 1.8 collective-permute-start.26
  143.3 2.3 %collective-permute-done.14 = f16[4,512,128]{2,1,0:T(8,128)(2,1)S(1)} collective-permute-done((f16[4,512,128]{2,1,0:T(8,128)(2,1)S(1)}, f16[4,512,128]{2,1,0:T(8,128)(2,1)S(1)}, u32[]{:S(2)}, u32[]{:S(2)}) %collective-permute-start.14) | collective-permute-done | bytes 524320 | tf_op jit(solution)/shard_map/ppermute | solution.py:327
  145.7 3.8 %collective-permute-done.26 = f16[1,512,128]{2,1,0:T(8,128)(2,1)S(1)} collective-permute-done((f16[1,512,128]{2,1,0:T(8,128)(2,1)S(1)}, f16[1,512,128]{2,1,0:T(8,128)(2,1)S(1)}, u32[]{:S(2)}, u32[]{:S(2)}) %collective-permute-start.26) | collective-permute-done | bytes 131104 | tf_op jit(solution)/shard_map/ppermute | solution.py:327
  149.5 2.3 collective-permute-done.30
  151.8 1.9 collective-permute-start.31
  153.8 1.2 bitcast_add_fusion.1
  155.0 1.3 collective-permute-start.27
  156.2 1.0 add_convert_fusion.8
  157.2 1.8 collective-permute-start.22
  159.0 7.6 %collective-permute-done.27 = bf16[1,512,128]{2,1,0:T(8,128)(2,1)S(1)} collective-permute-done((bf16[1,512,128]{2,1,0:T(8,128)(2,1)S(1)}, bf16[1,512,128]{2,1,0:T(8,128)(2,1)S(1)}, u32[]{:S(2)}, u32[]{:S(2)}) %collective-permute-start.27) | collective-permute-done | bytes 131104 | tf_op jit(solution)/shard_map/ppermute | solution.py:327
  166.7 2.0 collective-permute-start.16
  168.7 1.1 bitcast_add_fusion.3
  170.4 8.3 %collective-permute-done.28 = bf16[2,512,128]{2,1,0:T(8,128)(2,1)S(1)} collective-permute-done((bf16[2,512,128]{2,1,0:T(8,128)(2,1)S(1)}, bf16[2,512,128]{2,1,0:T(8,128)(2,1)S(1)}, u32[]{:S(2)}, u32[]{:S(2)}) %collective-permute-start.28) | collective-permute-done | bytes 262176 | tf_op jit(solution)/shard_map/ppermute | solution.py:327
  178.8 1.2 collective-permute-start.29
  180.1 3.4 %collective-permute-start.24 = (bf16[2,512,128]{2,1,0:T(8,128)(2,1)S(1)}, bf16[2,512,128]{2,1,0:T(8,128)(2,1)S(1)}, u32[]{:S(2)}, u32[]{:S(2)}) collective-permute-start(bf16[2,512,128]{2,1,0:T(8,128)(2,1)S(1)} %pad_maximum_fusion.5), channel_id=1, source_target_pairs={{0,8},{2,10},{4,12},{6,14},{8,0},{10,2},{12,4},{14,6},{16,24},{18,... | collective-permute-start | bytes 786440 | tf_op jit(solution)/shard_map/ppermute | solution.py:327
  183.8 7.5 %collective-permute-done.24 = bf16[2,512,128]{2,1,0:T(8,128)(2,1)S(1)} collective-permute-done((bf16[2,512,128]{2,1,0:T(8,128)(2,1)S(1)}, bf16[2,512,128]{2,1,0:T(8,128)(2,1)S(1)}, u32[]{:S(2)}, u32[]{:S(2)}) %collective-permute-start.24) | collective-permute-done | bytes 262176 | tf_op jit(solution)/shard_map/ppermute | solution.py:327
  191.5 1.4 assemble.4.refs_4_
  194.2 8.5 %collective-permute-done.18 = bf16[1,512,128]{2,1,0:T(8,128)(2,1)S(1)} collective-permute-done((bf16[1,512,128]{2,1,0:T(8,128)(2,1)S(1)}, bf16[1,512,128]{2,1,0:T(8,128)(2,1)S(1)}, u32[]{:S(2)}, u32[]{:S(2)}) %collective-permute-start.18) | collective-permute-done | bytes 131104 | tf_op jit(solution)/shard_map/ppermute | solution.py:327
  202.9 1.4 assemble.5.refs_4_
  204.3 1.5 collective-permute-done.25.refs_1_
  205.8 5.2 %collective-permute-done.19 = bf16[2,512,128]{2,1,0:T(8,128)(2,1)S(1)} collective-permute-done((bf16[2,512,128]{2,1,0:T(8,128)(2,1)S(1)}, bf16[2,512,128]{2,1,0:T(8,128)(2,1)S(1)}, u32[]{:S(2)}, u32[]{:S(2)}) %collective-permute-start.19) | collective-permute-done | bytes 262176 | tf_op jit(solution)/shard_map/ppermute | solution.py:327
  211.1 2.1 collective-permute-start.20
  213.1 1.4 assemble.6.refs_4_
  214.6 9.8 %collective-permute-done.20.refs_1_ = bf16[4,512,128]{2,1,0:T(8,128)(2,1)S(1)} collective-permute-done((bf16[4,512,128]{2,1,0:T(8,128)(2,1)S(1)}, bf16[4,512,128]{2,1,0:T(8,128)(2,1)S(1)}, u32[]{:S(2)}, u32[]{:S(2)}) %collective-permute-start.20) | collective-permute-done | bytes 524320 | tf_op jit(solution)/shard_map/ppermute | solution.py:327
  224.4 1.0 pad_maximum_fusion
  226.3 1.4 assemble.7
  (120 shorter events, 11.9 us)
Async XLA Ops:
  0.6 6.2 %copy-start.2 = (bf16[1,128,8192]{2,1,0:T(8,128)(2,1)S(1)}, bf16[1,128,8192]{2,1,0:T(8,128)(2,1)}, u32[]{:S(2)}) copy-start(bf16[1,128,8192]{2,1,0:T(8,128)(2,1)} %param.11) | copy-start | bytes 6291460
  0.6 9.9 %copy-start.22 = (s32[1,2,512]{2,1,0:T(2,128)S(1)}, s32[1,2,512]{2,1,0:T(2,128)}, u32[]{:S(2)}) copy-start(s32[1,2,512]{2,1,0:T(2,128)} %param.13) | copy-start | bytes 12292
  0.7 10.1 %copy-start.16 = (bf16[1,256,512]{2,1,0:T(8,128)(2,1)S(1)}, bf16[1,256,512]{2,1,0:T(8,128)(2,1)}, u32[]{:S(2)}) copy-start(bf16[1,256,512]{2,1,0:T(8,128)(2,1)} %param.12) | copy-start | bytes 786436
  3.8 31.1 %collective-permute-start.2 = (bf16[128,2048]{1,0:T(8,128)(2,1)}, bf16[128,2048]{1,0:T(8,128)(2,1)}, u32[]{:S(2)}, u32[]{:S(2)}) collective-permute-start(bf16[128,2048]{1,0:T(8,128)(2,1)} %slice.277), channel_id=1, source_target_pairs={{0,1},{1,0},{2,3},{3,2},{4,5},{5,4},{6,7},{7,6},{8,9},{9,8},{10,11... | collective-permute-start | bytes 1572872 | tf_op jit(solution)/shard_map/ppermute | solution.py:342
  6.8 24.2 %collective-permute-start.3 = (bf16[128,2048]{1,0:T(8,128)(2,1)S(1)}, bf16[128,2048]{1,0:T(8,128)(2,1)S(1)}, u32[]{:S(2)}, u32[]{:S(2)}) collective-permute-start(bf16[128,2048]{1,0:T(8,128)(2,1)S(1)} %slice.344), channel_id=1, source_target_pairs={{0,1},{1,0},{2,3},{3,2},{4,5},{5,4},{6,7},{7,6},{8,9},{9,8},{10,11... | collective-permute-start | bytes 1572872 | tf_op jit(solution)/shard_map/ppermute | solution.py:342
  7.7 34.6 %collective-permute-start.1 = (bf16[128,2048]{1,0:T(8,128)(2,1)}, bf16[128,2048]{1,0:T(8,128)(2,1)}, u32[]{:S(2)}, u32[]{:S(2)}) collective-permute-start(bf16[128,2048]{1,0:T(8,128)(2,1)} %slice.278), channel_id=1, source_target_pairs={{0,1},{1,0},{2,3},{3,2},{4,5},{5,4},{6,7},{7,6},{8,9},{9,8},{10,11... | collective-permute-start | bytes 1572872 | tf_op jit(solution)/shard_map/ppermute | solution.py:342
  10.5 42.2 %collective-permute-start = (bf16[128,2048]{1,0:T(8,128)(2,1)}, bf16[128,2048]{1,0:T(8,128)(2,1)}, u32[]{:S(2)}, u32[]{:S(2)}) collective-permute-start(bf16[128,2048]{1,0:T(8,128)(2,1)} %slice.279), channel_id=1, source_target_pairs={{0,1},{1,0},{2,3},{3,2},{4,5},{5,4},{6,7},{7,6},{8,9},{9,8},{10,11... | collective-permute-start | bytes 1572872 | tf_op jit(solution)/shard_map/ppermute | solution.py:342
  15.8 1.3 copy-start.5
  31.0 0.8 copy-start.12
  31.8 1.0 copy-start.13
  52.7 2.4 %copy-start.3 = (bf16[1,128,8192]{2,1,0:T(8,128)(2,1)S(1)}, bf16[1,128,8192]{2,1,0:T(8,128)(2,1)}, u32[]{:S(2)}) copy-start(bf16[1,128,8192]{2,1,0:T(8,128)(2,1)} %param.11) | copy-start | bytes 6291460
  52.7 3.0 %copy-start.6 = (bf16[8192,128]{1,0:T(8,128)(2,1)S(1)}, bf16[8192,128]{1,0:T(8,128)(2,1)}, u32[]{:S(2)}) copy-start(bf16[8192,128]{1,0:T(8,128)(2,1)} %copy-done.5) | copy-start | bytes 6291460
  55.1 34.9 %copy-start = (bf16[8192,128]{1,0:T(8,128)(2,1)}, bf16[8192,128]{1,0:T(8,128)(2,1)S(1)}, u32[]{:S(2)}) copy-start(bf16[8192,128]{1,0:T(8,128)(2,1)S(1)} %get-tuple-element.90) | copy-start | bytes 6291460
  66.5 35.5 %copy-start.11 = (f32[8,512,128]{2,1,0:T(8,128)}, f32[8,512,128]{2,1,0:T(8,128)S(1)}, u32[]{:S(2)}) copy-start(f32[8,512,128]{2,1,0:T(8,128)S(1)} %get-tuple-element.93) | copy-start | bytes 6291460
  66.6 2.7 %collective-permute-start.4 = (f16[8,512,128]{2,1,0:T(8,128)(2,1)S(1)}, f16[8,512,128]{2,1,0:T(8,128)(2,1)S(1)}, u32[]{:S(2)}, u32[]{:S(2)}) collective-permute-start(f16[8,512,128]{2,1,0:T(8,128)(2,1)S(1)} %convert_element_type.212), channel_id=1, source_target_pairs={{0,2},{2,0},{4,6},{6,4},{8,10},{10,8},{12,14},{14,12},{16,18},{18,... | collective-permute-start | bytes 3145736 | tf_op jit(solution)/shard_map/ppermute | solution.py:327
  69.3 32.6 %copy-start.15 = (f16[8,512,128]{2,1,0:T(8,128)(2,1)}, f16[8,512,128]{2,1,0:T(8,128)(2,1)S(1)}, u32[]{:S(2)}) copy-start(f16[8,512,128]{2,1,0:T(8,128)(2,1)S(1)} %collective-permute-done.4) | copy-start | bytes 3145732
  69.5 14.0 %collective-permute-start.5 = (f16[4,512,128]{2,1,0:T(8,128)(2,1)S(1)}, f16[4,512,128]{2,1,0:T(8,128)(2,1)S(1)}, u32[]{:S(2)}, u32[]{:S(2)}) collective-permute-start(f16[4,512,128]{2,1,0:T(8,128)(2,1)S(1)} %add_convert_fusion.3), channel_id=1, source_target_pairs={{0,4},{2,6},{4,0},{6,2},{8,12},{10,14},{12,8},{14,10},{16,20},{18,... | collective-permute-start | bytes 1572872 | tf_op jit(solution)/shard_map/ppermute | solution.py:327
  82.0 20.1 %copy-start.10 = (f32[8,512,128]{2,1,0:T(8,128)}, f32[8,512,128]{2,1,0:T(8,128)S(1)}, u32[]{:S(2)}) copy-start(f32[8,512,128]{2,1,0:T(8,128)S(1)} %get-tuple-element.99) | copy-start | bytes 6291460
  83.5 18.4 %copy-start.19 = (f16[4,512,128]{2,1,0:T(8,128)(2,1)}, f16[4,512,128]{2,1,0:T(8,128)(2,1)S(1)}, u32[]{:S(2)}) copy-start(f16[4,512,128]{2,1,0:T(8,128)(2,1)S(1)} %collective-permute-done.5) | copy-start | bytes 1572868
  83.7 2.7 %collective-permute-start.6 = (f16[8,512,128]{2,1,0:T(8,128)(2,1)S(1)}, f16[8,512,128]{2,1,0:T(8,128)(2,1)S(1)}, u32[]{:S(2)}, u32[]{:S(2)}) collective-permute-start(f16[8,512,128]{2,1,0:T(8,128)(2,1)S(1)} %convert_element_type.220), channel_id=1, source_target_pairs={{0,2},{2,0},{4,6},{6,4},{8,10},{10,8},{12,14},{14,12},{16,18},{18,... | collective-permute-start | bytes 3145736 | tf_op jit(solution)/shard_map/ppermute | solution.py:327
  86.4 15.7 %copy-start.14 = (f16[8,512,128]{2,1,0:T(8,128)(2,1)}, f16[8,512,128]{2,1,0:T(8,128)(2,1)S(1)}, u32[]{:S(2)}) copy-start(f16[8,512,128]{2,1,0:T(8,128)(2,1)S(1)} %collective-permute-done.6) | copy-start | bytes 3145732
  86.6 15.5 %collective-permute-start.8 = (f16[4,512,128]{2,1,0:T(8,128)(2,1)S(1)}, f16[4,512,128]{2,1,0:T(8,128)(2,1)S(1)}, u32[]{:S(2)}, u32[]{:S(2)}) collective-permute-start(f16[4,512,128]{2,1,0:T(8,128)(2,1)S(1)} %add_convert_fusion.2), channel_id=1, source_target_pairs={{0,4},{2,6},{4,0},{6,2},{8,12},{10,14},{12,8},{14,10},{16,20},{18,... | collective-permute-start | bytes 1572872 | tf_op jit(solution)/shard_map/ppermute | solution.py:327
  88.3 13.6 %collective-permute-start.7 = (f16[2,512,128]{2,1,0:T(8,128)(2,1)S(1)}, f16[2,512,128]{2,1,0:T(8,128)(2,1)S(1)}, u32[]{:S(2)}, u32[]{:S(2)}) collective-permute-start(f16[2,512,128]{2,1,0:T(8,128)(2,1)S(1)} %add_convert_fusion.7), channel_id=1, source_target_pairs={{0,8},{2,10},{4,12},{6,14},{8,0},{10,2},{12,4},{14,6},{16,24},{18,... | collective-permute-start | bytes 786440 | tf_op jit(solution)/shard_map/ppermute | solution.py:327
  100.6 1.7 copy-start.8
  102.0 0.7 copy-start.20
  102.1 0.8 copy-start.17
  102.9 3.0 %collective-permute-start.9 = (f16[8,512,128]{2,1,0:T(8,128)(2,1)}, f16[8,512,128]{2,1,0:T(8,128)(2,1)}, u32[]{:S(2)}, u32[]{:S(2)}) collective-permute-start(f16[8,512,128]{2,1,0:T(8,128)(2,1)} %convert_element_type.225), channel_id=1, source_target_pairs={{0,2},{2,0},{4,6},{6,4},{8,10},{10,8},{12,14},{14,12},{16,18},{18,... | collective-permute-start | bytes 3145736 | tf_op jit(solution)/shard_map/ppermute | solution.py:327
  104.0 7.8 %copy-start.1 = (bf16[8192,128]{1,0:T(8,128)(2,1)S(1)}, bf16[8192,128]{1,0:T(8,128)(2,1)}, u32[]{:S(2)}) copy-start(bf16[8192,128]{1,0:T(8,128)(2,1)} %copy-done) | copy-start | bytes 6291460
  104.0 7.8 %copy-start.4 = (bf16[1,128,8192]{2,1,0:T(8,128)(2,1)S(1)}, bf16[1,128,8192]{2,1,0:T(8,128)(2,1)}, u32[]{:S(2)}) copy-start(bf16[1,128,8192]{2,1,0:T(8,128)(2,1)} %param.11) | copy-start | bytes 6291460
  107.4 17.1 %collective-permute-start.12 = (f16[1,512,128]{2,1,0:T(8,128)(2,1)S(1)}, f16[1,512,128]{2,1,0:T(8,128)(2,1)S(1)}, u32[]{:S(2)}, u32[]{:S(2)}) collective-permute-start(f16[1,512,128]{2,1,0:T(8,128)(2,1)S(1)} %add_convert_fusion.11), channel_id=1, source_target_pairs={{0,16},{2,18},{4,20},{6,22},{8,24},{10,26},{12,28},{14,30},{16,0},... | collective-permute-start | bytes 393224 | tf_op jit(solution)/shard_map/ppermute | solution.py:327
  110.0 16.5 %collective-permute-start.11 = (f16[2,512,128]{2,1,0:T(8,128)(2,1)S(1)}, f16[2,512,128]{2,1,0:T(8,128)(2,1)S(1)}, u32[]{:S(2)}, u32[]{:S(2)}) collective-permute-start(f16[2,512,128]{2,1,0:T(8,128)(2,1)S(1)} %add_convert_fusion.6), channel_id=1, source_target_pairs={{0,8},{2,10},{4,12},{6,14},{8,0},{10,2},{12,4},{14,6},{16,24},{18,... | collective-permute-start | bytes 786440 | tf_op jit(solution)/shard_map/ppermute | solution.py:327
  110.5 17.1 %collective-permute-start.10 = (f16[4,512,128]{2,1,0:T(8,128)(2,1)S(1)}, f16[4,512,128]{2,1,0:T(8,128)(2,1)S(1)}, u32[]{:S(2)}, u32[]{:S(2)}) collective-permute-start(f16[4,512,128]{2,1,0:T(8,128)(2,1)S(1)} %add_convert_fusion.1), channel_id=1, source_target_pairs={{0,4},{2,6},{4,0},{6,2},{8,12},{10,14},{12,8},{14,10},{16,20},{18,... | collective-permute-start | bytes 1572872 | tf_op jit(solution)/shard_map/ppermute | solution.py:327
  111.9 1.6 copy-start.7
  124.3 1.0 copy-start.21
  124.3 2.2 copy-start.18
  124.3 3.3 %copy-start.9 = (f32[8,512,128]{2,1,0:T(8,128)S(1)}, f32[8,512,128]{2,1,0:T(8,128)}, u32[]{:S(2)}) copy-start(f32[8,512,128]{2,1,0:T(8,128)} %copy-done.8) | copy-start | bytes 6291460
  128.7 2.7 %collective-permute-start.13 = (f16[8,512,128]{2,1,0:T(8,128)(2,1)S(1)}, f16[8,512,128]{2,1,0:T(8,128)(2,1)S(1)}, u32[]{:S(2)}, u32[]{:S(2)}) collective-permute-start(f16[8,512,128]{2,1,0:T(8,128)(2,1)S(1)} %convert_element_type.244), channel_id=1, source_target_pairs={{0,2},{2,0},{4,6},{6,4},{8,10},{10,8},{12,14},{14,12},{16,18},{18,... | collective-permute-start | bytes 3145736 | tf_op jit(solution)/shard_map/ppermute | solution.py:327
  131.6 14.0 %collective-permute-start.14 = (f16[4,512,128]{2,1,0:T(8,128)(2,1)S(1)}, f16[4,512,128]{2,1,0:T(8,128)(2,1)S(1)}, u32[]{:S(2)}, u32[]{:S(2)}) collective-permute-start(f16[4,512,128]{2,1,0:T(8,128)(2,1)S(1)} %add_convert_fusion), channel_id=1, source_target_pairs={{0,4},{2,6},{4,0},{6,2},{8,12},{10,14},{12,8},{14,10},{16,20},{18,... | collective-permute-start | bytes 1572872 | tf_op jit(solution)/shard_map/ppermute | solution.py:327
  132.3 9.1 %collective-permute-start.15 = (bf16[1,512,128]{2,1,0:T(8,128)(2,1)S(1)}, bf16[1,512,128]{2,1,0:T(8,128)(2,1)S(1)}, u32[]{:S(2)}, u32[]{:S(2)}) collective-permute-start(bf16[1,512,128]{2,1,0:T(8,128)(2,1)S(1)} %get-tuple-element.121), channel_id=1, source_target_pairs={{0,16},{2,18},{4,20},{6,22},{8,24},{10,26},{12,28},{14,30},{16,0},... | collective-permute-start | bytes 393224 | tf_op jit(solution)/shard_map/ppermute | solution.py:327
  132.7 16.8 %collective-permute-start.21 = (f16[2,512,128]{2,1,0:T(8,128)(2,1)S(1)}, f16[2,512,128]{2,1,0:T(8,128)(2,1)S(1)}, u32[]{:S(2)}, u32[]{:S(2)}) collective-permute-start(f16[2,512,128]{2,1,0:T(8,128)(2,1)S(1)} %add_convert_fusion.5), channel_id=1, source_target_pairs={{0,8},{2,10},{4,12},{6,14},{8,0},{10,2},{12,4},{14,6},{16,24},{18,... | collective-permute-start | bytes 786440 | tf_op jit(solution)/shard_map/ppermute | solution.py:327
  141.5 10.3 %collective-permute-start.30 = (bf16[2,512,128]{2,1,0:T(8,128)(2,1)S(1)}, bf16[2,512,128]{2,1,0:T(8,128)(2,1)S(1)}, u32[]{:S(2)}, u32[]{:S(2)}) collective-permute-start(bf16[2,512,128]{2,1,0:T(8,128)(2,1)S(1)} %get-tuple-element.159), channel_id=1, source_target_pairs={{0,8},{2,10},{4,12},{6,14},{8,0},{10,2},{12,4},{14,6},{16,24},{18,... | collective-permute-start | bytes 786440 | tf_op jit(solution)/shard_map/ppermute | solution.py:327
  141.6 7.9 %collective-permute-start.26 = (f16[1,512,128]{2,1,0:T(8,128)(2,1)S(1)}, f16[1,512,128]{2,1,0:T(8,128)(2,1)S(1)}, u32[]{:S(2)}, u32[]{:S(2)}) collective-permute-start(f16[1,512,128]{2,1,0:T(8,128)(2,1)S(1)} %add_convert_fusion.10), channel_id=1, source_target_pairs={{0,16},{2,18},{4,20},{6,22},{8,24},{10,26},{12,28},{14,30},{16,0},... | collective-permute-start | bytes 393224 | tf_op jit(solution)/shard_map/ppermute | solution.py:327
  151.8 18.2 %collective-permute-start.31 = (bf16[4,512,128]{2,1,0:T(8,128)(2,1)S(1)}, bf16[4,512,128]{2,1,0:T(8,128)(2,1)S(1)}, u32[]{:S(2)}, u32[]{:S(2)}) collective-permute-start(bf16[4,512,128]{2,1,0:T(8,128)(2,1)S(1)} %constant_dynamic-update-slice_fusion.2.refs_0_), channel_id=1, source_target_pairs={{0,4},{2,6},{4,0},{6,2},{8,12},{10,14},{12,8},{14,10},{16,20},{18,... | collective-permute-start | bytes 1572872 | tf_op jit(solution)/shard_map/ppermute | solution.py:327
  155.0 11.6 %collective-permute-start.27 = (bf16[1,512,128]{2,1,0:T(8,128)(2,1)S(1)}, bf16[1,512,128]{2,1,0:T(8,128)(2,1)S(1)}, u32[]{:S(2)}, u32[]{:S(2)}) collective-permute-start(bf16[1,512,128]{2,1,0:T(8,128)(2,1)S(1)} %get-tuple-element.147), channel_id=1, source_target_pairs={{0,16},{2,18},{4,20},{6,22},{8,24},{10,26},{12,28},{14,30},{16,0},... | collective-permute-start | bytes 393224 | tf_op jit(solution)/shard_map/ppermute | solution.py:327
  157.2 11.5 %collective-permute-start.22 = (f16[1,512,128]{2,1,0:T(8,128)(2,1)S(1)}, f16[1,512,128]{2,1,0:T(8,128)(2,1)S(1)}, u32[]{:S(2)}, u32[]{:S(2)}) collective-permute-start(f16[1,512,128]{2,1,0:T(8,128)(2,1)S(1)} %add_convert_fusion.8), channel_id=1, source_target_pairs={{0,16},{2,18},{4,20},{6,22},{8,24},{10,26},{12,28},{14,30},{16,0},... | collective-permute-start | bytes 393224 | tf_op jit(solution)/shard_map/ppermute | solution.py:327
  166.6 12.1 %collective-permute-start.28 = (bf16[2,512,128]{2,1,0:T(8,128)(2,1)S(1)}, bf16[2,512,128]{2,1,0:T(8,128)(2,1)S(1)}, u32[]{:S(2)}, u32[]{:S(2)}) collective-permute-start(bf16[2,512,128]{2,1,0:T(8,128)(2,1)S(1)} %pad_maximum_fusion.6), channel_id=1, source_target_pairs={{0,8},{2,10},{4,12},{6,14},{8,0},{10,2},{12,4},{14,6},{16,24},{18,... | collective-permute-start | bytes 786440 | tf_op jit(solution)/shard_map/ppermute | solution.py:327
  166.7 16.8 %collective-permute-start.16 = (f16[2,512,128]{2,1,0:T(8,128)(2,1)S(1)}, f16[2,512,128]{2,1,0:T(8,128)(2,1)S(1)}, u32[]{:S(2)}, u32[]{:S(2)}) collective-permute-start(f16[2,512,128]{2,1,0:T(8,128)(2,1)S(1)} %add_convert_fusion.4), channel_id=1, source_target_pairs={{0,8},{2,10},{4,12},{6,14},{8,0},{10,2},{12,4},{14,6},{16,24},{18,... | collective-permute-start | bytes 786440 | tf_op jit(solution)/shard_map/ppermute | solution.py:327
  168.7 22.7 %collective-permute-start.32 = (bf16[4,512,128]{2,1,0:T(8,128)(2,1)S(1)}, bf16[4,512,128]{2,1,0:T(8,128)(2,1)S(1)}, u32[]{:S(2)}, u32[]{:S(2)}) collective-permute-start(bf16[4,512,128]{2,1,0:T(8,128)(2,1)S(1)} %constant_dynamic-update-slice_fusion.2.refs_0_), channel_id=1, source_target_pairs={{0,2},{2,0},{4,6},{6,4},{8,10},{10,8},{12,14},{14,12},{16,18},{18,... | collective-permute-start | bytes 1572872 | tf_op jit(solution)/shard_map/ppermute | solution.py:327
  169.8 10.3 %collective-permute-start.23 = (bf16[1,512,128]{2,1,0:T(8,128)(2,1)S(1)}, bf16[1,512,128]{2,1,0:T(8,128)(2,1)S(1)}, u32[]{:S(2)}, u32[]{:S(2)}) collective-permute-start(bf16[1,512,128]{2,1,0:T(8,128)(2,1)S(1)} %get-tuple-element.149), channel_id=1, source_target_pairs={{0,16},{2,18},{4,20},{6,22},{8,24},{10,26},{12,28},{14,30},{16,0},... | collective-permute-start | bytes 393224 | tf_op jit(solution)/shard_map/ppermute | solution.py:327
  170.0 21.5 %collective-permute-start.33 = (bf16[4,512,128]{2,1,0:T(8,128)(2,1)S(1)}, bf16[4,512,128]{2,1,0:T(8,128)(2,1)S(1)}, u32[]{:S(2)}, u32[]{:S(2)}) collective-permute-start(bf16[4,512,128]{2,1,0:T(8,128)(2,1)S(1)} %collective-permute-done.31.refs_1_), channel_id=1, source_target_pairs={{0,2},{2,0},{4,6},{6,4},{8,10},{10,8},{12,14},{14,12},{16,18},{18,... | collective-permute-start | bytes 1572872 | tf_op jit(solution)/shard_map/ppermute | solution.py:327
  178.8 14.2 %collective-permute-start.29 = (bf16[4,512,128]{2,1,0:T(8,128)(2,1)S(1)}, bf16[4,512,128]{2,1,0:T(8,128)(2,1)S(1)}, u32[]{:S(2)}, u32[]{:S(2)}) collective-permute-start(bf16[4,512,128]{2,1,0:T(8,128)(2,1)S(1)} %pad_maximum_fusion.3.refs_0_), channel_id=1, source_target_pairs={{0,4},{2,6},{4,0},{6,2},{8,12},{10,14},{12,8},{14,10},{16,20},{18,... | collective-permute-start | bytes 1572872 | tf_op jit(solution)/shard_map/ppermute | solution.py:327
  180.1 11.3 %collective-permute-start.24 = (bf16[2,512,128]{2,1,0:T(8,128)(2,1)S(1)}, bf16[2,512,128]{2,1,0:T(8,128)(2,1)S(1)}, u32[]{:S(2)}, u32[]{:S(2)}) collective-permute-start(bf16[2,512,128]{2,1,0:T(8,128)(2,1)S(1)} %pad_maximum_fusion.5), channel_id=1, source_target_pairs={{0,8},{2,10},{4,12},{6,14},{8,0},{10,2},{12,4},{14,6},{16,24},{18,... | collective-permute-start | bytes 786440 | tf_op jit(solution)/shard_map/ppermute | solution.py:327
  183.5 10.0 %collective-permute-start.17 = (f16[1,512,128]{2,1,0:T(8,128)(2,1)S(1)}, f16[1,512,128]{2,1,0:T(8,128)(2,1)S(1)}, u32[]{:S(2)}, u32[]{:S(2)}) collective-permute-start(f16[1,512,128]{2,1,0:T(8,128)(2,1)S(1)} %add_convert_fusion.9), channel_id=1, source_target_pairs={{0,16},{2,18},{4,20},{6,22},{8,24},{10,26},{12,28},{14,30},{16,0},... | collective-permute-start | bytes 393224 | tf_op jit(solution)/shard_map/ppermute | solution.py:327
  191.3 11.5 %collective-permute-start.34 = (bf16[4,512,128]{2,1,0:T(8,128)(2,1)S(1)}, bf16[4,512,128]{2,1,0:T(8,128)(2,1)S(1)}, u32[]{:S(2)}, u32[]{:S(2)}) collective-permute-start(bf16[4,512,128]{2,1,0:T(8,128)(2,1)S(1)} %pad_maximum_fusion.3.refs_0_), channel_id=1, source_target_pairs={{0,2},{2,0},{4,6},{6,4},{8,10},{10,8},{12,14},{14,12},{16,18},{18,... | collective-permute-start | bytes 1572872 | tf_op jit(solution)/shard_map/ppermute | solution.py:327
  191.4 14.4 %collective-permute-start.25 = (bf16[4,512,128]{2,1,0:T(8,128)(2,1)S(1)}, bf16[4,512,128]{2,1,0:T(8,128)(2,1)S(1)}, u32[]{:S(2)}, u32[]{:S(2)}) collective-permute-start(bf16[4,512,128]{2,1,0:T(8,128)(2,1)S(1)} %pad_maximum_fusion.2.refs_0_), channel_id=1, source_target_pairs={{0,4},{2,6},{4,0},{6,2},{8,12},{10,14},{12,8},{14,10},{16,20},{18,... | collective-permute-start | bytes 1572872 | tf_op jit(solution)/shard_map/ppermute | solution.py:327
  193.0 9.9 %collective-permute-start.35 = (bf16[4,512,128]{2,1,0:T(8,128)(2,1)S(1)}, bf16[4,512,128]{2,1,0:T(8,128)(2,1)S(1)}, u32[]{:S(2)}, u32[]{:S(2)}) collective-permute-start(bf16[4,512,128]{2,1,0:T(8,128)(2,1)S(1)} %collective-permute-done.29.refs_1_), channel_id=1, source_target_pairs={{0,2},{2,0},{4,6},{6,4},{8,10},{10,8},{12,14},{14,12},{16,18},{18,... | collective-permute-start | bytes 1572872 | tf_op jit(solution)/shard_map/ppermute | solution.py:327
  193.7 9.0 %collective-permute-start.18 = (bf16[1,512,128]{2,1,0:T(8,128)(2,1)S(1)}, bf16[1,512,128]{2,1,0:T(8,128)(2,1)S(1)}, u32[]{:S(2)}, u32[]{:S(2)}) collective-permute-start(bf16[1,512,128]{2,1,0:T(8,128)(2,1)S(1)} %get-tuple-element.151), channel_id=1, source_target_pairs={{0,16},{2,18},{4,20},{6,22},{8,24},{10,26},{12,28},{14,30},{16,0},... | collective-permute-start | bytes 393224 | tf_op jit(solution)/shard_map/ppermute | solution.py:327
  202.7 8.3 %collective-permute-start.19 = (bf16[2,512,128]{2,1,0:T(8,128)(2,1)S(1)}, bf16[2,512,128]{2,1,0:T(8,128)(2,1)S(1)}, u32[]{:S(2)}, u32[]{:S(2)}) collective-permute-start(bf16[2,512,128]{2,1,0:T(8,128)(2,1)S(1)} %pad_maximum_fusion.4), channel_id=1, source_target_pairs={{0,8},{2,10},{4,12},{6,14},{8,0},{10,2},{12,4},{14,6},{16,24},{18,... | collective-permute-start | bytes 786440 | tf_op jit(solution)/shard_map/ppermute | solution.py:327
  202.8 10.4 %collective-permute-start.36 = (bf16[4,512,128]{2,1,0:T(8,128)(2,1)S(1)}, bf16[4,512,128]{2,1,0:T(8,128)(2,1)S(1)}, u32[]{:S(2)}, u32[]{:S(2)}) collective-permute-start(bf16[4,512,128]{2,1,0:T(8,128)(2,1)S(1)} %pad_maximum_fusion.2.refs_0_), channel_id=1, source_target_pairs={{0,2},{2,0},{4,6},{6,4},{8,10},{10,8},{12,14},{14,12},{16,18},{18,... | collective-permute-start | bytes 1572872 | tf_op jit(solution)/shard_map/ppermute | solution.py:327
  205.8 7.3 %collective-permute-start.37 = (bf16[4,512,128]{2,1,0:T(8,128)(2,1)S(1)}, bf16[4,512,128]{2,1,0:T(8,128)(2,1)S(1)}, u32[]{:S(2)}, u32[]{:S(2)}) collective-permute-start(bf16[4,512,128]{2,1,0:T(8,128)(2,1)S(1)} %collective-permute-done.25.refs_1_), channel_id=1, source_target_pairs={{0,2},{2,0},{4,6},{6,4},{8,10},{10,8},{12,14},{14,12},{16,18},{18,... | collective-permute-start | bytes 1572872 | tf_op jit(solution)/shard_map/ppermute | solution.py:327
  211.1 13.4 %collective-permute-start.20 = (bf16[4,512,128]{2,1,0:T(8,128)(2,1)S(1)}, bf16[4,512,128]{2,1,0:T(8,128)(2,1)S(1)}, u32[]{:S(2)}, u32[]{:S(2)}) collective-permute-start(bf16[4,512,128]{2,1,0:T(8,128)(2,1)S(1)} %pad_maximum_fusion.1.refs_0_), channel_id=1, source_target_pairs={{0,4},{2,6},{4,0},{6,2},{8,12},{10,14},{12,8},{14,10},{16,20},{18,... | collective-permute-start | bytes 1572872 | tf_op jit(solution)/shard_map/ppermute | solution.py:327
  213.1 12.3 %collective-permute-start.38 = (bf16[4,512,128]{2,1,0:T(8,128)(2,1)S(1)}, bf16[4,512,128]{2,1,0:T(8,128)(2,1)S(1)}, u32[]{:S(2)}, u32[]{:S(2)}) collective-permute-start(bf16[4,512,128]{2,1,0:T(8,128)(2,1)S(1)} %pad_maximum_fusion.1.refs_0_), channel_id=1, source_target_pairs={{0,2},{2,0},{4,6},{6,4},{8,10},{10,8},{12,14},{14,12},{16,18},{18,... | collective-permute-start | bytes 1572872 | tf_op jit(solution)/shard_map/ppermute | solution.py:327
  224.4 1.9 collective-permute-start.39

commit v6 on v5

--- a/solution.py
+++ b/solution.py
@@ -265,46 +265,6 @@
     )(mine, *banks, *turned, pinned(start), pinned(first), pinned(second), *products, target, count)
 
 
-def assemble_kernel(chunk, offsets, place_ref, *refs):
-    received = refs[: len(offsets)]
-    out_ref, semaphore = refs[-2:]
-    width = received[0].shape[-1]
-    mine = place_ref[0]
-    copies = []
-    for ref, group in zip(received, offsets):
-        for entry, offset in enumerate(group):
-            copies.append(
-                pltpu.make_async_copy(
-                    ref.at[entry],
-                    out_ref.at[lax.bitwise_xor(mine, offset), :, pl.ds(chunk * width, width)],
-                    semaphore.at[len(copies)],
-                )
-            )
-    for copy in copies:
-        copy.start()
-    for copy in copies:
-        copy.wait()
-
-
-def assemble(chunk, place, received, offsets, shape, before):
-    vmem = pl.BlockSpec(memory_space=pltpu.VMEM)
-    return pl.pallas_call(
-        functools.partial(assemble_kernel, chunk, offsets),
-        in_specs=[pl.BlockSpec(memory_space=pltpu.SMEM)]
-        + [vmem] * len(received)
-        + [pl.BlockSpec(memory_space=pl.ANY)] * len(before),
-        out_specs=pl.BlockSpec(memory_space=pl.ANY),
-        out_shape=jax.ShapeDtypeStruct(shape, BF16),
-        input_output_aliases={1 + len(received): 0} if before else {},
-        scratch_shapes=[pltpu.SemaphoreType.DMA((sum(map(len, offsets)),))],
-        compiler_params=pltpu.CompilerParams(vmem_limit_bytes=12 * MIB),
-        cost_estimate=pl.CostEstimate(
-            flops=0, bytes_accessed=4 * shape[0] * shape[1] * received[0].shape[-1], transcendentals=0
-        ),
-        name="assemble",
-    )(place, *received, *before)
-
-
 def tied(first, second):
     return lax.optimization_barrier((first, second))
 
@@ -377,44 +337,32 @@
     def sent(outgoing, span):
         return [swapped(array, offset) for array, offset in zip(outgoing, span[1:])]
 
-    new_momentum = []
     result = ()
 
-    def chain(chunk, send, keep):
-        send = yield send
-        terms = [keep, swapped(send, 1)]
+    def chain(chunk, keep, arrived):
+        terms = [keep, arrived]
         for span in spans:
             outgoing, terms = parted(terms, span)
             outgoing = yield outgoing
-            terms = terms + held_back(sent(outgoing, span))
+            arrived = yield sent(outgoing, span)
+            terms = terms + arrived
         total = sum(term.astype(F32) for term in terms)[0]
         average = total * (1.0 / (WIRE_SCALE * reps))
         moved = 0.9 * shares[chunk][0] + average
-        stack = (shares[chunk][1].astype(F32) - 0.7 * (average + 0.9 * moved)).astype(BF16)[None]
-        offsets = [0]
-        for span in spans[:0:-1]:
-            stack = yield stack
-            arrived = held_back(sent([stack] * (len(span) - 1), span))
-            stack = jnp.concatenate([stack] + arrived)
-            offsets = [offset ^ far for far in span for offset in offsets]
-        stack = yield stack
-        across = swapped(stack, 2)
-        finished[chunk] = (moved, stack, across, offsets)
+        fresh = (shares[chunk][1].astype(F32) - 0.7 * (average + 0.9 * moved)).astype(BF16)
+        finished[chunk] = (moved, fresh)
+        yield fresh
 
     finished = {}
     running = {}
     formed = {}
-    gate = []
-
-    def held_back(arrived):
-        return tied(arrived, gate)[0] if gate else arrived
 
     def move_on(which, behind=()):
-        gate[:] = [formed[other] for other in behind]
-        try:
-            formed[which] = running[which].send(formed[which])
-        except StopIteration:
-            del formed[which]
+        which = [chunk for chunk in which if chunk not in finished]
+        arrived = {chunk: running[chunk].send(formed[chunk]) for chunk in which}
+        arrived, _ = tied(arrived, [formed[chunk] for chunk in behind])
+        for chunk in which:
+            formed[chunk] = running[chunk].send(arrived[chunk])
 
     token = place
     for chunk in range(chunks):
@@ -422,34 +370,50 @@
             chunk, width, token, banks, turned, start, first, second, products, target, count, tokens
         )
         send = send.astype(WIRE)
-        for earlier in list(formed):
-            move_on(earlier)
-            formed[earlier], send = tied(formed[earlier], send)
-        running[chunk] = chain(chunk, send, keep)
-        formed[chunk] = running[chunk].send(next(running[chunk]))
+        if chunk:
+            move_on(range(chunk))
+            formed, send = tied(formed, send)
+        running[chunk] = chain(chunk, keep, swapped(send, 1))
+        formed[chunk] = next(running[chunk])
         if chunk + 1 < chunks:
             formed, token = tied(formed, token)
-    if chunks == 4:
-        move_on(0, behind=[3])
-        move_on(3, behind=[0])
-        for which in (1, 2, 0):
-            move_on(which, behind=[3])
-    for which in range(chunks):
-        while which in formed:
-            move_on(which)
-
-    for chunk in range(chunks):
-        moved, stack, across, offsets = finished[chunk]
-        new_momentum.append(moved)
-        offsets = [[offset ^ low for offset in offsets] for low in (0, 2, 1, 3)]
-        if result:
-            across, *result = tied(across, result[0])
-        received = [stack, across, swapped(stack, 1), swapped(across, 1)]
-        result = (
-            assemble(chunk, place, received, offsets, (reps, rows, columns), result),
-        )
-
-    return result[0].reshape(depth, columns), jnp.concatenate(new_momentum, axis=1)
+
+    head = chunks - 1
+    move_on(range(head), behind=[head])
+    while head not in finished:
+        move_on(range(chunks))
+
+    group = max(chunks // 2, 1)
+    for begin in range(0, chunks, group):
+        fresh = jnp.concatenate([finished[chunk][1] for chunk in range(begin, begin + group)], axis=1)
+        gathered = lax.all_gather(fresh, "rep", axis=0, tiled=True)
+        result = (join(begin // group, columns, gathered, result),)
+    new_momentum = [finished[chunk][0] for chunk in range(chunks)]
+
+    return result[0], jnp.concatenate(new_momentum, axis=1)
+
+
+def join_kernel(part_ref, *refs):
+    refs[-1][...] = part_ref[...]
+
+
+def join(place, columns, part, before):
+    depth, width = part.shape
+    block = depth // 8
+    return pl.pallas_call(
+        join_kernel,
+        grid=(depth // block,),
+        in_specs=[pl.BlockSpec((block, width), lambda d: (d, 0))]
+        + [pl.BlockSpec(memory_space=pl.ANY)] * len(before),
+        out_specs=pl.BlockSpec((block, width), lambda d: (d, place)),
+        out_shape=jax.ShapeDtypeStruct((depth, columns), BF16),
+        input_output_aliases={1: 0} if before else {},
+        compiler_params=pltpu.CompilerParams(vmem_limit_bytes=8 * MIB),
+        cost_estimate=pl.CostEstimate(
+            flops=0, bytes_accessed=4 * depth * width, transcendentals=0
+        ),
+        name="join",
+    )(part, *before)
 
 
 def solution(mesh):

time: 229 us -> 277 us (1.21)
  waiting for transfers between devices: 101 us -> 132 us
  starting transfers between devices: 35.5 us -> 20.4 us
  between operations: 1.41 us -> 14.5 us
  other arithmetic: 12.6 us -> 23.7 us
  local copies, waits for them, and re-layouts: 14.7 us -> 21.1 us
    all_gather x0 -> x2, waiting for transfers between devices: none -> 52.6 us  [per_device(): gathered = lax.all_gather(fresh, 'rep', axis=0, tiled=True)]
    ppermute x36 -> x16, waiting for transfers between devices: 74.4 us -> 54.1 us  [swapped(): return lax.ppermute(array, 'rep', pairs)]
    ppermute x36 -> x16, starting transfers between devices: 30.4 us -> 15.3 us  [swapped(): return lax.ppermute(array, 'rep', pairs)]
    unnamed x48 -> x66, local copies, waits for them, and re-layouts: 6.97 us -> 12 us
    convert_element_type x12, other arithmetic: 5.62 us -> 10.4 us  [parted(): sum((term.astype(F32) for term in part)).astype(WIRE)]
    add x4, other arithmetic: 3.68 us -> 6.91 us  [chain(): moved = 0.9 * shares[chunk][0] + average]
    pallas_call x4 -> x2, Pallas kernels: 5.76 us -> 6.95 us  [join(): pl.pallas_call(join_kernel, grid=(depth // block,), in_specs=[pl.BlockSpe...]
  transfers between devices with their start and end apart: 40 -> 22, of which waited for: 20 -> 16; matrix products, arithmetic and copies ran while one was open for 6% -> 7% of each run, Pallas kernels for 21% -> 17%
where the time goes in v6:
time: 277 us; the launch traced here: 275 us
  waiting for transfers between devices  132 us (48%)
  Pallas kernels  63.7 us (23%)
  other arithmetic  23.7 us (9%)
  local copies, waits for them, and re-layouts  21.1 us (8%)
  starting transfers between devices  20.4 us (7%)
  between operations  14.5 us (5%)
    ppermute x16, waiting for transfers between devices, swapped(): return lax.ppermute(array, 'rep', pairs)  54.1 us
    all_gather x2, waiting for transfers between devices, per_device(): gathered = lax.all_gather(fresh, 'rep', axis=0, tiled=True)  52.6 us
    pallas_call x4, Pallas kernels, inner(): pl.pallas_call(functools.partial(inner_kernel, float(tokens)), grid_spec=...  42.9 us
    ppermute x4, waiting for transfers between devices, per_device(): parts.append(lax.ppermute(part, 'fsdp', [(0, 1), (1, 0)]))  25.3 us
    ppermute x16, starting transfers between devices, swapped(): return lax.ppermute(array, 'rep', pairs)  15.3 us
    unnamed x66, local copies, waits for them, and re-layouts  12 us
    convert_element_type x12, other arithmetic, parted(): sum((term.astype(F32) for term in part)).astype(WIRE)  10.4 us
    pallas_call x4, Pallas kernels, arrive(): pl.pallas_call(functools.partial(arrive_kernel, piece), grid=(1,), in_spe...  8.84 us
  transfers between devices with their start and end apart: 22, of which 16 were waited for; matrix products, arithmetic and copies ran while one was open for 7% of the time, Pallas kernels for 17%

profile of v6, /device:TPU:0, one launch (start us, length us, event | category | flops | bytes accessed | tf_op | source)
XLA Modules:
  0.0 275.5 jit_solution(12674595538509136366)
XLA Ops:
  7.2 2.0 slice.344
  9.3 1.9 slice.277
  11.2 3.0 %collective-permute-start.2 = (bf16[128,2048]{1,0:T(8,128)(2,1)}, bf16[128,2048]{1,0:T(8,128)(2,1)}, u32[]{:S(2)}, u32[]{:S(2)}) collective-permute-start(bf16[128,2048]{1,0:T(8,128)(2,1)} %slice.277), channel_id=1, source_target_pairs={{0,1},{1,0},{2,3},{3,2},{4,5},{5,4},{6,7},{7,6},{8,9},{9,8},{10,11... | collective-permute-start | bytes 1572872 | tf_op jit(solution)/shard_map/ppermute | solution.py:302
  14.2 0.8 slice.278
  15.0 2.0 collective-permute-start.1
  17.0 0.8 slice.279
  18.8 5.0 %forward.1 = (bf16[8192,128]{1,0:T(8,128)(2,1)S(1)}, f32[128,512]{1,0:T(8,128)S(1)}) custom-call(bf16[128,8192]{1,0:T(8,128)(2,1)S(1)} %bitcast.72, bf16[8192,512]{1,0:T(8,128)(2,1)} %weights_ref.9), custom_call_target="tpu_custom_call" | custom-call | flops 1073741824 | bytes 12582912 | tf_op jit(solution)/shard_map/forward/pallas_call | solution.py:34
  23.8 1.3 copy-done.5
  25.4 1.0 maximum_select_fusion.target_ref
  26.4 11.9 %collective-permute-done.3.part_ref = bf16[128,2048]{1,0:T(8,128)(2,1)S(1)} collective-permute-done((bf16[128,2048]{1,0:T(8,128)(2,1)}, bf16[128,2048]{1,0:T(8,128)(2,1)S(1)}, u32[]{:S(2)}, u32[]{:S(2)}) %collective-permute-start.3) | collective-permute-done | bytes 524320 | tf_op jit(solution)/shard_map/ppermute | solution.py:302
  38.3 0.8 copy-done.15
  39.1 1.0 copy-done.16
  40.1 2.0 arrive.4
  42.2 2.2 arrive.5
  44.4 5.2 %collective-permute-done.1.part_ref = bf16[128,2048]{1,0:T(8,128)(2,1)} collective-permute-done((bf16[128,2048]{1,0:T(8,128)(2,1)}, bf16[128,2048]{1,0:T(8,128)(2,1)}, u32[]{:S(2)}, u32[]{:S(2)}) %collective-permute-start.1) | collective-permute-done | bytes 524320 | tf_op jit(solution)/shard_map/ppermute | solution.py:302
  49.7 2.2 arrive.6
  51.9 8.2 %collective-permute-done.part_ref = bf16[128,2048]{1,0:T(8,128)(2,1)} collective-permute-done((bf16[128,2048]{1,0:T(8,128)(2,1)}, bf16[128,2048]{1,0:T(8,128)(2,1)}, u32[]{:S(2)}, u32[]{:S(2)}) %collective-permute-start) | collective-permute-done | bytes 524320 | tf_op jit(solution)/shard_map/ppermute | solution.py:302
  60.1 2.3 arrive.7
  63.1 10.7 %inner.4 = (f32[8,512,128]{2,1,0:T(8,128)S(1)}, f32[8,512,128]{2,1,0:T(8,128)S(1)}) custom-call(s32[1]{0:T(128)} %bitcast.mine_ref, bf16[128,8192]{1,0:T(8,128)(2,1)S(1)} %bitcast.73, bf16[128,8192]{1,0:T(8,128)(2,1)S(1)} %get-tuple-element.82.high_ref, bf16[4,2,2,512,128]{4,3,2,1,0:T(8,128)(2,1)S(1)} %bitcast.77, bf16[4,2,2,512,128]{4,3,2,1,0:T(8,128)(2,1)S(1)} %bitcast.64, ...), custom_call_target="tpu_custom_call" | custom-call | flops 1610612736 | bytes 20971520 | tf_op jit(solution)/shard_map/inner/pallas_call | solution.py:228
  74.1 2.6 collective-permute-done.4
  76.8 1.8 collective-permute-start.5
  78.6 10.7 %inner.5 = (f32[8,512,128]{2,1,0:T(8,128)S(1)}, f32[8,512,128]{2,1,0:T(8,128)S(1)}) custom-call(s32[1]{0:T(128)} %bitcast.mine_ref, bf16[128,8192]{1,0:T(8,128)(2,1)S(1)} %bitcast.74, bf16[128,8192]{1,0:T(8,128)(2,1)S(1)} %get-tuple-element.82.high_ref, bf16[4,2,2,512,128]{4,3,2,1,0:T(8,128)(2,1)S(1)} %bitcast.78, bf16[4,2,2,512,128]{4,3,2,1,0:T(8,128)(2,1)S(1)} %bitcast.65, ...), custom_call_target="tpu_custom_call" | custom-call | flops 1610612736 | bytes 20971520 | tf_op jit(solution)/shard_map/inner/pallas_call | solution.py:228
  89.5 1.4 collective-permute-done.5
  91.1 2.6 collective-permute-done.6
  93.9 1.8 collective-permute-start.8
  95.6 1.6 collective-permute-start.7
  97.2 10.7 %inner.6 = (f32[8,512,128]{2,1,0:T(8,128)S(1)}, f32[8,512,128]{2,1,0:T(8,128)S(1)}) custom-call(s32[1]{0:T(128)} %bitcast.mine_ref, bf16[128,8192]{1,0:T(8,128)(2,1)S(1)} %bitcast.75, bf16[128,8192]{1,0:T(8,128)(2,1)S(1)} %get-tuple-element.82.high_ref, bf16[4,2,2,512,128]{4,3,2,1,0:T(8,128)(2,1)S(1)} %bitcast.79, bf16[4,2,2,512,128]{4,3,2,1,0:T(8,128)(2,1)S(1)} %bitcast.66, ...), custom_call_target="tpu_custom_call" | custom-call | flops 1610612736 | bytes 20971520 | tf_op jit(solution)/shard_map/inner/pallas_call | solution.py:228
  107.9 1.2 convert_element_type.228
  109.2 1.0 add_convert_fusion.6
  111.0 3.0 %collective-permute-done.9 = f16[8,512,128]{2,1,0:T(8,128)(2,1)} collective-permute-done((f16[8,512,128]{2,1,0:T(8,128)(2,1)}, f16[8,512,128]{2,1,0:T(8,128)(2,1)}, u32[]{:S(2)}, u32[]{:S(2)}) %collective-permute-start.9) | collective-permute-done | bytes 1048608 | tf_op jit(solution)/shard_map/ppermute | solution.py:287
  113.9 1.6 add_convert_fusion.1
  116.2 0.8 fusion.13
  117.0 1.4 collective-permute-start.11
  118.4 1.8 fusion.12
  120.2 2.6 collective-permute-start.10
  122.8 1.6 copy-done.7
  124.4 10.9 %inner.7 = (f32[8,512,128]{2,1,0:T(8,128)S(1)}, f32[8,512,128]{2,1,0:T(8,128)S(1)}) custom-call(s32[1]{0:T(128)} %bitcast.mine_ref, bf16[128,8192]{1,0:T(8,128)(2,1)S(1)} %bitcast.76, bf16[128,8192]{1,0:T(8,128)(2,1)S(1)} %get-tuple-element.82.high_ref, bf16[4,2,2,512,128]{4,3,2,1,0:T(8,128)(2,1)S(1)} %bitcast.80, bf16[4,2,2,512,128]{4,3,2,1,0:T(8,128)(2,1)S(1)} %bitcast.67, ...), custom_call_target="tpu_custom_call" | custom-call | flops 1610612736 | bytes 20971520 | tf_op jit(solution)/shard_map/inner/pallas_call | solution.py:228
  135.5 2.1 copy-done.11
  137.6 1.2 add_convert_fusion.5
  138.9 1.1 add_convert_fusion.10
  139.9 2.0 bitcast_add_fusion.7
  142.9 1.7 collective-permute-done.15
  144.6 0.9 add_convert_fusion
  145.5 6.0 %collective-permute-done.13 = f16[1,512,128]{2,1,0:T(8,128)(2,1)S(1)} collective-permute-done((f16[1,512,128]{2,1,0:T(8,128)(2,1)S(1)}, f16[1,512,128]{2,1,0:T(8,128)(2,1)S(1)}, u32[]{:S(2)}, u32[]{:S(2)}) %collective-permute-start.13) | collective-permute-done | bytes 131104 | tf_op jit(solution)/shard_map/ppermute | solution.py:287
  151.6 1.9 collective-permute-done.14
  153.4 2.0 bitcast_add_fusion.1
  156.9 1.1 add_convert_fusion.9
  158.0 2.5 collective-permute-start.16
  160.5 5.9 %collective-permute-done.16 = f16[1,512,128]{2,1,0:T(8,128)(2,1)S(1)} collective-permute-done((f16[1,512,128]{2,1,0:T(8,128)(2,1)S(1)}, f16[1,512,128]{2,1,0:T(8,128)(2,1)S(1)}, u32[]{:S(2)}, u32[]{:S(2)}) %collective-permute-start.16) | collective-permute-done | bytes 131104 | tf_op jit(solution)/shard_map/ppermute | solution.py:287
  166.4 6.5 %collective-permute-done.17 = f16[4,512,128]{2,1,0:T(8,128)(2,1)S(1)} collective-permute-done((f16[4,512,128]{2,1,0:T(8,128)(2,1)}, f16[4,512,128]{2,1,0:T(8,128)(2,1)S(1)}, u32[]{:S(2)}, u32[]{:S(2)}) %collective-permute-start.17) | collective-permute-done | bytes 524320 | tf_op jit(solution)/shard_map/ppermute | solution.py:287
  172.9 1.2 add_convert_fusion.4
  174.5 9.1 %collective-permute-done.18 = f16[2,512,128]{2,1,0:T(8,128)(2,1)S(1)} collective-permute-done((f16[2,512,128]{2,1,0:T(8,128)(2,1)S(1)}, f16[2,512,128]{2,1,0:T(8,128)(2,1)S(1)}, u32[]{:S(2)}, u32[]{:S(2)}) %collective-permute-start.18) | collective-permute-done | bytes 262176 | tf_op jit(solution)/shard_map/ppermute | solution.py:287
  183.5 1.1 add_convert_fusion.8
  184.7 0.9 collective-permute-start.19
  185.6 1.8 bitcast_add_fusion.5
  187.5 13.3 %collective-permute-done.19 = f16[1,512,128]{2,1,0:T(8,128)(2,1)S(1)} collective-permute-done((f16[1,512,128]{2,1,0:T(8,128)(2,1)S(1)}, f16[1,512,128]{2,1,0:T(8,128)(2,1)S(1)}, u32[]{:S(2)}, u32[]{:S(2)}) %collective-permute-start.19) | collective-permute-done | bytes 131104 | tf_op jit(solution)/shard_map/ppermute | solution.py:287
  200.8 1.1 bitcast_add_fusion.3
  202.7 2.1 pad_maximum_fusion
  204.7 6.6 %all-gather.5.cloned.1.call-done.part_ref = bf16[8192,256]{1,0:T(8,128)(2,1)} async-done(((bf16[512,256]{1,0:T(8,128)(2,1)}), bf16[8192,256]{1,0:T(8,128)(2,1)}) %all-gather.5.cloned.1.call-update) | async-done | bytes 4194320 | tf_op jit(solution)/shard_map/all_gather | solution.py:389
  211.4 2.2 copy-done.8
  213.6 3.5 %join.2.refs_0_ = bf16[8192,512]{1,0:T(8,128)(2,1)} custom-call(bf16[8192,256]{1,0:T(8,128)(2,1)S(1)} %copy-done.8), custom_call_target="tpu_custom_call" | custom-call | bytes 8388608 | tf_op jit(solution)/shard_map/join/pallas_call | solution.py:403
  217.0 45.9 %all-gather.3.cloned.1.call-done.part_ref = bf16[8192,256]{1,0:T(8,128)(2,1)} async-done(((bf16[512,256]{1,0:T(8,128)(2,1)}), bf16[8192,256]{1,0:T(8,128)(2,1)}) %all-gather.3.cloned.1.call-update) | async-done | bytes 4194320 | tf_op jit(solution)/shard_map/all_gather | solution.py:389
  263.0 2.2 copy-done.9
  265.2 3.5 %join.3 = bf16[8192,512]{1,0:T(8,128)(2,1)} custom-call(bf16[8192,256]{1,0:T(8,128)(2,1)S(1)} %copy-done.9, bf16[8192,512]{1,0:T(8,128)(2,1)} %join.2.refs_0_), custom_call_target="tpu_custom_call", output_to_operand_aliasing={{}: (1, {})} | custom-call | bytes 8388608 | tf_op jit(solution)/shard_map/join/pallas_call | solution.py:403
  (97 shorter events, 7.9 us)
Async XLA Ops:
  7.2 7.0 %copy-start.2 = (bf16[1,128,8192]{2,1,0:T(8,128)(2,1)S(1)}, bf16[1,128,8192]{2,1,0:T(8,128)(2,1)}, u32[]{:S(2)}) copy-start(bf16[1,128,8192]{2,1,0:T(8,128)(2,1)} %param.11) | copy-start | bytes 6291460
  7.2 204.2 %all-gather.5.cloned.1.call-start = ((), (), s32[]{:S(2)}) async-start(), calls=%async_computation.1 | async-start | bytes 4456448 | tf_op jit(solution)/shard_map/all_gather | solution.py:389
  7.2 10.6 %copy-start.32 = (s32[1,2,512]{2,1,0:T(2,128)S(1)}, s32[1,2,512]{2,1,0:T(2,128)}, u32[]{:S(2)}) copy-start(s32[1,2,512]{2,1,0:T(2,128)} %param.13) | copy-start | bytes 12292
  7.2 10.9 %copy-start.20 = (bf16[1,256,512]{2,1,0:T(8,128)(2,1)S(1)}, bf16[1,256,512]{2,1,0:T(8,128)(2,1)}, u32[]{:S(2)}) copy-start(bf16[1,256,512]{2,1,0:T(8,128)(2,1)} %param.12) | copy-start | bytes 786436
  11.2 31.0 %collective-permute-start.2 = (bf16[128,2048]{1,0:T(8,128)(2,1)}, bf16[128,2048]{1,0:T(8,128)(2,1)}, u32[]{:S(2)}, u32[]{:S(2)}) collective-permute-start(bf16[128,2048]{1,0:T(8,128)(2,1)} %slice.277), channel_id=1, source_target_pairs={{0,1},{1,0},{2,3},{3,2},{4,5},{5,4},{6,7},{7,6},{8,9},{9,8},{10,11... | collective-permute-start | bytes 1572872 | tf_op jit(solution)/shard_map/ppermute | solution.py:302
  14.1 24.2 %collective-permute-start.3 = (bf16[128,2048]{1,0:T(8,128)(2,1)}, bf16[128,2048]{1,0:T(8,128)(2,1)S(1)}, u32[]{:S(2)}, u32[]{:S(2)}) collective-permute-start(bf16[128,2048]{1,0:T(8,128)(2,1)} %slice.344), channel_id=1, source_target_pairs={{0,1},{1,0},{2,3},{3,2},{4,5},{5,4},{6,7},{7,6},{8,9},{9,8},{10,11... | collective-permute-start | bytes 1572872 | tf_op jit(solution)/shard_map/ppermute | solution.py:302
  15.0 34.7 %collective-permute-start.1 = (bf16[128,2048]{1,0:T(8,128)(2,1)}, bf16[128,2048]{1,0:T(8,128)(2,1)}, u32[]{:S(2)}, u32[]{:S(2)}) collective-permute-start(bf16[128,2048]{1,0:T(8,128)(2,1)} %slice.278), channel_id=1, source_target_pairs={{0,1},{1,0},{2,3},{3,2},{4,5},{5,4},{6,7},{7,6},{8,9},{9,8},{10,11... | collective-permute-start | bytes 1572872 | tf_op jit(solution)/shard_map/ppermute | solution.py:302
  17.8 42.2 %collective-permute-start = (bf16[128,2048]{1,0:T(8,128)(2,1)}, bf16[128,2048]{1,0:T(8,128)(2,1)}, u32[]{:S(2)}, u32[]{:S(2)}) collective-permute-start(bf16[128,2048]{1,0:T(8,128)(2,1)} %slice.279), channel_id=1, source_target_pairs={{0,1},{1,0},{2,3},{3,2},{4,5},{5,4},{6,7},{7,6},{8,9},{9,8},{10,11... | collective-permute-start | bytes 1572872 | tf_op jit(solution)/shard_map/ppermute | solution.py:302
  23.7 1.3 copy-start.5
  38.3 0.8 copy-start.15
  39.1 1.0 copy-start.16
  60.1 2.4 copy-start.3
  60.1 3.0 %copy-start.6 = (bf16[8192,128]{1,0:T(8,128)(2,1)S(1)}, bf16[8192,128]{1,0:T(8,128)(2,1)}, u32[]{:S(2)}) copy-start(bf16[8192,128]{1,0:T(8,128)(2,1)} %copy-done.5) | copy-start | bytes 6291460
  62.4 34.8 %copy-start = (bf16[8192,128]{1,0:T(8,128)(2,1)}, bf16[8192,128]{1,0:T(8,128)(2,1)S(1)}, u32[]{:S(2)}) copy-start(bf16[8192,128]{1,0:T(8,128)(2,1)S(1)} %get-tuple-element.84) | copy-start | bytes 6291460
  73.8 36.4 %copy-start.13 = (f32[8,512,128]{2,1,0:T(8,128)}, f32[8,512,128]{2,1,0:T(8,128)S(1)}, u32[]{:S(2)}) copy-start(f32[8,512,128]{2,1,0:T(8,128)S(1)} %get-tuple-element.87) | copy-start | bytes 6291460
  74.0 2.7 collective-permute-start.4
  76.7 33.5 %copy-start.19 = (f16[8,512,128]{2,1,0:T(8,128)(2,1)}, f16[8,512,128]{2,1,0:T(8,128)(2,1)S(1)}, u32[]{:S(2)}) copy-start(f16[8,512,128]{2,1,0:T(8,128)(2,1)S(1)} %collective-permute-done.4) | copy-start | bytes 3145732
  76.8 14.0 %collective-permute-start.5 = (f16[4,512,128]{2,1,0:T(8,128)(2,1)S(1)}, f16[4,512,128]{2,1,0:T(8,128)(2,1)S(1)}, u32[]{:S(2)}, u32[]{:S(2)}) collective-permute-start(f16[4,512,128]{2,1,0:T(8,128)(2,1)S(1)} %add_convert_fusion.3), channel_id=1, source_target_pairs={{0,4},{2,6},{4,0},{6,2},{8,12},{10,14},{12,8},{14,10},{16,20},{18,... | collective-permute-start | bytes 1572872 | tf_op jit(solution)/shard_map/ppermute | solution.py:287
  89.3 19.9 %copy-start.12 = (f32[8,512,128]{2,1,0:T(8,128)}, f32[8,512,128]{2,1,0:T(8,128)S(1)}, u32[]{:S(2)}) copy-start(f32[8,512,128]{2,1,0:T(8,128)S(1)} %get-tuple-element.93) | copy-start | bytes 6291460
  90.9 19.3 %copy-start.26 = (f16[4,512,128]{2,1,0:T(8,128)(2,1)}, f16[4,512,128]{2,1,0:T(8,128)(2,1)S(1)}, u32[]{:S(2)}) copy-start(f16[4,512,128]{2,1,0:T(8,128)(2,1)S(1)} %collective-permute-done.5) | copy-start | bytes 1572868
  91.0 2.7 collective-permute-start.6
  93.7 15.5 %copy-start.18 = (f16[8,512,128]{2,1,0:T(8,128)(2,1)}, f16[8,512,128]{2,1,0:T(8,128)(2,1)S(1)}, u32[]{:S(2)}) copy-start(f16[8,512,128]{2,1,0:T(8,128)(2,1)S(1)} %collective-permute-done.6) | copy-start | bytes 3145732
  93.9 15.3 %collective-permute-start.8 = (f16[4,512,128]{2,1,0:T(8,128)(2,1)S(1)}, f16[4,512,128]{2,1,0:T(8,128)(2,1)S(1)}, u32[]{:S(2)}, u32[]{:S(2)}) collective-permute-start(f16[4,512,128]{2,1,0:T(8,128)(2,1)S(1)} %add_convert_fusion.2), channel_id=1, source_target_pairs={{0,4},{2,6},{4,0},{6,2},{8,12},{10,14},{12,8},{14,10},{16,20},{18,... | collective-permute-start | bytes 1572872 | tf_op jit(solution)/shard_map/ppermute | solution.py:287
  95.6 13.5 %collective-permute-start.7 = (f16[2,512,128]{2,1,0:T(8,128)(2,1)S(1)}, f16[2,512,128]{2,1,0:T(8,128)(2,1)S(1)}, u32[]{:S(2)}, u32[]{:S(2)}) collective-permute-start(f16[2,512,128]{2,1,0:T(8,128)(2,1)S(1)} %add_convert_fusion.7), channel_id=1, source_target_pairs={{0,8},{2,10},{4,12},{6,14},{8,0},{10,2},{12,4},{14,6},{16,24},{18,... | collective-permute-start | bytes 786440 | tf_op jit(solution)/shard_map/ppermute | solution.py:287
  107.9 2.3 copy-start.10
  109.2 1.8 copy-start.28
  109.2 1.8 copy-start.24
  110.9 3.0 %collective-permute-start.9 = (f16[8,512,128]{2,1,0:T(8,128)(2,1)}, f16[8,512,128]{2,1,0:T(8,128)(2,1)}, u32[]{:S(2)}, u32[]{:S(2)}) collective-permute-start(f16[8,512,128]{2,1,0:T(8,128)(2,1)} %convert_element_type.228), channel_id=1, source_target_pairs={{0,2},{2,0},{4,6},{6,4},{8,10},{10,8},{12,14},{14,12},{16,18},{18,... | collective-permute-start | bytes 3145736 | tf_op jit(solution)/shard_map/ppermute | solution.py:287
  110.9 5.3 %copy-start.17 = (f32[512,512]{1,0:T(8,128)S(1)}, f32[512,512]{1,0:T(8,128)}, u32[]{:S(2)}) copy-start(f32[512,512]{1,0:T(8,128)} %param.8) | copy-start | bytes 3145732
  113.9 8.8 %copy-start.4 = (bf16[1,128,8192]{2,1,0:T(8,128)(2,1)S(1)}, bf16[1,128,8192]{2,1,0:T(8,128)(2,1)}, u32[]{:S(2)}) copy-start(bf16[1,128,8192]{2,1,0:T(8,128)(2,1)} %param.11) | copy-start | bytes 6291460
  115.6 7.2 %copy-start.1 = (bf16[8192,128]{1,0:T(8,128)(2,1)S(1)}, bf16[8192,128]{1,0:T(8,128)(2,1)}, u32[]{:S(2)}) copy-start(bf16[8192,128]{1,0:T(8,128)(2,1)} %copy-done) | copy-start | bytes 6291460
  115.6 19.9 %collective-permute-start.12 = (f16[4,512,128]{2,1,0:T(8,128)(2,1)S(1)}, f16[4,512,128]{2,1,0:T(8,128)(2,1)S(1)}, u32[]{:S(2)}, u32[]{:S(2)}) collective-permute-start(f16[4,512,128]{2,1,0:T(8,128)(2,1)S(1)} %add_convert_fusion.1), channel_id=1, source_target_pairs={{0,4},{2,6},{4,0},{6,2},{8,12},{10,14},{12,8},{14,10},{16,20},{18,... | collective-permute-start | bytes 1572872 | tf_op jit(solution)/shard_map/ppermute | solution.py:287
  117.0 18.5 %collective-permute-start.11 = (f16[2,512,128]{2,1,0:T(8,128)(2,1)}, f16[2,512,128]{2,1,0:T(8,128)(2,1)S(1)}, u32[]{:S(2)}, u32[]{:S(2)}) collective-permute-start(f16[2,512,128]{2,1,0:T(8,128)(2,1)} %add_convert_fusion.6), channel_id=1, source_target_pairs={{0,8},{2,10},{4,12},{6,14},{8,0},{10,2},{12,4},{14,6},{16,24},{18,... | collective-permute-start | bytes 786440 | tf_op jit(solution)/shard_map/ppermute | solution.py:287
  120.2 15.2 %collective-permute-start.10 = (f16[1,512,128]{2,1,0:T(8,128)(2,1)}, f16[1,512,128]{2,1,0:T(8,128)(2,1)S(1)}, u32[]{:S(2)}, u32[]{:S(2)}) collective-permute-start(f16[1,512,128]{2,1,0:T(8,128)(2,1)} %add_convert_fusion.11), channel_id=1, source_target_pairs={{0,16},{2,18},{4,20},{6,22},{8,24},{10,26},{12,28},{14,30},{16,0},... | collective-permute-start | bytes 393224 | tf_op jit(solution)/shard_map/ppermute | solution.py:287
  122.8 1.6 copy-start.7
  135.2 9.3 %copy-start.14 = (f32[8,512,128]{2,1,0:T(8,128)}, f32[8,512,128]{2,1,0:T(8,128)S(1)}, u32[]{:S(2)}) copy-start(f32[8,512,128]{2,1,0:T(8,128)S(1)} %get-tuple-element.117) | copy-start | bytes 6291460
  135.3 2.3 copy-start.11
  135.3 3.6 %copy-start.25 = (f16[4,512,128]{2,1,0:T(8,128)(2,1)S(1)}, f16[4,512,128]{2,1,0:T(8,128)(2,1)}, u32[]{:S(2)}) copy-start(f16[4,512,128]{2,1,0:T(8,128)(2,1)} %copy-done.24) | copy-start | bytes 1572868
  135.3 4.7 %copy-start.29 = (f16[2,512,128]{2,1,0:T(8,128)(2,1)S(1)}, f16[2,512,128]{2,1,0:T(8,128)(2,1)}, u32[]{:S(2)}) copy-start(f16[2,512,128]{2,1,0:T(8,128)(2,1)} %copy-done.28) | copy-start | bytes 786436
  137.6 7.9 %copy-start.23 = (f16[4,512,128]{2,1,0:T(8,128)(2,1)}, f16[4,512,128]{2,1,0:T(8,128)(2,1)S(1)}, u32[]{:S(2)}) copy-start(f16[4,512,128]{2,1,0:T(8,128)(2,1)S(1)} %collective-permute-done.12) | copy-start | bytes 1572868
  141.9 2.7 collective-permute-start.15
  141.9 11.5 %collective-permute-start.14 = (f16[2,512,128]{2,1,0:T(8,128)(2,1)S(1)}, f16[2,512,128]{2,1,0:T(8,128)(2,1)S(1)}, u32[]{:S(2)}, u32[]{:S(2)}) collective-permute-start(f16[2,512,128]{2,1,0:T(8,128)(2,1)S(1)} %add_convert_fusion.5), channel_id=1, source_target_pairs={{0,8},{2,10},{4,12},{6,14},{8,0},{10,2},{12,4},{14,6},{16,24},{18,... | collective-permute-start | bytes 786440 | tf_op jit(solution)/shard_map/ppermute | solution.py:287
  142.5 9.0 %collective-permute-start.13 = (f16[1,512,128]{2,1,0:T(8,128)(2,1)S(1)}, f16[1,512,128]{2,1,0:T(8,128)(2,1)S(1)}, u32[]{:S(2)}, u32[]{:S(2)}) collective-permute-start(f16[1,512,128]{2,1,0:T(8,128)(2,1)S(1)} %add_convert_fusion.10), channel_id=1, source_target_pairs={{0,16},{2,18},{4,20},{6,22},{8,24},{10,26},{12,28},{14,30},{16,0},... | collective-permute-start | bytes 393224 | tf_op jit(solution)/shard_map/ppermute | solution.py:287
  153.4 2.0 copy-start.30
  156.2 106.8 %all-gather.3.cloned.1.call-start = ((), (), s32[]{:S(2)}) async-start(), calls=%async_computation | async-start | bytes 4456448 | tf_op jit(solution)/shard_map/all_gather | solution.py:389
  156.2 29.4 %copy-start.21 = (f32[512,128]{1,0:T(8,128)S(1)}, f32[512,128]{1,0:T(8,128)}, u32[]{:S(2)}) copy-start(f32[512,128]{1,0:T(8,128)} %get-tuple-element.121) | copy-start | bytes 786436
  156.2 29.4 %copy-start.27 = (bf16[512,128]{1,0:T(8,128)(2,1)S(1)}, bf16[512,128]{1,0:T(8,128)(2,1)}, u32[]{:S(2)}) copy-start(bf16[512,128]{1,0:T(8,128)(2,1)} %get-tuple-element.65) | copy-start | bytes 393220
  156.3 29.4 %copy-start.31 = (f16[2,512,128]{2,1,0:T(8,128)(2,1)S(1)}, f16[2,512,128]{2,1,0:T(8,128)(2,1)}, u32[]{:S(2)}) copy-start(f16[2,512,128]{2,1,0:T(8,128)(2,1)} %copy-done.30) | copy-start | bytes 786436
  156.3 16.6 %collective-permute-start.17 = (f16[4,512,128]{2,1,0:T(8,128)(2,1)}, f16[4,512,128]{2,1,0:T(8,128)(2,1)S(1)}, u32[]{:S(2)}, u32[]{:S(2)}) collective-permute-start(f16[4,512,128]{2,1,0:T(8,128)(2,1)} %add_convert_fusion), channel_id=1, source_target_pairs={{0,4},{2,6},{4,0},{6,2},{8,12},{10,14},{12,8},{14,10},{16,20},{18,... | collective-permute-start | bytes 1572872 | tf_op jit(solution)/shard_map/ppermute | solution.py:287
  158.0 8.4 %collective-permute-start.16 = (f16[1,512,128]{2,1,0:T(8,128)(2,1)S(1)}, f16[1,512,128]{2,1,0:T(8,128)(2,1)S(1)}, u32[]{:S(2)}, u32[]{:S(2)}) collective-permute-start(f16[1,512,128]{2,1,0:T(8,128)(2,1)S(1)} %add_convert_fusion.9), channel_id=1, source_target_pairs={{0,16},{2,18},{4,20},{6,22},{8,24},{10,26},{12,28},{14,30},{16,0},... | collective-permute-start | bytes 393224 | tf_op jit(solution)/shard_map/ppermute | solution.py:287
  174.1 9.5 %collective-permute-start.18 = (f16[2,512,128]{2,1,0:T(8,128)(2,1)S(1)}, f16[2,512,128]{2,1,0:T(8,128)(2,1)S(1)}, u32[]{:S(2)}, u32[]{:S(2)}) collective-permute-start(f16[2,512,128]{2,1,0:T(8,128)(2,1)S(1)} %add_convert_fusion.4), channel_id=1, source_target_pairs={{0,8},{2,10},{4,12},{6,14},{8,0},{10,2},{12,4},{14,6},{16,24},{18,... | collective-permute-start | bytes 786440 | tf_op jit(solution)/shard_map/ppermute | solution.py:287
  184.7 16.1 %collective-permute-start.19 = (f16[1,512,128]{2,1,0:T(8,128)(2,1)S(1)}, f16[1,512,128]{2,1,0:T(8,128)(2,1)S(1)}, u32[]{:S(2)}, u32[]{:S(2)}) collective-permute-start(f16[1,512,128]{2,1,0:T(8,128)(2,1)S(1)} %add_convert_fusion.8), channel_id=1, source_target_pairs={{0,16},{2,18},{4,20},{6,22},{8,24},{10,26},{12,28},{14,30},{16,0},... | collective-permute-start | bytes 393224 | tf_op jit(solution)/shard_map/ppermute | solution.py:287
  187.5 15.2 %copy-start.22 = (f32[512,128]{1,0:T(8,128)S(1)}, f32[512,128]{1,0:T(8,128)}, u32[]{:S(2)}) copy-start(f32[512,128]{1,0:T(8,128)} %get-tuple-element.136) | copy-start | bytes 786436
  211.4 2.2 copy-start.8
  263.0 2.2 copy-start.9
Sparse Core Ops, SparseCore 0:
  156.3 55.0 all-gather.4
  213.5 49.3 all-gather.2

commit v7 on v5

--- a/solution.py
+++ b/solution.py
@@ -108,8 +108,35 @@
     return place
 
 
+def fetch_kernel(chunk, first_ref, second_ref, first_out, second_out, semaphore):
+    width = first_out.shape[-1]
+    columns = pl.ds(chunk * width, width)
+    copies = [
+        pltpu.make_async_copy(source.at[..., columns], target, semaphore.at[index])
+        for index, (source, target) in enumerate(((first_ref, first_out), (second_ref, second_out)))
+    ]
+    for copy in copies:
+        copy.start()
+    for copy in copies:
+        copy.wait()
+
+
+def fetch(chunk, width, first, second):
+    out = jax.ShapeDtypeStruct(first.shape[:-1] + (width,), F32)
+    return pl.pallas_call(
+        functools.partial(fetch_kernel, chunk),
+        in_specs=[pl.BlockSpec(memory_space=pl.ANY)] * 2,
+        out_specs=[pl.BlockSpec(memory_space=pltpu.VMEM)] * 2,
+        out_shape=[out, out],
+        scratch_shapes=[pltpu.SemaphoreType.DMA((2,))],
+        compiler_params=pltpu.CompilerParams(vmem_limit_bytes=MIB),
+        name="fetch",
+    )(pinned(first), pinned(second))
+
+
 def inner_kernel(
     tokens,
+    fetched,
     mine_ref,
     low_ref,
     high_ref,
@@ -134,6 +161,8 @@
 ):
     step = pl.program_id(0)
     slab = pl.program_id(1)
+    if fetched:
+        first_ref, second_ref = first_ref.at[slab], second_ref.at[slab]
     pairs, cores, rows, _ = start_ref.shape
     mine = mine_ref[0]
     core = lax.rem(mine, cores)
@@ -146,7 +175,7 @@
     def descend(first, second, weights):
         root = second * lax.rsqrt(second)
         below = (100.0 * math.sqrt(0.05)) * root + 1e-06
-        return 0.99 * weights - first * lax.rsqrt(below * below)
+        return 0.99 * weights - first * pl.reciprocal(below, approx=True)
 
     def differentiate(pair, which, slot):
         turned = jnp.concatenate(
@@ -213,7 +242,7 @@
                 out_ref[place, piece] = change * WIRE_SCALE
 
 
-def inner(chunk, width, mine, banks, turned, start, first, second, products, target, count, tokens):
+def inner(chunk, width, fetched, mine, banks, turned, start, first, second, products, target, count, tokens):
     slabs, pairs, cores, rows, _ = start.shape
     half, depth = banks[0].shape
 
@@ -224,17 +253,18 @@
     tile = (None, pairs, cores, rows, width)
     state = pl.BlockSpec(tile, lambda s, z, c: (held(s, z), 0, 0, 0, chunk))
     product = pl.BlockSpec((half, width), lambda s, z, c: (0, chunk))
+    states = (first, second) if fetched else (pinned(first), pinned(second))
     elements = depth * width
     return pl.pallas_call(
-        functools.partial(inner_kernel, float(tokens)),
+        functools.partial(inner_kernel, float(tokens), fetched),
         grid_spec=pltpu.PrefetchScalarGridSpec(
             num_scalar_prefetch=1,
             grid=(2, slabs),
             in_specs=[whole] * 4
             + [
                 pl.BlockSpec(tile, lambda s, z, c: (z, 0, 0, 0, chunk)),
-                state,
-                state,
+                whole if fetched else state,
+                whole if fetched else state,
                 product,
                 product,
                 pl.BlockSpec((2 * half, width), lambda s, z, c: (0, chunk)),
@@ -262,7 +292,7 @@
             transcendentals=4 * elements,
         ),
         name="inner",
-    )(mine, *banks, *turned, pinned(start), pinned(first), pinned(second), *products, target, count)
+    )(mine, *banks, *turned, pinned(start), *states, *products, target, count)
 
 
 def assemble_kernel(chunk, offsets, place_ref, *refs):
@@ -328,6 +358,12 @@
 
     spans = [[0, 1 << bit] for bit in range(1, bits)]
 
+    cut = (SLABS, reps // (2 * SLABS), 2, rows, columns)
+    start = global_weights.reshape(cut)
+    first = first_moment.reshape(cut)
+    second = second_moment.reshape(cut)
+    early = fetch(0, width, first, second)
+
     own_bank = hidden_bank[0]
     target = target_bank[0]
     count = jnp.sum(
@@ -341,6 +377,7 @@
             part, source = tied(source[:, d * block : (d + 1) * block], source)
             parts.append(lax.ppermute(part, "fsdp", [(0, 1), (1, 0)]))
         own_turned, own_product = forward(own_bank, global_weights)
+        parts[0], early = tied(parts[0], early)
         joined = ()
         for d, part in enumerate(parts):
             joined = arrive(d, part, global_weights, joined)
@@ -356,11 +393,7 @@
         turned, products = zip(*(forward(bank, global_weights) for bank in banks))
     count = count[:, :, None]
 
-    cut = (SLABS, reps // (2 * SLABS), 2, rows, columns)
     turned = [array.reshape(cut[:4] + (half,)) for array in turned]
-    start = global_weights.reshape(cut)
-    first = first_moment.reshape(cut)
-    second = second_moment.reshape(cut)
     place = mine.reshape(1).astype(jnp.int32)
     my_start = lax.dynamic_slice_in_dim(global_weights, mine * rows, rows, 0)
     shares = [
@@ -377,67 +410,62 @@
     def sent(outgoing, span):
         return [swapped(array, offset) for array, offset in zip(outgoing, span[1:])]
 
-    new_momentum = []
     result = ()
 
-    def chain(chunk, send, keep):
-        send = yield send
-        terms = [keep, swapped(send, 1)]
+    def chain(chunk, keep, arrived):
+        terms = [keep, arrived]
         for span in spans:
             outgoing, terms = parted(terms, span)
             outgoing = yield outgoing
-            terms = terms + held_back(sent(outgoing, span))
+            arrived = yield sent(outgoing, span)
+            terms = terms + arrived
         total = sum(term.astype(F32) for term in terms)[0]
         average = total * (1.0 / (WIRE_SCALE * reps))
         moved = 0.9 * shares[chunk][0] + average
-        stack = (shares[chunk][1].astype(F32) - 0.7 * (average + 0.9 * moved)).astype(BF16)[None]
+        fresh = (shares[chunk][1].astype(F32) - 0.7 * (average + 0.9 * moved)).astype(BF16)
+        stack = yield fresh[None]
         offsets = [0]
         for span in spans[:0:-1]:
-            stack = yield stack
-            arrived = held_back(sent([stack] * (len(span) - 1), span))
-            stack = jnp.concatenate([stack] + arrived)
+            arrived = yield sent([stack], span)
             offsets = [offset ^ far for far in span for offset in offsets]
-        stack = yield stack
-        across = swapped(stack, 2)
+            stack = yield jnp.concatenate([stack] + arrived)
+        across, = yield sent([stack], spans[0])
         finished[chunk] = (moved, stack, across, offsets)
+        yield ()
 
     finished = {}
     running = {}
     formed = {}
-    gate = []
-
-    def held_back(arrived):
-        return tied(arrived, gate)[0] if gate else arrived
 
     def move_on(which, behind=()):
-        gate[:] = [formed[other] for other in behind]
-        try:
-            formed[which] = running[which].send(formed[which])
-        except StopIteration:
-            del formed[which]
+        which = [chunk for chunk in which if chunk not in finished]
+        arrived = {chunk: running[chunk].send(formed[chunk]) for chunk in which}
+        arrived, _ = tied(arrived, [formed[chunk] for chunk in behind])
+        for chunk in which:
+            formed[chunk] = running[chunk].send(arrived[chunk])
 
     token = place
     for chunk in range(chunks):
+        states = early if chunk == 0 else (first, second)
         send, keep = inner(
-            chunk, width, token, banks, turned, start, first, second, products, target, count, tokens
+            chunk, width, chunk == 0, token, banks, turned, start, *states, products, target, count, tokens
         )
         send = send.astype(WIRE)
-        for earlier in list(formed):
-            move_on(earlier)
-            formed[earlier], send = tied(formed[earlier], send)
-        running[chunk] = chain(chunk, send, keep)
-        formed[chunk] = running[chunk].send(next(running[chunk]))
+        if chunk:
+            move_on(range(chunk))
+            formed, send = tied(formed, send)
+        running[chunk] = chain(chunk, keep, swapped(send, 1))
+        formed[chunk] = next(running[chunk])
         if chunk + 1 < chunks:
             formed, token = tied(formed, token)
-    if chunks == 4:
-        move_on(0, behind=[3])
-        move_on(3, behind=[0])
-        for which in (1, 2, 0):
-            move_on(which, behind=[3])
-    for which in range(chunks):
-        while which in formed:
-            move_on(which)
-
+
+    head = chunks - 1
+    move_on(range(head), behind=[head])
+    for chunk in range(chunks):
+        while chunk not in finished:
+            move_on([chunk])
+
+    new_momentum = []
     for chunk in range(chunks):
         moved, stack, across, offsets = finished[chunk]
         new_momentum.append(moved)

time: 229 us -> 221 us (0.965)
  waiting for transfers between devices: 101 us -> 86.6 us
  local copies, waits for them, and re-layouts: 14.7 us -> 21.1 us
    ppermute x4, waiting for transfers between devices: 26.8 us -> 17.1 us  [per_device(): parts.append(lax.ppermute(part, 'fsdp', [(0, 1), (1, 0)]))]
    unnamed x48 -> x56, local copies, waits for them, and re-layouts: 6.97 us -> 14.7 us
    ppermute x36, waiting for transfers between devices: 74.4 us -> 69.5 us  [swapped(): return lax.ppermute(array, 'rep', pairs)]
    pallas_call x4 -> x5, Pallas kernels: 42.9 us -> 44.2 us  [the longest x4 40.7 us: inner(): pl.pallas_call(functools.partial(inner_kernel, float(tokens), fetched), g...]
  transfers between devices with their start and end apart: 40 -> 40, of which waited for: 20 -> 20; matrix products, arithmetic and copies ran while one was open for 6% -> 6% of each run, Pallas kernels for 21% -> 23%
where the time goes in v7:
time: 221 us; the launch traced here: 220 us
  waiting for transfers between devices  86.6 us (39%)
  Pallas kernels  63.8 us (29%)
  starting transfers between devices  34.7 us (16%)
  local copies, waits for them, and re-layouts  21.1 us (10%)
  other arithmetic  12.9 us (6%)
    ppermute x36, waiting for transfers between devices, swapped(): return lax.ppermute(array, 'rep', pairs)  69.5 us
    pallas_call x4, Pallas kernels, inner(): pl.pallas_call(functools.partial(inner_kernel, float(tokens), fetched), g...  40.7 us
    ppermute x36, starting transfers between devices, swapped(): return lax.ppermute(array, 'rep', pairs)  29.6 us
    ppermute x4, waiting for transfers between devices, per_device(): parts.append(lax.ppermute(part, 'fsdp', [(0, 1), (1, 0)]))  17.1 us
    unnamed x56, local copies, waits for them, and re-layouts  14.7 us
    pallas_call x4, Pallas kernels, arrive(): pl.pallas_call(functools.partial(arrive_kernel, piece), grid=(1,), in_spe...  8.82 us
    convert_element_type x12, other arithmetic, parted(): sum((term.astype(F32) for term in part)).astype(WIRE)  5.77 us
    pallas_call x4, Pallas kernels, assemble(): pl.pallas_call(functools.partial(assemble_kernel, chunk, offsets), in_spe...  5.75 us
  transfers between devices with their start and end apart: 40, of which 20 were waited for; matrix products, arithmetic and copies ran while one was open for 6% of the time, Pallas kernels for 23%

profile of v7, /device:TPU:0, one launch (start us, length us, event | category | flops | bytes accessed | tf_op | source)
XLA Modules:
  0.0 220.4 jit_solution(14733702779744133800)
XLA Ops:
  0.7 1.2 slice.344
  1.9 3.0 %collective-permute-start.3 = (bf16[128,2048]{1,0:T(8,128)(2,1)S(1)}, bf16[128,2048]{1,0:T(8,128)(2,1)S(1)}, u32[]{:S(2)}, u32[]{:S(2)}) collective-permute-start(bf16[128,2048]{1,0:T(8,128)(2,1)S(1)} %slice.344), channel_id=1, source_target_pairs={{0,1},{1,0},{2,3},{3,2},{4,5},{5,4},{6,7},{7,6},{8,9},{9,8},{10,11... | collective-permute-start | bytes 1572872 | tf_op jit(solution)/shard_map/ppermute | solution.py:378
  4.9 1.9 slice.277
  7.7 2.0 collective-permute-start.1
  10.9 5.0 %forward.1 = (bf16[8192,128]{1,0:T(8,128)(2,1)S(1)}, f32[128,512]{1,0:T(8,128)S(1)}) custom-call(bf16[128,8192]{1,0:T(8,128)(2,1)S(1)} %bitcast.89, bf16[8192,512]{1,0:T(8,128)(2,1)} %weights_ref.9), custom_call_target="tpu_custom_call" | custom-call | flops 1073741824 | bytes 12582912 | tf_op jit(solution)/shard_map/forward/pallas_call | solution.py:34
  15.9 1.3 copy-done.5
  17.5 3.5 %fetch.1 = (f32[4,2,2,512,128]{4,3,2,1,0:T(8,128)S(1)}, f32[4,2,2,512,128]{4,3,2,1,0:T(8,128)S(1)}) custom-call(f32[4,2,2,512,512]{4,3,2,1,0:T(8,128)} %bitcast.102, f32[4,2,2,512,512]{4,3,2,1,0:T(8,128)} %bitcast.106), custom_call_target="tpu_custom_call" | custom-call | tf_op jit(solution)/shard_map/fetch/pallas_call | solution.py:126
  21.1 2.0 copy-done.8
  23.1 2.0 copy-done.10
  27.1 2.0 arrive.4
  29.2 2.2 %arrive.5 = (bf16[128,8192]{1,0:T(8,128)(2,1)S(1)}, bf16[8192,128]{1,0:T(8,128)(2,1)S(1)}, f32[128,512]{1,0:T(8,128)S(1)}) custom-call(bf16[128,2048]{1,0:T(8,128)(2,1)} %collective-permute-done.2.part_ref, bf16[8192,512]{1,0:T(8,128)(2,1)} %weights_ref.9, ...), custom_call_target="tpu_custom_call", output_to_operand_aliasing={{0}: (2, {}), {1}: (3, {}), {2}: (4, {})} | custom-call | flops 268435456 | bytes 3670016 | tf_op jit(solution)/shard_map/arrive/pallas_call | solution.py:76
  31.4 8.9 %collective-permute-done.1.part_ref = bf16[128,2048]{1,0:T(8,128)(2,1)} collective-permute-done((bf16[128,2048]{1,0:T(8,128)(2,1)}, bf16[128,2048]{1,0:T(8,128)(2,1)}, u32[]{:S(2)}, u32[]{:S(2)}) %collective-permute-start.1) | collective-permute-done | bytes 524320 | tf_op jit(solution)/shard_map/ppermute | solution.py:378
  40.3 2.2 %arrive.6 = (bf16[128,8192]{1,0:T(8,128)(2,1)S(1)}, bf16[8192,128]{1,0:T(8,128)(2,1)S(1)}, f32[128,512]{1,0:T(8,128)S(1)}) custom-call(bf16[128,2048]{1,0:T(8,128)(2,1)} %collective-permute-done.1.part_ref, bf16[8192,512]{1,0:T(8,128)(2,1)} %weights_ref.9, ...), custom_call_target="tpu_custom_call", output_to_operand_aliasing={{0}: (2, {}), {1}: (3, {}), {2}: (4, {})} | custom-call | flops 268435456 | bytes 3670016 | tf_op jit(solution)/shard_map/arrive/pallas_call | solution.py:76
  42.5 8.2 %collective-permute-done.part_ref = bf16[128,2048]{1,0:T(8,128)(2,1)} collective-permute-done((bf16[128,2048]{1,0:T(8,128)(2,1)}, bf16[128,2048]{1,0:T(8,128)(2,1)}, u32[]{:S(2)}, u32[]{:S(2)}) %collective-permute-start) | collective-permute-done | bytes 524320 | tf_op jit(solution)/shard_map/ppermute | solution.py:378
  50.7 2.4 %arrive.7 = (bf16[128,8192]{1,0:T(8,128)(2,1)S(1)}, bf16[8192,128]{1,0:T(8,128)(2,1)S(1)}, f32[128,512]{1,0:T(8,128)S(1)}) custom-call(bf16[128,2048]{1,0:T(8,128)(2,1)} %collective-permute-done.part_ref, bf16[8192,512]{1,0:T(8,128)(2,1)} %weights_ref.9, ...), custom_call_target="tpu_custom_call", output_to_operand_aliasing={{0}: (2, {}), {1}: (3, {}), {2}: (4, {})} | custom-call | flops 268435456 | bytes 3670016 | tf_op jit(solution)/shard_map/arrive/pallas_call | solution.py:76
  53.7 2.0 copy-done.9
  55.7 1.2 copy-done.11
  56.9 8.9 %inner.4 = (f32[8,512,128]{2,1,0:T(8,128)S(1)}, f32[8,512,128]{2,1,0:T(8,128)S(1)}) custom-call(s32[1]{0:T(128)} %bitcast.mine_ref.place_ref, bf16[128,8192]{1,0:T(8,128)(2,1)S(1)} %bitcast.90, bf16[128,8192]{1,0:T(8,128)(2,1)S(1)} %get-tuple-element.96.high_ref, bf16[4,2,2,512,128]{4,3,2,1,0:T(8,128)(2,1)S(1)} %bitcast.94, ...), custom_call_target="tpu_custom_call" | custom-call | flops 1610612736 | bytes 20971520 | tf_op jit(solution)/shard_map/inner/pallas_call | solution.py:258
  66.0 2.6 %collective-permute-done.4 = f16[8,512,128]{2,1,0:T(8,128)(2,1)S(1)} collective-permute-done((f16[8,512,128]{2,1,0:T(8,128)(2,1)S(1)}, f16[8,512,128]{2,1,0:T(8,128)(2,1)S(1)}, u32[]{:S(2)}, u32[]{:S(2)}) %collective-permute-start.4) | collective-permute-done | bytes 1048608 | tf_op jit(solution)/shard_map/ppermute | solution.py:357
  68.8 1.8 collective-permute-start.5
  70.6 10.5 %inner.5 = (f32[8,512,128]{2,1,0:T(8,128)S(1)}, f32[8,512,128]{2,1,0:T(8,128)S(1)}) custom-call(s32[1]{0:T(128)} %bitcast.mine_ref.place_ref, bf16[128,8192]{1,0:T(8,128)(2,1)S(1)} %bitcast.91, bf16[128,8192]{1,0:T(8,128)(2,1)S(1)} %get-tuple-element.96.high_ref, bf16[4,2,2,512,128]{4,3,2,1,0:T(8,128)(2,1)S(1)} %bitcast.95, ...), custom_call_target="tpu_custom_call" | custom-call | flops 1610612736 | bytes 20971520 | tf_op jit(solution)/shard_map/inner/pallas_call | solution.py:258
  81.3 1.6 collective-permute-done.5
  83.1 2.6 %collective-permute-done.6 = f16[8,512,128]{2,1,0:T(8,128)(2,1)S(1)} collective-permute-done((f16[8,512,128]{2,1,0:T(8,128)(2,1)S(1)}, f16[8,512,128]{2,1,0:T(8,128)(2,1)S(1)}, u32[]{:S(2)}, u32[]{:S(2)}) %collective-permute-start.6) | collective-permute-done | bytes 1048608 | tf_op jit(solution)/shard_map/ppermute | solution.py:357
  85.9 1.8 collective-permute-start.8
  87.7 1.6 collective-permute-start.7
  89.2 10.5 %inner.6 = (f32[8,512,128]{2,1,0:T(8,128)S(1)}, f32[8,512,128]{2,1,0:T(8,128)S(1)}) custom-call(s32[1]{0:T(128)} %bitcast.mine_ref.place_ref, bf16[128,8192]{1,0:T(8,128)(2,1)S(1)} %bitcast.92, bf16[128,8192]{1,0:T(8,128)(2,1)S(1)} %get-tuple-element.96.high_ref, bf16[4,2,2,512,128]{4,3,2,1,0:T(8,128)(2,1)S(1)} %bitcast.96, ...), custom_call_target="tpu_custom_call" | custom-call | flops 1610612736 | bytes 20971520 | tf_op jit(solution)/shard_map/inner/pallas_call | solution.py:258
  99.8 1.3 convert_element_type.228
  102.0 3.0 %collective-permute-done.9 = f16[8,512,128]{2,1,0:T(8,128)(2,1)} collective-permute-done((f16[8,512,128]{2,1,0:T(8,128)(2,1)}, f16[8,512,128]{2,1,0:T(8,128)(2,1)}, u32[]{:S(2)}, u32[]{:S(2)}) %collective-permute-start.9) | collective-permute-done | bytes 1048608 | tf_op jit(solution)/shard_map/ppermute | solution.py:357
  105.0 1.6 add_convert_fusion.1
  107.3 1.6 collective-permute-start.11
  108.9 1.1 fusion.16
  110.1 2.7 %collective-permute-start.10 = (f16[1,512,128]{2,1,0:T(8,128)(2,1)S(1)}, f16[1,512,128]{2,1,0:T(8,128)(2,1)S(1)}, u32[]{:S(2)}, u32[]{:S(2)}) collective-permute-start(f16[1,512,128]{2,1,0:T(8,128)(2,1)S(1)} %add_convert_fusion.11), channel_id=1, source_target_pairs={{0,16},{2,18},{4,20},{6,22},{8,24},{10,26},{12,28},{14,30},{16,0},... | collective-permute-start | bytes 393224 | tf_op jit(solution)/shard_map/ppermute | solution.py:357
  112.7 1.6 copy-done.7
  114.3 10.7 %inner.7 = (f32[8,512,128]{2,1,0:T(8,128)S(1)}, f32[8,512,128]{2,1,0:T(8,128)S(1)}) custom-call(s32[1]{0:T(128)} %bitcast.mine_ref.place_ref, bf16[128,8192]{1,0:T(8,128)(2,1)S(1)} %bitcast.93, bf16[128,8192]{1,0:T(8,128)(2,1)S(1)} %get-tuple-element.96.high_ref, bf16[4,2,2,512,128]{4,3,2,1,0:T(8,128)(2,1)S(1)} %bitcast.97, ...), custom_call_target="tpu_custom_call" | custom-call | flops 1610612736 | bytes 20971520 | tf_op jit(solution)/shard_map/inner/pallas_call | solution.py:258
  125.2 1.4 copy-done.13
  126.6 1.1 add_convert_fusion.5
  128.8 1.3 bitcast_add_fusion.7
  131.0 2.6 %collective-permute-start.21 = (f16[1,512,128]{2,1,0:T(8,128)(2,1)S(1)}, f16[1,512,128]{2,1,0:T(8,128)(2,1)S(1)}, u32[]{:S(2)}, u32[]{:S(2)}) collective-permute-start(f16[1,512,128]{2,1,0:T(8,128)(2,1)S(1)} %add_convert_fusion.10), channel_id=1, source_target_pairs={{0,16},{2,18},{4,20},{6,22},{8,24},{10,26},{12,28},{14,30},{16,0},... | collective-permute-start | bytes 393224 | tf_op jit(solution)/shard_map/ppermute | solution.py:357
  133.8 1.6 collective-permute-start.14
  135.3 4.9 %collective-permute-done.20 = bf16[1,512,128]{2,1,0:T(8,128)(2,1)S(1)} collective-permute-done((bf16[1,512,128]{2,1,0:T(8,128)(2,1)S(1)}, bf16[1,512,128]{2,1,0:T(8,128)(2,1)S(1)}, u32[]{:S(2)}, u32[]{:S(2)}) %collective-permute-start.20) | collective-permute-done | bytes 131104 | tf_op jit(solution)/shard_map/ppermute | solution.py:357
  140.2 5.5 %collective-permute-done.21 = f16[1,512,128]{2,1,0:T(8,128)(2,1)S(1)} collective-permute-done((f16[1,512,128]{2,1,0:T(8,128)(2,1)S(1)}, f16[1,512,128]{2,1,0:T(8,128)(2,1)S(1)}, u32[]{:S(2)}, u32[]{:S(2)}) %collective-permute-start.21) | collective-permute-done | bytes 131104 | tf_op jit(solution)/shard_map/ppermute | solution.py:357
  145.8 1.2 bitcast_add_fusion.1
  147.0 1.9 collective-permute-start.27
  149.8 1.2 collective-permute-start.23
  151.0 8.3 %collective-permute-done.27 = bf16[1,512,128]{2,1,0:T(8,128)(2,1)S(1)} collective-permute-done((bf16[1,512,128]{2,1,0:T(8,128)(2,1)S(1)}, bf16[1,512,128]{2,1,0:T(8,128)(2,1)S(1)}, u32[]{:S(2)}, u32[]{:S(2)}) %collective-permute-start.27) | collective-permute-done | bytes 131104 | tf_op jit(solution)/shard_map/ppermute | solution.py:357
  159.5 1.8 collective-permute-done.23
  161.3 1.6 collective-permute-start.31
  164.1 2.5 %collective-permute-start.15 = (f16[2,512,128]{2,1,0:T(8,128)(2,1)S(1)}, f16[2,512,128]{2,1,0:T(8,128)(2,1)S(1)}, u32[]{:S(2)}, u32[]{:S(2)}) collective-permute-start(f16[2,512,128]{2,1,0:T(8,128)(2,1)S(1)} %add_convert_fusion.4), channel_id=1, source_target_pairs={{0,8},{2,10},{4,12},{6,14},{8,0},{10,2},{12,4},{14,6},{16,24},{18,... | collective-permute-start | bytes 786440 | tf_op jit(solution)/shard_map/ppermute | solution.py:357
  166.6 4.6 %collective-permute-done.24 = bf16[1,512,128]{2,1,0:T(8,128)(2,1)S(1)} collective-permute-done((bf16[1,512,128]{2,1,0:T(8,128)(2,1)S(1)}, bf16[1,512,128]{2,1,0:T(8,128)(2,1)S(1)}, u32[]{:S(2)}, u32[]{:S(2)}) %collective-permute-start.24) | collective-permute-done | bytes 131104 | tf_op jit(solution)/shard_map/ppermute | solution.py:357
  172.3 2.9 %collective-permute-done.31.refs_1_ = bf16[4,512,128]{2,1,0:T(8,128)(2,1)S(1)} collective-permute-done((bf16[4,512,128]{2,1,0:T(8,128)(2,1)S(1)}, bf16[4,512,128]{2,1,0:T(8,128)(2,1)S(1)}, u32[]{:S(2)}, u32[]{:S(2)}) %collective-permute-start.31) | collective-permute-done | bytes 524320 | tf_op jit(solution)/shard_map/ppermute | solution.py:357
  175.3 1.3 collective-permute-start.16
  176.7 3.6 %collective-permute-done.25 = bf16[2,512,128]{2,1,0:T(8,128)(2,1)S(1)} collective-permute-done((bf16[2,512,128]{2,1,0:T(8,128)(2,1)S(1)}, bf16[2,512,128]{2,1,0:T(8,128)(2,1)S(1)}, u32[]{:S(2)}, u32[]{:S(2)}) %collective-permute-start.25) | collective-permute-done | bytes 262176 | tf_op jit(solution)/shard_map/ppermute | solution.py:357
  180.3 1.2 collective-permute-start.26
  181.6 3.4 %collective-permute-done.16 = f16[1,512,128]{2,1,0:T(8,128)(2,1)S(1)} collective-permute-done((f16[1,512,128]{2,1,0:T(8,128)(2,1)S(1)}, f16[1,512,128]{2,1,0:T(8,128)(2,1)S(1)}, u32[]{:S(2)}, u32[]{:S(2)}) %collective-permute-start.16) | collective-permute-done | bytes 131104 | tf_op jit(solution)/shard_map/ppermute | solution.py:357
  185.3 1.3 collective-permute-done.29.refs_1_
  186.5 1.4 assemble.4.refs_4_
  188.6 5.1 %collective-permute-done.17 = bf16[1,512,128]{2,1,0:T(8,128)(2,1)S(1)} collective-permute-done((bf16[1,512,128]{2,1,0:T(8,128)(2,1)S(1)}, bf16[1,512,128]{2,1,0:T(8,128)(2,1)S(1)}, u32[]{:S(2)}, u32[]{:S(2)}) %collective-permute-start.17) | collective-permute-done | bytes 131104 | tf_op jit(solution)/shard_map/ppermute | solution.py:357
  193.9 1.5 collective-permute-done.26.refs_1_
  195.4 6.6 %collective-permute-done.18 = bf16[2,512,128]{2,1,0:T(8,128)(2,1)S(1)} collective-permute-done((bf16[2,512,128]{2,1,0:T(8,128)(2,1)S(1)}, bf16[2,512,128]{2,1,0:T(8,128)(2,1)S(1)}, u32[]{:S(2)}, u32[]{:S(2)}) %collective-permute-start.18) | collective-permute-done | bytes 262176 | tf_op jit(solution)/shard_map/ppermute | solution.py:357
  202.1 2.0 collective-permute-start.19
  204.1 1.4 assemble.5.refs_4_
  206.1 9.2 %collective-permute-done.19.refs_1_ = bf16[4,512,128]{2,1,0:T(8,128)(2,1)S(1)} collective-permute-done((bf16[4,512,128]{2,1,0:T(8,128)(2,1)S(1)}, bf16[4,512,128]{2,1,0:T(8,128)(2,1)S(1)}, u32[]{:S(2)}, u32[]{:S(2)}) %collective-permute-start.19) | collective-permute-done | bytes 524320 | tf_op jit(solution)/shard_map/ppermute | solution.py:357
  215.4 1.4 assemble.6.refs_4_
  218.8 1.4 assemble.7
  (130 shorter events, 17.0 us)
Async XLA Ops:
  0.6 6.2 %copy-start.2 = (bf16[1,128,8192]{2,1,0:T(8,128)(2,1)S(1)}, bf16[1,128,8192]{2,1,0:T(8,128)(2,1)}, u32[]{:S(2)}) copy-start(bf16[1,128,8192]{2,1,0:T(8,128)(2,1)} %param.11) | copy-start | bytes 6291460
  0.6 10.0 %copy-start.27 = (s32[1,2,512]{2,1,0:T(2,128)S(1)}, s32[1,2,512]{2,1,0:T(2,128)}, u32[]{:S(2)}) copy-start(s32[1,2,512]{2,1,0:T(2,128)} %param.13) | copy-start | bytes 12292
  0.7 10.2 %copy-start.21 = (bf16[1,256,512]{2,1,0:T(8,128)(2,1)S(1)}, bf16[1,256,512]{2,1,0:T(8,128)(2,1)}, u32[]{:S(2)}) copy-start(bf16[1,256,512]{2,1,0:T(8,128)(2,1)} %param.12) | copy-start | bytes 786436
  1.9 23.3 %collective-permute-start.3 = (bf16[128,2048]{1,0:T(8,128)(2,1)S(1)}, bf16[128,2048]{1,0:T(8,128)(2,1)S(1)}, u32[]{:S(2)}, u32[]{:S(2)}) collective-permute-start(bf16[128,2048]{1,0:T(8,128)(2,1)S(1)} %slice.344), channel_id=1, source_target_pairs={{0,1},{1,0},{2,3},{3,2},{4,5},{5,4},{6,7},{7,6},{8,9},{9,8},{10,11... | collective-permute-start | bytes 1572872 | tf_op jit(solution)/shard_map/ppermute | solution.py:378
  6.8 22.3 %collective-permute-start.2 = (bf16[128,2048]{1,0:T(8,128)(2,1)}, bf16[128,2048]{1,0:T(8,128)(2,1)}, u32[]{:S(2)}, u32[]{:S(2)}) collective-permute-start(bf16[128,2048]{1,0:T(8,128)(2,1)} %slice.277), channel_id=1, source_target_pairs={{0,1},{1,0},{2,3},{3,2},{4,5},{5,4},{6,7},{7,6},{8,9},{9,8},{10,11... | collective-permute-start | bytes 1572872 | tf_op jit(solution)/shard_map/ppermute | solution.py:378
  7.7 32.5 %collective-permute-start.1 = (bf16[128,2048]{1,0:T(8,128)(2,1)}, bf16[128,2048]{1,0:T(8,128)(2,1)}, u32[]{:S(2)}, u32[]{:S(2)}) collective-permute-start(bf16[128,2048]{1,0:T(8,128)(2,1)} %slice.278), channel_id=1, source_target_pairs={{0,1},{1,0},{2,3},{3,2},{4,5},{5,4},{6,7},{7,6},{8,9},{9,8},{10,11... | collective-permute-start | bytes 1572872 | tf_op jit(solution)/shard_map/ppermute | solution.py:378
  10.6 40.1 %collective-permute-start = (bf16[128,2048]{1,0:T(8,128)(2,1)}, bf16[128,2048]{1,0:T(8,128)(2,1)}, u32[]{:S(2)}, u32[]{:S(2)}) collective-permute-start(bf16[128,2048]{1,0:T(8,128)(2,1)} %slice.279), channel_id=1, source_target_pairs={{0,1},{1,0},{2,3},{3,2},{4,5},{5,4},{6,7},{7,6},{8,9},{9,8},{10,11... | collective-permute-start | bytes 1572872 | tf_op jit(solution)/shard_map/ppermute | solution.py:378
  15.9 1.3 copy-start.5
  21.1 2.0 copy-start.8
  23.1 2.0 copy-start.10
  50.7 2.4 %copy-start.3 = (bf16[1,128,8192]{2,1,0:T(8,128)(2,1)S(1)}, bf16[1,128,8192]{2,1,0:T(8,128)(2,1)}, u32[]{:S(2)}) copy-start(bf16[1,128,8192]{2,1,0:T(8,128)(2,1)} %param.11) | copy-start | bytes 6291460
  50.7 3.0 %copy-start.6 = (bf16[8192,128]{1,0:T(8,128)(2,1)S(1)}, bf16[8192,128]{1,0:T(8,128)(2,1)}, u32[]{:S(2)}) copy-start(bf16[8192,128]{1,0:T(8,128)(2,1)} %copy-done.5) | copy-start | bytes 6291460
  50.7 5.0 %copy-start.9 = (f32[4,2,2,512,128]{4,3,2,1,0:T(8,128)S(1)}, f32[4,2,2,512,128]{4,3,2,1,0:T(8,128)}, u32[]{:S(2)}) copy-start(f32[4,2,2,512,128]{4,3,2,1,0:T(8,128)} %copy-done.8) | copy-start | bytes 12582916
  50.7 6.2 %copy-start.11 = (f32[4,2,2,512,128]{4,3,2,1,0:T(8,128)S(1)}, f32[4,2,2,512,128]{4,3,2,1,0:T(8,128)}, u32[]{:S(2)}) copy-start(f32[4,2,2,512,128]{4,3,2,1,0:T(8,128)} %copy-done.10) | copy-start | bytes 12582916
  53.0 36.2 %copy-start = (bf16[8192,128]{1,0:T(8,128)(2,1)}, bf16[8192,128]{1,0:T(8,128)(2,1)S(1)}, u32[]{:S(2)}) copy-start(bf16[8192,128]{1,0:T(8,128)(2,1)S(1)} %get-tuple-element.98) | copy-start | bytes 6291460
  65.8 35.5 %copy-start.15 = (f32[8,512,128]{2,1,0:T(8,128)}, f32[8,512,128]{2,1,0:T(8,128)S(1)}, u32[]{:S(2)}) copy-start(f32[8,512,128]{2,1,0:T(8,128)S(1)} %get-tuple-element.103) | copy-start | bytes 6291460
  65.9 2.7 %collective-permute-start.4 = (f16[8,512,128]{2,1,0:T(8,128)(2,1)S(1)}, f16[8,512,128]{2,1,0:T(8,128)(2,1)S(1)}, u32[]{:S(2)}, u32[]{:S(2)}) collective-permute-start(f16[8,512,128]{2,1,0:T(8,128)(2,1)S(1)} %convert_element_type.212), channel_id=1, source_target_pairs={{0,2},{2,0},{4,6},{6,4},{8,10},{10,8},{12,14},{14,12},{16,18},{18,... | collective-permute-start | bytes 3145736 | tf_op jit(solution)/shard_map/ppermute | solution.py:357
  68.7 32.6 %copy-start.20 = (f16[8,512,128]{2,1,0:T(8,128)(2,1)}, f16[8,512,128]{2,1,0:T(8,128)(2,1)S(1)}, u32[]{:S(2)}) copy-start(f16[8,512,128]{2,1,0:T(8,128)(2,1)S(1)} %collective-permute-done.4) | copy-start | bytes 3145732
  68.8 14.0 %collective-permute-start.5 = (f16[4,512,128]{2,1,0:T(8,128)(2,1)S(1)}, f16[4,512,128]{2,1,0:T(8,128)(2,1)S(1)}, u32[]{:S(2)}, u32[]{:S(2)}) collective-permute-start(f16[4,512,128]{2,1,0:T(8,128)(2,1)S(1)} %add_convert_fusion.3), channel_id=1, source_target_pairs={{0,4},{2,6},{4,0},{6,2},{8,12},{10,14},{12,8},{14,10},{16,20},{18,... | collective-permute-start | bytes 1572872 | tf_op jit(solution)/shard_map/ppermute | solution.py:357
  81.1 19.9 %copy-start.14 = (f32[8,512,128]{2,1,0:T(8,128)}, f32[8,512,128]{2,1,0:T(8,128)S(1)}, u32[]{:S(2)}) copy-start(f32[8,512,128]{2,1,0:T(8,128)S(1)} %get-tuple-element.109) | copy-start | bytes 6291460
  82.9 18.4 %copy-start.24 = (f16[4,512,128]{2,1,0:T(8,128)(2,1)}, f16[4,512,128]{2,1,0:T(8,128)(2,1)S(1)}, u32[]{:S(2)}) copy-start(f16[4,512,128]{2,1,0:T(8,128)(2,1)S(1)} %collective-permute-done.5) | copy-start | bytes 1572868
  83.0 2.7 %collective-permute-start.6 = (f16[8,512,128]{2,1,0:T(8,128)(2,1)S(1)}, f16[8,512,128]{2,1,0:T(8,128)(2,1)S(1)}, u32[]{:S(2)}, u32[]{:S(2)}) collective-permute-start(f16[8,512,128]{2,1,0:T(8,128)(2,1)S(1)} %convert_element_type.220), channel_id=1, source_target_pairs={{0,2},{2,0},{4,6},{6,4},{8,10},{10,8},{12,14},{14,12},{16,18},{18,... | collective-permute-start | bytes 3145736 | tf_op jit(solution)/shard_map/ppermute | solution.py:357
  85.7 15.4 %copy-start.19 = (f16[8,512,128]{2,1,0:T(8,128)(2,1)}, f16[8,512,128]{2,1,0:T(8,128)(2,1)S(1)}, u32[]{:S(2)}) copy-start(f16[8,512,128]{2,1,0:T(8,128)(2,1)S(1)} %collective-permute-done.6) | copy-start | bytes 3145732
  85.9 15.2 %collective-permute-start.8 = (f16[4,512,128]{2,1,0:T(8,128)(2,1)S(1)}, f16[4,512,128]{2,1,0:T(8,128)(2,1)S(1)}, u32[]{:S(2)}, u32[]{:S(2)}) collective-permute-start(f16[4,512,128]{2,1,0:T(8,128)(2,1)S(1)} %add_convert_fusion.2), channel_id=1, source_target_pairs={{0,4},{2,6},{4,0},{6,2},{8,12},{10,14},{12,8},{14,10},{16,20},{18,... | collective-permute-start | bytes 1572872 | tf_op jit(solution)/shard_map/ppermute | solution.py:357
  87.7 13.4 %collective-permute-start.7 = (f16[2,512,128]{2,1,0:T(8,128)(2,1)S(1)}, f16[2,512,128]{2,1,0:T(8,128)(2,1)S(1)}, u32[]{:S(2)}, u32[]{:S(2)}) collective-permute-start(f16[2,512,128]{2,1,0:T(8,128)(2,1)S(1)} %add_convert_fusion.7), channel_id=1, source_target_pairs={{0,8},{2,10},{4,12},{6,14},{8,0},{10,2},{12,4},{14,6},{16,24},{18,... | collective-permute-start | bytes 786440 | tf_op jit(solution)/shard_map/ppermute | solution.py:357
  99.8 1.7 copy-start.12
  102.0 3.0 %collective-permute-start.9 = (f16[8,512,128]{2,1,0:T(8,128)(2,1)}, f16[8,512,128]{2,1,0:T(8,128)(2,1)}, u32[]{:S(2)}, u32[]{:S(2)}) collective-permute-start(f16[8,512,128]{2,1,0:T(8,128)(2,1)} %convert_element_type.228), channel_id=1, source_target_pairs={{0,2},{2,0},{4,6},{6,4},{8,10},{10,8},{12,14},{14,12},{16,18},{18,... | collective-permute-start | bytes 3145736 | tf_op jit(solution)/shard_map/ppermute | solution.py:357
  102.0 5.3 %copy-start.18 = (f32[512,512]{1,0:T(8,128)S(1)}, f32[512,512]{1,0:T(8,128)}, u32[]{:S(2)}) copy-start(f32[512,512]{1,0:T(8,128)} %param.8) | copy-start | bytes 3145732
  105.0 7.7 %copy-start.4 = (bf16[1,128,8192]{2,1,0:T(8,128)(2,1)S(1)}, bf16[1,128,8192]{2,1,0:T(8,128)(2,1)}, u32[]{:S(2)}) copy-start(bf16[1,128,8192]{2,1,0:T(8,128)(2,1)} %param.11) | copy-start | bytes 6291460
  106.6 6.1 %copy-start.1 = (bf16[8192,128]{1,0:T(8,128)(2,1)S(1)}, bf16[8192,128]{1,0:T(8,128)(2,1)}, u32[]{:S(2)}) copy-start(bf16[8192,128]{1,0:T(8,128)(2,1)} %copy-done) | copy-start | bytes 6291460
  106.7 18.6 %collective-permute-start.12 = (f16[4,512,128]{2,1,0:T(8,128)(2,1)S(1)}, f16[4,512,128]{2,1,0:T(8,128)(2,1)S(1)}, u32[]{:S(2)}, u32[]{:S(2)}) collective-permute-start(f16[4,512,128]{2,1,0:T(8,128)(2,1)S(1)} %add_convert_fusion.1), channel_id=1, source_target_pairs={{0,4},{2,6},{4,0},{6,2},{8,12},{10,14},{12,8},{14,10},{16,20},{18,... | collective-permute-start | bytes 1572872 | tf_op jit(solution)/shard_map/ppermute | solution.py:357
  107.3 17.9 %collective-permute-start.11 = (f16[2,512,128]{2,1,0:T(8,128)(2,1)S(1)}, f16[2,512,128]{2,1,0:T(8,128)(2,1)S(1)}, u32[]{:S(2)}, u32[]{:S(2)}) collective-permute-start(f16[2,512,128]{2,1,0:T(8,128)(2,1)S(1)} %add_convert_fusion.6), channel_id=1, source_target_pairs={{0,8},{2,10},{4,12},{6,14},{8,0},{10,2},{12,4},{14,6},{16,24},{18,... | collective-permute-start | bytes 786440 | tf_op jit(solution)/shard_map/ppermute | solution.py:357
  110.1 15.1 %collective-permute-start.10 = (f16[1,512,128]{2,1,0:T(8,128)(2,1)S(1)}, f16[1,512,128]{2,1,0:T(8,128)(2,1)S(1)}, u32[]{:S(2)}, u32[]{:S(2)}) collective-permute-start(f16[1,512,128]{2,1,0:T(8,128)(2,1)S(1)} %add_convert_fusion.11), channel_id=1, source_target_pairs={{0,16},{2,18},{4,20},{6,22},{8,24},{10,26},{12,28},{14,30},{16,0},... | collective-permute-start | bytes 393224 | tf_op jit(solution)/shard_map/ppermute | solution.py:357
  112.7 1.6 copy-start.7
  125.0 1.6 copy-start.13
  125.0 2.7 %copy-start.23 = (f16[4,512,128]{2,1,0:T(8,128)(2,1)S(1)}, f16[4,512,128]{2,1,0:T(8,128)(2,1)}, u32[]{:S(2)}) copy-start(f16[4,512,128]{2,1,0:T(8,128)(2,1)} %copy-done.22) | copy-start | bytes 1572868
  125.0 3.7 %copy-start.26 = (f16[2,512,128]{2,1,0:T(8,128)(2,1)S(1)}, f16[2,512,128]{2,1,0:T(8,128)(2,1)}, u32[]{:S(2)}) copy-start(f16[2,512,128]{2,1,0:T(8,128)(2,1)} %copy-done.25) | copy-start | bytes 786436
  130.1 3.6 %collective-permute-start.13 = (f16[8,512,128]{2,1,0:T(8,128)(2,1)S(1)}, f16[8,512,128]{2,1,0:T(8,128)(2,1)S(1)}, u32[]{:S(2)}, u32[]{:S(2)}) collective-permute-start(f16[8,512,128]{2,1,0:T(8,128)(2,1)S(1)} %convert_element_type.244), channel_id=1, source_target_pairs={{0,2},{2,0},{4,6},{6,4},{8,10},{10,8},{12,14},{14,12},{16,18},{18,... | collective-permute-start | bytes 3145736 | tf_op jit(solution)/shard_map/ppermute | solution.py:357
  130.1 15.5 %collective-permute-start.22 = (f16[2,512,128]{2,1,0:T(8,128)(2,1)S(1)}, f16[2,512,128]{2,1,0:T(8,128)(2,1)S(1)}, u32[]{:S(2)}, u32[]{:S(2)}) collective-permute-start(f16[2,512,128]{2,1,0:T(8,128)(2,1)S(1)} %add_convert_fusion.5), channel_id=1, source_target_pairs={{0,8},{2,10},{4,12},{6,14},{8,0},{10,2},{12,4},{14,6},{16,24},{18,... | collective-permute-start | bytes 786440 | tf_op jit(solution)/shard_map/ppermute | solution.py:357
  130.7 9.5 %collective-permute-start.20 = (bf16[1,512,128]{2,1,0:T(8,128)(2,1)S(1)}, bf16[1,512,128]{2,1,0:T(8,128)(2,1)S(1)}, u32[]{:S(2)}, u32[]{:S(2)}) collective-permute-start(bf16[1,512,128]{2,1,0:T(8,128)(2,1)S(1)} %get-tuple-element.135), channel_id=1, source_target_pairs={{0,16},{2,18},{4,20},{6,22},{8,24},{10,26},{12,28},{14,30},{16,0},... | collective-permute-start | bytes 393224 | tf_op jit(solution)/shard_map/ppermute | solution.py:357
  131.0 14.6 %collective-permute-start.21 = (f16[1,512,128]{2,1,0:T(8,128)(2,1)S(1)}, f16[1,512,128]{2,1,0:T(8,128)(2,1)S(1)}, u32[]{:S(2)}, u32[]{:S(2)}) collective-permute-start(f16[1,512,128]{2,1,0:T(8,128)(2,1)S(1)} %add_convert_fusion.10), channel_id=1, source_target_pairs={{0,16},{2,18},{4,20},{6,22},{8,24},{10,26},{12,28},{14,30},{16,0},... | collective-permute-start | bytes 393224 | tf_op jit(solution)/shard_map/ppermute | solution.py:357
  133.8 30.2 %collective-permute-start.14 = (f16[4,512,128]{2,1,0:T(8,128)(2,1)S(1)}, f16[4,512,128]{2,1,0:T(8,128)(2,1)S(1)}, u32[]{:S(2)}, u32[]{:S(2)}) collective-permute-start(f16[4,512,128]{2,1,0:T(8,128)(2,1)S(1)} %add_convert_fusion), channel_id=1, source_target_pairs={{0,4},{2,6},{4,0},{6,2},{8,12},{10,14},{12,8},{14,10},{16,20},{18,... | collective-permute-start | bytes 1572872 | tf_op jit(solution)/shard_map/ppermute | solution.py:357
  145.7 15.5 %collective-permute-start.30 = (bf16[2,512,128]{2,1,0:T(8,128)(2,1)S(1)}, bf16[2,512,128]{2,1,0:T(8,128)(2,1)S(1)}, u32[]{:S(2)}, u32[]{:S(2)}) collective-permute-start(bf16[2,512,128]{2,1,0:T(8,128)(2,1)S(1)} %pad_maximum_fusion.8), channel_id=1, source_target_pairs={{0,8},{2,10},{4,12},{6,14},{8,0},{10,2},{12,4},{14,6},{16,24},{18,... | collective-permute-start | bytes 786440 | tf_op jit(solution)/shard_map/ppermute | solution.py:357
  147.0 12.4 %collective-permute-start.27 = (bf16[1,512,128]{2,1,0:T(8,128)(2,1)S(1)}, bf16[1,512,128]{2,1,0:T(8,128)(2,1)S(1)}, u32[]{:S(2)}, u32[]{:S(2)}) collective-permute-start(bf16[1,512,128]{2,1,0:T(8,128)(2,1)S(1)} %get-tuple-element.157), channel_id=1, source_target_pairs={{0,16},{2,18},{4,20},{6,22},{8,24},{10,26},{12,28},{14,30},{16,0},... | collective-permute-start | bytes 393224 | tf_op jit(solution)/shard_map/ppermute | solution.py:357
  149.8 11.4 %collective-permute-start.23 = (f16[1,512,128]{2,1,0:T(8,128)(2,1)S(1)}, f16[1,512,128]{2,1,0:T(8,128)(2,1)S(1)}, u32[]{:S(2)}, u32[]{:S(2)}) collective-permute-start(f16[1,512,128]{2,1,0:T(8,128)(2,1)S(1)} %add_convert_fusion.8), channel_id=1, source_target_pairs={{0,16},{2,18},{4,20},{6,22},{8,24},{10,26},{12,28},{14,30},{16,0},... | collective-permute-start | bytes 393224 | tf_op jit(solution)/shard_map/ppermute | solution.py:357
  159.4 12.4 %collective-permute-start.28 = (bf16[2,512,128]{2,1,0:T(8,128)(2,1)S(1)}, bf16[2,512,128]{2,1,0:T(8,128)(2,1)S(1)}, u32[]{:S(2)}, u32[]{:S(2)}) collective-permute-start(bf16[2,512,128]{2,1,0:T(8,128)(2,1)S(1)} %pad_maximum_fusion.7), channel_id=1, source_target_pairs={{0,8},{2,10},{4,12},{6,14},{8,0},{10,2},{12,4},{14,6},{16,24},{18,... | collective-permute-start | bytes 786440 | tf_op jit(solution)/shard_map/ppermute | solution.py:357
  161.3 13.9 %collective-permute-start.31 = (bf16[4,512,128]{2,1,0:T(8,128)(2,1)S(1)}, bf16[4,512,128]{2,1,0:T(8,128)(2,1)S(1)}, u32[]{:S(2)}, u32[]{:S(2)}) collective-permute-start(bf16[4,512,128]{2,1,0:T(8,128)(2,1)S(1)} %pad_maximum_fusion.4.refs_0_), channel_id=1, source_target_pairs={{0,4},{2,6},{4,0},{6,2},{8,12},{10,14},{12,8},{14,10},{16,20},{18,... | collective-permute-start | bytes 1572872 | tf_op jit(solution)/shard_map/ppermute | solution.py:357
  163.9 7.3 %collective-permute-start.24 = (bf16[1,512,128]{2,1,0:T(8,128)(2,1)S(1)}, bf16[1,512,128]{2,1,0:T(8,128)(2,1)S(1)}, u32[]{:S(2)}, u32[]{:S(2)}) collective-permute-start(bf16[1,512,128]{2,1,0:T(8,128)(2,1)S(1)} %get-tuple-element.159), channel_id=1, source_target_pairs={{0,16},{2,18},{4,20},{6,22},{8,24},{10,26},{12,28},{14,30},{16,0},... | collective-permute-start | bytes 393224 | tf_op jit(solution)/shard_map/ppermute | solution.py:357
  164.1 11.1 %collective-permute-start.15 = (f16[2,512,128]{2,1,0:T(8,128)(2,1)S(1)}, f16[2,512,128]{2,1,0:T(8,128)(2,1)S(1)}, u32[]{:S(2)}, u32[]{:S(2)}) collective-permute-start(f16[2,512,128]{2,1,0:T(8,128)(2,1)S(1)} %add_convert_fusion.4), channel_id=1, source_target_pairs={{0,8},{2,10},{4,12},{6,14},{8,0},{10,2},{12,4},{14,6},{16,24},{18,... | collective-permute-start | bytes 786440 | tf_op jit(solution)/shard_map/ppermute | solution.py:357
  166.6 19.9 %collective-permute-start.32 = (bf16[4,512,128]{2,1,0:T(8,128)(2,1)S(1)}, bf16[4,512,128]{2,1,0:T(8,128)(2,1)S(1)}, u32[]{:S(2)}, u32[]{:S(2)}) collective-permute-start(bf16[4,512,128]{2,1,0:T(8,128)(2,1)S(1)} %pad_maximum_fusion.4.refs_0_), channel_id=1, source_target_pairs={{0,2},{2,0},{4,6},{6,4},{8,10},{10,8},{12,14},{14,12},{16,18},{18,... | collective-permute-start | bytes 1572872 | tf_op jit(solution)/shard_map/ppermute | solution.py:357
  171.2 9.0 %collective-permute-start.25 = (bf16[2,512,128]{2,1,0:T(8,128)(2,1)S(1)}, bf16[2,512,128]{2,1,0:T(8,128)(2,1)S(1)}, u32[]{:S(2)}, u32[]{:S(2)}) collective-permute-start(bf16[2,512,128]{2,1,0:T(8,128)(2,1)S(1)} %pad_maximum_fusion.6), channel_id=1, source_target_pairs={{0,8},{2,10},{4,12},{6,14},{8,0},{10,2},{12,4},{14,6},{16,24},{18,... | collective-permute-start | bytes 786440 | tf_op jit(solution)/shard_map/ppermute | solution.py:357
  171.8 14.7 %collective-permute-start.29 = (bf16[4,512,128]{2,1,0:T(8,128)(2,1)S(1)}, bf16[4,512,128]{2,1,0:T(8,128)(2,1)S(1)}, u32[]{:S(2)}, u32[]{:S(2)}) collective-permute-start(bf16[4,512,128]{2,1,0:T(8,128)(2,1)S(1)} %pad_maximum_fusion.3.refs_0_), channel_id=1, source_target_pairs={{0,4},{2,6},{4,0},{6,2},{8,12},{10,14},{12,8},{14,10},{16,20},{18,... | collective-permute-start | bytes 1572872 | tf_op jit(solution)/shard_map/ppermute | solution.py:357
  175.2 11.3 %collective-permute-start.33 = (bf16[4,512,128]{2,1,0:T(8,128)(2,1)S(1)}, bf16[4,512,128]{2,1,0:T(8,128)(2,1)S(1)}, u32[]{:S(2)}, u32[]{:S(2)}) collective-permute-start(bf16[4,512,128]{2,1,0:T(8,128)(2,1)S(1)} %collective-permute-done.31.refs_1_), channel_id=1, source_target_pairs={{0,2},{2,0},{4,6},{6,4},{8,10},{10,8},{12,14},{14,12},{16,18},{18,... | collective-permute-start | bytes 1572872 | tf_op jit(solution)/shard_map/ppermute | solution.py:357
  175.3 9.7 %collective-permute-start.16 = (f16[1,512,128]{2,1,0:T(8,128)(2,1)S(1)}, f16[1,512,128]{2,1,0:T(8,128)(2,1)S(1)}, u32[]{:S(2)}, u32[]{:S(2)}) collective-permute-start(f16[1,512,128]{2,1,0:T(8,128)(2,1)S(1)} %add_convert_fusion.9), channel_id=1, source_target_pairs={{0,16},{2,18},{4,20},{6,22},{8,24},{10,26},{12,28},{14,30},{16,0},... | collective-permute-start | bytes 393224 | tf_op jit(solution)/shard_map/ppermute | solution.py:357
  180.3 15.0 %collective-permute-start.26 = (bf16[4,512,128]{2,1,0:T(8,128)(2,1)S(1)}, bf16[4,512,128]{2,1,0:T(8,128)(2,1)S(1)}, u32[]{:S(2)}, u32[]{:S(2)}) collective-permute-start(bf16[4,512,128]{2,1,0:T(8,128)(2,1)S(1)} %pad_maximum_fusion.2.refs_0_), channel_id=1, source_target_pairs={{0,4},{2,6},{4,0},{6,2},{8,12},{10,14},{12,8},{14,10},{16,20},{18,... | collective-permute-start | bytes 1572872 | tf_op jit(solution)/shard_map/ppermute | solution.py:357
  185.2 8.5 %collective-permute-start.17 = (bf16[1,512,128]{2,1,0:T(8,128)(2,1)S(1)}, bf16[1,512,128]{2,1,0:T(8,128)(2,1)S(1)}, u32[]{:S(2)}, u32[]{:S(2)}) collective-permute-start(bf16[1,512,128]{2,1,0:T(8,128)(2,1)S(1)} %get-tuple-element.161), channel_id=1, source_target_pairs={{0,16},{2,18},{4,20},{6,22},{8,24},{10,26},{12,28},{14,30},{16,0},... | collective-permute-start | bytes 393224 | tf_op jit(solution)/shard_map/ppermute | solution.py:357
  186.5 17.6 %collective-permute-start.34 = (bf16[4,512,128]{2,1,0:T(8,128)(2,1)S(1)}, bf16[4,512,128]{2,1,0:T(8,128)(2,1)S(1)}, u32[]{:S(2)}, u32[]{:S(2)}) collective-permute-start(bf16[4,512,128]{2,1,0:T(8,128)(2,1)S(1)} %pad_maximum_fusion.3.refs_0_), channel_id=1, source_target_pairs={{0,2},{2,0},{4,6},{6,4},{8,10},{10,8},{12,14},{14,12},{16,18},{18,... | collective-permute-start | bytes 1572872 | tf_op jit(solution)/shard_map/ppermute | solution.py:357
  188.0 16.1 %collective-permute-start.35 = (bf16[4,512,128]{2,1,0:T(8,128)(2,1)S(1)}, bf16[4,512,128]{2,1,0:T(8,128)(2,1)S(1)}, u32[]{:S(2)}, u32[]{:S(2)}) collective-permute-start(bf16[4,512,128]{2,1,0:T(8,128)(2,1)S(1)} %collective-permute-done.29.refs_1_), channel_id=1, source_target_pairs={{0,2},{2,0},{4,6},{6,4},{8,10},{10,8},{12,14},{14,12},{16,18},{18,... | collective-permute-start | bytes 1572872 | tf_op jit(solution)/shard_map/ppermute | solution.py:357
  193.7 8.3 %collective-permute-start.18 = (bf16[2,512,128]{2,1,0:T(8,128)(2,1)S(1)}, bf16[2,512,128]{2,1,0:T(8,128)(2,1)S(1)}, u32[]{:S(2)}, u32[]{:S(2)}) collective-permute-start(bf16[2,512,128]{2,1,0:T(8,128)(2,1)S(1)} %pad_maximum_fusion.5), channel_id=1, source_target_pairs={{0,8},{2,10},{4,12},{6,14},{8,0},{10,2},{12,4},{14,6},{16,24},{18,... | collective-permute-start | bytes 786440 | tf_op jit(solution)/shard_map/ppermute | solution.py:357
  193.8 21.6 %collective-permute-start.36 = (bf16[4,512,128]{2,1,0:T(8,128)(2,1)S(1)}, bf16[4,512,128]{2,1,0:T(8,128)(2,1)S(1)}, u32[]{:S(2)}, u32[]{:S(2)}) collective-permute-start(bf16[4,512,128]{2,1,0:T(8,128)(2,1)S(1)} %pad_maximum_fusion.2.refs_0_), channel_id=1, source_target_pairs={{0,2},{2,0},{4,6},{6,4},{8,10},{10,8},{12,14},{14,12},{16,18},{18,... | collective-permute-start | bytes 1572872 | tf_op jit(solution)/shard_map/ppermute | solution.py:357
  202.1 13.3 %collective-permute-start.19 = (bf16[4,512,128]{2,1,0:T(8,128)(2,1)S(1)}, bf16[4,512,128]{2,1,0:T(8,128)(2,1)S(1)}, u32[]{:S(2)}, u32[]{:S(2)}) collective-permute-start(bf16[4,512,128]{2,1,0:T(8,128)(2,1)S(1)} %pad_maximum_fusion.1.refs_0_), channel_id=1, source_target_pairs={{0,4},{2,6},{4,0},{6,2},{8,12},{10,14},{12,8},{14,10},{16,20},{18,... | collective-permute-start | bytes 1572872 | tf_op jit(solution)/shard_map/ppermute | solution.py:357
  205.6 9.8 %collective-permute-start.37 = (bf16[4,512,128]{2,1,0:T(8,128)(2,1)S(1)}, bf16[4,512,128]{2,1,0:T(8,128)(2,1)S(1)}, u32[]{:S(2)}, u32[]{:S(2)}) collective-permute-start(bf16[4,512,128]{2,1,0:T(8,128)(2,1)S(1)} %collective-permute-done.26.refs_1_), channel_id=1, source_target_pairs={{0,2},{2,0},{4,6},{6,4},{8,10},{10,8},{12,14},{14,12},{16,18},{18,... | collective-permute-start | bytes 1572872 | tf_op jit(solution)/shard_map/ppermute | solution.py:357
  205.6 12.3 %collective-permute-start.38 = (bf16[4,512,128]{2,1,0:T(8,128)(2,1)S(1)}, bf16[4,512,128]{2,1,0:T(8,128)(2,1)S(1)}, u32[]{:S(2)}, u32[]{:S(2)}) collective-permute-start(bf16[4,512,128]{2,1,0:T(8,128)(2,1)S(1)} %pad_maximum_fusion.1.refs_0_), channel_id=1, source_target_pairs={{0,2},{2,0},{4,6},{6,4},{8,10},{10,8},{12,14},{14,12},{16,18},{18,... | collective-permute-start | bytes 1572872 | tf_op jit(solution)/shard_map/ppermute | solution.py:357
  216.8 2.0 collective-permute-start.39
  (4 other events, 3.4 us)

commit v8 on v7

--- a/solution.py
+++ b/solution.py
@@ -13,7 +13,7 @@
 WIRE_SCALE = 64.0
 LANES = 128
 SLABS = 4
-PIECE = 64
+PIECE = 32
 MIB = 1024 * 1024
 
 
@@ -108,35 +108,8 @@
     return place
 
 
-def fetch_kernel(chunk, first_ref, second_ref, first_out, second_out, semaphore):
-    width = first_out.shape[-1]
-    columns = pl.ds(chunk * width, width)
-    copies = [
-        pltpu.make_async_copy(source.at[..., columns], target, semaphore.at[index])
-        for index, (source, target) in enumerate(((first_ref, first_out), (second_ref, second_out)))
-    ]
-    for copy in copies:
-        copy.start()
-    for copy in copies:
-        copy.wait()
-
-
-def fetch(chunk, width, first, second):
-    out = jax.ShapeDtypeStruct(first.shape[:-1] + (width,), F32)
-    return pl.pallas_call(
-        functools.partial(fetch_kernel, chunk),
-        in_specs=[pl.BlockSpec(memory_space=pl.ANY)] * 2,
-        out_specs=[pl.BlockSpec(memory_space=pltpu.VMEM)] * 2,
-        out_shape=[out, out],
-        scratch_shapes=[pltpu.SemaphoreType.DMA((2,))],
-        compiler_params=pltpu.CompilerParams(vmem_limit_bytes=MIB),
-        name="fetch",
-    )(pinned(first), pinned(second))
-
-
 def inner_kernel(
     tokens,
-    fetched,
     mine_ref,
     low_ref,
     high_ref,
@@ -149,24 +122,18 @@
     high_product_ref,
     target_ref,
     count_ref,
-    send_ref,
-    keep_ref,
-    first_state,
-    second_state,
-    weights_state,
-    output_state,
-    residual_state,
-    gradient_state,
-    rounded_state,
+    *rest,
 ):
+    *change_refs, first_state, second_state, output_state, residual_state, gradient_state, rounded_state = rest
+    send_refs, keep_refs = change_refs[::2], change_refs[1::2]
     step = pl.program_id(0)
     slab = pl.program_id(1)
-    if fetched:
-        first_ref, second_ref = first_ref.at[slab], second_ref.at[slab]
     pairs, cores, rows, _ = start_ref.shape
     mine = mine_ref[0]
     core = lax.rem(mine, cores)
     pieces = [pl.ds(begin, PIECE) for begin in range(0, rows, PIECE)]
+    slots = [(slot, *divmod(slot, cores)) for slot in range(pairs * cores)]
+    held = gradient_state.shape[0]
 
     def weigh(output, which):
         residual = ((output - target_ref[...].astype(F32)) / tokens).astype(BF16)
@@ -175,13 +142,13 @@
     def descend(first, second, weights):
         root = second * lax.rsqrt(second)
         below = (100.0 * math.sqrt(0.05)) * root + 1e-06
-        return 0.99 * weights - first * pl.reciprocal(below, approx=True)
+        return 0.99 * weights - first * lax.rsqrt(below * below)
 
     def differentiate(pair, which, slot):
         turned = jnp.concatenate(
             [low_turned_ref[slab, pair, which], high_turned_ref[slab, pair, which]], axis=1
         )
-        gradient_state[slot] = jnp.dot(
+        gradient_state[slot % held] = jnp.dot(
             turned, residual_state[...], preferred_element_type=F32
         )
 
@@ -189,7 +156,7 @@
         begin = (slab * pairs * cores + slot) * rows
         place = pl.ds(pl.multiple_of(begin, rows), rows)
         picked = jnp.concatenate([low_ref[:, place], high_ref[:, place]], axis=0)
-        return jnp.dot(picked, rounded_state[slot], preferred_element_type=F32)
+        return jnp.dot(picked, rounded_state[slot % held], preferred_element_type=F32)
 
     @pl.when((step == 0) & (slab == 0))
     def _():
@@ -200,49 +167,48 @@
     def _():
         weigh(output_state[...], 1)
 
-    slots = [(slot, *divmod(slot, cores)) for slot in range(pairs * cores)]
-
     @pl.when(step == 0)
     def _():
-        total = jnp.zeros(output_state.shape, F32)
         differentiate(0, 0, 0)
         for slot, pair, which in slots:
             if slot + 1 < len(slots):
                 ahead, *place = slots[slot + 1]
                 differentiate(*place, ahead)
             for piece in pieces:
-                gradient = gradient_state[slot, piece]
+                gradient = gradient_state[slot % held, piece]
                 first = 9.0 * first_ref[pair, which, piece] + gradient
                 second = 19.0 * second_ref[pair, which, piece] + gradient * gradient
                 weights = descend(first, second, start_ref[pair, which, piece].astype(F32))
                 first_state[slab, pair, which, piece] = first
                 second_state[slab, pair, which, piece] = second
-                weights_state[slab, pair, which, piece] = weights
-                rounded_state[slot, piece] = weights.astype(BF16)
-            if slot:
-                total += project(slot - 1)
-        output_state[...] += total + project(len(slots) - 1)
+                rounded_state[slot % held, piece] = weights.astype(BF16)
+            output_state[...] += project(slot)
 
     @pl.when(step == 1)
     def _():
-        sides = ((1 - core, send_ref), (core, keep_ref))
+        sides = ((1 - core, send_refs), (core, keep_refs))
         differentiate(0, sides[0][0], 0)
         for slot, pair, side in slots:
             if slot + 1 < len(slots):
                 ahead, next_pair, next_side = slots[slot + 1]
                 differentiate(next_pair, sides[next_side][0], ahead)
-            which, out_ref = sides[side]
+            which, out_refs = sides[side]
             place = changed_place(mine, slab, pair, pairs)
             for piece in pieces:
-                gradient = gradient_state[slot, piece]
-                first = 0.9 * first_state[slab, pair, which, piece] + gradient
-                second = 0.95 * second_state[slab, pair, which, piece] + gradient * gradient
-                weights = descend(first, second, weights_state[slab, pair, which, piece])
-                change = start_ref[pair, which, piece].astype(F32) - weights
-                out_ref[place, piece] = change * WIRE_SCALE
-
-
-def inner(chunk, width, fetched, mine, banks, turned, start, first, second, products, target, count, tokens):
+                gradient = gradient_state[slot % held, piece]
+                first = first_state[slab, pair, which, piece]
+                second = second_state[slab, pair, which, piece]
+                start = start_ref[pair, which, piece].astype(F32)
+                weights = descend(first, second, start)
+                first = 0.9 * first + gradient
+                second = 0.95 * second + gradient * gradient
+                change = (start - descend(first, second, weights)) * WIRE_SCALE
+                for index, out_ref in enumerate(out_refs):
+                    part = out_ref.shape[-1]
+                    out_ref[place, piece] = change[:, index * part : (index + 1) * part]
+
+
+def inner(call, width, part, mine, banks, turned, start, first, second, products, target, count, tokens):
     slabs, pairs, cores, rows, _ = start.shape
     half, depth = banks[0].shape
 
@@ -251,48 +217,45 @@
 
     whole = pl.BlockSpec(memory_space=pltpu.VMEM)
     tile = (None, pairs, cores, rows, width)
-    state = pl.BlockSpec(tile, lambda s, z, c: (held(s, z), 0, 0, 0, chunk))
-    product = pl.BlockSpec((half, width), lambda s, z, c: (0, chunk))
-    states = (first, second) if fetched else (pinned(first), pinned(second))
+    state = pl.BlockSpec(tile, lambda s, z, c: (held(s, z), 0, 0, 0, call))
+    product = pl.BlockSpec((half, width), lambda s, z, c: (0, call))
+    change = jax.ShapeDtypeStruct((slabs * pairs, rows, part), F32)
+    outputs = 2 * (width // part)
     elements = depth * width
     return pl.pallas_call(
-        functools.partial(inner_kernel, float(tokens), fetched),
+        functools.partial(inner_kernel, float(tokens)),
         grid_spec=pltpu.PrefetchScalarGridSpec(
             num_scalar_prefetch=1,
             grid=(2, slabs),
             in_specs=[whole] * 4
             + [
-                pl.BlockSpec(tile, lambda s, z, c: (z, 0, 0, 0, chunk)),
-                whole if fetched else state,
-                whole if fetched else state,
+                pl.BlockSpec(tile, lambda s, z, c: (z, 0, 0, 0, call)),
+                state,
+                state,
                 product,
                 product,
-                pl.BlockSpec((2 * half, width), lambda s, z, c: (0, chunk)),
+                pl.BlockSpec((2 * half, width), lambda s, z, c: (0, call)),
                 pl.BlockSpec(count.shape, lambda s, z, c: (0, 0, 0)),
             ],
-            out_specs=[whole, whole],
+            out_specs=[whole] * outputs,
             scratch_shapes=[
-                pltpu.VMEM((slabs, pairs, cores, rows, width), F32),
                 pltpu.VMEM((slabs, pairs, cores, rows, width), F32),
                 pltpu.VMEM((slabs, pairs, cores, rows, width), F32),
                 pltpu.VMEM((2 * half, width), F32),
                 pltpu.VMEM((2 * half, width), BF16),
-                pltpu.VMEM((pairs * cores, rows, width), F32),
-                pltpu.VMEM((pairs * cores, rows, width), BF16),
+                pltpu.VMEM((2, rows, width), F32),
+                pltpu.VMEM((2, rows, width), BF16),
             ],
         ),
-        out_shape=[
-            jax.ShapeDtypeStruct((slabs * pairs, rows, width), F32),
-            jax.ShapeDtypeStruct((slabs * pairs, rows, width), F32),
-        ],
-        compiler_params=pltpu.CompilerParams(vmem_limit_bytes=22 * MIB),
+        out_shape=[change] * outputs,
+        compiler_params=pltpu.CompilerParams(vmem_limit_bytes=32 * MIB),
         cost_estimate=pl.CostEstimate(
             flops=12 * half * elements,
             bytes_accessed=20 * elements,
-            transcendentals=4 * elements,
+            transcendentals=6 * elements,
         ),
         name="inner",
-    )(mine, *banks, *turned, pinned(start), *states, *products, target, count)
+    )(mine, *banks, *turned, pinned(start), pinned(first), pinned(second), *products, target, count)
 
 
 def assemble_kernel(chunk, offsets, place_ref, *refs):
@@ -362,7 +325,6 @@
     start = global_weights.reshape(cut)
     first = first_moment.reshape(cut)
     second = second_moment.reshape(cut)
-    early = fetch(0, width, first, second)
 
     own_bank = hidden_bank[0]
     target = target_bank[0]
@@ -377,7 +339,6 @@
             part, source = tied(source[:, d * block : (d + 1) * block], source)
             parts.append(lax.ppermute(part, "fsdp", [(0, 1), (1, 0)]))
         own_turned, own_product = forward(own_bank, global_weights)
-        parts[0], early = tied(parts[0], early)
         joined = ()
         for d, part in enumerate(parts):
             joined = arrive(d, part, global_weights, joined)
@@ -445,22 +406,22 @@
             formed[chunk] = running[chunk].send(arrived[chunk])
 
     token = place
-    for chunk in range(chunks):
-        states = early if chunk == 0 else (first, second)
-        send, keep = inner(
-            chunk, width, chunk == 0, token, banks, turned, start, *states, products, target, count, tokens
+    wide = min(columns, 2 * LANES)
+    for call in range(columns // wide):
+        changes = inner(
+            call, wide, width, token, banks, turned, start, first, second, products, target, count, tokens
         )
-        send = send.astype(WIRE)
-        if chunk:
-            move_on(range(chunk))
-            formed, send = tied(formed, send)
-        running[chunk] = chain(chunk, keep, swapped(send, 1))
-        formed[chunk] = next(running[chunk])
-        if chunk + 1 < chunks:
+        fresh = range(call * (wide // width), (call + 1) * (wide // width))
+        sends = [send.astype(WIRE) for send in changes[::2]]
+        if call:
+            move_on([0])
+            sends, _ = tied(sends, formed[0])
+        for chunk, send, keep in zip(fresh, sends, changes[1::2]):
+            running[chunk] = chain(chunk, keep, swapped(send, 1))
+            formed[chunk] = next(running[chunk])
+        if fresh[-1] + 1 < chunks:
             formed, token = tied(formed, token)
-
-    head = chunks - 1
-    move_on(range(head), behind=[head])
+    move_on(range(fresh[0]), behind=fresh)
     for chunk in range(chunks):
         while chunk not in finished:
             move_on([chunk])

time: 221 us -> 220 us (level)
  waiting for transfers between devices: 86.6 us -> 98.2 us
  local copies, waits for them, and re-layouts: 21.1 us -> 13.5 us
  Pallas kernels: 63.8 us -> 56.4 us
  other arithmetic: 12.9 us -> 18 us
  starting transfers between devices: 34.7 us -> 32.4 us
    unnamed x56 -> x34, local copies, waits for them, and re-layouts: 14.7 us -> 2.98 us
    ppermute x4, waiting for transfers between devices: 17.1 us -> 24.6 us  [per_device(): parts.append(lax.ppermute(part, 'fsdp', [(0, 1), (1, 0)]))]
    pallas_call x5 -> x2, Pallas kernels: 44.2 us -> 37 us  [inner(): pl.pallas_call(functools.partial(inner_kernel, float(tokens)), grid_spec=...]
    ppermute x36, waiting for transfers between devices: 69.5 us -> 73.6 us  [swapped(): return lax.ppermute(array, 'rep', pairs)]
    convert_element_type x12, other arithmetic: 5.77 us -> 9.18 us  [parted(): sum((term.astype(F32) for term in part)).astype(WIRE)]
    ppermute x36, starting transfers between devices: 29.6 us -> 27.3 us  [swapped(): return lax.ppermute(array, 'rep', pairs)]
  transfers between devices with their start and end apart: 40 -> 40, of which waited for: 20 -> 23; matrix products, arithmetic and copies ran while one was open for 6% -> 11% of each run, Pallas kernels for 23% -> 16%
where the time goes in v8:
time: 220 us
  waiting for transfers between devices  98.2 us (45%)
  Pallas kernels  56.4 us (26%)
  starting transfers between devices  32.4 us (15%)
  other arithmetic  18 us (8%)
  local copies, waits for them, and re-layouts  13.5 us (6%)
    ppermute x36, waiting for transfers between devices, swapped(): return lax.ppermute(array, 'rep', pairs)  73.6 us
    pallas_call x2, Pallas kernels, inner(): pl.pallas_call(functools.partial(inner_kernel, float(tokens)), grid_spec=...  37 us
    ppermute x36, starting transfers between devices, swapped(): return lax.ppermute(array, 'rep', pairs)  27.3 us
    ppermute x4, waiting for transfers between devices, per_device(): parts.append(lax.ppermute(part, 'fsdp', [(0, 1), (1, 0)]))  24.6 us
    convert_element_type x12, other arithmetic, parted(): sum((term.astype(F32) for term in part)).astype(WIRE)  9.18 us
    pallas_call x4, Pallas kernels, arrive(): pl.pallas_call(functools.partial(arrive_kernel, piece), grid=(1,), in_spe...  8.66 us
    pallas_call x4, Pallas kernels, assemble(): pl.pallas_call(functools.partial(assemble_kernel, chunk, offsets), in_spe...  5.76 us
    slice x4, local copies, waits for them, and re-layouts, per_device(): part, source = tied(source[:, d * block:(d + 1) * block], source)  5.61 us
  transfers between devices with their start and end apart: 40, of which 23 were waited for; matrix products, arithmetic and copies ran while one was open for 11% of the time, Pallas kernels for 16%

profile of v8, /device:TPU:0, one launch (start us, length us, event | category | flops | bytes accessed | tf_op | source)
XLA Modules:
  0.0 219.8 jit_solution(5880123271282157523)
XLA Ops:
  0.7 2.1 slice.344
  2.7 1.9 slice.277
  4.6 3.0 %collective-permute-start.2 = (bf16[128,2048]{1,0:T(8,128)(2,1)}, bf16[128,2048]{1,0:T(8,128)(2,1)}, u32[]{:S(2)}, u32[]{:S(2)}) collective-permute-start(bf16[128,2048]{1,0:T(8,128)(2,1)} %slice.277), channel_id=1, source_target_pairs={{0,1},{1,0},{2,3},{3,2},{4,5},{5,4},{6,7},{7,6},{8,9},{9,8},{10,11... | collective-permute-start | bytes 1572872 | tf_op jit(solution)/shard_map/ppermute | solution.py:340
  8.4 2.0 collective-permute-start.1
  12.2 5.0 %forward.1 = (bf16[8192,128]{1,0:T(8,128)(2,1)S(1)}, f32[128,512]{1,0:T(8,128)S(1)}) custom-call(bf16[128,8192]{1,0:T(8,128)(2,1)S(1)} %bitcast.87, bf16[8192,512]{1,0:T(8,128)(2,1)} %weights_ref.9), custom_call_target="tpu_custom_call" | custom-call | flops 1073741824 | bytes 12582912 | tf_op jit(solution)/shard_map/forward/pallas_call | solution.py:34
  17.2 1.3 copy-done.1
  18.5 0.9 copy.31
  20.2 1.1 maximum_select_fusion.target_ref
  21.3 1.0 broadcast_select_fusion.count_ref
  22.3 9.6 %collective-permute-done.3.part_ref = bf16[128,2048]{1,0:T(8,128)(2,1)} collective-permute-done((bf16[128,2048]{1,0:T(8,128)(2,1)}, bf16[128,2048]{1,0:T(8,128)(2,1)}, u32[]{:S(2)}, u32[]{:S(2)}) %collective-permute-start.3) | collective-permute-done | bytes 524320 | tf_op jit(solution)/shard_map/ppermute | solution.py:340
  31.9 2.2 %arrive.4 = (bf16[128,8192]{1,0:T(8,128)(2,1)S(1)}, bf16[8192,128]{1,0:T(8,128)(2,1)S(1)}, f32[128,512]{1,0:T(8,128)S(1)}) custom-call(bf16[128,2048]{1,0:T(8,128)(2,1)} %collective-permute-done.3.part_ref, bf16[8192,512]{1,0:T(8,128)(2,1)} %weights_ref.9), custom_call_target="tpu_custom_call" | custom-call | flops 268435456 | bytes 3670016 | tf_op jit(solution)/shard_map/arrive/pallas_call | solution.py:76
  34.1 2.2 %arrive.5 = (bf16[128,8192]{1,0:T(8,128)(2,1)S(1)}, bf16[8192,128]{1,0:T(8,128)(2,1)S(1)}, f32[128,512]{1,0:T(8,128)S(1)}) custom-call(bf16[128,2048]{1,0:T(8,128)(2,1)} %collective-permute-done.2.part_ref, bf16[8192,512]{1,0:T(8,128)(2,1)} %weights_ref.9, ...), custom_call_target="tpu_custom_call", output_to_operand_aliasing={{0}: (2, {}), {1}: (3, {}), {2}: (4, {})} | custom-call | flops 268435456 | bytes 3670016 | tf_op jit(solution)/shard_map/arrive/pallas_call | solution.py:76
  36.3 6.7 %collective-permute-done.1.part_ref = bf16[128,2048]{1,0:T(8,128)(2,1)S(1)} collective-permute-done((bf16[128,2048]{1,0:T(8,128)(2,1)}, bf16[128,2048]{1,0:T(8,128)(2,1)S(1)}, u32[]{:S(2)}, u32[]{:S(2)}) %collective-permute-start.1) | collective-permute-done | bytes 524320 | tf_op jit(solution)/shard_map/ppermute | solution.py:340
  43.0 2.0 arrive.6
  45.0 8.4 %collective-permute-done.part_ref = bf16[128,2048]{1,0:T(8,128)(2,1)S(1)} collective-permute-done((bf16[128,2048]{1,0:T(8,128)(2,1)}, bf16[128,2048]{1,0:T(8,128)(2,1)S(1)}, u32[]{:S(2)}, u32[]{:S(2)}) %collective-permute-start) | collective-permute-done | bytes 524320 | tf_op jit(solution)/shard_map/ppermute | solution.py:340
  53.4 2.2 arrive.7
  55.6 18.4 %inner.2 = (f32[8,512,128]{2,1,0:T(8,128)S(1)}, f32[8,512,128]{2,1,0:T(8,128)S(1)}, f32[8,512,128]{2,1,0:T(8,128)S(1)}, f32[8,512,128]{2,1,0:T(8,128)S(1)}) custom-call(s32[1]{0:T(128)} %bitcast.mine_ref.place_ref, bf16[128,8192]{1,0:T(8,128)(2,1)S(1)} %bitcast.88, bf16[128,8192]{1,0:T(8,128)(2,1)S(1)} %get-tuple-element.69.high_ref, ...), custom_call_target="tpu_custom_call" | custom-call | flops 3221225472 | bytes 41943040 | tf_op jit(solution)/shard_map/inner/pallas_call | solution.py:225
  75.0 1.9 collective-permute-done.5
  77.0 1.1 add_convert_fusion.2
  78.6 1.8 collective-permute-start.6
  80.4 18.6 %inner.3 = (f32[8,512,128]{2,1,0:T(8,128)S(1)}, f32[8,512,128]{2,1,0:T(8,128)S(1)}, f32[8,512,128]{2,1,0:T(8,128)S(1)}, f32[8,512,128]{2,1,0:T(8,128)S(1)}) custom-call(s32[1]{0:T(128)} %bitcast.mine_ref.place_ref, bf16[128,8192]{1,0:T(8,128)(2,1)S(1)} %bitcast.89, bf16[128,8192]{1,0:T(8,128)(2,1)S(1)} %get-tuple-element.69.high_ref, ...), custom_call_target="tpu_custom_call" | custom-call | flops 3221225472 | bytes 41943040 | tf_op jit(solution)/shard_map/inner/pallas_call | solution.py:225
  99.0 1.3 convert_element_type.218
  102.7 1.4 fusion.16
  104.5 1.8 collective-permute-start.21
  106.7 1.3 add_convert_fusion
  108.0 1.2 add_convert_fusion.1
  109.2 9.0 %collective-permute-done.22 = f16[4,512,128]{2,1,0:T(8,128)(2,1)S(1)} collective-permute-done((f16[4,512,128]{2,1,0:T(8,128)(2,1)}, f16[4,512,128]{2,1,0:T(8,128)(2,1)S(1)}, u32[]{:S(2)}, u32[]{:S(2)}) %collective-permute-start.22) | collective-permute-done | bytes 524320 | tf_op jit(solution)/shard_map/ppermute | solution.py:320
  118.3 1.1 add_convert_fusion.8
  119.3 2.7 %collective-permute-start.28 = (f16[1,512,128]{2,1,0:T(8,128)(2,1)S(1)}, f16[1,512,128]{2,1,0:T(8,128)(2,1)S(1)}, u32[]{:S(2)}, u32[]{:S(2)}) collective-permute-start(f16[1,512,128]{2,1,0:T(8,128)(2,1)S(1)} %add_convert_fusion.8), channel_id=1, source_target_pairs={{0,16},{2,18},{4,20},{6,22},{8,24},{10,26},{12,28},{14,30},{16,0},... | collective-permute-start | bytes 393224 | tf_op jit(solution)/shard_map/ppermute | solution.py:320
  122.1 1.6 collective-permute-start.23
  123.7 1.1 constant_dynamic-slice_fusion
  125.5 2.1 collective-permute-done.28
  127.6 1.2 bitcast_add_fusion.1
  128.7 1.8 collective-permute-start.29
  130.5 1.8 collective-permute-done.23
  133.1 8.3 %collective-permute-done.29 = bf16[1,512,128]{2,1,0:T(8,128)(2,1)S(1)} collective-permute-done((bf16[1,512,128]{2,1,0:T(8,128)(2,1)S(1)}, bf16[1,512,128]{2,1,0:T(8,128)(2,1)S(1)}, u32[]{:S(2)}, u32[]{:S(2)}) %collective-permute-start.29) | collective-permute-done | bytes 131104 | tf_op jit(solution)/shard_map/ppermute | solution.py:320
  141.4 1.3 collective-permute-done.24
  143.4 1.1 add_convert_fusion.5
  144.5 2.5 %collective-permute-start.16 = (f16[2,512,128]{2,1,0:T(8,128)(2,1)S(1)}, f16[2,512,128]{2,1,0:T(8,128)(2,1)S(1)}, u32[]{:S(2)}, u32[]{:S(2)}) collective-permute-start(f16[2,512,128]{2,1,0:T(8,128)(2,1)S(1)} %add_convert_fusion.5), channel_id=1, source_target_pairs={{0,8},{2,10},{4,12},{6,14},{8,0},{10,2},{12,4},{14,6},{16,24},{18,... | collective-permute-start | bytes 786440 | tf_op jit(solution)/shard_map/ppermute | solution.py:320
  147.0 1.6 collective-permute-done.8
  148.6 1.1 add_convert_fusion.6
  150.7 2.6 %collective-permute-start.26 = (bf16[2,512,128]{2,1,0:T(8,128)(2,1)S(1)}, bf16[2,512,128]{2,1,0:T(8,128)(2,1)S(1)}, u32[]{:S(2)}, u32[]{:S(2)}) collective-permute-start(bf16[2,512,128]{2,1,0:T(8,128)(2,1)S(1)} %pad_maximum_fusion.7), channel_id=1, source_target_pairs={{0,8},{2,10},{4,12},{6,14},{8,0},{10,2},{12,4},{14,6},{16,24},{18,... | collective-permute-start | bytes 786440 | tf_op jit(solution)/shard_map/ppermute | solution.py:320
  153.9 4.9 %collective-permute-done.16 = f16[2,512,128]{2,1,0:T(8,128)(2,1)S(1)} collective-permute-done((f16[2,512,128]{2,1,0:T(8,128)(2,1)S(1)}, f16[2,512,128]{2,1,0:T(8,128)(2,1)S(1)}, u32[]{:S(2)}, u32[]{:S(2)}) %collective-permute-start.16) | collective-permute-done | bytes 262176 | tf_op jit(solution)/shard_map/ppermute | solution.py:320
  158.9 1.0 add_convert_fusion.10
  160.0 7.3 %collective-permute-done.9 = f16[2,512,128]{2,1,0:T(8,128)(2,1)S(1)} collective-permute-done((f16[2,512,128]{2,1,0:T(8,128)(2,1)S(1)}, f16[2,512,128]{2,1,0:T(8,128)(2,1)S(1)}, u32[]{:S(2)}, u32[]{:S(2)}) %collective-permute-start.9) | collective-permute-done | bytes 262176 | tf_op jit(solution)/shard_map/ppermute | solution.py:320
  167.3 3.5 %collective-permute-done.26 = bf16[2,512,128]{2,1,0:T(8,128)(2,1)S(1)} collective-permute-done((bf16[2,512,128]{2,1,0:T(8,128)(2,1)S(1)}, bf16[2,512,128]{2,1,0:T(8,128)(2,1)S(1)}, u32[]{:S(2)}, u32[]{:S(2)}) %collective-permute-start.26) | collective-permute-done | bytes 262176 | tf_op jit(solution)/shard_map/ppermute | solution.py:320
  171.4 1.1 bitcast_add_fusion.5
  173.1 1.0 add_convert_fusion.11
  174.0 2.5 %collective-permute-start.10 = (f16[1,512,128]{2,1,0:T(8,128)(2,1)S(1)}, f16[1,512,128]{2,1,0:T(8,128)(2,1)S(1)}, u32[]{:S(2)}, u32[]{:S(2)}) collective-permute-start(f16[1,512,128]{2,1,0:T(8,128)(2,1)S(1)} %add_convert_fusion.11), channel_id=1, source_target_pairs={{0,16},{2,18},{4,20},{6,22},{8,24},{10,26},{12,28},{14,30},{16,0},... | collective-permute-start | bytes 393224 | tf_op jit(solution)/shard_map/ppermute | solution.py:320
  176.5 7.2 %collective-permute-done.18 = bf16[1,512,128]{2,1,0:T(8,128)(2,1)S(1)} collective-permute-done((bf16[1,512,128]{2,1,0:T(8,128)(2,1)S(1)}, bf16[1,512,128]{2,1,0:T(8,128)(2,1)S(1)}, u32[]{:S(2)}, u32[]{:S(2)}) %collective-permute-start.18) | collective-permute-done | bytes 131104 | tf_op jit(solution)/shard_map/ppermute | solution.py:320
  183.8 1.4 collective-permute-done.10
  185.2 1.1 bitcast_add_fusion.7
  186.3 3.9 %collective-permute-done.19 = bf16[2,512,128]{2,1,0:T(8,128)(2,1)S(1)} collective-permute-done((bf16[2,512,128]{2,1,0:T(8,128)(2,1)S(1)}, bf16[2,512,128]{2,1,0:T(8,128)(2,1)S(1)}, u32[]{:S(2)}, u32[]{:S(2)}) %collective-permute-start.19) | collective-permute-done | bytes 262176 | tf_op jit(solution)/shard_map/ppermute | solution.py:320
  190.8 1.6 collective-permute-start.20
  192.4 1.4 assemble.4.refs_4_
  193.9 3.0 %collective-permute-done.11 = bf16[1,512,128]{2,1,0:T(8,128)(2,1)S(1)} collective-permute-done((bf16[1,512,128]{2,1,0:T(8,128)(2,1)S(1)}, bf16[1,512,128]{2,1,0:T(8,128)(2,1)S(1)}, u32[]{:S(2)}, u32[]{:S(2)}) %collective-permute-start.11) | collective-permute-done | bytes 131104 | tf_op jit(solution)/shard_map/ppermute | solution.py:320
  197.1 6.3 %collective-permute-done.12 = bf16[2,512,128]{2,1,0:T(8,128)(2,1)S(1)} collective-permute-done((bf16[2,512,128]{2,1,0:T(8,128)(2,1)S(1)}, bf16[2,512,128]{2,1,0:T(8,128)(2,1)S(1)}, u32[]{:S(2)}, u32[]{:S(2)}) %collective-permute-start.12) | collective-permute-done | bytes 262176 | tf_op jit(solution)/shard_map/ppermute | solution.py:320
  203.4 1.2 collective-permute-start.13
  204.6 1.4 assemble.5.refs_4_
  206.7 8.1 %collective-permute-done.13.refs_1_ = bf16[4,512,128]{2,1,0:T(8,128)(2,1)S(1)} collective-permute-done((bf16[4,512,128]{2,1,0:T(8,128)(2,1)S(1)}, bf16[4,512,128]{2,1,0:T(8,128)(2,1)S(1)}, u32[]{:S(2)}, u32[]{:S(2)}) %collective-permute-start.13) | collective-permute-done | bytes 524320 | tf_op jit(solution)/shard_map/ppermute | solution.py:320
  214.8 1.4 assemble.6.refs_4_
  216.3 1.0 pad_maximum_fusion
  217.3 0.9 collective-permute-done.39.refs_3_
  218.2 1.4 assemble.7
  (105 shorter events, 15.0 us)
Async XLA Ops:
  0.6 7.0 %copy-start = (bf16[1,128,8192]{2,1,0:T(8,128)(2,1)S(1)}, bf16[1,128,8192]{2,1,0:T(8,128)(2,1)}, u32[]{:S(2)}) copy-start(bf16[1,128,8192]{2,1,0:T(8,128)(2,1)} %param.11) | copy-start | bytes 6291460
  0.6 10.7 %copy-start.16 = (s32[1,2,512]{2,1,0:T(2,128)S(1)}, s32[1,2,512]{2,1,0:T(2,128)}, u32[]{:S(2)}) copy-start(s32[1,2,512]{2,1,0:T(2,128)} %param.13) | copy-start | bytes 12292
  0.7 10.9 %copy-start.13 = (bf16[1,256,512]{2,1,0:T(8,128)(2,1)S(1)}, bf16[1,256,512]{2,1,0:T(8,128)(2,1)}, u32[]{:S(2)}) copy-start(bf16[1,256,512]{2,1,0:T(8,128)(2,1)} %param.12) | copy-start | bytes 786436
  4.6 29.5 %collective-permute-start.2 = (bf16[128,2048]{1,0:T(8,128)(2,1)}, bf16[128,2048]{1,0:T(8,128)(2,1)}, u32[]{:S(2)}, u32[]{:S(2)}) collective-permute-start(bf16[128,2048]{1,0:T(8,128)(2,1)} %slice.277), channel_id=1, source_target_pairs={{0,1},{1,0},{2,3},{3,2},{4,5},{5,4},{6,7},{7,6},{8,9},{9,8},{10,11... | collective-permute-start | bytes 1572872 | tf_op jit(solution)/shard_map/ppermute | solution.py:340
  7.6 24.3 %collective-permute-start.3 = (bf16[128,2048]{1,0:T(8,128)(2,1)}, bf16[128,2048]{1,0:T(8,128)(2,1)}, u32[]{:S(2)}, u32[]{:S(2)}) collective-permute-start(bf16[128,2048]{1,0:T(8,128)(2,1)} %slice.344), channel_id=1, source_target_pairs={{0,1},{1,0},{2,3},{3,2},{4,5},{5,4},{6,7},{7,6},{8,9},{9,8},{10,11... | collective-permute-start | bytes 1572872 | tf_op jit(solution)/shard_map/ppermute | solution.py:340
  8.4 34.6 %collective-permute-start.1 = (bf16[128,2048]{1,0:T(8,128)(2,1)}, bf16[128,2048]{1,0:T(8,128)(2,1)S(1)}, u32[]{:S(2)}, u32[]{:S(2)}) collective-permute-start(bf16[128,2048]{1,0:T(8,128)(2,1)} %slice.278), channel_id=1, source_target_pairs={{0,1},{1,0},{2,3},{3,2},{4,5},{5,4},{6,7},{7,6},{8,9},{9,8},{10,11... | collective-permute-start | bytes 1572872 | tf_op jit(solution)/shard_map/ppermute | solution.py:340
  11.3 42.1 %collective-permute-start = (bf16[128,2048]{1,0:T(8,128)(2,1)}, bf16[128,2048]{1,0:T(8,128)(2,1)S(1)}, u32[]{:S(2)}, u32[]{:S(2)}) collective-permute-start(bf16[128,2048]{1,0:T(8,128)(2,1)} %slice.279), channel_id=1, source_target_pairs={{0,1},{1,0},{2,3},{3,2},{4,5},{5,4},{6,7},{7,6},{8,9},{9,8},{10,11... | collective-permute-start | bytes 1572872 | tf_op jit(solution)/shard_map/ppermute | solution.py:340
  17.2 1.3 copy-start.1
  53.4 2.2 %copy-start.2 = (bf16[8192,128]{1,0:T(8,128)(2,1)S(1)}, bf16[8192,128]{1,0:T(8,128)(2,1)}, u32[]{:S(2)}) copy-start(bf16[8192,128]{1,0:T(8,128)(2,1)} %copy-done.1) | copy-start | bytes 6291460
  74.1 2.9 %copy-start.7 = (f32[8,512,128]{2,1,0:T(8,128)}, f32[8,512,128]{2,1,0:T(8,128)S(1)}, u32[]{:S(2)}) copy-start(f32[8,512,128]{2,1,0:T(8,128)S(1)} %get-tuple-element.76) | copy-start | bytes 6291460
  74.1 27.3 %copy-start.9 = (f32[8,512,128]{2,1,0:T(8,128)}, f32[8,512,128]{2,1,0:T(8,128)S(1)}, u32[]{:S(2)}) copy-start(f32[8,512,128]{2,1,0:T(8,128)S(1)} %get-tuple-element.74) | copy-start | bytes 6291460
  74.2 2.7 %collective-permute-start.5 = (f16[8,512,128]{2,1,0:T(8,128)(2,1)S(1)}, f16[8,512,128]{2,1,0:T(8,128)(2,1)S(1)}, u32[]{:S(2)}, u32[]{:S(2)}) collective-permute-start(f16[8,512,128]{2,1,0:T(8,128)(2,1)S(1)} %convert_element_type.215), channel_id=1, source_target_pairs={{0,2},{2,0},{4,6},{6,4},{8,10},{10,8},{12,14},{14,12},{16,18},{18,... | collective-permute-start | bytes 3145736 | tf_op jit(solution)/shard_map/ppermute | solution.py:320
  74.5 4.0 %collective-permute-start.4 = (f16[8,512,128]{2,1,0:T(8,128)(2,1)S(1)}, f16[8,512,128]{2,1,0:T(8,128)(2,1)S(1)}, u32[]{:S(2)}, u32[]{:S(2)}) collective-permute-start(f16[8,512,128]{2,1,0:T(8,128)(2,1)S(1)} %convert_element_type.212), channel_id=1, source_target_pairs={{0,2},{2,0},{4,6},{6,4},{8,10},{10,8},{12,14},{14,12},{16,18},{18,... | collective-permute-start | bytes 3145736 | tf_op jit(solution)/shard_map/ppermute | solution.py:320
  77.0 1.6 copy-start.10
  78.5 22.9 %copy-start.12 = (f16[8,512,128]{2,1,0:T(8,128)(2,1)}, f16[8,512,128]{2,1,0:T(8,128)(2,1)S(1)}, u32[]{:S(2)}) copy-start(f16[8,512,128]{2,1,0:T(8,128)(2,1)S(1)} %collective-permute-done.4) | copy-start | bytes 3145732
  78.6 22.8 %collective-permute-start.6 = (f16[4,512,128]{2,1,0:T(8,128)(2,1)S(1)}, f16[4,512,128]{2,1,0:T(8,128)(2,1)S(1)}, u32[]{:S(2)}, u32[]{:S(2)}) collective-permute-start(f16[4,512,128]{2,1,0:T(8,128)(2,1)S(1)} %add_convert_fusion.3), channel_id=1, source_target_pairs={{0,4},{2,6},{4,0},{6,2},{8,12},{10,14},{12,8},{14,10},{16,20},{18,... | collective-permute-start | bytes 1572872 | tf_op jit(solution)/shard_map/ppermute | solution.py:320
  99.0 1.6 copy-start.3
  99.0 2.4 %copy-start.5 = (f32[8,512,128]{2,1,0:T(8,128)}, f32[8,512,128]{2,1,0:T(8,128)S(1)}, u32[]{:S(2)}) copy-start(f32[8,512,128]{2,1,0:T(8,128)S(1)} %get-tuple-element.86) | copy-start | bytes 6291460
  101.4 0.8 copy-start.14
  101.4 5.3 %copy-start.6 = (f32[8,512,128]{2,1,0:T(8,128)S(1)}, f32[8,512,128]{2,1,0:T(8,128)}, u32[]{:S(2)}) copy-start(f32[8,512,128]{2,1,0:T(8,128)} %copy-done.5) | copy-start | bytes 6291460
  102.2 4.5 %collective-permute-start.14 = (f16[8,512,128]{2,1,0:T(8,128)(2,1)}, f16[8,512,128]{2,1,0:T(8,128)(2,1)}, u32[]{:S(2)}, u32[]{:S(2)}) collective-permute-start(f16[8,512,128]{2,1,0:T(8,128)(2,1)} %convert_element_type.218), channel_id=1, source_target_pairs={{0,2},{2,0},{4,6},{6,4},{8,10},{10,8},{12,14},{14,12},{16,18},{18,... | collective-permute-start | bytes 3145736 | tf_op jit(solution)/shard_map/ppermute | solution.py:320
  102.2 5.8 %collective-permute-start.7 = (f16[8,512,128]{2,1,0:T(8,128)(2,1)S(1)}, f16[8,512,128]{2,1,0:T(8,128)(2,1)}, u32[]{:S(2)}, u32[]{:S(2)}) collective-permute-start(f16[8,512,128]{2,1,0:T(8,128)(2,1)S(1)} %convert_element_type.219), channel_id=1, source_target_pairs={{0,2},{2,0},{4,6},{6,4},{8,10},{10,8},{12,14},{14,12},{16,18},{18,... | collective-permute-start | bytes 3145736 | tf_op jit(solution)/shard_map/ppermute | solution.py:320
  102.7 5.3 %copy-start.4 = (f32[8,512,128]{2,1,0:T(8,128)S(1)}, f32[8,512,128]{2,1,0:T(8,128)}, u32[]{:S(2)}) copy-start(f32[8,512,128]{2,1,0:T(8,128)} %copy-done.3) | copy-start | bytes 6291460
  104.2 14.1 %collective-permute-start.22 = (f16[4,512,128]{2,1,0:T(8,128)(2,1)}, f16[4,512,128]{2,1,0:T(8,128)(2,1)S(1)}, u32[]{:S(2)}, u32[]{:S(2)}) collective-permute-start(f16[4,512,128]{2,1,0:T(8,128)(2,1)} %add_convert_fusion.2), channel_id=1, source_target_pairs={{0,4},{2,6},{4,0},{6,2},{8,12},{10,14},{12,8},{14,10},{16,20},{18,... | collective-permute-start | bytes 1572872 | tf_op jit(solution)/shard_map/ppermute | solution.py:320
  104.5 13.7 %collective-permute-start.21 = (f16[2,512,128]{2,1,0:T(8,128)(2,1)S(1)}, f16[2,512,128]{2,1,0:T(8,128)(2,1)S(1)}, u32[]{:S(2)}, u32[]{:S(2)}) collective-permute-start(f16[2,512,128]{2,1,0:T(8,128)(2,1)S(1)} %add_convert_fusion.7), channel_id=1, source_target_pairs={{0,8},{2,10},{4,12},{6,14},{8,0},{10,2},{12,4},{14,6},{16,24},{18,... | collective-permute-start | bytes 786440 | tf_op jit(solution)/shard_map/ppermute | solution.py:320
  106.7 11.6 %copy-start.15 = (f16[4,512,128]{2,1,0:T(8,128)(2,1)S(1)}, f16[4,512,128]{2,1,0:T(8,128)(2,1)}, u32[]{:S(2)}) copy-start(f16[4,512,128]{2,1,0:T(8,128)(2,1)} %copy-done.14) | copy-start | bytes 1572868
  106.7 15.3 %copy-start.8 = (f32[8,512,128]{2,1,0:T(8,128)S(1)}, f32[8,512,128]{2,1,0:T(8,128)}, u32[]{:S(2)}) copy-start(f32[8,512,128]{2,1,0:T(8,128)} %copy-done.7) | copy-start | bytes 6291460
  106.7 15.3 %copy-start.11 = (f16[8,512,128]{2,1,0:T(8,128)(2,1)S(1)}, f16[8,512,128]{2,1,0:T(8,128)(2,1)}, u32[]{:S(2)}) copy-start(f16[8,512,128]{2,1,0:T(8,128)(2,1)} %copy-done.10) | copy-start | bytes 3145732
  119.3 8.2 %collective-permute-start.28 = (f16[1,512,128]{2,1,0:T(8,128)(2,1)S(1)}, f16[1,512,128]{2,1,0:T(8,128)(2,1)S(1)}, u32[]{:S(2)}, u32[]{:S(2)}) collective-permute-start(f16[1,512,128]{2,1,0:T(8,128)(2,1)S(1)} %add_convert_fusion.8), channel_id=1, source_target_pairs={{0,16},{2,18},{4,20},{6,22},{8,24},{10,26},{12,28},{14,30},{16,0},... | collective-permute-start | bytes 393224 | tf_op jit(solution)/shard_map/ppermute | solution.py:320
  122.1 10.2 %collective-permute-start.23 = (f16[2,512,128]{2,1,0:T(8,128)(2,1)S(1)}, f16[2,512,128]{2,1,0:T(8,128)(2,1)S(1)}, u32[]{:S(2)}, u32[]{:S(2)}) collective-permute-start(f16[2,512,128]{2,1,0:T(8,128)(2,1)S(1)} %add_convert_fusion.4), channel_id=1, source_target_pairs={{0,8},{2,10},{4,12},{6,14},{8,0},{10,2},{12,4},{14,6},{16,24},{18,... | collective-permute-start | bytes 786440 | tf_op jit(solution)/shard_map/ppermute | solution.py:320
  124.9 18.5 %collective-permute-start.15 = (f16[4,512,128]{2,1,0:T(8,128)(2,1)S(1)}, f16[4,512,128]{2,1,0:T(8,128)(2,1)S(1)}, u32[]{:S(2)}, u32[]{:S(2)}) collective-permute-start(f16[4,512,128]{2,1,0:T(8,128)(2,1)S(1)} %add_convert_fusion), channel_id=1, source_target_pairs={{0,4},{2,6},{4,0},{6,2},{8,12},{10,14},{12,8},{14,10},{16,20},{18,... | collective-permute-start | bytes 1572872 | tf_op jit(solution)/shard_map/ppermute | solution.py:320
  128.7 12.6 %collective-permute-start.29 = (bf16[1,512,128]{2,1,0:T(8,128)(2,1)S(1)}, bf16[1,512,128]{2,1,0:T(8,128)(2,1)S(1)}, u32[]{:S(2)}, u32[]{:S(2)}) collective-permute-start(bf16[1,512,128]{2,1,0:T(8,128)(2,1)S(1)} %get-tuple-element.107), channel_id=1, source_target_pairs={{0,16},{2,18},{4,20},{6,22},{8,24},{10,26},{12,28},{14,30},{16,0},... | collective-permute-start | bytes 393224 | tf_op jit(solution)/shard_map/ppermute | solution.py:320
  132.4 10.3 %collective-permute-start.24 = (f16[1,512,128]{2,1,0:T(8,128)(2,1)S(1)}, f16[1,512,128]{2,1,0:T(8,128)(2,1)S(1)}, u32[]{:S(2)}, u32[]{:S(2)}) collective-permute-start(f16[1,512,128]{2,1,0:T(8,128)(2,1)S(1)} %add_convert_fusion.9), channel_id=1, source_target_pairs={{0,16},{2,18},{4,20},{6,22},{8,24},{10,26},{12,28},{14,30},{16,0},... | collective-permute-start | bytes 393224 | tf_op jit(solution)/shard_map/ppermute | solution.py:320
  132.5 16.1 %collective-permute-start.8 = (f16[4,512,128]{2,1,0:T(8,128)(2,1)S(1)}, f16[4,512,128]{2,1,0:T(8,128)(2,1)S(1)}, u32[]{:S(2)}, u32[]{:S(2)}) collective-permute-start(f16[4,512,128]{2,1,0:T(8,128)(2,1)S(1)} %add_convert_fusion.1), channel_id=1, source_target_pairs={{0,4},{2,6},{4,0},{6,2},{8,12},{10,14},{12,8},{14,10},{16,20},{18,... | collective-permute-start | bytes 1572872 | tf_op jit(solution)/shard_map/ppermute | solution.py:320
  141.4 11.9 %collective-permute-start.30 = (bf16[2,512,128]{2,1,0:T(8,128)(2,1)S(1)}, bf16[2,512,128]{2,1,0:T(8,128)(2,1)S(1)}, u32[]{:S(2)}, u32[]{:S(2)}) collective-permute-start(bf16[2,512,128]{2,1,0:T(8,128)(2,1)S(1)} %pad_maximum_fusion.8), channel_id=1, source_target_pairs={{0,8},{2,10},{4,12},{6,14},{8,0},{10,2},{12,4},{14,6},{16,24},{18,... | collective-permute-start | bytes 786440 | tf_op jit(solution)/shard_map/ppermute | solution.py:320
  142.9 7.8 %collective-permute-start.25 = (bf16[1,512,128]{2,1,0:T(8,128)(2,1)S(1)}, bf16[1,512,128]{2,1,0:T(8,128)(2,1)S(1)}, u32[]{:S(2)}, u32[]{:S(2)}) collective-permute-start(bf16[1,512,128]{2,1,0:T(8,128)(2,1)S(1)} %get-tuple-element.109), channel_id=1, source_target_pairs={{0,16},{2,18},{4,20},{6,22},{8,24},{10,26},{12,28},{14,30},{16,0},... | collective-permute-start | bytes 393224 | tf_op jit(solution)/shard_map/ppermute | solution.py:320
  144.5 14.4 %collective-permute-start.16 = (f16[2,512,128]{2,1,0:T(8,128)(2,1)S(1)}, f16[2,512,128]{2,1,0:T(8,128)(2,1)S(1)}, u32[]{:S(2)}, u32[]{:S(2)}) collective-permute-start(f16[2,512,128]{2,1,0:T(8,128)(2,1)S(1)} %add_convert_fusion.5), channel_id=1, source_target_pairs={{0,8},{2,10},{4,12},{6,14},{8,0},{10,2},{12,4},{14,6},{16,24},{18,... | collective-permute-start | bytes 786440 | tf_op jit(solution)/shard_map/ppermute | solution.py:320
  149.7 17.6 %collective-permute-start.9 = (f16[2,512,128]{2,1,0:T(8,128)(2,1)S(1)}, f16[2,512,128]{2,1,0:T(8,128)(2,1)S(1)}, u32[]{:S(2)}, u32[]{:S(2)}) collective-permute-start(f16[2,512,128]{2,1,0:T(8,128)(2,1)S(1)} %add_convert_fusion.6), channel_id=1, source_target_pairs={{0,8},{2,10},{4,12},{6,14},{8,0},{10,2},{12,4},{14,6},{16,24},{18,... | collective-permute-start | bytes 786440 | tf_op jit(solution)/shard_map/ppermute | solution.py:320
  150.7 20.0 %collective-permute-start.26 = (bf16[2,512,128]{2,1,0:T(8,128)(2,1)S(1)}, bf16[2,512,128]{2,1,0:T(8,128)(2,1)S(1)}, u32[]{:S(2)}, u32[]{:S(2)}) collective-permute-start(bf16[2,512,128]{2,1,0:T(8,128)(2,1)S(1)} %pad_maximum_fusion.7), channel_id=1, source_target_pairs={{0,8},{2,10},{4,12},{6,14},{8,0},{10,2},{12,4},{14,6},{16,24},{18,... | collective-permute-start | bytes 786440 | tf_op jit(solution)/shard_map/ppermute | solution.py:320
  153.3 19.7 %collective-permute-start.31 = (bf16[4,512,128]{2,1,0:T(8,128)(2,1)S(1)}, bf16[4,512,128]{2,1,0:T(8,128)(2,1)S(1)}, u32[]{:S(2)}, u32[]{:S(2)}) collective-permute-start(bf16[4,512,128]{2,1,0:T(8,128)(2,1)S(1)} %pad_maximum_fusion.4.refs_0_), channel_id=1, source_target_pairs={{0,4},{2,6},{4,0},{6,2},{8,12},{10,14},{12,8},{14,10},{16,20},{18,... | collective-permute-start | bytes 1572872 | tf_op jit(solution)/shard_map/ppermute | solution.py:320
  159.8 11.6 %collective-permute-start.17 = (f16[1,512,128]{2,1,0:T(8,128)(2,1)S(1)}, f16[1,512,128]{2,1,0:T(8,128)(2,1)S(1)}, u32[]{:S(2)}, u32[]{:S(2)}) collective-permute-start(f16[1,512,128]{2,1,0:T(8,128)(2,1)S(1)} %add_convert_fusion.10), channel_id=1, source_target_pairs={{0,16},{2,18},{4,20},{6,22},{8,24},{10,26},{12,28},{14,30},{16,0},... | collective-permute-start | bytes 393224 | tf_op jit(solution)/shard_map/ppermute | solution.py:320
  159.9 32.5 %collective-permute-start.32 = (bf16[4,512,128]{2,1,0:T(8,128)(2,1)S(1)}, bf16[4,512,128]{2,1,0:T(8,128)(2,1)S(1)}, u32[]{:S(2)}, u32[]{:S(2)}) collective-permute-start(bf16[4,512,128]{2,1,0:T(8,128)(2,1)S(1)} %pad_maximum_fusion.4.refs_0_), channel_id=1, source_target_pairs={{0,2},{2,0},{4,6},{6,4},{8,10},{10,8},{12,14},{14,12},{16,18},{18,... | collective-permute-start | bytes 1572872 | tf_op jit(solution)/shard_map/ppermute | solution.py:320
  170.8 20.0 %collective-permute-start.27 = (bf16[4,512,128]{2,1,0:T(8,128)(2,1)S(1)}, bf16[4,512,128]{2,1,0:T(8,128)(2,1)S(1)}, u32[]{:S(2)}, u32[]{:S(2)}) collective-permute-start(bf16[4,512,128]{2,1,0:T(8,128)(2,1)S(1)} %pad_maximum_fusion.3.refs_0_), channel_id=1, source_target_pairs={{0,4},{2,6},{4,0},{6,2},{8,12},{10,14},{12,8},{14,10},{16,20},{18,... | collective-permute-start | bytes 1572872 | tf_op jit(solution)/shard_map/ppermute | solution.py:320
  172.5 11.2 %collective-permute-start.18 = (bf16[1,512,128]{2,1,0:T(8,128)(2,1)S(1)}, bf16[1,512,128]{2,1,0:T(8,128)(2,1)S(1)}, u32[]{:S(2)}, u32[]{:S(2)}) collective-permute-start(bf16[1,512,128]{2,1,0:T(8,128)(2,1)S(1)} %get-tuple-element.111), channel_id=1, source_target_pairs={{0,16},{2,18},{4,20},{6,22},{8,24},{10,26},{12,28},{14,30},{16,0},... | collective-permute-start | bytes 393224 | tf_op jit(solution)/shard_map/ppermute | solution.py:320
  173.1 19.3 %collective-permute-start.33 = (bf16[4,512,128]{2,1,0:T(8,128)(2,1)S(1)}, bf16[4,512,128]{2,1,0:T(8,128)(2,1)S(1)}, u32[]{:S(2)}, u32[]{:S(2)}) collective-permute-start(bf16[4,512,128]{2,1,0:T(8,128)(2,1)S(1)} %collective-permute-done.31.refs_1_), channel_id=1, source_target_pairs={{0,2},{2,0},{4,6},{6,4},{8,10},{10,8},{12,14},{14,12},{16,18},{18,... | collective-permute-start | bytes 1572872 | tf_op jit(solution)/shard_map/ppermute | solution.py:320
  174.0 11.1 %collective-permute-start.10 = (f16[1,512,128]{2,1,0:T(8,128)(2,1)S(1)}, f16[1,512,128]{2,1,0:T(8,128)(2,1)S(1)}, u32[]{:S(2)}, u32[]{:S(2)}) collective-permute-start(f16[1,512,128]{2,1,0:T(8,128)(2,1)S(1)} %add_convert_fusion.11), channel_id=1, source_target_pairs={{0,16},{2,18},{4,20},{6,22},{8,24},{10,26},{12,28},{14,30},{16,0},... | collective-permute-start | bytes 393224 | tf_op jit(solution)/shard_map/ppermute | solution.py:320
  183.7 6.4 %collective-permute-start.19 = (bf16[2,512,128]{2,1,0:T(8,128)(2,1)S(1)}, bf16[2,512,128]{2,1,0:T(8,128)(2,1)S(1)}, u32[]{:S(2)}, u32[]{:S(2)}) collective-permute-start(bf16[2,512,128]{2,1,0:T(8,128)(2,1)S(1)} %pad_maximum_fusion.6), channel_id=1, source_target_pairs={{0,8},{2,10},{4,12},{6,14},{8,0},{10,2},{12,4},{14,6},{16,24},{18,... | collective-permute-start | bytes 786440 | tf_op jit(solution)/shard_map/ppermute | solution.py:320
  185.2 19.4 %collective-permute-start.34 = (bf16[4,512,128]{2,1,0:T(8,128)(2,1)S(1)}, bf16[4,512,128]{2,1,0:T(8,128)(2,1)S(1)}, u32[]{:S(2)}, u32[]{:S(2)}) collective-permute-start(bf16[4,512,128]{2,1,0:T(8,128)(2,1)S(1)} %pad_maximum_fusion.3.refs_0_), channel_id=1, source_target_pairs={{0,2},{2,0},{4,6},{6,4},{8,10},{10,8},{12,14},{14,12},{16,18},{18,... | collective-permute-start | bytes 1572872 | tf_op jit(solution)/shard_map/ppermute | solution.py:320
  190.2 6.7 %collective-permute-start.11 = (bf16[1,512,128]{2,1,0:T(8,128)(2,1)S(1)}, bf16[1,512,128]{2,1,0:T(8,128)(2,1)S(1)}, u32[]{:S(2)}, u32[]{:S(2)}) collective-permute-start(bf16[1,512,128]{2,1,0:T(8,128)(2,1)S(1)} %get-tuple-element.113), channel_id=1, source_target_pairs={{0,16},{2,18},{4,20},{6,22},{8,24},{10,26},{12,28},{14,30},{16,0},... | collective-permute-start | bytes 393224 | tf_op jit(solution)/shard_map/ppermute | solution.py:320
  190.8 13.8 %collective-permute-start.20 = (bf16[4,512,128]{2,1,0:T(8,128)(2,1)S(1)}, bf16[4,512,128]{2,1,0:T(8,128)(2,1)S(1)}, u32[]{:S(2)}, u32[]{:S(2)}) collective-permute-start(bf16[4,512,128]{2,1,0:T(8,128)(2,1)S(1)} %pad_maximum_fusion.2.refs_0_), channel_id=1, source_target_pairs={{0,4},{2,6},{4,0},{6,2},{8,12},{10,14},{12,8},{14,10},{16,20},{18,... | collective-permute-start | bytes 1572872 | tf_op jit(solution)/shard_map/ppermute | solution.py:320
  193.8 10.8 %collective-permute-start.35 = (bf16[4,512,128]{2,1,0:T(8,128)(2,1)S(1)}, bf16[4,512,128]{2,1,0:T(8,128)(2,1)S(1)}, u32[]{:S(2)}, u32[]{:S(2)}) collective-permute-start(bf16[4,512,128]{2,1,0:T(8,128)(2,1)S(1)} %collective-permute-done.27.refs_1_), channel_id=1, source_target_pairs={{0,2},{2,0},{4,6},{6,4},{8,10},{10,8},{12,14},{14,12},{16,18},{18,... | collective-permute-start | bytes 1572872 | tf_op jit(solution)/shard_map/ppermute | solution.py:320
  196.9 6.4 %collective-permute-start.12 = (bf16[2,512,128]{2,1,0:T(8,128)(2,1)S(1)}, bf16[2,512,128]{2,1,0:T(8,128)(2,1)S(1)}, u32[]{:S(2)}, u32[]{:S(2)}) collective-permute-start(bf16[2,512,128]{2,1,0:T(8,128)(2,1)S(1)} %pad_maximum_fusion.5), channel_id=1, source_target_pairs={{0,8},{2,10},{4,12},{6,14},{8,0},{10,2},{12,4},{14,6},{16,24},{18,... | collective-permute-start | bytes 786440 | tf_op jit(solution)/shard_map/ppermute | solution.py:320
  197.0 17.8 %collective-permute-start.36 = (bf16[4,512,128]{2,1,0:T(8,128)(2,1)S(1)}, bf16[4,512,128]{2,1,0:T(8,128)(2,1)S(1)}, u32[]{:S(2)}, u32[]{:S(2)}) collective-permute-start(bf16[4,512,128]{2,1,0:T(8,128)(2,1)S(1)} %pad_maximum_fusion.2.refs_0_), channel_id=1, source_target_pairs={{0,2},{2,0},{4,6},{6,4},{8,10},{10,8},{12,14},{14,12},{16,18},{18,... | collective-permute-start | bytes 1572872 | tf_op jit(solution)/shard_map/ppermute | solution.py:320
  203.4 11.4 %collective-permute-start.13 = (bf16[4,512,128]{2,1,0:T(8,128)(2,1)S(1)}, bf16[4,512,128]{2,1,0:T(8,128)(2,1)S(1)}, u32[]{:S(2)}, u32[]{:S(2)}) collective-permute-start(bf16[4,512,128]{2,1,0:T(8,128)(2,1)S(1)} %pad_maximum_fusion.1.refs_0_), channel_id=1, source_target_pairs={{0,4},{2,6},{4,0},{6,2},{8,12},{10,14},{12,8},{14,10},{16,20},{18,... | collective-permute-start | bytes 1572872 | tf_op jit(solution)/shard_map/ppermute | solution.py:320
  206.1 8.7 %collective-permute-start.37 = (bf16[4,512,128]{2,1,0:T(8,128)(2,1)S(1)}, bf16[4,512,128]{2,1,0:T(8,128)(2,1)S(1)}, u32[]{:S(2)}, u32[]{:S(2)}) collective-permute-start(bf16[4,512,128]{2,1,0:T(8,128)(2,1)S(1)} %collective-permute-done.20.refs_1_), channel_id=1, source_target_pairs={{0,2},{2,0},{4,6},{6,4},{8,10},{10,8},{12,14},{14,12},{16,18},{18,... | collective-permute-start | bytes 1572872 | tf_op jit(solution)/shard_map/ppermute | solution.py:320
  206.2 11.2 %collective-permute-start.38 = (bf16[4,512,128]{2,1,0:T(8,128)(2,1)S(1)}, bf16[4,512,128]{2,1,0:T(8,128)(2,1)S(1)}, u32[]{:S(2)}, u32[]{:S(2)}) collective-permute-start(bf16[4,512,128]{2,1,0:T(8,128)(2,1)S(1)} %pad_maximum_fusion.1.refs_0_), channel_id=1, source_target_pairs={{0,2},{2,0},{4,6},{6,4},{8,10},{10,8},{12,14},{14,12},{16,18},{18,... | collective-permute-start | bytes 1572872 | tf_op jit(solution)/shard_map/ppermute | solution.py:320
  216.2 2.0 collective-permute-start.39

commit v9 on v8

--- a/solution.py
+++ b/solution.py
@@ -13,7 +13,7 @@
 WIRE_SCALE = 64.0
 LANES = 128
 SLABS = 4
-PIECE = 32
+PIECE = 8192
 MIB = 1024 * 1024
 
 
@@ -131,7 +131,8 @@
     pairs, cores, rows, _ = start_ref.shape
     mine = mine_ref[0]
     core = lax.rem(mine, cores)
-    pieces = [pl.ds(begin, PIECE) for begin in range(0, rows, PIECE)]
+    height = PIECE // start_ref.shape[-1]
+    pieces = [pl.ds(begin, height) for begin in range(0, rows, height)]
     slots = [(slot, *divmod(slot, cores)) for slot in range(pairs * cores)]
     held = gradient_state.shape[0]
 
@@ -258,7 +259,7 @@
     )(mine, *banks, *turned, pinned(start), pinned(first), pinned(second), *products, target, count)
 
 
-def assemble_kernel(chunk, offsets, place_ref, *refs):
+def assemble_kernel(begin, offsets, place_ref, *refs):
     received = refs[: len(offsets)]
     out_ref, semaphore = refs[-2:]
     width = received[0].shape[-1]
@@ -269,7 +270,7 @@
             copies.append(
                 pltpu.make_async_copy(
                     ref.at[entry],
-                    out_ref.at[lax.bitwise_xor(mine, offset), :, pl.ds(chunk * width, width)],
+                    out_ref.at[lax.bitwise_xor(mine, offset), :, pl.ds(begin, width)],
                     semaphore.at[len(copies)],
                 )
             )
@@ -279,10 +280,10 @@
         copy.wait()
 
 
-def assemble(chunk, place, received, offsets, shape, before):
+def assemble(begin, place, received, offsets, shape, before):
     vmem = pl.BlockSpec(memory_space=pltpu.VMEM)
     return pl.pallas_call(
-        functools.partial(assemble_kernel, chunk, offsets),
+        functools.partial(assemble_kernel, begin, offsets),
         in_specs=[pl.BlockSpec(memory_space=pltpu.SMEM)]
         + [vmem] * len(received)
         + [pl.BlockSpec(memory_space=pl.ANY)] * len(before),
@@ -356,10 +357,19 @@
 
     turned = [array.reshape(cut[:4] + (half,)) for array in turned]
     place = mine.reshape(1).astype(jnp.int32)
-    my_start = lax.dynamic_slice_in_dim(global_weights, mine * rows, rows, 0)
+    if chunks == 4:
+        calls = [(2 * width, width), (0, 2 * width), (3 * width, width)]
+    else:
+        calls = [(begin, width) for begin in range(0, columns, width)]
+    begins = [begin + part for begin, wide in calls for part in range(0, wide, width)]
+
+    def start_rows(owner):
+        return lax.dynamic_slice_in_dim(global_weights, owner * rows, rows, 0)
+
+    pair_start = jnp.stack([start_rows(mine), start_rows(mine ^ spans[-1][1])])
     shares = [
-        tied(momentum[:, begin : begin + width], my_start[:, begin : begin + width])
-        for begin in range(0, columns, width)
+        tied(momentum[:, begin : begin + width], pair_start[:, :, begin : begin + width])
+        for begin in begins
     ]
 
     def parted(terms, span):
@@ -375,18 +385,24 @@
 
     def chain(chunk, keep, arrived):
         terms = [keep, arrived]
-        for span in spans:
+        for span in spans[:-1]:
             outgoing, terms = parted(terms, span)
             outgoing = yield outgoing
             arrived = yield sent(outgoing, span)
             terms = terms + arrived
-        total = sum(term.astype(F32) for term in terms)[0]
-        average = total * (1.0 / (WIRE_SCALE * reps))
-        moved = 0.9 * shares[chunk][0] + average
-        fresh = (shares[chunk][1].astype(F32) - 0.7 * (average + 0.9 * moved)).astype(BF16)
-        stack = yield fresh[None]
-        offsets = [0]
-        for span in spans[:0:-1]:
+        scale = WIRE_SCALE * reps
+        momentum_share, starts = shares[chunk]
+        total = sum(term.astype(F32) for term in terms)
+        pushed = (0.81 / 1.9 * scale) * momentum_share
+        rounded = jnp.stack([total[0] + pushed, total[1]]).astype(WIRE)
+        rounded = lax.optimization_barrier((yield rounded))
+        arrived, = yield sent([rounded], spans[-1])
+        moved = 0.9 * momentum_share + (total[0] + arrived[1].astype(F32)) * (1.0 / scale)
+        both = rounded.astype(F32) + arrived[::-1].astype(F32)
+        stack = (starts.astype(F32) - (1.33 / scale) * both).astype(BF16)
+        offsets = list(spans[-1])
+        stack = yield stack
+        for span in spans[-2:0:-1]:
             arrived = yield sent([stack], span)
             offsets = [offset ^ far for far in span for offset in offsets]
             stack = yield jnp.concatenate([stack] + arrived)
@@ -406,37 +422,37 @@
             formed[chunk] = running[chunk].send(arrived[chunk])
 
     token = place
-    wide = min(columns, 2 * LANES)
-    for call in range(columns // wide):
+    fresh = range(0)
+    for begin, wide in calls:
         changes = inner(
-            call, wide, width, token, banks, turned, start, first, second, products, target, count, tokens
+            begin // wide, wide, width, token, banks, turned, start, first, second, products, target, count, tokens
         )
-        fresh = range(call * (wide // width), (call + 1) * (wide // width))
         sends = [send.astype(WIRE) for send in changes[::2]]
-        if call:
-            move_on([0])
-            sends, _ = tied(sends, formed[0])
+        if fresh:
+            ready = range(fresh[0] + 1)
+            move_on(ready)
+            sends, _ = tied(sends, [formed[chunk] for chunk in ready])
+        fresh = range(fresh.stop, fresh.stop + wide // width)
         for chunk, send, keep in zip(fresh, sends, changes[1::2]):
             running[chunk] = chain(chunk, keep, swapped(send, 1))
             formed[chunk] = next(running[chunk])
-        if fresh[-1] + 1 < chunks:
+        if fresh.stop < chunks:
             formed, token = tied(formed, token)
     move_on(range(fresh[0]), behind=fresh)
     for chunk in range(chunks):
         while chunk not in finished:
             move_on([chunk])
 
-    new_momentum = []
     for chunk in range(chunks):
-        moved, stack, across, offsets = finished[chunk]
-        new_momentum.append(moved)
+        _, stack, across, offsets = finished[chunk]
         offsets = [[offset ^ low for offset in offsets] for low in (0, 2, 1, 3)]
         if result:
             across, *result = tied(across, result[0])
         received = [stack, across, swapped(stack, 1), swapped(across, 1)]
         result = (
-            assemble(chunk, place, received, offsets, (reps, rows, columns), result),
+            assemble(begins[chunk], place, received, offsets, (reps, rows, columns), result),
         )
+    new_momentum = [finished[chunk][0] for chunk in sorted(range(chunks), key=begins.__getitem__)]
 
     return result[0].reshape(depth, columns), jnp.concatenate(new_momentum, axis=1)
 

time: 220 us -> 219 us (level)
  waiting for transfers between devices: 98.2 us -> 92.4 us
  Pallas kernels: 56.4 us -> 62 us
  other arithmetic: 18 us -> 14.6 us
  starting transfers between devices: 32.4 us -> 34.8 us
    ppermute x36 -> x32, waiting for transfers between devices: 73.6 us -> 65.6 us  [swapped(): return lax.ppermute(array, 'rep', pairs)]
    pallas_call x2 -> x3, Pallas kernels: 37 us -> 42.5 us  [inner(): pl.pallas_call(functools.partial(inner_kernel, float(tokens)), grid_spec=...]
    convert_element_type x12 -> x8, other arithmetic: 9.18 us -> 5.17 us  [parted(): sum((term.astype(F32) for term in part)).astype(WIRE)]
    ppermute x36 -> x32, starting transfers between devices: 27.3 us -> 29.8 us  [swapped(): return lax.ppermute(array, 'rep', pairs)]
    unnamed x34 -> x40, local copies, waits for them, and re-layouts: 2.98 us -> 5.35 us
    ppermute x4, waiting for transfers between devices: 24.6 us -> 26.9 us  [per_device(): parts.append(lax.ppermute(part, 'fsdp', [(0, 1), (1, 0)]))]
  transfers between devices with their start and end apart: 40 -> 36, of which waited for: 23 -> 18; matrix products, arithmetic and copies ran while one was open for 11% -> 7% of each run, Pallas kernels for 16% -> 21%
where the time goes in v9:
time: 219 us
  waiting for transfers between devices  92.4 us (42%)
  Pallas kernels  62 us (28%)
  starting transfers between devices  34.8 us (16%)
  other arithmetic  14.6 us (7%)
  local copies, waits for them, and re-layouts  13.4 us (6%)
    ppermute x32, waiting for transfers between devices, swapped(): return lax.ppermute(array, 'rep', pairs)  65.6 us
    pallas_call x3, Pallas kernels, inner(): pl.pallas_call(functools.partial(inner_kernel, float(tokens)), grid_spec=...  42.5 us
    ppermute x32, starting transfers between devices, swapped(): return lax.ppermute(array, 'rep', pairs)  29.8 us
    ppermute x4, waiting for transfers between devices, per_device(): parts.append(lax.ppermute(part, 'fsdp', [(0, 1), (1, 0)]))  26.9 us
    pallas_call x4, Pallas kernels, arrive(): pl.pallas_call(functools.partial(arrive_kernel, piece), grid=(1,), in_spe...  8.81 us
    pallas_call x4, Pallas kernels, assemble(): pl.pallas_call(functools.partial(assemble_kernel, begin, offsets), in_spe...  5.76 us
    unnamed x40, local copies, waits for them, and re-layouts  5.35 us
    convert_element_type x8, other arithmetic, parted(): sum((term.astype(F32) for term in part)).astype(WIRE)  5.17 us
  transfers between devices with their start and end apart: 36, of which 18 were waited for; matrix products, arithmetic and copies ran while one was open for 7% of the time, Pallas kernels for 21%

profile of v9, /device:TPU:0, one launch (start us, length us, event | category | flops | bytes accessed | tf_op | source)
XLA Modules:
  0.0 218.6 jit_solution(12681908650342889741)
XLA Ops:
  0.7 1.2 slice.286
  1.9 1.9 slice.225
  3.8 3.0 %collective-permute-start.2 = (bf16[128,2048]{1,0:T(8,128)(2,1)}, bf16[128,2048]{1,0:T(8,128)(2,1)}, u32[]{:S(2)}, u32[]{:S(2)}) collective-permute-start(bf16[128,2048]{1,0:T(8,128)(2,1)} %slice.225), channel_id=1, source_target_pairs={{0,1},{1,0},{2,3},{3,2},{4,5},{5,4},{6,7},{7,6},{8,9},{9,8},{10,11... | collective-permute-start | bytes 1572872 | tf_op jit(solution)/shard_map/ppermute | solution.py:341
  6.8 0.8 slice.226
  7.6 2.0 collective-permute-start.1
  9.6 0.8 slice.227
  10.8 5.0 %forward.1 = (bf16[8192,128]{1,0:T(8,128)(2,1)S(1)}, f32[128,512]{1,0:T(8,128)S(1)}) custom-call(bf16[128,8192]{1,0:T(8,128)(2,1)S(1)} %bitcast.90, bf16[8192,512]{1,0:T(8,128)(2,1)} %weights_ref.9), custom_call_target="tpu_custom_call" | custom-call | flops 1073741824 | bytes 12582912 | tf_op jit(solution)/shard_map/forward/pallas_call | solution.py:34
  15.8 1.3 copy-done.5
  17.5 13.4 %collective-permute-done.3.part_ref = bf16[128,2048]{1,0:T(8,128)(2,1)S(1)} collective-permute-done((bf16[128,2048]{1,0:T(8,128)(2,1)S(1)}, bf16[128,2048]{1,0:T(8,128)(2,1)S(1)}, u32[]{:S(2)}, u32[]{:S(2)}) %collective-permute-start.3) | collective-permute-done | bytes 524320 | tf_op jit(solution)/shard_map/ppermute | solution.py:341
  31.0 0.8 copy-done.13
  31.7 1.0 copy-done.14
  32.8 2.0 arrive.4
  34.8 2.2 %arrive.5 = (bf16[128,8192]{1,0:T(8,128)(2,1)S(1)}, bf16[8192,128]{1,0:T(8,128)(2,1)S(1)}, f32[128,512]{1,0:T(8,128)S(1)}) custom-call(bf16[128,2048]{1,0:T(8,128)(2,1)} %collective-permute-done.2.part_ref, bf16[8192,512]{1,0:T(8,128)(2,1)} %weights_ref.9, ...), custom_call_target="tpu_custom_call", output_to_operand_aliasing={{0}: (2, {}), {1}: (3, {}), {2}: (4, {})} | custom-call | flops 268435456 | bytes 3670016 | tf_op jit(solution)/shard_map/arrive/pallas_call | solution.py:76
  37.1 5.2 %collective-permute-done.1.part_ref = bf16[128,2048]{1,0:T(8,128)(2,1)} collective-permute-done((bf16[128,2048]{1,0:T(8,128)(2,1)}, bf16[128,2048]{1,0:T(8,128)(2,1)}, u32[]{:S(2)}, u32[]{:S(2)}) %collective-permute-start.1) | collective-permute-done | bytes 524320 | tf_op jit(solution)/shard_map/ppermute | solution.py:341
  42.3 2.2 %arrive.6 = (bf16[128,8192]{1,0:T(8,128)(2,1)S(1)}, bf16[8192,128]{1,0:T(8,128)(2,1)S(1)}, f32[128,512]{1,0:T(8,128)S(1)}) custom-call(bf16[128,2048]{1,0:T(8,128)(2,1)} %collective-permute-done.1.part_ref, bf16[8192,512]{1,0:T(8,128)(2,1)} %weights_ref.9, ...), custom_call_target="tpu_custom_call", output_to_operand_aliasing={{0}: (2, {}), {1}: (3, {}), {2}: (4, {})} | custom-call | flops 268435456 | bytes 3670016 | tf_op jit(solution)/shard_map/arrive/pallas_call | solution.py:76
  44.5 8.2 %collective-permute-done.part_ref = bf16[128,2048]{1,0:T(8,128)(2,1)} collective-permute-done((bf16[128,2048]{1,0:T(8,128)(2,1)}, bf16[128,2048]{1,0:T(8,128)(2,1)}, u32[]{:S(2)}, u32[]{:S(2)}) %collective-permute-start) | collective-permute-done | bytes 524320 | tf_op jit(solution)/shard_map/ppermute | solution.py:341
  52.7 2.3 %arrive.7 = (bf16[128,8192]{1,0:T(8,128)(2,1)S(1)}, bf16[8192,128]{1,0:T(8,128)(2,1)S(1)}, f32[128,512]{1,0:T(8,128)S(1)}) custom-call(bf16[128,2048]{1,0:T(8,128)(2,1)} %collective-permute-done.part_ref, bf16[8192,512]{1,0:T(8,128)(2,1)} %weights_ref.9, ...), custom_call_target="tpu_custom_call", output_to_operand_aliasing={{0}: (2, {}), {1}: (3, {}), {2}: (4, {})} | custom-call | flops 268435456 | bytes 3670016 | tf_op jit(solution)/shard_map/arrive/pallas_call | solution.py:76
  55.7 12.0 %inner.3 = (f32[8,512,128]{2,1,0:T(8,128)S(1)}, f32[8,512,128]{2,1,0:T(8,128)S(1)}) custom-call(s32[1]{0:T(128)} %bitcast.mine_ref.place_ref, bf16[128,8192]{1,0:T(8,128)(2,1)S(1)} %bitcast.91, bf16[128,8192]{1,0:T(8,128)(2,1)S(1)} %get-tuple-element.76.high_ref, bf16[4,2,2,512,128]{4,3,2,1,0:T(8,128)(2,1)S(1)} %bitcast.94, ...), custom_call_target="tpu_custom_call" | custom-call | flops 1610612736 | bytes 20971520 | tf_op jit(solution)/shard_map/inner/pallas_call | solution.py:226
  67.9 2.6 %collective-permute-done.4 = f16[8,512,128]{2,1,0:T(8,128)(2,1)S(1)} collective-permute-done((f16[8,512,128]{2,1,0:T(8,128)(2,1)S(1)}, f16[8,512,128]{2,1,0:T(8,128)(2,1)S(1)}, u32[]{:S(2)}, u32[]{:S(2)}) %collective-permute-start.4) | collective-permute-done | bytes 1048608 | tf_op jit(solution)/shard_map/ppermute | solution.py:321
  70.7 1.8 collective-permute-start.5
  72.5 18.4 %inner.4 = (f32[8,512,128]{2,1,0:T(8,128)S(1)}, f32[8,512,128]{2,1,0:T(8,128)S(1)}, f32[8,512,128]{2,1,0:T(8,128)S(1)}, f32[8,512,128]{2,1,0:T(8,128)S(1)}) custom-call(s32[1]{0:T(128)} %bitcast.mine_ref.place_ref, bf16[128,8192]{1,0:T(8,128)(2,1)S(1)} %bitcast.92, bf16[128,8192]{1,0:T(8,128)(2,1)S(1)} %get-tuple-element.76.high_ref, ...), custom_call_target="tpu_custom_call" | custom-call | flops 3221225472 | bytes 41943040 | tf_op jit(solution)/shard_map/inner/pallas_call | solution.py:226
  91.0 1.3 convert_element_type.210
  92.3 1.3 convert_element_type.211
  94.9 1.4 dynamic-slice_bitcast_fusion
  96.3 1.1 collective-permute-done.7
  97.4 1.2 add_convert_fusion.1
  98.9 1.3 add_convert_fusion.2
  100.7 1.5 fusion.15
  102.1 2.0 collective-permute-start.8
  104.3 12.1 %inner.5 = (f32[8,512,128]{2,1,0:T(8,128)S(1)}, f32[8,512,128]{2,1,0:T(8,128)S(1)}) custom-call(s32[1]{0:T(128)} %bitcast.mine_ref.place_ref, bf16[128,8192]{1,0:T(8,128)(2,1)S(1)} %bitcast.93, bf16[128,8192]{1,0:T(8,128)(2,1)S(1)} %get-tuple-element.76.high_ref, bf16[4,2,2,512,128]{4,3,2,1,0:T(8,128)(2,1)S(1)} %bitcast.96, ...), custom_call_target="tpu_custom_call" | custom-call | flops 1610612736 | bytes 20971520 | tf_op jit(solution)/shard_map/inner/pallas_call | solution.py:226
  116.6 0.9 copy-done.18
  117.5 1.2 convert_add_fusion.3
  118.9 1.1 add_convert_fusion.6
  120.0 1.3 collective-permute-start.18
  121.7 2.6 %collective-permute-start.16 = (f16[2,512,128]{2,1,0:T(8,128)(2,1)S(1)}, f16[2,512,128]{2,1,0:T(8,128)(2,1)S(1)}, u32[]{:S(2)}, u32[]{:S(2)}) collective-permute-start(f16[2,512,128]{2,1,0:T(8,128)(2,1)S(1)} %pad_maximum_fusion.6), channel_id=1, source_target_pairs={{0,16},{2,18},{4,20},{6,22},{8,24},{10,26},{12,28},{14,30},{16,0},... | collective-permute-start | bytes 786440 | tf_op jit(solution)/shard_map/ppermute | solution.py:321
  124.5 0.9 collective-permute-start.11
  125.4 9.4 %collective-permute-done.18 = f16[4,512,128]{2,1,0:T(8,128)(2,1)S(1)} collective-permute-done((f16[4,512,128]{2,1,0:T(8,128)(2,1)S(1)}, f16[4,512,128]{2,1,0:T(8,128)(2,1)S(1)}, u32[]{:S(2)}, u32[]{:S(2)}) %collective-permute-start.18) | collective-permute-done | bytes 524320 | tf_op jit(solution)/shard_map/ppermute | solution.py:321
  135.3 1.1 convert_add_fusion
  136.5 2.7 %collective-permute-start.26 = (bf16[2,512,128]{2,1,0:T(8,128)(2,1)S(1)}, bf16[2,512,128]{2,1,0:T(8,128)(2,1)S(1)}, u32[]{:S(2)}, u32[]{:S(2)}) collective-permute-start(bf16[2,512,128]{2,1,0:T(8,128)(2,1)S(1)} %subtract_convert_fusion), channel_id=1, source_target_pairs={{0,8},{2,10},{4,12},{6,14},{8,0},{10,2},{12,4},{14,6},{16,24},{18,... | collective-permute-start | bytes 786440 | tf_op jit(solution)/shard_map/ppermute | solution.py:321
  139.3 2.8 %collective-permute-start.23 = (f16[2,512,128]{2,1,0:T(8,128)(2,1)S(1)}, f16[2,512,128]{2,1,0:T(8,128)(2,1)S(1)}, u32[]{:S(2)}, u32[]{:S(2)}) collective-permute-start(f16[2,512,128]{2,1,0:T(8,128)(2,1)S(1)} %pad_maximum_fusion.9), channel_id=1, source_target_pairs={{0,16},{2,18},{4,20},{6,22},{8,24},{10,26},{12,28},{14,30},{16,0},... | collective-permute-start | bytes 786440 | tf_op jit(solution)/shard_map/ppermute | solution.py:321
  142.0 1.1 add_convert_fusion.4
  143.2 8.8 %collective-permute-done.26 = bf16[2,512,128]{2,1,0:T(8,128)(2,1)S(1)} collective-permute-done((bf16[2,512,128]{2,1,0:T(8,128)(2,1)S(1)}, bf16[2,512,128]{2,1,0:T(8,128)(2,1)S(1)}, u32[]{:S(2)}, u32[]{:S(2)}) %collective-permute-start.26) | collective-permute-done | bytes 262176 | tf_op jit(solution)/shard_map/ppermute | solution.py:321
  152.0 0.9 collective-permute-start.27
  153.0 2.0 collective-permute-start.24
  155.0 2.1 collective-permute-done.19
  157.1 1.1 convert_add_fusion.1
  158.3 1.9 collective-permute-start.20
  160.2 1.7 collective-permute-start.12
  162.0 4.1 %collective-permute-done.24 = bf16[2,512,128]{2,1,0:T(8,128)(2,1)S(1)} collective-permute-done((bf16[2,512,128]{2,1,0:T(8,128)(2,1)S(1)}, bf16[2,512,128]{2,1,0:T(8,128)(2,1)S(1)}, u32[]{:S(2)}, u32[]{:S(2)}) %collective-permute-start.24) | collective-permute-done | bytes 262176 | tf_op jit(solution)/shard_map/ppermute | solution.py:321
  166.1 1.5 collective-permute-start.25
  167.6 3.7 %collective-permute-done.20 = f16[2,512,128]{2,1,0:T(8,128)(2,1)S(1)} collective-permute-done((f16[2,512,128]{2,1,0:T(8,128)(2,1)S(1)}, f16[2,512,128]{2,1,0:T(8,128)(2,1)S(1)}, u32[]{:S(2)}, u32[]{:S(2)}) %collective-permute-start.20) | collective-permute-done | bytes 262176 | tf_op jit(solution)/shard_map/ppermute | solution.py:321
  172.2 1.8 collective-permute-done.12
  174.2 2.2 collective-permute-start.13
  176.4 5.4 %collective-permute-done.21 = bf16[2,512,128]{2,1,0:T(8,128)(2,1)S(1)} collective-permute-done((bf16[2,512,128]{2,1,0:T(8,128)(2,1)S(1)}, bf16[2,512,128]{2,1,0:T(8,128)(2,1)S(1)}, u32[]{:S(2)}, u32[]{:S(2)}) %collective-permute-start.21) | collective-permute-done | bytes 262176 | tf_op jit(solution)/shard_map/ppermute | solution.py:321
  181.8 6.8 %collective-permute-done.13 = f16[2,512,128]{2,1,0:T(8,128)(2,1)S(1)} collective-permute-done((f16[2,512,128]{2,1,0:T(8,128)(2,1)S(1)}, f16[2,512,128]{2,1,0:T(8,128)(2,1)S(1)}, u32[]{:S(2)}, u32[]{:S(2)}) %collective-permute-start.13) | collective-permute-done | bytes 262176 | tf_op jit(solution)/shard_map/ppermute | solution.py:321
  188.6 0.8 collective-permute-start.22
  189.4 1.4 assemble.4.refs_4_
  191.7 8.1 %collective-permute-done.14 = bf16[2,512,128]{2,1,0:T(8,128)(2,1)S(1)} collective-permute-done((bf16[2,512,128]{2,1,0:T(8,128)(2,1)S(1)}, bf16[2,512,128]{2,1,0:T(8,128)(2,1)S(1)}, u32[]{:S(2)}, u32[]{:S(2)}) %collective-permute-start.14) | collective-permute-done | bytes 262176 | tf_op jit(solution)/shard_map/ppermute | solution.py:321
  199.9 1.3 collective-permute-start.15
  201.2 1.4 assemble.5.refs_4_
  203.4 10.1 %collective-permute-done.15.refs_1_ = bf16[4,512,128]{2,1,0:T(8,128)(2,1)S(1)} collective-permute-done((bf16[4,512,128]{2,1,0:T(8,128)(2,1)S(1)}, bf16[4,512,128]{2,1,0:T(8,128)(2,1)S(1)}, u32[]{:S(2)}, u32[]{:S(2)}) %collective-permute-start.15) | collective-permute-done | bytes 524320 | tf_op jit(solution)/shard_map/ppermute | solution.py:321
  213.5 1.4 assemble.6.refs_4_
  215.2 1.0 pad_maximum_fusion
  217.0 1.4 assemble.7
  (117 shorter events, 9.9 us)
Async XLA Ops:
  0.6 6.2 %copy-start.2 = (bf16[1,128,8192]{2,1,0:T(8,128)(2,1)S(1)}, bf16[1,128,8192]{2,1,0:T(8,128)(2,1)}, u32[]{:S(2)}) copy-start(bf16[1,128,8192]{2,1,0:T(8,128)(2,1)} %param.11) | copy-start | bytes 6291460
  0.6 9.9 %copy-start.19 = (s32[1,2,512]{2,1,0:T(2,128)S(1)}, s32[1,2,512]{2,1,0:T(2,128)}, u32[]{:S(2)}) copy-start(s32[1,2,512]{2,1,0:T(2,128)} %param.13) | copy-start | bytes 12292
  0.7 10.1 %copy-start.16 = (bf16[1,256,512]{2,1,0:T(8,128)(2,1)S(1)}, bf16[1,256,512]{2,1,0:T(8,128)(2,1)}, u32[]{:S(2)}) copy-start(bf16[1,256,512]{2,1,0:T(8,128)(2,1)} %param.12) | copy-start | bytes 786436
  3.8 31.0 %collective-permute-start.2 = (bf16[128,2048]{1,0:T(8,128)(2,1)}, bf16[128,2048]{1,0:T(8,128)(2,1)}, u32[]{:S(2)}, u32[]{:S(2)}) collective-permute-start(bf16[128,2048]{1,0:T(8,128)(2,1)} %slice.225), channel_id=1, source_target_pairs={{0,1},{1,0},{2,3},{3,2},{4,5},{5,4},{6,7},{7,6},{8,9},{9,8},{10,11... | collective-permute-start | bytes 1572872 | tf_op jit(solution)/shard_map/ppermute | solution.py:341
  6.8 24.2 %collective-permute-start.3 = (bf16[128,2048]{1,0:T(8,128)(2,1)S(1)}, bf16[128,2048]{1,0:T(8,128)(2,1)S(1)}, u32[]{:S(2)}, u32[]{:S(2)}) collective-permute-start(bf16[128,2048]{1,0:T(8,128)(2,1)S(1)} %slice.286), channel_id=1, source_target_pairs={{0,1},{1,0},{2,3},{3,2},{4,5},{5,4},{6,7},{7,6},{8,9},{9,8},{10,11... | collective-permute-start | bytes 1572872 | tf_op jit(solution)/shard_map/ppermute | solution.py:341
  7.6 34.7 %collective-permute-start.1 = (bf16[128,2048]{1,0:T(8,128)(2,1)}, bf16[128,2048]{1,0:T(8,128)(2,1)}, u32[]{:S(2)}, u32[]{:S(2)}) collective-permute-start(bf16[128,2048]{1,0:T(8,128)(2,1)} %slice.226), channel_id=1, source_target_pairs={{0,1},{1,0},{2,3},{3,2},{4,5},{5,4},{6,7},{7,6},{8,9},{9,8},{10,11... | collective-permute-start | bytes 1572872 | tf_op jit(solution)/shard_map/ppermute | solution.py:341
  10.5 42.2 %collective-permute-start = (bf16[128,2048]{1,0:T(8,128)(2,1)}, bf16[128,2048]{1,0:T(8,128)(2,1)}, u32[]{:S(2)}, u32[]{:S(2)}) collective-permute-start(bf16[128,2048]{1,0:T(8,128)(2,1)} %slice.227), channel_id=1, source_target_pairs={{0,1},{1,0},{2,3},{3,2},{4,5},{5,4},{6,7},{7,6},{8,9},{9,8},{10,11... | collective-permute-start | bytes 1572872 | tf_op jit(solution)/shard_map/ppermute | solution.py:341
  15.8 1.3 copy-start.5
  31.0 0.8 copy-start.13
  31.7 1.0 copy-start.14
  52.7 2.4 %copy-start.3 = (bf16[1,128,8192]{2,1,0:T(8,128)(2,1)S(1)}, bf16[1,128,8192]{2,1,0:T(8,128)(2,1)}, u32[]{:S(2)}) copy-start(bf16[1,128,8192]{2,1,0:T(8,128)(2,1)} %param.11) | copy-start | bytes 6291460
  52.7 3.0 %copy-start.6 = (bf16[8192,128]{1,0:T(8,128)(2,1)S(1)}, bf16[8192,128]{1,0:T(8,128)(2,1)}, u32[]{:S(2)}) copy-start(bf16[8192,128]{1,0:T(8,128)(2,1)} %copy-done.5) | copy-start | bytes 6291460
  55.1 17.5 %copy-start = (bf16[8192,128]{1,0:T(8,128)(2,1)}, bf16[8192,128]{1,0:T(8,128)(2,1)S(1)}, u32[]{:S(2)}) copy-start(bf16[8192,128]{1,0:T(8,128)(2,1)S(1)} %get-tuple-element.78) | copy-start | bytes 6291460
  67.7 25.9 %copy-start.12 = (f32[8,512,128]{2,1,0:T(8,128)}, f32[8,512,128]{2,1,0:T(8,128)S(1)}, u32[]{:S(2)}) copy-start(f32[8,512,128]{2,1,0:T(8,128)S(1)} %get-tuple-element.81) | copy-start | bytes 6291460
  67.8 2.7 %collective-permute-start.4 = (f16[8,512,128]{2,1,0:T(8,128)(2,1)S(1)}, f16[8,512,128]{2,1,0:T(8,128)(2,1)S(1)}, u32[]{:S(2)}, u32[]{:S(2)}) collective-permute-start(f16[8,512,128]{2,1,0:T(8,128)(2,1)S(1)} %convert_element_type.204), channel_id=1, source_target_pairs={{0,2},{2,0},{4,6},{6,4},{8,10},{10,8},{12,14},{14,12},{16,18},{18,... | collective-permute-start | bytes 3145736 | tf_op jit(solution)/shard_map/ppermute | solution.py:321
  70.6 23.1 %copy-start.15 = (f16[8,512,128]{2,1,0:T(8,128)(2,1)}, f16[8,512,128]{2,1,0:T(8,128)(2,1)S(1)}, u32[]{:S(2)}) copy-start(f16[8,512,128]{2,1,0:T(8,128)(2,1)S(1)} %collective-permute-done.4) | copy-start | bytes 3145732
  70.7 22.9 %collective-permute-start.5 = (f16[4,512,128]{2,1,0:T(8,128)(2,1)S(1)}, f16[4,512,128]{2,1,0:T(8,128)(2,1)S(1)}, u32[]{:S(2)}, u32[]{:S(2)}) collective-permute-start(f16[4,512,128]{2,1,0:T(8,128)(2,1)S(1)} %add_convert_fusion.3), channel_id=1, source_target_pairs={{0,4},{2,6},{4,0},{6,2},{8,12},{10,14},{12,8},{14,10},{16,20},{18,... | collective-permute-start | bytes 1572872 | tf_op jit(solution)/shard_map/ppermute | solution.py:321
  90.9 2.7 %copy-start.8 = (f32[8,512,128]{2,1,0:T(8,128)}, f32[8,512,128]{2,1,0:T(8,128)S(1)}, u32[]{:S(2)}) copy-start(f32[8,512,128]{2,1,0:T(8,128)S(1)} %get-tuple-element.89) | copy-start | bytes 6291460
  90.9 2.7 %copy-start.10 = (f32[8,512,128]{2,1,0:T(8,128)}, f32[8,512,128]{2,1,0:T(8,128)S(1)}, u32[]{:S(2)}) copy-start(f32[8,512,128]{2,1,0:T(8,128)S(1)} %get-tuple-element.85) | copy-start | bytes 6291460
  93.6 0.8 copy-start.17
  94.4 3.0 %collective-permute-start.7 = (f16[8,512,128]{2,1,0:T(8,128)(2,1)}, f16[8,512,128]{2,1,0:T(8,128)(2,1)}, u32[]{:S(2)}, u32[]{:S(2)}) collective-permute-start(f16[8,512,128]{2,1,0:T(8,128)(2,1)} %convert_element_type.211), channel_id=1, source_target_pairs={{0,2},{2,0},{4,6},{6,4},{8,10},{10,8},{12,14},{14,12},{16,18},{18,... | collective-permute-start | bytes 3145736 | tf_op jit(solution)/shard_map/ppermute | solution.py:321
  94.4 4.5 %collective-permute-start.6 = (f16[8,512,128]{2,1,0:T(8,128)(2,1)}, f16[8,512,128]{2,1,0:T(8,128)(2,1)}, u32[]{:S(2)}, u32[]{:S(2)}) collective-permute-start(f16[8,512,128]{2,1,0:T(8,128)(2,1)} %convert_element_type.210), channel_id=1, source_target_pairs={{0,2},{2,0},{4,6},{6,4},{8,10},{10,8},{12,14},{14,12},{16,18},{18,... | collective-permute-start | bytes 3145736 | tf_op jit(solution)/shard_map/ppermute | solution.py:321
  94.9 2.5 %copy-start.9 = (f32[8,512,128]{2,1,0:T(8,128)S(1)}, f32[8,512,128]{2,1,0:T(8,128)}, u32[]{:S(2)}) copy-start(f32[8,512,128]{2,1,0:T(8,128)} %copy-done.8) | copy-start | bytes 6291460
  94.9 4.0 %copy-start.11 = (f32[8,512,128]{2,1,0:T(8,128)S(1)}, f32[8,512,128]{2,1,0:T(8,128)}, u32[]{:S(2)}) copy-start(f32[8,512,128]{2,1,0:T(8,128)} %copy-done.10) | copy-start | bytes 6291460
  98.9 5.4 %copy-start.7 = (bf16[8192,128]{1,0:T(8,128)(2,1)S(1)}, bf16[8192,128]{1,0:T(8,128)(2,1)}, u32[]{:S(2)}) copy-start(bf16[8192,128]{1,0:T(8,128)(2,1)} %copy-done.5) | copy-start | bytes 6291460
  100.3 4.0 %copy-start.1 = (bf16[8192,128]{1,0:T(8,128)(2,1)S(1)}, bf16[8192,128]{1,0:T(8,128)(2,1)}, u32[]{:S(2)}) copy-start(bf16[8192,128]{1,0:T(8,128)(2,1)} %copy-done) | copy-start | bytes 6291460
  100.3 4.0 %copy-start.4 = (bf16[1,128,8192]{2,1,0:T(8,128)(2,1)S(1)}, bf16[1,128,8192]{2,1,0:T(8,128)(2,1)}, u32[]{:S(2)}) copy-start(bf16[1,128,8192]{2,1,0:T(8,128)(2,1)} %param.11) | copy-start | bytes 6291460
  100.3 16.3 %collective-permute-start.9 = (f16[4,512,128]{2,1,0:T(8,128)(2,1)S(1)}, f16[4,512,128]{2,1,0:T(8,128)(2,1)S(1)}, u32[]{:S(2)}, u32[]{:S(2)}) collective-permute-start(f16[4,512,128]{2,1,0:T(8,128)(2,1)S(1)} %add_convert_fusion.2), channel_id=1, source_target_pairs={{0,4},{2,6},{4,0},{6,2},{8,12},{10,14},{12,8},{14,10},{16,20},{18,... | collective-permute-start | bytes 1572872 | tf_op jit(solution)/shard_map/ppermute | solution.py:321
  102.1 14.5 %collective-permute-start.8 = (f16[2,512,128]{2,1,0:T(8,128)(2,1)S(1)}, f16[2,512,128]{2,1,0:T(8,128)(2,1)S(1)}, u32[]{:S(2)}, u32[]{:S(2)}) collective-permute-start(f16[2,512,128]{2,1,0:T(8,128)(2,1)S(1)} %add_convert_fusion.7), channel_id=1, source_target_pairs={{0,8},{2,10},{4,12},{6,14},{8,0},{10,2},{12,4},{14,6},{16,24},{18,... | collective-permute-start | bytes 786440 | tf_op jit(solution)/shard_map/ppermute | solution.py:321
  116.4 1.0 copy-start.18
  119.9 4.4 %collective-permute-start.10 = (f16[8,512,128]{2,1,0:T(8,128)(2,1)S(1)}, f16[8,512,128]{2,1,0:T(8,128)(2,1)S(1)}, u32[]{:S(2)}, u32[]{:S(2)}) collective-permute-start(f16[8,512,128]{2,1,0:T(8,128)(2,1)S(1)} %convert_element_type.216), channel_id=1, source_target_pairs={{0,2},{2,0},{4,6},{6,4},{8,10},{10,8},{12,14},{14,12},{16,18},{18,... | collective-permute-start | bytes 3145736 | tf_op jit(solution)/shard_map/ppermute | solution.py:321
  120.0 14.8 %collective-permute-start.18 = (f16[4,512,128]{2,1,0:T(8,128)(2,1)S(1)}, f16[4,512,128]{2,1,0:T(8,128)(2,1)S(1)}, u32[]{:S(2)}, u32[]{:S(2)}) collective-permute-start(f16[4,512,128]{2,1,0:T(8,128)(2,1)S(1)} %add_convert_fusion.1), channel_id=1, source_target_pairs={{0,4},{2,6},{4,0},{6,2},{8,12},{10,14},{12,8},{14,10},{16,20},{18,... | collective-permute-start | bytes 1572872 | tf_op jit(solution)/shard_map/ppermute | solution.py:321
  121.3 14.0 %collective-permute-start.17 = (f16[2,512,128]{2,1,0:T(8,128)(2,1)S(1)}, f16[2,512,128]{2,1,0:T(8,128)(2,1)S(1)}, u32[]{:S(2)}, u32[]{:S(2)}) collective-permute-start(f16[2,512,128]{2,1,0:T(8,128)(2,1)S(1)} %add_convert_fusion.6), channel_id=1, source_target_pairs={{0,8},{2,10},{4,12},{6,14},{8,0},{10,2},{12,4},{14,6},{16,24},{18,... | collective-permute-start | bytes 786440 | tf_op jit(solution)/shard_map/ppermute | solution.py:321
  121.7 13.5 %collective-permute-start.16 = (f16[2,512,128]{2,1,0:T(8,128)(2,1)S(1)}, f16[2,512,128]{2,1,0:T(8,128)(2,1)S(1)}, u32[]{:S(2)}, u32[]{:S(2)}) collective-permute-start(f16[2,512,128]{2,1,0:T(8,128)(2,1)S(1)} %pad_maximum_fusion.6), channel_id=1, source_target_pairs={{0,16},{2,18},{4,20},{6,22},{8,24},{10,26},{12,28},{14,30},{16,0},... | collective-permute-start | bytes 786440 | tf_op jit(solution)/shard_map/ppermute | solution.py:321
  124.5 35.7 %collective-permute-start.11 = (f16[4,512,128]{2,1,0:T(8,128)(2,1)S(1)}, f16[4,512,128]{2,1,0:T(8,128)(2,1)S(1)}, u32[]{:S(2)}, u32[]{:S(2)}) collective-permute-start(f16[4,512,128]{2,1,0:T(8,128)(2,1)S(1)} %add_convert_fusion), channel_id=1, source_target_pairs={{0,4},{2,6},{4,0},{6,2},{8,12},{10,14},{12,8},{14,10},{16,20},{18,... | collective-permute-start | bytes 1572872 | tf_op jit(solution)/shard_map/ppermute | solution.py:321
  136.5 15.4 %collective-permute-start.26 = (bf16[2,512,128]{2,1,0:T(8,128)(2,1)S(1)}, bf16[2,512,128]{2,1,0:T(8,128)(2,1)S(1)}, u32[]{:S(2)}, u32[]{:S(2)}) collective-permute-start(bf16[2,512,128]{2,1,0:T(8,128)(2,1)S(1)} %subtract_convert_fusion), channel_id=1, source_target_pairs={{0,8},{2,10},{4,12},{6,14},{8,0},{10,2},{12,4},{14,6},{16,24},{18,... | collective-permute-start | bytes 786440 | tf_op jit(solution)/shard_map/ppermute | solution.py:321
  139.3 13.6 %collective-permute-start.23 = (f16[2,512,128]{2,1,0:T(8,128)(2,1)S(1)}, f16[2,512,128]{2,1,0:T(8,128)(2,1)S(1)}, u32[]{:S(2)}, u32[]{:S(2)}) collective-permute-start(f16[2,512,128]{2,1,0:T(8,128)(2,1)S(1)} %pad_maximum_fusion.9), channel_id=1, source_target_pairs={{0,16},{2,18},{4,20},{6,22},{8,24},{10,26},{12,28},{14,30},{16,0},... | collective-permute-start | bytes 786440 | tf_op jit(solution)/shard_map/ppermute | solution.py:321
  143.1 14.0 %collective-permute-start.19 = (f16[2,512,128]{2,1,0:T(8,128)(2,1)S(1)}, f16[2,512,128]{2,1,0:T(8,128)(2,1)S(1)}, u32[]{:S(2)}, u32[]{:S(2)}) collective-permute-start(f16[2,512,128]{2,1,0:T(8,128)(2,1)S(1)} %add_convert_fusion.4), channel_id=1, source_target_pairs={{0,8},{2,10},{4,12},{6,14},{8,0},{10,2},{12,4},{14,6},{16,24},{18,... | collective-permute-start | bytes 786440 | tf_op jit(solution)/shard_map/ppermute | solution.py:321
  152.0 20.2 %collective-permute-start.27 = (bf16[4,512,128]{2,1,0:T(8,128)(2,1)S(1)}, bf16[4,512,128]{2,1,0:T(8,128)(2,1)S(1)}, u32[]{:S(2)}, u32[]{:S(2)}) collective-permute-start(bf16[4,512,128]{2,1,0:T(8,128)(2,1)S(1)} %pad_maximum_fusion.4.refs_0_), channel_id=1, source_target_pairs={{0,4},{2,6},{4,0},{6,2},{8,12},{10,14},{12,8},{14,10},{16,20},{18,... | collective-permute-start | bytes 1572872 | tf_op jit(solution)/shard_map/ppermute | solution.py:321
  152.9 36.6 %collective-permute-start.28 = (bf16[4,512,128]{2,1,0:T(8,128)(2,1)S(1)}, bf16[4,512,128]{2,1,0:T(8,128)(2,1)S(1)}, u32[]{:S(2)}, u32[]{:S(2)}) collective-permute-start(bf16[4,512,128]{2,1,0:T(8,128)(2,1)S(1)} %pad_maximum_fusion.4.refs_0_), channel_id=1, source_target_pairs={{0,2},{2,0},{4,6},{6,4},{8,10},{10,8},{12,14},{14,12},{16,18},{18,... | collective-permute-start | bytes 1572872 | tf_op jit(solution)/shard_map/ppermute | solution.py:321
  153.0 13.0 %collective-permute-start.24 = (bf16[2,512,128]{2,1,0:T(8,128)(2,1)S(1)}, bf16[2,512,128]{2,1,0:T(8,128)(2,1)S(1)}, u32[]{:S(2)}, u32[]{:S(2)}) collective-permute-start(bf16[2,512,128]{2,1,0:T(8,128)(2,1)S(1)} %subtract_convert_fusion.1), channel_id=1, source_target_pairs={{0,8},{2,10},{4,12},{6,14},{8,0},{10,2},{12,4},{14,6},{16,24},{18,... | collective-permute-start | bytes 786440 | tf_op jit(solution)/shard_map/ppermute | solution.py:321
  158.3 13.1 %collective-permute-start.20 = (f16[2,512,128]{2,1,0:T(8,128)(2,1)S(1)}, f16[2,512,128]{2,1,0:T(8,128)(2,1)S(1)}, u32[]{:S(2)}, u32[]{:S(2)}) collective-permute-start(f16[2,512,128]{2,1,0:T(8,128)(2,1)S(1)} %pad_maximum_fusion.8), channel_id=1, source_target_pairs={{0,16},{2,18},{4,20},{6,22},{8,24},{10,26},{12,28},{14,30},{16,0},... | collective-permute-start | bytes 786440 | tf_op jit(solution)/shard_map/ppermute | solution.py:321
  160.2 13.7 %collective-permute-start.12 = (f16[2,512,128]{2,1,0:T(8,128)(2,1)S(1)}, f16[2,512,128]{2,1,0:T(8,128)(2,1)S(1)}, u32[]{:S(2)}, u32[]{:S(2)}) collective-permute-start(f16[2,512,128]{2,1,0:T(8,128)(2,1)S(1)} %add_convert_fusion.5), channel_id=1, source_target_pairs={{0,8},{2,10},{4,12},{6,14},{8,0},{10,2},{12,4},{14,6},{16,24},{18,... | collective-permute-start | bytes 786440 | tf_op jit(solution)/shard_map/ppermute | solution.py:321
  166.1 23.3 %collective-permute-start.25 = (bf16[4,512,128]{2,1,0:T(8,128)(2,1)S(1)}, bf16[4,512,128]{2,1,0:T(8,128)(2,1)S(1)}, u32[]{:S(2)}, u32[]{:S(2)}) collective-permute-start(bf16[4,512,128]{2,1,0:T(8,128)(2,1)S(1)} %pad_maximum_fusion.3.refs_0_), channel_id=1, source_target_pairs={{0,4},{2,6},{4,0},{6,2},{8,12},{10,14},{12,8},{14,10},{16,20},{18,... | collective-permute-start | bytes 1572872 | tf_op jit(solution)/shard_map/ppermute | solution.py:321
  171.5 10.3 %collective-permute-start.21 = (bf16[2,512,128]{2,1,0:T(8,128)(2,1)S(1)}, bf16[2,512,128]{2,1,0:T(8,128)(2,1)S(1)}, u32[]{:S(2)}, u32[]{:S(2)}) collective-permute-start(bf16[2,512,128]{2,1,0:T(8,128)(2,1)S(1)} %subtract_convert_fusion.2), channel_id=1, source_target_pairs={{0,8},{2,10},{4,12},{6,14},{8,0},{10,2},{12,4},{14,6},{16,24},{18,... | collective-permute-start | bytes 786440 | tf_op jit(solution)/shard_map/ppermute | solution.py:321
  172.2 17.3 %collective-permute-start.29 = (bf16[4,512,128]{2,1,0:T(8,128)(2,1)S(1)}, bf16[4,512,128]{2,1,0:T(8,128)(2,1)S(1)}, u32[]{:S(2)}, u32[]{:S(2)}) collective-permute-start(bf16[4,512,128]{2,1,0:T(8,128)(2,1)S(1)} %collective-permute-done.27.refs_1_), channel_id=1, source_target_pairs={{0,2},{2,0},{4,6},{6,4},{8,10},{10,8},{12,14},{14,12},{16,18},{18,... | collective-permute-start | bytes 1572872 | tf_op jit(solution)/shard_map/ppermute | solution.py:321
  174.2 14.4 %collective-permute-start.13 = (f16[2,512,128]{2,1,0:T(8,128)(2,1)S(1)}, f16[2,512,128]{2,1,0:T(8,128)(2,1)S(1)}, u32[]{:S(2)}, u32[]{:S(2)}) collective-permute-start(f16[2,512,128]{2,1,0:T(8,128)(2,1)S(1)} %pad_maximum_fusion.7), channel_id=1, source_target_pairs={{0,16},{2,18},{4,20},{6,22},{8,24},{10,26},{12,28},{14,30},{16,0},... | collective-permute-start | bytes 786440 | tf_op jit(solution)/shard_map/ppermute | solution.py:321
  181.8 19.4 %collective-permute-start.30 = (bf16[4,512,128]{2,1,0:T(8,128)(2,1)S(1)}, bf16[4,512,128]{2,1,0:T(8,128)(2,1)S(1)}, u32[]{:S(2)}, u32[]{:S(2)}) collective-permute-start(bf16[4,512,128]{2,1,0:T(8,128)(2,1)S(1)} %pad_maximum_fusion.3.refs_0_), channel_id=1, source_target_pairs={{0,2},{2,0},{4,6},{6,4},{8,10},{10,8},{12,14},{14,12},{16,18},{18,... | collective-permute-start | bytes 1572872 | tf_op jit(solution)/shard_map/ppermute | solution.py:321
  188.6 12.6 %collective-permute-start.22 = (bf16[4,512,128]{2,1,0:T(8,128)(2,1)S(1)}, bf16[4,512,128]{2,1,0:T(8,128)(2,1)S(1)}, u32[]{:S(2)}, u32[]{:S(2)}) collective-permute-start(bf16[4,512,128]{2,1,0:T(8,128)(2,1)S(1)} %pad_maximum_fusion.2.refs_0_), channel_id=1, source_target_pairs={{0,4},{2,6},{4,0},{6,2},{8,12},{10,14},{12,8},{14,10},{16,20},{18,... | collective-permute-start | bytes 1572872 | tf_op jit(solution)/shard_map/ppermute | solution.py:321
  190.9 10.3 %collective-permute-start.31 = (bf16[4,512,128]{2,1,0:T(8,128)(2,1)S(1)}, bf16[4,512,128]{2,1,0:T(8,128)(2,1)S(1)}, u32[]{:S(2)}, u32[]{:S(2)}) collective-permute-start(bf16[4,512,128]{2,1,0:T(8,128)(2,1)S(1)} %collective-permute-done.25.refs_1_), channel_id=1, source_target_pairs={{0,2},{2,0},{4,6},{6,4},{8,10},{10,8},{12,14},{14,12},{16,18},{18,... | collective-permute-start | bytes 1572872 | tf_op jit(solution)/shard_map/ppermute | solution.py:321
  191.1 8.8 %collective-permute-start.14 = (bf16[2,512,128]{2,1,0:T(8,128)(2,1)S(1)}, bf16[2,512,128]{2,1,0:T(8,128)(2,1)S(1)}, u32[]{:S(2)}, u32[]{:S(2)}) collective-permute-start(bf16[2,512,128]{2,1,0:T(8,128)(2,1)S(1)} %subtract_convert_fusion.3), channel_id=1, source_target_pairs={{0,8},{2,10},{4,12},{6,14},{8,0},{10,2},{12,4},{14,6},{16,24},{18,... | collective-permute-start | bytes 786440 | tf_op jit(solution)/shard_map/ppermute | solution.py:321
  191.4 22.1 %collective-permute-start.32 = (bf16[4,512,128]{2,1,0:T(8,128)(2,1)S(1)}, bf16[4,512,128]{2,1,0:T(8,128)(2,1)S(1)}, u32[]{:S(2)}, u32[]{:S(2)}) collective-permute-start(bf16[4,512,128]{2,1,0:T(8,128)(2,1)S(1)} %pad_maximum_fusion.2.refs_0_), channel_id=1, source_target_pairs={{0,2},{2,0},{4,6},{6,4},{8,10},{10,8},{12,14},{14,12},{16,18},{18,... | collective-permute-start | bytes 1572872 | tf_op jit(solution)/shard_map/ppermute | solution.py:321
  199.9 13.6 %collective-permute-start.15 = (bf16[4,512,128]{2,1,0:T(8,128)(2,1)S(1)}, bf16[4,512,128]{2,1,0:T(8,128)(2,1)S(1)}, u32[]{:S(2)}, u32[]{:S(2)}) collective-permute-start(bf16[4,512,128]{2,1,0:T(8,128)(2,1)S(1)} %pad_maximum_fusion.1.refs_0_), channel_id=1, source_target_pairs={{0,4},{2,6},{4,0},{6,2},{8,12},{10,14},{12,8},{14,10},{16,20},{18,... | collective-permute-start | bytes 1572872 | tf_op jit(solution)/shard_map/ppermute | solution.py:321
  202.6 10.9 %collective-permute-start.33 = (bf16[4,512,128]{2,1,0:T(8,128)(2,1)S(1)}, bf16[4,512,128]{2,1,0:T(8,128)(2,1)S(1)}, u32[]{:S(2)}, u32[]{:S(2)}) collective-permute-start(bf16[4,512,128]{2,1,0:T(8,128)(2,1)S(1)} %collective-permute-done.22.refs_1_), channel_id=1, source_target_pairs={{0,2},{2,0},{4,6},{6,4},{8,10},{10,8},{12,14},{14,12},{16,18},{18,... | collective-permute-start | bytes 1572872 | tf_op jit(solution)/shard_map/ppermute | solution.py:321
  202.8 13.4 %collective-permute-start.34 = (bf16[4,512,128]{2,1,0:T(8,128)(2,1)S(1)}, bf16[4,512,128]{2,1,0:T(8,128)(2,1)S(1)}, u32[]{:S(2)}, u32[]{:S(2)}) collective-permute-start(bf16[4,512,128]{2,1,0:T(8,128)(2,1)S(1)} %pad_maximum_fusion.1.refs_0_), channel_id=1, source_target_pairs={{0,2},{2,0},{4,6},{6,4},{8,10},{10,8},{12,14},{14,12},{16,18},{18,... | collective-permute-start | bytes 1572872 | tf_op jit(solution)/shard_map/ppermute | solution.py:321
  215.0 2.0 collective-permute-start.35

commit v10 on v9

--- a/solution.py
+++ b/solution.py
@@ -13,7 +13,7 @@
 WIRE_SCALE = 64.0
 LANES = 128
 SLABS = 4
-PIECE = 8192
+PIECE = 4096
 MIB = 1024 * 1024
 
 
@@ -358,7 +358,7 @@
     turned = [array.reshape(cut[:4] + (half,)) for array in turned]
     place = mine.reshape(1).astype(jnp.int32)
     if chunks == 4:
-        calls = [(2 * width, width), (0, 2 * width), (3 * width, width)]
+        calls = [(0, 2 * width), (2 * width, width), (3 * width, width)]
     else:
         calls = [(begin, width) for begin in range(0, columns, width)]
     begins = [begin + part for begin, wide in calls for part in range(0, wide, width)]
@@ -439,6 +439,8 @@
         if fresh.stop < chunks:
             formed, token = tied(formed, token)
     move_on(range(fresh[0]), behind=fresh)
+    move_on(fresh, behind=range(fresh[0]))
+    move_on(range(fresh[0])[:1], behind=fresh)
     for chunk in range(chunks):
         while chunk not in finished:
             move_on([chunk])
@@ -446,7 +448,7 @@
     for chunk in range(chunks):
         _, stack, across, offsets = finished[chunk]
         offsets = [[offset ^ low for offset in offsets] for low in (0, 2, 1, 3)]
-        if result:
+        if result and chunk + 1 < chunks:
             across, *result = tied(across, result[0])
         received = [stack, across, swapped(stack, 1), swapped(across, 1)]
         result = (

time: 219 us -> 234 us (1.068)
  waiting for transfers between devices: 92.4 us -> 112 us
  other arithmetic: 14.6 us -> 11.3 us
    ppermute x32, waiting for transfers between devices: 65.6 us -> 85.5 us  [swapped(): return lax.ppermute(array, 'rep', pairs)]
    unnamed x40 -> x44, local copies, waits for them, and re-layouts: 5.35 us -> 4.56 us
  transfers between devices with their start and end apart: 36 -> 36, of which waited for: 18 -> 19; matrix products, arithmetic and copies ran while one was open for 7% -> 5% of each run, Pallas kernels for 21% -> 17%
where the time goes in v10:
time: 234 us
  waiting for transfers between devices  112 us (48%)
  Pallas kernels  62 us (26%)
  starting transfers between devices  34.1 us (15%)
  local copies, waits for them, and re-layouts  12.4 us (5%)
  other arithmetic  11.3 us (5%)
    ppermute x32, waiting for transfers between devices, swapped(): return lax.ppermute(array, 'rep', pairs)  85.5 us
    pallas_call x3, Pallas kernels, inner(): pl.pallas_call(functools.partial(inner_kernel, float(tokens)), grid_spec=...  42.5 us
    ppermute x32, starting transfers between devices, swapped(): return lax.ppermute(array, 'rep', pairs)  29.1 us
    ppermute x4, waiting for transfers between devices, per_device(): parts.append(lax.ppermute(part, 'fsdp', [(0, 1), (1, 0)]))  26.8 us
    pallas_call x4, Pallas kernels, arrive(): pl.pallas_call(functools.partial(arrive_kernel, piece), grid=(1,), in_spe...  8.84 us
    pallas_call x4, Pallas kernels, assemble(): pl.pallas_call(functools.partial(assemble_kernel, begin, offsets), in_spe...  5.76 us
    ppermute x4, starting transfers between devices, per_device(): parts.append(lax.ppermute(part, 'fsdp', [(0, 1), (1, 0)]))  5.03 us
    pallas_call x1, Pallas kernels, forward(): pl.pallas_call(forward_kernel, grid=(SLABS,), in_specs=[pl.BlockSpec((row...  4.98 us
  transfers between devices with their start and end apart: 36, of which 19 were waited for; matrix products, arithmetic and copies ran while one was open for 5% of the time, Pallas kernels for 17%

profile of v10, /device:TPU:0, one launch (start us, length us, event | category | flops | bytes accessed | tf_op | source)
XLA Modules:
  0.0 233.6 jit_solution(7756250992330904190)
XLA Ops:
  0.7 1.2 slice.286
  1.9 1.9 slice.225
  3.8 3.0 %collective-permute-start.2 = (bf16[128,2048]{1,0:T(8,128)(2,1)}, bf16[128,2048]{1,0:T(8,128)(2,1)}, u32[]{:S(2)}, u32[]{:S(2)}) collective-permute-start(bf16[128,2048]{1,0:T(8,128)(2,1)} %slice.225), channel_id=1, source_target_pairs={{0,1},{1,0},{2,3},{3,2},{4,5},{5,4},{6,7},{7,6},{8,9},{9,8},{10,11... | collective-permute-start | bytes 1572872 | tf_op jit(solution)/shard_map/ppermute | solution.py:341
  6.8 0.8 slice.226
  7.7 2.0 collective-permute-start.1
  9.6 0.8 slice.227
  10.8 5.0 %forward.1 = (bf16[8192,128]{1,0:T(8,128)(2,1)S(1)}, f32[128,512]{1,0:T(8,128)S(1)}) custom-call(bf16[128,8192]{1,0:T(8,128)(2,1)S(1)} %bitcast.90, bf16[8192,512]{1,0:T(8,128)(2,1)} %weights_ref.9), custom_call_target="tpu_custom_call" | custom-call | flops 1073741824 | bytes 12582912 | tf_op jit(solution)/shard_map/forward/pallas_call | solution.py:34
  15.8 1.3 copy-done.5
  17.5 13.4 %collective-permute-done.3.part_ref = bf16[128,2048]{1,0:T(8,128)(2,1)S(1)} collective-permute-done((bf16[128,2048]{1,0:T(8,128)(2,1)S(1)}, bf16[128,2048]{1,0:T(8,128)(2,1)S(1)}, u32[]{:S(2)}, u32[]{:S(2)}) %collective-permute-start.3) | collective-permute-done | bytes 524320 | tf_op jit(solution)/shard_map/ppermute | solution.py:341
  31.0 0.8 copy-done.13
  31.8 1.0 copy-done.14
  32.8 2.0 arrive.4
  34.8 2.2 arrive.5
  37.1 5.2 %collective-permute-done.1.part_ref = bf16[128,2048]{1,0:T(8,128)(2,1)} collective-permute-done((bf16[128,2048]{1,0:T(8,128)(2,1)}, bf16[128,2048]{1,0:T(8,128)(2,1)}, u32[]{:S(2)}, u32[]{:S(2)}) %collective-permute-start.1) | collective-permute-done | bytes 524320 | tf_op jit(solution)/shard_map/ppermute | solution.py:341
  42.3 2.2 arrive.6
  44.5 8.2 %collective-permute-done.part_ref = bf16[128,2048]{1,0:T(8,128)(2,1)} collective-permute-done((bf16[128,2048]{1,0:T(8,128)(2,1)}, bf16[128,2048]{1,0:T(8,128)(2,1)}, u32[]{:S(2)}, u32[]{:S(2)}) %collective-permute-start) | collective-permute-done | bytes 524320 | tf_op jit(solution)/shard_map/ppermute | solution.py:341
  52.7 2.3 %arrive.7 = (bf16[128,8192]{1,0:T(8,128)(2,1)S(1)}, bf16[8192,128]{1,0:T(8,128)(2,1)S(1)}, f32[128,512]{1,0:T(8,128)S(1)}) custom-call(bf16[128,2048]{1,0:T(8,128)(2,1)} %collective-permute-done.part_ref, bf16[8192,512]{1,0:T(8,128)(2,1)} %weights_ref.9, ...), custom_call_target="tpu_custom_call", output_to_operand_aliasing={{0}: (2, {}), {1}: (3, {}), {2}: (4, {})} | custom-call | flops 268435456 | bytes 3670016 | tf_op jit(solution)/shard_map/arrive/pallas_call | solution.py:76
  55.1 0.6 copy-done.6
  55.7 18.5 %inner.3 = (f32[8,512,128]{2,1,0:T(8,128)S(1)}, f32[8,512,128]{2,1,0:T(8,128)S(1)}, f32[8,512,128]{2,1,0:T(8,128)S(1)}, f32[8,512,128]{2,1,0:T(8,128)S(1)}) custom-call(s32[1]{0:T(128)} %bitcast.mine_ref.place_ref, bf16[128,8192]{1,0:T(8,128)(2,1)S(1)} %bitcast.91, bf16[128,8192]{1,0:T(8,128)(2,1)S(1)} %get-tuple-element.77.high_ref, ...), custom_call_target="tpu_custom_call" | custom-call | flops 3221225472 | bytes 41943040 | tf_op jit(solution)/shard_map/inner/pallas_call | solution.py:226
  75.2 1.9 collective-permute-done.5
  77.1 1.1 add_convert_fusion.2
  78.7 1.8 collective-permute-start.6
  80.5 11.9 %inner.4 = (f32[8,512,128]{2,1,0:T(8,128)S(1)}, f32[8,512,128]{2,1,0:T(8,128)S(1)}) custom-call(s32[1]{0:T(128)} %bitcast.mine_ref.place_ref, bf16[128,8192]{1,0:T(8,128)(2,1)S(1)} %bitcast.92, bf16[128,8192]{1,0:T(8,128)(2,1)S(1)} %get-tuple-element.77.high_ref, bf16[4,2,2,512,128]{4,3,2,1,0:T(8,128)(2,1)S(1)} %bitcast.95, ...), custom_call_target="tpu_custom_call" | custom-call | flops 1610612736 | bytes 20971520 | tf_op jit(solution)/shard_map/inner/pallas_call | solution.py:226
  92.4 1.3 convert_element_type.213
  94.6 1.4 dynamic-slice_bitcast_fusion
  96.0 1.6 collective-permute-done.7
  97.6 1.3 add_convert_fusion.1
  99.0 0.8 collective-permute-start.10
  99.7 1.3 collective-permute-start.9
  101.0 1.3 fusion.15
  102.3 1.6 collective-permute-start.8
  104.2 12.1 %inner.5 = (f32[8,512,128]{2,1,0:T(8,128)S(1)}, f32[8,512,128]{2,1,0:T(8,128)S(1)}) custom-call(s32[1]{0:T(128)} %bitcast.mine_ref.place_ref, bf16[128,8192]{1,0:T(8,128)(2,1)S(1)} %bitcast.93, bf16[128,8192]{1,0:T(8,128)(2,1)S(1)} %get-tuple-element.77.high_ref, bf16[4,2,2,512,128]{4,3,2,1,0:T(8,128)(2,1)S(1)} %bitcast.96, ...), custom_call_target="tpu_custom_call" | custom-call | flops 1610612736 | bytes 20971520 | tf_op jit(solution)/shard_map/inner/pallas_call | solution.py:226
  116.5 7.7 %collective-permute-done.9 = f16[4,512,128]{2,1,0:T(8,128)(2,1)S(1)} collective-permute-done((f16[4,512,128]{2,1,0:T(8,128)(2,1)}, f16[4,512,128]{2,1,0:T(8,128)(2,1)S(1)}, u32[]{:S(2)}, u32[]{:S(2)}) %collective-permute-start.9) | collective-permute-done | bytes 524320 | tf_op jit(solution)/shard_map/ppermute | solution.py:321
  124.2 1.2 convert_add_fusion.3
  125.6 1.1 add_convert_fusion.5
  126.9 1.6 collective-permute-start.15
  129.0 2.6 %collective-permute-start.13 = (f16[2,512,128]{2,1,0:T(8,128)(2,1)S(1)}, f16[2,512,128]{2,1,0:T(8,128)(2,1)S(1)}, u32[]{:S(2)}, u32[]{:S(2)}) collective-permute-start(f16[2,512,128]{2,1,0:T(8,128)(2,1)S(1)} %pad_maximum_fusion.6), channel_id=1, source_target_pairs={{0,16},{2,18},{4,20},{6,22},{8,24},{10,26},{12,28},{14,30},{16,0},... | collective-permute-start | bytes 786440 | tf_op jit(solution)/shard_map/ppermute | solution.py:321
  131.7 0.8 collective-permute-start.12
  132.5 9.2 %collective-permute-done.15 = f16[2,512,128]{2,1,0:T(8,128)(2,1)S(1)} collective-permute-done((f16[2,512,128]{2,1,0:T(8,128)(2,1)S(1)}, f16[2,512,128]{2,1,0:T(8,128)(2,1)S(1)}, u32[]{:S(2)}, u32[]{:S(2)}) %collective-permute-start.15) | collective-permute-done | bytes 262176 | tf_op jit(solution)/shard_map/ppermute | solution.py:321
  141.7 5.2 %collective-permute-done.14 = f16[2,512,128]{2,1,0:T(8,128)(2,1)S(1)} collective-permute-done((f16[2,512,128]{2,1,0:T(8,128)(2,1)S(1)}, f16[2,512,128]{2,1,0:T(8,128)(2,1)S(1)}, u32[]{:S(2)}, u32[]{:S(2)}) %collective-permute-start.14) | collective-permute-done | bytes 262176 | tf_op jit(solution)/shard_map/ppermute | solution.py:321
  146.9 1.1 convert_add_fusion.1
  148.3 2.5 %collective-permute-start.25 = (f16[2,512,128]{2,1,0:T(8,128)(2,1)S(1)}, f16[2,512,128]{2,1,0:T(8,128)(2,1)S(1)}, u32[]{:S(2)}, u32[]{:S(2)}) collective-permute-start(f16[2,512,128]{2,1,0:T(8,128)(2,1)S(1)} %get-tuple-element.134), channel_id=1, source_target_pairs={{0,16},{2,18},{4,20},{6,22},{8,24},{10,26},{12,28},{14,30},{16,0},... | collective-permute-start | bytes 786440 | tf_op jit(solution)/shard_map/ppermute | solution.py:321
  151.5 2.7 %collective-permute-start.28 = (bf16[2,512,128]{2,1,0:T(8,128)(2,1)S(1)}, bf16[2,512,128]{2,1,0:T(8,128)(2,1)S(1)}, u32[]{:S(2)}, u32[]{:S(2)}) collective-permute-start(bf16[2,512,128]{2,1,0:T(8,128)(2,1)S(1)} %subtract_convert_fusion.3), channel_id=1, source_target_pairs={{0,8},{2,10},{4,12},{6,14},{8,0},{10,2},{12,4},{14,6},{16,24},{18,... | collective-permute-start | bytes 786440 | tf_op jit(solution)/shard_map/ppermute | solution.py:321
  154.1 15.6 %collective-permute-done.25 = f16[2,512,128]{2,1,0:T(8,128)(2,1)S(1)} collective-permute-done((f16[2,512,128]{2,1,0:T(8,128)(2,1)S(1)}, f16[2,512,128]{2,1,0:T(8,128)(2,1)S(1)}, u32[]{:S(2)}, u32[]{:S(2)}) %collective-permute-start.25) | collective-permute-done | bytes 262176 | tf_op jit(solution)/shard_map/ppermute | solution.py:321
  170.1 2.1 collective-permute-start.16
  172.1 2.0 collective-permute-done.22
  174.2 0.8 collective-permute-start.29
  175.0 4.8 %collective-permute-done.26 = bf16[2,512,128]{2,1,0:T(8,128)(2,1)S(1)} collective-permute-done((bf16[2,512,128]{2,1,0:T(8,128)(2,1)S(1)}, bf16[2,512,128]{2,1,0:T(8,128)(2,1)S(1)}, u32[]{:S(2)}, u32[]{:S(2)}) %collective-permute-start.26) | collective-permute-done | bytes 262176 | tf_op jit(solution)/shard_map/ppermute | solution.py:321
  179.7 5.5 %collective-permute-done.16 = f16[2,512,128]{2,1,0:T(8,128)(2,1)S(1)} collective-permute-done((f16[2,512,128]{2,1,0:T(8,128)(2,1)S(1)}, f16[2,512,128]{2,1,0:T(8,128)(2,1)S(1)}, u32[]{:S(2)}, u32[]{:S(2)}) %collective-permute-start.16) | collective-permute-done | bytes 262176 | tf_op jit(solution)/shard_map/ppermute | solution.py:321
  185.5 1.5 collective-permute-start.17
  187.1 0.8 collective-permute-start.27
  188.0 2.5 %collective-permute-start.23 = (bf16[2,512,128]{2,1,0:T(8,128)(2,1)S(1)}, bf16[2,512,128]{2,1,0:T(8,128)(2,1)S(1)}, u32[]{:S(2)}, u32[]{:S(2)}) collective-permute-start(bf16[2,512,128]{2,1,0:T(8,128)(2,1)S(1)} %subtract_convert_fusion.1), channel_id=1, source_target_pairs={{0,8},{2,10},{4,12},{6,14},{8,0},{10,2},{12,4},{14,6},{16,24},{18,... | collective-permute-start | bytes 786440 | tf_op jit(solution)/shard_map/ppermute | solution.py:321
  191.1 9.4 %collective-permute-done.17 = f16[2,512,128]{2,1,0:T(8,128)(2,1)S(1)} collective-permute-done((f16[2,512,128]{2,1,0:T(8,128)(2,1)S(1)}, f16[2,512,128]{2,1,0:T(8,128)(2,1)S(1)}, u32[]{:S(2)}, u32[]{:S(2)}) %collective-permute-start.17) | collective-permute-done | bytes 262176 | tf_op jit(solution)/shard_map/ppermute | solution.py:321
  200.6 0.6 collective-permute-done.23
  201.3 1.4 collective-permute-start.24
  202.7 5.4 %collective-permute-done.18 = bf16[2,512,128]{2,1,0:T(8,128)(2,1)S(1)} collective-permute-done((bf16[2,512,128]{2,1,0:T(8,128)(2,1)S(1)}, bf16[2,512,128]{2,1,0:T(8,128)(2,1)S(1)}, u32[]{:S(2)}, u32[]{:S(2)}) %collective-permute-start.18) | collective-permute-done | bytes 262176 | tf_op jit(solution)/shard_map/ppermute | solution.py:321
  208.1 0.8 collective-permute-start.19
  208.9 1.4 assemble.4.refs_4_
  211.1 5.0 %collective-permute-done.24.refs_1_ = bf16[4,512,128]{2,1,0:T(8,128)(2,1)S(1)} collective-permute-done((bf16[4,512,128]{2,1,0:T(8,128)(2,1)S(1)}, bf16[4,512,128]{2,1,0:T(8,128)(2,1)S(1)}, u32[]{:S(2)}, u32[]{:S(2)}) %collective-permute-start.24) | collective-permute-done | bytes 524320 | tf_op jit(solution)/shard_map/ppermute | solution.py:321
  216.1 10.8 %collective-permute-done.19.refs_1_ = bf16[4,512,128]{2,1,0:T(8,128)(2,1)S(1)} collective-permute-done((bf16[4,512,128]{2,1,0:T(8,128)(2,1)S(1)}, bf16[4,512,128]{2,1,0:T(8,128)(2,1)S(1)}, u32[]{:S(2)}, u32[]{:S(2)}) %collective-permute-start.19) | collective-permute-done | bytes 524320 | tf_op jit(solution)/shard_map/ppermute | solution.py:321
  227.0 1.4 assemble.5.refs_4_
  229.1 1.0 pad_maximum_fusion
  230.5 1.4 assemble.6.refs_4_
  232.0 1.4 assemble.7
  (120 shorter events, 8.6 us)
Async XLA Ops:
  0.6 6.2 %copy-start.2 = (bf16[1,128,8192]{2,1,0:T(8,128)(2,1)S(1)}, bf16[1,128,8192]{2,1,0:T(8,128)(2,1)}, u32[]{:S(2)}) copy-start(bf16[1,128,8192]{2,1,0:T(8,128)(2,1)} %param.11) | copy-start | bytes 6291460
  0.6 9.9 %copy-start.21 = (s32[1,2,512]{2,1,0:T(2,128)S(1)}, s32[1,2,512]{2,1,0:T(2,128)}, u32[]{:S(2)}) copy-start(s32[1,2,512]{2,1,0:T(2,128)} %param.13) | copy-start | bytes 12292
  0.7 10.1 %copy-start.18 = (bf16[1,256,512]{2,1,0:T(8,128)(2,1)S(1)}, bf16[1,256,512]{2,1,0:T(8,128)(2,1)}, u32[]{:S(2)}) copy-start(bf16[1,256,512]{2,1,0:T(8,128)(2,1)} %param.12) | copy-start | bytes 786436
  3.8 31.0 %collective-permute-start.2 = (bf16[128,2048]{1,0:T(8,128)(2,1)}, bf16[128,2048]{1,0:T(8,128)(2,1)}, u32[]{:S(2)}, u32[]{:S(2)}) collective-permute-start(bf16[128,2048]{1,0:T(8,128)(2,1)} %slice.225), channel_id=1, source_target_pairs={{0,1},{1,0},{2,3},{3,2},{4,5},{5,4},{6,7},{7,6},{8,9},{9,8},{10,11... | collective-permute-start | bytes 1572872 | tf_op jit(solution)/shard_map/ppermute | solution.py:341
  6.8 24.2 %collective-permute-start.3 = (bf16[128,2048]{1,0:T(8,128)(2,1)S(1)}, bf16[128,2048]{1,0:T(8,128)(2,1)S(1)}, u32[]{:S(2)}, u32[]{:S(2)}) collective-permute-start(bf16[128,2048]{1,0:T(8,128)(2,1)S(1)} %slice.286), channel_id=1, source_target_pairs={{0,1},{1,0},{2,3},{3,2},{4,5},{5,4},{6,7},{7,6},{8,9},{9,8},{10,11... | collective-permute-start | bytes 1572872 | tf_op jit(solution)/shard_map/ppermute | solution.py:341
  7.7 34.6 %collective-permute-start.1 = (bf16[128,2048]{1,0:T(8,128)(2,1)}, bf16[128,2048]{1,0:T(8,128)(2,1)}, u32[]{:S(2)}, u32[]{:S(2)}) collective-permute-start(bf16[128,2048]{1,0:T(8,128)(2,1)} %slice.226), channel_id=1, source_target_pairs={{0,1},{1,0},{2,3},{3,2},{4,5},{5,4},{6,7},{7,6},{8,9},{9,8},{10,11... | collective-permute-start | bytes 1572872 | tf_op jit(solution)/shard_map/ppermute | solution.py:341
  10.5 42.2 %collective-permute-start = (bf16[128,2048]{1,0:T(8,128)(2,1)}, bf16[128,2048]{1,0:T(8,128)(2,1)}, u32[]{:S(2)}, u32[]{:S(2)}) collective-permute-start(bf16[128,2048]{1,0:T(8,128)(2,1)} %slice.227), channel_id=1, source_target_pairs={{0,1},{1,0},{2,3},{3,2},{4,5},{5,4},{6,7},{7,6},{8,9},{9,8},{10,11... | collective-permute-start | bytes 1572872 | tf_op jit(solution)/shard_map/ppermute | solution.py:341
  15.8 1.3 copy-start.5
  31.0 0.8 copy-start.13
  31.8 1.0 copy-start.14
  52.7 2.4 %copy-start.3 = (bf16[1,128,8192]{2,1,0:T(8,128)(2,1)S(1)}, bf16[1,128,8192]{2,1,0:T(8,128)(2,1)}, u32[]{:S(2)}) copy-start(bf16[1,128,8192]{2,1,0:T(8,128)(2,1)} %param.11) | copy-start | bytes 6291460
  52.7 3.0 %copy-start.6 = (bf16[8192,128]{1,0:T(8,128)(2,1)S(1)}, bf16[8192,128]{1,0:T(8,128)(2,1)}, u32[]{:S(2)}) copy-start(bf16[8192,128]{1,0:T(8,128)(2,1)} %copy-done.5) | copy-start | bytes 6291460
  55.1 25.5 %copy-start = (bf16[8192,128]{1,0:T(8,128)(2,1)}, bf16[8192,128]{1,0:T(8,128)(2,1)S(1)}, u32[]{:S(2)}) copy-start(bf16[8192,128]{1,0:T(8,128)(2,1)S(1)} %get-tuple-element.79) | copy-start | bytes 6291460
  74.2 2.9 %copy-start.8 = (f32[8,512,128]{2,1,0:T(8,128)}, f32[8,512,128]{2,1,0:T(8,128)S(1)}, u32[]{:S(2)}) copy-start(f32[8,512,128]{2,1,0:T(8,128)S(1)} %get-tuple-element.84) | copy-start | bytes 6291460
  74.2 19.6 %copy-start.12 = (f32[8,512,128]{2,1,0:T(8,128)}, f32[8,512,128]{2,1,0:T(8,128)S(1)}, u32[]{:S(2)}) copy-start(f32[8,512,128]{2,1,0:T(8,128)S(1)} %get-tuple-element.82) | copy-start | bytes 6291460
  74.4 2.7 %collective-permute-start.5 = (f16[8,512,128]{2,1,0:T(8,128)(2,1)S(1)}, f16[8,512,128]{2,1,0:T(8,128)(2,1)S(1)}, u32[]{:S(2)}, u32[]{:S(2)}) collective-permute-start(f16[8,512,128]{2,1,0:T(8,128)(2,1)S(1)} %convert_element_type.208), channel_id=1, source_target_pairs={{0,2},{2,0},{4,6},{6,4},{8,10},{10,8},{12,14},{14,12},{16,18},{18,... | collective-permute-start | bytes 3145736 | tf_op jit(solution)/shard_map/ppermute | solution.py:321
  74.6 4.0 %collective-permute-start.4 = (f16[8,512,128]{2,1,0:T(8,128)(2,1)S(1)}, f16[8,512,128]{2,1,0:T(8,128)(2,1)S(1)}, u32[]{:S(2)}, u32[]{:S(2)}) collective-permute-start(f16[8,512,128]{2,1,0:T(8,128)(2,1)S(1)} %convert_element_type.204), channel_id=1, source_target_pairs={{0,2},{2,0},{4,6},{6,4},{8,10},{10,8},{12,14},{14,12},{16,18},{18,... | collective-permute-start | bytes 3145736 | tf_op jit(solution)/shard_map/ppermute | solution.py:321
  77.1 1.6 copy-start.15
  78.6 15.2 %copy-start.17 = (f16[8,512,128]{2,1,0:T(8,128)(2,1)}, f16[8,512,128]{2,1,0:T(8,128)(2,1)S(1)}, u32[]{:S(2)}) copy-start(f16[8,512,128]{2,1,0:T(8,128)(2,1)S(1)} %collective-permute-done.4) | copy-start | bytes 3145732
  78.7 15.0 %collective-permute-start.6 = (f16[4,512,128]{2,1,0:T(8,128)(2,1)S(1)}, f16[4,512,128]{2,1,0:T(8,128)(2,1)S(1)}, u32[]{:S(2)}, u32[]{:S(2)}) collective-permute-start(f16[4,512,128]{2,1,0:T(8,128)(2,1)S(1)} %add_convert_fusion.3), channel_id=1, source_target_pairs={{0,4},{2,6},{4,0},{6,2},{8,12},{10,14},{12,8},{14,10},{16,20},{18,... | collective-permute-start | bytes 1572872 | tf_op jit(solution)/shard_map/ppermute | solution.py:321
  92.4 1.7 copy-start.10
  93.8 0.8 copy-start.19
  94.6 3.0 %collective-permute-start.7 = (f16[8,512,128]{2,1,0:T(8,128)(2,1)}, f16[8,512,128]{2,1,0:T(8,128)(2,1)}, u32[]{:S(2)}, u32[]{:S(2)}) collective-permute-start(f16[8,512,128]{2,1,0:T(8,128)(2,1)} %convert_element_type.213), channel_id=1, source_target_pairs={{0,2},{2,0},{4,6},{6,4},{8,10},{10,8},{12,14},{14,12},{16,18},{18,... | collective-permute-start | bytes 3145736 | tf_op jit(solution)/shard_map/ppermute | solution.py:321
  94.6 3.0 %copy-start.11 = (f32[8,512,128]{2,1,0:T(8,128)S(1)}, f32[8,512,128]{2,1,0:T(8,128)}, u32[]{:S(2)}) copy-start(f32[8,512,128]{2,1,0:T(8,128)} %copy-done.10) | copy-start | bytes 6291460
  97.6 6.6 %copy-start.7 = (bf16[8192,128]{1,0:T(8,128)(2,1)S(1)}, bf16[8192,128]{1,0:T(8,128)(2,1)}, u32[]{:S(2)}) copy-start(bf16[8192,128]{1,0:T(8,128)(2,1)} %copy-done.5) | copy-start | bytes 6291460
  98.9 5.2 %copy-start.1 = (bf16[8192,128]{1,0:T(8,128)(2,1)S(1)}, bf16[8192,128]{1,0:T(8,128)(2,1)}, u32[]{:S(2)}) copy-start(bf16[8192,128]{1,0:T(8,128)(2,1)} %copy-done) | copy-start | bytes 6291460
  98.9 5.2 %copy-start.4 = (bf16[1,128,8192]{2,1,0:T(8,128)(2,1)S(1)}, bf16[1,128,8192]{2,1,0:T(8,128)(2,1)}, u32[]{:S(2)}) copy-start(bf16[1,128,8192]{2,1,0:T(8,128)(2,1)} %param.11) | copy-start | bytes 6291460
  99.0 17.5 %collective-permute-start.10 = (f16[4,512,128]{2,1,0:T(8,128)(2,1)S(1)}, f16[4,512,128]{2,1,0:T(8,128)(2,1)S(1)}, u32[]{:S(2)}, u32[]{:S(2)}) collective-permute-start(f16[4,512,128]{2,1,0:T(8,128)(2,1)S(1)} %add_convert_fusion.1), channel_id=1, source_target_pairs={{0,4},{2,6},{4,0},{6,2},{8,12},{10,14},{12,8},{14,10},{16,20},{18,... | collective-permute-start | bytes 1572872 | tf_op jit(solution)/shard_map/ppermute | solution.py:321
  99.7 24.5 %collective-permute-start.9 = (f16[4,512,128]{2,1,0:T(8,128)(2,1)}, f16[4,512,128]{2,1,0:T(8,128)(2,1)S(1)}, u32[]{:S(2)}, u32[]{:S(2)}) collective-permute-start(f16[4,512,128]{2,1,0:T(8,128)(2,1)} %add_convert_fusion.2), channel_id=1, source_target_pairs={{0,4},{2,6},{4,0},{6,2},{8,12},{10,14},{12,8},{14,10},{16,20},{18,... | collective-permute-start | bytes 1572872 | tf_op jit(solution)/shard_map/ppermute | solution.py:321
  102.3 14.2 %collective-permute-start.8 = (f16[2,512,128]{2,1,0:T(8,128)(2,1)S(1)}, f16[2,512,128]{2,1,0:T(8,128)(2,1)S(1)}, u32[]{:S(2)}, u32[]{:S(2)}) collective-permute-start(f16[2,512,128]{2,1,0:T(8,128)(2,1)S(1)} %add_convert_fusion.7), channel_id=1, source_target_pairs={{0,8},{2,10},{4,12},{6,14},{8,0},{10,2},{12,4},{14,6},{16,24},{18,... | collective-permute-start | bytes 786440 | tf_op jit(solution)/shard_map/ppermute | solution.py:321
  116.3 7.9 %copy-start.20 = (f16[4,512,128]{2,1,0:T(8,128)(2,1)S(1)}, f16[4,512,128]{2,1,0:T(8,128)(2,1)}, u32[]{:S(2)}) copy-start(f16[4,512,128]{2,1,0:T(8,128)(2,1)} %copy-done.19) | copy-start | bytes 1572868
  116.5 10.2 %copy-start.9 = (f32[8,512,128]{2,1,0:T(8,128)S(1)}, f32[8,512,128]{2,1,0:T(8,128)}, u32[]{:S(2)}) copy-start(f32[8,512,128]{2,1,0:T(8,128)} %copy-done.8) | copy-start | bytes 6291460
  116.5 10.2 %copy-start.16 = (f16[8,512,128]{2,1,0:T(8,128)(2,1)S(1)}, f16[8,512,128]{2,1,0:T(8,128)(2,1)}, u32[]{:S(2)}) copy-start(f16[8,512,128]{2,1,0:T(8,128)(2,1)} %copy-done.15) | copy-start | bytes 3145732
  126.8 4.8 %collective-permute-start.11 = (f16[8,512,128]{2,1,0:T(8,128)(2,1)S(1)}, f16[8,512,128]{2,1,0:T(8,128)(2,1)S(1)}, u32[]{:S(2)}, u32[]{:S(2)}) collective-permute-start(f16[8,512,128]{2,1,0:T(8,128)(2,1)S(1)} %convert_element_type.216), channel_id=1, source_target_pairs={{0,2},{2,0},{4,6},{6,4},{8,10},{10,8},{12,14},{14,12},{16,18},{18,... | collective-permute-start | bytes 3145736 | tf_op jit(solution)/shard_map/ppermute | solution.py:321
  126.9 14.8 %collective-permute-start.15 = (f16[2,512,128]{2,1,0:T(8,128)(2,1)S(1)}, f16[2,512,128]{2,1,0:T(8,128)(2,1)S(1)}, u32[]{:S(2)}, u32[]{:S(2)}) collective-permute-start(f16[2,512,128]{2,1,0:T(8,128)(2,1)S(1)} %add_convert_fusion.5), channel_id=1, source_target_pairs={{0,8},{2,10},{4,12},{6,14},{8,0},{10,2},{12,4},{14,6},{16,24},{18,... | collective-permute-start | bytes 786440 | tf_op jit(solution)/shard_map/ppermute | solution.py:321
  128.5 18.3 %collective-permute-start.14 = (f16[2,512,128]{2,1,0:T(8,128)(2,1)S(1)}, f16[2,512,128]{2,1,0:T(8,128)(2,1)S(1)}, u32[]{:S(2)}, u32[]{:S(2)}) collective-permute-start(f16[2,512,128]{2,1,0:T(8,128)(2,1)S(1)} %add_convert_fusion.6), channel_id=1, source_target_pairs={{0,8},{2,10},{4,12},{6,14},{8,0},{10,2},{12,4},{14,6},{16,24},{18,... | collective-permute-start | bytes 786440 | tf_op jit(solution)/shard_map/ppermute | solution.py:321
  129.0 17.9 %collective-permute-start.13 = (f16[2,512,128]{2,1,0:T(8,128)(2,1)S(1)}, f16[2,512,128]{2,1,0:T(8,128)(2,1)S(1)}, u32[]{:S(2)}, u32[]{:S(2)}) collective-permute-start(f16[2,512,128]{2,1,0:T(8,128)(2,1)S(1)} %pad_maximum_fusion.6), channel_id=1, source_target_pairs={{0,16},{2,18},{4,20},{6,22},{8,24},{10,26},{12,28},{14,30},{16,0},... | collective-permute-start | bytes 786440 | tf_op jit(solution)/shard_map/ppermute | solution.py:321
  131.7 38.2 %collective-permute-start.12 = (f16[4,512,128]{2,1,0:T(8,128)(2,1)S(1)}, f16[4,512,128]{2,1,0:T(8,128)(2,1)S(1)}, u32[]{:S(2)}, u32[]{:S(2)}) collective-permute-start(f16[4,512,128]{2,1,0:T(8,128)(2,1)S(1)} %add_convert_fusion), channel_id=1, source_target_pairs={{0,4},{2,6},{4,0},{6,2},{8,12},{10,14},{12,8},{14,10},{16,20},{18,... | collective-permute-start | bytes 1572872 | tf_op jit(solution)/shard_map/ppermute | solution.py:321
  148.3 21.4 %collective-permute-start.25 = (f16[2,512,128]{2,1,0:T(8,128)(2,1)S(1)}, f16[2,512,128]{2,1,0:T(8,128)(2,1)S(1)}, u32[]{:S(2)}, u32[]{:S(2)}) collective-permute-start(f16[2,512,128]{2,1,0:T(8,128)(2,1)S(1)} %get-tuple-element.134), channel_id=1, source_target_pairs={{0,16},{2,18},{4,20},{6,22},{8,24},{10,26},{12,28},{14,30},{16,0},... | collective-permute-start | bytes 786440 | tf_op jit(solution)/shard_map/ppermute | solution.py:321
  150.9 23.3 %collective-permute-start.22 = (f16[2,512,128]{2,1,0:T(8,128)(2,1)S(1)}, f16[2,512,128]{2,1,0:T(8,128)(2,1)S(1)}, u32[]{:S(2)}, u32[]{:S(2)}) collective-permute-start(f16[2,512,128]{2,1,0:T(8,128)(2,1)S(1)} %get-tuple-element.135), channel_id=1, source_target_pairs={{0,16},{2,18},{4,20},{6,22},{8,24},{10,26},{12,28},{14,30},{16,0},... | collective-permute-start | bytes 786440 | tf_op jit(solution)/shard_map/ppermute | solution.py:321
  151.5 22.7 %collective-permute-start.28 = (bf16[2,512,128]{2,1,0:T(8,128)(2,1)S(1)}, bf16[2,512,128]{2,1,0:T(8,128)(2,1)S(1)}, u32[]{:S(2)}, u32[]{:S(2)}) collective-permute-start(bf16[2,512,128]{2,1,0:T(8,128)(2,1)S(1)} %subtract_convert_fusion.3), channel_id=1, source_target_pairs={{0,8},{2,10},{4,12},{6,14},{8,0},{10,2},{12,4},{14,6},{16,24},{18,... | collective-permute-start | bytes 786440 | tf_op jit(solution)/shard_map/ppermute | solution.py:321
  169.9 9.9 %collective-permute-start.26 = (bf16[2,512,128]{2,1,0:T(8,128)(2,1)S(1)}, bf16[2,512,128]{2,1,0:T(8,128)(2,1)S(1)}, u32[]{:S(2)}, u32[]{:S(2)}) collective-permute-start(bf16[2,512,128]{2,1,0:T(8,128)(2,1)S(1)} %subtract_convert_fusion), channel_id=1, source_target_pairs={{0,8},{2,10},{4,12},{6,14},{8,0},{10,2},{12,4},{14,6},{16,24},{18,... | collective-permute-start | bytes 786440 | tf_op jit(solution)/shard_map/ppermute | solution.py:321
  170.1 15.2 %collective-permute-start.16 = (f16[2,512,128]{2,1,0:T(8,128)(2,1)S(1)}, f16[2,512,128]{2,1,0:T(8,128)(2,1)S(1)}, u32[]{:S(2)}, u32[]{:S(2)}) collective-permute-start(f16[2,512,128]{2,1,0:T(8,128)(2,1)S(1)} %add_convert_fusion.4), channel_id=1, source_target_pairs={{0,8},{2,10},{4,12},{6,14},{8,0},{10,2},{12,4},{14,6},{16,24},{18,... | collective-permute-start | bytes 786440 | tf_op jit(solution)/shard_map/ppermute | solution.py:321
  174.2 16.4 %collective-permute-start.29 = (bf16[4,512,128]{2,1,0:T(8,128)(2,1)S(1)}, bf16[4,512,128]{2,1,0:T(8,128)(2,1)S(1)}, u32[]{:S(2)}, u32[]{:S(2)}) collective-permute-start(bf16[4,512,128]{2,1,0:T(8,128)(2,1)S(1)} %pad_maximum_fusion.4.refs_0_), channel_id=1, source_target_pairs={{0,4},{2,6},{4,0},{6,2},{8,12},{10,14},{12,8},{14,10},{16,20},{18,... | collective-permute-start | bytes 1572872 | tf_op jit(solution)/shard_map/ppermute | solution.py:321
  185.5 14.9 %collective-permute-start.17 = (f16[2,512,128]{2,1,0:T(8,128)(2,1)S(1)}, f16[2,512,128]{2,1,0:T(8,128)(2,1)S(1)}, u32[]{:S(2)}, u32[]{:S(2)}) collective-permute-start(f16[2,512,128]{2,1,0:T(8,128)(2,1)S(1)} %pad_maximum_fusion.9), channel_id=1, source_target_pairs={{0,16},{2,18},{4,20},{6,22},{8,24},{10,26},{12,28},{14,30},{16,0},... | collective-permute-start | bytes 786440 | tf_op jit(solution)/shard_map/ppermute | solution.py:321
  187.1 14.2 %collective-permute-start.27 = (bf16[4,512,128]{2,1,0:T(8,128)(2,1)S(1)}, bf16[4,512,128]{2,1,0:T(8,128)(2,1)S(1)}, u32[]{:S(2)}, u32[]{:S(2)}) collective-permute-start(bf16[4,512,128]{2,1,0:T(8,128)(2,1)S(1)} %pad_maximum_fusion.3.refs_0_), channel_id=1, source_target_pairs={{0,4},{2,6},{4,0},{6,2},{8,12},{10,14},{12,8},{14,10},{16,20},{18,... | collective-permute-start | bytes 1572872 | tf_op jit(solution)/shard_map/ppermute | solution.py:321
  188.0 13.3 %collective-permute-start.23 = (bf16[2,512,128]{2,1,0:T(8,128)(2,1)S(1)}, bf16[2,512,128]{2,1,0:T(8,128)(2,1)S(1)}, u32[]{:S(2)}, u32[]{:S(2)}) collective-permute-start(bf16[2,512,128]{2,1,0:T(8,128)(2,1)S(1)} %subtract_convert_fusion.1), channel_id=1, source_target_pairs={{0,8},{2,10},{4,12},{6,14},{8,0},{10,2},{12,4},{14,6},{16,24},{18,... | collective-permute-start | bytes 786440 | tf_op jit(solution)/shard_map/ppermute | solution.py:321
  190.6 18.4 %collective-permute-start.30 = (bf16[4,512,128]{2,1,0:T(8,128)(2,1)S(1)}, bf16[4,512,128]{2,1,0:T(8,128)(2,1)S(1)}, u32[]{:S(2)}, u32[]{:S(2)}) collective-permute-start(bf16[4,512,128]{2,1,0:T(8,128)(2,1)S(1)} %pad_maximum_fusion.4.refs_0_), channel_id=1, source_target_pairs={{0,2},{2,0},{4,6},{6,4},{8,10},{10,8},{12,14},{14,12},{16,18},{18,... | collective-permute-start | bytes 1572872 | tf_op jit(solution)/shard_map/ppermute | solution.py:321
  190.6 18.4 %collective-permute-start.31 = (bf16[4,512,128]{2,1,0:T(8,128)(2,1)S(1)}, bf16[4,512,128]{2,1,0:T(8,128)(2,1)S(1)}, u32[]{:S(2)}, u32[]{:S(2)}) collective-permute-start(bf16[4,512,128]{2,1,0:T(8,128)(2,1)S(1)} %collective-permute-done.29.refs_1_), channel_id=1, source_target_pairs={{0,2},{2,0},{4,6},{6,4},{8,10},{10,8},{12,14},{14,12},{16,18},{18,... | collective-permute-start | bytes 1572872 | tf_op jit(solution)/shard_map/ppermute | solution.py:321
  200.6 7.5 %collective-permute-start.18 = (bf16[2,512,128]{2,1,0:T(8,128)(2,1)S(1)}, bf16[2,512,128]{2,1,0:T(8,128)(2,1)S(1)}, u32[]{:S(2)}, u32[]{:S(2)}) collective-permute-start(bf16[2,512,128]{2,1,0:T(8,128)(2,1)S(1)} %subtract_convert_fusion.2), channel_id=1, source_target_pairs={{0,8},{2,10},{4,12},{6,14},{8,0},{10,2},{12,4},{14,6},{16,24},{18,... | collective-permute-start | bytes 786440 | tf_op jit(solution)/shard_map/ppermute | solution.py:321
  201.3 25.7 %collective-permute-start.32 = (bf16[4,512,128]{2,1,0:T(8,128)(2,1)S(1)}, bf16[4,512,128]{2,1,0:T(8,128)(2,1)S(1)}, u32[]{:S(2)}, u32[]{:S(2)}) collective-permute-start(bf16[4,512,128]{2,1,0:T(8,128)(2,1)S(1)} %pad_maximum_fusion.3.refs_0_), channel_id=1, source_target_pairs={{0,2},{2,0},{4,6},{6,4},{8,10},{10,8},{12,14},{14,12},{16,18},{18,... | collective-permute-start | bytes 1572872 | tf_op jit(solution)/shard_map/ppermute | solution.py:321
  201.3 14.8 %collective-permute-start.24 = (bf16[4,512,128]{2,1,0:T(8,128)(2,1)S(1)}, bf16[4,512,128]{2,1,0:T(8,128)(2,1)S(1)}, u32[]{:S(2)}, u32[]{:S(2)}) collective-permute-start(bf16[4,512,128]{2,1,0:T(8,128)(2,1)S(1)} %pad_maximum_fusion.2.refs_0_), channel_id=1, source_target_pairs={{0,4},{2,6},{4,0},{6,2},{8,12},{10,14},{12,8},{14,10},{16,20},{18,... | collective-permute-start | bytes 1572872 | tf_op jit(solution)/shard_map/ppermute | solution.py:321
  208.1 18.8 %collective-permute-start.19 = (bf16[4,512,128]{2,1,0:T(8,128)(2,1)S(1)}, bf16[4,512,128]{2,1,0:T(8,128)(2,1)S(1)}, u32[]{:S(2)}, u32[]{:S(2)}) collective-permute-start(bf16[4,512,128]{2,1,0:T(8,128)(2,1)S(1)} %pad_maximum_fusion.1.refs_0_), channel_id=1, source_target_pairs={{0,4},{2,6},{4,0},{6,2},{8,12},{10,14},{12,8},{14,10},{16,20},{18,... | collective-permute-start | bytes 1572872 | tf_op jit(solution)/shard_map/ppermute | solution.py:321
  210.4 16.6 %collective-permute-start.33 = (bf16[4,512,128]{2,1,0:T(8,128)(2,1)S(1)}, bf16[4,512,128]{2,1,0:T(8,128)(2,1)S(1)}, u32[]{:S(2)}, u32[]{:S(2)}) collective-permute-start(bf16[4,512,128]{2,1,0:T(8,128)(2,1)S(1)} %collective-permute-done.27.refs_1_), channel_id=1, source_target_pairs={{0,2},{2,0},{4,6},{6,4},{8,10},{10,8},{12,14},{14,12},{16,18},{18,... | collective-permute-start | bytes 1572872 | tf_op jit(solution)/shard_map/ppermute | solution.py:321
  210.6 19.6 %collective-permute-start.34 = (bf16[4,512,128]{2,1,0:T(8,128)(2,1)S(1)}, bf16[4,512,128]{2,1,0:T(8,128)(2,1)S(1)}, u32[]{:S(2)}, u32[]{:S(2)}) collective-permute-start(bf16[4,512,128]{2,1,0:T(8,128)(2,1)S(1)} %pad_maximum_fusion.2.refs_0_), channel_id=1, source_target_pairs={{0,2},{2,0},{4,6},{6,4},{8,10},{10,8},{12,14},{14,12},{16,18},{18,... | collective-permute-start | bytes 1572872 | tf_op jit(solution)/shard_map/ppermute | solution.py:321
  216.1 15.9 %collective-permute-start.20 = (bf16[4,512,128]{2,1,0:T(8,128)(2,1)S(1)}, bf16[4,512,128]{2,1,0:T(8,128)(2,1)S(1)}, u32[]{:S(2)}, u32[]{:S(2)}) collective-permute-start(bf16[4,512,128]{2,1,0:T(8,128)(2,1)S(1)} %pad_maximum_fusion.1.refs_0_), channel_id=1, source_target_pairs={{0,2},{2,0},{4,6},{6,4},{8,10},{10,8},{12,14},{14,12},{16,18},{18,... | collective-permute-start | bytes 1572872 | tf_op jit(solution)/shard_map/ppermute | solution.py:321
  227.0 5.0 %collective-permute-start.21 = (bf16[4,512,128]{2,1,0:T(8,128)(2,1)S(1)}, bf16[4,512,128]{2,1,0:T(8,128)(2,1)S(1)}, u32[]{:S(2)}, u32[]{:S(2)}) collective-permute-start(bf16[4,512,128]{2,1,0:T(8,128)(2,1)S(1)} %collective-permute-done.19.refs_1_), channel_id=1, source_target_pairs={{0,2},{2,0},{4,6},{6,4},{8,10},{10,8},{12,14},{14,12},{16,18},{18,... | collective-permute-start | bytes 1572872 | tf_op jit(solution)/shard_map/ppermute | solution.py:321
  228.4 2.1 collective-permute-start.35

commit v11 on v9

--- a/solution.py
+++ b/solution.py
@@ -110,6 +110,7 @@
 
 def inner_kernel(
     tokens,
+    kept,
     mine_ref,
     low_ref,
     high_ref,
@@ -124,7 +125,8 @@
     count_ref,
     *rest,
 ):
-    *change_refs, first_state, second_state, output_state, residual_state, gradient_state, rounded_state = rest
+    *rest, first_state, second_state, output_state, residual_state, gradient_state, rounded_state = rest
+    change_refs, weights_state = (rest[:-1], rest[-1]) if kept else (rest, None)
     send_refs, keep_refs = change_refs[::2], change_refs[1::2]
     step = pl.program_id(0)
     slab = pl.program_id(1)
@@ -182,6 +184,8 @@
                 weights = descend(first, second, start_ref[pair, which, piece].astype(F32))
                 first_state[slab, pair, which, piece] = first
                 second_state[slab, pair, which, piece] = second
+                if kept:
+                    weights_state[slab, pair, which, piece] = weights
                 rounded_state[slot % held, piece] = weights.astype(BF16)
             output_state[...] += project(slot)
 
@@ -200,7 +204,10 @@
                 first = first_state[slab, pair, which, piece]
                 second = second_state[slab, pair, which, piece]
                 start = start_ref[pair, which, piece].astype(F32)
-                weights = descend(first, second, start)
+                if kept:
+                    weights = weights_state[slab, pair, which, piece]
+                else:
+                    weights = descend(first, second, start)
                 first = 0.9 * first + gradient
                 second = 0.95 * second + gradient * gradient
                 change = (start - descend(first, second, weights)) * WIRE_SCALE
@@ -222,9 +229,10 @@
     product = pl.BlockSpec((half, width), lambda s, z, c: (0, call))
     change = jax.ShapeDtypeStruct((slabs * pairs, rows, part), F32)
     outputs = 2 * (width // part)
+    kept = width == part
     elements = depth * width
     return pl.pallas_call(
-        functools.partial(inner_kernel, float(tokens)),
+        functools.partial(inner_kernel, float(tokens), kept),
         grid_spec=pltpu.PrefetchScalarGridSpec(
             num_scalar_prefetch=1,
             grid=(2, slabs),
@@ -239,9 +247,8 @@
                 pl.BlockSpec(count.shape, lambda s, z, c: (0, 0, 0)),
             ],
             out_specs=[whole] * outputs,
-            scratch_shapes=[
-                pltpu.VMEM((slabs, pairs, cores, rows, width), F32),
-                pltpu.VMEM((slabs, pairs, cores, rows, width), F32),
+            scratch_shapes=[pltpu.VMEM((slabs, pairs, cores, rows, width), F32)] * (2 + kept)
+            + [
                 pltpu.VMEM((2 * half, width), F32),
                 pltpu.VMEM((2 * half, width), BF16),
                 pltpu.VMEM((2, rows, width), F32),
@@ -438,7 +445,10 @@
             formed[chunk] = next(running[chunk])
         if fresh.stop < chunks:
             formed, token = tied(formed, token)
-    move_on(range(fresh[0]), behind=fresh)
+    others = range(fresh[0])
+    move_on(others, behind=fresh)
+    move_on(fresh, behind=others)
+    move_on(others, behind=fresh)
     for chunk in range(chunks):
         while chunk not in finished:
             move_on([chunk])
@@ -446,7 +456,7 @@
     for chunk in range(chunks):
         _, stack, across, offsets = finished[chunk]
         offsets = [[offset ^ low for offset in offsets] for low in (0, 2, 1, 3)]
-        if result:
+        if result and chunk + 1 < chunks:
             across, *result = tied(across, result[0])
         received = [stack, across, swapped(stack, 1), swapped(across, 1)]
         result = (

time: 219 us -> 220 us (level)
  waiting for transfers between devices: 92.4 us -> 97.1 us
    ppermute x32, waiting for transfers between devices: 65.6 us -> 70.2 us  [swapped(): return lax.ppermute(array, 'rep', pairs)]
  transfers between devices with their start and end apart: 36 -> 36, of which waited for: 18 -> 19; matrix products, arithmetic and copies ran while one was open for 7% -> 7% of each run, Pallas kernels for 21% -> 21%
where the time goes in v11:
time: 220 us; the launch traced here: 219 us
  waiting for transfers between devices  97.1 us (44%)
  Pallas kernels  60 us (27%)
  starting transfers between devices  32.6 us (15%)
  other arithmetic  14.6 us (7%)
  local copies, waits for them, and re-layouts  13.4 us (6%)
    ppermute x32, waiting for transfers between devices, swapped(): return lax.ppermute(array, 'rep', pairs)  70.2 us
    pallas_call x3, Pallas kernels, inner(): pl.pallas_call(functools.partial(inner_kernel, float(tokens), kept), grid...  40.5 us
    ppermute x32, starting transfers between devices, swapped(): return lax.ppermute(array, 'rep', pairs)  27.6 us
    ppermute x4, waiting for transfers between devices, per_device(): parts.append(lax.ppermute(part, 'fsdp', [(0, 1), (1, 0)]))  26.9 us
    pallas_call x4, Pallas kernels, arrive(): pl.pallas_call(functools.partial(arrive_kernel, piece), grid=(1,), in_spe...  8.81 us
    pallas_call x4, Pallas kernels, assemble(): pl.pallas_call(functools.partial(assemble_kernel, begin, offsets), in_spe...  5.76 us
    unnamed x40, local copies, waits for them, and re-layouts  5.35 us
    convert_element_type x8, other arithmetic, parted(): sum((term.astype(F32) for term in part)).astype(WIRE)  5.17 us
  transfers between devices with their start and end apart: 36, of which 19 were waited for; matrix products, arithmetic and copies ran while one was open for 7% of the time, Pallas kernels for 21%

profile of v11, /device:TPU:0, one launch (start us, length us, event | category | flops | bytes accessed | tf_op | source)
XLA Modules:
  0.0 219.1 jit_solution(7890128874410391112)
XLA Ops:
  0.7 1.2 slice.286
  1.9 1.9 slice.225
  3.8 3.0 %collective-permute-start.2 = (bf16[128,2048]{1,0:T(8,128)(2,1)}, bf16[128,2048]{1,0:T(8,128)(2,1)}, u32[]{:S(2)}, u32[]{:S(2)}) collective-permute-start(bf16[128,2048]{1,0:T(8,128)(2,1)} %slice.225), channel_id=1, source_target_pairs={{0,1},{1,0},{2,3},{3,2},{4,5},{5,4},{6,7},{7,6},{8,9},{9,8},{10,11... | collective-permute-start | bytes 1572872 | tf_op jit(solution)/shard_map/ppermute | solution.py:348
  6.8 0.8 slice.226
  7.6 2.0 collective-permute-start.1
  9.6 0.8 slice.227
  10.8 5.0 %forward.1 = (bf16[8192,128]{1,0:T(8,128)(2,1)S(1)}, f32[128,512]{1,0:T(8,128)S(1)}) custom-call(bf16[128,8192]{1,0:T(8,128)(2,1)S(1)} %bitcast.88, bf16[8192,512]{1,0:T(8,128)(2,1)} %weights_ref.9), custom_call_target="tpu_custom_call" | custom-call | flops 1073741824 | bytes 12582912 | tf_op jit(solution)/shard_map/forward/pallas_call | solution.py:34
  15.8 1.3 copy-done.5
  17.5 13.4 %collective-permute-done.3.part_ref = bf16[128,2048]{1,0:T(8,128)(2,1)S(1)} collective-permute-done((bf16[128,2048]{1,0:T(8,128)(2,1)S(1)}, bf16[128,2048]{1,0:T(8,128)(2,1)S(1)}, u32[]{:S(2)}, u32[]{:S(2)}) %collective-permute-start.3) | collective-permute-done | bytes 524320 | tf_op jit(solution)/shard_map/ppermute | solution.py:348
  31.0 0.8 copy-done.13
  31.7 1.0 copy-done.14
  32.8 2.0 arrive.4
  34.8 2.2 %arrive.5 = (bf16[128,8192]{1,0:T(8,128)(2,1)S(1)}, bf16[8192,128]{1,0:T(8,128)(2,1)S(1)}, f32[128,512]{1,0:T(8,128)S(1)}) custom-call(bf16[128,2048]{1,0:T(8,128)(2,1)} %collective-permute-done.2.part_ref, bf16[8192,512]{1,0:T(8,128)(2,1)} %weights_ref.9, ...), custom_call_target="tpu_custom_call", output_to_operand_aliasing={{0}: (2, {}), {1}: (3, {}), {2}: (4, {})} | custom-call | flops 268435456 | bytes 3670016 | tf_op jit(solution)/shard_map/arrive/pallas_call | solution.py:76
  37.1 5.2 %collective-permute-done.1.part_ref = bf16[128,2048]{1,0:T(8,128)(2,1)} collective-permute-done((bf16[128,2048]{1,0:T(8,128)(2,1)}, bf16[128,2048]{1,0:T(8,128)(2,1)}, u32[]{:S(2)}, u32[]{:S(2)}) %collective-permute-start.1) | collective-permute-done | bytes 524320 | tf_op jit(solution)/shard_map/ppermute | solution.py:348
  42.3 2.2 %arrive.6 = (bf16[128,8192]{1,0:T(8,128)(2,1)S(1)}, bf16[8192,128]{1,0:T(8,128)(2,1)S(1)}, f32[128,512]{1,0:T(8,128)S(1)}) custom-call(bf16[128,2048]{1,0:T(8,128)(2,1)} %collective-permute-done.1.part_ref, bf16[8192,512]{1,0:T(8,128)(2,1)} %weights_ref.9, ...), custom_call_target="tpu_custom_call", output_to_operand_aliasing={{0}: (2, {}), {1}: (3, {}), {2}: (4, {})} | custom-call | flops 268435456 | bytes 3670016 | tf_op jit(solution)/shard_map/arrive/pallas_call | solution.py:76
  44.5 8.2 %collective-permute-done.part_ref = bf16[128,2048]{1,0:T(8,128)(2,1)} collective-permute-done((bf16[128,2048]{1,0:T(8,128)(2,1)}, bf16[128,2048]{1,0:T(8,128)(2,1)}, u32[]{:S(2)}, u32[]{:S(2)}) %collective-permute-start) | collective-permute-done | bytes 524320 | tf_op jit(solution)/shard_map/ppermute | solution.py:348
  52.7 2.3 %arrive.7 = (bf16[128,8192]{1,0:T(8,128)(2,1)S(1)}, bf16[8192,128]{1,0:T(8,128)(2,1)S(1)}, f32[128,512]{1,0:T(8,128)S(1)}) custom-call(bf16[128,2048]{1,0:T(8,128)(2,1)} %collective-permute-done.part_ref, bf16[8192,512]{1,0:T(8,128)(2,1)} %weights_ref.9, ...), custom_call_target="tpu_custom_call", output_to_operand_aliasing={{0}: (2, {}), {1}: (3, {}), {2}: (4, {})} | custom-call | flops 268435456 | bytes 3670016 | tf_op jit(solution)/shard_map/arrive/pallas_call | solution.py:76
  55.7 11.0 %inner.3 = (f32[8,512,128]{2,1,0:T(8,128)S(1)}, f32[8,512,128]{2,1,0:T(8,128)S(1)}) custom-call(s32[1]{0:T(128)} %bitcast.mine_ref.place_ref, bf16[128,8192]{1,0:T(8,128)(2,1)S(1)} %bitcast.89, bf16[128,8192]{1,0:T(8,128)(2,1)S(1)} %get-tuple-element.78.high_ref, bf16[4,2,2,512,128]{4,3,2,1,0:T(8,128)(2,1)S(1)} %bitcast.92, ...), custom_call_target="tpu_custom_call" | custom-call | flops 1610612736 | bytes 20971520 | tf_op jit(solution)/shard_map/inner/pallas_call | solution.py:234
  66.9 2.6 %collective-permute-done.4 = f16[8,512,128]{2,1,0:T(8,128)(2,1)S(1)} collective-permute-done((f16[8,512,128]{2,1,0:T(8,128)(2,1)S(1)}, f16[8,512,128]{2,1,0:T(8,128)(2,1)S(1)}, u32[]{:S(2)}, u32[]{:S(2)}) %collective-permute-start.4) | collective-permute-done | bytes 1048608 | tf_op jit(solution)/shard_map/ppermute | solution.py:328
  69.7 1.8 collective-permute-start.5
  71.5 18.4 %inner.4 = (f32[8,512,128]{2,1,0:T(8,128)S(1)}, f32[8,512,128]{2,1,0:T(8,128)S(1)}, f32[8,512,128]{2,1,0:T(8,128)S(1)}, f32[8,512,128]{2,1,0:T(8,128)S(1)}) custom-call(s32[1]{0:T(128)} %bitcast.mine_ref.place_ref, bf16[128,8192]{1,0:T(8,128)(2,1)S(1)} %bitcast.90, bf16[128,8192]{1,0:T(8,128)(2,1)S(1)} %get-tuple-element.78.high_ref, ...), custom_call_target="tpu_custom_call" | custom-call | flops 3221225472 | bytes 41943040 | tf_op jit(solution)/shard_map/inner/pallas_call | solution.py:234
  90.0 1.3 convert_element_type.210
  91.3 1.3 convert_element_type.211
  93.9 1.4 dynamic-slice_bitcast_fusion
  95.4 1.1 collective-permute-done.7
  96.4 1.2 add_convert_fusion.1
  97.9 1.3 add_convert_fusion.2
  99.7 1.5 fusion.15
  101.1 2.0 collective-permute-start.8
  103.3 11.1 %inner.5 = (f32[8,512,128]{2,1,0:T(8,128)S(1)}, f32[8,512,128]{2,1,0:T(8,128)S(1)}) custom-call(s32[1]{0:T(128)} %bitcast.mine_ref.place_ref, bf16[128,8192]{1,0:T(8,128)(2,1)S(1)} %bitcast.91, bf16[128,8192]{1,0:T(8,128)(2,1)S(1)} %get-tuple-element.78.high_ref, bf16[4,2,2,512,128]{4,3,2,1,0:T(8,128)(2,1)S(1)} %bitcast.94, ...), custom_call_target="tpu_custom_call" | custom-call | flops 1610612736 | bytes 20971520 | tf_op jit(solution)/shard_map/inner/pallas_call | solution.py:234
  114.6 0.9 copy-done.18
  115.5 1.2 convert_add_fusion.3
  116.9 1.1 add_convert_fusion.6
  118.0 1.3 collective-permute-start.14
  119.8 2.6 %collective-permute-start.12 = (f16[2,512,128]{2,1,0:T(8,128)(2,1)S(1)}, f16[2,512,128]{2,1,0:T(8,128)(2,1)S(1)}, u32[]{:S(2)}, u32[]{:S(2)}) collective-permute-start(f16[2,512,128]{2,1,0:T(8,128)(2,1)S(1)} %pad_maximum_fusion.6), channel_id=1, source_target_pairs={{0,16},{2,18},{4,20},{6,22},{8,24},{10,26},{12,28},{14,30},{16,0},... | collective-permute-start | bytes 786440 | tf_op jit(solution)/shard_map/ppermute | solution.py:328
  122.5 0.9 collective-permute-start.11
  123.4 9.4 %collective-permute-done.14 = f16[4,512,128]{2,1,0:T(8,128)(2,1)S(1)} collective-permute-done((f16[4,512,128]{2,1,0:T(8,128)(2,1)S(1)}, f16[4,512,128]{2,1,0:T(8,128)(2,1)S(1)}, u32[]{:S(2)}, u32[]{:S(2)}) %collective-permute-start.14) | collective-permute-done | bytes 524320 | tf_op jit(solution)/shard_map/ppermute | solution.py:328
  133.3 1.1 add_convert_fusion.5
  134.4 2.6 %collective-permute-start.23 = (f16[2,512,128]{2,1,0:T(8,128)(2,1)S(1)}, f16[2,512,128]{2,1,0:T(8,128)(2,1)S(1)}, u32[]{:S(2)}, u32[]{:S(2)}) collective-permute-start(f16[2,512,128]{2,1,0:T(8,128)(2,1)S(1)} %add_convert_fusion.5), channel_id=1, source_target_pairs={{0,8},{2,10},{4,12},{6,14},{8,0},{10,2},{12,4},{14,6},{16,24},{18,... | collective-permute-start | bytes 786440 | tf_op jit(solution)/shard_map/ppermute | solution.py:328
  137.0 1.1 convert_add_fusion.2
  138.2 2.8 %collective-permute-start.22 = (f16[2,512,128]{2,1,0:T(8,128)(2,1)S(1)}, f16[2,512,128]{2,1,0:T(8,128)(2,1)S(1)}, u32[]{:S(2)}, u32[]{:S(2)}) collective-permute-start(f16[2,512,128]{2,1,0:T(8,128)(2,1)S(1)} %pad_maximum_fusion.7), channel_id=1, source_target_pairs={{0,16},{2,18},{4,20},{6,22},{8,24},{10,26},{12,28},{14,30},{16,0},... | collective-permute-start | bytes 786440 | tf_op jit(solution)/shard_map/ppermute | solution.py:328
  141.2 2.4 %collective-permute-done.11 = f16[4,512,128]{2,1,0:T(8,128)(2,1)S(1)} collective-permute-done((f16[4,512,128]{2,1,0:T(8,128)(2,1)S(1)}, f16[4,512,128]{2,1,0:T(8,128)(2,1)S(1)}, u32[]{:S(2)}, u32[]{:S(2)}) %collective-permute-start.11) | collective-permute-done | bytes 524320 | tf_op jit(solution)/shard_map/ppermute | solution.py:328
  143.9 4.2 %collective-permute-done.23 = f16[2,512,128]{2,1,0:T(8,128)(2,1)S(1)} collective-permute-done((f16[2,512,128]{2,1,0:T(8,128)(2,1)S(1)}, f16[2,512,128]{2,1,0:T(8,128)(2,1)S(1)}, u32[]{:S(2)}, u32[]{:S(2)}) %collective-permute-start.23) | collective-permute-done | bytes 262176 | tf_op jit(solution)/shard_map/ppermute | solution.py:328
  148.1 4.1 %collective-permute-done.22 = f16[2,512,128]{2,1,0:T(8,128)(2,1)S(1)} collective-permute-done((f16[2,512,128]{2,1,0:T(8,128)(2,1)S(1)}, f16[2,512,128]{2,1,0:T(8,128)(2,1)S(1)}, u32[]{:S(2)}, u32[]{:S(2)}) %collective-permute-start.22) | collective-permute-done | bytes 262176 | tf_op jit(solution)/shard_map/ppermute | solution.py:328
  152.3 3.2 %collective-permute-done.21 = bf16[2,512,128]{2,1,0:T(8,128)(2,1)S(1)} collective-permute-done((bf16[2,512,128]{2,1,0:T(8,128)(2,1)S(1)}, bf16[2,512,128]{2,1,0:T(8,128)(2,1)S(1)}, u32[]{:S(2)}, u32[]{:S(2)}) %collective-permute-start.21) | collective-permute-done | bytes 262176 | tf_op jit(solution)/shard_map/ppermute | solution.py:328
  155.5 0.9 collective-permute-start.29
  156.4 1.1 convert_add_fusion
  157.6 2.8 %collective-permute-start.24 = (f16[2,512,128]{2,1,0:T(8,128)(2,1)S(1)}, f16[2,512,128]{2,1,0:T(8,128)(2,1)S(1)}, u32[]{:S(2)}, u32[]{:S(2)}) collective-permute-start(f16[2,512,128]{2,1,0:T(8,128)(2,1)S(1)} %pad_maximum_fusion.9), channel_id=1, source_target_pairs={{0,16},{2,18},{4,20},{6,22},{8,24},{10,26},{12,28},{14,30},{16,0},... | collective-permute-start | bytes 786440 | tf_op jit(solution)/shard_map/ppermute | solution.py:328
  160.6 2.0 collective-permute-start.27
  163.2 11.6 %collective-permute-done.27 = bf16[2,512,128]{2,1,0:T(8,128)(2,1)S(1)} collective-permute-done((bf16[2,512,128]{2,1,0:T(8,128)(2,1)S(1)}, bf16[2,512,128]{2,1,0:T(8,128)(2,1)S(1)}, u32[]{:S(2)}, u32[]{:S(2)}) %collective-permute-start.27) | collective-permute-done | bytes 262176 | tf_op jit(solution)/shard_map/ppermute | solution.py:328
  174.9 1.2 collective-permute-start.28
  176.7 7.7 %collective-permute-done.16 = f16[2,512,128]{2,1,0:T(8,128)(2,1)S(1)} collective-permute-done((f16[2,512,128]{2,1,0:T(8,128)(2,1)S(1)}, f16[2,512,128]{2,1,0:T(8,128)(2,1)S(1)}, u32[]{:S(2)}, u32[]{:S(2)}) %collective-permute-start.16) | collective-permute-done | bytes 262176 | tf_op jit(solution)/shard_map/ppermute | solution.py:328
  184.6 0.7 collective-permute-start.17
  185.3 1.5 collective-permute-done.25
  186.8 0.9 collective-permute-start.26
  187.8 4.8 %collective-permute-done.17 = bf16[2,512,128]{2,1,0:T(8,128)(2,1)S(1)} collective-permute-done((bf16[2,512,128]{2,1,0:T(8,128)(2,1)S(1)}, bf16[2,512,128]{2,1,0:T(8,128)(2,1)S(1)}, u32[]{:S(2)}, u32[]{:S(2)}) %collective-permute-start.17) | collective-permute-done | bytes 262176 | tf_op jit(solution)/shard_map/ppermute | solution.py:328
  192.6 1.3 collective-permute-start.18
  193.9 1.4 assemble.4.refs_4_
  196.1 5.6 %collective-permute-done.26.refs_1_ = bf16[4,512,128]{2,1,0:T(8,128)(2,1)S(1)} collective-permute-done((bf16[4,512,128]{2,1,0:T(8,128)(2,1)S(1)}, bf16[4,512,128]{2,1,0:T(8,128)(2,1)S(1)}, u32[]{:S(2)}, u32[]{:S(2)}) %collective-permute-start.26) | collective-permute-done | bytes 524320 | tf_op jit(solution)/shard_map/ppermute | solution.py:328
  201.6 10.8 %collective-permute-done.18.refs_1_ = bf16[4,512,128]{2,1,0:T(8,128)(2,1)S(1)} collective-permute-done((bf16[4,512,128]{2,1,0:T(8,128)(2,1)S(1)}, bf16[4,512,128]{2,1,0:T(8,128)(2,1)S(1)}, u32[]{:S(2)}, u32[]{:S(2)}) %collective-permute-start.18) | collective-permute-done | bytes 524320 | tf_op jit(solution)/shard_map/ppermute | solution.py:328
  212.5 1.4 assemble.5.refs_4_
  214.6 1.0 pad_maximum_fusion
  216.1 1.4 assemble.6.refs_4_
  217.5 1.4 assemble.7
  (117 shorter events, 9.7 us)
Async XLA Ops:
  0.6 6.2 %copy-start.2 = (bf16[1,128,8192]{2,1,0:T(8,128)(2,1)S(1)}, bf16[1,128,8192]{2,1,0:T(8,128)(2,1)}, u32[]{:S(2)}) copy-start(bf16[1,128,8192]{2,1,0:T(8,128)(2,1)} %param.11) | copy-start | bytes 6291460
  0.6 9.9 %copy-start.19 = (s32[1,2,512]{2,1,0:T(2,128)S(1)}, s32[1,2,512]{2,1,0:T(2,128)}, u32[]{:S(2)}) copy-start(s32[1,2,512]{2,1,0:T(2,128)} %param.13) | copy-start | bytes 12292
  0.7 10.1 %copy-start.16 = (bf16[1,256,512]{2,1,0:T(8,128)(2,1)S(1)}, bf16[1,256,512]{2,1,0:T(8,128)(2,1)}, u32[]{:S(2)}) copy-start(bf16[1,256,512]{2,1,0:T(8,128)(2,1)} %param.12) | copy-start | bytes 786436
  3.8 31.0 %collective-permute-start.2 = (bf16[128,2048]{1,0:T(8,128)(2,1)}, bf16[128,2048]{1,0:T(8,128)(2,1)}, u32[]{:S(2)}, u32[]{:S(2)}) collective-permute-start(bf16[128,2048]{1,0:T(8,128)(2,1)} %slice.225), channel_id=1, source_target_pairs={{0,1},{1,0},{2,3},{3,2},{4,5},{5,4},{6,7},{7,6},{8,9},{9,8},{10,11... | collective-permute-start | bytes 1572872 | tf_op jit(solution)/shard_map/ppermute | solution.py:348
  6.8 24.2 %collective-permute-start.3 = (bf16[128,2048]{1,0:T(8,128)(2,1)S(1)}, bf16[128,2048]{1,0:T(8,128)(2,1)S(1)}, u32[]{:S(2)}, u32[]{:S(2)}) collective-permute-start(bf16[128,2048]{1,0:T(8,128)(2,1)S(1)} %slice.286), channel_id=1, source_target_pairs={{0,1},{1,0},{2,3},{3,2},{4,5},{5,4},{6,7},{7,6},{8,9},{9,8},{10,11... | collective-permute-start | bytes 1572872 | tf_op jit(solution)/shard_map/ppermute | solution.py:348
  7.6 34.7 %collective-permute-start.1 = (bf16[128,2048]{1,0:T(8,128)(2,1)}, bf16[128,2048]{1,0:T(8,128)(2,1)}, u32[]{:S(2)}, u32[]{:S(2)}) collective-permute-start(bf16[128,2048]{1,0:T(8,128)(2,1)} %slice.226), channel_id=1, source_target_pairs={{0,1},{1,0},{2,3},{3,2},{4,5},{5,4},{6,7},{7,6},{8,9},{9,8},{10,11... | collective-permute-start | bytes 1572872 | tf_op jit(solution)/shard_map/ppermute | solution.py:348
  10.5 42.2 %collective-permute-start = (bf16[128,2048]{1,0:T(8,128)(2,1)}, bf16[128,2048]{1,0:T(8,128)(2,1)}, u32[]{:S(2)}, u32[]{:S(2)}) collective-permute-start(bf16[128,2048]{1,0:T(8,128)(2,1)} %slice.227), channel_id=1, source_target_pairs={{0,1},{1,0},{2,3},{3,2},{4,5},{5,4},{6,7},{7,6},{8,9},{9,8},{10,11... | collective-permute-start | bytes 1572872 | tf_op jit(solution)/shard_map/ppermute | solution.py:348
  15.8 1.3 copy-start.5
  31.0 0.8 copy-start.13
  31.7 1.0 copy-start.14
  52.7 2.4 %copy-start.3 = (bf16[1,128,8192]{2,1,0:T(8,128)(2,1)S(1)}, bf16[1,128,8192]{2,1,0:T(8,128)(2,1)}, u32[]{:S(2)}) copy-start(bf16[1,128,8192]{2,1,0:T(8,128)(2,1)} %param.11) | copy-start | bytes 6291460
  52.7 3.0 %copy-start.6 = (bf16[8192,128]{1,0:T(8,128)(2,1)S(1)}, bf16[8192,128]{1,0:T(8,128)(2,1)}, u32[]{:S(2)}) copy-start(bf16[8192,128]{1,0:T(8,128)(2,1)} %copy-done.5) | copy-start | bytes 6291460
  55.1 16.5 %copy-start = (bf16[8192,128]{1,0:T(8,128)(2,1)}, bf16[8192,128]{1,0:T(8,128)(2,1)S(1)}, u32[]{:S(2)}) copy-start(bf16[8192,128]{1,0:T(8,128)(2,1)S(1)} %get-tuple-element.80) | copy-start | bytes 6291460
  66.7 25.9 %copy-start.12 = (f32[8,512,128]{2,1,0:T(8,128)}, f32[8,512,128]{2,1,0:T(8,128)S(1)}, u32[]{:S(2)}) copy-start(f32[8,512,128]{2,1,0:T(8,128)S(1)} %get-tuple-element.83) | copy-start | bytes 6291460
  66.8 2.7 %collective-permute-start.4 = (f16[8,512,128]{2,1,0:T(8,128)(2,1)S(1)}, f16[8,512,128]{2,1,0:T(8,128)(2,1)S(1)}, u32[]{:S(2)}, u32[]{:S(2)}) collective-permute-start(f16[8,512,128]{2,1,0:T(8,128)(2,1)S(1)} %convert_element_type.204), channel_id=1, source_target_pairs={{0,2},{2,0},{4,6},{6,4},{8,10},{10,8},{12,14},{14,12},{16,18},{18,... | collective-permute-start | bytes 3145736 | tf_op jit(solution)/shard_map/ppermute | solution.py:328
  69.6 23.1 %copy-start.15 = (f16[8,512,128]{2,1,0:T(8,128)(2,1)}, f16[8,512,128]{2,1,0:T(8,128)(2,1)S(1)}, u32[]{:S(2)}) copy-start(f16[8,512,128]{2,1,0:T(8,128)(2,1)S(1)} %collective-permute-done.4) | copy-start | bytes 3145732
  69.7 22.9 %collective-permute-start.5 = (f16[4,512,128]{2,1,0:T(8,128)(2,1)S(1)}, f16[4,512,128]{2,1,0:T(8,128)(2,1)S(1)}, u32[]{:S(2)}, u32[]{:S(2)}) collective-permute-start(f16[4,512,128]{2,1,0:T(8,128)(2,1)S(1)} %add_convert_fusion.3), channel_id=1, source_target_pairs={{0,4},{2,6},{4,0},{6,2},{8,12},{10,14},{12,8},{14,10},{16,20},{18,... | collective-permute-start | bytes 1572872 | tf_op jit(solution)/shard_map/ppermute | solution.py:328
  89.9 2.7 %copy-start.8 = (f32[8,512,128]{2,1,0:T(8,128)}, f32[8,512,128]{2,1,0:T(8,128)S(1)}, u32[]{:S(2)}) copy-start(f32[8,512,128]{2,1,0:T(8,128)S(1)} %get-tuple-element.91) | copy-start | bytes 6291460
  90.0 2.7 %copy-start.10 = (f32[8,512,128]{2,1,0:T(8,128)}, f32[8,512,128]{2,1,0:T(8,128)S(1)}, u32[]{:S(2)}) copy-start(f32[8,512,128]{2,1,0:T(8,128)S(1)} %get-tuple-element.87) | copy-start | bytes 6291460
  92.6 0.8 copy-start.17
  93.4 3.0 %collective-permute-start.7 = (f16[8,512,128]{2,1,0:T(8,128)(2,1)}, f16[8,512,128]{2,1,0:T(8,128)(2,1)}, u32[]{:S(2)}, u32[]{:S(2)}) collective-permute-start(f16[8,512,128]{2,1,0:T(8,128)(2,1)} %convert_element_type.211), channel_id=1, source_target_pairs={{0,2},{2,0},{4,6},{6,4},{8,10},{10,8},{12,14},{14,12},{16,18},{18,... | collective-permute-start | bytes 3145736 | tf_op jit(solution)/shard_map/ppermute | solution.py:328
  93.4 4.5 %collective-permute-start.6 = (f16[8,512,128]{2,1,0:T(8,128)(2,1)}, f16[8,512,128]{2,1,0:T(8,128)(2,1)}, u32[]{:S(2)}, u32[]{:S(2)}) collective-permute-start(f16[8,512,128]{2,1,0:T(8,128)(2,1)} %convert_element_type.210), channel_id=1, source_target_pairs={{0,2},{2,0},{4,6},{6,4},{8,10},{10,8},{12,14},{14,12},{16,18},{18,... | collective-permute-start | bytes 3145736 | tf_op jit(solution)/shard_map/ppermute | solution.py:328
  93.9 2.5 %copy-start.9 = (f32[8,512,128]{2,1,0:T(8,128)S(1)}, f32[8,512,128]{2,1,0:T(8,128)}, u32[]{:S(2)}) copy-start(f32[8,512,128]{2,1,0:T(8,128)} %copy-done.8) | copy-start | bytes 6291460
  93.9 4.0 %copy-start.11 = (f32[8,512,128]{2,1,0:T(8,128)S(1)}, f32[8,512,128]{2,1,0:T(8,128)}, u32[]{:S(2)}) copy-start(f32[8,512,128]{2,1,0:T(8,128)} %copy-done.10) | copy-start | bytes 6291460
  97.9 5.4 %copy-start.7 = (bf16[8192,128]{1,0:T(8,128)(2,1)S(1)}, bf16[8192,128]{1,0:T(8,128)(2,1)}, u32[]{:S(2)}) copy-start(bf16[8192,128]{1,0:T(8,128)(2,1)} %copy-done.5) | copy-start | bytes 6291460
  99.3 4.0 %copy-start.1 = (bf16[8192,128]{1,0:T(8,128)(2,1)S(1)}, bf16[8192,128]{1,0:T(8,128)(2,1)}, u32[]{:S(2)}) copy-start(bf16[8192,128]{1,0:T(8,128)(2,1)} %copy-done) | copy-start | bytes 6291460
  99.3 4.0 %copy-start.4 = (bf16[1,128,8192]{2,1,0:T(8,128)(2,1)S(1)}, bf16[1,128,8192]{2,1,0:T(8,128)(2,1)}, u32[]{:S(2)}) copy-start(bf16[1,128,8192]{2,1,0:T(8,128)(2,1)} %param.11) | copy-start | bytes 6291460
  99.3 15.3 %collective-permute-start.9 = (f16[4,512,128]{2,1,0:T(8,128)(2,1)S(1)}, f16[4,512,128]{2,1,0:T(8,128)(2,1)S(1)}, u32[]{:S(2)}, u32[]{:S(2)}) collective-permute-start(f16[4,512,128]{2,1,0:T(8,128)(2,1)S(1)} %add_convert_fusion.2), channel_id=1, source_target_pairs={{0,4},{2,6},{4,0},{6,2},{8,12},{10,14},{12,8},{14,10},{16,20},{18,... | collective-permute-start | bytes 1572872 | tf_op jit(solution)/shard_map/ppermute | solution.py:328
  101.1 13.5 %collective-permute-start.8 = (f16[2,512,128]{2,1,0:T(8,128)(2,1)S(1)}, f16[2,512,128]{2,1,0:T(8,128)(2,1)S(1)}, u32[]{:S(2)}, u32[]{:S(2)}) collective-permute-start(f16[2,512,128]{2,1,0:T(8,128)(2,1)S(1)} %add_convert_fusion.7), channel_id=1, source_target_pairs={{0,8},{2,10},{4,12},{6,14},{8,0},{10,2},{12,4},{14,6},{16,24},{18,... | collective-permute-start | bytes 786440 | tf_op jit(solution)/shard_map/ppermute | solution.py:328
  114.4 1.0 copy-start.18
  118.0 4.4 %collective-permute-start.10 = (f16[8,512,128]{2,1,0:T(8,128)(2,1)S(1)}, f16[8,512,128]{2,1,0:T(8,128)(2,1)S(1)}, u32[]{:S(2)}, u32[]{:S(2)}) collective-permute-start(f16[8,512,128]{2,1,0:T(8,128)(2,1)S(1)} %convert_element_type.216), channel_id=1, source_target_pairs={{0,2},{2,0},{4,6},{6,4},{8,10},{10,8},{12,14},{14,12},{16,18},{18,... | collective-permute-start | bytes 3145736 | tf_op jit(solution)/shard_map/ppermute | solution.py:328
  118.0 14.8 %collective-permute-start.14 = (f16[4,512,128]{2,1,0:T(8,128)(2,1)S(1)}, f16[4,512,128]{2,1,0:T(8,128)(2,1)S(1)}, u32[]{:S(2)}, u32[]{:S(2)}) collective-permute-start(f16[4,512,128]{2,1,0:T(8,128)(2,1)S(1)} %add_convert_fusion.1), channel_id=1, source_target_pairs={{0,4},{2,6},{4,0},{6,2},{8,12},{10,14},{12,8},{14,10},{16,20},{18,... | collective-permute-start | bytes 1572872 | tf_op jit(solution)/shard_map/ppermute | solution.py:328
  119.3 14.0 %collective-permute-start.13 = (f16[2,512,128]{2,1,0:T(8,128)(2,1)S(1)}, f16[2,512,128]{2,1,0:T(8,128)(2,1)S(1)}, u32[]{:S(2)}, u32[]{:S(2)}) collective-permute-start(f16[2,512,128]{2,1,0:T(8,128)(2,1)S(1)} %add_convert_fusion.6), channel_id=1, source_target_pairs={{0,8},{2,10},{4,12},{6,14},{8,0},{10,2},{12,4},{14,6},{16,24},{18,... | collective-permute-start | bytes 786440 | tf_op jit(solution)/shard_map/ppermute | solution.py:328
  119.8 13.6 %collective-permute-start.12 = (f16[2,512,128]{2,1,0:T(8,128)(2,1)S(1)}, f16[2,512,128]{2,1,0:T(8,128)(2,1)S(1)}, u32[]{:S(2)}, u32[]{:S(2)}) collective-permute-start(f16[2,512,128]{2,1,0:T(8,128)(2,1)S(1)} %pad_maximum_fusion.6), channel_id=1, source_target_pairs={{0,16},{2,18},{4,20},{6,22},{8,24},{10,26},{12,28},{14,30},{16,0},... | collective-permute-start | bytes 786440 | tf_op jit(solution)/shard_map/ppermute | solution.py:328
  122.5 21.1 %collective-permute-start.11 = (f16[4,512,128]{2,1,0:T(8,128)(2,1)S(1)}, f16[4,512,128]{2,1,0:T(8,128)(2,1)S(1)}, u32[]{:S(2)}, u32[]{:S(2)}) collective-permute-start(f16[4,512,128]{2,1,0:T(8,128)(2,1)S(1)} %add_convert_fusion), channel_id=1, source_target_pairs={{0,4},{2,6},{4,0},{6,2},{8,12},{10,14},{12,8},{14,10},{16,20},{18,... | collective-permute-start | bytes 1572872 | tf_op jit(solution)/shard_map/ppermute | solution.py:328
  134.4 13.7 %collective-permute-start.23 = (f16[2,512,128]{2,1,0:T(8,128)(2,1)S(1)}, f16[2,512,128]{2,1,0:T(8,128)(2,1)S(1)}, u32[]{:S(2)}, u32[]{:S(2)}) collective-permute-start(f16[2,512,128]{2,1,0:T(8,128)(2,1)S(1)} %add_convert_fusion.5), channel_id=1, source_target_pairs={{0,8},{2,10},{4,12},{6,14},{8,0},{10,2},{12,4},{14,6},{16,24},{18,... | collective-permute-start | bytes 786440 | tf_op jit(solution)/shard_map/ppermute | solution.py:328
  138.2 14.0 %collective-permute-start.22 = (f16[2,512,128]{2,1,0:T(8,128)(2,1)S(1)}, f16[2,512,128]{2,1,0:T(8,128)(2,1)S(1)}, u32[]{:S(2)}, u32[]{:S(2)}) collective-permute-start(f16[2,512,128]{2,1,0:T(8,128)(2,1)S(1)} %pad_maximum_fusion.7), channel_id=1, source_target_pairs={{0,16},{2,18},{4,20},{6,22},{8,24},{10,26},{12,28},{14,30},{16,0},... | collective-permute-start | bytes 786440 | tf_op jit(solution)/shard_map/ppermute | solution.py:328
  141.1 14.3 %collective-permute-start.21 = (bf16[2,512,128]{2,1,0:T(8,128)(2,1)S(1)}, bf16[2,512,128]{2,1,0:T(8,128)(2,1)S(1)}, u32[]{:S(2)}, u32[]{:S(2)}) collective-permute-start(bf16[2,512,128]{2,1,0:T(8,128)(2,1)S(1)} %subtract_convert_fusion.3), channel_id=1, source_target_pairs={{0,8},{2,10},{4,12},{6,14},{8,0},{10,2},{12,4},{14,6},{16,24},{18,... | collective-permute-start | bytes 786440 | tf_op jit(solution)/shard_map/ppermute | solution.py:328
  143.7 18.9 %collective-permute-start.15 = (f16[2,512,128]{2,1,0:T(8,128)(2,1)S(1)}, f16[2,512,128]{2,1,0:T(8,128)(2,1)S(1)}, u32[]{:S(2)}, u32[]{:S(2)}) collective-permute-start(f16[2,512,128]{2,1,0:T(8,128)(2,1)S(1)} %add_convert_fusion.4), channel_id=1, source_target_pairs={{0,8},{2,10},{4,12},{6,14},{8,0},{10,2},{12,4},{14,6},{16,24},{18,... | collective-permute-start | bytes 786440 | tf_op jit(solution)/shard_map/ppermute | solution.py:328
  155.5 21.2 %collective-permute-start.29 = (bf16[4,512,128]{2,1,0:T(8,128)(2,1)S(1)}, bf16[4,512,128]{2,1,0:T(8,128)(2,1)S(1)}, u32[]{:S(2)}, u32[]{:S(2)}) collective-permute-start(bf16[4,512,128]{2,1,0:T(8,128)(2,1)S(1)} %pad_maximum_fusion.4.refs_0_), channel_id=1, source_target_pairs={{0,4},{2,6},{4,0},{6,2},{8,12},{10,14},{12,8},{14,10},{16,20},{18,... | collective-permute-start | bytes 1572872 | tf_op jit(solution)/shard_map/ppermute | solution.py:328
  156.4 37.5 %collective-permute-start.30 = (bf16[4,512,128]{2,1,0:T(8,128)(2,1)S(1)}, bf16[4,512,128]{2,1,0:T(8,128)(2,1)S(1)}, u32[]{:S(2)}, u32[]{:S(2)}) collective-permute-start(bf16[4,512,128]{2,1,0:T(8,128)(2,1)S(1)} %pad_maximum_fusion.4.refs_0_), channel_id=1, source_target_pairs={{0,2},{2,0},{4,6},{6,4},{8,10},{10,8},{12,14},{14,12},{16,18},{18,... | collective-permute-start | bytes 1572872 | tf_op jit(solution)/shard_map/ppermute | solution.py:328
  157.6 18.5 %collective-permute-start.24 = (f16[2,512,128]{2,1,0:T(8,128)(2,1)S(1)}, f16[2,512,128]{2,1,0:T(8,128)(2,1)S(1)}, u32[]{:S(2)}, u32[]{:S(2)}) collective-permute-start(f16[2,512,128]{2,1,0:T(8,128)(2,1)S(1)} %pad_maximum_fusion.9), channel_id=1, source_target_pairs={{0,16},{2,18},{4,20},{6,22},{8,24},{10,26},{12,28},{14,30},{16,0},... | collective-permute-start | bytes 786440 | tf_op jit(solution)/shard_map/ppermute | solution.py:328
  160.6 14.2 %collective-permute-start.27 = (bf16[2,512,128]{2,1,0:T(8,128)(2,1)S(1)}, bf16[2,512,128]{2,1,0:T(8,128)(2,1)S(1)}, u32[]{:S(2)}, u32[]{:S(2)}) collective-permute-start(bf16[2,512,128]{2,1,0:T(8,128)(2,1)S(1)} %subtract_convert_fusion), channel_id=1, source_target_pairs={{0,8},{2,10},{4,12},{6,14},{8,0},{10,2},{12,4},{14,6},{16,24},{18,... | collective-permute-start | bytes 786440 | tf_op jit(solution)/shard_map/ppermute | solution.py:328
  162.9 21.5 %collective-permute-start.16 = (f16[2,512,128]{2,1,0:T(8,128)(2,1)S(1)}, f16[2,512,128]{2,1,0:T(8,128)(2,1)S(1)}, u32[]{:S(2)}, u32[]{:S(2)}) collective-permute-start(f16[2,512,128]{2,1,0:T(8,128)(2,1)S(1)} %pad_maximum_fusion.8), channel_id=1, source_target_pairs={{0,16},{2,18},{4,20},{6,22},{8,24},{10,26},{12,28},{14,30},{16,0},... | collective-permute-start | bytes 786440 | tf_op jit(solution)/shard_map/ppermute | solution.py:328
  174.9 12.0 %collective-permute-start.28 = (bf16[4,512,128]{2,1,0:T(8,128)(2,1)S(1)}, bf16[4,512,128]{2,1,0:T(8,128)(2,1)S(1)}, u32[]{:S(2)}, u32[]{:S(2)}) collective-permute-start(bf16[4,512,128]{2,1,0:T(8,128)(2,1)S(1)} %pad_maximum_fusion.3.refs_0_), channel_id=1, source_target_pairs={{0,4},{2,6},{4,0},{6,2},{8,12},{10,14},{12,8},{14,10},{16,20},{18,... | collective-permute-start | bytes 1572872 | tf_op jit(solution)/shard_map/ppermute | solution.py:328
  176.2 10.5 %collective-permute-start.25 = (bf16[2,512,128]{2,1,0:T(8,128)(2,1)S(1)}, bf16[2,512,128]{2,1,0:T(8,128)(2,1)S(1)}, u32[]{:S(2)}, u32[]{:S(2)}) collective-permute-start(bf16[2,512,128]{2,1,0:T(8,128)(2,1)S(1)} %subtract_convert_fusion.1), channel_id=1, source_target_pairs={{0,8},{2,10},{4,12},{6,14},{8,0},{10,2},{12,4},{14,6},{16,24},{18,... | collective-permute-start | bytes 786440 | tf_op jit(solution)/shard_map/ppermute | solution.py:328
  176.7 17.1 %collective-permute-start.31 = (bf16[4,512,128]{2,1,0:T(8,128)(2,1)S(1)}, bf16[4,512,128]{2,1,0:T(8,128)(2,1)S(1)}, u32[]{:S(2)}, u32[]{:S(2)}) collective-permute-start(bf16[4,512,128]{2,1,0:T(8,128)(2,1)S(1)} %collective-permute-done.29.refs_1_), channel_id=1, source_target_pairs={{0,2},{2,0},{4,6},{6,4},{8,10},{10,8},{12,14},{14,12},{16,18},{18,... | collective-permute-start | bytes 1572872 | tf_op jit(solution)/shard_map/ppermute | solution.py:328
  184.6 8.0 %collective-permute-start.17 = (bf16[2,512,128]{2,1,0:T(8,128)(2,1)S(1)}, bf16[2,512,128]{2,1,0:T(8,128)(2,1)S(1)}, u32[]{:S(2)}, u32[]{:S(2)}) collective-permute-start(bf16[2,512,128]{2,1,0:T(8,128)(2,1)S(1)} %subtract_convert_fusion.2), channel_id=1, source_target_pairs={{0,8},{2,10},{4,12},{6,14},{8,0},{10,2},{12,4},{14,6},{16,24},{18,... | collective-permute-start | bytes 786440 | tf_op jit(solution)/shard_map/ppermute | solution.py:328
  186.8 25.7 %collective-permute-start.32 = (bf16[4,512,128]{2,1,0:T(8,128)(2,1)S(1)}, bf16[4,512,128]{2,1,0:T(8,128)(2,1)S(1)}, u32[]{:S(2)}, u32[]{:S(2)}) collective-permute-start(bf16[4,512,128]{2,1,0:T(8,128)(2,1)S(1)} %pad_maximum_fusion.3.refs_0_), channel_id=1, source_target_pairs={{0,2},{2,0},{4,6},{6,4},{8,10},{10,8},{12,14},{14,12},{16,18},{18,... | collective-permute-start | bytes 1572872 | tf_op jit(solution)/shard_map/ppermute | solution.py:328
  186.8 14.8 %collective-permute-start.26 = (bf16[4,512,128]{2,1,0:T(8,128)(2,1)S(1)}, bf16[4,512,128]{2,1,0:T(8,128)(2,1)S(1)}, u32[]{:S(2)}, u32[]{:S(2)}) collective-permute-start(bf16[4,512,128]{2,1,0:T(8,128)(2,1)S(1)} %pad_maximum_fusion.2.refs_0_), channel_id=1, source_target_pairs={{0,4},{2,6},{4,0},{6,2},{8,12},{10,14},{12,8},{14,10},{16,20},{18,... | collective-permute-start | bytes 1572872 | tf_op jit(solution)/shard_map/ppermute | solution.py:328
  192.6 19.9 %collective-permute-start.18 = (bf16[4,512,128]{2,1,0:T(8,128)(2,1)S(1)}, bf16[4,512,128]{2,1,0:T(8,128)(2,1)S(1)}, u32[]{:S(2)}, u32[]{:S(2)}) collective-permute-start(bf16[4,512,128]{2,1,0:T(8,128)(2,1)S(1)} %pad_maximum_fusion.1.refs_0_), channel_id=1, source_target_pairs={{0,4},{2,6},{4,0},{6,2},{8,12},{10,14},{12,8},{14,10},{16,20},{18,... | collective-permute-start | bytes 1572872 | tf_op jit(solution)/shard_map/ppermute | solution.py:328
  195.3 17.2 %collective-permute-start.33 = (bf16[4,512,128]{2,1,0:T(8,128)(2,1)S(1)}, bf16[4,512,128]{2,1,0:T(8,128)(2,1)S(1)}, u32[]{:S(2)}, u32[]{:S(2)}) collective-permute-start(bf16[4,512,128]{2,1,0:T(8,128)(2,1)S(1)} %collective-permute-done.28.refs_1_), channel_id=1, source_target_pairs={{0,2},{2,0},{4,6},{6,4},{8,10},{10,8},{12,14},{14,12},{16,18},{18,... | collective-permute-start | bytes 1572872 | tf_op jit(solution)/shard_map/ppermute | solution.py:328
  195.5 20.2 %collective-permute-start.34 = (bf16[4,512,128]{2,1,0:T(8,128)(2,1)S(1)}, bf16[4,512,128]{2,1,0:T(8,128)(2,1)S(1)}, u32[]{:S(2)}, u32[]{:S(2)}) collective-permute-start(bf16[4,512,128]{2,1,0:T(8,128)(2,1)S(1)} %pad_maximum_fusion.2.refs_0_), channel_id=1, source_target_pairs={{0,2},{2,0},{4,6},{6,4},{8,10},{10,8},{12,14},{14,12},{16,18},{18,... | collective-permute-start | bytes 1572872 | tf_op jit(solution)/shard_map/ppermute | solution.py:328
  201.6 15.9 %collective-permute-start.19 = (bf16[4,512,128]{2,1,0:T(8,128)(2,1)S(1)}, bf16[4,512,128]{2,1,0:T(8,128)(2,1)S(1)}, u32[]{:S(2)}, u32[]{:S(2)}) collective-permute-start(bf16[4,512,128]{2,1,0:T(8,128)(2,1)S(1)} %pad_maximum_fusion.1.refs_0_), channel_id=1, source_target_pairs={{0,2},{2,0},{4,6},{6,4},{8,10},{10,8},{12,14},{14,12},{16,18},{18,... | collective-permute-start | bytes 1572872 | tf_op jit(solution)/shard_map/ppermute | solution.py:328
  212.5 5.0 %collective-permute-start.20 = (bf16[4,512,128]{2,1,0:T(8,128)(2,1)S(1)}, bf16[4,512,128]{2,1,0:T(8,128)(2,1)S(1)}, u32[]{:S(2)}, u32[]{:S(2)}) collective-permute-start(bf16[4,512,128]{2,1,0:T(8,128)(2,1)S(1)} %collective-permute-done.18.refs_1_), channel_id=1, source_target_pairs={{0,2},{2,0},{4,6},{6,4},{8,10},{10,8},{12,14},{14,12},{16,18},{18,... | collective-permute-start | bytes 1572872 | tf_op jit(solution)/shard_map/ppermute | solution.py:328
  213.9 2.1 collective-permute-start.35

commit v12 on v11

--- a/solution.py
+++ b/solution.py
@@ -409,12 +409,14 @@
         stack = (starts.astype(F32) - (1.33 / scale) * both).astype(BF16)
         offsets = list(spans[-1])
         stack = yield stack
-        for span in spans[-2:0:-1]:
+        back = spans[-2::-1] if chunk + 1 < chunks or chunks == 1 else spans[:-1]
+        for span in back[:-1]:
             arrived = yield sent([stack], span)
             offsets = [offset ^ far for far in span for offset in offsets]
             stack = yield jnp.concatenate([stack] + arrived)
-        across, = yield sent([stack], spans[0])
-        finished[chunk] = (moved, stack, across, offsets)
+        across, = yield sent([stack], back[-1])
+        ends = [0, back[-1][1], 1, back[-1][1] ^ 1]
+        finished[chunk] = (moved, stack, across, [[offset ^ end for offset in offsets] for end in ends])
         yield ()
 
     finished = {}
@@ -436,26 +438,28 @@
         )
         sends = [send.astype(WIRE) for send in changes[::2]]
         if fresh:
-            ready = range(fresh[0] + 1)
-            move_on(ready)
-            sends, _ = tied(sends, [formed[chunk] for chunk in ready])
+            move_on(range(fresh[0] + 1))
+            sends, _ = tied(sends, [formed[chunk] for chunk in range(fresh.stop)])
         fresh = range(fresh.stop, fresh.stop + wide // width)
         for chunk, send, keep in zip(fresh, sends, changes[1::2]):
             running[chunk] = chain(chunk, keep, swapped(send, 1))
             formed[chunk] = next(running[chunk])
         if fresh.stop < chunks:
-            formed, token = tied(formed, token)
-    others = range(fresh[0])
-    move_on(others, behind=fresh)
-    move_on(fresh, behind=others)
-    move_on(others, behind=fresh)
+            early = {chunk: formed[chunk] for chunk in range(fresh[0] + 1)}
+            early, token = tied(early, token)
+            formed.update(early)
+    if chunks == 4:
+        move_on([0], behind=[3])
+        move_on([1, 2], behind=[0])
+        move_on([3], behind=[1, 2])
+        move_on([0], behind=[3])
+        move_on([1, 2], behind=[0])
     for chunk in range(chunks):
         while chunk not in finished:
             move_on([chunk])
 
     for chunk in range(chunks):
         _, stack, across, offsets = finished[chunk]
-        offsets = [[offset ^ low for offset in offsets] for low in (0, 2, 1, 3)]
         if result and chunk + 1 < chunks:
             across, *result = tied(across, result[0])
         received = [stack, across, swapped(stack, 1), swapped(across, 1)]

time: 220 us -> 210 us (0.955)
  waiting for transfers between devices: 97.1 us -> 86.8 us
    ppermute x32, waiting for transfers between devices: 70.2 us -> 59.9 us  [swapped(): return lax.ppermute(array, 'rep', pairs)]
  transfers between devices with their start and end apart: 36 -> 36, of which waited for: 19 -> 17; matrix products, arithmetic and copies ran while one was open for 7% -> 8% of each run, Pallas kernels for 21% -> 22%
where the time goes in v12:
time: 210 us
  waiting for transfers between devices  86.8 us (41%)
  Pallas kernels  60 us (29%)
  starting transfers between devices  32.9 us (16%)
  other arithmetic  14.7 us (7%)
  local copies, waits for them, and re-layouts  13.9 us (7%)
    ppermute x32, waiting for transfers between devices, swapped(): return lax.ppermute(array, 'rep', pairs)  59.9 us
    pallas_call x3, Pallas kernels, inner(): pl.pallas_call(functools.partial(inner_kernel, float(tokens), kept), grid...  40.5 us
    ppermute x32, starting transfers between devices, swapped(): return lax.ppermute(array, 'rep', pairs)  27.8 us
    ppermute x4, waiting for transfers between devices, per_device(): parts.append(lax.ppermute(part, 'fsdp', [(0, 1), (1, 0)]))  26.9 us
    pallas_call x4, Pallas kernels, arrive(): pl.pallas_call(functools.partial(arrive_kernel, piece), grid=(1,), in_spe...  8.81 us
    unnamed x40, local copies, waits for them, and re-layouts  5.9 us
    pallas_call x4, Pallas kernels, assemble(): pl.pallas_call(functools.partial(assemble_kernel, begin, offsets), in_spe...  5.76 us
    convert_element_type x8, other arithmetic, parted(): sum((term.astype(F32) for term in part)).astype(WIRE)  5.21 us
  transfers between devices with their start and end apart: 36, of which 17 were waited for; matrix products, arithmetic and copies ran while one was open for 8% of the time, Pallas kernels for 22%

profile of v12, /device:TPU:0, one launch (start us, length us, event | category | flops | bytes accessed | tf_op | source)
XLA Modules:
  0.0 209.7 jit_solution(12487450156532528324)
XLA Ops:
  0.7 1.2 slice.286
  1.9 1.9 slice.225
  3.8 3.0 %collective-permute-start.2 = (bf16[128,2048]{1,0:T(8,128)(2,1)}, bf16[128,2048]{1,0:T(8,128)(2,1)}, u32[]{:S(2)}, u32[]{:S(2)}) collective-permute-start(bf16[128,2048]{1,0:T(8,128)(2,1)} %slice.225), channel_id=1, source_target_pairs={{0,1},{1,0},{2,3},{3,2},{4,5},{5,4},{6,7},{7,6},{8,9},{9,8},{10,11... | collective-permute-start | bytes 1572872 | tf_op jit(solution)/shard_map/ppermute | solution.py:348
  6.8 0.8 slice.226
  7.6 2.0 collective-permute-start.1
  9.6 0.8 slice.227
  10.8 5.0 %forward.1 = (bf16[8192,128]{1,0:T(8,128)(2,1)S(1)}, f32[128,512]{1,0:T(8,128)S(1)}) custom-call(bf16[128,8192]{1,0:T(8,128)(2,1)S(1)} %bitcast.88, bf16[8192,512]{1,0:T(8,128)(2,1)} %weights_ref.9), custom_call_target="tpu_custom_call" | custom-call | flops 1073741824 | bytes 12582912 | tf_op jit(solution)/shard_map/forward/pallas_call | solution.py:34
  15.8 1.3 copy-done.5
  17.5 13.4 %collective-permute-done.3.part_ref = bf16[128,2048]{1,0:T(8,128)(2,1)S(1)} collective-permute-done((bf16[128,2048]{1,0:T(8,128)(2,1)S(1)}, bf16[128,2048]{1,0:T(8,128)(2,1)S(1)}, u32[]{:S(2)}, u32[]{:S(2)}) %collective-permute-start.3) | collective-permute-done | bytes 524320 | tf_op jit(solution)/shard_map/ppermute | solution.py:348
  31.0 0.8 copy-done.13
  31.7 1.0 copy-done.14
  32.8 2.0 arrive.4
  34.8 2.2 %arrive.5 = (bf16[128,8192]{1,0:T(8,128)(2,1)S(1)}, bf16[8192,128]{1,0:T(8,128)(2,1)S(1)}, f32[128,512]{1,0:T(8,128)S(1)}) custom-call(bf16[128,2048]{1,0:T(8,128)(2,1)} %collective-permute-done.2.part_ref, bf16[8192,512]{1,0:T(8,128)(2,1)} %weights_ref.9, ...), custom_call_target="tpu_custom_call", output_to_operand_aliasing={{0}: (2, {}), {1}: (3, {}), {2}: (4, {})} | custom-call | flops 268435456 | bytes 3670016 | tf_op jit(solution)/shard_map/arrive/pallas_call | solution.py:76
  37.1 5.2 %collective-permute-done.1.part_ref = bf16[128,2048]{1,0:T(8,128)(2,1)} collective-permute-done((bf16[128,2048]{1,0:T(8,128)(2,1)}, bf16[128,2048]{1,0:T(8,128)(2,1)}, u32[]{:S(2)}, u32[]{:S(2)}) %collective-permute-start.1) | collective-permute-done | bytes 524320 | tf_op jit(solution)/shard_map/ppermute | solution.py:348
  42.3 2.2 %arrive.6 = (bf16[128,8192]{1,0:T(8,128)(2,1)S(1)}, bf16[8192,128]{1,0:T(8,128)(2,1)S(1)}, f32[128,512]{1,0:T(8,128)S(1)}) custom-call(bf16[128,2048]{1,0:T(8,128)(2,1)} %collective-permute-done.1.part_ref, bf16[8192,512]{1,0:T(8,128)(2,1)} %weights_ref.9, ...), custom_call_target="tpu_custom_call", output_to_operand_aliasing={{0}: (2, {}), {1}: (3, {}), {2}: (4, {})} | custom-call | flops 268435456 | bytes 3670016 | tf_op jit(solution)/shard_map/arrive/pallas_call | solution.py:76
  44.5 8.2 %collective-permute-done.part_ref = bf16[128,2048]{1,0:T(8,128)(2,1)} collective-permute-done((bf16[128,2048]{1,0:T(8,128)(2,1)}, bf16[128,2048]{1,0:T(8,128)(2,1)}, u32[]{:S(2)}, u32[]{:S(2)}) %collective-permute-start) | collective-permute-done | bytes 524320 | tf_op jit(solution)/shard_map/ppermute | solution.py:348
  52.7 2.3 %arrive.7 = (bf16[128,8192]{1,0:T(8,128)(2,1)S(1)}, bf16[8192,128]{1,0:T(8,128)(2,1)S(1)}, f32[128,512]{1,0:T(8,128)S(1)}) custom-call(bf16[128,2048]{1,0:T(8,128)(2,1)} %collective-permute-done.part_ref, bf16[8192,512]{1,0:T(8,128)(2,1)} %weights_ref.9, ...), custom_call_target="tpu_custom_call", output_to_operand_aliasing={{0}: (2, {}), {1}: (3, {}), {2}: (4, {})} | custom-call | flops 268435456 | bytes 3670016 | tf_op jit(solution)/shard_map/arrive/pallas_call | solution.py:76
  55.1 0.6 copy-done.6
  55.7 11.0 %inner.3 = (f32[8,512,128]{2,1,0:T(8,128)S(1)}, f32[8,512,128]{2,1,0:T(8,128)S(1)}) custom-call(s32[1]{0:T(128)} %bitcast.mine_ref.place_ref, bf16[128,8192]{1,0:T(8,128)(2,1)S(1)} %bitcast.89, bf16[128,8192]{1,0:T(8,128)(2,1)S(1)} %get-tuple-element.77.high_ref, bf16[4,2,2,512,128]{4,3,2,1,0:T(8,128)(2,1)S(1)} %bitcast.92, ...), custom_call_target="tpu_custom_call" | custom-call | flops 1610612736 | bytes 20971520 | tf_op jit(solution)/shard_map/inner/pallas_call | solution.py:234
  66.9 2.6 %collective-permute-done.4 = f16[8,512,128]{2,1,0:T(8,128)(2,1)S(1)} collective-permute-done((f16[8,512,128]{2,1,0:T(8,128)(2,1)S(1)}, f16[8,512,128]{2,1,0:T(8,128)(2,1)S(1)}, u32[]{:S(2)}, u32[]{:S(2)}) %collective-permute-start.4) | collective-permute-done | bytes 1048608 | tf_op jit(solution)/shard_map/ppermute | solution.py:328
  69.7 1.8 collective-permute-start.5
  71.5 18.4 %inner.4 = (f32[8,512,128]{2,1,0:T(8,128)S(1)}, f32[8,512,128]{2,1,0:T(8,128)S(1)}, f32[8,512,128]{2,1,0:T(8,128)S(1)}, f32[8,512,128]{2,1,0:T(8,128)S(1)}) custom-call(s32[1]{0:T(128)} %bitcast.mine_ref.place_ref, bf16[128,8192]{1,0:T(8,128)(2,1)S(1)} %bitcast.90, bf16[128,8192]{1,0:T(8,128)(2,1)S(1)} %get-tuple-element.77.high_ref, ...), custom_call_target="tpu_custom_call" | custom-call | flops 3221225472 | bytes 41943040 | tf_op jit(solution)/shard_map/inner/pallas_call | solution.py:234
  90.0 1.3 convert_element_type.210
  91.3 1.3 convert_element_type.211
  92.8 0.6 copy-done.17
  93.9 1.4 dynamic-slice_bitcast_fusion
  95.4 1.4 fusion.15
  96.8 1.3 add_convert_fusion.2
  98.7 1.9 collective-permute-start.7
  100.6 11.1 %inner.5 = (f32[8,512,128]{2,1,0:T(8,128)S(1)}, f32[8,512,128]{2,1,0:T(8,128)S(1)}) custom-call(s32[1]{0:T(128)} %bitcast.mine_ref.place_ref, bf16[128,8192]{1,0:T(8,128)(2,1)S(1)} %bitcast.91, bf16[128,8192]{1,0:T(8,128)(2,1)S(1)} %get-tuple-element.77.high_ref, bf16[4,2,2,512,128]{4,3,2,1,0:T(8,128)(2,1)S(1)} %bitcast.94, ...), custom_call_target="tpu_custom_call" | custom-call | flops 1610612736 | bytes 20971520 | tf_op jit(solution)/shard_map/inner/pallas_call | solution.py:234
  111.9 1.4 copy-done.9
  113.3 1.2 add_convert_fusion.1
  114.6 1.2 convert_add_fusion.3
  116.0 1.1 add_convert_fusion.6
  117.1 1.6 collective-permute-start.13
  119.1 2.6 %collective-permute-start.14 = (f16[2,512,128]{2,1,0:T(8,128)(2,1)S(1)}, f16[2,512,128]{2,1,0:T(8,128)(2,1)S(1)}, u32[]{:S(2)}, u32[]{:S(2)}) collective-permute-start(f16[2,512,128]{2,1,0:T(8,128)(2,1)S(1)} %pad_maximum_fusion.6), channel_id=1, source_target_pairs={{0,16},{2,18},{4,20},{6,22},{8,24},{10,26},{12,28},{14,30},{16,0},... | collective-permute-start | bytes 786440 | tf_op jit(solution)/shard_map/ppermute | solution.py:328
  121.9 0.6 collective-permute-start.11
  122.5 8.2 %collective-permute-done.14 = f16[2,512,128]{2,1,0:T(8,128)(2,1)S(1)} collective-permute-done((f16[2,512,128]{2,1,0:T(8,128)(2,1)S(1)}, f16[2,512,128]{2,1,0:T(8,128)(2,1)S(1)}, u32[]{:S(2)}, u32[]{:S(2)}) %collective-permute-start.14) | collective-permute-done | bytes 262176 | tf_op jit(solution)/shard_map/ppermute | solution.py:328
  130.8 4.6 %collective-permute-start.23 = (bf16[2,512,128]{2,1,0:T(8,128)(2,1)S(1)}, bf16[2,512,128]{2,1,0:T(8,128)(2,1)S(1)}, u32[]{:S(2)}, u32[]{:S(2)}) collective-permute-start(bf16[2,512,128]{2,1,0:T(8,128)(2,1)S(1)} %subtract_convert_fusion.3), channel_id=1, source_target_pairs={{0,8},{2,10},{4,12},{6,14},{8,0},{10,2},{12,4},{14,6},{16,24},{18,... | collective-permute-start | bytes 786440 | tf_op jit(solution)/shard_map/ppermute | solution.py:328
  135.5 1.1 add_convert_fusion.5
  136.6 1.1 convert_add_fusion.2
  137.9 2.8 %collective-permute-start.21 = (f16[2,512,128]{2,1,0:T(8,128)(2,1)S(1)}, f16[2,512,128]{2,1,0:T(8,128)(2,1)S(1)}, u32[]{:S(2)}, u32[]{:S(2)}) collective-permute-start(f16[2,512,128]{2,1,0:T(8,128)(2,1)S(1)} %pad_maximum_fusion.7), channel_id=1, source_target_pairs={{0,16},{2,18},{4,20},{6,22},{8,24},{10,26},{12,28},{14,30},{16,0},... | collective-permute-start | bytes 786440 | tf_op jit(solution)/shard_map/ppermute | solution.py:328
  140.6 2.1 collective-permute-done.11
  143.1 5.1 %collective-permute-done.23 = bf16[2,512,128]{2,1,0:T(8,128)(2,1)S(1)} collective-permute-done((bf16[2,512,128]{2,1,0:T(8,128)(2,1)S(1)}, bf16[2,512,128]{2,1,0:T(8,128)(2,1)S(1)}, u32[]{:S(2)}, u32[]{:S(2)}) %collective-permute-start.23) | collective-permute-done | bytes 262176 | tf_op jit(solution)/shard_map/ppermute | solution.py:328
  148.3 0.6 collective-permute-start.29
  148.9 5.0 %collective-permute-done.22 = f16[2,512,128]{2,1,0:T(8,128)(2,1)S(1)} collective-permute-done((f16[2,512,128]{2,1,0:T(8,128)(2,1)S(1)}, f16[2,512,128]{2,1,0:T(8,128)(2,1)S(1)}, u32[]{:S(2)}, u32[]{:S(2)}) %collective-permute-start.22) | collective-permute-done | bytes 262176 | tf_op jit(solution)/shard_map/ppermute | solution.py:328
  153.9 1.1 convert_add_fusion
  155.1 3.0 %collective-permute-start.24 = (f16[2,512,128]{2,1,0:T(8,128)(2,1)S(1)}, f16[2,512,128]{2,1,0:T(8,128)(2,1)S(1)}, u32[]{:S(2)}, u32[]{:S(2)}) collective-permute-start(f16[2,512,128]{2,1,0:T(8,128)(2,1)S(1)} %pad_maximum_fusion.9), channel_id=1, source_target_pairs={{0,16},{2,18},{4,20},{6,22},{8,24},{10,26},{12,28},{14,30},{16,0},... | collective-permute-start | bytes 786440 | tf_op jit(solution)/shard_map/ppermute | solution.py:328
  158.3 1.9 collective-permute-start.27
  160.1 3.3 %collective-permute-done.15 = f16[2,512,128]{2,1,0:T(8,128)(2,1)S(1)} collective-permute-done((f16[2,512,128]{2,1,0:T(8,128)(2,1)S(1)}, f16[2,512,128]{2,1,0:T(8,128)(2,1)S(1)}, u32[]{:S(2)}, u32[]{:S(2)}) %collective-permute-start.15) | collective-permute-done | bytes 262176 | tf_op jit(solution)/shard_map/ppermute | solution.py:328
  163.7 1.5 collective-permute-start.16
  165.2 8.0 %collective-permute-done.27 = bf16[2,512,128]{2,1,0:T(8,128)(2,1)S(1)} collective-permute-done((bf16[2,512,128]{2,1,0:T(8,128)(2,1)S(1)}, bf16[2,512,128]{2,1,0:T(8,128)(2,1)S(1)}, u32[]{:S(2)}, u32[]{:S(2)}) %collective-permute-start.27) | collective-permute-done | bytes 262176 | tf_op jit(solution)/shard_map/ppermute | solution.py:328
  173.2 0.6 collective-permute-start.28
  174.1 4.4 %collective-permute-done.16 = f16[2,512,128]{2,1,0:T(8,128)(2,1)S(1)} collective-permute-done((f16[2,512,128]{2,1,0:T(8,128)(2,1)S(1)}, f16[2,512,128]{2,1,0:T(8,128)(2,1)S(1)}, u32[]{:S(2)}, u32[]{:S(2)}) %collective-permute-start.16) | collective-permute-done | bytes 262176 | tf_op jit(solution)/shard_map/ppermute | solution.py:328
  179.3 1.7 collective-permute-done.25
  181.0 7.1 %collective-permute-done.28.refs_1_ = bf16[4,512,128]{2,1,0:T(8,128)(2,1)S(1)} collective-permute-done((bf16[4,512,128]{2,1,0:T(8,128)(2,1)S(1)}, bf16[4,512,128]{2,1,0:T(8,128)(2,1)S(1)}, u32[]{:S(2)}, u32[]{:S(2)}) %collective-permute-start.28) | collective-permute-done | bytes 524320 | tf_op jit(solution)/shard_map/ppermute | solution.py:328
  188.7 5.1 %collective-permute-done.17 = bf16[2,512,128]{2,1,0:T(8,128)(2,1)S(1)} collective-permute-done((bf16[2,512,128]{2,1,0:T(8,128)(2,1)S(1)}, bf16[2,512,128]{2,1,0:T(8,128)(2,1)S(1)}, u32[]{:S(2)}, u32[]{:S(2)}) %collective-permute-start.17) | collective-permute-done | bytes 262176 | tf_op jit(solution)/shard_map/ppermute | solution.py:328
  193.9 1.4 assemble.4.refs_4_
  196.1 5.1 %collective-permute-done.26.refs_1_ = bf16[4,512,128]{2,1,0:T(8,128)(2,1)S(1)} collective-permute-done((bf16[4,512,128]{2,1,0:T(8,128)(2,1)S(1)}, bf16[4,512,128]{2,1,0:T(8,128)(2,1)S(1)}, u32[]{:S(2)}, u32[]{:S(2)}) %collective-permute-start.26) | collective-permute-done | bytes 524320 | tf_op jit(solution)/shard_map/ppermute | solution.py:328
  201.3 1.8 collective-permute-done.18.refs_1_
  203.1 1.4 assemble.5.refs_4_
  205.2 1.0 pad_maximum_fusion
  206.6 1.4 assemble.6.refs_4_
  208.1 1.4 assemble.7
  (117 shorter events, 8.3 us)
Async XLA Ops:
  0.6 6.2 %copy-start.2 = (bf16[1,128,8192]{2,1,0:T(8,128)(2,1)S(1)}, bf16[1,128,8192]{2,1,0:T(8,128)(2,1)}, u32[]{:S(2)}) copy-start(bf16[1,128,8192]{2,1,0:T(8,128)(2,1)} %param.11) | copy-start | bytes 6291460
  0.6 9.9 %copy-start.19 = (s32[1,2,512]{2,1,0:T(2,128)S(1)}, s32[1,2,512]{2,1,0:T(2,128)}, u32[]{:S(2)}) copy-start(s32[1,2,512]{2,1,0:T(2,128)} %param.13) | copy-start | bytes 12292
  0.7 10.1 %copy-start.16 = (bf16[1,256,512]{2,1,0:T(8,128)(2,1)S(1)}, bf16[1,256,512]{2,1,0:T(8,128)(2,1)}, u32[]{:S(2)}) copy-start(bf16[1,256,512]{2,1,0:T(8,128)(2,1)} %param.12) | copy-start | bytes 786436
  3.8 31.0 %collective-permute-start.2 = (bf16[128,2048]{1,0:T(8,128)(2,1)}, bf16[128,2048]{1,0:T(8,128)(2,1)}, u32[]{:S(2)}, u32[]{:S(2)}) collective-permute-start(bf16[128,2048]{1,0:T(8,128)(2,1)} %slice.225), channel_id=1, source_target_pairs={{0,1},{1,0},{2,3},{3,2},{4,5},{5,4},{6,7},{7,6},{8,9},{9,8},{10,11... | collective-permute-start | bytes 1572872 | tf_op jit(solution)/shard_map/ppermute | solution.py:348
  6.8 24.2 %collective-permute-start.3 = (bf16[128,2048]{1,0:T(8,128)(2,1)S(1)}, bf16[128,2048]{1,0:T(8,128)(2,1)S(1)}, u32[]{:S(2)}, u32[]{:S(2)}) collective-permute-start(bf16[128,2048]{1,0:T(8,128)(2,1)S(1)} %slice.286), channel_id=1, source_target_pairs={{0,1},{1,0},{2,3},{3,2},{4,5},{5,4},{6,7},{7,6},{8,9},{9,8},{10,11... | collective-permute-start | bytes 1572872 | tf_op jit(solution)/shard_map/ppermute | solution.py:348
  7.6 34.7 %collective-permute-start.1 = (bf16[128,2048]{1,0:T(8,128)(2,1)}, bf16[128,2048]{1,0:T(8,128)(2,1)}, u32[]{:S(2)}, u32[]{:S(2)}) collective-permute-start(bf16[128,2048]{1,0:T(8,128)(2,1)} %slice.226), channel_id=1, source_target_pairs={{0,1},{1,0},{2,3},{3,2},{4,5},{5,4},{6,7},{7,6},{8,9},{9,8},{10,11... | collective-permute-start | bytes 1572872 | tf_op jit(solution)/shard_map/ppermute | solution.py:348
  10.5 42.2 %collective-permute-start = (bf16[128,2048]{1,0:T(8,128)(2,1)}, bf16[128,2048]{1,0:T(8,128)(2,1)}, u32[]{:S(2)}, u32[]{:S(2)}) collective-permute-start(bf16[128,2048]{1,0:T(8,128)(2,1)} %slice.227), channel_id=1, source_target_pairs={{0,1},{1,0},{2,3},{3,2},{4,5},{5,4},{6,7},{7,6},{8,9},{9,8},{10,11... | collective-permute-start | bytes 1572872 | tf_op jit(solution)/shard_map/ppermute | solution.py:348
  15.8 1.3 copy-start.5
  31.0 0.8 copy-start.13
  31.7 1.0 copy-start.14
  52.7 2.4 %copy-start.3 = (bf16[1,128,8192]{2,1,0:T(8,128)(2,1)S(1)}, bf16[1,128,8192]{2,1,0:T(8,128)(2,1)}, u32[]{:S(2)}) copy-start(bf16[1,128,8192]{2,1,0:T(8,128)(2,1)} %param.11) | copy-start | bytes 6291460
  52.7 3.0 %copy-start.6 = (bf16[8192,128]{1,0:T(8,128)(2,1)S(1)}, bf16[8192,128]{1,0:T(8,128)(2,1)}, u32[]{:S(2)}) copy-start(bf16[8192,128]{1,0:T(8,128)(2,1)} %copy-done.5) | copy-start | bytes 6291460
  55.1 16.5 %copy-start = (bf16[8192,128]{1,0:T(8,128)(2,1)}, bf16[8192,128]{1,0:T(8,128)(2,1)S(1)}, u32[]{:S(2)}) copy-start(bf16[8192,128]{1,0:T(8,128)(2,1)S(1)} %get-tuple-element.79) | copy-start | bytes 6291460
  66.7 25.9 %copy-start.12 = (f32[8,512,128]{2,1,0:T(8,128)}, f32[8,512,128]{2,1,0:T(8,128)S(1)}, u32[]{:S(2)}) copy-start(f32[8,512,128]{2,1,0:T(8,128)S(1)} %get-tuple-element.82) | copy-start | bytes 6291460
  66.8 2.7 %collective-permute-start.4 = (f16[8,512,128]{2,1,0:T(8,128)(2,1)S(1)}, f16[8,512,128]{2,1,0:T(8,128)(2,1)S(1)}, u32[]{:S(2)}, u32[]{:S(2)}) collective-permute-start(f16[8,512,128]{2,1,0:T(8,128)(2,1)S(1)} %convert_element_type.204), channel_id=1, source_target_pairs={{0,2},{2,0},{4,6},{6,4},{8,10},{10,8},{12,14},{14,12},{16,18},{18,... | collective-permute-start | bytes 3145736 | tf_op jit(solution)/shard_map/ppermute | solution.py:328
  69.6 23.1 %copy-start.15 = (f16[8,512,128]{2,1,0:T(8,128)(2,1)}, f16[8,512,128]{2,1,0:T(8,128)(2,1)S(1)}, u32[]{:S(2)}) copy-start(f16[8,512,128]{2,1,0:T(8,128)(2,1)S(1)} %collective-permute-done.4) | copy-start | bytes 3145732
  69.7 22.9 %collective-permute-start.5 = (f16[4,512,128]{2,1,0:T(8,128)(2,1)S(1)}, f16[4,512,128]{2,1,0:T(8,128)(2,1)S(1)}, u32[]{:S(2)}, u32[]{:S(2)}) collective-permute-start(f16[4,512,128]{2,1,0:T(8,128)(2,1)S(1)} %add_convert_fusion.3), channel_id=1, source_target_pairs={{0,4},{2,6},{4,0},{6,2},{8,12},{10,14},{12,8},{14,10},{16,20},{18,... | collective-permute-start | bytes 1572872 | tf_op jit(solution)/shard_map/ppermute | solution.py:328
  89.9 2.7 %copy-start.8 = (f32[8,512,128]{2,1,0:T(8,128)}, f32[8,512,128]{2,1,0:T(8,128)S(1)}, u32[]{:S(2)}) copy-start(f32[8,512,128]{2,1,0:T(8,128)S(1)} %get-tuple-element.98) | copy-start | bytes 6291460
  90.0 2.7 %copy-start.10 = (f32[8,512,128]{2,1,0:T(8,128)}, f32[8,512,128]{2,1,0:T(8,128)S(1)}, u32[]{:S(2)}) copy-start(f32[8,512,128]{2,1,0:T(8,128)S(1)} %get-tuple-element.86) | copy-start | bytes 6291460
  92.6 0.8 copy-start.17
  93.4 3.4 %collective-permute-start.6 = (f16[8,512,128]{2,1,0:T(8,128)(2,1)}, f16[8,512,128]{2,1,0:T(8,128)(2,1)}, u32[]{:S(2)}, u32[]{:S(2)}) collective-permute-start(f16[8,512,128]{2,1,0:T(8,128)(2,1)} %convert_element_type.210), channel_id=1, source_target_pairs={{0,2},{2,0},{4,6},{6,4},{8,10},{10,8},{12,14},{14,12},{16,18},{18,... | collective-permute-start | bytes 3145736 | tf_op jit(solution)/shard_map/ppermute | solution.py:328
  93.4 18.5 %collective-permute-start.9 = (f16[8,512,128]{2,1,0:T(8,128)(2,1)}, f16[8,512,128]{2,1,0:T(8,128)(2,1)}, u32[]{:S(2)}, u32[]{:S(2)}) collective-permute-start(f16[8,512,128]{2,1,0:T(8,128)(2,1)} %convert_element_type.211), channel_id=1, source_target_pairs={{0,2},{2,0},{4,6},{6,4},{8,10},{10,8},{12,14},{14,12},{16,18},{18,... | collective-permute-start | bytes 3145736 | tf_op jit(solution)/shard_map/ppermute | solution.py:328
  93.9 2.9 %copy-start.11 = (f32[8,512,128]{2,1,0:T(8,128)S(1)}, f32[8,512,128]{2,1,0:T(8,128)}, u32[]{:S(2)}) copy-start(f32[8,512,128]{2,1,0:T(8,128)} %copy-done.10) | copy-start | bytes 6291460
  95.4 5.3 %copy-start.7 = (bf16[8192,128]{1,0:T(8,128)(2,1)S(1)}, bf16[8192,128]{1,0:T(8,128)(2,1)}, u32[]{:S(2)}) copy-start(bf16[8192,128]{1,0:T(8,128)(2,1)} %copy-done.5) | copy-start | bytes 6291460
  96.8 3.8 %copy-start.1 = (bf16[8192,128]{1,0:T(8,128)(2,1)S(1)}, bf16[8192,128]{1,0:T(8,128)(2,1)}, u32[]{:S(2)}) copy-start(bf16[8192,128]{1,0:T(8,128)(2,1)} %copy-done) | copy-start | bytes 6291460
  96.8 3.8 %copy-start.4 = (bf16[1,128,8192]{2,1,0:T(8,128)(2,1)S(1)}, bf16[1,128,8192]{2,1,0:T(8,128)(2,1)}, u32[]{:S(2)}) copy-start(bf16[1,128,8192]{2,1,0:T(8,128)(2,1)} %param.11) | copy-start | bytes 6291460
  98.2 16.4 %collective-permute-start.8 = (f16[4,512,128]{2,1,0:T(8,128)(2,1)S(1)}, f16[4,512,128]{2,1,0:T(8,128)(2,1)S(1)}, u32[]{:S(2)}, u32[]{:S(2)}) collective-permute-start(f16[4,512,128]{2,1,0:T(8,128)(2,1)S(1)} %add_convert_fusion.2), channel_id=1, source_target_pairs={{0,4},{2,6},{4,0},{6,2},{8,12},{10,14},{12,8},{14,10},{16,20},{18,... | collective-permute-start | bytes 1572872 | tf_op jit(solution)/shard_map/ppermute | solution.py:328
  98.7 15.8 %collective-permute-start.7 = (f16[2,512,128]{2,1,0:T(8,128)(2,1)S(1)}, f16[2,512,128]{2,1,0:T(8,128)(2,1)S(1)}, u32[]{:S(2)}, u32[]{:S(2)}) collective-permute-start(f16[2,512,128]{2,1,0:T(8,128)(2,1)S(1)} %add_convert_fusion.7), channel_id=1, source_target_pairs={{0,8},{2,10},{4,12},{6,14},{8,0},{10,2},{12,4},{14,6},{16,24},{18,... | collective-permute-start | bytes 786440 | tf_op jit(solution)/shard_map/ppermute | solution.py:328
  111.7 1.6 copy-start.9
  111.7 2.8 %copy-start.18 = (f16[4,512,128]{2,1,0:T(8,128)(2,1)S(1)}, f16[4,512,128]{2,1,0:T(8,128)(2,1)}, u32[]{:S(2)}) copy-start(f16[4,512,128]{2,1,0:T(8,128)(2,1)} %copy-done.17) | copy-start | bytes 1572868
  117.0 4.7 %collective-permute-start.10 = (f16[8,512,128]{2,1,0:T(8,128)(2,1)S(1)}, f16[8,512,128]{2,1,0:T(8,128)(2,1)S(1)}, u32[]{:S(2)}, u32[]{:S(2)}) collective-permute-start(f16[8,512,128]{2,1,0:T(8,128)(2,1)S(1)} %convert_element_type.214), channel_id=1, source_target_pairs={{0,2},{2,0},{4,6},{6,4},{8,10},{10,8},{12,14},{14,12},{16,18},{18,... | collective-permute-start | bytes 3145736 | tf_op jit(solution)/shard_map/ppermute | solution.py:328
  117.1 18.3 %collective-permute-start.13 = (f16[4,512,128]{2,1,0:T(8,128)(2,1)S(1)}, f16[4,512,128]{2,1,0:T(8,128)(2,1)S(1)}, u32[]{:S(2)}, u32[]{:S(2)}) collective-permute-start(f16[4,512,128]{2,1,0:T(8,128)(2,1)S(1)} %add_convert_fusion.1), channel_id=1, source_target_pairs={{0,4},{2,6},{4,0},{6,2},{8,12},{10,14},{12,8},{14,10},{16,20},{18,... | collective-permute-start | bytes 1572872 | tf_op jit(solution)/shard_map/ppermute | solution.py:328
  118.7 16.8 %collective-permute-start.12 = (f16[2,512,128]{2,1,0:T(8,128)(2,1)S(1)}, f16[2,512,128]{2,1,0:T(8,128)(2,1)S(1)}, u32[]{:S(2)}, u32[]{:S(2)}) collective-permute-start(f16[2,512,128]{2,1,0:T(8,128)(2,1)S(1)} %add_convert_fusion.6), channel_id=1, source_target_pairs={{0,8},{2,10},{4,12},{6,14},{8,0},{10,2},{12,4},{14,6},{16,24},{18,... | collective-permute-start | bytes 786440 | tf_op jit(solution)/shard_map/ppermute | solution.py:328
  119.1 11.6 %collective-permute-start.14 = (f16[2,512,128]{2,1,0:T(8,128)(2,1)S(1)}, f16[2,512,128]{2,1,0:T(8,128)(2,1)S(1)}, u32[]{:S(2)}, u32[]{:S(2)}) collective-permute-start(f16[2,512,128]{2,1,0:T(8,128)(2,1)S(1)} %pad_maximum_fusion.6), channel_id=1, source_target_pairs={{0,16},{2,18},{4,20},{6,22},{8,24},{10,26},{12,28},{14,30},{16,0},... | collective-permute-start | bytes 786440 | tf_op jit(solution)/shard_map/ppermute | solution.py:328
  121.9 20.8 %collective-permute-start.11 = (f16[4,512,128]{2,1,0:T(8,128)(2,1)S(1)}, f16[4,512,128]{2,1,0:T(8,128)(2,1)S(1)}, u32[]{:S(2)}, u32[]{:S(2)}) collective-permute-start(f16[4,512,128]{2,1,0:T(8,128)(2,1)S(1)} %add_convert_fusion), channel_id=1, source_target_pairs={{0,4},{2,6},{4,0},{6,2},{8,12},{10,14},{12,8},{14,10},{16,20},{18,... | collective-permute-start | bytes 1572872 | tf_op jit(solution)/shard_map/ppermute | solution.py:328
  130.8 17.5 %collective-permute-start.23 = (bf16[2,512,128]{2,1,0:T(8,128)(2,1)S(1)}, bf16[2,512,128]{2,1,0:T(8,128)(2,1)S(1)}, u32[]{:S(2)}, u32[]{:S(2)}) collective-permute-start(bf16[2,512,128]{2,1,0:T(8,128)(2,1)S(1)} %subtract_convert_fusion.3), channel_id=1, source_target_pairs={{0,8},{2,10},{4,12},{6,14},{8,0},{10,2},{12,4},{14,6},{16,24},{18,... | collective-permute-start | bytes 786440 | tf_op jit(solution)/shard_map/ppermute | solution.py:328
  136.5 17.4 %collective-permute-start.22 = (f16[2,512,128]{2,1,0:T(8,128)(2,1)S(1)}, f16[2,512,128]{2,1,0:T(8,128)(2,1)S(1)}, u32[]{:S(2)}, u32[]{:S(2)}) collective-permute-start(f16[2,512,128]{2,1,0:T(8,128)(2,1)S(1)} %add_convert_fusion.5), channel_id=1, source_target_pairs={{0,8},{2,10},{4,12},{6,14},{8,0},{10,2},{12,4},{14,6},{16,24},{18,... | collective-permute-start | bytes 786440 | tf_op jit(solution)/shard_map/ppermute | solution.py:328
  137.9 16.0 %collective-permute-start.21 = (f16[2,512,128]{2,1,0:T(8,128)(2,1)S(1)}, f16[2,512,128]{2,1,0:T(8,128)(2,1)S(1)}, u32[]{:S(2)}, u32[]{:S(2)}) collective-permute-start(f16[2,512,128]{2,1,0:T(8,128)(2,1)S(1)} %pad_maximum_fusion.7), channel_id=1, source_target_pairs={{0,16},{2,18},{4,20},{6,22},{8,24},{10,26},{12,28},{14,30},{16,0},... | collective-permute-start | bytes 786440 | tf_op jit(solution)/shard_map/ppermute | solution.py:328
  142.8 20.6 %collective-permute-start.15 = (f16[2,512,128]{2,1,0:T(8,128)(2,1)S(1)}, f16[2,512,128]{2,1,0:T(8,128)(2,1)S(1)}, u32[]{:S(2)}, u32[]{:S(2)}) collective-permute-start(f16[2,512,128]{2,1,0:T(8,128)(2,1)S(1)} %add_convert_fusion.4), channel_id=1, source_target_pairs={{0,8},{2,10},{4,12},{6,14},{8,0},{10,2},{12,4},{14,6},{16,24},{18,... | collective-permute-start | bytes 786440 | tf_op jit(solution)/shard_map/ppermute | solution.py:328
  148.3 25.7 %collective-permute-start.29 = (bf16[4,512,128]{2,1,0:T(8,128)(2,1)S(1)}, bf16[4,512,128]{2,1,0:T(8,128)(2,1)S(1)}, u32[]{:S(2)}, u32[]{:S(2)}) collective-permute-start(bf16[4,512,128]{2,1,0:T(8,128)(2,1)S(1)} %pad_maximum_fusion.2.refs_0_), channel_id=1, source_target_pairs={{0,4},{2,6},{4,0},{6,2},{8,12},{10,14},{12,8},{14,10},{16,20},{18,... | collective-permute-start | bytes 1572872 | tf_op jit(solution)/shard_map/ppermute | solution.py:328
  148.9 44.9 %collective-permute-start.30 = (bf16[4,512,128]{2,1,0:T(8,128)(2,1)S(1)}, bf16[4,512,128]{2,1,0:T(8,128)(2,1)S(1)}, u32[]{:S(2)}, u32[]{:S(2)}) collective-permute-start(bf16[4,512,128]{2,1,0:T(8,128)(2,1)S(1)} %pad_maximum_fusion.2.refs_0_), channel_id=1, source_target_pairs={{0,2},{2,0},{4,6},{6,4},{8,10},{10,8},{12,14},{14,12},{16,18},{18,... | collective-permute-start | bytes 1572872 | tf_op jit(solution)/shard_map/ppermute | solution.py:328
  155.1 18.7 %collective-permute-start.24 = (f16[2,512,128]{2,1,0:T(8,128)(2,1)S(1)}, f16[2,512,128]{2,1,0:T(8,128)(2,1)S(1)}, u32[]{:S(2)}, u32[]{:S(2)}) collective-permute-start(f16[2,512,128]{2,1,0:T(8,128)(2,1)S(1)} %pad_maximum_fusion.9), channel_id=1, source_target_pairs={{0,16},{2,18},{4,20},{6,22},{8,24},{10,26},{12,28},{14,30},{16,0},... | collective-permute-start | bytes 786440 | tf_op jit(solution)/shard_map/ppermute | solution.py:328
  158.3 14.9 %collective-permute-start.27 = (bf16[2,512,128]{2,1,0:T(8,128)(2,1)S(1)}, bf16[2,512,128]{2,1,0:T(8,128)(2,1)S(1)}, u32[]{:S(2)}, u32[]{:S(2)}) collective-permute-start(bf16[2,512,128]{2,1,0:T(8,128)(2,1)S(1)} %subtract_convert_fusion), channel_id=1, source_target_pairs={{0,8},{2,10},{4,12},{6,14},{8,0},{10,2},{12,4},{14,6},{16,24},{18,... | collective-permute-start | bytes 786440 | tf_op jit(solution)/shard_map/ppermute | solution.py:328
  163.7 14.9 %collective-permute-start.16 = (f16[2,512,128]{2,1,0:T(8,128)(2,1)S(1)}, f16[2,512,128]{2,1,0:T(8,128)(2,1)S(1)}, u32[]{:S(2)}, u32[]{:S(2)}) collective-permute-start(f16[2,512,128]{2,1,0:T(8,128)(2,1)S(1)} %pad_maximum_fusion.8), channel_id=1, source_target_pairs={{0,16},{2,18},{4,20},{6,22},{8,24},{10,26},{12,28},{14,30},{16,0},... | collective-permute-start | bytes 786440 | tf_op jit(solution)/shard_map/ppermute | solution.py:328
  173.2 14.9 %collective-permute-start.28 = (bf16[4,512,128]{2,1,0:T(8,128)(2,1)S(1)}, bf16[4,512,128]{2,1,0:T(8,128)(2,1)S(1)}, u32[]{:S(2)}, u32[]{:S(2)}) collective-permute-start(bf16[4,512,128]{2,1,0:T(8,128)(2,1)S(1)} %pad_maximum_fusion.4.refs_0_), channel_id=1, source_target_pairs={{0,4},{2,6},{4,0},{6,2},{8,12},{10,14},{12,8},{14,10},{16,20},{18,... | collective-permute-start | bytes 1572872 | tf_op jit(solution)/shard_map/ppermute | solution.py:328
  173.9 7.0 %collective-permute-start.25 = (bf16[2,512,128]{2,1,0:T(8,128)(2,1)S(1)}, bf16[2,512,128]{2,1,0:T(8,128)(2,1)S(1)}, u32[]{:S(2)}, u32[]{:S(2)}) collective-permute-start(bf16[2,512,128]{2,1,0:T(8,128)(2,1)S(1)} %subtract_convert_fusion.1), channel_id=1, source_target_pairs={{0,8},{2,10},{4,12},{6,14},{8,0},{10,2},{12,4},{14,6},{16,24},{18,... | collective-permute-start | bytes 786440 | tf_op jit(solution)/shard_map/ppermute | solution.py:328
  174.0 19.9 %collective-permute-start.31 = (bf16[4,512,128]{2,1,0:T(8,128)(2,1)S(1)}, bf16[4,512,128]{2,1,0:T(8,128)(2,1)S(1)}, u32[]{:S(2)}, u32[]{:S(2)}) collective-permute-start(bf16[4,512,128]{2,1,0:T(8,128)(2,1)S(1)} %collective-permute-done.29.refs_1_), channel_id=1, source_target_pairs={{0,2},{2,0},{4,6},{6,4},{8,10},{10,8},{12,14},{14,12},{16,18},{18,... | collective-permute-start | bytes 1572872 | tf_op jit(solution)/shard_map/ppermute | solution.py:328
  178.7 15.1 %collective-permute-start.17 = (bf16[2,512,128]{2,1,0:T(8,128)(2,1)S(1)}, bf16[2,512,128]{2,1,0:T(8,128)(2,1)S(1)}, u32[]{:S(2)}, u32[]{:S(2)}) collective-permute-start(bf16[2,512,128]{2,1,0:T(8,128)(2,1)S(1)} %subtract_convert_fusion.2), channel_id=1, source_target_pairs={{0,4},{2,6},{4,0},{6,2},{8,12},{10,14},{12,8},{14,10},{16,20},{18,... | collective-permute-start | bytes 786440 | tf_op jit(solution)/shard_map/ppermute | solution.py:328
  181.0 22.1 %collective-permute-start.32 = (bf16[4,512,128]{2,1,0:T(8,128)(2,1)S(1)}, bf16[4,512,128]{2,1,0:T(8,128)(2,1)S(1)}, u32[]{:S(2)}, u32[]{:S(2)}) collective-permute-start(bf16[4,512,128]{2,1,0:T(8,128)(2,1)S(1)} %pad_maximum_fusion.4.refs_0_), channel_id=1, source_target_pairs={{0,2},{2,0},{4,6},{6,4},{8,10},{10,8},{12,14},{14,12},{16,18},{18,... | collective-permute-start | bytes 1572872 | tf_op jit(solution)/shard_map/ppermute | solution.py:328
  188.1 13.1 %collective-permute-start.26 = (bf16[4,512,128]{2,1,0:T(8,128)(2,1)S(1)}, bf16[4,512,128]{2,1,0:T(8,128)(2,1)S(1)}, u32[]{:S(2)}, u32[]{:S(2)}) collective-permute-start(bf16[4,512,128]{2,1,0:T(8,128)(2,1)S(1)} %pad_maximum_fusion.3.refs_0_), channel_id=1, source_target_pairs={{0,4},{2,6},{4,0},{6,2},{8,12},{10,14},{12,8},{14,10},{16,20},{18,... | collective-permute-start | bytes 1572872 | tf_op jit(solution)/shard_map/ppermute | solution.py:328
  193.8 9.2 %collective-permute-start.18 = (bf16[4,512,128]{2,1,0:T(8,128)(2,1)S(1)}, bf16[4,512,128]{2,1,0:T(8,128)(2,1)S(1)}, u32[]{:S(2)}, u32[]{:S(2)}) collective-permute-start(bf16[4,512,128]{2,1,0:T(8,128)(2,1)S(1)} %pad_maximum_fusion.1.refs_0_), channel_id=1, source_target_pairs={{0,8},{2,10},{4,12},{6,14},{8,0},{10,2},{12,4},{14,6},{16,24},{18,... | collective-permute-start | bytes 1572872 | tf_op jit(solution)/shard_map/ppermute | solution.py:328
  195.3 7.7 %collective-permute-start.33 = (bf16[4,512,128]{2,1,0:T(8,128)(2,1)S(1)}, bf16[4,512,128]{2,1,0:T(8,128)(2,1)S(1)}, u32[]{:S(2)}, u32[]{:S(2)}) collective-permute-start(bf16[4,512,128]{2,1,0:T(8,128)(2,1)S(1)} %collective-permute-done.28.refs_1_), channel_id=1, source_target_pairs={{0,2},{2,0},{4,6},{6,4},{8,10},{10,8},{12,14},{14,12},{16,18},{18,... | collective-permute-start | bytes 1572872 | tf_op jit(solution)/shard_map/ppermute | solution.py:328
  195.6 10.7 %collective-permute-start.34 = (bf16[4,512,128]{2,1,0:T(8,128)(2,1)S(1)}, bf16[4,512,128]{2,1,0:T(8,128)(2,1)S(1)}, u32[]{:S(2)}, u32[]{:S(2)}) collective-permute-start(bf16[4,512,128]{2,1,0:T(8,128)(2,1)S(1)} %pad_maximum_fusion.3.refs_0_), channel_id=1, source_target_pairs={{0,2},{2,0},{4,6},{6,4},{8,10},{10,8},{12,14},{14,12},{16,18},{18,... | collective-permute-start | bytes 1572872 | tf_op jit(solution)/shard_map/ppermute | solution.py:328
  201.3 6.8 %collective-permute-start.19 = (bf16[4,512,128]{2,1,0:T(8,128)(2,1)S(1)}, bf16[4,512,128]{2,1,0:T(8,128)(2,1)S(1)}, u32[]{:S(2)}, u32[]{:S(2)}) collective-permute-start(bf16[4,512,128]{2,1,0:T(8,128)(2,1)S(1)} %pad_maximum_fusion.1.refs_0_), channel_id=1, source_target_pairs={{0,2},{2,0},{4,6},{6,4},{8,10},{10,8},{12,14},{14,12},{16,18},{18,... | collective-permute-start | bytes 1572872 | tf_op jit(solution)/shard_map/ppermute | solution.py:328
  203.0 5.0 %collective-permute-start.20 = (bf16[4,512,128]{2,1,0:T(8,128)(2,1)S(1)}, bf16[4,512,128]{2,1,0:T(8,128)(2,1)S(1)}, u32[]{:S(2)}, u32[]{:S(2)}) collective-permute-start(bf16[4,512,128]{2,1,0:T(8,128)(2,1)S(1)} %collective-permute-done.18.refs_1_), channel_id=1, source_target_pairs={{0,2},{2,0},{4,6},{6,4},{8,10},{10,8},{12,14},{14,12},{16,18},{18,... | collective-permute-start | bytes 1572872 | tf_op jit(solution)/shard_map/ppermute | solution.py:328
  204.5 2.1 %collective-permute-start.35 = (bf16[4,512,128]{2,1,0:T(8,128)(2,1)S(1)}, bf16[4,512,128]{2,1,0:T(8,128)(2,1)S(1)}, u32[]{:S(2)}, u32[]{:S(2)}) collective-permute-start(bf16[4,512,128]{2,1,0:T(8,128)(2,1)S(1)} %collective-permute-done.26.refs_1_), channel_id=1, source_target_pairs={{0,2},{2,0},{4,6},{6,4},{8,10},{10,8},{12,14},{14,12},{16,18},{18,... | collective-permute-start | bytes 1572872 | tf_op jit(solution)/shard_map/ppermute | solution.py:328

commit v13 on v12

--- a/solution.py
+++ b/solution.py
@@ -266,13 +266,12 @@
     )(mine, *banks, *turned, pinned(start), pinned(first), pinned(second), *products, target, count)
 
 
-def assemble_kernel(begin, offsets, place_ref, *refs):
-    received = refs[: len(offsets)]
+def assemble_kernel(begins, offsets, place_ref, *refs):
     out_ref, semaphore = refs[-2:]
-    width = received[0].shape[-1]
+    width = refs[0].shape[-1]
     mine = place_ref[0]
     copies = []
-    for ref, group in zip(received, offsets):
+    for ref, begin, group in zip(refs, begins, offsets):
         for entry, offset in enumerate(group):
             copies.append(
                 pltpu.make_async_copy(
@@ -287,10 +286,11 @@
         copy.wait()
 
 
-def assemble(begin, place, received, offsets, shape, before):
+def assemble(place, blocks, shape, before):
+    begins, received, offsets = zip(*blocks)
     vmem = pl.BlockSpec(memory_space=pltpu.VMEM)
     return pl.pallas_call(
-        functools.partial(assemble_kernel, begin, offsets),
+        functools.partial(assemble_kernel, begins, offsets),
         in_specs=[pl.BlockSpec(memory_space=pltpu.SMEM)]
         + [vmem] * len(received)
         + [pl.BlockSpec(memory_space=pl.ANY)] * len(before),
@@ -300,7 +300,7 @@
         scratch_shapes=[pltpu.SemaphoreType.DMA((sum(map(len, offsets)),))],
         compiler_params=pltpu.CompilerParams(vmem_limit_bytes=12 * MIB),
         cost_estimate=pl.CostEstimate(
-            flops=0, bytes_accessed=4 * shape[0] * shape[1] * received[0].shape[-1], transcendentals=0
+            flops=0, bytes_accessed=4 * sum(array.size for array in received), transcendentals=0
         ),
         name="assemble",
     )(place, *received, *before)
@@ -432,6 +432,7 @@
 
     token = place
     fresh = range(0)
+    later = {}
     for begin, wide in calls:
         changes = inner(
             begin // wide, wide, width, token, banks, turned, start, first, second, products, target, count, tokens
@@ -439,33 +440,39 @@
         sends = [send.astype(WIRE) for send in changes[::2]]
         if fresh:
             move_on(range(fresh[0] + 1))
+            for chunk in fresh[1:]:
+                keep, arrived = later.pop(chunk)
+                arrived, _ = tied(arrived, [formed[other] for other in range(fresh[0] + 1)])
+                running[chunk] = chain(chunk, keep, arrived)
+                formed[chunk] = next(running[chunk])
             sends, _ = tied(sends, [formed[chunk] for chunk in range(fresh.stop)])
         fresh = range(fresh.stop, fresh.stop + wide // width)
         for chunk, send, keep in zip(fresh, sends, changes[1::2]):
-            running[chunk] = chain(chunk, keep, swapped(send, 1))
-            formed[chunk] = next(running[chunk])
+            later[chunk] = (keep, swapped(send, 1))
+        running[fresh[0]] = chain(fresh[0], *later.pop(fresh[0]))
+        formed[fresh[0]] = next(running[fresh[0]])
         if fresh.stop < chunks:
-            early = {chunk: formed[chunk] for chunk in range(fresh[0] + 1)}
-            early, token = tied(early, token)
-            formed.update(early)
+            formed, token = tied(formed, token)
     if chunks == 4:
-        move_on([0], behind=[3])
-        move_on([1, 2], behind=[0])
-        move_on([3], behind=[1, 2])
-        move_on([0], behind=[3])
-        move_on([1, 2], behind=[0])
+        before = 3
+        for which in (1, 0, 2, 3, 0, 1, 2):
+            move_on([which], behind=[before])
+            before = which
     for chunk in range(chunks):
         while chunk not in finished:
             move_on([chunk])
 
+    blocks = []
     for chunk in range(chunks):
         _, stack, across, offsets = finished[chunk]
-        if result and chunk + 1 < chunks:
+        if chunk == 1 and result:
             across, *result = tied(across, result[0])
         received = [stack, across, swapped(stack, 1), swapped(across, 1)]
-        result = (
-            assemble(begins[chunk], place, received, offsets, (reps, rows, columns), result),
-        )
+        blocks += [(begins[chunk], array, group) for array, group in zip(received, offsets)]
+        if chunk + 2 != chunks:
+            result = (assemble(place, blocks, (reps, rows, columns), result),)
+            blocks = []
+
     new_momentum = [finished[chunk][0] for chunk in sorted(range(chunks), key=begins.__getitem__)]
 
     return result[0].reshape(depth, columns), jnp.concatenate(new_momentum, axis=1)

time: 210 us -> 206 us (0.981)
  waiting for transfers between devices: 86.8 us -> 82.5 us
  starting transfers between devices: 32.9 us -> 36.8 us
  other arithmetic: 14.7 us -> 11.6 us
    ppermute x32, waiting for transfers between devices: 59.9 us -> 55.6 us  [swapped(): return lax.ppermute(array, 'rep', pairs)]
    ppermute x32, starting transfers between devices: 27.8 us -> 31.8 us  [swapped(): return lax.ppermute(array, 'rep', pairs)]
    pallas_call x4 -> x3, Pallas kernels: 5.76 us -> 5.14 us  [assemble(): pl.pallas_call(functools.partial(assemble_kernel, begins, offsets), in_sp...]
  transfers between devices with their start and end apart: 36 -> 36, of which waited for: 17 -> 15; matrix products, arithmetic and copies ran while one was open for 8% -> 7% of each run, Pallas kernels for 22% -> 21%
where the time goes in v13:
time: 206 us; the launch traced here: 205 us
  waiting for transfers between devices  82.5 us (40%)
  Pallas kernels  59.4 us (29%)
  starting transfers between devices  36.8 us (18%)
  local copies, waits for them, and re-layouts  13.4 us (7%)
  other arithmetic  11.6 us (6%)
    ppermute x32, waiting for transfers between devices, swapped(): return lax.ppermute(array, 'rep', pairs)  55.6 us
    pallas_call x3, Pallas kernels, inner(): pl.pallas_call(functools.partial(inner_kernel, float(tokens), kept), grid...  40.5 us
    ppermute x32, starting transfers between devices, swapped(): return lax.ppermute(array, 'rep', pairs)  31.8 us
    ppermute x4, waiting for transfers between devices, per_device(): parts.append(lax.ppermute(part, 'fsdp', [(0, 1), (1, 0)]))  26.9 us
    pallas_call x4, Pallas kernels, arrive(): pl.pallas_call(functools.partial(arrive_kernel, piece), grid=(1,), in_spe...  8.81 us
    unnamed x40, local copies, waits for them, and re-layouts  5.38 us
    pallas_call x3, Pallas kernels, assemble(): pl.pallas_call(functools.partial(assemble_kernel, begins, offsets), in_sp...  5.14 us
    ppermute x4, starting transfers between devices, per_device(): parts.append(lax.ppermute(part, 'fsdp', [(0, 1), (1, 0)]))  5.03 us
  transfers between devices with their start and end apart: 36, of which 15 were waited for; matrix products, arithmetic and copies ran while one was open for 7% of the time, Pallas kernels for 21%

profile of v13, /device:TPU:0, one launch (start us, length us, event | category | flops | bytes accessed | tf_op | source)
XLA Modules:
  0.0 205.2 jit_solution(9117533184684215443)
XLA Ops:
  0.7 1.2 slice.286
  1.9 1.9 slice.225
  3.8 3.0 %collective-permute-start.2 = (bf16[128,2048]{1,0:T(8,128)(2,1)}, bf16[128,2048]{1,0:T(8,128)(2,1)}, u32[]{:S(2)}, u32[]{:S(2)}) collective-permute-start(bf16[128,2048]{1,0:T(8,128)(2,1)} %slice.225), channel_id=1, source_target_pairs={{0,1},{1,0},{2,3},{3,2},{4,5},{5,4},{6,7},{7,6},{8,9},{9,8},{10,11... | collective-permute-start | bytes 1572872 | tf_op jit(solution)/shard_map/ppermute | solution.py:348
  6.8 0.8 slice.226
  7.6 2.0 collective-permute-start.1
  9.6 0.8 slice.227
  10.8 5.0 %forward.1 = (bf16[8192,128]{1,0:T(8,128)(2,1)S(1)}, f32[128,512]{1,0:T(8,128)S(1)}) custom-call(bf16[128,8192]{1,0:T(8,128)(2,1)S(1)} %bitcast.88, bf16[8192,512]{1,0:T(8,128)(2,1)} %weights_ref.9), custom_call_target="tpu_custom_call" | custom-call | flops 1073741824 | bytes 12582912 | tf_op jit(solution)/shard_map/forward/pallas_call | solution.py:34
  15.8 1.3 copy-done.5
  17.5 13.4 %collective-permute-done.3.part_ref = bf16[128,2048]{1,0:T(8,128)(2,1)S(1)} collective-permute-done((bf16[128,2048]{1,0:T(8,128)(2,1)S(1)}, bf16[128,2048]{1,0:T(8,128)(2,1)S(1)}, u32[]{:S(2)}, u32[]{:S(2)}) %collective-permute-start.3) | collective-permute-done | bytes 524320 | tf_op jit(solution)/shard_map/ppermute | solution.py:348
  31.0 0.8 copy-done.13
  31.7 1.0 copy-done.14
  32.8 2.0 arrive.4
  34.8 2.2 %arrive.5 = (bf16[128,8192]{1,0:T(8,128)(2,1)S(1)}, bf16[8192,128]{1,0:T(8,128)(2,1)S(1)}, f32[128,512]{1,0:T(8,128)S(1)}) custom-call(bf16[128,2048]{1,0:T(8,128)(2,1)} %collective-permute-done.2.part_ref, bf16[8192,512]{1,0:T(8,128)(2,1)} %weights_ref.9, ...), custom_call_target="tpu_custom_call", output_to_operand_aliasing={{0}: (2, {}), {1}: (3, {}), {2}: (4, {})} | custom-call | flops 268435456 | bytes 3670016 | tf_op jit(solution)/shard_map/arrive/pallas_call | solution.py:76
  37.1 5.2 %collective-permute-done.1.part_ref = bf16[128,2048]{1,0:T(8,128)(2,1)} collective-permute-done((bf16[128,2048]{1,0:T(8,128)(2,1)}, bf16[128,2048]{1,0:T(8,128)(2,1)}, u32[]{:S(2)}, u32[]{:S(2)}) %collective-permute-start.1) | collective-permute-done | bytes 524320 | tf_op jit(solution)/shard_map/ppermute | solution.py:348
  42.3 2.2 %arrive.6 = (bf16[128,8192]{1,0:T(8,128)(2,1)S(1)}, bf16[8192,128]{1,0:T(8,128)(2,1)S(1)}, f32[128,512]{1,0:T(8,128)S(1)}) custom-call(bf16[128,2048]{1,0:T(8,128)(2,1)} %collective-permute-done.1.part_ref, bf16[8192,512]{1,0:T(8,128)(2,1)} %weights_ref.9, ...), custom_call_target="tpu_custom_call", output_to_operand_aliasing={{0}: (2, {}), {1}: (3, {}), {2}: (4, {})} | custom-call | flops 268435456 | bytes 3670016 | tf_op jit(solution)/shard_map/arrive/pallas_call | solution.py:76
  44.5 8.2 %collective-permute-done.part_ref = bf16[128,2048]{1,0:T(8,128)(2,1)} collective-permute-done((bf16[128,2048]{1,0:T(8,128)(2,1)}, bf16[128,2048]{1,0:T(8,128)(2,1)}, u32[]{:S(2)}, u32[]{:S(2)}) %collective-permute-start) | collective-permute-done | bytes 524320 | tf_op jit(solution)/shard_map/ppermute | solution.py:348
  52.7 2.3 %arrive.7 = (bf16[128,8192]{1,0:T(8,128)(2,1)S(1)}, bf16[8192,128]{1,0:T(8,128)(2,1)S(1)}, f32[128,512]{1,0:T(8,128)S(1)}) custom-call(bf16[128,2048]{1,0:T(8,128)(2,1)} %collective-permute-done.part_ref, bf16[8192,512]{1,0:T(8,128)(2,1)} %weights_ref.9, ...), custom_call_target="tpu_custom_call", output_to_operand_aliasing={{0}: (2, {}), {1}: (3, {}), {2}: (4, {})} | custom-call | flops 268435456 | bytes 3670016 | tf_op jit(solution)/shard_map/arrive/pallas_call | solution.py:76
  55.1 0.6 copy-done.6
  55.7 11.0 %inner.3 = (f32[8,512,128]{2,1,0:T(8,128)S(1)}, f32[8,512,128]{2,1,0:T(8,128)S(1)}) custom-call(s32[1]{0:T(128)} %bitcast.mine_ref.place_ref, bf16[128,8192]{1,0:T(8,128)(2,1)S(1)} %bitcast.89, bf16[128,8192]{1,0:T(8,128)(2,1)S(1)} %get-tuple-element.76.high_ref, bf16[4,2,2,512,128]{4,3,2,1,0:T(8,128)(2,1)S(1)} %bitcast.92, ...), custom_call_target="tpu_custom_call" | custom-call | flops 1610612736 | bytes 20971520 | tf_op jit(solution)/shard_map/inner/pallas_call | solution.py:234
  66.9 2.6 %collective-permute-done.4 = f16[8,512,128]{2,1,0:T(8,128)(2,1)S(1)} collective-permute-done((f16[8,512,128]{2,1,0:T(8,128)(2,1)S(1)}, f16[8,512,128]{2,1,0:T(8,128)(2,1)S(1)}, u32[]{:S(2)}, u32[]{:S(2)}) %collective-permute-start.4) | collective-permute-done | bytes 1048608 | tf_op jit(solution)/shard_map/ppermute | solution.py:328
  69.7 1.8 collective-permute-start.5
  71.5 18.4 %inner.4 = (f32[8,512,128]{2,1,0:T(8,128)S(1)}, f32[8,512,128]{2,1,0:T(8,128)S(1)}, f32[8,512,128]{2,1,0:T(8,128)S(1)}, f32[8,512,128]{2,1,0:T(8,128)S(1)}) custom-call(s32[1]{0:T(128)} %bitcast.mine_ref.place_ref, bf16[128,8192]{1,0:T(8,128)(2,1)S(1)} %bitcast.90, bf16[128,8192]{1,0:T(8,128)(2,1)S(1)} %get-tuple-element.76.high_ref, ...), custom_call_target="tpu_custom_call" | custom-call | flops 3221225472 | bytes 41943040 | tf_op jit(solution)/shard_map/inner/pallas_call | solution.py:234
  90.0 1.3 convert_element_type.207
  91.2 1.4 convert_element_type.208
  92.8 0.7 copy-done.17
  93.5 1.4 dynamic-slice_bitcast_fusion
  94.9 1.6 collective-permute-done.7
  96.5 1.3 add_convert_fusion.2
  98.2 1.5 fusion.15
  99.7 2.0 collective-permute-start.8
  101.9 11.1 %inner.5 = (f32[8,512,128]{2,1,0:T(8,128)S(1)}, f32[8,512,128]{2,1,0:T(8,128)S(1)}) custom-call(s32[1]{0:T(128)} %bitcast.mine_ref.place_ref, bf16[128,8192]{1,0:T(8,128)(2,1)S(1)} %bitcast.91, bf16[128,8192]{1,0:T(8,128)(2,1)S(1)} %get-tuple-element.76.high_ref, bf16[4,2,2,512,128]{4,3,2,1,0:T(8,128)(2,1)S(1)} %bitcast.94, ...), custom_call_target="tpu_custom_call" | custom-call | flops 1610612736 | bytes 20971520 | tf_op jit(solution)/shard_map/inner/pallas_call | solution.py:234
  113.2 0.9 copy-done.18
  114.1 1.2 convert_add_fusion.3
  115.5 1.1 add_convert_fusion.6
  117.4 1.5 collective-permute-start.10
  118.9 2.6 %collective-permute-start.11 = (f16[2,512,128]{2,1,0:T(8,128)(2,1)S(1)}, f16[2,512,128]{2,1,0:T(8,128)(2,1)S(1)}, u32[]{:S(2)}, u32[]{:S(2)}) collective-permute-start(f16[2,512,128]{2,1,0:T(8,128)(2,1)S(1)} %pad_maximum_fusion.6), channel_id=1, source_target_pairs={{0,16},{2,18},{4,20},{6,22},{8,24},{10,26},{12,28},{14,30},{16,0},... | collective-permute-start | bytes 786440 | tf_op jit(solution)/shard_map/ppermute | solution.py:328
  121.7 0.9 collective-permute-start.17
  122.6 8.6 %collective-permute-done.12 = f16[2,512,128]{2,1,0:T(8,128)(2,1)S(1)} collective-permute-done((f16[2,512,128]{2,1,0:T(8,128)(2,1)S(1)}, f16[2,512,128]{2,1,0:T(8,128)(2,1)S(1)}, u32[]{:S(2)}, u32[]{:S(2)}) %collective-permute-start.12) | collective-permute-done | bytes 262176 | tf_op jit(solution)/shard_map/ppermute | solution.py:328
  131.2 1.1 convert_add_fusion.2
  132.6 1.6 collective-permute-start.16
  134.3 3.4 %collective-permute-start.15 = (f16[2,512,128]{2,1,0:T(8,128)(2,1)S(1)}, f16[2,512,128]{2,1,0:T(8,128)(2,1)S(1)}, u32[]{:S(2)}, u32[]{:S(2)}) collective-permute-start(f16[2,512,128]{2,1,0:T(8,128)(2,1)S(1)} %pad_maximum_fusion.7), channel_id=1, source_target_pairs={{0,16},{2,18},{4,20},{6,22},{8,24},{10,26},{12,28},{14,30},{16,0},... | collective-permute-start | bytes 786440 | tf_op jit(solution)/shard_map/ppermute | solution.py:328
  137.8 4.7 %collective-permute-done.17 = f16[4,512,128]{2,1,0:T(8,128)(2,1)S(1)} collective-permute-done((f16[4,512,128]{2,1,0:T(8,128)(2,1)S(1)}, f16[4,512,128]{2,1,0:T(8,128)(2,1)S(1)}, u32[]{:S(2)}, u32[]{:S(2)}) %collective-permute-start.17) | collective-permute-done | bytes 524320 | tf_op jit(solution)/shard_map/ppermute | solution.py:328
  142.6 1.7 collective-permute-start.23
  144.4 3.1 %collective-permute-done.16 = bf16[2,512,128]{2,1,0:T(8,128)(2,1)S(1)} collective-permute-done((bf16[2,512,128]{2,1,0:T(8,128)(2,1)S(1)}, bf16[2,512,128]{2,1,0:T(8,128)(2,1)S(1)}, u32[]{:S(2)}, u32[]{:S(2)}) %collective-permute-start.16) | collective-permute-done | bytes 262176 | tf_op jit(solution)/shard_map/ppermute | solution.py:328
  147.5 1.3 collective-permute-start.31
  148.9 1.7 collective-permute-start.29
  150.7 2.4 %collective-permute-done.14 = f16[2,512,128]{2,1,0:T(8,128)(2,1)S(1)} collective-permute-done((f16[2,512,128]{2,1,0:T(8,128)(2,1)S(1)}, f16[2,512,128]{2,1,0:T(8,128)(2,1)S(1)}, u32[]{:S(2)}, u32[]{:S(2)}) %collective-permute-start.14) | collective-permute-done | bytes 262176 | tf_op jit(solution)/shard_map/ppermute | solution.py:328
  153.4 3.1 %collective-permute-start.18 = (f16[2,512,128]{2,1,0:T(8,128)(2,1)S(1)}, f16[2,512,128]{2,1,0:T(8,128)(2,1)S(1)}, u32[]{:S(2)}, u32[]{:S(2)}) collective-permute-start(f16[2,512,128]{2,1,0:T(8,128)(2,1)S(1)} %pad_maximum_fusion.8), channel_id=1, source_target_pairs={{0,16},{2,18},{4,20},{6,22},{8,24},{10,26},{12,28},{14,30},{16,0},... | collective-permute-start | bytes 786440 | tf_op jit(solution)/shard_map/ppermute | solution.py:328
  156.4 7.9 %collective-permute-done.23 = f16[2,512,128]{2,1,0:T(8,128)(2,1)S(1)} collective-permute-done((f16[2,512,128]{2,1,0:T(8,128)(2,1)S(1)}, f16[2,512,128]{2,1,0:T(8,128)(2,1)S(1)}, u32[]{:S(2)}, u32[]{:S(2)}) %collective-permute-start.23) | collective-permute-done | bytes 262176 | tf_op jit(solution)/shard_map/ppermute | solution.py:328
  164.6 1.4 collective-permute-start.24
  166.1 3.4 %collective-permute-done.29 = bf16[2,512,128]{2,1,0:T(8,128)(2,1)S(1)} collective-permute-done((bf16[2,512,128]{2,1,0:T(8,128)(2,1)S(1)}, bf16[2,512,128]{2,1,0:T(8,128)(2,1)S(1)}, u32[]{:S(2)}, u32[]{:S(2)}) %collective-permute-start.29) | collective-permute-done | bytes 262176 | tf_op jit(solution)/shard_map/ppermute | solution.py:328
  169.5 1.2 collective-permute-start.30
  170.9 2.4 %collective-permute-start.19 = (bf16[2,512,128]{2,1,0:T(8,128)(2,1)S(1)}, bf16[2,512,128]{2,1,0:T(8,128)(2,1)S(1)}, u32[]{:S(2)}, u32[]{:S(2)}) collective-permute-start(bf16[2,512,128]{2,1,0:T(8,128)(2,1)S(1)} %subtract_convert_fusion.1), channel_id=1, source_target_pairs={{0,8},{2,10},{4,12},{6,14},{8,0},{10,2},{12,4},{14,6},{16,24},{18,... | collective-permute-start | bytes 786440 | tf_op jit(solution)/shard_map/ppermute | solution.py:328
  173.2 7.2 %collective-permute-done.24 = f16[2,512,128]{2,1,0:T(8,128)(2,1)S(1)} collective-permute-done((f16[2,512,128]{2,1,0:T(8,128)(2,1)S(1)}, f16[2,512,128]{2,1,0:T(8,128)(2,1)S(1)}, u32[]{:S(2)}, u32[]{:S(2)}) %collective-permute-start.24) | collective-permute-done | bytes 262176 | tf_op jit(solution)/shard_map/ppermute | solution.py:328
  180.5 1.0 collective-permute-start.25
  182.1 1.2 collective-permute-start.20
  183.3 6.6 %collective-permute-done.25 = bf16[2,512,128]{2,1,0:T(8,128)(2,1)S(1)} collective-permute-done((bf16[2,512,128]{2,1,0:T(8,128)(2,1)S(1)}, bf16[2,512,128]{2,1,0:T(8,128)(2,1)S(1)}, u32[]{:S(2)}, u32[]{:S(2)}) %collective-permute-start.25) | collective-permute-done | bytes 262176 | tf_op jit(solution)/shard_map/ppermute | solution.py:328
  190.2 0.6 collective-permute-start.21
  190.8 1.4 assemble.3.refs_4_
  192.3 6.4 %collective-permute-done.20.refs_1_ = bf16[4,512,128]{2,1,0:T(8,128)(2,1)S(1)} collective-permute-done((bf16[4,512,128]{2,1,0:T(8,128)(2,1)S(1)}, bf16[4,512,128]{2,1,0:T(8,128)(2,1)S(1)}, u32[]{:S(2)}, u32[]{:S(2)}) %collective-permute-start.20) | collective-permute-done | bytes 524320 | tf_op jit(solution)/shard_map/ppermute | solution.py:328
  198.7 1.0 collective-permute-done.26.refs_5_
  200.3 1.0 pad_maximum_fusion
  201.3 1.4 assemble.4.refs_8_
  202.8 2.3 %assemble.5 = bf16[16,512,512]{2,1,0:T(8,128)(2,1)} custom-call(s32[1]{0:T(128)} %bitcast.mine_ref.place_ref, bf16[4,512,128]{2,1,0:T(8,128)(2,1)S(1)} %pad_maximum_fusion.2.refs_0_, bf16[4,512,128]{2,1,0:T(8,128)(2,1)S(1)} %collective-permute-done.20.refs_1_, ...), custom_call_target="tpu_custom_call", output_to_operand_aliasing={{}: (9, {})} | custom-call | bytes 8388608 | tf_op jit(solution)/shard_map/assemble/pallas_call | solution.py:292
  (116 shorter events, 6.2 us)
Async XLA Ops:
  0.6 6.2 %copy-start.2 = (bf16[1,128,8192]{2,1,0:T(8,128)(2,1)S(1)}, bf16[1,128,8192]{2,1,0:T(8,128)(2,1)}, u32[]{:S(2)}) copy-start(bf16[1,128,8192]{2,1,0:T(8,128)(2,1)} %param.11) | copy-start | bytes 6291460
  0.6 9.9 %copy-start.19 = (s32[1,2,512]{2,1,0:T(2,128)S(1)}, s32[1,2,512]{2,1,0:T(2,128)}, u32[]{:S(2)}) copy-start(s32[1,2,512]{2,1,0:T(2,128)} %param.13) | copy-start | bytes 12292
  0.7 10.1 %copy-start.16 = (bf16[1,256,512]{2,1,0:T(8,128)(2,1)S(1)}, bf16[1,256,512]{2,1,0:T(8,128)(2,1)}, u32[]{:S(2)}) copy-start(bf16[1,256,512]{2,1,0:T(8,128)(2,1)} %param.12) | copy-start | bytes 786436
  3.8 31.0 %collective-permute-start.2 = (bf16[128,2048]{1,0:T(8,128)(2,1)}, bf16[128,2048]{1,0:T(8,128)(2,1)}, u32[]{:S(2)}, u32[]{:S(2)}) collective-permute-start(bf16[128,2048]{1,0:T(8,128)(2,1)} %slice.225), channel_id=1, source_target_pairs={{0,1},{1,0},{2,3},{3,2},{4,5},{5,4},{6,7},{7,6},{8,9},{9,8},{10,11... | collective-permute-start | bytes 1572872 | tf_op jit(solution)/shard_map/ppermute | solution.py:348
  6.8 24.2 %collective-permute-start.3 = (bf16[128,2048]{1,0:T(8,128)(2,1)S(1)}, bf16[128,2048]{1,0:T(8,128)(2,1)S(1)}, u32[]{:S(2)}, u32[]{:S(2)}) collective-permute-start(bf16[128,2048]{1,0:T(8,128)(2,1)S(1)} %slice.286), channel_id=1, source_target_pairs={{0,1},{1,0},{2,3},{3,2},{4,5},{5,4},{6,7},{7,6},{8,9},{9,8},{10,11... | collective-permute-start | bytes 1572872 | tf_op jit(solution)/shard_map/ppermute | solution.py:348
  7.6 34.7 %collective-permute-start.1 = (bf16[128,2048]{1,0:T(8,128)(2,1)}, bf16[128,2048]{1,0:T(8,128)(2,1)}, u32[]{:S(2)}, u32[]{:S(2)}) collective-permute-start(bf16[128,2048]{1,0:T(8,128)(2,1)} %slice.226), channel_id=1, source_target_pairs={{0,1},{1,0},{2,3},{3,2},{4,5},{5,4},{6,7},{7,6},{8,9},{9,8},{10,11... | collective-permute-start | bytes 1572872 | tf_op jit(solution)/shard_map/ppermute | solution.py:348
  10.5 42.2 %collective-permute-start = (bf16[128,2048]{1,0:T(8,128)(2,1)}, bf16[128,2048]{1,0:T(8,128)(2,1)}, u32[]{:S(2)}, u32[]{:S(2)}) collective-permute-start(bf16[128,2048]{1,0:T(8,128)(2,1)} %slice.227), channel_id=1, source_target_pairs={{0,1},{1,0},{2,3},{3,2},{4,5},{5,4},{6,7},{7,6},{8,9},{9,8},{10,11... | collective-permute-start | bytes 1572872 | tf_op jit(solution)/shard_map/ppermute | solution.py:348
  15.8 1.3 copy-start.5
  31.0 0.8 copy-start.13
  31.7 1.0 copy-start.14
  52.7 2.4 %copy-start.3 = (bf16[1,128,8192]{2,1,0:T(8,128)(2,1)S(1)}, bf16[1,128,8192]{2,1,0:T(8,128)(2,1)}, u32[]{:S(2)}) copy-start(bf16[1,128,8192]{2,1,0:T(8,128)(2,1)} %param.11) | copy-start | bytes 6291460
  52.7 3.0 %copy-start.6 = (bf16[8192,128]{1,0:T(8,128)(2,1)S(1)}, bf16[8192,128]{1,0:T(8,128)(2,1)}, u32[]{:S(2)}) copy-start(bf16[8192,128]{1,0:T(8,128)(2,1)} %copy-done.5) | copy-start | bytes 6291460
  55.1 16.5 %copy-start = (bf16[8192,128]{1,0:T(8,128)(2,1)}, bf16[8192,128]{1,0:T(8,128)(2,1)S(1)}, u32[]{:S(2)}) copy-start(bf16[8192,128]{1,0:T(8,128)(2,1)S(1)} %get-tuple-element.78) | copy-start | bytes 6291460
  66.7 25.9 %copy-start.12 = (f32[8,512,128]{2,1,0:T(8,128)}, f32[8,512,128]{2,1,0:T(8,128)S(1)}, u32[]{:S(2)}) copy-start(f32[8,512,128]{2,1,0:T(8,128)S(1)} %get-tuple-element.81) | copy-start | bytes 6291460
  66.8 2.7 %collective-permute-start.4 = (f16[8,512,128]{2,1,0:T(8,128)(2,1)S(1)}, f16[8,512,128]{2,1,0:T(8,128)(2,1)S(1)}, u32[]{:S(2)}, u32[]{:S(2)}) collective-permute-start(f16[8,512,128]{2,1,0:T(8,128)(2,1)S(1)} %convert_element_type.204), channel_id=1, source_target_pairs={{0,2},{2,0},{4,6},{6,4},{8,10},{10,8},{12,14},{14,12},{16,18},{18,... | collective-permute-start | bytes 3145736 | tf_op jit(solution)/shard_map/ppermute | solution.py:328
  69.6 23.1 %copy-start.15 = (f16[8,512,128]{2,1,0:T(8,128)(2,1)}, f16[8,512,128]{2,1,0:T(8,128)(2,1)S(1)}, u32[]{:S(2)}) copy-start(f16[8,512,128]{2,1,0:T(8,128)(2,1)S(1)} %collective-permute-done.4) | copy-start | bytes 3145732
  69.7 22.9 %collective-permute-start.5 = (f16[4,512,128]{2,1,0:T(8,128)(2,1)S(1)}, f16[4,512,128]{2,1,0:T(8,128)(2,1)S(1)}, u32[]{:S(2)}, u32[]{:S(2)}) collective-permute-start(f16[4,512,128]{2,1,0:T(8,128)(2,1)S(1)} %add_convert_fusion.3), channel_id=1, source_target_pairs={{0,4},{2,6},{4,0},{6,2},{8,12},{10,14},{12,8},{14,10},{16,20},{18,... | collective-permute-start | bytes 1572872 | tf_op jit(solution)/shard_map/ppermute | solution.py:328
  89.9 2.7 %copy-start.8 = (f32[8,512,128]{2,1,0:T(8,128)}, f32[8,512,128]{2,1,0:T(8,128)S(1)}, u32[]{:S(2)}) copy-start(f32[8,512,128]{2,1,0:T(8,128)S(1)} %get-tuple-element.84) | copy-start | bytes 6291460
  90.0 2.7 %copy-start.10 = (f32[8,512,128]{2,1,0:T(8,128)}, f32[8,512,128]{2,1,0:T(8,128)S(1)}, u32[]{:S(2)}) copy-start(f32[8,512,128]{2,1,0:T(8,128)S(1)} %get-tuple-element.89) | copy-start | bytes 6291460
  92.6 0.8 copy-start.17
  93.5 3.0 %collective-permute-start.7 = (f16[8,512,128]{2,1,0:T(8,128)(2,1)}, f16[8,512,128]{2,1,0:T(8,128)(2,1)}, u32[]{:S(2)}, u32[]{:S(2)}) collective-permute-start(f16[8,512,128]{2,1,0:T(8,128)(2,1)} %convert_element_type.207), channel_id=1, source_target_pairs={{0,2},{2,0},{4,6},{6,4},{8,10},{10,8},{12,14},{14,12},{16,18},{18,... | collective-permute-start | bytes 3145736 | tf_op jit(solution)/shard_map/ppermute | solution.py:328
  93.5 3.0 %copy-start.11 = (f32[8,512,128]{2,1,0:T(8,128)S(1)}, f32[8,512,128]{2,1,0:T(8,128)}, u32[]{:S(2)}) copy-start(f32[8,512,128]{2,1,0:T(8,128)} %copy-done.10) | copy-start | bytes 6291460
  96.5 5.4 %copy-start.7 = (bf16[8192,128]{1,0:T(8,128)(2,1)S(1)}, bf16[8192,128]{1,0:T(8,128)(2,1)}, u32[]{:S(2)}) copy-start(bf16[8192,128]{1,0:T(8,128)(2,1)} %copy-done.5) | copy-start | bytes 6291460
  97.8 4.1 %copy-start.1 = (bf16[8192,128]{1,0:T(8,128)(2,1)S(1)}, bf16[8192,128]{1,0:T(8,128)(2,1)}, u32[]{:S(2)}) copy-start(bf16[8192,128]{1,0:T(8,128)(2,1)} %copy-done) | copy-start | bytes 6291460
  97.8 4.1 %copy-start.4 = (bf16[1,128,8192]{2,1,0:T(8,128)(2,1)S(1)}, bf16[1,128,8192]{2,1,0:T(8,128)(2,1)}, u32[]{:S(2)}) copy-start(bf16[1,128,8192]{2,1,0:T(8,128)(2,1)} %param.11) | copy-start | bytes 6291460
  97.8 15.4 %collective-permute-start.9 = (f16[4,512,128]{2,1,0:T(8,128)(2,1)S(1)}, f16[4,512,128]{2,1,0:T(8,128)(2,1)S(1)}, u32[]{:S(2)}, u32[]{:S(2)}) collective-permute-start(f16[4,512,128]{2,1,0:T(8,128)(2,1)S(1)} %add_convert_fusion.2), channel_id=1, source_target_pairs={{0,4},{2,6},{4,0},{6,2},{8,12},{10,14},{12,8},{14,10},{16,20},{18,... | collective-permute-start | bytes 1572872 | tf_op jit(solution)/shard_map/ppermute | solution.py:328
  99.7 13.6 %collective-permute-start.8 = (f16[2,512,128]{2,1,0:T(8,128)(2,1)S(1)}, f16[2,512,128]{2,1,0:T(8,128)(2,1)S(1)}, u32[]{:S(2)}, u32[]{:S(2)}) collective-permute-start(f16[2,512,128]{2,1,0:T(8,128)(2,1)S(1)} %add_convert_fusion.7), channel_id=1, source_target_pairs={{0,8},{2,10},{4,12},{6,14},{8,0},{10,2},{12,4},{14,6},{16,24},{18,... | collective-permute-start | bytes 786440 | tf_op jit(solution)/shard_map/ppermute | solution.py:328
  101.8 14.7 %collective-permute-start.6 = (f16[8,512,128]{2,1,0:T(8,128)(2,1)}, f16[8,512,128]{2,1,0:T(8,128)(2,1)S(1)}, u32[]{:S(2)}, u32[]{:S(2)}) collective-permute-start(f16[8,512,128]{2,1,0:T(8,128)(2,1)} %convert_element_type.208), channel_id=1, source_target_pairs={{0,2},{2,0},{4,6},{6,4},{8,10},{10,8},{12,14},{14,12},{16,18},{18,... | collective-permute-start | bytes 3145736 | tf_op jit(solution)/shard_map/ppermute | solution.py:328
  113.1 1.0 copy-start.18
  113.2 3.4 %copy-start.9 = (f32[8,512,128]{2,1,0:T(8,128)S(1)}, f32[8,512,128]{2,1,0:T(8,128)}, u32[]{:S(2)}) copy-start(f32[8,512,128]{2,1,0:T(8,128)} %copy-done.8) | copy-start | bytes 6291460
  116.8 4.8 %collective-permute-start.13 = (f16[8,512,128]{2,1,0:T(8,128)(2,1)S(1)}, f16[8,512,128]{2,1,0:T(8,128)(2,1)S(1)}, u32[]{:S(2)}, u32[]{:S(2)}) collective-permute-start(f16[8,512,128]{2,1,0:T(8,128)(2,1)S(1)} %convert_element_type.227), channel_id=1, source_target_pairs={{0,2},{2,0},{4,6},{6,4},{8,10},{10,8},{12,14},{14,12},{16,18},{18,... | collective-permute-start | bytes 3145736 | tf_op jit(solution)/shard_map/ppermute | solution.py:328
  117.3 13.9 %collective-permute-start.12 = (f16[2,512,128]{2,1,0:T(8,128)(2,1)S(1)}, f16[2,512,128]{2,1,0:T(8,128)(2,1)S(1)}, u32[]{:S(2)}, u32[]{:S(2)}) collective-permute-start(f16[2,512,128]{2,1,0:T(8,128)(2,1)S(1)} %add_convert_fusion.6), channel_id=1, source_target_pairs={{0,8},{2,10},{4,12},{6,14},{8,0},{10,2},{12,4},{14,6},{16,24},{18,... | collective-permute-start | bytes 786440 | tf_op jit(solution)/shard_map/ppermute | solution.py:328
  117.4 16.8 %collective-permute-start.10 = (f16[4,512,128]{2,1,0:T(8,128)(2,1)S(1)}, f16[4,512,128]{2,1,0:T(8,128)(2,1)S(1)}, u32[]{:S(2)}, u32[]{:S(2)}) collective-permute-start(f16[4,512,128]{2,1,0:T(8,128)(2,1)S(1)} %add_convert_fusion.1), channel_id=1, source_target_pairs={{0,4},{2,6},{4,0},{6,2},{8,12},{10,14},{12,8},{14,10},{16,20},{18,... | collective-permute-start | bytes 1572872 | tf_op jit(solution)/shard_map/ppermute | solution.py:328
  118.9 13.5 %collective-permute-start.11 = (f16[2,512,128]{2,1,0:T(8,128)(2,1)S(1)}, f16[2,512,128]{2,1,0:T(8,128)(2,1)S(1)}, u32[]{:S(2)}, u32[]{:S(2)}) collective-permute-start(f16[2,512,128]{2,1,0:T(8,128)(2,1)S(1)} %pad_maximum_fusion.6), channel_id=1, source_target_pairs={{0,16},{2,18},{4,20},{6,22},{8,24},{10,26},{12,28},{14,30},{16,0},... | collective-permute-start | bytes 786440 | tf_op jit(solution)/shard_map/ppermute | solution.py:328
  121.7 20.8 %collective-permute-start.17 = (f16[4,512,128]{2,1,0:T(8,128)(2,1)S(1)}, f16[4,512,128]{2,1,0:T(8,128)(2,1)S(1)}, u32[]{:S(2)}, u32[]{:S(2)}) collective-permute-start(f16[4,512,128]{2,1,0:T(8,128)(2,1)S(1)} %add_convert_fusion), channel_id=1, source_target_pairs={{0,4},{2,6},{4,0},{6,2},{8,12},{10,14},{12,8},{14,10},{16,20},{18,... | collective-permute-start | bytes 1572872 | tf_op jit(solution)/shard_map/ppermute | solution.py:328
  132.6 14.9 %collective-permute-start.16 = (bf16[2,512,128]{2,1,0:T(8,128)(2,1)S(1)}, bf16[2,512,128]{2,1,0:T(8,128)(2,1)S(1)}, u32[]{:S(2)}, u32[]{:S(2)}) collective-permute-start(bf16[2,512,128]{2,1,0:T(8,128)(2,1)S(1)} %subtract_convert_fusion.3), channel_id=1, source_target_pairs={{0,8},{2,10},{4,12},{6,14},{8,0},{10,2},{12,4},{14,6},{16,24},{18,... | collective-permute-start | bytes 786440 | tf_op jit(solution)/shard_map/ppermute | solution.py:328
  134.3 14.5 %collective-permute-start.15 = (f16[2,512,128]{2,1,0:T(8,128)(2,1)S(1)}, f16[2,512,128]{2,1,0:T(8,128)(2,1)S(1)}, u32[]{:S(2)}, u32[]{:S(2)}) collective-permute-start(f16[2,512,128]{2,1,0:T(8,128)(2,1)S(1)} %pad_maximum_fusion.7), channel_id=1, source_target_pairs={{0,16},{2,18},{4,20},{6,22},{8,24},{10,26},{12,28},{14,30},{16,0},... | collective-permute-start | bytes 786440 | tf_op jit(solution)/shard_map/ppermute | solution.py:328
  137.8 15.3 %collective-permute-start.14 = (f16[2,512,128]{2,1,0:T(8,128)(2,1)S(1)}, f16[2,512,128]{2,1,0:T(8,128)(2,1)S(1)}, u32[]{:S(2)}, u32[]{:S(2)}) collective-permute-start(f16[2,512,128]{2,1,0:T(8,128)(2,1)S(1)} %add_convert_fusion.5), channel_id=1, source_target_pairs={{0,8},{2,10},{4,12},{6,14},{8,0},{10,2},{12,4},{14,6},{16,24},{18,... | collective-permute-start | bytes 786440 | tf_op jit(solution)/shard_map/ppermute | solution.py:328
  142.6 21.7 %collective-permute-start.23 = (f16[2,512,128]{2,1,0:T(8,128)(2,1)S(1)}, f16[2,512,128]{2,1,0:T(8,128)(2,1)S(1)}, u32[]{:S(2)}, u32[]{:S(2)}) collective-permute-start(f16[2,512,128]{2,1,0:T(8,128)(2,1)S(1)} %add_convert_fusion.4), channel_id=1, source_target_pairs={{0,8},{2,10},{4,12},{6,14},{8,0},{10,2},{12,4},{14,6},{16,24},{18,... | collective-permute-start | bytes 786440 | tf_op jit(solution)/shard_map/ppermute | solution.py:328
  147.5 34.0 %collective-permute-start.31 = (bf16[4,512,128]{2,1,0:T(8,128)(2,1)S(1)}, bf16[4,512,128]{2,1,0:T(8,128)(2,1)S(1)}, u32[]{:S(2)}, u32[]{:S(2)}) collective-permute-start(bf16[4,512,128]{2,1,0:T(8,128)(2,1)S(1)} %pad_maximum_fusion.1.refs_0_), channel_id=1, source_target_pairs={{0,4},{2,6},{4,0},{6,2},{8,12},{10,14},{12,8},{14,10},{16,20},{18,... | collective-permute-start | bytes 1572872 | tf_op jit(solution)/shard_map/ppermute | solution.py:328
  148.9 20.5 %collective-permute-start.29 = (bf16[2,512,128]{2,1,0:T(8,128)(2,1)S(1)}, bf16[2,512,128]{2,1,0:T(8,128)(2,1)S(1)}, u32[]{:S(2)}, u32[]{:S(2)}) collective-permute-start(bf16[2,512,128]{2,1,0:T(8,128)(2,1)S(1)} %subtract_convert_fusion.2), channel_id=1, source_target_pairs={{0,8},{2,10},{4,12},{6,14},{8,0},{10,2},{12,4},{14,6},{16,24},{18,... | collective-permute-start | bytes 786440 | tf_op jit(solution)/shard_map/ppermute | solution.py:328
  153.4 17.4 %collective-permute-start.18 = (f16[2,512,128]{2,1,0:T(8,128)(2,1)S(1)}, f16[2,512,128]{2,1,0:T(8,128)(2,1)S(1)}, u32[]{:S(2)}, u32[]{:S(2)}) collective-permute-start(f16[2,512,128]{2,1,0:T(8,128)(2,1)S(1)} %pad_maximum_fusion.8), channel_id=1, source_target_pairs={{0,16},{2,18},{4,20},{6,22},{8,24},{10,26},{12,28},{14,30},{16,0},... | collective-permute-start | bytes 786440 | tf_op jit(solution)/shard_map/ppermute | solution.py:328
  164.6 15.8 %collective-permute-start.24 = (f16[2,512,128]{2,1,0:T(8,128)(2,1)S(1)}, f16[2,512,128]{2,1,0:T(8,128)(2,1)S(1)}, u32[]{:S(2)}, u32[]{:S(2)}) collective-permute-start(f16[2,512,128]{2,1,0:T(8,128)(2,1)S(1)} %pad_maximum_fusion.9), channel_id=1, source_target_pairs={{0,16},{2,18},{4,20},{6,22},{8,24},{10,26},{12,28},{14,30},{16,0},... | collective-permute-start | bytes 786440 | tf_op jit(solution)/shard_map/ppermute | solution.py:328
  169.5 20.4 %collective-permute-start.30 = (bf16[4,512,128]{2,1,0:T(8,128)(2,1)S(1)}, bf16[4,512,128]{2,1,0:T(8,128)(2,1)S(1)}, u32[]{:S(2)}, u32[]{:S(2)}) collective-permute-start(bf16[4,512,128]{2,1,0:T(8,128)(2,1)S(1)} %pad_maximum_fusion.4.refs_0_), channel_id=1, source_target_pairs={{0,4},{2,6},{4,0},{6,2},{8,12},{10,14},{12,8},{14,10},{16,20},{18,... | collective-permute-start | bytes 1572872 | tf_op jit(solution)/shard_map/ppermute | solution.py:328
  170.9 11.1 %collective-permute-start.19 = (bf16[2,512,128]{2,1,0:T(8,128)(2,1)S(1)}, bf16[2,512,128]{2,1,0:T(8,128)(2,1)S(1)}, u32[]{:S(2)}, u32[]{:S(2)}) collective-permute-start(bf16[2,512,128]{2,1,0:T(8,128)(2,1)S(1)} %subtract_convert_fusion.1), channel_id=1, source_target_pairs={{0,8},{2,10},{4,12},{6,14},{8,0},{10,2},{12,4},{14,6},{16,24},{18,... | collective-permute-start | bytes 786440 | tf_op jit(solution)/shard_map/ppermute | solution.py:328
  180.5 9.3 %collective-permute-start.25 = (bf16[2,512,128]{2,1,0:T(8,128)(2,1)S(1)}, bf16[2,512,128]{2,1,0:T(8,128)(2,1)S(1)}, u32[]{:S(2)}, u32[]{:S(2)}) collective-permute-start(bf16[2,512,128]{2,1,0:T(8,128)(2,1)S(1)} %subtract_convert_fusion), channel_id=1, source_target_pairs={{0,4},{2,6},{4,0},{6,2},{8,12},{10,14},{12,8},{14,10},{16,20},{18,... | collective-permute-start | bytes 786440 | tf_op jit(solution)/shard_map/ppermute | solution.py:328
  181.5 8.7 %collective-permute-start.32 = (bf16[4,512,128]{2,1,0:T(8,128)(2,1)S(1)}, bf16[4,512,128]{2,1,0:T(8,128)(2,1)S(1)}, u32[]{:S(2)}, u32[]{:S(2)}) collective-permute-start(bf16[4,512,128]{2,1,0:T(8,128)(2,1)S(1)} %pad_maximum_fusion.1.refs_0_), channel_id=1, source_target_pairs={{0,2},{2,0},{4,6},{6,4},{8,10},{10,8},{12,14},{14,12},{16,18},{18,... | collective-permute-start | bytes 1572872 | tf_op jit(solution)/shard_map/ppermute | solution.py:328
  181.5 9.2 %collective-permute-start.33 = (bf16[4,512,128]{2,1,0:T(8,128)(2,1)S(1)}, bf16[4,512,128]{2,1,0:T(8,128)(2,1)S(1)}, u32[]{:S(2)}, u32[]{:S(2)}) collective-permute-start(bf16[4,512,128]{2,1,0:T(8,128)(2,1)S(1)} %collective-permute-done.31.refs_1_), channel_id=1, source_target_pairs={{0,2},{2,0},{4,6},{6,4},{8,10},{10,8},{12,14},{14,12},{16,18},{18,... | collective-permute-start | bytes 1572872 | tf_op jit(solution)/shard_map/ppermute | solution.py:328
  182.1 16.6 %collective-permute-start.20 = (bf16[4,512,128]{2,1,0:T(8,128)(2,1)S(1)}, bf16[4,512,128]{2,1,0:T(8,128)(2,1)S(1)}, u32[]{:S(2)}, u32[]{:S(2)}) collective-permute-start(bf16[4,512,128]{2,1,0:T(8,128)(2,1)S(1)} %pad_maximum_fusion.2.refs_0_), channel_id=1, source_target_pairs={{0,4},{2,6},{4,0},{6,2},{8,12},{10,14},{12,8},{14,10},{16,20},{18,... | collective-permute-start | bytes 1572872 | tf_op jit(solution)/shard_map/ppermute | solution.py:328
  189.9 9.7 %collective-permute-start.26 = (bf16[4,512,128]{2,1,0:T(8,128)(2,1)S(1)}, bf16[4,512,128]{2,1,0:T(8,128)(2,1)S(1)}, u32[]{:S(2)}, u32[]{:S(2)}) collective-permute-start(bf16[4,512,128]{2,1,0:T(8,128)(2,1)S(1)} %pad_maximum_fusion.3.refs_4_), channel_id=1, source_target_pairs={{0,8},{2,10},{4,12},{6,14},{8,0},{10,2},{12,4},{14,6},{16,24},{18,... | collective-permute-start | bytes 1572872 | tf_op jit(solution)/shard_map/ppermute | solution.py:328
  190.0 9.7 %collective-permute-start.34 = (bf16[4,512,128]{2,1,0:T(8,128)(2,1)S(1)}, bf16[4,512,128]{2,1,0:T(8,128)(2,1)S(1)}, u32[]{:S(2)}, u32[]{:S(2)}) collective-permute-start(bf16[4,512,128]{2,1,0:T(8,128)(2,1)S(1)} %pad_maximum_fusion.4.refs_0_), channel_id=1, source_target_pairs={{0,2},{2,0},{4,6},{6,4},{8,10},{10,8},{12,14},{14,12},{16,18},{18,... | collective-permute-start | bytes 1572872 | tf_op jit(solution)/shard_map/ppermute | solution.py:328
  190.2 12.6 %collective-permute-start.21 = (bf16[4,512,128]{2,1,0:T(8,128)(2,1)S(1)}, bf16[4,512,128]{2,1,0:T(8,128)(2,1)S(1)}, u32[]{:S(2)}, u32[]{:S(2)}) collective-permute-start(bf16[4,512,128]{2,1,0:T(8,128)(2,1)S(1)} %pad_maximum_fusion.2.refs_0_), channel_id=1, source_target_pairs={{0,2},{2,0},{4,6},{6,4},{8,10},{10,8},{12,14},{14,12},{16,18},{18,... | collective-permute-start | bytes 1572872 | tf_op jit(solution)/shard_map/ppermute | solution.py:328
  190.8 12.0 %collective-permute-start.27 = (bf16[4,512,128]{2,1,0:T(8,128)(2,1)S(1)}, bf16[4,512,128]{2,1,0:T(8,128)(2,1)S(1)}, u32[]{:S(2)}, u32[]{:S(2)}) collective-permute-start(bf16[4,512,128]{2,1,0:T(8,128)(2,1)S(1)} %pad_maximum_fusion.3.refs_4_), channel_id=1, source_target_pairs={{0,2},{2,0},{4,6},{6,4},{8,10},{10,8},{12,14},{14,12},{16,18},{18,... | collective-permute-start | bytes 1572872 | tf_op jit(solution)/shard_map/ppermute | solution.py:328
  198.7 2.6 %collective-permute-start.35 = (bf16[4,512,128]{2,1,0:T(8,128)(2,1)S(1)}, bf16[4,512,128]{2,1,0:T(8,128)(2,1)S(1)}, u32[]{:S(2)}, u32[]{:S(2)}) collective-permute-start(bf16[4,512,128]{2,1,0:T(8,128)(2,1)S(1)} %collective-permute-done.30.refs_1_), channel_id=1, source_target_pairs={{0,2},{2,0},{4,6},{6,4},{8,10},{10,8},{12,14},{14,12},{16,18},{18,... | collective-permute-start | bytes 1572872 | tf_op jit(solution)/shard_map/ppermute | solution.py:328
  199.6 3.1 %collective-permute-start.22 = (bf16[4,512,128]{2,1,0:T(8,128)(2,1)S(1)}, bf16[4,512,128]{2,1,0:T(8,128)(2,1)S(1)}, u32[]{:S(2)}, u32[]{:S(2)}) collective-permute-start(bf16[4,512,128]{2,1,0:T(8,128)(2,1)S(1)} %collective-permute-done.20.refs_1_), channel_id=1, source_target_pairs={{0,2},{2,0},{4,6},{6,4},{8,10},{10,8},{12,14},{14,12},{16,18},{18,... | collective-permute-start | bytes 1572872 | tf_op jit(solution)/shard_map/ppermute | solution.py:328
  199.6 3.1 %collective-permute-start.28 = (bf16[4,512,128]{2,1,0:T(8,128)(2,1)S(1)}, bf16[4,512,128]{2,1,0:T(8,128)(2,1)S(1)}, u32[]{:S(2)}, u32[]{:S(2)}) collective-permute-start(bf16[4,512,128]{2,1,0:T(8,128)(2,1)S(1)} %collective-permute-done.26.refs_5_), channel_id=1, source_target_pairs={{0,2},{2,0},{4,6},{6,4},{8,10},{10,8},{12,14},{14,12},{16,18},{18,... | collective-permute-start | bytes 1572872 | tf_op jit(solution)/shard_map/ppermute | solution.py:328

commit v14 on v13

--- a/solution.py
+++ b/solution.py
@@ -18,81 +18,37 @@
 
 
 def forward_kernel(part_ref, weights_ref, turned_ref, product_ref):
-    @pl.when(pl.program_id(0) == 0)
-    def _():
-        product_ref[...] = jnp.zeros_like(product_ref)
-
-    part = part_ref[...]
-    turned_ref[...] = part.T
-    product_ref[...] += jnp.dot(part, weights_ref[...], preferred_element_type=F32)
+    depth = part_ref.shape[1]
+    block = depth // SLABS
+    product = jnp.zeros(product_ref.shape, F32)
+    for begin in range(0, depth, block):
+        place = pl.ds(begin, block)
+        part = part_ref[:, place]
+        product += jnp.dot(part, weights_ref[place, :], preferred_element_type=F32)
+        turned_ref[place, :] = part.T
+    product_ref[...] = product
 
 
 def forward(part, weights):
     rows, depth = part.shape
     columns = weights.shape[1]
-    block = depth // SLABS
+    vmem = pl.BlockSpec(memory_space=pltpu.VMEM)
     return pl.pallas_call(
         forward_kernel,
-        grid=(SLABS,),
-        in_specs=[
-            pl.BlockSpec((rows, block), lambda d: (0, d)),
-            pl.BlockSpec((block, columns), lambda d: (d, 0)),
-        ],
-        out_specs=[
-            pl.BlockSpec((block, rows), lambda d: (d, 0)),
-            pl.BlockSpec((rows, columns), lambda d: (0, 0)),
-        ],
+        in_specs=[vmem, vmem],
+        out_specs=[vmem, vmem],
         out_shape=[
             jax.ShapeDtypeStruct((depth, rows), BF16),
             jax.ShapeDtypeStruct((rows, columns), F32),
         ],
-        compiler_params=pltpu.CompilerParams(vmem_limit_bytes=14 * MIB),
+        compiler_params=pltpu.CompilerParams(vmem_limit_bytes=8 * MIB),
         cost_estimate=pl.CostEstimate(
             flops=2 * rows * depth * columns,
             bytes_accessed=2 * depth * columns + 4 * rows * depth,
             transcendentals=0,
         ),
         name="forward",
-    )(part, pinned(weights))
-
-
-def arrive_kernel(piece, part_ref, weights_ref, *refs):
-    natural_ref, turned_ref, product_ref = refs[-3:]
-    block = part_ref.shape[1]
-    place = pl.ds(piece * block, block)
-    part = part_ref[...]
-    natural_ref[:, place] = part
-    turned_ref[place, :] = part.T
-    product = jnp.dot(part, weights_ref[...], preferred_element_type=F32)
-    if len(refs) > 3:
-        product = product + refs[2][...]
-    product_ref[...] = product
-
-
-def arrive(piece, part, weights, before):
-    rows, block = part.shape
-    depth, columns = weights.shape
-    whole = pl.BlockSpec(memory_space=pltpu.VMEM)
-    return pl.pallas_call(
-        functools.partial(arrive_kernel, piece),
-        grid=(1,),
-        in_specs=[whole, pl.BlockSpec((block, columns), lambda d: (piece, 0))]
-        + [whole] * len(before),
-        out_specs=[whole] * 3,
-        out_shape=[
-            jax.ShapeDtypeStruct((rows, depth), BF16),
-            jax.ShapeDtypeStruct((depth, rows), BF16),
-            jax.ShapeDtypeStruct((rows, columns), F32),
-        ],
-        input_output_aliases={2: 0, 3: 1, 4: 2} if before else {},
-        compiler_params=pltpu.CompilerParams(vmem_limit_bytes=10 * MIB),
-        cost_estimate=pl.CostEstimate(
-            flops=2 * rows * block * columns,
-            bytes_accessed=2 * block * columns + 6 * rows * block,
-            transcendentals=0,
-        ),
-        name="arrive",
-    )(part, pinned(weights), *before)
+    )(part, weights)
 
 
 def pinned(array):
@@ -340,29 +296,15 @@
         ids[:, :, None] == jnp.arange(store, dtype=ids.dtype)[None, None, :], axis=1
     ).astype(F32)
     if shards == 2:
-        block = depth // SLABS
-        parts = []
-        source = own_bank
-        for d in range(SLABS):
-            part, source = tied(source[:, d * block : (d + 1) * block], source)
-            parts.append(lax.ppermute(part, "fsdp", [(0, 1), (1, 0)]))
-        own_turned, own_product = forward(own_bank, global_weights)
-        joined = ()
-        for d, part in enumerate(parts):
-            joined = arrive(d, part, global_weights, joined)
-        banks = (own_bank, joined[0])
-        turned = (own_turned, joined[1])
-        products = (own_product, joined[2])
+        banks = (own_bank, lax.ppermute(own_bank, "fsdp", [(0, 1), (1, 0)]))
         swap = lax.axis_index("fsdp") == 1
         target = jnp.where(swap, jnp.roll(target, half, axis=0), target)
         count = jnp.where(swap, jnp.roll(count, half, axis=1), count)
     else:
         whole = lax.all_gather(own_bank, "fsdp", axis=0, tiled=True)
         banks = (whole[:half], whole[half:])
-        turned, products = zip(*(forward(bank, global_weights) for bank in banks))
     count = count[:, :, None]
 
-    turned = [array.reshape(cut[:4] + (half,)) for array in turned]
     place = mine.reshape(1).astype(jnp.int32)
     if chunks == 4:
         calls = [(2 * width, width), (0, 2 * width), (3 * width, width)]
@@ -378,6 +320,12 @@
         tied(momentum[:, begin : begin + width], pair_start[:, :, begin : begin + width])
         for begin in begins
     ]
+
+    own = forward(banks[0], global_weights)
+    received, (shares, own) = tied(banks[1], (shares, own))
+    turned, products = zip(own, forward(received, global_weights))
+    banks = (banks[0], received)
+    turned = [array.reshape(cut[:4] + (half,)) for array in turned]
 
     def parted(terms, span):
         size = terms[0].shape[0] // len(span)

time: 206 us -> 202 us (0.981)
  waiting for transfers between devices: 82.5 us -> 104 us
  Pallas kernels: 59.4 us -> 52.1 us
  local copies, waits for them, and re-layouts: 13.4 us -> 6.74 us
  starting transfers between devices: 36.8 us -> 30.8 us
  other arithmetic: 11.6 us -> 6.68 us
    ppermute x32, waiting for transfers between devices: 55.6 us -> 67.8 us  [swapped(): return lax.ppermute(array, 'rep', pairs)]
    pallas_call x5 -> x2, Pallas kernels: 13.8 us -> 4.23 us  [forward(): pl.pallas_call(forward_kernel, in_specs=[vmem, vmem], out_specs=[vmem, vm...]
    ppermute x4 -> x1, waiting for transfers between devices: 26.9 us -> 35.8 us  [per_device(): banks = (own_bank, lax.ppermute(own_bank, 'fsdp', [(0, 1), (1, 0)]))]
    slice x4 -> x0, local copies, waits for them, and re-layouts: 4.81 us -> none  [per_device(): part, source = tied(source[:, d * block:(d + 1) * block], source)]
    ppermute x32, starting transfers between devices: 31.8 us -> 27.8 us  [swapped(): return lax.ppermute(array, 'rep', pairs)]
    convert_element_type x4, other arithmetic: 2.93 us -> 0.57 us  [per_device(): sends = [send.astype(WIRE) for send in changes[::2]]]
    pallas_call x3, Pallas kernels: 40.5 us -> 42.7 us  [inner(): pl.pallas_call(functools.partial(inner_kernel, float(tokens), kept), grid...]
    convert_element_type x8, other arithmetic: 3.21 us -> 1.05 us  [parted(): sum((term.astype(F32) for term in part)).astype(WIRE)]
  transfers between devices with their start and end apart: 36 -> 33, of which waited for: 15 -> 16; matrix products, arithmetic and copies ran while one was open for 7% -> 4% of each run, Pallas kernels for 21% -> 17%
where the time goes in v14:
time: 202 us; the launch traced here: 201 us
  waiting for transfers between devices  104 us (51%)
  Pallas kernels  52.1 us (26%)
  starting transfers between devices  30.8 us (15%)
  local copies, waits for them, and re-layouts  6.74 us (3%)
  other arithmetic  6.68 us (3%)
    ppermute x32, waiting for transfers between devices, swapped(): return lax.ppermute(array, 'rep', pairs)  67.8 us
    pallas_call x3, Pallas kernels, inner(): pl.pallas_call(functools.partial(inner_kernel, float(tokens), kept), grid...  42.7 us
    ppermute x1, waiting for transfers between devices, per_device(): banks = (own_bank, lax.ppermute(own_bank, 'fsdp', [(0, 1), (1, 0)]))  35.8 us
    ppermute x32, starting transfers between devices, swapped(): return lax.ppermute(array, 'rep', pairs)  27.8 us
    pallas_call x3, Pallas kernels, assemble(): pl.pallas_call(functools.partial(assemble_kernel, begins, offsets), in_sp...  5.14 us
    unnamed x20, local copies, waits for them, and re-layouts  4.29 us
    pallas_call x2, Pallas kernels, forward(): pl.pallas_call(forward_kernel, in_specs=[vmem, vmem], out_specs=[vmem, vm...  4.23 us
  transfers between devices with their start and end apart: 33, of which 16 were waited for; matrix products, arithmetic and copies ran while one was open for 4% of the time, Pallas kernels for 17%

profile of v14, /device:TPU:0, one launch (start us, length us, event | category | flops | bytes accessed | tf_op | source)
XLA Modules:
  0.0 201.2 jit_solution(13935323105826696857)
XLA Ops:
  0.6 3.0 %collective-permute-start = (bf16[128,8192]{1,0:T(8,128)(2,1)}, bf16[128,8192]{1,0:T(8,128)(2,1)}, u32[]{:S(2)}, u32[]{:S(2)}) collective-permute-start(bf16[128,8192]{1,0:T(8,128)(2,1)} %bitcast.84), channel_id=1, source_target_pairs={{0,1},{1,0},{2,3},{3,2},{4,5},{5,4},{6,7},{7,6},{8,9},{9,8},{10,11... | collective-permute-start | bytes 6291464 | tf_op jit(solution)/shard_map/ppermute | solution.py:299
  3.7 0.9 convert_reduce_fusion
  4.6 0.1 copy.21
  4.8 0.9 copy.22
  5.6 1.4 dynamic-slice_bitcast_fusion
  7.0 1.1 pad_maximum_fusion.5
  8.1 0.9 copy-done.2
  9.0 3.4 %copy-done = bf16[8192,512]{1,0:T(8,128)(2,1)S(1)} copy-done((bf16[8192,512]{1,0:T(8,128)(2,1)S(1)}, bf16[8192,512]{1,0:T(8,128)(2,1)}, u32[]{:S(2)}) %copy-start) | copy-done | bytes 8388632
  12.4 1.3 forward.2
  13.8 35.8 %collective-permute-done.part_ref.high_ref = bf16[128,8192]{1,0:T(8,128)(2,1)} collective-permute-done((bf16[128,8192]{1,0:T(8,128)(2,1)}, bf16[128,8192]{1,0:T(8,128)(2,1)}, u32[]{:S(2)}, u32[]{:S(2)}) %collective-permute-start) | collective-permute-done | bytes 2097184 | tf_op jit(solution)/shard_map/ppermute | solution.py:299
  49.6 3.0 %forward.3 = (bf16[8192,128]{1,0:T(8,128)(2,1)S(1)}, f32[128,512]{1,0:T(8,128)S(1)}) custom-call(bf16[128,8192]{1,0:T(8,128)(2,1)} %collective-permute-done.part_ref.high_ref, bf16[8192,512]{1,0:T(8,128)(2,1)S(1)} %copy-done.1), custom_call_target="tpu_custom_call" | custom-call | flops 1073741824 | bytes 12582912 | tf_op jit(solution)/shard_map/forward/pallas_call | solution.py:36
  52.6 11.8 %inner.3 = (f32[8,512,128]{2,1,0:T(8,128)S(1)}, f32[8,512,128]{2,1,0:T(8,128)S(1)}) custom-call(s32[1]{0:T(128)} %bitcast.mine_ref.place_ref, bf16[128,8192]{1,0:T(8,128)(2,1)S(1)} %bitcast.86, bf16[128,8192]{1,0:T(8,128)(2,1)} %collective-permute-done.part_ref.high_ref, bf16[4,2,2,512,128]{4,3,2,1,0:T(8,128)(2,1)S(1)} %bitcast.89, ...), custom_call_target="tpu_custom_call" | custom-call | flops 1610612736 | bytes 20971520 | tf_op jit(solution)/shard_map/inner/pallas_call | solution.py:190
  64.4 0.1 convert_element_type.204
  64.7 2.6 %collective-permute-done.1 = f16[8,512,128]{2,1,0:T(8,128)(2,1)S(1)} collective-permute-done((f16[8,512,128]{2,1,0:T(8,128)(2,1)S(1)}, f16[8,512,128]{2,1,0:T(8,128)(2,1)S(1)}, u32[]{:S(2)}, u32[]{:S(2)}) %collective-permute-start.1) | collective-permute-done | bytes 1048608 | tf_op jit(solution)/shard_map/ppermute | solution.py:284
  67.3 0.1 add_convert_fusion.3
  67.5 1.8 collective-permute-start.2
  69.2 19.1 %inner.4 = (f32[8,512,128]{2,1,0:T(8,128)S(1)}, f32[8,512,128]{2,1,0:T(8,128)S(1)}, f32[8,512,128]{2,1,0:T(8,128)S(1)}, f32[8,512,128]{2,1,0:T(8,128)S(1)}) custom-call(s32[1]{0:T(128)} %bitcast.mine_ref.place_ref, bf16[128,8192]{1,0:T(8,128)(2,1)S(1)} %bitcast.87, bf16[128,8192]{1,0:T(8,128)(2,1)} %collective-permute-done.part_ref.high_ref, ...), custom_call_target="tpu_custom_call" | custom-call | flops 3221225472 | bytes 41943040 | tf_op jit(solution)/shard_map/inner/pallas_call | solution.py:190
  88.3 0.1 convert_element_type.207
  88.5 0.1 convert_element_type.208
  88.8 2.6 %collective-permute-done.4 = f16[8,512,128]{2,1,0:T(8,128)(2,1)S(1)} collective-permute-done((f16[8,512,128]{2,1,0:T(8,128)(2,1)S(1)}, f16[8,512,128]{2,1,0:T(8,128)(2,1)S(1)}, u32[]{:S(2)}, u32[]{:S(2)}) %collective-permute-start.4) | collective-permute-done | bytes 1048608 | tf_op jit(solution)/shard_map/ppermute | solution.py:284
  91.5 0.1 add_convert_fusion.2
  91.6 0.4 collective-permute-start.6
  92.0 1.8 collective-permute-start.5
  93.8 11.8 %inner.5 = (f32[8,512,128]{2,1,0:T(8,128)S(1)}, f32[8,512,128]{2,1,0:T(8,128)S(1)}) custom-call(s32[1]{0:T(128)} %bitcast.mine_ref.place_ref, bf16[128,8192]{1,0:T(8,128)(2,1)S(1)} %bitcast.88, bf16[128,8192]{1,0:T(8,128)(2,1)} %collective-permute-done.part_ref.high_ref, bf16[4,2,2,512,128]{4,3,2,1,0:T(8,128)(2,1)S(1)} %bitcast.91, ...), custom_call_target="tpu_custom_call" | custom-call | flops 1610612736 | bytes 20971520 | tf_op jit(solution)/shard_map/inner/pallas_call | solution.py:190
  105.6 0.1 convert_element_type.227
  106.2 0.1 add_convert_fusion.1
  106.4 0.6 collective-permute-start.10
  106.9 1.0 collective-permute-start.9
  107.9 1.0 collective-permute-start.7
  108.9 2.6 %collective-permute-start.8 = (f16[2,512,128]{2,1,0:T(8,128)(2,1)S(1)}, f16[2,512,128]{2,1,0:T(8,128)(2,1)S(1)}, u32[]{:S(2)}, u32[]{:S(2)}) collective-permute-start(f16[2,512,128]{2,1,0:T(8,128)(2,1)S(1)} %pad_maximum_fusion.6), channel_id=1, source_target_pairs={{0,16},{2,18},{4,20},{6,22},{8,24},{10,26},{12,28},{14,30},{16,0},... | collective-permute-start | bytes 786440 | tf_op jit(solution)/shard_map/ppermute | solution.py:284
  111.5 0.2 add_convert_fusion
  111.6 1.1 collective-permute-start.14
  112.8 7.9 %collective-permute-done.9 = f16[2,512,128]{2,1,0:T(8,128)(2,1)S(1)} collective-permute-done((f16[2,512,128]{2,1,0:T(8,128)(2,1)S(1)}, f16[2,512,128]{2,1,0:T(8,128)(2,1)S(1)}, u32[]{:S(2)}, u32[]{:S(2)}) %collective-permute-start.9) | collective-permute-done | bytes 262176 | tf_op jit(solution)/shard_map/ppermute | solution.py:284
  120.6 0.1 convert_add_fusion.2
  120.9 2.2 %collective-permute-done.8 = f16[2,512,128]{2,1,0:T(8,128)(2,1)S(1)} collective-permute-done((f16[2,512,128]{2,1,0:T(8,128)(2,1)S(1)}, f16[2,512,128]{2,1,0:T(8,128)(2,1)S(1)}, u32[]{:S(2)}, u32[]{:S(2)}) %collective-permute-start.8) | collective-permute-done | bytes 262176 | tf_op jit(solution)/shard_map/ppermute | solution.py:284
  123.3 0.8 collective-permute-start.13
  124.3 1.3 collective-permute-start.11
  125.6 2.2 %collective-permute-start.12 = (f16[2,512,128]{2,1,0:T(8,128)(2,1)S(1)}, f16[2,512,128]{2,1,0:T(8,128)(2,1)S(1)}, u32[]{:S(2)}, u32[]{:S(2)}) collective-permute-start(f16[2,512,128]{2,1,0:T(8,128)(2,1)S(1)} %pad_maximum_fusion.7), channel_id=1, source_target_pairs={{0,16},{2,18},{4,20},{6,22},{8,24},{10,26},{12,28},{14,30},{16,0},... | collective-permute-start | bytes 786440 | tf_op jit(solution)/shard_map/ppermute | solution.py:284
  127.8 5.3 %collective-permute-done.14 = f16[4,512,128]{2,1,0:T(8,128)(2,1)S(1)} collective-permute-done((f16[4,512,128]{2,1,0:T(8,128)(2,1)S(1)}, f16[4,512,128]{2,1,0:T(8,128)(2,1)S(1)}, u32[]{:S(2)}, u32[]{:S(2)}) %collective-permute-start.14) | collective-permute-done | bytes 524320 | tf_op jit(solution)/shard_map/ppermute | solution.py:284
  133.3 0.7 collective-permute-start.20
  134.0 4.2 %collective-permute-done.13 = bf16[2,512,128]{2,1,0:T(8,128)(2,1)S(1)} collective-permute-done((bf16[2,512,128]{2,1,0:T(8,128)(2,1)S(1)}, bf16[2,512,128]{2,1,0:T(8,128)(2,1)S(1)}, u32[]{:S(2)}, u32[]{:S(2)}) %collective-permute-start.13) | collective-permute-done | bytes 262176 | tf_op jit(solution)/shard_map/ppermute | solution.py:284
  138.3 1.1 collective-permute-start.28
  139.4 2.8 %collective-permute-done.12 = f16[2,512,128]{2,1,0:T(8,128)(2,1)S(1)} collective-permute-done((f16[2,512,128]{2,1,0:T(8,128)(2,1)S(1)}, f16[2,512,128]{2,1,0:T(8,128)(2,1)S(1)}, u32[]{:S(2)}, u32[]{:S(2)}) %collective-permute-start.12) | collective-permute-done | bytes 262176 | tf_op jit(solution)/shard_map/ppermute | solution.py:284
  142.3 3.9 %collective-permute-start.26 = (bf16[2,512,128]{2,1,0:T(8,128)(2,1)S(1)}, bf16[2,512,128]{2,1,0:T(8,128)(2,1)S(1)}, u32[]{:S(2)}, u32[]{:S(2)}) collective-permute-start(bf16[2,512,128]{2,1,0:T(8,128)(2,1)S(1)} %subtract_convert_fusion.2), channel_id=1, source_target_pairs={{0,8},{2,10},{4,12},{6,14},{8,0},{10,2},{12,4},{14,6},{16,24},{18,... | collective-permute-start | bytes 786440 | tf_op jit(solution)/shard_map/ppermute | solution.py:284
  146.5 2.1 %collective-permute-start.15 = (f16[2,512,128]{2,1,0:T(8,128)(2,1)S(1)}, f16[2,512,128]{2,1,0:T(8,128)(2,1)S(1)}, u32[]{:S(2)}, u32[]{:S(2)}) collective-permute-start(f16[2,512,128]{2,1,0:T(8,128)(2,1)S(1)} %pad_maximum_fusion.8), channel_id=1, source_target_pairs={{0,16},{2,18},{4,20},{6,22},{8,24},{10,26},{12,28},{14,30},{16,0},... | collective-permute-start | bytes 786440 | tf_op jit(solution)/shard_map/ppermute | solution.py:284
  148.6 6.5 %collective-permute-done.20 = f16[2,512,128]{2,1,0:T(8,128)(2,1)S(1)} collective-permute-done((f16[2,512,128]{2,1,0:T(8,128)(2,1)S(1)}, f16[2,512,128]{2,1,0:T(8,128)(2,1)S(1)}, u32[]{:S(2)}, u32[]{:S(2)}) %collective-permute-start.20) | collective-permute-done | bytes 262176 | tf_op jit(solution)/shard_map/ppermute | solution.py:284
  155.4 11.4 %collective-permute-done.15 = f16[2,512,128]{2,1,0:T(8,128)(2,1)S(1)} collective-permute-done((f16[2,512,128]{2,1,0:T(8,128)(2,1)S(1)}, f16[2,512,128]{2,1,0:T(8,128)(2,1)S(1)}, u32[]{:S(2)}, u32[]{:S(2)}) %collective-permute-start.15) | collective-permute-done | bytes 262176 | tf_op jit(solution)/shard_map/ppermute | solution.py:284
  166.8 0.1 subtract_convert_fusion.1
  167.0 1.4 collective-permute-start.16
  168.5 1.7 collective-permute-done.21
  170.3 0.5 collective-permute-start.22
  170.8 2.6 %collective-permute-done.16 = bf16[2,512,128]{2,1,0:T(8,128)(2,1)S(1)} collective-permute-done((bf16[2,512,128]{2,1,0:T(8,128)(2,1)S(1)}, bf16[2,512,128]{2,1,0:T(8,128)(2,1)S(1)}, u32[]{:S(2)}, u32[]{:S(2)}) %collective-permute-start.16) | collective-permute-done | bytes 262176 | tf_op jit(solution)/shard_map/ppermute | solution.py:284
  173.5 0.3 collective-permute-start.17
  173.8 12.3 %collective-permute-done.22 = bf16[2,512,128]{2,1,0:T(8,128)(2,1)S(1)} collective-permute-done((bf16[2,512,128]{2,1,0:T(8,128)(2,1)S(1)}, bf16[2,512,128]{2,1,0:T(8,128)(2,1)S(1)}, u32[]{:S(2)}, u32[]{:S(2)}) %collective-permute-start.22) | collective-permute-done | bytes 262176 | tf_op jit(solution)/shard_map/ppermute | solution.py:284
  186.1 1.9 collective-permute-start.23
  188.1 3.6 %collective-permute-done.17.refs_1_ = bf16[4,512,128]{2,1,0:T(8,128)(2,1)S(1)} collective-permute-done((bf16[4,512,128]{2,1,0:T(8,128)(2,1)S(1)}, bf16[4,512,128]{2,1,0:T(8,128)(2,1)S(1)}, u32[]{:S(2)}, u32[]{:S(2)}) %collective-permute-start.17) | collective-permute-done | bytes 524320 | tf_op jit(solution)/shard_map/ppermute | solution.py:284
  191.7 0.5 collective-permute-start.24
  192.3 1.4 assemble.3.refs_4_
  193.7 1.6 collective-permute-done.23.refs_5_
  195.4 0.5 collective-permute-start.25
  196.0 1.0 pad_maximum_fusion
  197.0 0.2 collective-permute-done.32.refs_3_
  197.3 1.4 assemble.4.refs_8_
  198.8 2.3 %assemble.5 = bf16[16,512,512]{2,1,0:T(8,128)(2,1)} custom-call(s32[1]{0:T(128)} %bitcast.mine_ref.place_ref, bf16[4,512,128]{2,1,0:T(8,128)(2,1)S(1)} %pad_maximum_fusion.2.refs_0_, bf16[4,512,128]{2,1,0:T(8,128)(2,1)S(1)} %collective-permute-done.17.refs_1_, ...), custom_call_target="tpu_custom_call", output_to_operand_aliasing={{}: (9, {})} | custom-call | bytes 8388608 | tf_op jit(solution)/shard_map/assemble/pallas_call | solution.py:248
  (83 shorter events, 2.8 us)
Async XLA Ops:
  0.6 49.0 %collective-permute-start = (bf16[128,8192]{1,0:T(8,128)(2,1)}, bf16[128,8192]{1,0:T(8,128)(2,1)}, u32[]{:S(2)}, u32[]{:S(2)}) collective-permute-start(bf16[128,8192]{1,0:T(8,128)(2,1)} %bitcast.84), channel_id=1, source_target_pairs={{0,1},{1,0},{2,3},{3,2},{4,5},{5,4},{6,7},{7,6},{8,9},{9,8},{10,11... | collective-permute-start | bytes 6291464 | tf_op jit(solution)/shard_map/ppermute | solution.py:299
  5.6 2.4 %copy-start.3 = (f32[512,512]{1,0:T(8,128)S(1)}, f32[512,512]{1,0:T(8,128)}, u32[]{:S(2)}) copy-start(f32[512,512]{1,0:T(8,128)} %param.8) | copy-start | bytes 3145732
  7.0 2.0 %copy-start.2 = (bf16[1,128,8192]{2,1,0:T(8,128)(2,1)S(1)}, bf16[1,128,8192]{2,1,0:T(8,128)(2,1)}, u32[]{:S(2)}) copy-start(bf16[1,128,8192]{2,1,0:T(8,128)(2,1)} %param.11) | copy-start | bytes 6291460
  9.0 3.4 %copy-start = (bf16[8192,512]{1,0:T(8,128)(2,1)S(1)}, bf16[8192,512]{1,0:T(8,128)(2,1)}, u32[]{:S(2)}) copy-start(bf16[8192,512]{1,0:T(8,128)(2,1)} %weights_ref.3) | copy-start | bytes 25165828
  12.4 1.3 copy-start.4
  12.4 1.4 copy-start.5
  12.4 37.2 %copy-start.1 = (bf16[8192,512]{1,0:T(8,128)(2,1)S(1)}, bf16[8192,512]{1,0:T(8,128)(2,1)}, u32[]{:S(2)}) copy-start(bf16[8192,512]{1,0:T(8,128)(2,1)} %weights_ref.3) | copy-start | bytes 25165828
  64.6 2.7 %collective-permute-start.1 = (f16[8,512,128]{2,1,0:T(8,128)(2,1)S(1)}, f16[8,512,128]{2,1,0:T(8,128)(2,1)S(1)}, u32[]{:S(2)}, u32[]{:S(2)}) collective-permute-start(f16[8,512,128]{2,1,0:T(8,128)(2,1)S(1)} %convert_element_type.204), channel_id=1, source_target_pairs={{0,2},{2,0},{4,6},{6,4},{8,10},{10,8},{12,14},{14,12},{16,18},{18,... | collective-permute-start | bytes 3145736 | tf_op jit(solution)/shard_map/ppermute | solution.py:284
  67.5 21.1 %collective-permute-start.2 = (f16[4,512,128]{2,1,0:T(8,128)(2,1)S(1)}, f16[4,512,128]{2,1,0:T(8,128)(2,1)S(1)}, u32[]{:S(2)}, u32[]{:S(2)}) collective-permute-start(f16[4,512,128]{2,1,0:T(8,128)(2,1)S(1)} %add_convert_fusion.3), channel_id=1, source_target_pairs={{0,4},{2,6},{4,0},{6,2},{8,12},{10,14},{12,8},{14,10},{16,20},{18,... | collective-permute-start | bytes 1572872 | tf_op jit(solution)/shard_map/ppermute | solution.py:284
  88.7 2.7 %collective-permute-start.4 = (f16[8,512,128]{2,1,0:T(8,128)(2,1)S(1)}, f16[8,512,128]{2,1,0:T(8,128)(2,1)S(1)}, u32[]{:S(2)}, u32[]{:S(2)}) collective-permute-start(f16[8,512,128]{2,1,0:T(8,128)(2,1)S(1)} %convert_element_type.207), channel_id=1, source_target_pairs={{0,2},{2,0},{4,6},{6,4},{8,10},{10,8},{12,14},{14,12},{16,18},{18,... | collective-permute-start | bytes 3145736 | tf_op jit(solution)/shard_map/ppermute | solution.py:284
  91.6 14.2 %collective-permute-start.6 = (f16[4,512,128]{2,1,0:T(8,128)(2,1)S(1)}, f16[4,512,128]{2,1,0:T(8,128)(2,1)S(1)}, u32[]{:S(2)}, u32[]{:S(2)}) collective-permute-start(f16[4,512,128]{2,1,0:T(8,128)(2,1)S(1)} %add_convert_fusion.2), channel_id=1, source_target_pairs={{0,4},{2,6},{4,0},{6,2},{8,12},{10,14},{12,8},{14,10},{16,20},{18,... | collective-permute-start | bytes 1572872 | tf_op jit(solution)/shard_map/ppermute | solution.py:284
  92.0 13.8 %collective-permute-start.5 = (f16[2,512,128]{2,1,0:T(8,128)(2,1)S(1)}, f16[2,512,128]{2,1,0:T(8,128)(2,1)S(1)}, u32[]{:S(2)}, u32[]{:S(2)}) collective-permute-start(f16[2,512,128]{2,1,0:T(8,128)(2,1)S(1)} %add_convert_fusion.7), channel_id=1, source_target_pairs={{0,8},{2,10},{4,12},{6,14},{8,0},{10,2},{12,4},{14,6},{16,24},{18,... | collective-permute-start | bytes 786440 | tf_op jit(solution)/shard_map/ppermute | solution.py:284
  93.8 12.4 %collective-permute-start.3 = (f16[8,512,128]{2,1,0:T(8,128)(2,1)S(1)}, f16[8,512,128]{2,1,0:T(8,128)(2,1)S(1)}, u32[]{:S(2)}, u32[]{:S(2)}) collective-permute-start(f16[8,512,128]{2,1,0:T(8,128)(2,1)S(1)} %convert_element_type.208), channel_id=1, source_target_pairs={{0,2},{2,0},{4,6},{6,4},{8,10},{10,8},{12,14},{14,12},{16,18},{18,... | collective-permute-start | bytes 3145736 | tf_op jit(solution)/shard_map/ppermute | solution.py:284
  106.4 5.1 %collective-permute-start.10 = (f16[8,512,128]{2,1,0:T(8,128)(2,1)S(1)}, f16[8,512,128]{2,1,0:T(8,128)(2,1)S(1)}, u32[]{:S(2)}, u32[]{:S(2)}) collective-permute-start(f16[8,512,128]{2,1,0:T(8,128)(2,1)S(1)} %convert_element_type.227), channel_id=1, source_target_pairs={{0,2},{2,0},{4,6},{6,4},{8,10},{10,8},{12,14},{14,12},{16,18},{18,... | collective-permute-start | bytes 3145736 | tf_op jit(solution)/shard_map/ppermute | solution.py:284
  106.9 13.7 %collective-permute-start.9 = (f16[2,512,128]{2,1,0:T(8,128)(2,1)S(1)}, f16[2,512,128]{2,1,0:T(8,128)(2,1)S(1)}, u32[]{:S(2)}, u32[]{:S(2)}) collective-permute-start(f16[2,512,128]{2,1,0:T(8,128)(2,1)S(1)} %add_convert_fusion.6), channel_id=1, source_target_pairs={{0,8},{2,10},{4,12},{6,14},{8,0},{10,2},{12,4},{14,6},{16,24},{18,... | collective-permute-start | bytes 786440 | tf_op jit(solution)/shard_map/ppermute | solution.py:284
  107.9 16.2 %collective-permute-start.7 = (f16[4,512,128]{2,1,0:T(8,128)(2,1)S(1)}, f16[4,512,128]{2,1,0:T(8,128)(2,1)S(1)}, u32[]{:S(2)}, u32[]{:S(2)}) collective-permute-start(f16[4,512,128]{2,1,0:T(8,128)(2,1)S(1)} %add_convert_fusion.1), channel_id=1, source_target_pairs={{0,4},{2,6},{4,0},{6,2},{8,12},{10,14},{12,8},{14,10},{16,20},{18,... | collective-permute-start | bytes 1572872 | tf_op jit(solution)/shard_map/ppermute | solution.py:284
  108.9 14.3 %collective-permute-start.8 = (f16[2,512,128]{2,1,0:T(8,128)(2,1)S(1)}, f16[2,512,128]{2,1,0:T(8,128)(2,1)S(1)}, u32[]{:S(2)}, u32[]{:S(2)}) collective-permute-start(f16[2,512,128]{2,1,0:T(8,128)(2,1)S(1)} %pad_maximum_fusion.6), channel_id=1, source_target_pairs={{0,16},{2,18},{4,20},{6,22},{8,24},{10,26},{12,28},{14,30},{16,0},... | collective-permute-start | bytes 786440 | tf_op jit(solution)/shard_map/ppermute | solution.py:284
  111.6 11.5 %copy-start.9 = (bf16[2,512,128]{2,1,0:T(8,128)(2,1)S(1)}, bf16[2,512,128]{2,1,0:T(8,128)(2,1)}, u32[]{:S(2)}) copy-start(bf16[2,512,128]{2,1,0:T(8,128)(2,1)} %get-tuple-element.85) | copy-start | bytes 786436
  111.6 21.5 %collective-permute-start.14 = (f16[4,512,128]{2,1,0:T(8,128)(2,1)S(1)}, f16[4,512,128]{2,1,0:T(8,128)(2,1)S(1)}, u32[]{:S(2)}, u32[]{:S(2)}) collective-permute-start(f16[4,512,128]{2,1,0:T(8,128)(2,1)S(1)} %add_convert_fusion), channel_id=1, source_target_pairs={{0,4},{2,6},{4,0},{6,2},{8,12},{10,14},{12,8},{14,10},{16,20},{18,... | collective-permute-start | bytes 1572872 | tf_op jit(solution)/shard_map/ppermute | solution.py:284
  123.3 18.9 %copy-start.8 = (bf16[2,512,128]{2,1,0:T(8,128)(2,1)S(1)}, bf16[2,512,128]{2,1,0:T(8,128)(2,1)}, u32[]{:S(2)}) copy-start(bf16[2,512,128]{2,1,0:T(8,128)(2,1)} %get-tuple-element.94) | copy-start | bytes 786436
  123.3 14.9 %collective-permute-start.13 = (bf16[2,512,128]{2,1,0:T(8,128)(2,1)S(1)}, bf16[2,512,128]{2,1,0:T(8,128)(2,1)S(1)}, u32[]{:S(2)}, u32[]{:S(2)}) collective-permute-start(bf16[2,512,128]{2,1,0:T(8,128)(2,1)S(1)} %subtract_convert_fusion.3), channel_id=1, source_target_pairs={{0,8},{2,10},{4,12},{6,14},{8,0},{10,2},{12,4},{14,6},{16,24},{18,... | collective-permute-start | bytes 786440 | tf_op jit(solution)/shard_map/ppermute | solution.py:284
  124.3 21.9 %collective-permute-start.11 = (f16[2,512,128]{2,1,0:T(8,128)(2,1)S(1)}, f16[2,512,128]{2,1,0:T(8,128)(2,1)S(1)}, u32[]{:S(2)}, u32[]{:S(2)}) collective-permute-start(f16[2,512,128]{2,1,0:T(8,128)(2,1)S(1)} %add_convert_fusion.5), channel_id=1, source_target_pairs={{0,8},{2,10},{4,12},{6,14},{8,0},{10,2},{12,4},{14,6},{16,24},{18,... | collective-permute-start | bytes 786440 | tf_op jit(solution)/shard_map/ppermute | solution.py:284
  125.6 16.6 %collective-permute-start.12 = (f16[2,512,128]{2,1,0:T(8,128)(2,1)S(1)}, f16[2,512,128]{2,1,0:T(8,128)(2,1)S(1)}, u32[]{:S(2)}, u32[]{:S(2)}) collective-permute-start(f16[2,512,128]{2,1,0:T(8,128)(2,1)S(1)} %pad_maximum_fusion.7), channel_id=1, source_target_pairs={{0,16},{2,18},{4,20},{6,22},{8,24},{10,26},{12,28},{14,30},{16,0},... | collective-permute-start | bytes 786440 | tf_op jit(solution)/shard_map/ppermute | solution.py:284
  133.3 21.8 %collective-permute-start.20 = (f16[2,512,128]{2,1,0:T(8,128)(2,1)S(1)}, f16[2,512,128]{2,1,0:T(8,128)(2,1)S(1)}, u32[]{:S(2)}, u32[]{:S(2)}) collective-permute-start(f16[2,512,128]{2,1,0:T(8,128)(2,1)S(1)} %add_convert_fusion.4), channel_id=1, source_target_pairs={{0,8},{2,10},{4,12},{6,14},{8,0},{10,2},{12,4},{14,6},{16,24},{18,... | collective-permute-start | bytes 786440 | tf_op jit(solution)/shard_map/ppermute | solution.py:284
  138.3 35.5 %collective-permute-start.28 = (bf16[4,512,128]{2,1,0:T(8,128)(2,1)S(1)}, bf16[4,512,128]{2,1,0:T(8,128)(2,1)S(1)}, u32[]{:S(2)}, u32[]{:S(2)}) collective-permute-start(bf16[4,512,128]{2,1,0:T(8,128)(2,1)S(1)} %pad_maximum_fusion.1.refs_0_), channel_id=1, source_target_pairs={{0,4},{2,6},{4,0},{6,2},{8,12},{10,14},{12,8},{14,10},{16,20},{18,... | collective-permute-start | bytes 1572872 | tf_op jit(solution)/shard_map/ppermute | solution.py:284
  142.3 26.1 %collective-permute-start.26 = (bf16[2,512,128]{2,1,0:T(8,128)(2,1)S(1)}, bf16[2,512,128]{2,1,0:T(8,128)(2,1)S(1)}, u32[]{:S(2)}, u32[]{:S(2)}) collective-permute-start(bf16[2,512,128]{2,1,0:T(8,128)(2,1)S(1)} %subtract_convert_fusion.2), channel_id=1, source_target_pairs={{0,8},{2,10},{4,12},{6,14},{8,0},{10,2},{12,4},{14,6},{16,24},{18,... | collective-permute-start | bytes 786440 | tf_op jit(solution)/shard_map/ppermute | solution.py:284
  146.4 20.5 %copy-start.7 = (bf16[2,512,128]{2,1,0:T(8,128)(2,1)S(1)}, bf16[2,512,128]{2,1,0:T(8,128)(2,1)}, u32[]{:S(2)}) copy-start(bf16[2,512,128]{2,1,0:T(8,128)(2,1)} %get-tuple-element.63) | copy-start | bytes 786436
  146.5 20.4 %collective-permute-start.15 = (f16[2,512,128]{2,1,0:T(8,128)(2,1)S(1)}, f16[2,512,128]{2,1,0:T(8,128)(2,1)S(1)}, u32[]{:S(2)}, u32[]{:S(2)}) collective-permute-start(f16[2,512,128]{2,1,0:T(8,128)(2,1)S(1)} %pad_maximum_fusion.8), channel_id=1, source_target_pairs={{0,16},{2,18},{4,20},{6,22},{8,24},{10,26},{12,28},{14,30},{16,0},... | collective-permute-start | bytes 786440 | tf_op jit(solution)/shard_map/ppermute | solution.py:284
  155.2 15.0 %copy-start.6 = (bf16[2,512,128]{2,1,0:T(8,128)(2,1)S(1)}, bf16[2,512,128]{2,1,0:T(8,128)(2,1)}, u32[]{:S(2)}) copy-start(bf16[2,512,128]{2,1,0:T(8,128)(2,1)} %get-tuple-element.100) | copy-start | bytes 786436
  155.4 14.8 %collective-permute-start.21 = (f16[2,512,128]{2,1,0:T(8,128)(2,1)S(1)}, f16[2,512,128]{2,1,0:T(8,128)(2,1)S(1)}, u32[]{:S(2)}, u32[]{:S(2)}) collective-permute-start(f16[2,512,128]{2,1,0:T(8,128)(2,1)S(1)} %pad_maximum_fusion.9), channel_id=1, source_target_pairs={{0,16},{2,18},{4,20},{6,22},{8,24},{10,26},{12,28},{14,30},{16,0},... | collective-permute-start | bytes 786440 | tf_op jit(solution)/shard_map/ppermute | solution.py:284
  167.0 6.4 %collective-permute-start.16 = (bf16[2,512,128]{2,1,0:T(8,128)(2,1)S(1)}, bf16[2,512,128]{2,1,0:T(8,128)(2,1)S(1)}, u32[]{:S(2)}, u32[]{:S(2)}) collective-permute-start(bf16[2,512,128]{2,1,0:T(8,128)(2,1)S(1)} %subtract_convert_fusion.1), channel_id=1, source_target_pairs={{0,8},{2,10},{4,12},{6,14},{8,0},{10,2},{12,4},{14,6},{16,24},{18,... | collective-permute-start | bytes 786440 | tf_op jit(solution)/shard_map/ppermute | solution.py:284
  168.4 19.6 %collective-permute-start.27 = (bf16[4,512,128]{2,1,0:T(8,128)(2,1)S(1)}, bf16[4,512,128]{2,1,0:T(8,128)(2,1)S(1)}, u32[]{:S(2)}, u32[]{:S(2)}) collective-permute-start(bf16[4,512,128]{2,1,0:T(8,128)(2,1)S(1)} %pad_maximum_fusion.4.refs_0_), channel_id=1, source_target_pairs={{0,4},{2,6},{4,0},{6,2},{8,12},{10,14},{12,8},{14,10},{16,20},{18,... | collective-permute-start | bytes 1572872 | tf_op jit(solution)/shard_map/ppermute | solution.py:284
  170.3 15.7 %collective-permute-start.22 = (bf16[2,512,128]{2,1,0:T(8,128)(2,1)S(1)}, bf16[2,512,128]{2,1,0:T(8,128)(2,1)S(1)}, u32[]{:S(2)}, u32[]{:S(2)}) collective-permute-start(bf16[2,512,128]{2,1,0:T(8,128)(2,1)S(1)} %subtract_convert_fusion), channel_id=1, source_target_pairs={{0,4},{2,6},{4,0},{6,2},{8,12},{10,14},{12,8},{14,10},{16,20},{18,... | collective-permute-start | bytes 786440 | tf_op jit(solution)/shard_map/ppermute | solution.py:284
  170.8 20.9 %collective-permute-start.29 = (bf16[4,512,128]{2,1,0:T(8,128)(2,1)S(1)}, bf16[4,512,128]{2,1,0:T(8,128)(2,1)S(1)}, u32[]{:S(2)}, u32[]{:S(2)}) collective-permute-start(bf16[4,512,128]{2,1,0:T(8,128)(2,1)S(1)} %pad_maximum_fusion.1.refs_0_), channel_id=1, source_target_pairs={{0,2},{2,0},{4,6},{6,4},{8,10},{10,8},{12,14},{14,12},{16,18},{18,... | collective-permute-start | bytes 1572872 | tf_op jit(solution)/shard_map/ppermute | solution.py:284
  173.5 18.2 %collective-permute-start.17 = (bf16[4,512,128]{2,1,0:T(8,128)(2,1)S(1)}, bf16[4,512,128]{2,1,0:T(8,128)(2,1)S(1)}, u32[]{:S(2)}, u32[]{:S(2)}) collective-permute-start(bf16[4,512,128]{2,1,0:T(8,128)(2,1)S(1)} %pad_maximum_fusion.2.refs_0_), channel_id=1, source_target_pairs={{0,4},{2,6},{4,0},{6,2},{8,12},{10,14},{12,8},{14,10},{16,20},{18,... | collective-permute-start | bytes 1572872 | tf_op jit(solution)/shard_map/ppermute | solution.py:284
  173.8 18.4 %collective-permute-start.30 = (bf16[4,512,128]{2,1,0:T(8,128)(2,1)S(1)}, bf16[4,512,128]{2,1,0:T(8,128)(2,1)S(1)}, u32[]{:S(2)}, u32[]{:S(2)}) collective-permute-start(bf16[4,512,128]{2,1,0:T(8,128)(2,1)S(1)} %collective-permute-done.28.refs_1_), channel_id=1, source_target_pairs={{0,2},{2,0},{4,6},{6,4},{8,10},{10,8},{12,14},{14,12},{16,18},{18,... | collective-permute-start | bytes 1572872 | tf_op jit(solution)/shard_map/ppermute | solution.py:284
  186.1 9.2 %collective-permute-start.23 = (bf16[4,512,128]{2,1,0:T(8,128)(2,1)S(1)}, bf16[4,512,128]{2,1,0:T(8,128)(2,1)S(1)}, u32[]{:S(2)}, u32[]{:S(2)}) collective-permute-start(bf16[4,512,128]{2,1,0:T(8,128)(2,1)S(1)} %pad_maximum_fusion.3.refs_4_), channel_id=1, source_target_pairs={{0,8},{2,10},{4,12},{6,14},{8,0},{10,2},{12,4},{14,6},{16,24},{18,... | collective-permute-start | bytes 1572872 | tf_op jit(solution)/shard_map/ppermute | solution.py:284
  188.0 7.4 %collective-permute-start.31 = (bf16[4,512,128]{2,1,0:T(8,128)(2,1)S(1)}, bf16[4,512,128]{2,1,0:T(8,128)(2,1)S(1)}, u32[]{:S(2)}, u32[]{:S(2)}) collective-permute-start(bf16[4,512,128]{2,1,0:T(8,128)(2,1)S(1)} %pad_maximum_fusion.4.refs_0_), channel_id=1, source_target_pairs={{0,2},{2,0},{4,6},{6,4},{8,10},{10,8},{12,14},{14,12},{16,18},{18,... | collective-permute-start | bytes 1572872 | tf_op jit(solution)/shard_map/ppermute | solution.py:284
  191.7 7.0 %collective-permute-start.18 = (bf16[4,512,128]{2,1,0:T(8,128)(2,1)S(1)}, bf16[4,512,128]{2,1,0:T(8,128)(2,1)S(1)}, u32[]{:S(2)}, u32[]{:S(2)}) collective-permute-start(bf16[4,512,128]{2,1,0:T(8,128)(2,1)S(1)} %pad_maximum_fusion.2.refs_0_), channel_id=1, source_target_pairs={{0,2},{2,0},{4,6},{6,4},{8,10},{10,8},{12,14},{14,12},{16,18},{18,... | collective-permute-start | bytes 1572872 | tf_op jit(solution)/shard_map/ppermute | solution.py:284
  191.7 7.0 %collective-permute-start.24 = (bf16[4,512,128]{2,1,0:T(8,128)(2,1)S(1)}, bf16[4,512,128]{2,1,0:T(8,128)(2,1)S(1)}, u32[]{:S(2)}, u32[]{:S(2)}) collective-permute-start(bf16[4,512,128]{2,1,0:T(8,128)(2,1)S(1)} %pad_maximum_fusion.3.refs_4_), channel_id=1, source_target_pairs={{0,2},{2,0},{4,6},{6,4},{8,10},{10,8},{12,14},{14,12},{16,18},{18,... | collective-permute-start | bytes 1572872 | tf_op jit(solution)/shard_map/ppermute | solution.py:284
  192.2 6.5 %collective-permute-start.19 = (bf16[4,512,128]{2,1,0:T(8,128)(2,1)S(1)}, bf16[4,512,128]{2,1,0:T(8,128)(2,1)S(1)}, u32[]{:S(2)}, u32[]{:S(2)}) collective-permute-start(bf16[4,512,128]{2,1,0:T(8,128)(2,1)S(1)} %collective-permute-done.17.refs_1_), channel_id=1, source_target_pairs={{0,2},{2,0},{4,6},{6,4},{8,10},{10,8},{12,14},{14,12},{16,18},{18,... | collective-permute-start | bytes 1572872 | tf_op jit(solution)/shard_map/ppermute | solution.py:284
  195.4 1.9 collective-permute-start.32
  195.4 3.4 %collective-permute-start.25 = (bf16[4,512,128]{2,1,0:T(8,128)(2,1)S(1)}, bf16[4,512,128]{2,1,0:T(8,128)(2,1)S(1)}, u32[]{:S(2)}, u32[]{:S(2)}) collective-permute-start(bf16[4,512,128]{2,1,0:T(8,128)(2,1)S(1)} %collective-permute-done.23.refs_5_), channel_id=1, source_target_pairs={{0,2},{2,0},{4,6},{6,4},{8,10},{10,8},{12,14},{14,12},{16,18},{18,... | collective-permute-start | bytes 1572872 | tf_op jit(solution)/shard_map/ppermute | solution.py:284

commit v15 on v14

--- a/solution.py
+++ b/solution.py
@@ -357,7 +357,7 @@
         stack = (starts.astype(F32) - (1.33 / scale) * both).astype(BF16)
         offsets = list(spans[-1])
         stack = yield stack
-        back = spans[-2::-1] if chunk + 1 < chunks or chunks == 1 else spans[:-1]
+        back = spans[:-1] if chunk % 2 else spans[-2::-1]
         for span in back[:-1]:
             arrived = yield sent([stack], span)
             offsets = [offset ^ far for far in span for offset in offsets]

time: 202 us -> 196 us (0.970)
  waiting for transfers between devices: 104 us -> 97.2 us
    ppermute x32, waiting for transfers between devices: 67.8 us -> 61.4 us  [swapped(): return lax.ppermute(array, 'rep', pairs)]
  transfers between devices with their start and end apart: 33 -> 33, of which waited for: 16 -> 17; matrix products, arithmetic and copies ran while one was open for 4% -> 4% of each run, Pallas kernels for 17% -> 18%
where the time goes in v15:
time: 196 us; the launch traced here: 195 us
  waiting for transfers between devices  97.2 us (50%)
  Pallas kernels  52.1 us (27%)
  starting transfers between devices  31.1 us (16%)
  local copies, waits for them, and re-layouts  6.74 us (3%)
  other arithmetic  6.68 us (3%)
    ppermute x32, waiting for transfers between devices, swapped(): return lax.ppermute(array, 'rep', pairs)  61.4 us
    pallas_call x3, Pallas kernels, inner(): pl.pallas_call(functools.partial(inner_kernel, float(tokens), kept), grid...  42.7 us
    ppermute x1, waiting for transfers between devices, per_device(): banks = (own_bank, lax.ppermute(own_bank, 'fsdp', [(0, 1), (1, 0)]))  35.8 us
    ppermute x32, starting transfers between devices, swapped(): return lax.ppermute(array, 'rep', pairs)  28.1 us
    pallas_call x3, Pallas kernels, assemble(): pl.pallas_call(functools.partial(assemble_kernel, begins, offsets), in_sp...  5.14 us
    unnamed x20, local copies, waits for them, and re-layouts  4.29 us
    pallas_call x2, Pallas kernels, forward(): pl.pallas_call(forward_kernel, in_specs=[vmem, vmem], out_specs=[vmem, vm...  4.23 us
  transfers between devices with their start and end apart: 33, of which 17 were waited for; matrix products, arithmetic and copies ran while one was open for 4% of the time, Pallas kernels for 18%

profile of v15, /device:TPU:0, one launch (start us, length us, event | category | flops | bytes accessed | tf_op | source)
XLA Modules:
  0.0 195.2 jit_solution(1025290747588891448)
XLA Ops:
  0.6 3.0 %collective-permute-start = (bf16[128,8192]{1,0:T(8,128)(2,1)}, bf16[128,8192]{1,0:T(8,128)(2,1)}, u32[]{:S(2)}, u32[]{:S(2)}) collective-permute-start(bf16[128,8192]{1,0:T(8,128)(2,1)} %bitcast.84), channel_id=1, source_target_pairs={{0,1},{1,0},{2,3},{3,2},{4,5},{5,4},{6,7},{7,6},{8,9},{9,8},{10,11... | collective-permute-start | bytes 6291464 | tf_op jit(solution)/shard_map/ppermute | solution.py:299
  3.7 0.9 convert_reduce_fusion
  4.6 0.1 copy.21
  4.8 0.9 copy.22
  5.6 1.4 dynamic-slice_bitcast_fusion
  7.0 1.1 pad_maximum_fusion.5
  8.1 0.9 copy-done.2
  9.0 3.4 %copy-done = bf16[8192,512]{1,0:T(8,128)(2,1)S(1)} copy-done((bf16[8192,512]{1,0:T(8,128)(2,1)S(1)}, bf16[8192,512]{1,0:T(8,128)(2,1)}, u32[]{:S(2)}) %copy-start) | copy-done | bytes 8388632
  12.4 1.3 forward.2
  13.8 35.8 %collective-permute-done.part_ref.high_ref = bf16[128,8192]{1,0:T(8,128)(2,1)} collective-permute-done((bf16[128,8192]{1,0:T(8,128)(2,1)}, bf16[128,8192]{1,0:T(8,128)(2,1)}, u32[]{:S(2)}, u32[]{:S(2)}) %collective-permute-start) | collective-permute-done | bytes 2097184 | tf_op jit(solution)/shard_map/ppermute | solution.py:299
  49.6 3.0 %forward.3 = (bf16[8192,128]{1,0:T(8,128)(2,1)S(1)}, f32[128,512]{1,0:T(8,128)S(1)}) custom-call(bf16[128,8192]{1,0:T(8,128)(2,1)} %collective-permute-done.part_ref.high_ref, bf16[8192,512]{1,0:T(8,128)(2,1)S(1)} %copy-done.1), custom_call_target="tpu_custom_call" | custom-call | flops 1073741824 | bytes 12582912 | tf_op jit(solution)/shard_map/forward/pallas_call | solution.py:36
  52.6 11.8 %inner.3 = (f32[8,512,128]{2,1,0:T(8,128)S(1)}, f32[8,512,128]{2,1,0:T(8,128)S(1)}) custom-call(s32[1]{0:T(128)} %bitcast.mine_ref.place_ref, bf16[128,8192]{1,0:T(8,128)(2,1)S(1)} %bitcast.86, bf16[128,8192]{1,0:T(8,128)(2,1)} %collective-permute-done.part_ref.high_ref, bf16[4,2,2,512,128]{4,3,2,1,0:T(8,128)(2,1)S(1)} %bitcast.89, ...), custom_call_target="tpu_custom_call" | custom-call | flops 1610612736 | bytes 20971520 | tf_op jit(solution)/shard_map/inner/pallas_call | solution.py:190
  64.4 0.1 convert_element_type.204
  64.7 2.6 %collective-permute-done.1 = f16[8,512,128]{2,1,0:T(8,128)(2,1)S(1)} collective-permute-done((f16[8,512,128]{2,1,0:T(8,128)(2,1)S(1)}, f16[8,512,128]{2,1,0:T(8,128)(2,1)S(1)}, u32[]{:S(2)}, u32[]{:S(2)}) %collective-permute-start.1) | collective-permute-done | bytes 1048608 | tf_op jit(solution)/shard_map/ppermute | solution.py:284
  67.3 0.1 add_convert_fusion.3
  67.5 1.8 collective-permute-start.2
  69.2 19.1 %inner.4 = (f32[8,512,128]{2,1,0:T(8,128)S(1)}, f32[8,512,128]{2,1,0:T(8,128)S(1)}, f32[8,512,128]{2,1,0:T(8,128)S(1)}, f32[8,512,128]{2,1,0:T(8,128)S(1)}) custom-call(s32[1]{0:T(128)} %bitcast.mine_ref.place_ref, bf16[128,8192]{1,0:T(8,128)(2,1)S(1)} %bitcast.87, bf16[128,8192]{1,0:T(8,128)(2,1)} %collective-permute-done.part_ref.high_ref, ...), custom_call_target="tpu_custom_call" | custom-call | flops 3221225472 | bytes 41943040 | tf_op jit(solution)/shard_map/inner/pallas_call | solution.py:190
  88.3 0.1 convert_element_type.207
  88.5 0.1 convert_element_type.208
  88.8 2.6 %collective-permute-done.4 = f16[8,512,128]{2,1,0:T(8,128)(2,1)S(1)} collective-permute-done((f16[8,512,128]{2,1,0:T(8,128)(2,1)S(1)}, f16[8,512,128]{2,1,0:T(8,128)(2,1)S(1)}, u32[]{:S(2)}, u32[]{:S(2)}) %collective-permute-start.4) | collective-permute-done | bytes 1048608 | tf_op jit(solution)/shard_map/ppermute | solution.py:284
  91.5 0.1 add_convert_fusion.2
  91.6 0.4 collective-permute-start.6
  92.0 1.8 collective-permute-start.5
  93.8 11.8 %inner.5 = (f32[8,512,128]{2,1,0:T(8,128)S(1)}, f32[8,512,128]{2,1,0:T(8,128)S(1)}) custom-call(s32[1]{0:T(128)} %bitcast.mine_ref.place_ref, bf16[128,8192]{1,0:T(8,128)(2,1)S(1)} %bitcast.88, bf16[128,8192]{1,0:T(8,128)(2,1)} %collective-permute-done.part_ref.high_ref, bf16[4,2,2,512,128]{4,3,2,1,0:T(8,128)(2,1)S(1)} %bitcast.91, ...), custom_call_target="tpu_custom_call" | custom-call | flops 1610612736 | bytes 20971520 | tf_op jit(solution)/shard_map/inner/pallas_call | solution.py:190
  105.6 0.1 convert_element_type.227
  106.2 0.1 add_convert_fusion.1
  106.4 0.6 collective-permute-start.10
  106.9 1.0 collective-permute-start.9
  107.9 1.0 collective-permute-start.7
  108.9 2.6 %collective-permute-start.8 = (f16[2,512,128]{2,1,0:T(8,128)(2,1)S(1)}, f16[2,512,128]{2,1,0:T(8,128)(2,1)S(1)}, u32[]{:S(2)}, u32[]{:S(2)}) collective-permute-start(f16[2,512,128]{2,1,0:T(8,128)(2,1)S(1)} %pad_maximum_fusion.6), channel_id=1, source_target_pairs={{0,16},{2,18},{4,20},{6,22},{8,24},{10,26},{12,28},{14,30},{16,0},... | collective-permute-start | bytes 786440 | tf_op jit(solution)/shard_map/ppermute | solution.py:284
  111.5 0.2 add_convert_fusion
  111.6 1.1 collective-permute-start.14
  112.8 7.9 %collective-permute-done.9 = f16[2,512,128]{2,1,0:T(8,128)(2,1)S(1)} collective-permute-done((f16[2,512,128]{2,1,0:T(8,128)(2,1)S(1)}, f16[2,512,128]{2,1,0:T(8,128)(2,1)S(1)}, u32[]{:S(2)}, u32[]{:S(2)}) %collective-permute-start.9) | collective-permute-done | bytes 262176 | tf_op jit(solution)/shard_map/ppermute | solution.py:284
  120.9 2.2 %collective-permute-done.8 = f16[2,512,128]{2,1,0:T(8,128)(2,1)S(1)} collective-permute-done((f16[2,512,128]{2,1,0:T(8,128)(2,1)S(1)}, f16[2,512,128]{2,1,0:T(8,128)(2,1)S(1)}, u32[]{:S(2)}, u32[]{:S(2)}) %collective-permute-start.8) | collective-permute-done | bytes 262176 | tf_op jit(solution)/shard_map/ppermute | solution.py:284
  123.3 0.8 collective-permute-start.13
  124.3 1.3 collective-permute-start.11
  125.6 2.2 %collective-permute-start.12 = (f16[2,512,128]{2,1,0:T(8,128)(2,1)S(1)}, f16[2,512,128]{2,1,0:T(8,128)(2,1)S(1)}, u32[]{:S(2)}, u32[]{:S(2)}) collective-permute-start(f16[2,512,128]{2,1,0:T(8,128)(2,1)S(1)} %pad_maximum_fusion.7), channel_id=1, source_target_pairs={{0,16},{2,18},{4,20},{6,22},{8,24},{10,26},{12,28},{14,30},{16,0},... | collective-permute-start | bytes 786440 | tf_op jit(solution)/shard_map/ppermute | solution.py:284
  127.8 5.3 %collective-permute-done.14 = f16[4,512,128]{2,1,0:T(8,128)(2,1)S(1)} collective-permute-done((f16[4,512,128]{2,1,0:T(8,128)(2,1)S(1)}, f16[4,512,128]{2,1,0:T(8,128)(2,1)S(1)}, u32[]{:S(2)}, u32[]{:S(2)}) %collective-permute-start.14) | collective-permute-done | bytes 524320 | tf_op jit(solution)/shard_map/ppermute | solution.py:284
  133.3 0.7 collective-permute-start.20
  134.0 4.2 %collective-permute-done.13 = bf16[2,512,128]{2,1,0:T(8,128)(2,1)S(1)} collective-permute-done((bf16[2,512,128]{2,1,0:T(8,128)(2,1)S(1)}, bf16[2,512,128]{2,1,0:T(8,128)(2,1)S(1)}, u32[]{:S(2)}, u32[]{:S(2)}) %collective-permute-start.13) | collective-permute-done | bytes 262176 | tf_op jit(solution)/shard_map/ppermute | solution.py:284
  138.3 1.1 collective-permute-start.28
  139.4 2.8 %collective-permute-done.12 = f16[2,512,128]{2,1,0:T(8,128)(2,1)S(1)} collective-permute-done((f16[2,512,128]{2,1,0:T(8,128)(2,1)S(1)}, f16[2,512,128]{2,1,0:T(8,128)(2,1)S(1)}, u32[]{:S(2)}, u32[]{:S(2)}) %collective-permute-start.12) | collective-permute-done | bytes 262176 | tf_op jit(solution)/shard_map/ppermute | solution.py:284
  142.3 1.1 collective-permute-start.26
  143.7 3.5 %collective-permute-start.15 = (f16[2,512,128]{2,1,0:T(8,128)(2,1)S(1)}, f16[2,512,128]{2,1,0:T(8,128)(2,1)S(1)}, u32[]{:S(2)}, u32[]{:S(2)}) collective-permute-start(f16[2,512,128]{2,1,0:T(8,128)(2,1)S(1)} %pad_maximum_fusion.8), channel_id=1, source_target_pairs={{0,16},{2,18},{4,20},{6,22},{8,24},{10,26},{12,28},{14,30},{16,0},... | collective-permute-start | bytes 786440 | tf_op jit(solution)/shard_map/ppermute | solution.py:284
  147.2 2.1 %collective-permute-done.20 = f16[2,512,128]{2,1,0:T(8,128)(2,1)S(1)} collective-permute-done((f16[2,512,128]{2,1,0:T(8,128)(2,1)S(1)}, f16[2,512,128]{2,1,0:T(8,128)(2,1)S(1)}, u32[]{:S(2)}, u32[]{:S(2)}) %collective-permute-start.20) | collective-permute-done | bytes 262176 | tf_op jit(solution)/shard_map/ppermute | solution.py:284
  149.6 2.4 %collective-permute-start.21 = (f16[2,512,128]{2,1,0:T(8,128)(2,1)S(1)}, f16[2,512,128]{2,1,0:T(8,128)(2,1)S(1)}, u32[]{:S(2)}, u32[]{:S(2)}) collective-permute-start(f16[2,512,128]{2,1,0:T(8,128)(2,1)S(1)} %pad_maximum_fusion.9), channel_id=1, source_target_pairs={{0,16},{2,18},{4,20},{6,22},{8,24},{10,26},{12,28},{14,30},{16,0},... | collective-permute-start | bytes 786440 | tf_op jit(solution)/shard_map/ppermute | solution.py:284
  152.0 12.2 %collective-permute-done.15 = f16[2,512,128]{2,1,0:T(8,128)(2,1)S(1)} collective-permute-done((f16[2,512,128]{2,1,0:T(8,128)(2,1)S(1)}, f16[2,512,128]{2,1,0:T(8,128)(2,1)S(1)}, u32[]{:S(2)}, u32[]{:S(2)}) %collective-permute-start.15) | collective-permute-done | bytes 262176 | tf_op jit(solution)/shard_map/ppermute | solution.py:284
  164.2 0.1 subtract_convert_fusion.1
  164.5 2.1 %collective-permute-start.27 = (bf16[4,512,128]{2,1,0:T(8,128)(2,1)S(1)}, bf16[4,512,128]{2,1,0:T(8,128)(2,1)S(1)}, u32[]{:S(2)}, u32[]{:S(2)}) collective-permute-start(bf16[4,512,128]{2,1,0:T(8,128)(2,1)S(1)} %pad_maximum_fusion.4.refs_0_), channel_id=1, source_target_pairs={{0,8},{2,10},{4,12},{6,14},{8,0},{10,2},{12,4},{14,6},{16,24},{18,... | collective-permute-start | bytes 1572872 | tf_op jit(solution)/shard_map/ppermute | solution.py:284
  166.5 1.0 collective-permute-done.21
  167.7 1.0 collective-permute-start.22
  168.7 3.7 %collective-permute-done.16 = bf16[2,512,128]{2,1,0:T(8,128)(2,1)S(1)} collective-permute-done((bf16[2,512,128]{2,1,0:T(8,128)(2,1)S(1)}, bf16[2,512,128]{2,1,0:T(8,128)(2,1)S(1)}, u32[]{:S(2)}, u32[]{:S(2)}) %collective-permute-start.16) | collective-permute-done | bytes 262176 | tf_op jit(solution)/shard_map/ppermute | solution.py:284
  172.5 0.2 collective-permute-start.17
  172.7 3.6 %collective-permute-done.22 = bf16[2,512,128]{2,1,0:T(8,128)(2,1)S(1)} collective-permute-done((bf16[2,512,128]{2,1,0:T(8,128)(2,1)S(1)}, bf16[2,512,128]{2,1,0:T(8,128)(2,1)S(1)}, u32[]{:S(2)}, u32[]{:S(2)}) %collective-permute-start.22) | collective-permute-done | bytes 262176 | tf_op jit(solution)/shard_map/ppermute | solution.py:284
  176.5 3.6 %collective-permute-done.27.refs_1_ = bf16[4,512,128]{2,1,0:T(8,128)(2,1)S(1)} collective-permute-done((bf16[4,512,128]{2,1,0:T(8,128)(2,1)S(1)}, bf16[4,512,128]{2,1,0:T(8,128)(2,1)S(1)}, u32[]{:S(2)}, u32[]{:S(2)}) %collective-permute-start.27) | collective-permute-done | bytes 524320 | tf_op jit(solution)/shard_map/ppermute | solution.py:284
  180.3 5.1 %collective-permute-done.17.refs_1_ = bf16[4,512,128]{2,1,0:T(8,128)(2,1)S(1)} collective-permute-done((bf16[4,512,128]{2,1,0:T(8,128)(2,1)S(1)}, bf16[4,512,128]{2,1,0:T(8,128)(2,1)S(1)}, u32[]{:S(2)}, u32[]{:S(2)}) %collective-permute-start.17) | collective-permute-done | bytes 524320 | tf_op jit(solution)/shard_map/ppermute | solution.py:284
  185.4 0.5 collective-permute-start.24
  186.0 1.4 assemble.3.refs_4_
  187.4 1.9 collective-permute-done.23.refs_5_
  189.3 0.5 collective-permute-start.25
  189.9 1.0 pad_maximum_fusion
  191.0 0.2 collective-permute-done.32.refs_3_
  191.2 1.4 assemble.4.refs_8_
  192.7 2.3 %assemble.5 = bf16[16,512,512]{2,1,0:T(8,128)(2,1)} custom-call(s32[1]{0:T(128)} %bitcast.mine_ref.place_ref, bf16[4,512,128]{2,1,0:T(8,128)(2,1)S(1)} %pad_maximum_fusion.2.refs_0_, bf16[4,512,128]{2,1,0:T(8,128)(2,1)S(1)} %collective-permute-done.17.refs_1_, ...), custom_call_target="tpu_custom_call", output_to_operand_aliasing={{}: (9, {})} | custom-call | bytes 8388608 | tf_op jit(solution)/shard_map/assemble/pallas_call | solution.py:248
  (83 shorter events, 2.9 us)
Async XLA Ops:
  0.6 49.0 %collective-permute-start = (bf16[128,8192]{1,0:T(8,128)(2,1)}, bf16[128,8192]{1,0:T(8,128)(2,1)}, u32[]{:S(2)}, u32[]{:S(2)}) collective-permute-start(bf16[128,8192]{1,0:T(8,128)(2,1)} %bitcast.84), channel_id=1, source_target_pairs={{0,1},{1,0},{2,3},{3,2},{4,5},{5,4},{6,7},{7,6},{8,9},{9,8},{10,11... | collective-permute-start | bytes 6291464 | tf_op jit(solution)/shard_map/ppermute | solution.py:299
  5.6 2.4 %copy-start.3 = (f32[512,512]{1,0:T(8,128)S(1)}, f32[512,512]{1,0:T(8,128)}, u32[]{:S(2)}) copy-start(f32[512,512]{1,0:T(8,128)} %param.8) | copy-start | bytes 3145732
  7.0 2.0 %copy-start.2 = (bf16[1,128,8192]{2,1,0:T(8,128)(2,1)S(1)}, bf16[1,128,8192]{2,1,0:T(8,128)(2,1)}, u32[]{:S(2)}) copy-start(bf16[1,128,8192]{2,1,0:T(8,128)(2,1)} %param.11) | copy-start | bytes 6291460
  9.0 3.4 %copy-start = (bf16[8192,512]{1,0:T(8,128)(2,1)S(1)}, bf16[8192,512]{1,0:T(8,128)(2,1)}, u32[]{:S(2)}) copy-start(bf16[8192,512]{1,0:T(8,128)(2,1)} %weights_ref.3) | copy-start | bytes 25165828
  12.4 1.3 copy-start.4
  12.4 1.4 copy-start.5
  12.4 37.2 %copy-start.1 = (bf16[8192,512]{1,0:T(8,128)(2,1)S(1)}, bf16[8192,512]{1,0:T(8,128)(2,1)}, u32[]{:S(2)}) copy-start(bf16[8192,512]{1,0:T(8,128)(2,1)} %weights_ref.3) | copy-start | bytes 25165828
  64.6 2.7 %collective-permute-start.1 = (f16[8,512,128]{2,1,0:T(8,128)(2,1)S(1)}, f16[8,512,128]{2,1,0:T(8,128)(2,1)S(1)}, u32[]{:S(2)}, u32[]{:S(2)}) collective-permute-start(f16[8,512,128]{2,1,0:T(8,128)(2,1)S(1)} %convert_element_type.204), channel_id=1, source_target_pairs={{0,2},{2,0},{4,6},{6,4},{8,10},{10,8},{12,14},{14,12},{16,18},{18,... | collective-permute-start | bytes 3145736 | tf_op jit(solution)/shard_map/ppermute | solution.py:284
  67.5 21.1 %collective-permute-start.2 = (f16[4,512,128]{2,1,0:T(8,128)(2,1)S(1)}, f16[4,512,128]{2,1,0:T(8,128)(2,1)S(1)}, u32[]{:S(2)}, u32[]{:S(2)}) collective-permute-start(f16[4,512,128]{2,1,0:T(8,128)(2,1)S(1)} %add_convert_fusion.3), channel_id=1, source_target_pairs={{0,4},{2,6},{4,0},{6,2},{8,12},{10,14},{12,8},{14,10},{16,20},{18,... | collective-permute-start | bytes 1572872 | tf_op jit(solution)/shard_map/ppermute | solution.py:284
  88.7 2.7 %collective-permute-start.4 = (f16[8,512,128]{2,1,0:T(8,128)(2,1)S(1)}, f16[8,512,128]{2,1,0:T(8,128)(2,1)S(1)}, u32[]{:S(2)}, u32[]{:S(2)}) collective-permute-start(f16[8,512,128]{2,1,0:T(8,128)(2,1)S(1)} %convert_element_type.207), channel_id=1, source_target_pairs={{0,2},{2,0},{4,6},{6,4},{8,10},{10,8},{12,14},{14,12},{16,18},{18,... | collective-permute-start | bytes 3145736 | tf_op jit(solution)/shard_map/ppermute | solution.py:284
  91.6 14.2 %collective-permute-start.6 = (f16[4,512,128]{2,1,0:T(8,128)(2,1)S(1)}, f16[4,512,128]{2,1,0:T(8,128)(2,1)S(1)}, u32[]{:S(2)}, u32[]{:S(2)}) collective-permute-start(f16[4,512,128]{2,1,0:T(8,128)(2,1)S(1)} %add_convert_fusion.2), channel_id=1, source_target_pairs={{0,4},{2,6},{4,0},{6,2},{8,12},{10,14},{12,8},{14,10},{16,20},{18,... | collective-permute-start | bytes 1572872 | tf_op jit(solution)/shard_map/ppermute | solution.py:284
  92.0 13.8 %collective-permute-start.5 = (f16[2,512,128]{2,1,0:T(8,128)(2,1)S(1)}, f16[2,512,128]{2,1,0:T(8,128)(2,1)S(1)}, u32[]{:S(2)}, u32[]{:S(2)}) collective-permute-start(f16[2,512,128]{2,1,0:T(8,128)(2,1)S(1)} %add_convert_fusion.7), channel_id=1, source_target_pairs={{0,8},{2,10},{4,12},{6,14},{8,0},{10,2},{12,4},{14,6},{16,24},{18,... | collective-permute-start | bytes 786440 | tf_op jit(solution)/shard_map/ppermute | solution.py:284
  93.8 12.4 %collective-permute-start.3 = (f16[8,512,128]{2,1,0:T(8,128)(2,1)S(1)}, f16[8,512,128]{2,1,0:T(8,128)(2,1)S(1)}, u32[]{:S(2)}, u32[]{:S(2)}) collective-permute-start(f16[8,512,128]{2,1,0:T(8,128)(2,1)S(1)} %convert_element_type.208), channel_id=1, source_target_pairs={{0,2},{2,0},{4,6},{6,4},{8,10},{10,8},{12,14},{14,12},{16,18},{18,... | collective-permute-start | bytes 3145736 | tf_op jit(solution)/shard_map/ppermute | solution.py:284
  106.4 5.1 %collective-permute-start.10 = (f16[8,512,128]{2,1,0:T(8,128)(2,1)S(1)}, f16[8,512,128]{2,1,0:T(8,128)(2,1)S(1)}, u32[]{:S(2)}, u32[]{:S(2)}) collective-permute-start(f16[8,512,128]{2,1,0:T(8,128)(2,1)S(1)} %convert_element_type.227), channel_id=1, source_target_pairs={{0,2},{2,0},{4,6},{6,4},{8,10},{10,8},{12,14},{14,12},{16,18},{18,... | collective-permute-start | bytes 3145736 | tf_op jit(solution)/shard_map/ppermute | solution.py:284
  106.9 13.7 %collective-permute-start.9 = (f16[2,512,128]{2,1,0:T(8,128)(2,1)S(1)}, f16[2,512,128]{2,1,0:T(8,128)(2,1)S(1)}, u32[]{:S(2)}, u32[]{:S(2)}) collective-permute-start(f16[2,512,128]{2,1,0:T(8,128)(2,1)S(1)} %add_convert_fusion.6), channel_id=1, source_target_pairs={{0,8},{2,10},{4,12},{6,14},{8,0},{10,2},{12,4},{14,6},{16,24},{18,... | collective-permute-start | bytes 786440 | tf_op jit(solution)/shard_map/ppermute | solution.py:284
  107.9 16.2 %collective-permute-start.7 = (f16[4,512,128]{2,1,0:T(8,128)(2,1)S(1)}, f16[4,512,128]{2,1,0:T(8,128)(2,1)S(1)}, u32[]{:S(2)}, u32[]{:S(2)}) collective-permute-start(f16[4,512,128]{2,1,0:T(8,128)(2,1)S(1)} %add_convert_fusion.1), channel_id=1, source_target_pairs={{0,4},{2,6},{4,0},{6,2},{8,12},{10,14},{12,8},{14,10},{16,20},{18,... | collective-permute-start | bytes 1572872 | tf_op jit(solution)/shard_map/ppermute | solution.py:284
  108.9 14.3 %collective-permute-start.8 = (f16[2,512,128]{2,1,0:T(8,128)(2,1)S(1)}, f16[2,512,128]{2,1,0:T(8,128)(2,1)S(1)}, u32[]{:S(2)}, u32[]{:S(2)}) collective-permute-start(f16[2,512,128]{2,1,0:T(8,128)(2,1)S(1)} %pad_maximum_fusion.6), channel_id=1, source_target_pairs={{0,16},{2,18},{4,20},{6,22},{8,24},{10,26},{12,28},{14,30},{16,0},... | collective-permute-start | bytes 786440 | tf_op jit(solution)/shard_map/ppermute | solution.py:284
  111.6 11.5 %copy-start.9 = (bf16[2,512,128]{2,1,0:T(8,128)(2,1)S(1)}, bf16[2,512,128]{2,1,0:T(8,128)(2,1)}, u32[]{:S(2)}) copy-start(bf16[2,512,128]{2,1,0:T(8,128)(2,1)} %get-tuple-element.85) | copy-start | bytes 786436
  111.6 21.5 %collective-permute-start.14 = (f16[4,512,128]{2,1,0:T(8,128)(2,1)S(1)}, f16[4,512,128]{2,1,0:T(8,128)(2,1)S(1)}, u32[]{:S(2)}, u32[]{:S(2)}) collective-permute-start(f16[4,512,128]{2,1,0:T(8,128)(2,1)S(1)} %add_convert_fusion), channel_id=1, source_target_pairs={{0,4},{2,6},{4,0},{6,2},{8,12},{10,14},{12,8},{14,10},{16,20},{18,... | collective-permute-start | bytes 1572872 | tf_op jit(solution)/shard_map/ppermute | solution.py:284
  123.3 18.9 %copy-start.8 = (bf16[2,512,128]{2,1,0:T(8,128)(2,1)S(1)}, bf16[2,512,128]{2,1,0:T(8,128)(2,1)}, u32[]{:S(2)}) copy-start(bf16[2,512,128]{2,1,0:T(8,128)(2,1)} %get-tuple-element.94) | copy-start | bytes 786436
  123.3 14.9 %collective-permute-start.13 = (bf16[2,512,128]{2,1,0:T(8,128)(2,1)S(1)}, bf16[2,512,128]{2,1,0:T(8,128)(2,1)S(1)}, u32[]{:S(2)}, u32[]{:S(2)}) collective-permute-start(bf16[2,512,128]{2,1,0:T(8,128)(2,1)S(1)} %subtract_convert_fusion.3), channel_id=1, source_target_pairs={{0,8},{2,10},{4,12},{6,14},{8,0},{10,2},{12,4},{14,6},{16,24},{18,... | collective-permute-start | bytes 786440 | tf_op jit(solution)/shard_map/ppermute | solution.py:284
  124.3 19.2 %collective-permute-start.11 = (f16[2,512,128]{2,1,0:T(8,128)(2,1)S(1)}, f16[2,512,128]{2,1,0:T(8,128)(2,1)S(1)}, u32[]{:S(2)}, u32[]{:S(2)}) collective-permute-start(f16[2,512,128]{2,1,0:T(8,128)(2,1)S(1)} %add_convert_fusion.5), channel_id=1, source_target_pairs={{0,8},{2,10},{4,12},{6,14},{8,0},{10,2},{12,4},{14,6},{16,24},{18,... | collective-permute-start | bytes 786440 | tf_op jit(solution)/shard_map/ppermute | solution.py:284
  125.6 16.6 %collective-permute-start.12 = (f16[2,512,128]{2,1,0:T(8,128)(2,1)S(1)}, f16[2,512,128]{2,1,0:T(8,128)(2,1)S(1)}, u32[]{:S(2)}, u32[]{:S(2)}) collective-permute-start(f16[2,512,128]{2,1,0:T(8,128)(2,1)S(1)} %pad_maximum_fusion.7), channel_id=1, source_target_pairs={{0,16},{2,18},{4,20},{6,22},{8,24},{10,26},{12,28},{14,30},{16,0},... | collective-permute-start | bytes 786440 | tf_op jit(solution)/shard_map/ppermute | solution.py:284
  133.3 16.1 %collective-permute-start.20 = (f16[2,512,128]{2,1,0:T(8,128)(2,1)S(1)}, f16[2,512,128]{2,1,0:T(8,128)(2,1)S(1)}, u32[]{:S(2)}, u32[]{:S(2)}) collective-permute-start(f16[2,512,128]{2,1,0:T(8,128)(2,1)S(1)} %add_convert_fusion.4), channel_id=1, source_target_pairs={{0,8},{2,10},{4,12},{6,14},{8,0},{10,2},{12,4},{14,6},{16,24},{18,... | collective-permute-start | bytes 786440 | tf_op jit(solution)/shard_map/ppermute | solution.py:284
  138.3 34.4 %collective-permute-start.28 = (bf16[4,512,128]{2,1,0:T(8,128)(2,1)S(1)}, bf16[4,512,128]{2,1,0:T(8,128)(2,1)S(1)}, u32[]{:S(2)}, u32[]{:S(2)}) collective-permute-start(bf16[4,512,128]{2,1,0:T(8,128)(2,1)S(1)} %pad_maximum_fusion.1.refs_0_), channel_id=1, source_target_pairs={{0,4},{2,6},{4,0},{6,2},{8,12},{10,14},{12,8},{14,10},{16,20},{18,... | collective-permute-start | bytes 1572872 | tf_op jit(solution)/shard_map/ppermute | solution.py:284
  142.3 22.1 %collective-permute-start.26 = (bf16[2,512,128]{2,1,0:T(8,128)(2,1)S(1)}, bf16[2,512,128]{2,1,0:T(8,128)(2,1)S(1)}, u32[]{:S(2)}, u32[]{:S(2)}) collective-permute-start(bf16[2,512,128]{2,1,0:T(8,128)(2,1)S(1)} %subtract_convert_fusion.2), channel_id=1, source_target_pairs={{0,4},{2,6},{4,0},{6,2},{8,12},{10,14},{12,8},{14,10},{16,20},{18,... | collective-permute-start | bytes 786440 | tf_op jit(solution)/shard_map/ppermute | solution.py:284
  143.6 20.6 %copy-start.7 = (bf16[2,512,128]{2,1,0:T(8,128)(2,1)S(1)}, bf16[2,512,128]{2,1,0:T(8,128)(2,1)}, u32[]{:S(2)}) copy-start(bf16[2,512,128]{2,1,0:T(8,128)(2,1)} %get-tuple-element.63) | copy-start | bytes 786436
  143.7 20.5 %collective-permute-start.15 = (f16[2,512,128]{2,1,0:T(8,128)(2,1)S(1)}, f16[2,512,128]{2,1,0:T(8,128)(2,1)S(1)}, u32[]{:S(2)}, u32[]{:S(2)}) collective-permute-start(f16[2,512,128]{2,1,0:T(8,128)(2,1)S(1)} %pad_maximum_fusion.8), channel_id=1, source_target_pairs={{0,16},{2,18},{4,20},{6,22},{8,24},{10,26},{12,28},{14,30},{16,0},... | collective-permute-start | bytes 786440 | tf_op jit(solution)/shard_map/ppermute | solution.py:284
  149.4 18.1 %copy-start.6 = (bf16[2,512,128]{2,1,0:T(8,128)(2,1)S(1)}, bf16[2,512,128]{2,1,0:T(8,128)(2,1)}, u32[]{:S(2)}) copy-start(bf16[2,512,128]{2,1,0:T(8,128)(2,1)} %get-tuple-element.100) | copy-start | bytes 786436
  149.6 18.0 %collective-permute-start.21 = (f16[2,512,128]{2,1,0:T(8,128)(2,1)S(1)}, f16[2,512,128]{2,1,0:T(8,128)(2,1)S(1)}, u32[]{:S(2)}, u32[]{:S(2)}) collective-permute-start(f16[2,512,128]{2,1,0:T(8,128)(2,1)S(1)} %pad_maximum_fusion.9), channel_id=1, source_target_pairs={{0,16},{2,18},{4,20},{6,22},{8,24},{10,26},{12,28},{14,30},{16,0},... | collective-permute-start | bytes 786440 | tf_op jit(solution)/shard_map/ppermute | solution.py:284
  164.3 8.1 %collective-permute-start.16 = (bf16[2,512,128]{2,1,0:T(8,128)(2,1)S(1)}, bf16[2,512,128]{2,1,0:T(8,128)(2,1)S(1)}, u32[]{:S(2)}, u32[]{:S(2)}) collective-permute-start(bf16[2,512,128]{2,1,0:T(8,128)(2,1)S(1)} %subtract_convert_fusion.1), channel_id=1, source_target_pairs={{0,8},{2,10},{4,12},{6,14},{8,0},{10,2},{12,4},{14,6},{16,24},{18,... | collective-permute-start | bytes 786440 | tf_op jit(solution)/shard_map/ppermute | solution.py:284
  164.5 15.7 %collective-permute-start.27 = (bf16[4,512,128]{2,1,0:T(8,128)(2,1)S(1)}, bf16[4,512,128]{2,1,0:T(8,128)(2,1)S(1)}, u32[]{:S(2)}, u32[]{:S(2)}) collective-permute-start(bf16[4,512,128]{2,1,0:T(8,128)(2,1)S(1)} %pad_maximum_fusion.4.refs_0_), channel_id=1, source_target_pairs={{0,8},{2,10},{4,12},{6,14},{8,0},{10,2},{12,4},{14,6},{16,24},{18,... | collective-permute-start | bytes 1572872 | tf_op jit(solution)/shard_map/ppermute | solution.py:284
  167.7 8.7 %collective-permute-start.22 = (bf16[2,512,128]{2,1,0:T(8,128)(2,1)S(1)}, bf16[2,512,128]{2,1,0:T(8,128)(2,1)S(1)}, u32[]{:S(2)}, u32[]{:S(2)}) collective-permute-start(bf16[2,512,128]{2,1,0:T(8,128)(2,1)S(1)} %subtract_convert_fusion), channel_id=1, source_target_pairs={{0,4},{2,6},{4,0},{6,2},{8,12},{10,14},{12,8},{14,10},{16,20},{18,... | collective-permute-start | bytes 786440 | tf_op jit(solution)/shard_map/ppermute | solution.py:284
  168.7 16.6 %collective-permute-start.29 = (bf16[4,512,128]{2,1,0:T(8,128)(2,1)S(1)}, bf16[4,512,128]{2,1,0:T(8,128)(2,1)S(1)}, u32[]{:S(2)}, u32[]{:S(2)}) collective-permute-start(bf16[4,512,128]{2,1,0:T(8,128)(2,1)S(1)} %pad_maximum_fusion.1.refs_0_), channel_id=1, source_target_pairs={{0,2},{2,0},{4,6},{6,4},{8,10},{10,8},{12,14},{14,12},{16,18},{18,... | collective-permute-start | bytes 1572872 | tf_op jit(solution)/shard_map/ppermute | solution.py:284
  172.5 12.9 %collective-permute-start.17 = (bf16[4,512,128]{2,1,0:T(8,128)(2,1)S(1)}, bf16[4,512,128]{2,1,0:T(8,128)(2,1)S(1)}, u32[]{:S(2)}, u32[]{:S(2)}) collective-permute-start(bf16[4,512,128]{2,1,0:T(8,128)(2,1)S(1)} %pad_maximum_fusion.2.refs_0_), channel_id=1, source_target_pairs={{0,4},{2,6},{4,0},{6,2},{8,12},{10,14},{12,8},{14,10},{16,20},{18,... | collective-permute-start | bytes 1572872 | tf_op jit(solution)/shard_map/ppermute | solution.py:284
  172.7 13.2 %collective-permute-start.30 = (bf16[4,512,128]{2,1,0:T(8,128)(2,1)S(1)}, bf16[4,512,128]{2,1,0:T(8,128)(2,1)S(1)}, u32[]{:S(2)}, u32[]{:S(2)}) collective-permute-start(bf16[4,512,128]{2,1,0:T(8,128)(2,1)S(1)} %collective-permute-done.28.refs_1_), channel_id=1, source_target_pairs={{0,2},{2,0},{4,6},{6,4},{8,10},{10,8},{12,14},{14,12},{16,18},{18,... | collective-permute-start | bytes 1572872 | tf_op jit(solution)/shard_map/ppermute | solution.py:284
  176.4 12.9 %collective-permute-start.23 = (bf16[4,512,128]{2,1,0:T(8,128)(2,1)S(1)}, bf16[4,512,128]{2,1,0:T(8,128)(2,1)S(1)}, u32[]{:S(2)}, u32[]{:S(2)}) collective-permute-start(bf16[4,512,128]{2,1,0:T(8,128)(2,1)S(1)} %pad_maximum_fusion.3.refs_4_), channel_id=1, source_target_pairs={{0,8},{2,10},{4,12},{6,14},{8,0},{10,2},{12,4},{14,6},{16,24},{18,... | collective-permute-start | bytes 1572872 | tf_op jit(solution)/shard_map/ppermute | solution.py:284
  180.1 9.2 %collective-permute-start.31 = (bf16[4,512,128]{2,1,0:T(8,128)(2,1)S(1)}, bf16[4,512,128]{2,1,0:T(8,128)(2,1)S(1)}, u32[]{:S(2)}, u32[]{:S(2)}) collective-permute-start(bf16[4,512,128]{2,1,0:T(8,128)(2,1)S(1)} %pad_maximum_fusion.4.refs_0_), channel_id=1, source_target_pairs={{0,2},{2,0},{4,6},{6,4},{8,10},{10,8},{12,14},{14,12},{16,18},{18,... | collective-permute-start | bytes 1572872 | tf_op jit(solution)/shard_map/ppermute | solution.py:284
  185.4 7.3 %collective-permute-start.18 = (bf16[4,512,128]{2,1,0:T(8,128)(2,1)S(1)}, bf16[4,512,128]{2,1,0:T(8,128)(2,1)S(1)}, u32[]{:S(2)}, u32[]{:S(2)}) collective-permute-start(bf16[4,512,128]{2,1,0:T(8,128)(2,1)S(1)} %pad_maximum_fusion.2.refs_0_), channel_id=1, source_target_pairs={{0,2},{2,0},{4,6},{6,4},{8,10},{10,8},{12,14},{14,12},{16,18},{18,... | collective-permute-start | bytes 1572872 | tf_op jit(solution)/shard_map/ppermute | solution.py:284
  185.4 7.3 %collective-permute-start.24 = (bf16[4,512,128]{2,1,0:T(8,128)(2,1)S(1)}, bf16[4,512,128]{2,1,0:T(8,128)(2,1)S(1)}, u32[]{:S(2)}, u32[]{:S(2)}) collective-permute-start(bf16[4,512,128]{2,1,0:T(8,128)(2,1)S(1)} %pad_maximum_fusion.3.refs_4_), channel_id=1, source_target_pairs={{0,2},{2,0},{4,6},{6,4},{8,10},{10,8},{12,14},{14,12},{16,18},{18,... | collective-permute-start | bytes 1572872 | tf_op jit(solution)/shard_map/ppermute | solution.py:284
  185.9 6.8 %collective-permute-start.19 = (bf16[4,512,128]{2,1,0:T(8,128)(2,1)S(1)}, bf16[4,512,128]{2,1,0:T(8,128)(2,1)S(1)}, u32[]{:S(2)}, u32[]{:S(2)}) collective-permute-start(bf16[4,512,128]{2,1,0:T(8,128)(2,1)S(1)} %collective-permute-done.17.refs_1_), channel_id=1, source_target_pairs={{0,2},{2,0},{4,6},{6,4},{8,10},{10,8},{12,14},{14,12},{16,18},{18,... | collective-permute-start | bytes 1572872 | tf_op jit(solution)/shard_map/ppermute | solution.py:284
  189.3 1.9 collective-permute-start.32
  189.3 3.4 %collective-permute-start.25 = (bf16[4,512,128]{2,1,0:T(8,128)(2,1)S(1)}, bf16[4,512,128]{2,1,0:T(8,128)(2,1)S(1)}, u32[]{:S(2)}, u32[]{:S(2)}) collective-permute-start(bf16[4,512,128]{2,1,0:T(8,128)(2,1)S(1)} %collective-permute-done.23.refs_5_), channel_id=1, source_target_pairs={{0,2},{2,0},{4,6},{6,4},{8,10},{10,8},{12,14},{14,12},{16,18},{18,... | collective-permute-start | bytes 1572872 | tf_op jit(solution)/shard_map/ppermute | solution.py:284

commit v16 on v15

--- a/solution.py
+++ b/solution.py
@@ -55,11 +55,10 @@
     return pltpu.with_memory_space_constraint(array, pltpu.HBM)
 
 
-def changed_place(mine, slab, pair, pairs):
+def changed_place(mine, slab, pair, pairs, order):
     offset = lax.bitwise_xor(slab * pairs + pair, mine // 2)
-    bits = (SLABS * pairs).bit_length() - 1
     place = jnp.int32(0)
-    for bit in range(bits):
+    for bit in order:
         place = place * 2 + lax.rem(lax.shift_right_logical(offset, bit), 2)
     return place
 
@@ -67,6 +66,7 @@
 def inner_kernel(
     tokens,
     kept,
+    orders,
     mine_ref,
     low_ref,
     high_ref,
@@ -154,7 +154,7 @@
                 ahead, next_pair, next_side = slots[slot + 1]
                 differentiate(next_pair, sides[next_side][0], ahead)
             which, out_refs = sides[side]
-            place = changed_place(mine, slab, pair, pairs)
+            places = [changed_place(mine, slab, pair, pairs, order) for order in orders]
             for piece in pieces:
                 gradient = gradient_state[slot % held, piece]
                 first = first_state[slab, pair, which, piece]
@@ -169,10 +169,10 @@
                 change = (start - descend(first, second, weights)) * WIRE_SCALE
                 for index, out_ref in enumerate(out_refs):
                     part = out_ref.shape[-1]
-                    out_ref[place, piece] = change[:, index * part : (index + 1) * part]
-
-
-def inner(call, width, part, mine, banks, turned, start, first, second, products, target, count, tokens):
+                    out_ref[places[index], piece] = change[:, index * part : (index + 1) * part]
+
+
+def inner(call, width, part, orders, mine, banks, turned, start, first, second, products, target, count, tokens):
     slabs, pairs, cores, rows, _ = start.shape
     half, depth = banks[0].shape
 
@@ -188,7 +188,7 @@
     kept = width == part
     elements = depth * width
     return pl.pallas_call(
-        functools.partial(inner_kernel, float(tokens), kept),
+        functools.partial(inner_kernel, float(tokens), kept, orders),
         grid_spec=pltpu.PrefetchScalarGridSpec(
             num_scalar_prefetch=1,
             grid=(2, slabs),
@@ -338,9 +338,13 @@
 
     result = ()
 
+    def order_of(chunk):
+        order = list(range(len(spans)))
+        return [1, 0] + order[2:] if chunk == 2 else order
+
     def chain(chunk, keep, arrived):
         terms = [keep, arrived]
-        for span in spans[:-1]:
+        for span in [spans[bit] for bit in order_of(chunk)][:-1]:
             outgoing, terms = parted(terms, span)
             outgoing = yield outgoing
             arrived = yield sent(outgoing, span)
@@ -383,7 +387,20 @@
     later = {}
     for begin, wide in calls:
         changes = inner(
-            begin // wide, wide, width, token, banks, turned, start, first, second, products, target, count, tokens
+            begin // wide,
+            wide,
+            width,
+            [order_of(chunk) for chunk in range(fresh.stop, fresh.stop + wide // width)],
+            token,
+            banks,
+            turned,
+            start,
+            first,
+            second,
+            products,
+            target,
+            count,
+            tokens,
         )
         sends = [send.astype(WIRE) for send in changes[::2]]
         if fresh:
@@ -403,7 +420,7 @@
             formed, token = tied(formed, token)
     if chunks == 4:
         before = 3
-        for which in (1, 0, 2, 3, 0, 1, 2):
+        for which in (1, 0, 3, 2, 0, 1, 3, 2):
             move_on([which], behind=[before])
             before = which
     for chunk in range(chunks):

time: 196 us -> 208 us (1.061)
  waiting for transfers between devices: 97.2 us -> 111 us
    ppermute x32, waiting for transfers between devices: 61.4 us -> 74.9 us  [swapped(): return lax.ppermute(array, 'rep', pairs)]
  transfers between devices with their start and end apart: 33 -> 33, of which waited for: 17 -> 15; matrix products, arithmetic and copies ran while one was open for 4% -> 4% of each run, Pallas kernels for 18% -> 17%
where the time goes in v16:
time: 208 us
  waiting for transfers between devices  111 us (53%)
  Pallas kernels  52.1 us (25%)
  starting transfers between devices  30 us (14%)
  local copies, waits for them, and re-layouts  6.74 us (3%)
  other arithmetic  6.68 us (3%)
    ppermute x32, waiting for transfers between devices, swapped(): return lax.ppermute(array, 'rep', pairs)  74.9 us
    pallas_call x3, Pallas kernels, inner(): pl.pallas_call(functools.partial(inner_kernel, float(tokens), kept, order...  42.7 us
    ppermute x1, waiting for transfers between devices, per_device(): banks = (own_bank, lax.ppermute(own_bank, 'fsdp', [(0, 1), (1, 0)]))  35.8 us
    ppermute x32, starting transfers between devices, swapped(): return lax.ppermute(array, 'rep', pairs)  26.9 us
    pallas_call x3, Pallas kernels, assemble(): pl.pallas_call(functools.partial(assemble_kernel, begins, offsets), in_sp...  5.14 us
    unnamed x20, local copies, waits for them, and re-layouts  4.29 us
    pallas_call x2, Pallas kernels, forward(): pl.pallas_call(forward_kernel, in_specs=[vmem, vmem], out_specs=[vmem, vm...  4.23 us
  transfers between devices with their start and end apart: 33, of which 15 were waited for; matrix products, arithmetic and copies ran while one was open for 4% of the time, Pallas kernels for 17%

profile of v16, /device:TPU:0, one launch (start us, length us, event | category | flops | bytes accessed | tf_op | source)
XLA Modules:
  0.0 207.5 jit_solution(8360799074252232632)
XLA Ops:
  0.6 3.0 %collective-permute-start = (bf16[128,8192]{1,0:T(8,128)(2,1)}, bf16[128,8192]{1,0:T(8,128)(2,1)}, u32[]{:S(2)}, u32[]{:S(2)}) collective-permute-start(bf16[128,8192]{1,0:T(8,128)(2,1)} %bitcast.84), channel_id=1, source_target_pairs={{0,1},{1,0},{2,3},{3,2},{4,5},{5,4},{6,7},{7,6},{8,9},{9,8},{10,11... | collective-permute-start | bytes 6291464 | tf_op jit(solution)/shard_map/ppermute | solution.py:299
  3.7 0.9 convert_reduce_fusion
  4.6 0.1 copy.21
  4.8 0.9 copy.22
  5.6 1.4 dynamic-slice_bitcast_fusion
  7.0 1.1 pad_maximum_fusion.5
  8.1 0.9 copy-done.2
  9.0 3.4 %copy-done = bf16[8192,512]{1,0:T(8,128)(2,1)S(1)} copy-done((bf16[8192,512]{1,0:T(8,128)(2,1)S(1)}, bf16[8192,512]{1,0:T(8,128)(2,1)}, u32[]{:S(2)}) %copy-start) | copy-done | bytes 8388632
  12.4 1.3 forward.2
  13.8 35.8 %collective-permute-done.part_ref.high_ref = bf16[128,8192]{1,0:T(8,128)(2,1)} collective-permute-done((bf16[128,8192]{1,0:T(8,128)(2,1)}, bf16[128,8192]{1,0:T(8,128)(2,1)}, u32[]{:S(2)}, u32[]{:S(2)}) %collective-permute-start) | collective-permute-done | bytes 2097184 | tf_op jit(solution)/shard_map/ppermute | solution.py:299
  49.6 3.0 %forward.3 = (bf16[8192,128]{1,0:T(8,128)(2,1)S(1)}, f32[128,512]{1,0:T(8,128)S(1)}) custom-call(bf16[128,8192]{1,0:T(8,128)(2,1)} %collective-permute-done.part_ref.high_ref, bf16[8192,512]{1,0:T(8,128)(2,1)S(1)} %copy-done.1), custom_call_target="tpu_custom_call" | custom-call | flops 1073741824 | bytes 12582912 | tf_op jit(solution)/shard_map/forward/pallas_call | solution.py:36
  52.6 11.8 %inner.3 = (f32[8,512,128]{2,1,0:T(8,128)S(1)}, f32[8,512,128]{2,1,0:T(8,128)S(1)}) custom-call(s32[1]{0:T(128)} %bitcast.mine_ref.place_ref, bf16[128,8192]{1,0:T(8,128)(2,1)S(1)} %bitcast.86, bf16[128,8192]{1,0:T(8,128)(2,1)} %collective-permute-done.part_ref.high_ref, bf16[4,2,2,512,128]{4,3,2,1,0:T(8,128)(2,1)S(1)} %bitcast.89, ...), custom_call_target="tpu_custom_call" | custom-call | flops 1610612736 | bytes 20971520 | tf_op jit(solution)/shard_map/inner/pallas_call | solution.py:190
  64.4 0.1 convert_element_type.204
  64.7 2.6 %collective-permute-done.1 = f16[8,512,128]{2,1,0:T(8,128)(2,1)S(1)} collective-permute-done((f16[8,512,128]{2,1,0:T(8,128)(2,1)S(1)}, f16[8,512,128]{2,1,0:T(8,128)(2,1)S(1)}, u32[]{:S(2)}, u32[]{:S(2)}) %collective-permute-start.1) | collective-permute-done | bytes 1048608 | tf_op jit(solution)/shard_map/ppermute | solution.py:284
  67.3 0.1 add_convert_fusion.3
  67.5 1.8 collective-permute-start.2
  69.2 19.0 %inner.4 = (f32[8,512,128]{2,1,0:T(8,128)S(1)}, f32[8,512,128]{2,1,0:T(8,128)S(1)}, f32[8,512,128]{2,1,0:T(8,128)S(1)}, f32[8,512,128]{2,1,0:T(8,128)S(1)}) custom-call(s32[1]{0:T(128)} %bitcast.mine_ref.place_ref, bf16[128,8192]{1,0:T(8,128)(2,1)S(1)} %bitcast.87, bf16[128,8192]{1,0:T(8,128)(2,1)} %collective-permute-done.part_ref.high_ref, ...), custom_call_target="tpu_custom_call" | custom-call | flops 3221225472 | bytes 41943040 | tf_op jit(solution)/shard_map/inner/pallas_call | solution.py:190
  88.3 0.1 convert_element_type.207
  88.4 0.1 convert_element_type.208
  88.8 2.6 %collective-permute-done.4 = f16[8,512,128]{2,1,0:T(8,128)(2,1)S(1)} collective-permute-done((f16[8,512,128]{2,1,0:T(8,128)(2,1)S(1)}, f16[8,512,128]{2,1,0:T(8,128)(2,1)S(1)}, u32[]{:S(2)}, u32[]{:S(2)}) %collective-permute-start.4) | collective-permute-done | bytes 1048608 | tf_op jit(solution)/shard_map/ppermute | solution.py:284
  91.4 0.1 add_convert_fusion.2
  91.6 0.4 collective-permute-start.6
  91.9 1.8 collective-permute-start.5
  93.7 11.8 %inner.5 = (f32[8,512,128]{2,1,0:T(8,128)S(1)}, f32[8,512,128]{2,1,0:T(8,128)S(1)}) custom-call(s32[1]{0:T(128)} %bitcast.mine_ref.place_ref, bf16[128,8192]{1,0:T(8,128)(2,1)S(1)} %bitcast.88, bf16[128,8192]{1,0:T(8,128)(2,1)} %collective-permute-done.part_ref.high_ref, bf16[4,2,2,512,128]{4,3,2,1,0:T(8,128)(2,1)S(1)} %bitcast.91, ...), custom_call_target="tpu_custom_call" | custom-call | flops 1610612736 | bytes 20971520 | tf_op jit(solution)/shard_map/inner/pallas_call | solution.py:190
  105.6 0.1 convert_element_type.223
  106.2 0.1 add_convert_fusion.1
  106.3 0.6 collective-permute-start.8
  106.9 1.0 collective-permute-start.11
  107.9 1.0 collective-permute-start.7
  108.9 2.6 %collective-permute-start.10 = (f16[2,512,128]{2,1,0:T(8,128)(2,1)S(1)}, f16[2,512,128]{2,1,0:T(8,128)(2,1)S(1)}, u32[]{:S(2)}, u32[]{:S(2)}) collective-permute-start(f16[2,512,128]{2,1,0:T(8,128)(2,1)S(1)} %pad_maximum_fusion.6), channel_id=1, source_target_pairs={{0,16},{2,18},{4,20},{6,22},{8,24},{10,26},{12,28},{14,30},{16,0},... | collective-permute-start | bytes 786440 | tf_op jit(solution)/shard_map/ppermute | solution.py:284
  111.5 0.1 add_convert_fusion
  111.7 1.6 collective-permute-start.9
  113.2 8.4 %collective-permute-done.11 = f16[2,512,128]{2,1,0:T(8,128)(2,1)S(1)} collective-permute-done((f16[2,512,128]{2,1,0:T(8,128)(2,1)S(1)}, f16[2,512,128]{2,1,0:T(8,128)(2,1)S(1)}, u32[]{:S(2)}, u32[]{:S(2)}) %collective-permute-start.11) | collective-permute-done | bytes 262176 | tf_op jit(solution)/shard_map/ppermute | solution.py:284
  121.7 0.1 convert_add_fusion.2
  122.0 8.9 %collective-permute-done.10 = f16[2,512,128]{2,1,0:T(8,128)(2,1)S(1)} collective-permute-done((f16[2,512,128]{2,1,0:T(8,128)(2,1)S(1)}, f16[2,512,128]{2,1,0:T(8,128)(2,1)S(1)}, u32[]{:S(2)}, u32[]{:S(2)}) %collective-permute-start.10) | collective-permute-done | bytes 262176 | tf_op jit(solution)/shard_map/ppermute | solution.py:284
  130.9 0.1 subtract_convert_fusion.3
  131.1 3.8 %collective-permute-start.15 = (bf16[2,512,128]{2,1,0:T(8,128)(2,1)S(1)}, bf16[2,512,128]{2,1,0:T(8,128)(2,1)S(1)}, u32[]{:S(2)}, u32[]{:S(2)}) collective-permute-start(bf16[2,512,128]{2,1,0:T(8,128)(2,1)S(1)} %subtract_convert_fusion.3), channel_id=1, source_target_pairs={{0,8},{2,10},{4,12},{6,14},{8,0},{10,2},{12,4},{14,6},{16,24},{18,... | collective-permute-start | bytes 786440 | tf_op jit(solution)/shard_map/ppermute | solution.py:284
  135.0 1.7 collective-permute-start.13
  136.8 0.7 collective-permute-start.12
  137.5 9.5 %collective-permute-done.15 = bf16[2,512,128]{2,1,0:T(8,128)(2,1)S(1)} collective-permute-done((bf16[2,512,128]{2,1,0:T(8,128)(2,1)S(1)}, bf16[2,512,128]{2,1,0:T(8,128)(2,1)S(1)}, u32[]{:S(2)}, u32[]{:S(2)}) %collective-permute-start.15) | collective-permute-done | bytes 262176 | tf_op jit(solution)/shard_map/ppermute | solution.py:284
  147.1 0.7 collective-permute-start.28
  147.8 0.6 collective-permute-done.14
  148.5 1.9 collective-permute-start.26
  150.4 1.4 collective-permute-done.13
  152.2 1.9 collective-permute-start.21
  154.3 1.1 collective-permute-start.16
  155.4 7.9 %collective-permute-done.26 = bf16[2,512,128]{2,1,0:T(8,128)(2,1)S(1)} collective-permute-done((bf16[2,512,128]{2,1,0:T(8,128)(2,1)S(1)}, bf16[2,512,128]{2,1,0:T(8,128)(2,1)S(1)}, u32[]{:S(2)}, u32[]{:S(2)}) %collective-permute-start.26) | collective-permute-done | bytes 262176 | tf_op jit(solution)/shard_map/ppermute | solution.py:284
  163.4 9.0 %collective-permute-done.21 = f16[2,512,128]{2,1,0:T(8,128)(2,1)S(1)} collective-permute-done((f16[2,512,128]{2,1,0:T(8,128)(2,1)S(1)}, f16[2,512,128]{2,1,0:T(8,128)(2,1)S(1)}, u32[]{:S(2)}, u32[]{:S(2)}) %collective-permute-start.21) | collective-permute-done | bytes 262176 | tf_op jit(solution)/shard_map/ppermute | solution.py:284
  172.4 0.1 subtract_convert_fusion
  172.6 1.5 collective-permute-start.22
  174.1 2.9 %collective-permute-done.16 = f16[2,512,128]{2,1,0:T(8,128)(2,1)S(1)} collective-permute-done((f16[2,512,128]{2,1,0:T(8,128)(2,1)S(1)}, f16[2,512,128]{2,1,0:T(8,128)(2,1)S(1)}, u32[]{:S(2)}, u32[]{:S(2)}) %collective-permute-start.16) | collective-permute-done | bytes 262176 | tf_op jit(solution)/shard_map/ppermute | solution.py:284
  176.9 0.1 subtract_convert_fusion.1
  177.2 0.5 collective-permute-start.30
  177.7 1.3 collective-permute-done.22
  179.0 0.8 collective-permute-start.23
  179.8 12.8 %collective-permute-done.17 = bf16[2,512,128]{2,1,0:T(8,128)(2,1)S(1)} collective-permute-done((bf16[2,512,128]{2,1,0:T(8,128)(2,1)S(1)}, bf16[2,512,128]{2,1,0:T(8,128)(2,1)S(1)}, u32[]{:S(2)}, u32[]{:S(2)}) %collective-permute-start.17) | collective-permute-done | bytes 262176 | tf_op jit(solution)/shard_map/ppermute | solution.py:284
  193.0 0.6 collective-permute-start.24
  193.6 1.4 assemble.3.refs_4_
  195.1 5.0 %collective-permute-done.23.refs_5_ = bf16[4,512,128]{2,1,0:T(8,128)(2,1)S(1)} collective-permute-done((bf16[4,512,128]{2,1,0:T(8,128)(2,1)S(1)}, bf16[4,512,128]{2,1,0:T(8,128)(2,1)S(1)}, u32[]{:S(2)}, u32[]{:S(2)}) %collective-permute-start.23) | collective-permute-done | bytes 524320 | tf_op jit(solution)/shard_map/ppermute | solution.py:284
  200.1 1.8 collective-permute-done.18.refs_1_
  201.9 0.5 collective-permute-start.20
  202.5 1.0 pad_maximum_fusion
  203.6 1.4 assemble.4.refs_8_
  205.1 2.3 %assemble.5 = bf16[16,512,512]{2,1,0:T(8,128)(2,1)} custom-call(s32[1]{0:T(128)} %bitcast.mine_ref.place_ref, bf16[4,512,128]{2,1,0:T(8,128)(2,1)S(1)} %pad_maximum_fusion.2.refs_0_, bf16[4,512,128]{2,1,0:T(8,128)(2,1)S(1)} %collective-permute-done.18.refs_1_, ...), custom_call_target="tpu_custom_call", output_to_operand_aliasing={{}: (9, {})} | custom-call | bytes 8388608 | tf_op jit(solution)/shard_map/assemble/pallas_call | solution.py:248
  (83 shorter events, 2.8 us)
Async XLA Ops:
  0.6 49.0 %collective-permute-start = (bf16[128,8192]{1,0:T(8,128)(2,1)}, bf16[128,8192]{1,0:T(8,128)(2,1)}, u32[]{:S(2)}, u32[]{:S(2)}) collective-permute-start(bf16[128,8192]{1,0:T(8,128)(2,1)} %bitcast.84), channel_id=1, source_target_pairs={{0,1},{1,0},{2,3},{3,2},{4,5},{5,4},{6,7},{7,6},{8,9},{9,8},{10,11... | collective-permute-start | bytes 6291464 | tf_op jit(solution)/shard_map/ppermute | solution.py:299
  5.6 2.4 %copy-start.3 = (f32[512,512]{1,0:T(8,128)S(1)}, f32[512,512]{1,0:T(8,128)}, u32[]{:S(2)}) copy-start(f32[512,512]{1,0:T(8,128)} %param.8) | copy-start | bytes 3145732
  7.0 2.0 copy-start.2
  9.0 3.4 %copy-start = (bf16[8192,512]{1,0:T(8,128)(2,1)S(1)}, bf16[8192,512]{1,0:T(8,128)(2,1)}, u32[]{:S(2)}) copy-start(bf16[8192,512]{1,0:T(8,128)(2,1)} %weights_ref.3) | copy-start | bytes 25165828
  12.4 1.3 copy-start.4
  12.4 1.4 copy-start.5
  12.4 37.2 %copy-start.1 = (bf16[8192,512]{1,0:T(8,128)(2,1)S(1)}, bf16[8192,512]{1,0:T(8,128)(2,1)}, u32[]{:S(2)}) copy-start(bf16[8192,512]{1,0:T(8,128)(2,1)} %weights_ref.3) | copy-start | bytes 25165828
  64.6 2.7 %collective-permute-start.1 = (f16[8,512,128]{2,1,0:T(8,128)(2,1)S(1)}, f16[8,512,128]{2,1,0:T(8,128)(2,1)S(1)}, u32[]{:S(2)}, u32[]{:S(2)}) collective-permute-start(f16[8,512,128]{2,1,0:T(8,128)(2,1)S(1)} %convert_element_type.204), channel_id=1, source_target_pairs={{0,2},{2,0},{4,6},{6,4},{8,10},{10,8},{12,14},{14,12},{16,18},{18,... | collective-permute-start | bytes 3145736 | tf_op jit(solution)/shard_map/ppermute | solution.py:284
  67.5 21.1 %collective-permute-start.2 = (f16[4,512,128]{2,1,0:T(8,128)(2,1)S(1)}, f16[4,512,128]{2,1,0:T(8,128)(2,1)S(1)}, u32[]{:S(2)}, u32[]{:S(2)}) collective-permute-start(f16[4,512,128]{2,1,0:T(8,128)(2,1)S(1)} %add_convert_fusion.3), channel_id=1, source_target_pairs={{0,4},{2,6},{4,0},{6,2},{8,12},{10,14},{12,8},{14,10},{16,20},{18,... | collective-permute-start | bytes 1572872 | tf_op jit(solution)/shard_map/ppermute | solution.py:284
  88.7 2.7 %collective-permute-start.4 = (f16[8,512,128]{2,1,0:T(8,128)(2,1)S(1)}, f16[8,512,128]{2,1,0:T(8,128)(2,1)S(1)}, u32[]{:S(2)}, u32[]{:S(2)}) collective-permute-start(f16[8,512,128]{2,1,0:T(8,128)(2,1)S(1)} %convert_element_type.207), channel_id=1, source_target_pairs={{0,2},{2,0},{4,6},{6,4},{8,10},{10,8},{12,14},{14,12},{16,18},{18,... | collective-permute-start | bytes 3145736 | tf_op jit(solution)/shard_map/ppermute | solution.py:284
  91.6 14.2 %collective-permute-start.6 = (f16[4,512,128]{2,1,0:T(8,128)(2,1)S(1)}, f16[4,512,128]{2,1,0:T(8,128)(2,1)S(1)}, u32[]{:S(2)}, u32[]{:S(2)}) collective-permute-start(f16[4,512,128]{2,1,0:T(8,128)(2,1)S(1)} %add_convert_fusion.2), channel_id=1, source_target_pairs={{0,4},{2,6},{4,0},{6,2},{8,12},{10,14},{12,8},{14,10},{16,20},{18,... | collective-permute-start | bytes 1572872 | tf_op jit(solution)/shard_map/ppermute | solution.py:284
  91.9 13.8 %collective-permute-start.5 = (f16[2,512,128]{2,1,0:T(8,128)(2,1)S(1)}, f16[2,512,128]{2,1,0:T(8,128)(2,1)S(1)}, u32[]{:S(2)}, u32[]{:S(2)}) collective-permute-start(f16[2,512,128]{2,1,0:T(8,128)(2,1)S(1)} %add_convert_fusion.7), channel_id=1, source_target_pairs={{0,8},{2,10},{4,12},{6,14},{8,0},{10,2},{12,4},{14,6},{16,24},{18,... | collective-permute-start | bytes 786440 | tf_op jit(solution)/shard_map/ppermute | solution.py:284
  93.7 12.4 %collective-permute-start.3 = (f16[8,512,128]{2,1,0:T(8,128)(2,1)S(1)}, f16[8,512,128]{2,1,0:T(8,128)(2,1)S(1)}, u32[]{:S(2)}, u32[]{:S(2)}) collective-permute-start(f16[8,512,128]{2,1,0:T(8,128)(2,1)S(1)} %convert_element_type.208), channel_id=1, source_target_pairs={{0,2},{2,0},{4,6},{6,4},{8,10},{10,8},{12,14},{14,12},{16,18},{18,... | collective-permute-start | bytes 3145736 | tf_op jit(solution)/shard_map/ppermute | solution.py:284
  106.3 5.2 %collective-permute-start.8 = (f16[8,512,128]{2,1,0:T(8,128)(2,1)S(1)}, f16[8,512,128]{2,1,0:T(8,128)(2,1)S(1)}, u32[]{:S(2)}, u32[]{:S(2)}) collective-permute-start(f16[8,512,128]{2,1,0:T(8,128)(2,1)S(1)} %convert_element_type.223), channel_id=1, source_target_pairs={{0,2},{2,0},{4,6},{6,4},{8,10},{10,8},{12,14},{14,12},{16,18},{18,... | collective-permute-start | bytes 3145736 | tf_op jit(solution)/shard_map/ppermute | solution.py:284
  106.9 14.8 %collective-permute-start.11 = (f16[2,512,128]{2,1,0:T(8,128)(2,1)S(1)}, f16[2,512,128]{2,1,0:T(8,128)(2,1)S(1)}, u32[]{:S(2)}, u32[]{:S(2)}) collective-permute-start(f16[2,512,128]{2,1,0:T(8,128)(2,1)S(1)} %add_convert_fusion.6), channel_id=1, source_target_pairs={{0,8},{2,10},{4,12},{6,14},{8,0},{10,2},{12,4},{14,6},{16,24},{18,... | collective-permute-start | bytes 786440 | tf_op jit(solution)/shard_map/ppermute | solution.py:284
  107.9 28.8 %collective-permute-start.7 = (f16[4,512,128]{2,1,0:T(8,128)(2,1)S(1)}, f16[4,512,128]{2,1,0:T(8,128)(2,1)S(1)}, u32[]{:S(2)}, u32[]{:S(2)}) collective-permute-start(f16[4,512,128]{2,1,0:T(8,128)(2,1)S(1)} %add_convert_fusion.1), channel_id=1, source_target_pairs={{0,8},{2,10},{4,12},{6,14},{8,0},{10,2},{12,4},{14,6},{16,24},{18,... | collective-permute-start | bytes 1572872 | tf_op jit(solution)/shard_map/ppermute | solution.py:284
  108.9 22.0 %collective-permute-start.10 = (f16[2,512,128]{2,1,0:T(8,128)(2,1)S(1)}, f16[2,512,128]{2,1,0:T(8,128)(2,1)S(1)}, u32[]{:S(2)}, u32[]{:S(2)}) collective-permute-start(f16[2,512,128]{2,1,0:T(8,128)(2,1)S(1)} %pad_maximum_fusion.6), channel_id=1, source_target_pairs={{0,16},{2,18},{4,20},{6,22},{8,24},{10,26},{12,28},{14,30},{16,0},... | collective-permute-start | bytes 786440 | tf_op jit(solution)/shard_map/ppermute | solution.py:284
  111.7 19.3 %copy-start.9 = (bf16[2,512,128]{2,1,0:T(8,128)(2,1)S(1)}, bf16[2,512,128]{2,1,0:T(8,128)(2,1)}, u32[]{:S(2)}) copy-start(bf16[2,512,128]{2,1,0:T(8,128)(2,1)} %get-tuple-element.90) | copy-start | bytes 786436
  111.7 23.2 %collective-permute-start.9 = (f16[4,512,128]{2,1,0:T(8,128)(2,1)S(1)}, f16[4,512,128]{2,1,0:T(8,128)(2,1)S(1)}, u32[]{:S(2)}, u32[]{:S(2)}) collective-permute-start(f16[4,512,128]{2,1,0:T(8,128)(2,1)S(1)} %add_convert_fusion), channel_id=1, source_target_pairs={{0,4},{2,6},{4,0},{6,2},{8,12},{10,14},{12,8},{14,10},{16,20},{18,... | collective-permute-start | bytes 1572872 | tf_op jit(solution)/shard_map/ppermute | solution.py:284
  131.0 17.3 %copy-start.8 = (bf16[2,512,128]{2,1,0:T(8,128)(2,1)S(1)}, bf16[2,512,128]{2,1,0:T(8,128)(2,1)}, u32[]{:S(2)}) copy-start(bf16[2,512,128]{2,1,0:T(8,128)(2,1)} %get-tuple-element.96) | copy-start | bytes 786436
  131.1 16.0 %collective-permute-start.15 = (bf16[2,512,128]{2,1,0:T(8,128)(2,1)S(1)}, bf16[2,512,128]{2,1,0:T(8,128)(2,1)S(1)}, u32[]{:S(2)}, u32[]{:S(2)}) collective-permute-start(bf16[2,512,128]{2,1,0:T(8,128)(2,1)S(1)} %subtract_convert_fusion.3), channel_id=1, source_target_pairs={{0,8},{2,10},{4,12},{6,14},{8,0},{10,2},{12,4},{14,6},{16,24},{18,... | collective-permute-start | bytes 786440 | tf_op jit(solution)/shard_map/ppermute | solution.py:284
  134.8 13.5 %collective-permute-start.14 = (f16[2,512,128]{2,1,0:T(8,128)(2,1)S(1)}, f16[2,512,128]{2,1,0:T(8,128)(2,1)S(1)}, u32[]{:S(2)}, u32[]{:S(2)}) collective-permute-start(f16[2,512,128]{2,1,0:T(8,128)(2,1)S(1)} %pad_maximum_fusion.7), channel_id=1, source_target_pairs={{0,16},{2,18},{4,20},{6,22},{8,24},{10,26},{12,28},{14,30},{16,0},... | collective-permute-start | bytes 786440 | tf_op jit(solution)/shard_map/ppermute | solution.py:284
  135.0 16.8 %collective-permute-start.13 = (f16[2,512,128]{2,1,0:T(8,128)(2,1)S(1)}, f16[2,512,128]{2,1,0:T(8,128)(2,1)S(1)}, u32[]{:S(2)}, u32[]{:S(2)}) collective-permute-start(f16[2,512,128]{2,1,0:T(8,128)(2,1)S(1)} %add_convert_fusion.5), channel_id=1, source_target_pairs={{0,8},{2,10},{4,12},{6,14},{8,0},{10,2},{12,4},{14,6},{16,24},{18,... | collective-permute-start | bytes 786440 | tf_op jit(solution)/shard_map/ppermute | solution.py:284
  136.8 15.2 %collective-permute-start.12 = (f16[2,512,128]{2,1,0:T(8,128)(2,1)S(1)}, f16[2,512,128]{2,1,0:T(8,128)(2,1)S(1)}, u32[]{:S(2)}, u32[]{:S(2)}) collective-permute-start(f16[2,512,128]{2,1,0:T(8,128)(2,1)S(1)} %add_convert_fusion.4), channel_id=1, source_target_pairs={{0,4},{2,6},{4,0},{6,2},{8,12},{10,14},{12,8},{14,10},{16,20},{18,... | collective-permute-start | bytes 786440 | tf_op jit(solution)/shard_map/ppermute | solution.py:284
  147.1 30.2 %collective-permute-start.28 = (bf16[4,512,128]{2,1,0:T(8,128)(2,1)S(1)}, bf16[4,512,128]{2,1,0:T(8,128)(2,1)S(1)}, u32[]{:S(2)}, u32[]{:S(2)}) collective-permute-start(bf16[4,512,128]{2,1,0:T(8,128)(2,1)S(1)} %pad_maximum_fusion.1.refs_0_), channel_id=1, source_target_pairs={{0,4},{2,6},{4,0},{6,2},{8,12},{10,14},{12,8},{14,10},{16,20},{18,... | collective-permute-start | bytes 1572872 | tf_op jit(solution)/shard_map/ppermute | solution.py:284
  148.5 14.8 %collective-permute-start.26 = (bf16[2,512,128]{2,1,0:T(8,128)(2,1)S(1)}, bf16[2,512,128]{2,1,0:T(8,128)(2,1)S(1)}, u32[]{:S(2)}, u32[]{:S(2)}) collective-permute-start(bf16[2,512,128]{2,1,0:T(8,128)(2,1)S(1)} %subtract_convert_fusion.2), channel_id=1, source_target_pairs={{0,4},{2,6},{4,0},{6,2},{8,12},{10,14},{12,8},{14,10},{16,20},{18,... | collective-permute-start | bytes 786440 | tf_op jit(solution)/shard_map/ppermute | solution.py:284
  152.1 20.4 %copy-start.7 = (bf16[2,512,128]{2,1,0:T(8,128)(2,1)S(1)}, bf16[2,512,128]{2,1,0:T(8,128)(2,1)}, u32[]{:S(2)}) copy-start(bf16[2,512,128]{2,1,0:T(8,128)(2,1)} %get-tuple-element.103) | copy-start | bytes 786436
  152.2 24.7 %copy-start.6 = (bf16[2,512,128]{2,1,0:T(8,128)(2,1)S(1)}, bf16[2,512,128]{2,1,0:T(8,128)(2,1)}, u32[]{:S(2)}) copy-start(bf16[2,512,128]{2,1,0:T(8,128)(2,1)} %get-tuple-element.64) | copy-start | bytes 786436
  152.2 20.2 %collective-permute-start.21 = (f16[2,512,128]{2,1,0:T(8,128)(2,1)S(1)}, f16[2,512,128]{2,1,0:T(8,128)(2,1)S(1)}, u32[]{:S(2)}, u32[]{:S(2)}) collective-permute-start(f16[2,512,128]{2,1,0:T(8,128)(2,1)S(1)} %pad_maximum_fusion.8), channel_id=1, source_target_pairs={{0,16},{2,18},{4,20},{6,22},{8,24},{10,26},{12,28},{14,30},{16,0},... | collective-permute-start | bytes 786440 | tf_op jit(solution)/shard_map/ppermute | solution.py:284
  154.3 22.6 %collective-permute-start.16 = (f16[2,512,128]{2,1,0:T(8,128)(2,1)S(1)}, f16[2,512,128]{2,1,0:T(8,128)(2,1)S(1)}, u32[]{:S(2)}, u32[]{:S(2)}) collective-permute-start(f16[2,512,128]{2,1,0:T(8,128)(2,1)S(1)} %pad_maximum_fusion.9), channel_id=1, source_target_pairs={{0,16},{2,18},{4,20},{6,22},{8,24},{10,26},{12,28},{14,30},{16,0},... | collective-permute-start | bytes 786440 | tf_op jit(solution)/shard_map/ppermute | solution.py:284
  163.3 29.4 %collective-permute-start.27 = (bf16[4,512,128]{2,1,0:T(8,128)(2,1)S(1)}, bf16[4,512,128]{2,1,0:T(8,128)(2,1)S(1)}, u32[]{:S(2)}, u32[]{:S(2)}) collective-permute-start(bf16[4,512,128]{2,1,0:T(8,128)(2,1)S(1)} %pad_maximum_fusion.4.refs_0_), channel_id=1, source_target_pairs={{0,8},{2,10},{4,12},{6,14},{8,0},{10,2},{12,4},{14,6},{16,24},{18,... | collective-permute-start | bytes 1572872 | tf_op jit(solution)/shard_map/ppermute | solution.py:284
  172.6 6.4 %collective-permute-start.22 = (bf16[2,512,128]{2,1,0:T(8,128)(2,1)S(1)}, bf16[2,512,128]{2,1,0:T(8,128)(2,1)S(1)}, u32[]{:S(2)}, u32[]{:S(2)}) collective-permute-start(bf16[2,512,128]{2,1,0:T(8,128)(2,1)S(1)} %subtract_convert_fusion), channel_id=1, source_target_pairs={{0,4},{2,6},{4,0},{6,2},{8,12},{10,14},{12,8},{14,10},{16,20},{18,... | collective-permute-start | bytes 786440 | tf_op jit(solution)/shard_map/ppermute | solution.py:284
  177.1 15.5 %collective-permute-start.17 = (bf16[2,512,128]{2,1,0:T(8,128)(2,1)S(1)}, bf16[2,512,128]{2,1,0:T(8,128)(2,1)S(1)}, u32[]{:S(2)}, u32[]{:S(2)}) collective-permute-start(bf16[2,512,128]{2,1,0:T(8,128)(2,1)S(1)} %subtract_convert_fusion.1), channel_id=1, source_target_pairs={{0,8},{2,10},{4,12},{6,14},{8,0},{10,2},{12,4},{14,6},{16,24},{18,... | collective-permute-start | bytes 786440 | tf_op jit(solution)/shard_map/ppermute | solution.py:284
  177.2 15.8 %collective-permute-start.29 = (bf16[4,512,128]{2,1,0:T(8,128)(2,1)S(1)}, bf16[4,512,128]{2,1,0:T(8,128)(2,1)S(1)}, u32[]{:S(2)}, u32[]{:S(2)}) collective-permute-start(bf16[4,512,128]{2,1,0:T(8,128)(2,1)S(1)} %pad_maximum_fusion.1.refs_0_), channel_id=1, source_target_pairs={{0,2},{2,0},{4,6},{6,4},{8,10},{10,8},{12,14},{14,12},{16,18},{18,... | collective-permute-start | bytes 1572872 | tf_op jit(solution)/shard_map/ppermute | solution.py:284
  177.2 16.3 %collective-permute-start.30 = (bf16[4,512,128]{2,1,0:T(8,128)(2,1)S(1)}, bf16[4,512,128]{2,1,0:T(8,128)(2,1)S(1)}, u32[]{:S(2)}, u32[]{:S(2)}) collective-permute-start(bf16[4,512,128]{2,1,0:T(8,128)(2,1)S(1)} %collective-permute-done.28.refs_1_), channel_id=1, source_target_pairs={{0,2},{2,0},{4,6},{6,4},{8,10},{10,8},{12,14},{14,12},{16,18},{18,... | collective-permute-start | bytes 1572872 | tf_op jit(solution)/shard_map/ppermute | solution.py:284
  179.0 21.0 %collective-permute-start.23 = (bf16[4,512,128]{2,1,0:T(8,128)(2,1)S(1)}, bf16[4,512,128]{2,1,0:T(8,128)(2,1)S(1)}, u32[]{:S(2)}, u32[]{:S(2)}) collective-permute-start(bf16[4,512,128]{2,1,0:T(8,128)(2,1)S(1)} %pad_maximum_fusion.3.refs_4_), channel_id=1, source_target_pairs={{0,8},{2,10},{4,12},{6,14},{8,0},{10,2},{12,4},{14,6},{16,24},{18,... | collective-permute-start | bytes 1572872 | tf_op jit(solution)/shard_map/ppermute | solution.py:284
  192.6 9.2 %collective-permute-start.18 = (bf16[4,512,128]{2,1,0:T(8,128)(2,1)S(1)}, bf16[4,512,128]{2,1,0:T(8,128)(2,1)S(1)}, u32[]{:S(2)}, u32[]{:S(2)}) collective-permute-start(bf16[4,512,128]{2,1,0:T(8,128)(2,1)S(1)} %pad_maximum_fusion.2.refs_0_), channel_id=1, source_target_pairs={{0,4},{2,6},{4,0},{6,2},{8,12},{10,14},{12,8},{14,10},{16,20},{18,... | collective-permute-start | bytes 1572872 | tf_op jit(solution)/shard_map/ppermute | solution.py:284
  192.7 9.2 %collective-permute-start.31 = (bf16[4,512,128]{2,1,0:T(8,128)(2,1)S(1)}, bf16[4,512,128]{2,1,0:T(8,128)(2,1)S(1)}, u32[]{:S(2)}, u32[]{:S(2)}) collective-permute-start(bf16[4,512,128]{2,1,0:T(8,128)(2,1)S(1)} %pad_maximum_fusion.4.refs_0_), channel_id=1, source_target_pairs={{0,2},{2,0},{4,6},{6,4},{8,10},{10,8},{12,14},{14,12},{16,18},{18,... | collective-permute-start | bytes 1572872 | tf_op jit(solution)/shard_map/ppermute | solution.py:284
  193.0 12.0 %collective-permute-start.24 = (bf16[4,512,128]{2,1,0:T(8,128)(2,1)S(1)}, bf16[4,512,128]{2,1,0:T(8,128)(2,1)S(1)}, u32[]{:S(2)}, u32[]{:S(2)}) collective-permute-start(bf16[4,512,128]{2,1,0:T(8,128)(2,1)S(1)} %pad_maximum_fusion.3.refs_4_), channel_id=1, source_target_pairs={{0,2},{2,0},{4,6},{6,4},{8,10},{10,8},{12,14},{14,12},{16,18},{18,... | collective-permute-start | bytes 1572872 | tf_op jit(solution)/shard_map/ppermute | solution.py:284
  193.5 11.5 %collective-permute-start.19 = (bf16[4,512,128]{2,1,0:T(8,128)(2,1)S(1)}, bf16[4,512,128]{2,1,0:T(8,128)(2,1)S(1)}, u32[]{:S(2)}, u32[]{:S(2)}) collective-permute-start(bf16[4,512,128]{2,1,0:T(8,128)(2,1)S(1)} %pad_maximum_fusion.2.refs_0_), channel_id=1, source_target_pairs={{0,2},{2,0},{4,6},{6,4},{8,10},{10,8},{12,14},{14,12},{16,18},{18,... | collective-permute-start | bytes 1572872 | tf_op jit(solution)/shard_map/ppermute | solution.py:284
  200.1 3.5 %collective-permute-start.32 = (bf16[4,512,128]{2,1,0:T(8,128)(2,1)S(1)}, bf16[4,512,128]{2,1,0:T(8,128)(2,1)S(1)}, u32[]{:S(2)}, u32[]{:S(2)}) collective-permute-start(bf16[4,512,128]{2,1,0:T(8,128)(2,1)S(1)} %collective-permute-done.27.refs_1_), channel_id=1, source_target_pairs={{0,2},{2,0},{4,6},{6,4},{8,10},{10,8},{12,14},{14,12},{16,18},{18,... | collective-permute-start | bytes 1572872 | tf_op jit(solution)/shard_map/ppermute | solution.py:284
  201.9 3.1 %collective-permute-start.25 = (bf16[4,512,128]{2,1,0:T(8,128)(2,1)S(1)}, bf16[4,512,128]{2,1,0:T(8,128)(2,1)S(1)}, u32[]{:S(2)}, u32[]{:S(2)}) collective-permute-start(bf16[4,512,128]{2,1,0:T(8,128)(2,1)S(1)} %collective-permute-done.23.refs_5_), channel_id=1, source_target_pairs={{0,2},{2,0},{4,6},{6,4},{8,10},{10,8},{12,14},{14,12},{16,18},{18,... | collective-permute-start | bytes 1572872 | tf_op jit(solution)/shard_map/ppermute | solution.py:284
  201.9 3.1 %collective-permute-start.20 = (bf16[4,512,128]{2,1,0:T(8,128)(2,1)S(1)}, bf16[4,512,128]{2,1,0:T(8,128)(2,1)S(1)}, u32[]{:S(2)}, u32[]{:S(2)}) collective-permute-start(bf16[4,512,128]{2,1,0:T(8,128)(2,1)S(1)} %collective-permute-done.18.refs_1_), channel_id=1, source_target_pairs={{0,2},{2,0},{4,6},{6,4},{8,10},{10,8},{12,14},{14,12},{16,18},{18,... | collective-permute-start | bytes 1572872 | tf_op jit(solution)/shard_map/ppermute | solution.py:284

commit v17 on v15

--- a/solution.py
+++ b/solution.py
@@ -55,6 +55,32 @@
     return pltpu.with_memory_space_constraint(array, pltpu.HBM)
 
 
+def fetch_kernel(chunk, first_ref, second_ref, first_out, second_out, semaphore):
+    width = first_out.shape[-1]
+    columns = pl.ds(chunk * width, width)
+    copies = [
+        pltpu.make_async_copy(source.at[..., columns], target, semaphore.at[index])
+        for index, (source, target) in enumerate(((first_ref, first_out), (second_ref, second_out)))
+    ]
+    for copy in copies:
+        copy.start()
+    for copy in copies:
+        copy.wait()
+
+
+def fetch(chunk, width, first, second):
+    out = jax.ShapeDtypeStruct(first.shape[:-1] + (width,), F32)
+    return pl.pallas_call(
+        functools.partial(fetch_kernel, chunk),
+        in_specs=[pl.BlockSpec(memory_space=pl.ANY)] * 2,
+        out_specs=[pl.BlockSpec(memory_space=pltpu.VMEM)] * 2,
+        out_shape=[out, out],
+        scratch_shapes=[pltpu.SemaphoreType.DMA((2,))],
+        compiler_params=pltpu.CompilerParams(vmem_limit_bytes=MIB),
+        name="fetch",
+    )(pinned(first), pinned(second))
+
+
 def changed_place(mine, slab, pair, pairs):
     offset = lax.bitwise_xor(slab * pairs + pair, mine // 2)
     bits = (SLABS * pairs).bit_length() - 1
@@ -67,6 +93,7 @@
 def inner_kernel(
     tokens,
     kept,
+    fetched,
     mine_ref,
     low_ref,
     high_ref,
@@ -86,6 +113,8 @@
     send_refs, keep_refs = change_refs[::2], change_refs[1::2]
     step = pl.program_id(0)
     slab = pl.program_id(1)
+    if fetched:
+        first_ref, second_ref = first_ref.at[slab], second_ref.at[slab]
     pairs, cores, rows, _ = start_ref.shape
     mine = mine_ref[0]
     core = lax.rem(mine, cores)
@@ -172,7 +201,7 @@
                     out_ref[place, piece] = change[:, index * part : (index + 1) * part]
 
 
-def inner(call, width, part, mine, banks, turned, start, first, second, products, target, count, tokens):
+def inner(call, width, part, fetched, mine, banks, turned, start, first, second, products, target, count, tokens):
     slabs, pairs, cores, rows, _ = start.shape
     half, depth = banks[0].shape
 
@@ -187,16 +216,17 @@
     outputs = 2 * (width // part)
     kept = width == part
     elements = depth * width
+    states = (first, second) if fetched else (pinned(first), pinned(second))
     return pl.pallas_call(
-        functools.partial(inner_kernel, float(tokens), kept),
+        functools.partial(inner_kernel, float(tokens), kept, fetched),
         grid_spec=pltpu.PrefetchScalarGridSpec(
             num_scalar_prefetch=1,
             grid=(2, slabs),
             in_specs=[whole] * 4
             + [
                 pl.BlockSpec(tile, lambda s, z, c: (z, 0, 0, 0, call)),
-                state,
-                state,
+                whole if fetched else state,
+                whole if fetched else state,
                 product,
                 product,
                 pl.BlockSpec((2 * half, width), lambda s, z, c: (0, call)),
@@ -212,14 +242,14 @@
             ],
         ),
         out_shape=[change] * outputs,
-        compiler_params=pltpu.CompilerParams(vmem_limit_bytes=32 * MIB),
+        compiler_params=pltpu.CompilerParams(vmem_limit_bytes=(22 if kept else 32) * MIB),
         cost_estimate=pl.CostEstimate(
             flops=12 * half * elements,
             bytes_accessed=20 * elements,
             transcendentals=6 * elements,
         ),
         name="inner",
-    )(mine, *banks, *turned, pinned(start), pinned(first), pinned(second), *products, target, count)
+    )(mine, *banks, *turned, pinned(start), *states, *products, target, count)
 
 
 def assemble_kernel(begins, offsets, place_ref, *refs):
@@ -322,7 +352,8 @@
     ]
 
     own = forward(banks[0], global_weights)
-    received, (shares, own) = tied(banks[1], (shares, own))
+    early = fetch(calls[0][0] // width, width, first, second)
+    received, (shares, own, early) = tied(banks[1], (shares, own, early))
     turned, products = zip(own, forward(received, global_weights))
     banks = (banks[0], received)
     turned = [array.reshape(cut[:4] + (half,)) for array in turned]
@@ -382,8 +413,9 @@
     fresh = range(0)
     later = {}
     for begin, wide in calls:
+        states = (first, second) if fresh else early
         changes = inner(
-            begin // wide, wide, width, token, banks, turned, start, first, second, products, target, count, tokens
+            begin // wide, wide, width, not fresh, token, banks, turned, start, *states, products, target, count, tokens
         )
         sends = [send.astype(WIRE) for send in changes[::2]]
         if fresh:

time: 196 us -> 190 us (0.969)
  waiting for transfers between devices: 97.2 us -> 93 us
    ppermute x1, waiting for transfers between devices: 35.8 us -> 31.4 us  [per_device(): banks = (own_bank, lax.ppermute(own_bank, 'fsdp', [(0, 1), (1, 0)]))]
    unnamed x20 -> x26, local copies, waits for them, and re-layouts: 4.29 us -> 4.79 us
    pallas_call x3 -> x4, Pallas kernels: 42.7 us -> 43 us  [the longest x3 39.4 us: inner(): pl.pallas_call(functools.partial(inner_kernel, float(tokens), kept, fetch...]
  transfers between devices with their start and end apart: 33 -> 33, of which waited for: 17 -> 19; matrix products, arithmetic and copies ran while one was open for 4% -> 4% of each run, Pallas kernels for 18% -> 20%
where the time goes in v17:
time: 190 us
  waiting for transfers between devices  93 us (49%)
  Pallas kernels  50.9 us (27%)
  starting transfers between devices  30.6 us (16%)
  local copies, waits for them, and re-layouts  7.25 us (4%)
  other arithmetic  6.79 us (4%)
    ppermute x32, waiting for transfers between devices, swapped(): return lax.ppermute(array, 'rep', pairs)  61.6 us
    pallas_call x3, Pallas kernels, inner(): pl.pallas_call(functools.partial(inner_kernel, float(tokens), kept, fetch...  39.4 us
    ppermute x1, waiting for transfers between devices, per_device(): banks = (own_bank, lax.ppermute(own_bank, 'fsdp', [(0, 1), (1, 0)]))  31.4 us
    ppermute x32, starting transfers between devices, swapped(): return lax.ppermute(array, 'rep', pairs)  27.6 us
    pallas_call x3, Pallas kernels, assemble(): pl.pallas_call(functools.partial(assemble_kernel, begins, offsets), in_sp...  5.14 us
    unnamed x26, local copies, waits for them, and re-layouts  4.79 us
  transfers between devices with their start and end apart: 33, of which 19 were waited for; matrix products, arithmetic and copies ran while one was open for 4% of the time, Pallas kernels for 20%

profile of v17, /device:TPU:0, one launch (start us, length us, event | category | flops | bytes accessed | tf_op | source)
XLA Modules:
  0.0 189.9 jit_solution(5445261202534777505)
XLA Ops:
  0.6 3.0 %collective-permute-start = (bf16[128,8192]{1,0:T(8,128)(2,1)}, bf16[128,8192]{1,0:T(8,128)(2,1)S(1)}, u32[]{:S(2)}, u32[]{:S(2)}) collective-permute-start(bf16[128,8192]{1,0:T(8,128)(2,1)} %bitcast.86), channel_id=1, source_target_pairs={{0,1},{1,0},{2,3},{3,2},{4,5},{5,4},{6,7},{7,6},{8,9},{9,8},{10,11... | collective-permute-start | bytes 6291464 | tf_op jit(solution)/shard_map/ppermute | solution.py:329
  3.7 0.9 convert_reduce_fusion
  4.6 0.1 copy.21
  4.8 0.9 copy.22
  5.6 1.4 dynamic-slice_bitcast_fusion
  7.0 1.1 pad_maximum_fusion.5
  8.2 3.6 %fetch.1 = (f32[4,2,2,512,128]{4,3,2,1,0:T(8,128)S(1)}, f32[4,2,2,512,128]{4,3,2,1,0:T(8,128)S(1)}) custom-call(f32[4,2,2,512,512]{4,3,2,1,0:T(8,128)} %bitcast.97, f32[4,2,2,512,512]{4,3,2,1,0:T(8,128)} %bitcast.100), custom_call_target="tpu_custom_call" | custom-call | tf_op jit(solution)/shard_map/fetch/pallas_call | solution.py:73
  11.8 0.6 copy-done.1
  12.4 4.2 %copy-done = bf16[8192,512]{1,0:T(8,128)(2,1)S(1)} copy-done((bf16[8192,512]{1,0:T(8,128)(2,1)S(1)}, bf16[8192,512]{1,0:T(8,128)(2,1)}, u32[]{:S(2)}) %copy-start) | copy-done | bytes 8388632
  16.6 1.3 forward.2
  18.1 31.4 %collective-permute-done.part_ref.high_ref = bf16[128,8192]{1,0:T(8,128)(2,1)S(1)} collective-permute-done((bf16[128,8192]{1,0:T(8,128)(2,1)}, bf16[128,8192]{1,0:T(8,128)(2,1)S(1)}, u32[]{:S(2)}, u32[]{:S(2)}) %collective-permute-start) | collective-permute-done | bytes 2097184 | tf_op jit(solution)/shard_map/ppermute | solution.py:329
  49.5 1.4 forward.3
  50.9 9.7 %inner.3 = (f32[8,512,128]{2,1,0:T(8,128)S(1)}, f32[8,512,128]{2,1,0:T(8,128)S(1)}) custom-call(s32[1]{0:T(128)} %bitcast.mine_ref.place_ref, bf16[128,8192]{1,0:T(8,128)(2,1)S(1)} %bitcast.88, bf16[128,8192]{1,0:T(8,128)(2,1)S(1)} %collective-permute-done.part_ref.high_ref, bf16[4,2,2,512,128]{4,3,2,1,0:T(8,128)(2,1)S(1)} %bitcast.91, ...), custom_call_target="tpu_custom_call" | custom-call | flops 1610612736 | bytes 20971520 | tf_op jit(solution)/shard_map/inner/pallas_call | solution.py:220
  60.6 0.1 convert_element_type.204
  60.8 2.6 %collective-permute-done.1 = f16[8,512,128]{2,1,0:T(8,128)(2,1)S(1)} collective-permute-done((f16[8,512,128]{2,1,0:T(8,128)(2,1)S(1)}, f16[8,512,128]{2,1,0:T(8,128)(2,1)S(1)}, u32[]{:S(2)}, u32[]{:S(2)}) %collective-permute-start.1) | collective-permute-done | bytes 1048608 | tf_op jit(solution)/shard_map/ppermute | solution.py:314
  63.6 1.8 collective-permute-start.2
  65.4 18.5 %inner.4 = (f32[8,512,128]{2,1,0:T(8,128)S(1)}, f32[8,512,128]{2,1,0:T(8,128)S(1)}, f32[8,512,128]{2,1,0:T(8,128)S(1)}, f32[8,512,128]{2,1,0:T(8,128)S(1)}) custom-call(s32[1]{0:T(128)} %bitcast.mine_ref.place_ref, bf16[128,8192]{1,0:T(8,128)(2,1)S(1)} %bitcast.89, bf16[128,8192]{1,0:T(8,128)(2,1)S(1)} %collective-permute-done.part_ref.high_ref, ...), custom_call_target="tpu_custom_call" | custom-call | flops 3221225472 | bytes 41943040 | tf_op jit(solution)/shard_map/inner/pallas_call | solution.py:220
  84.0 0.1 convert_element_type.208
  84.4 2.6 %collective-permute-done.4 = f16[8,512,128]{2,1,0:T(8,128)(2,1)S(1)} collective-permute-done((f16[8,512,128]{2,1,0:T(8,128)(2,1)S(1)}, f16[8,512,128]{2,1,0:T(8,128)(2,1)S(1)}, u32[]{:S(2)}, u32[]{:S(2)}) %collective-permute-start.4) | collective-permute-done | bytes 1048608 | tf_op jit(solution)/shard_map/ppermute | solution.py:314
  87.0 0.2 add_convert_fusion.2
  87.2 0.4 collective-permute-start.6
  87.6 1.8 collective-permute-start.5
  89.4 11.2 %inner.5 = (f32[8,512,128]{2,1,0:T(8,128)S(1)}, f32[8,512,128]{2,1,0:T(8,128)S(1)}) custom-call(s32[1]{0:T(128)} %bitcast.mine_ref.place_ref, bf16[128,8192]{1,0:T(8,128)(2,1)S(1)} %bitcast.90, bf16[128,8192]{1,0:T(8,128)(2,1)S(1)} %collective-permute-done.part_ref.high_ref, bf16[4,2,2,512,128]{4,3,2,1,0:T(8,128)(2,1)S(1)} %bitcast.93, ...), custom_call_target="tpu_custom_call" | custom-call | flops 1610612736 | bytes 20971520 | tf_op jit(solution)/shard_map/inner/pallas_call | solution.py:220
  100.6 0.1 convert_element_type.227
  100.8 0.5 collective-permute-done.6
  101.9 1.6 collective-permute-start.9
  103.5 0.5 collective-permute-start.7
  104.1 2.6 %collective-permute-start.8 = (f16[2,512,128]{2,1,0:T(8,128)(2,1)S(1)}, f16[2,512,128]{2,1,0:T(8,128)(2,1)S(1)}, u32[]{:S(2)}, u32[]{:S(2)}) collective-permute-start(f16[2,512,128]{2,1,0:T(8,128)(2,1)S(1)} %pad_maximum_fusion.6), channel_id=1, source_target_pairs={{0,16},{2,18},{4,20},{6,22},{8,24},{10,26},{12,28},{14,30},{16,0},... | collective-permute-start | bytes 786440 | tf_op jit(solution)/shard_map/ppermute | solution.py:314
  106.7 0.2 add_convert_fusion
  106.8 1.6 collective-permute-start.14
  108.4 7.5 %collective-permute-done.9 = f16[2,512,128]{2,1,0:T(8,128)(2,1)S(1)} collective-permute-done((f16[2,512,128]{2,1,0:T(8,128)(2,1)S(1)}, f16[2,512,128]{2,1,0:T(8,128)(2,1)S(1)}, u32[]{:S(2)}, u32[]{:S(2)}) %collective-permute-start.9) | collective-permute-done | bytes 262176 | tf_op jit(solution)/shard_map/ppermute | solution.py:314
  116.1 2.6 %collective-permute-done.8 = f16[2,512,128]{2,1,0:T(8,128)(2,1)S(1)} collective-permute-done((f16[2,512,128]{2,1,0:T(8,128)(2,1)S(1)}, f16[2,512,128]{2,1,0:T(8,128)(2,1)S(1)}, u32[]{:S(2)}, u32[]{:S(2)}) %collective-permute-start.8) | collective-permute-done | bytes 262176 | tf_op jit(solution)/shard_map/ppermute | solution.py:314
  118.9 0.3 collective-permute-start.13
  119.2 1.9 %collective-permute-start.11 = (f16[2,512,128]{2,1,0:T(8,128)(2,1)S(1)}, f16[2,512,128]{2,1,0:T(8,128)(2,1)S(1)}, u32[]{:S(2)}, u32[]{:S(2)}) collective-permute-start(f16[2,512,128]{2,1,0:T(8,128)(2,1)S(1)} %add_convert_fusion.5), channel_id=1, source_target_pairs={{0,8},{2,10},{4,12},{6,14},{8,0},{10,2},{12,4},{14,6},{16,24},{18,... | collective-permute-start | bytes 786440 | tf_op jit(solution)/shard_map/ppermute | solution.py:314
  121.1 1.6 collective-permute-start.12
  122.8 6.0 %collective-permute-done.14 = f16[4,512,128]{2,1,0:T(8,128)(2,1)S(1)} collective-permute-done((f16[4,512,128]{2,1,0:T(8,128)(2,1)S(1)}, f16[4,512,128]{2,1,0:T(8,128)(2,1)S(1)}, u32[]{:S(2)}, u32[]{:S(2)}) %collective-permute-start.14) | collective-permute-done | bytes 524320 | tf_op jit(solution)/shard_map/ppermute | solution.py:314
  128.9 0.5 collective-permute-start.20
  129.4 4.2 %collective-permute-done.13 = bf16[2,512,128]{2,1,0:T(8,128)(2,1)S(1)} collective-permute-done((bf16[2,512,128]{2,1,0:T(8,128)(2,1)S(1)}, bf16[2,512,128]{2,1,0:T(8,128)(2,1)S(1)}, u32[]{:S(2)}, u32[]{:S(2)}) %collective-permute-start.13) | collective-permute-done | bytes 262176 | tf_op jit(solution)/shard_map/ppermute | solution.py:314
  133.6 1.2 collective-permute-start.28
  134.9 2.2 %collective-permute-done.12 = f16[2,512,128]{2,1,0:T(8,128)(2,1)S(1)} collective-permute-done((f16[2,512,128]{2,1,0:T(8,128)(2,1)S(1)}, f16[2,512,128]{2,1,0:T(8,128)(2,1)S(1)}, u32[]{:S(2)}, u32[]{:S(2)}) %collective-permute-start.12) | collective-permute-done | bytes 262176 | tf_op jit(solution)/shard_map/ppermute | solution.py:314
  137.2 1.4 collective-permute-start.26
  138.6 0.6 collective-permute-done.11
  139.5 2.8 %collective-permute-start.15 = (f16[2,512,128]{2,1,0:T(8,128)(2,1)S(1)}, f16[2,512,128]{2,1,0:T(8,128)(2,1)S(1)}, u32[]{:S(2)}, u32[]{:S(2)}) collective-permute-start(f16[2,512,128]{2,1,0:T(8,128)(2,1)S(1)} %pad_maximum_fusion.8), channel_id=1, source_target_pairs={{0,16},{2,18},{4,20},{6,22},{8,24},{10,26},{12,28},{14,30},{16,0},... | collective-permute-start | bytes 786440 | tf_op jit(solution)/shard_map/ppermute | solution.py:314
  142.4 3.3 %collective-permute-done.20 = f16[2,512,128]{2,1,0:T(8,128)(2,1)S(1)} collective-permute-done((f16[2,512,128]{2,1,0:T(8,128)(2,1)S(1)}, f16[2,512,128]{2,1,0:T(8,128)(2,1)S(1)}, u32[]{:S(2)}, u32[]{:S(2)}) %collective-permute-start.20) | collective-permute-done | bytes 262176 | tf_op jit(solution)/shard_map/ppermute | solution.py:314
  145.9 1.0 collective-permute-start.21
  146.9 12.5 %collective-permute-done.15 = f16[2,512,128]{2,1,0:T(8,128)(2,1)S(1)} collective-permute-done((f16[2,512,128]{2,1,0:T(8,128)(2,1)S(1)}, f16[2,512,128]{2,1,0:T(8,128)(2,1)S(1)}, u32[]{:S(2)}, u32[]{:S(2)}) %collective-permute-start.15) | collective-permute-done | bytes 262176 | tf_op jit(solution)/shard_map/ppermute | solution.py:314
  159.5 0.3 collective-permute-start.16
  159.9 1.8 collective-permute-start.27
  161.7 1.1 collective-permute-done.21
  162.9 1.2 collective-permute-start.22
  164.1 3.1 %collective-permute-done.16 = bf16[2,512,128]{2,1,0:T(8,128)(2,1)S(1)} collective-permute-done((bf16[2,512,128]{2,1,0:T(8,128)(2,1)S(1)}, bf16[2,512,128]{2,1,0:T(8,128)(2,1)S(1)}, u32[]{:S(2)}, u32[]{:S(2)}) %collective-permute-start.16) | collective-permute-done | bytes 262176 | tf_op jit(solution)/shard_map/ppermute | solution.py:314
  167.3 1.7 collective-permute-start.17
  169.0 2.4 %collective-permute-done.22 = bf16[2,512,128]{2,1,0:T(8,128)(2,1)S(1)} collective-permute-done((bf16[2,512,128]{2,1,0:T(8,128)(2,1)S(1)}, bf16[2,512,128]{2,1,0:T(8,128)(2,1)S(1)}, u32[]{:S(2)}, u32[]{:S(2)}) %collective-permute-start.22) | collective-permute-done | bytes 262176 | tf_op jit(solution)/shard_map/ppermute | solution.py:314
  171.4 0.2 collective-permute-start.23
  171.6 1.8 collective-permute-done.27.refs_1_
  173.5 7.0 %collective-permute-done.17.refs_1_ = bf16[4,512,128]{2,1,0:T(8,128)(2,1)S(1)} collective-permute-done((bf16[4,512,128]{2,1,0:T(8,128)(2,1)S(1)}, bf16[4,512,128]{2,1,0:T(8,128)(2,1)S(1)}, u32[]{:S(2)}, u32[]{:S(2)}) %collective-permute-start.17) | collective-permute-done | bytes 524320 | tf_op jit(solution)/shard_map/ppermute | solution.py:314
  180.6 0.5 collective-permute-start.24
  181.2 1.4 assemble.3.refs_4_
  182.6 1.5 collective-permute-done.23.refs_5_
  184.1 0.5 collective-permute-start.25
  184.7 1.1 pad_maximum_fusion
  185.8 0.2 collective-permute-done.32.refs_3_
  186.0 1.4 assemble.4.refs_8_
  187.5 2.3 %assemble.5 = bf16[16,512,512]{2,1,0:T(8,128)(2,1)} custom-call(s32[1]{0:T(128)} %bitcast.mine_ref.place_ref, bf16[4,512,128]{2,1,0:T(8,128)(2,1)S(1)} %pad_maximum_fusion.2.refs_0_, bf16[4,512,128]{2,1,0:T(8,128)(2,1)S(1)} %collective-permute-done.17.refs_1_, ...), custom_call_target="tpu_custom_call", output_to_operand_aliasing={{}: (9, {})} | custom-call | bytes 8388608 | tf_op jit(solution)/shard_map/assemble/pallas_call | solution.py:278
  (91 shorter events, 3.5 us)
Async XLA Ops:
  0.6 48.9 %collective-permute-start = (bf16[128,8192]{1,0:T(8,128)(2,1)}, bf16[128,8192]{1,0:T(8,128)(2,1)S(1)}, u32[]{:S(2)}, u32[]{:S(2)}) collective-permute-start(bf16[128,8192]{1,0:T(8,128)(2,1)} %bitcast.86), channel_id=1, source_target_pairs={{0,1},{1,0},{2,3},{3,2},{4,5},{5,4},{6,7},{7,6},{8,9},{9,8},{10,11... | collective-permute-start | bytes 6291464 | tf_op jit(solution)/shard_map/ppermute | solution.py:329
  5.6 2.5 %copy-start.4 = (f32[512,512]{1,0:T(8,128)S(1)}, f32[512,512]{1,0:T(8,128)}, u32[]{:S(2)}) copy-start(f32[512,512]{1,0:T(8,128)} %param.8) | copy-start | bytes 3145732
  8.1 41.4 %slice-start = ((s8[8388608]{0:T(1024)(128)(4,1)}), s8[4194304]{0:T(1024)(128)(4,1)S(1)}, s32[]{:S(2)}) async-start(s8[8388608]{0:T(1024)(128)(4,1)} %bitcast.84), calls=%async_computation | async-start | bytes 8388608
  8.2 4.2 %copy-start.1 = (bf16[1,128,8192]{2,1,0:T(8,128)(2,1)S(1)}, bf16[1,128,8192]{2,1,0:T(8,128)(2,1)}, u32[]{:S(2)}) copy-start(bf16[1,128,8192]{2,1,0:T(8,128)(2,1)} %param.11) | copy-start | bytes 6291460
  8.2 41.3 %slice-start.1 = ((s8[8388608]{0:T(1024)(128)(4,1)}), s8[4194304]{0:T(1024)(128)(4,1)S(1)}, s32[]{:S(2)}) async-start(s8[8388608]{0:T(1024)(128)(4,1)} %bitcast.84), calls=%async_computation.1 | async-start | bytes 8388608
  12.4 4.2 %copy-start = (bf16[8192,512]{1,0:T(8,128)(2,1)S(1)}, bf16[8192,512]{1,0:T(8,128)(2,1)}, u32[]{:S(2)}) copy-start(bf16[8192,512]{1,0:T(8,128)(2,1)} %weights_ref.3) | copy-start | bytes 25165828
  16.6 1.4 copy-start.5
  16.6 1.5 copy-start.6
  17.9 47.4 %copy-start.2 = (bf16[8192,128]{1,0:T(8,128)(2,1)}, bf16[8192,128]{1,0:T(8,128)(2,1)S(1)}, u32[]{:S(2)}) copy-start(bf16[8192,128]{1,0:T(8,128)(2,1)S(1)} %get-tuple-element.71) | copy-start | bytes 6291460
  60.7 2.7 %collective-permute-start.1 = (f16[8,512,128]{2,1,0:T(8,128)(2,1)S(1)}, f16[8,512,128]{2,1,0:T(8,128)(2,1)S(1)}, u32[]{:S(2)}, u32[]{:S(2)}) collective-permute-start(f16[8,512,128]{2,1,0:T(8,128)(2,1)S(1)} %convert_element_type.204), channel_id=1, source_target_pairs={{0,2},{2,0},{4,6},{6,4},{8,10},{10,8},{12,14},{14,12},{16,18},{18,... | collective-permute-start | bytes 3145736 | tf_op jit(solution)/shard_map/ppermute | solution.py:314
  63.6 20.6 %collective-permute-start.2 = (f16[4,512,128]{2,1,0:T(8,128)(2,1)S(1)}, f16[4,512,128]{2,1,0:T(8,128)(2,1)S(1)}, u32[]{:S(2)}, u32[]{:S(2)}) collective-permute-start(f16[4,512,128]{2,1,0:T(8,128)(2,1)S(1)} %add_convert_fusion.3), channel_id=1, source_target_pairs={{0,4},{2,6},{4,0},{6,2},{8,12},{10,14},{12,8},{14,10},{16,20},{18,... | collective-permute-start | bytes 1572872 | tf_op jit(solution)/shard_map/ppermute | solution.py:314
  84.2 5.2 %copy-start.3 = (bf16[8192,128]{1,0:T(8,128)(2,1)S(1)}, bf16[8192,128]{1,0:T(8,128)(2,1)}, u32[]{:S(2)}) copy-start(bf16[8192,128]{1,0:T(8,128)(2,1)} %copy-done.2) | copy-start | bytes 6291460
  84.3 2.7 %collective-permute-start.4 = (f16[8,512,128]{2,1,0:T(8,128)(2,1)S(1)}, f16[8,512,128]{2,1,0:T(8,128)(2,1)S(1)}, u32[]{:S(2)}, u32[]{:S(2)}) collective-permute-start(f16[8,512,128]{2,1,0:T(8,128)(2,1)S(1)} %convert_element_type.207), channel_id=1, source_target_pairs={{0,2},{2,0},{4,6},{6,4},{8,10},{10,8},{12,14},{14,12},{16,18},{18,... | collective-permute-start | bytes 3145736 | tf_op jit(solution)/shard_map/ppermute | solution.py:314
  87.2 14.0 %collective-permute-start.6 = (f16[4,512,128]{2,1,0:T(8,128)(2,1)S(1)}, f16[4,512,128]{2,1,0:T(8,128)(2,1)S(1)}, u32[]{:S(2)}, u32[]{:S(2)}) collective-permute-start(f16[4,512,128]{2,1,0:T(8,128)(2,1)S(1)} %add_convert_fusion.2), channel_id=1, source_target_pairs={{0,4},{2,6},{4,0},{6,2},{8,12},{10,14},{12,8},{14,10},{16,20},{18,... | collective-permute-start | bytes 1572872 | tf_op jit(solution)/shard_map/ppermute | solution.py:314
  87.6 13.2 %collective-permute-start.5 = (f16[2,512,128]{2,1,0:T(8,128)(2,1)S(1)}, f16[2,512,128]{2,1,0:T(8,128)(2,1)S(1)}, u32[]{:S(2)}, u32[]{:S(2)}) collective-permute-start(f16[2,512,128]{2,1,0:T(8,128)(2,1)S(1)} %add_convert_fusion.7), channel_id=1, source_target_pairs={{0,8},{2,10},{4,12},{6,14},{8,0},{10,2},{12,4},{14,6},{16,24},{18,... | collective-permute-start | bytes 786440 | tf_op jit(solution)/shard_map/ppermute | solution.py:314
  89.4 12.3 %collective-permute-start.3 = (f16[8,512,128]{2,1,0:T(8,128)(2,1)S(1)}, f16[8,512,128]{2,1,0:T(8,128)(2,1)S(1)}, u32[]{:S(2)}, u32[]{:S(2)}) collective-permute-start(f16[8,512,128]{2,1,0:T(8,128)(2,1)S(1)} %convert_element_type.208), channel_id=1, source_target_pairs={{0,2},{2,0},{4,6},{6,4},{8,10},{10,8},{12,14},{14,12},{16,18},{18,... | collective-permute-start | bytes 3145736 | tf_op jit(solution)/shard_map/ppermute | solution.py:314
  101.8 4.9 %collective-permute-start.10 = (f16[8,512,128]{2,1,0:T(8,128)(2,1)S(1)}, f16[8,512,128]{2,1,0:T(8,128)(2,1)S(1)}, u32[]{:S(2)}, u32[]{:S(2)}) collective-permute-start(f16[8,512,128]{2,1,0:T(8,128)(2,1)S(1)} %convert_element_type.227), channel_id=1, source_target_pairs={{0,2},{2,0},{4,6},{6,4},{8,10},{10,8},{12,14},{14,12},{16,18},{18,... | collective-permute-start | bytes 3145736 | tf_op jit(solution)/shard_map/ppermute | solution.py:314
  101.9 13.9 %collective-permute-start.9 = (f16[2,512,128]{2,1,0:T(8,128)(2,1)S(1)}, f16[2,512,128]{2,1,0:T(8,128)(2,1)S(1)}, u32[]{:S(2)}, u32[]{:S(2)}) collective-permute-start(f16[2,512,128]{2,1,0:T(8,128)(2,1)S(1)} %add_convert_fusion.6), channel_id=1, source_target_pairs={{0,8},{2,10},{4,12},{6,14},{8,0},{10,2},{12,4},{14,6},{16,24},{18,... | collective-permute-start | bytes 786440 | tf_op jit(solution)/shard_map/ppermute | solution.py:314
  103.5 15.6 %collective-permute-start.7 = (f16[4,512,128]{2,1,0:T(8,128)(2,1)S(1)}, f16[4,512,128]{2,1,0:T(8,128)(2,1)S(1)}, u32[]{:S(2)}, u32[]{:S(2)}) collective-permute-start(f16[4,512,128]{2,1,0:T(8,128)(2,1)S(1)} %add_convert_fusion.1), channel_id=1, source_target_pairs={{0,4},{2,6},{4,0},{6,2},{8,12},{10,14},{12,8},{14,10},{16,20},{18,... | collective-permute-start | bytes 1572872 | tf_op jit(solution)/shard_map/ppermute | solution.py:314
  104.1 14.7 %collective-permute-start.8 = (f16[2,512,128]{2,1,0:T(8,128)(2,1)S(1)}, f16[2,512,128]{2,1,0:T(8,128)(2,1)S(1)}, u32[]{:S(2)}, u32[]{:S(2)}) collective-permute-start(f16[2,512,128]{2,1,0:T(8,128)(2,1)S(1)} %pad_maximum_fusion.6), channel_id=1, source_target_pairs={{0,16},{2,18},{4,20},{6,22},{8,24},{10,26},{12,28},{14,30},{16,0},... | collective-permute-start | bytes 786440 | tf_op jit(solution)/shard_map/ppermute | solution.py:314
  106.8 11.9 %copy-start.10 = (bf16[2,512,128]{2,1,0:T(8,128)(2,1)S(1)}, bf16[2,512,128]{2,1,0:T(8,128)(2,1)}, u32[]{:S(2)}) copy-start(bf16[2,512,128]{2,1,0:T(8,128)(2,1)} %get-tuple-element.93) | copy-start | bytes 786436
  106.8 21.9 %collective-permute-start.14 = (f16[4,512,128]{2,1,0:T(8,128)(2,1)S(1)}, f16[4,512,128]{2,1,0:T(8,128)(2,1)S(1)}, u32[]{:S(2)}, u32[]{:S(2)}) collective-permute-start(f16[4,512,128]{2,1,0:T(8,128)(2,1)S(1)} %add_convert_fusion), channel_id=1, source_target_pairs={{0,4},{2,6},{4,0},{6,2},{8,12},{10,14},{12,8},{14,10},{16,20},{18,... | collective-permute-start | bytes 1572872 | tf_op jit(solution)/shard_map/ppermute | solution.py:314
  116.1 21.0 %copy-start.9 = (bf16[2,512,128]{2,1,0:T(8,128)(2,1)S(1)}, bf16[2,512,128]{2,1,0:T(8,128)(2,1)}, u32[]{:S(2)}) copy-start(bf16[2,512,128]{2,1,0:T(8,128)(2,1)} %get-tuple-element.102) | copy-start | bytes 786436
  118.9 14.7 %collective-permute-start.13 = (bf16[2,512,128]{2,1,0:T(8,128)(2,1)S(1)}, bf16[2,512,128]{2,1,0:T(8,128)(2,1)S(1)}, u32[]{:S(2)}, u32[]{:S(2)}) collective-permute-start(bf16[2,512,128]{2,1,0:T(8,128)(2,1)S(1)} %subtract_convert_fusion.3), channel_id=1, source_target_pairs={{0,8},{2,10},{4,12},{6,14},{8,0},{10,2},{12,4},{14,6},{16,24},{18,... | collective-permute-start | bytes 786440 | tf_op jit(solution)/shard_map/ppermute | solution.py:314
  119.2 20.0 %collective-permute-start.11 = (f16[2,512,128]{2,1,0:T(8,128)(2,1)S(1)}, f16[2,512,128]{2,1,0:T(8,128)(2,1)S(1)}, u32[]{:S(2)}, u32[]{:S(2)}) collective-permute-start(f16[2,512,128]{2,1,0:T(8,128)(2,1)S(1)} %add_convert_fusion.5), channel_id=1, source_target_pairs={{0,8},{2,10},{4,12},{6,14},{8,0},{10,2},{12,4},{14,6},{16,24},{18,... | collective-permute-start | bytes 786440 | tf_op jit(solution)/shard_map/ppermute | solution.py:314
  121.1 16.0 %collective-permute-start.12 = (f16[2,512,128]{2,1,0:T(8,128)(2,1)S(1)}, f16[2,512,128]{2,1,0:T(8,128)(2,1)S(1)}, u32[]{:S(2)}, u32[]{:S(2)}) collective-permute-start(f16[2,512,128]{2,1,0:T(8,128)(2,1)S(1)} %pad_maximum_fusion.7), channel_id=1, source_target_pairs={{0,16},{2,18},{4,20},{6,22},{8,24},{10,26},{12,28},{14,30},{16,0},... | collective-permute-start | bytes 786440 | tf_op jit(solution)/shard_map/ppermute | solution.py:314
  128.9 16.8 %collective-permute-start.20 = (f16[2,512,128]{2,1,0:T(8,128)(2,1)S(1)}, f16[2,512,128]{2,1,0:T(8,128)(2,1)S(1)}, u32[]{:S(2)}, u32[]{:S(2)}) collective-permute-start(f16[2,512,128]{2,1,0:T(8,128)(2,1)S(1)} %add_convert_fusion.4), channel_id=1, source_target_pairs={{0,8},{2,10},{4,12},{6,14},{8,0},{10,2},{12,4},{14,6},{16,24},{18,... | collective-permute-start | bytes 786440 | tf_op jit(solution)/shard_map/ppermute | solution.py:314
  133.6 35.3 %collective-permute-start.28 = (bf16[4,512,128]{2,1,0:T(8,128)(2,1)S(1)}, bf16[4,512,128]{2,1,0:T(8,128)(2,1)S(1)}, u32[]{:S(2)}, u32[]{:S(2)}) collective-permute-start(bf16[4,512,128]{2,1,0:T(8,128)(2,1)S(1)} %pad_maximum_fusion.1.refs_0_), channel_id=1, source_target_pairs={{0,4},{2,6},{4,0},{6,2},{8,12},{10,14},{12,8},{14,10},{16,20},{18,... | collective-permute-start | bytes 1572872 | tf_op jit(solution)/shard_map/ppermute | solution.py:314
  137.2 22.6 %collective-permute-start.26 = (bf16[2,512,128]{2,1,0:T(8,128)(2,1)S(1)}, bf16[2,512,128]{2,1,0:T(8,128)(2,1)S(1)}, u32[]{:S(2)}, u32[]{:S(2)}) collective-permute-start(bf16[2,512,128]{2,1,0:T(8,128)(2,1)S(1)} %subtract_convert_fusion.2), channel_id=1, source_target_pairs={{0,4},{2,6},{4,0},{6,2},{8,12},{10,14},{12,8},{14,10},{16,20},{18,... | collective-permute-start | bytes 786440 | tf_op jit(solution)/shard_map/ppermute | solution.py:314
  139.4 19.9 %copy-start.8 = (bf16[2,512,128]{2,1,0:T(8,128)(2,1)S(1)}, bf16[2,512,128]{2,1,0:T(8,128)(2,1)}, u32[]{:S(2)}) copy-start(bf16[2,512,128]{2,1,0:T(8,128)(2,1)} %get-tuple-element.69) | copy-start | bytes 786436
  139.5 19.8 %collective-permute-start.15 = (f16[2,512,128]{2,1,0:T(8,128)(2,1)S(1)}, f16[2,512,128]{2,1,0:T(8,128)(2,1)S(1)}, u32[]{:S(2)}, u32[]{:S(2)}) collective-permute-start(f16[2,512,128]{2,1,0:T(8,128)(2,1)S(1)} %pad_maximum_fusion.8), channel_id=1, source_target_pairs={{0,16},{2,18},{4,20},{6,22},{8,24},{10,26},{12,28},{14,30},{16,0},... | collective-permute-start | bytes 786440 | tf_op jit(solution)/shard_map/ppermute | solution.py:314
  145.8 17.0 %copy-start.7 = (bf16[2,512,128]{2,1,0:T(8,128)(2,1)S(1)}, bf16[2,512,128]{2,1,0:T(8,128)(2,1)}, u32[]{:S(2)}) copy-start(bf16[2,512,128]{2,1,0:T(8,128)(2,1)} %get-tuple-element.108) | copy-start | bytes 786436
  145.9 16.8 %collective-permute-start.21 = (f16[2,512,128]{2,1,0:T(8,128)(2,1)S(1)}, f16[2,512,128]{2,1,0:T(8,128)(2,1)S(1)}, u32[]{:S(2)}, u32[]{:S(2)}) collective-permute-start(f16[2,512,128]{2,1,0:T(8,128)(2,1)S(1)} %pad_maximum_fusion.9), channel_id=1, source_target_pairs={{0,16},{2,18},{4,20},{6,22},{8,24},{10,26},{12,28},{14,30},{16,0},... | collective-permute-start | bytes 786440 | tf_op jit(solution)/shard_map/ppermute | solution.py:314
  159.5 7.7 %collective-permute-start.16 = (bf16[2,512,128]{2,1,0:T(8,128)(2,1)S(1)}, bf16[2,512,128]{2,1,0:T(8,128)(2,1)S(1)}, u32[]{:S(2)}, u32[]{:S(2)}) collective-permute-start(bf16[2,512,128]{2,1,0:T(8,128)(2,1)S(1)} %subtract_convert_fusion.1), channel_id=1, source_target_pairs={{0,8},{2,10},{4,12},{6,14},{8,0},{10,2},{12,4},{14,6},{16,24},{18,... | collective-permute-start | bytes 786440 | tf_op jit(solution)/shard_map/ppermute | solution.py:314
  159.9 13.5 %collective-permute-start.27 = (bf16[4,512,128]{2,1,0:T(8,128)(2,1)S(1)}, bf16[4,512,128]{2,1,0:T(8,128)(2,1)S(1)}, u32[]{:S(2)}, u32[]{:S(2)}) collective-permute-start(bf16[4,512,128]{2,1,0:T(8,128)(2,1)S(1)} %pad_maximum_fusion.4.refs_0_), channel_id=1, source_target_pairs={{0,8},{2,10},{4,12},{6,14},{8,0},{10,2},{12,4},{14,6},{16,24},{18,... | collective-permute-start | bytes 1572872 | tf_op jit(solution)/shard_map/ppermute | solution.py:314
  162.9 8.5 %collective-permute-start.22 = (bf16[2,512,128]{2,1,0:T(8,128)(2,1)S(1)}, bf16[2,512,128]{2,1,0:T(8,128)(2,1)S(1)}, u32[]{:S(2)}, u32[]{:S(2)}) collective-permute-start(bf16[2,512,128]{2,1,0:T(8,128)(2,1)S(1)} %subtract_convert_fusion), channel_id=1, source_target_pairs={{0,4},{2,6},{4,0},{6,2},{8,12},{10,14},{12,8},{14,10},{16,20},{18,... | collective-permute-start | bytes 786440 | tf_op jit(solution)/shard_map/ppermute | solution.py:314
  164.1 16.5 %collective-permute-start.29 = (bf16[4,512,128]{2,1,0:T(8,128)(2,1)S(1)}, bf16[4,512,128]{2,1,0:T(8,128)(2,1)S(1)}, u32[]{:S(2)}, u32[]{:S(2)}) collective-permute-start(bf16[4,512,128]{2,1,0:T(8,128)(2,1)S(1)} %pad_maximum_fusion.1.refs_0_), channel_id=1, source_target_pairs={{0,2},{2,0},{4,6},{6,4},{8,10},{10,8},{12,14},{14,12},{16,18},{18,... | collective-permute-start | bytes 1572872 | tf_op jit(solution)/shard_map/ppermute | solution.py:314
  167.3 13.3 %collective-permute-start.17 = (bf16[4,512,128]{2,1,0:T(8,128)(2,1)S(1)}, bf16[4,512,128]{2,1,0:T(8,128)(2,1)S(1)}, u32[]{:S(2)}, u32[]{:S(2)}) collective-permute-start(bf16[4,512,128]{2,1,0:T(8,128)(2,1)S(1)} %pad_maximum_fusion.2.refs_0_), channel_id=1, source_target_pairs={{0,4},{2,6},{4,0},{6,2},{8,12},{10,14},{12,8},{14,10},{16,20},{18,... | collective-permute-start | bytes 1572872 | tf_op jit(solution)/shard_map/ppermute | solution.py:314
  169.0 12.1 %collective-permute-start.30 = (bf16[4,512,128]{2,1,0:T(8,128)(2,1)S(1)}, bf16[4,512,128]{2,1,0:T(8,128)(2,1)S(1)}, u32[]{:S(2)}, u32[]{:S(2)}) collective-permute-start(bf16[4,512,128]{2,1,0:T(8,128)(2,1)S(1)} %collective-permute-done.28.refs_1_), channel_id=1, source_target_pairs={{0,2},{2,0},{4,6},{6,4},{8,10},{10,8},{12,14},{14,12},{16,18},{18,... | collective-permute-start | bytes 1572872 | tf_op jit(solution)/shard_map/ppermute | solution.py:314
  171.4 12.7 %collective-permute-start.23 = (bf16[4,512,128]{2,1,0:T(8,128)(2,1)S(1)}, bf16[4,512,128]{2,1,0:T(8,128)(2,1)S(1)}, u32[]{:S(2)}, u32[]{:S(2)}) collective-permute-start(bf16[4,512,128]{2,1,0:T(8,128)(2,1)S(1)} %pad_maximum_fusion.3.refs_4_), channel_id=1, source_target_pairs={{0,8},{2,10},{4,12},{6,14},{8,0},{10,2},{12,4},{14,6},{16,24},{18,... | collective-permute-start | bytes 1572872 | tf_op jit(solution)/shard_map/ppermute | solution.py:314
  173.4 10.7 %collective-permute-start.31 = (bf16[4,512,128]{2,1,0:T(8,128)(2,1)S(1)}, bf16[4,512,128]{2,1,0:T(8,128)(2,1)S(1)}, u32[]{:S(2)}, u32[]{:S(2)}) collective-permute-start(bf16[4,512,128]{2,1,0:T(8,128)(2,1)S(1)} %pad_maximum_fusion.4.refs_0_), channel_id=1, source_target_pairs={{0,2},{2,0},{4,6},{6,4},{8,10},{10,8},{12,14},{14,12},{16,18},{18,... | collective-permute-start | bytes 1572872 | tf_op jit(solution)/shard_map/ppermute | solution.py:314
  180.6 6.9 %collective-permute-start.18 = (bf16[4,512,128]{2,1,0:T(8,128)(2,1)S(1)}, bf16[4,512,128]{2,1,0:T(8,128)(2,1)S(1)}, u32[]{:S(2)}, u32[]{:S(2)}) collective-permute-start(bf16[4,512,128]{2,1,0:T(8,128)(2,1)S(1)} %pad_maximum_fusion.2.refs_0_), channel_id=1, source_target_pairs={{0,2},{2,0},{4,6},{6,4},{8,10},{10,8},{12,14},{14,12},{16,18},{18,... | collective-permute-start | bytes 1572872 | tf_op jit(solution)/shard_map/ppermute | solution.py:314
  180.6 6.9 %collective-permute-start.24 = (bf16[4,512,128]{2,1,0:T(8,128)(2,1)S(1)}, bf16[4,512,128]{2,1,0:T(8,128)(2,1)S(1)}, u32[]{:S(2)}, u32[]{:S(2)}) collective-permute-start(bf16[4,512,128]{2,1,0:T(8,128)(2,1)S(1)} %pad_maximum_fusion.3.refs_4_), channel_id=1, source_target_pairs={{0,2},{2,0},{4,6},{6,4},{8,10},{10,8},{12,14},{14,12},{16,18},{18,... | collective-permute-start | bytes 1572872 | tf_op jit(solution)/shard_map/ppermute | solution.py:314
  181.1 6.4 %collective-permute-start.19 = (bf16[4,512,128]{2,1,0:T(8,128)(2,1)S(1)}, bf16[4,512,128]{2,1,0:T(8,128)(2,1)S(1)}, u32[]{:S(2)}, u32[]{:S(2)}) collective-permute-start(bf16[4,512,128]{2,1,0:T(8,128)(2,1)S(1)} %collective-permute-done.17.refs_1_), channel_id=1, source_target_pairs={{0,2},{2,0},{4,6},{6,4},{8,10},{10,8},{12,14},{14,12},{16,18},{18,... | collective-permute-start | bytes 1572872 | tf_op jit(solution)/shard_map/ppermute | solution.py:314
  184.1 1.9 %collective-permute-start.32 = (bf16[4,512,128]{2,1,0:T(8,128)(2,1)S(1)}, bf16[4,512,128]{2,1,0:T(8,128)(2,1)S(1)}, u32[]{:S(2)}, u32[]{:S(2)}) collective-permute-start(bf16[4,512,128]{2,1,0:T(8,128)(2,1)S(1)} %collective-permute-done.27.refs_1_), channel_id=1, source_target_pairs={{0,2},{2,0},{4,6},{6,4},{8,10},{10,8},{12,14},{14,12},{16,18},{18,... | collective-permute-start | bytes 1572872 | tf_op jit(solution)/shard_map/ppermute | solution.py:314
  184.1 3.4 %collective-permute-start.25 = (bf16[4,512,128]{2,1,0:T(8,128)(2,1)S(1)}, bf16[4,512,128]{2,1,0:T(8,128)(2,1)S(1)}, u32[]{:S(2)}, u32[]{:S(2)}) collective-permute-start(bf16[4,512,128]{2,1,0:T(8,128)(2,1)S(1)} %collective-permute-done.23.refs_5_), channel_id=1, source_target_pairs={{0,2},{2,0},{4,6},{6,4},{8,10},{10,8},{12,14},{14,12},{16,18},{18,... | collective-permute-start | bytes 1572872 | tf_op jit(solution)/shard_map/ppermute | solution.py:314
